TPU v7x, 32 devices: a whole 2x2x4 slice. The times are simulated.
32 devices in a mesh: groups: 2 (over x), tp: 8 (over z, y), attn: 2 (over core).
Axes of the slice: x: 2, y: 2, z: 4, core: 2. Of those that a mesh axis runs over, the one named last changes fastest.
Arguments:
- hidden_in: bfloat16 [256, 8192], P(('groups', 'tp', 'attn')), parts along dimension 0, may hold values from -6 to 6
- norm_gain: float32 [8192], replicated, may hold values from 0.1 to 1.9
- w_query: bfloat16 [8192, 8192], P(None, ('tp', 'attn')), may hold values from -0.0625 to 0.0625
- w_key: bfloat16 [8192, 1024], P(None, ('tp', 'attn')), may hold values from -0.0625 to 0.0625
- w_value: bfloat16 [8192, 1024], P(None, ('tp', 'attn')), may hold values from -0.0625 to 0.0625
- w_out: bfloat16 [8192, 8192], P(('tp', 'attn')), may hold values from -0.5 to 0.5
- key_pages: bfloat16 [32, 64, 32, 1024], P(('groups', 'tp', 'attn')), parts along dimension 0
- value_pages: bfloat16 [32, 64, 32, 1024], P(('groups', 'tp', 'attn')), parts along dimension 0, may hold values from -6 to 6
- page_table: int32 [32, 16, 4], P(('groups', 'tp', 'attn')), parts along dimension 0, may hold values from 0 to 63, as said below
- kv_owner: int32 [256], P('groups'), parts along dimension 0, may hold values from 0 to 15, as said below
- cached: int32 [256], P('groups'), parts along dimension 0, may hold values from 1 to 128, as said below
Outputs:
- hidden_out: bfloat16 [256, 8192], P(('groups', 'tp', 'attn')), parts along dimension 0
There are 2 independent parts, one for each index of `groups`. A program takes and returns all parts, laid end to end along the dimension named above; an argument that names none is the same for every part. Nothing has to cross between parts.
Inputs may be any that keep to these rules, and one draw needn't show every extreme that they name: `kv_owner`: no device holds the caches of more than 16 requests, and some device holds exactly 16. Some request has exactly 128 cached tokens. `page_table`: the pages named in one device's table are all different.
All inputs are finite; a program needn't handle non-finite values.
Results may differ from a plain program's by a relative error of at most 0.0065.
The roundings to bfloat16 on the way count: a program that leaves them out, or rounds other values in their place, can miss the bound.
Values may be sent and summed in bfloat16 or wider, within the bound.
No kernel may reach another device: no remote copies, remote signals or barrier semaphores. Data moves between devices by JAX's collectives and lax.ppermute only.
A program may use at most 128 MiB of HBM per device.

v0:
```python
import jax
import jax.numpy as jnp
from jax import lax
from jax.sharding import PartitionSpec as P

HEAD = 128


epsilon = 1e-05
rope_base = 500000.0


def rotate(vectors, position):
    halfway = vectors.shape[-1] // 2
    offsets = jnp.arange(halfway, dtype=jnp.float32)
    frequency = rope_base ** (-(2.0 * offsets) / vectors.shape[-1])
    angles = position.astype(jnp.float32)[..., None] * frequency
    cosine_part = jnp.cos(angles)
    sine_part = jnp.sin(angles)
    lower = vectors[..., :halfway]
    upper = vectors[..., halfway:]
    return jnp.concatenate(
        [lower * cosine_part - upper * sine_part, upper * cosine_part + lower * sine_part], axis=-1
    )


def on_device(
    hidden_in,
    norm_gain,
    w_query,
    w_key,
    w_value,
    w_out,
    key_pages,
    value_pages,
    page_table,
    kv_owner,
    cached,
):
    owners = lax.axis_size(("tp", "attn"))
    slot_count = page_table.shape[1]
    page_count = page_table.shape[2]
    per_query = w_query.shape[1]
    per_key = w_key.shape[1]
    row_width = per_query + 2 * per_key
    heads_dev = per_query // HEAD
    kv_heads = per_key * owners // HEAD
    all_heads = heads_dev * owners
    group_size = all_heads // kv_heads
    page_size = key_pages.shape[2]
    span = page_count * page_size
    score_scale = HEAD ** (-0.5)
    inputs = hidden_in.astype(jnp.float32)
    factor = lax.rsqrt(jnp.mean(inputs * inputs, axis=1, keepdims=True) + epsilon)
    normed = (inputs * factor * norm_gain).astype(jnp.bfloat16)
    shard_rows = lax.all_gather(normed, ("tp", "attn"), axis=0, tiled=True)
    query_part = jnp.dot(shard_rows, w_query, preferred_element_type=jnp.float32).astype(
        jnp.bfloat16
    )
    key_part = jnp.dot(shard_rows, w_key, preferred_element_type=jnp.float32).astype(jnp.bfloat16)
    value_part = jnp.dot(shard_rows, w_value, preferred_element_type=jnp.float32).astype(
        jnp.bfloat16
    )
    projected = jnp.concatenate([query_part, key_part, value_part], axis=1)
    onehot = (kv_owner[:, None] == jnp.arange(owners, dtype=jnp.int32)[None, :]).astype(jnp.int32)
    slot_index = jnp.sum((jnp.cumsum(onehot, axis=0) - onehot) * onehot, axis=1)
    outbound = (
        jnp.zeros((owners, slot_count, row_width), jnp.bfloat16)
        .at[kv_owner, slot_index]
        .set(projected)
    )
    inbound = lax.all_to_all(outbound, ("tp", "attn"), split_axis=0, concat_axis=0, tiled=True)
    device_id = lax.axis_index(("tp", "attn"))
    mine_mask = (
        (kv_owner == device_id)[:, None]
        & (slot_index[:, None] == jnp.arange(slot_count, dtype=jnp.int32)[None, :])
    ).astype(jnp.int32)
    lengths = jnp.sum(mine_mask * cached[:, None], axis=0)
    query_in = inbound[:, :, :per_query].reshape(owners, slot_count, heads_dev, HEAD)
    query_in = query_in.transpose(0, 2, 1, 3).reshape(all_heads, slot_count, HEAD)
    key_in = (
        inbound[:, :, per_query : per_query + per_key]
        .transpose(1, 0, 2)
        .reshape(slot_count, kv_heads, HEAD)
    )
    value_in = (
        inbound[:, :, per_query + per_key :].transpose(1, 0, 2).reshape(slot_count, kv_heads, HEAD)
    )
    query_rot = rotate(query_in.astype(jnp.float32), lengths[None, :]).astype(jnp.bfloat16)
    key_rot = rotate(key_in.astype(jnp.float32), lengths[:, None]).astype(jnp.bfloat16)
    grouped = query_rot.reshape(kv_heads, group_size, slot_count, HEAD)
    key_rows = jnp.take(key_pages[0], page_table[0], axis=0).reshape(
        slot_count, span, kv_heads, HEAD
    )
    value_rows = jnp.take(value_pages[0], page_table[0], axis=0).reshape(
        slot_count, span, kv_heads, HEAD
    )
    scores = (
        jnp.einsum("gjsd,slgd->gjsl", grouped, key_rows, preferred_element_type=jnp.float32)
        * score_scale
    )
    own_score = (
        jnp.einsum("gjsd,sgd->gjs", grouped, key_rot, preferred_element_type=jnp.float32)
        * score_scale
    )
    positions = jnp.arange(span, dtype=jnp.int32)
    valid_mask = positions[None, :] < lengths[:, None]
    masked = jnp.where(valid_mask[None, None], scores, -1e30)
    row_max = jnp.maximum(jnp.max(masked, axis=3), own_score)
    exp_terms = jnp.where(valid_mask[None, None], jnp.exp(masked - row_max[..., None]), 0.0)
    own_exp = jnp.exp(own_score - row_max)
    denominator = jnp.sum(exp_terms, axis=3) + own_exp
    weights = (exp_terms / denominator[..., None]).astype(jnp.bfloat16)
    own_weight = (own_exp / denominator).astype(jnp.bfloat16)
    mixed_heads = jnp.einsum(
        "gjsl,slgd->gjsd", weights, value_rows, preferred_element_type=jnp.float32
    )
    mixed_heads = (
        mixed_heads
        + own_weight.astype(jnp.float32)[..., None]
        * value_in.transpose(1, 0, 2).astype(jnp.float32)[:, None]
    )
    attended = mixed_heads.astype(jnp.bfloat16).reshape(owners, heads_dev, slot_count, HEAD)
    attended = attended.transpose(0, 2, 1, 3).reshape(owners, slot_count, per_query)
    returned = lax.all_to_all(attended, ("tp", "attn"), split_axis=0, concat_axis=0, tiled=True)
    head_rows = returned[kv_owner, slot_index]
    summed = lax.psum_scatter(
        jnp.dot(head_rows, w_out, preferred_element_type=jnp.float32),
        ("tp", "attn"),
        scatter_dimension=0,
        tiled=True,
    )
    return (inputs + summed).astype(jnp.bfloat16)


def solution(mesh):
    placed = (
        P(("groups", "tp", "attn"), None),
        P(),
        P(None, ("tp", "attn")),
        P(None, ("tp", "attn")),
        P(None, ("tp", "attn")),
        P(("tp", "attn"), None),
        P(("groups", "tp", "attn"), None, None, None),
        P(("groups", "tp", "attn"), None, None, None),
        P(("groups", "tp", "attn"), None, None),
        P("groups"),
        P("groups"),
    )
    return jax.shard_map(
        on_device,
        mesh=mesh,
        in_specs=placed,
        out_specs=P(("groups", "tp", "attn"), None),
        check_vma=False,
    )
```

profile of v0, /device:TPU:0, one launch (start us, length us, event | category | flops | bytes accessed | tf_op | source)
XLA Modules:
  0.0 206.1 jit_solution(16045914749853384093)
XLA Ops:
  6.5 1.2 fusion.23
  7.7 1.7 fusion.25
  9.4 0.7 compare_select_fusion
  10.3 0.7 compare_and_fusion
  11.1 5.0 %gather_fusion.2 = bf16[64,32,1024]{2,1,0:T(8,128)(2,1)} fusion(bf16[64,32,1024]{2,1,0:T(8,128)(2,1)} %bitcast.97, s32[1024]{0:T(1024)S(1)} %pad_clamp_fusion), kind=kCustom, calls=%fused_computation.1.clone | custom fusion | bytes 8388864 | tf_op jit(solution)/shard_map/jit(_take)/gather | solution.py:92
  16.0 5.0 %gather_fusion.1 = bf16[64,32,1024]{2,1,0:T(8,128)(2,1)} fusion(bf16[64,32,1024]{2,1,0:T(8,128)(2,1)} %bitcast.98, s32[1024]{0:T(1024)S(1)} %pad_clamp_fusion), kind=kCustom, calls=%fused_computation.clone | custom fusion | bytes 8388864 | tf_op jit(solution)/shard_map/jit(_take)/gather | solution.py:95
  21.5 5.9 %broadcast_select_fusion = (bf16[16,4,32,1024]{3,2,1,0:T(8,128)(2,1)}, bf16[16,4,32,1024]{3,2,1,0:T(8,128)(2,1)}) fusion(bf16[16,4,32,1024]{3,2,1,0:T(8,128)(2,1)} %bitcast.93, pred[16,4]{1,0:T(8,128)(4,1)S(1)} %copy.47, bf16[16,4,32,1024]{3,2,1,0:T(8,128)(2,1)} %bitcast.94), kind=kLoop, calls=%fused_computation.8 | loop fusion | flops 4194304 | bytes 16777280 | tf_op jit(solution)/shard_map/jit(_take)/select_n | solution.py:92
  27.4 26.3 %all-gather.2.cloned.1.call-done = bf16[128,8192]{1,0:T(8,128)(2,1)} async-done(((bf16[8,8192]{1,0:T(8,128)(2,1)}), bf16[128,8192]{1,0:T(8,128)(2,1)}) %all-gather.2.cloned.1.call-update) | async-done | bytes 2097168 | tf_op jit(solution)/shard_map/all_gather | solution.py:56
  53.7 2.6 %convolution_convert_fusion.1 = bf16[128,64]{0,1:T(8,128)(2,1)S(1)} fusion(bf16[128,8192]{1,0:T(8,128)(2,1)} %all-gather.2.cloned.1.call-done, bf16[8192,64]{0,1:T(8,128)(2,1)S(1)} %copy-done), kind=kOutput, calls=%fused_computation.17 | convolution fusion | flops 134225920 | bytes 3162112 | tf_op jit(solution)/shard_map/dot_general | solution.py:61
  56.4 2.7 %convolution_convert_fusion.2 = bf16[128,64]{0,1:T(8,128)(2,1)S(1)} fusion(bf16[128,8192]{1,0:T(8,128)(2,1)} %all-gather.2.cloned.1.call-done, bf16[8192,64]{0,1:T(8,128)(2,1)} %param.16), kind=kOutput, calls=%fused_computation.18 | convolution fusion | flops 134225920 | bytes 3162112 | tf_op jit(solution)/shard_map/dot_general | solution.py:60
  59.2 4.6 %convolution_convert_fusion = bf16[128,512]{1,0:T(8,128)(2,1)S(1)} fusion(bf16[128,8192]{1,0:T(8,128)(2,1)S(1)} %copy-done.1, bf16[8192,512]{1,0:T(8,128)(2,1)} %param.15), kind=kOutput, calls=%fused_computation.16 | convolution fusion | flops 1073807360 | bytes 10616832 | tf_op jit(solution)/shard_map/dot_general | solution.py:57
  64.0 0.8 broadcast_in_dim.35
  64.7 17.1 %scatter_fusion = bf16[16,16,640]{2,1,0:T(8,128)(2,1)} fusion(bf16[16,16,640]{2,1,0:T(8,128)(2,1)} %broadcast_in_dim.35, s32[128]{0:T(128)S(1)} %get-tuple-element.21, bf16[128,640]{1,0:T(8,128)(2,1)S(1)} %pad_maximum_fusion.2), kind=kCustom, calls=%fused_computation.3 | custom fusion | bytes 492544 | tf_op jit(solution)/shard_map/scatter | solution.py:70
  81.9 3.5 %all-to-all-start = ((bf16[16,16,640]{2,1,0:T(8,128)(2,1)}), bf16[16,16,640]{2,1,0:T(8,128)(2,1)S(1)}, u32[]{:S(2)}, u32[]{:S(2)}) async-start(bf16[16,16,640]{2,1,0:T(8,128)(2,1)} %scatter_fusion), calls=%async_computation | async-start | bytes 655360 | tf_op jit(solution)/shard_map/all_to_all | solution.py:72
  85.8 5.4 %copy.65 = bf16[256,8,8,128]{3,2,1,0:T(8,128)(2,1)} copy(bf16[256,8,8,128]{3,1,2,0:T(8,128)(2,1)} %bitcast.96) | data formatting | bytes 8388608
  91.2 3.0 %copy.66 = bf16[256,8,8,128]{3,2,1,0:T(8,128)(2,1)} copy(bf16[256,8,8,128]{3,1,2,0:T(8,128)(2,1)S(1)} %bitcast.95) | data formatting | bytes 8388608
  94.5 2.0 all-to-all-done
  97.9 4.8 %fusion.46 = (f32[8,8,16]{1,2,0:T(8,128)S(1)}, f32[8,8,16,128]{3,1,2,0:T(8,128)S(1)}) fusion(bf16[8,8,16,64]{3,1,2,0:T(8,128)(2,1)S(1)} %copy.54, bf16[8,8,16,64]{3,1,2,0:T(8,128)(2,1)S(1)} %copy.53, bf16[16,128,8,128]{3,2,1,0:T(8,128)(2,1)} %bitcast.100, pred[16,128]{1,0:T(8,128)(4,1)S(1)} %iota_compare_fusion.2), kind=kOutput, calls=%fused_computation.80 | convolution fusion | flops 34470912 | bytes 4986880 | tf_op jit(solution)/shard_map/gjsd,slgd->gjsl/dot_general | solution.py:99
  103.2 1.4 fusion.13
  104.6 13.8 %all_to_all.10 = bf16[16,16,512]{2,1,0:T(8,128)(2,1)S(1)} all-to-all(bf16[16,16,512]{2,1,0:T(8,128)(2,1)S(1)} %bitcast.105), channel_id=1, replica_groups=mesh['groups'=2,'tp'=8,'attn'=2] {'tp','attn'}, dimensions={0} | all-to-all | bytes 524288 | tf_op jit(solution)/shard_map/all_to_all | solution.py:125
  118.4 1.3 gather_fusion
  119.8 6.6 %fusion.47 = f32[128,8192]{1,0:T(8,128)} fusion(bf16[128,512]{1,0:T(8,128)(2,1)S(1)} %gather_fusion, bf16[512,8192]{1,0:T(8,128)(2,1)} %param.18), kind=kOutput, calls=%fused_computation.81 | convolution fusion | flops 1073741824 | bytes 12713984 | tf_op jit(solution)/shard_map/dot_general | solution.py:128
  126.4 71.3 %reduce-scatter.2.cloned.1.call-done = f32[8,8192]{1,0:T(8,128)} async-done(((f32[128,8192]{1,0:T(8,128)}), f32[8,8192]{1,0:T(8,128)}) %reduce-scatter.2.cloned.1.call-update) | async-done | bytes 262160 | tf_op jit(solution)/shard_map/reduce_scatter | solution.py:127
  197.7 1.6 fusion.26
  (56 shorter events, 3.5 us)
Async XLA Ops:
  6.5 47.1 %copy-start = (bf16[8192,64]{0,1:T(8,128)(2,1)S(1)}, bf16[8192,64]{0,1:T(8,128)(2,1)}, u32[]{:S(2)}) copy-start(bf16[8192,64]{0,1:T(8,128)(2,1)} %param.17) | copy-start | bytes 3145732
  6.5 47.1 %all-gather.2.cloned.1.call-start = ((), (), s32[]{:S(2)}) async-start(), calls=%async_computation.3 | async-start | bytes 2228224 | tf_op jit(solution)/shard_map/all_gather | solution.py:56
  16.0 5.0 %copy-start.5 = (s32[128]{0:T(128)S(1)}, s32[128]{0:T(128)}, u32[]{:S(2)}) copy-start(s32[128]{0:T(128)} %param.22) | copy-start | bytes 1540
  53.7 5.5 %copy-start.1 = (bf16[128,8192]{1,0:T(8,128)(2,1)S(1)}, bf16[128,8192]{1,0:T(8,128)(2,1)}, u32[]{:S(2)}) copy-start(bf16[128,8192]{1,0:T(8,128)(2,1)} %all-gather.2.cloned.1.call-done) | copy-start | bytes 6291460
  63.9 21.8 %copy-start.6 = (s32[128]{0:T(128)S(1)}, s32[128]{0:T(128)}, u32[]{:S(2)}) copy-start(s32[128]{0:T(128)} %param.23) | copy-start | bytes 1540
  81.9 14.6 %all-to-all-start = ((bf16[16,16,640]{2,1,0:T(8,128)(2,1)}), bf16[16,16,640]{2,1,0:T(8,128)(2,1)S(1)}, u32[]{:S(2)}, u32[]{:S(2)}) async-start(bf16[16,16,640]{2,1,0:T(8,128)(2,1)} %scatter_fusion), calls=%async_computation | async-start | bytes 655360 | tf_op jit(solution)/shard_map/all_to_all | solution.py:72
  85.4 112.2 %reduce-scatter.2.cloned.1.call-start = ((), (), s32[]{:S(2)}) async-start(), calls=%async_computation.4 | async-start | bytes 4456448 | tf_op jit(solution)/shard_map/reduce_scatter | solution.py:127
  85.8 5.4 %copy-start.2 = (bf16[16,4,32,1024]{3,2,1,0:T(8,128)(2,1)S(1)}, bf16[16,4,32,1024]{3,2,1,0:T(8,128)(2,1)}, u32[]{:S(2)}) copy-start(bf16[16,4,32,1024]{3,2,1,0:T(8,128)(2,1)} %get-tuple-element.18) | copy-start | bytes 12582916
  97.5 5.6 %copy-start.3 = (bf16[256,8,8,128]{3,2,1,0:T(8,128)(2,1)S(1)}, bf16[256,8,8,128]{3,2,1,0:T(8,128)(2,1)}, u32[]{:S(2)}) copy-start(bf16[256,8,8,128]{3,2,1,0:T(8,128)(2,1)} %copy.65) | copy-start | bytes 12582916
  126.3 71.3 %copy-start.4 = (bf16[8,8192]{1,0:T(8,128)(2,1)S(1)}, bf16[8,8192]{1,0:T(8,128)(2,1)}, u32[]{:S(2)}) copy-start(bf16[8,8192]{1,0:T(8,128)(2,1)} %param.13) | copy-start | bytes 393220
Sparse Core Ops, SparseCore 0:
  9.5 44.0 all-gather.1
  126.5 71.1 reduce-scatter.1
where the time goes:
time: 207 us; the launch traced here: 206 us
  waiting for transfers between devices  99.6 us (48%)
  local copies, waits for them, and re-layouts  38.7 us (19%)
  matrix products  23 us (11%)
  blocking collectives  13.8 us (7%)
  between operations  13.7 us (7%)
  other arithmetic  13.6 us (7%)
  starting transfers between devices  3.77 us (2%)
    reduce_scatter x1, waiting for transfers between devices, on_device(): lax.psum_scatter(jnp.dot(head_rows, w_out, preferred_element_type=jnp.flo...  71.3 us
    all_gather x1, waiting for transfers between devices, on_device(): shard_rows = lax.all_gather(normed, ('tp', 'attn'), axis=0, tiled=True)  26.3 us
    scatter x1, local copies, waits for them, and re-layouts, on_device(): outbound = jnp.zeros((owners, slot_count, row_width), jnp.bfloat16).at[kv...  17.1 us
    all_to_all x1, blocking collectives, on_device(): lax.all_to_all(attended, ('tp', 'attn'), split_axis=0, concat_axis=0, til...  13.8 us
    unnamed x16, local copies, waits for them, and re-layouts  8.48 us
    dot_general x1, matrix products, on_device(): jnp.dot(head_rows, w_out, preferred_element_type=jnp.float32)  6.58 us
    select_n x1, other arithmetic, on_device(): jnp.take(key_pages[0], page_table[0], axis=0)  5.89 us
    gather x1, local copies, waits for them, and re-layouts, on_device(): jnp.take(value_pages[0], page_table[0], axis=0)  4.96 us
  transfers between devices with their start and end apart: 3, of which 3 were waited for; matrix products, arithmetic and copies ran while one was open for 13% of the time, Pallas kernels for 0%

commit v1 on v0

--- a/solution.py
+++ b/solution.py
@@ -4,7 +4,7 @@
 from jax.sharding import PartitionSpec as P
 
 HEAD = 128
-
+AXES = ("tp", "attn")
 
 epsilon = 1e-05
 rope_base = 500000.0
@@ -22,6 +22,70 @@
     return jnp.concatenate(
         [lower * cosine_part - upper * sine_part, upper * cosine_part + lower * sine_part], axis=-1
     )
+
+
+class Grid:
+    def __init__(self):
+        tp = lax.axis_size("tp")
+        self.core = lax.axis_size("attn")
+        self.near = 2 if tp % 2 == 0 else 1
+        self.far = tp // self.near
+        self.size = tp * self.core
+
+    def index(self, far, near, core):
+        return (far * self.near + near) * self.core + core
+
+    def perm(self, far=0, near=0, core=0):
+        pairs = []
+        for f in range(self.far):
+            for n in range(self.near):
+                for c in range(self.core):
+                    to = self.index(
+                        (f + far) % self.far, (n + near) % self.near, (c + core) % self.core
+                    )
+                    pairs.append((self.index(f, n, c), to))
+        return pairs
+
+    def send(self, x, far=0, near=0, core=0):
+        return lax.ppermute(x, AXES, self.perm(far, near, core))
+
+    def blocks(self, sign):
+        me = lax.axis_index(AXES)
+        c = me % self.core
+        n = (me // self.core) % self.near
+        f = me // (self.core * self.near)
+        places = []
+        for dc in range(self.core):
+            for dn in range(self.near):
+                for df in range(self.far):
+                    places.append(
+                        self.index(
+                            (f + sign * df) % self.far,
+                            (n + sign * dn) % self.near,
+                            (c + sign * dc) % self.core,
+                        )
+                    )
+        return jnp.stack(places)
+
+
+def gather_rows(grid, x):
+    parts = [x] + [grid.send(x, far=d) for d in range(1, grid.far)]
+    x = jnp.concatenate(parts, axis=0)
+    x = jnp.concatenate([x] + [grid.send(x, near=d) for d in range(1, grid.near)], axis=0)
+    return jnp.concatenate([x] + [grid.send(x, core=d) for d in range(1, grid.core)], axis=0)
+
+
+def scatter_sum(grid, x):
+    for axis, count in (("core", grid.core), ("near", grid.near), ("far", grid.far)):
+        rows = x.shape[0] // count
+        got = [
+            grid.send(x[d * rows : (d + 1) * rows].astype(jnp.bfloat16), **{axis: d})
+            for d in range(1, count)
+        ]
+        x = x[:rows]
+        for part in got:
+            x = x + part.astype(jnp.float32)
+    return x
 
 
 def on_device(
@@ -37,7 +101,8 @@
     kv_owner,
     cached,
 ):
-    owners = lax.axis_size(("tp", "attn"))
+    grid = Grid()
+    owners = grid.size
     slot_count = page_table.shape[1]
     page_count = page_table.shape[2]
     per_query = w_query.shape[1]
@@ -50,27 +115,43 @@
     page_size = key_pages.shape[2]
     span = page_count * page_size
     score_scale = HEAD ** (-0.5)
+    requests = kv_owner.shape[0]
+    rows_dev = requests // owners
+    width = hidden_in.shape[1]
+
+    onehot = (kv_owner[:, None] == jnp.arange(owners, dtype=jnp.int32)[None, :]).astype(jnp.int32)
+    slot_index = jnp.sum((jnp.cumsum(onehot, axis=0) - onehot) * onehot, axis=1)
+    place = kv_owner * slot_count + slot_index
+
+    def reordered(blocks):
+        pick = blocks[:, None] == jnp.arange(owners, dtype=jnp.int32)[None, :]
+        moved = jnp.where(pick[:, :, None], place.reshape(1, owners, rows_dev), 0)
+        return jnp.sum(moved, axis=1).reshape(requests)
+
+    slots = jnp.arange(owners * slot_count, dtype=jnp.int32)
+    place_in = reordered(grid.blocks(-1))
+    place_out = reordered(grid.blocks(1))
+    route_in = (slots[:, None] == place_in[None, :]).astype(jnp.bfloat16)
+    route_out = (place_out[:, None] == slots[None, :]).astype(jnp.bfloat16)
+
     inputs = hidden_in.astype(jnp.float32)
     factor = lax.rsqrt(jnp.mean(inputs * inputs, axis=1, keepdims=True) + epsilon)
     normed = (inputs * factor * norm_gain).astype(jnp.bfloat16)
-    shard_rows = lax.all_gather(normed, ("tp", "attn"), axis=0, tiled=True)
-    query_part = jnp.dot(shard_rows, w_query, preferred_element_type=jnp.float32).astype(
-        jnp.bfloat16
-    )
-    key_part = jnp.dot(shard_rows, w_key, preferred_element_type=jnp.float32).astype(jnp.bfloat16)
-    value_part = jnp.dot(shard_rows, w_value, preferred_element_type=jnp.float32).astype(
-        jnp.bfloat16
-    )
-    projected = jnp.concatenate([query_part, key_part, value_part], axis=1)
-    onehot = (kv_owner[:, None] == jnp.arange(owners, dtype=jnp.int32)[None, :]).astype(jnp.int32)
-    slot_index = jnp.sum((jnp.cumsum(onehot, axis=0) - onehot) * onehot, axis=1)
-    outbound = (
-        jnp.zeros((owners, slot_count, row_width), jnp.bfloat16)
-        .at[kv_owner, slot_index]
-        .set(projected)
-    )
-    inbound = lax.all_to_all(outbound, ("tp", "attn"), split_axis=0, concat_axis=0, tiled=True)
-    device_id = lax.axis_index(("tp", "attn"))
+
+    w_all = jnp.concatenate([w_query, w_key, w_value], axis=1)
+    chunks = 2
+    step = width // chunks
+    projected = 0.0
+    for i in range(chunks):
+        part = gather_rows(grid, normed[:, i * step : (i + 1) * step])
+        projected = projected + jnp.dot(
+            part, w_all[i * step : (i + 1) * step], preferred_element_type=jnp.float32
+        )
+    projected = projected.astype(jnp.bfloat16)
+    outbound = jnp.dot(route_in, projected, preferred_element_type=jnp.float32)
+    outbound = outbound.astype(jnp.bfloat16).reshape(owners, slot_count, row_width)
+    inbound = lax.all_to_all(outbound, AXES, split_axis=0, concat_axis=0, tiled=True)
+    device_id = lax.axis_index(AXES)
     mine_mask = (
         (kv_owner == device_id)[:, None]
         & (slot_index[:, None] == jnp.arange(slot_count, dtype=jnp.int32)[None, :])
@@ -122,14 +203,17 @@
     )
     attended = mixed_heads.astype(jnp.bfloat16).reshape(owners, heads_dev, slot_count, HEAD)
     attended = attended.transpose(0, 2, 1, 3).reshape(owners, slot_count, per_query)
-    returned = lax.all_to_all(attended, ("tp", "attn"), split_axis=0, concat_axis=0, tiled=True)
-    head_rows = returned[kv_owner, slot_index]
-    summed = lax.psum_scatter(
-        jnp.dot(head_rows, w_out, preferred_element_type=jnp.float32),
-        ("tp", "attn"),
-        scatter_dimension=0,
-        tiled=True,
-    )
+    returned = lax.all_to_all(attended, AXES, split_axis=0, concat_axis=0, tiled=True)
+    returned = returned.reshape(owners * slot_count, per_query)
+    head_rows = jnp.dot(route_out, returned, preferred_element_type=jnp.float32)
+    head_rows = head_rows.astype(jnp.bfloat16)
+    sums = []
+    for i in range(chunks):
+        partial = jnp.dot(
+            head_rows, w_out[:, i * step : (i + 1) * step], preferred_element_type=jnp.float32
+        )
+        sums.append(scatter_sum(grid, partial))
+    summed = jnp.concatenate(sums, axis=1)
     return (inputs + summed).astype(jnp.bfloat16)
 
 

time: 207 us -> 142 us (0.69)
  waiting for transfers between devices: 99.6 us -> 31 us
  starting transfers between devices: 3.77 us -> 31.9 us
  other arithmetic: 13.6 us -> 27.6 us
  blocking collectives: 13.8 us -> 0 us
  between operations: 13.7 us -> 0.52 us
  local copies, waits for them, and re-layouts: 38.7 us -> 30.1 us
  matrix products: 23 us -> 20.5 us
    reduce_scatter x1 -> x0, waiting for transfers between devices: 71.3 us -> none  [on_device(): lax.psum_scatter(jnp.dot(head_rows, w_out, preferred_element_type=jnp.flo...]
    all_gather x1 -> x0, waiting for transfers between devices: 26.3 us -> none  [on_device(): shard_rows = lax.all_gather(normed, ('tp', 'attn'), axis=0, tiled=True)]
    ppermute x0 -> x20, starting transfers between devices: none -> 23.9 us  [send(): return lax.ppermute(x, AXES, self.perm(far, near, core))]
    ppermute x0 -> x20, waiting for transfers between devices: none -> 18.9 us  [send(): return lax.ppermute(x, AXES, self.perm(far, near, core))]
    scatter x1 -> x0, local copies, waits for them, and re-layouts: 17.1 us -> none  [on_device(): outbound = jnp.zeros((owners, slot_count, row_width), jnp.bfloat16).at[kv...]
    all_to_all x1 -> x0, blocking collectives: 13.8 us -> none  [on_device(): lax.all_to_all(attended, ('tp', 'attn'), split_axis=0, concat_axis=0, til...]
    concatenate x3, other arithmetic: 0.12 us -> 13.7 us  [the longest x1 12.8 us: on_device(): w_all = jnp.concatenate([w_query, w_key, w_value], axis=1)]
    all_to_all x1 -> x2, waiting for transfers between devices: 2.02 us -> 12.1 us  [the longest x1 9.96 us: on_device(): lax.all_to_all(attended, AXES, split_axis=0, concat_axis=0, tiled=True)]
  transfers between devices with their start and end apart: 3 -> 22, of which waited for: 3 -> 10; matrix products, arithmetic and copies ran while one was open for 13% -> 40% of each run, Pallas kernels for 0% -> 0%
where the time goes in v1:
time: 142 us
  starting transfers between devices  31.9 us (22%)
  waiting for transfers between devices  31 us (22%)
  local copies, waits for them, and re-layouts  30.1 us (21%)
  other arithmetic  27.6 us (19%)
  matrix products  20.5 us (14%)
    ppermute x20, starting transfers between devices, send(): return lax.ppermute(x, AXES, self.perm(far, near, core))  23.9 us
    ppermute x20, waiting for transfers between devices, send(): return lax.ppermute(x, AXES, self.perm(far, near, core))  18.9 us
    unnamed x33, local copies, waits for them, and re-layouts  16.2 us
    concatenate x1, other arithmetic, on_device(): w_all = jnp.concatenate([w_query, w_key, w_value], axis=1)  12.8 us
    all_to_all x1, waiting for transfers between devices, on_device(): lax.all_to_all(attended, AXES, split_axis=0, concat_axis=0, tiled=True)  9.96 us
    dot_general x2, matrix products, on_device(): jnp.dot(head_rows, w_out[:, i * step:(i + 1) * step], preferred_element_t...  5.81 us
    gather x1, local copies, waits for them, and re-layouts, on_device(): jnp.take(key_pages[0], page_table[0], axis=0)  5.05 us
    gather x1, local copies, waits for them, and re-layouts, on_device(): jnp.take(value_pages[0], page_table[0], axis=0)  4.98 us
  transfers between devices with their start and end apart: 22, of which 10 were waited for; matrix products, arithmetic and copies ran while one was open for 40% of the time, Pallas kernels for 0%

profile of v1, /device:TPU:0, one launch (start us, length us, event | category | flops | bytes accessed | tf_op | source)
XLA Modules:
  0.0 141.7 jit_solution(3804652381523081151)
XLA Ops:
  2.9 3.0 %collective-permute-start.5 = (bf16[8,4096]{1,0:T(8,128)(2,1)}, bf16[8,4096]{1,0:T(8,128)(2,1)S(1)}, u32[]{:S(2)}, u32[]{:S(2)}) collective-permute-start(bf16[8,4096]{1,0:T(8,128)(2,1)} %get-tuple-element.36), channel_id=1, source_target_pairs={{0,4},{1,5},{2,6},{3,7},{4,8},{5,9},{6,10},{7,11},{8,12},{9,13},{1... | collective-permute-start | bytes 196616 | tf_op jit(solution)/shard_map/ppermute | solution.py:50
  6.0 2.6 %collective-permute-start.6 = (bf16[8,4096]{1,0:T(8,128)(2,1)}, bf16[8,4096]{1,0:T(8,128)(2,1)S(1)}, u32[]{:S(2)}, u32[]{:S(2)}) collective-permute-start(bf16[8,4096]{1,0:T(8,128)(2,1)} %get-tuple-element.36), channel_id=1, source_target_pairs={{0,8},{1,9},{2,10},{3,11},{4,12},{5,13},{6,14},{7,15},{8,0},{9,1},... | collective-permute-start | bytes 196616 | tf_op jit(solution)/shard_map/ppermute | solution.py:50
  20.0 5.0 %gather_fusion = bf16[64,32,1024]{2,1,0:T(8,128)(2,1)} fusion(bf16[64,32,1024]{2,1,0:T(8,128)(2,1)} %bitcast.103, s32[1024]{0:T(1024)S(1)} %pad_clamp_fusion), kind=kCustom, calls=%fused_computation.clone | custom fusion | bytes 8388864 | tf_op jit(solution)/shard_map/jit(_take)/gather | solution.py:176
  25.0 5.0 %gather_fusion.1 = bf16[64,32,1024]{2,1,0:T(8,128)(2,1)} fusion(bf16[64,32,1024]{2,1,0:T(8,128)(2,1)} %bitcast.104, s32[1024]{0:T(1024)S(1)} %pad_clamp_fusion), kind=kCustom, calls=%fused_computation.1.clone | custom fusion | bytes 8388864 | tf_op jit(solution)/shard_map/jit(_take)/gather | solution.py:173
  30.4 12.8 %pad_maximum_fusion = bf16[8192,640]{1,0:T(8,128)(2,1)} fusion(bf16[8192,64]{1,0:T(8,128)(2,1)} %copy.54, bf16[8192,64]{1,0:T(8,128)(2,1)S(1)} %copy.53, bf16[8192,512]{1,0:T(8,128)(2,1)} %param.15), kind=kLoop, calls=%fused_computation.2 | loop fusion | flops 31457280 | bytes 20971520 | tf_op jit(solution)/shard_map/concatenate | solution.py:141
  43.2 3.7 %broadcast_select_fusion = (bf16[16,4,32,1024]{3,2,1,0:T(8,128)(2,1)}, bf16[16,4,32,1024]{3,2,1,0:T(8,128)(2,1)}) fusion(bf16[16,4,32,1024]{3,2,1,0:T(8,128)(2,1)S(1)} %bitcast.100, pred[16,4]{1,0:T(8,128)(4,1)S(1)} %copy.49, bf16[16,4,32,1024]{3,2,1,0:T(8,128)(2,1)S(1)} %bitcast.99), kind=kLoop, calls=%fused_computation.15 | loop fusion | flops 4194304 | bytes 16777280 | tf_op jit(solution)/shard_map/jit(_take)/select_n | solution.py:173
  47.7 2.9 %collective-permute-start.2 = (bf16[8,4096]{1,0:T(8,128)(2,1)S(1)}, bf16[8,4096]{1,0:T(8,128)(2,1)S(1)}, u32[]{:S(2)}, u32[]{:S(2)}) collective-permute-start(bf16[8,4096]{1,0:T(8,128)(2,1)S(1)} %get-tuple-element.37), channel_id=1, source_target_pairs={{0,12},{1,13},{2,14},{3,15},{4,0},{5,1},{6,2},{7,3},{8,4},{9,5},{1... | collective-permute-start | bytes 196616 | tf_op jit(solution)/shard_map/ppermute | solution.py:50
  56.9 3.8 %collective-permute-done.8 = bf16[32,4096]{1,0:T(8,128)(2,1)S(1)} collective-permute-done((bf16[32,4096]{1,0:T(8,128)(2,1)S(1)}, bf16[32,4096]{1,0:T(8,128)(2,1)S(1)}, u32[]{:S(2)}, u32[]{:S(2)}) %collective-permute-start.8) | collective-permute-done | bytes 262176 | tf_op jit(solution)/shard_map/ppermute | solution.py:50
  61.5 2.3 %collective-permute-done.3 = bf16[32,4096]{1,0:T(8,128)(2,1)S(1)} collective-permute-done((bf16[32,4096]{1,0:T(8,128)(2,1)S(1)}, bf16[32,4096]{1,0:T(8,128)(2,1)S(1)}, u32[]{:S(2)}, u32[]{:S(2)}) %collective-permute-start.3) | collective-permute-done | bytes 262176 | tf_op jit(solution)/shard_map/ppermute | solution.py:50
  64.7 3.8 %fusion = f32[128,640]{1,0:T(8,128)S(1)} fusion(bf16[128,4096]{1,0:T(8,128)(2,1)} %constant_dynamic-update-slice_fusion.16, bf16[8192,640]{1,0:T(8,128)(2,1)} %pad_maximum_fusion), kind=kOutput, calls=%fused_computation.3 | convolution fusion | flops 671088640 | bytes 6619136 | tf_op jit(solution)/shard_map/dot_general | solution.py:147
  68.6 4.4 %convolution_convert_fusion = bf16[256,640]{1,0:T(8,128)(2,1)} fusion(f32[128,640]{1,0:T(8,128)S(1)} %fusion, bf16[128,4096]{1,0:T(8,128)(2,1)S(1)} %constant_dynamic-update-slice_fusion.5, bf16[8192,640]{1,0:T(8,128)(2,1)} %pad_maximum_fusion, s32[128]{0:T(128)S(1)} %eq.216), kind=kOutput, calls=%fused_computation.18 | convolution fusion | flops 713392128 | bytes 6947328 | tf_op jit(solution)/shard_map/dot_general | solution.py:151
  73.0 4.2 %all-to-all-start = ((bf16[16,16,640]{2,1,0:T(8,128)(2,1)}), bf16[16,16,640]{2,1,0:T(8,128)(2,1)S(1)}, u32[]{:S(2)}, u32[]{:S(2)}) async-start(bf16[16,16,640]{2,1,0:T(8,128)(2,1)} %bitcast.36), calls=%async_computation | async-start | bytes 655360 | tf_op jit(solution)/shard_map/all_to_all | solution.py:153
  77.4 5.4 %copy.68 = bf16[256,8,8,128]{3,2,1,0:T(8,128)(2,1)} copy(bf16[256,8,8,128]{3,1,2,0:T(8,128)(2,1)} %bitcast.102) | data formatting | bytes 8388608
  82.8 3.1 %copy.67 = bf16[256,8,8,128]{3,2,1,0:T(8,128)(2,1)} copy(bf16[256,8,8,128]{3,1,2,0:T(8,128)(2,1)S(1)} %bitcast.101) | data formatting | bytes 8388608
  86.1 2.2 %all-to-all-done = bf16[16,16,640]{2,1,0:T(8,128)(2,1)S(1)} async-done(((bf16[16,16,640]{2,1,0:T(8,128)(2,1)}), bf16[16,16,640]{2,1,0:T(8,128)(2,1)S(1)}, u32[]{:S(2)}, u32[]{:S(2)}) %all-to-all-start) | async-done | bytes 327712 | tf_op jit(solution)/shard_map/all_to_all | solution.py:153
  90.7 2.4 %fusion.68 = (f32[8,8,16]{1,2,0:T(8,128)S(1)}, f32[8,8,16,128]{3,1,2,0:T(8,128)S(1)}) fusion(bf16[8,8,16,64]{3,1,2,0:T(8,128)(2,1)S(1)} %copy.56, bf16[8,8,16,64]{3,1,2,0:T(8,128)(2,1)S(1)} %copy.55, bf16[16,128,8,128]{3,2,1,0:T(8,128)(2,1)S(1)} %bitcast.106, pred[16,128]{1,0:T(8,128)(4,1)S(1)} %iota_compare_fusion.7), kind=kOutput, calls=%fused_computation.129 | convolution fusion | flops 34470912 | bytes 4986880 | tf_op jit(solution)/shard_map/gjsd,slgd->gjsl/dot_general | solution.py:180
  93.8 3.5 %fusion.21 = bf16[8,8,16,128]{3,1,2,0:T(8,128)(2,1)S(1)} fusion(bf16[16,128,8,128]{3,2,1,0:T(8,128)(2,1)} %bitcast.105, f32[8,8,16,128]{3,1,2,0:T(8,128)S(1)} %get-tuple-element.57, f32[8,16,128]{2,1,0:T(8,128)S(1)} %copy.61, f32[8,8,16]{1,2,0:T(8,128)S(1)} %get-tuple-element.31, f32[8,8,16]{1,2,0:T(8,128)S(1)} %get-tuple-element.30, ...), kind=kOutput, calls=%fused_computation.21 | convolution fusion | flops 34471936 | bytes 5060608 | tf_op jit(solution)/shard_map/gjsl,slgd->gjsd/dot_general | solution.py:196
  98.1 3.8 %all-to-all-start.1 = ((bf16[16,16,512]{2,1,0:T(8,128)(2,1)}), bf16[16,16,512]{2,1,0:T(8,128)(2,1)S(1)}, u32[]{:S(2)}, u32[]{:S(2)}) async-start(bf16[16,16,512]{2,1,0:T(8,128)(2,1)} %bitcast.98), calls=%async_computation.1 | async-start | bytes 524288 | tf_op jit(solution)/shard_map/all_to_all | solution.py:206
  102.0 10.0 %all-to-all-done.1 = bf16[16,16,512]{2,1,0:T(8,128)(2,1)S(1)} async-done(((bf16[16,16,512]{2,1,0:T(8,128)(2,1)}), bf16[16,16,512]{2,1,0:T(8,128)(2,1)S(1)}, u32[]{:S(2)}, u32[]{:S(2)}) %all-to-all-start.1) | async-done | bytes 262176 | tf_op jit(solution)/shard_map/all_to_all | solution.py:206
  112.2 2.9 %fusion.10 = f32[128,4096]{1,0:T(8,128)S(1)} fusion(bf16[128,512]{1,0:T(8,128)(2,1)S(1)} %convolution_convert_fusion.1, bf16[512,8192]{1,0:T(8,128)(2,1)} %param.18), kind=kOutput, calls=%fused_computation.13 | convolution fusion | flops 536870912 | bytes 6422528 | tf_op jit(solution)/shard_map/dot_general | solution.py:212
  115.3 2.9 %fusion.8 = f32[128,4096]{1,0:T(8,128)S(1)} fusion(bf16[128,512]{1,0:T(8,128)(2,1)S(1)} %convolution_convert_fusion.1, bf16[512,8192]{1,0:T(8,128)(2,1)} %param.18), kind=kOutput, calls=%fused_computation.11 | convolution fusion | flops 536870912 | bytes 6422528 | tf_op jit(solution)/shard_map/dot_general | solution.py:212
  121.3 6.9 %collective-permute-done.11 = bf16[32,4096]{1,0:T(8,128)(2,1)S(1)} collective-permute-done((bf16[32,4096]{1,0:T(8,128)(2,1)S(1)}, bf16[32,4096]{1,0:T(8,128)(2,1)S(1)}, u32[]{:S(2)}, u32[]{:S(2)}) %collective-permute-start.11) | collective-permute-done | bytes 262176 | tf_op jit(solution)/shard_map/ppermute | solution.py:50
  129.8 2.5 %collective-permute-start.14 = (bf16[8,4096]{1,0:T(8,128)(2,1)S(1)}, bf16[8,4096]{1,0:T(8,128)(2,1)S(1)}, u32[]{:S(2)}, u32[]{:S(2)}) collective-permute-start(bf16[8,4096]{1,0:T(8,128)(2,1)S(1)} %get-tuple-element.21), channel_id=1, source_target_pairs={{0,12},{1,13},{2,14},{3,15},{4,0},{5,1},{6,2},{7,3},{8,4},{9,5},{1... | collective-permute-start | bytes 196616 | tf_op jit(solution)/shard_map/ppermute | solution.py:50
  134.9 2.3 %collective-permute-start.19 = (bf16[8,4096]{1,0:T(8,128)(2,1)S(1)}, bf16[8,4096]{1,0:T(8,128)(2,1)S(1)}, u32[]{:S(2)}, u32[]{:S(2)}) collective-permute-start(bf16[8,4096]{1,0:T(8,128)(2,1)S(1)} %get-tuple-element.24), channel_id=1, source_target_pairs={{0,12},{1,13},{2,14},{3,15},{4,0},{5,1},{6,2},{7,3},{8,4},{9,5},{1... | collective-permute-start | bytes 196616 | tf_op jit(solution)/shard_map/ppermute | solution.py:50
  (130 shorter events, 39.7 us)
Async XLA Ops:
  0.0 18.1 %copy-start.5 = (bf16[8192,64]{0,1:T(8,128)(2,1)S(1)}, bf16[8192,64]{0,1:T(8,128)(2,1)}, u32[]{:S(2)}) copy-start(bf16[8192,64]{0,1:T(8,128)(2,1)} %param.17) | copy-start | bytes 3145732
  2.9 44.8 %collective-permute-start.5 = (bf16[8,4096]{1,0:T(8,128)(2,1)}, bf16[8,4096]{1,0:T(8,128)(2,1)S(1)}, u32[]{:S(2)}, u32[]{:S(2)}) collective-permute-start(bf16[8,4096]{1,0:T(8,128)(2,1)} %get-tuple-element.36), channel_id=1, source_target_pairs={{0,4},{1,5},{2,6},{3,7},{4,8},{5,9},{6,10},{7,11},{8,12},{9,13},{1... | collective-permute-start | bytes 196616 | tf_op jit(solution)/shard_map/ppermute | solution.py:50
  6.0 44.6 %collective-permute-start.6 = (bf16[8,4096]{1,0:T(8,128)(2,1)}, bf16[8,4096]{1,0:T(8,128)(2,1)S(1)}, u32[]{:S(2)}, u32[]{:S(2)}) collective-permute-start(bf16[8,4096]{1,0:T(8,128)(2,1)} %get-tuple-element.36), channel_id=1, source_target_pairs={{0,8},{1,9},{2,10},{3,11},{4,12},{5,13},{6,14},{7,15},{8,0},{9,1},... | collective-permute-start | bytes 196616 | tf_op jit(solution)/shard_map/ppermute | solution.py:50
  8.5 42.0 %collective-permute-start.7 = (bf16[8,4096]{1,0:T(8,128)(2,1)}, bf16[8,4096]{1,0:T(8,128)(2,1)S(1)}, u32[]{:S(2)}, u32[]{:S(2)}) collective-permute-start(bf16[8,4096]{1,0:T(8,128)(2,1)} %get-tuple-element.36), channel_id=1, source_target_pairs={{0,12},{1,13},{2,14},{3,15},{4,0},{5,1},{6,2},{7,3},{8,4},{9,5},{1... | collective-permute-start | bytes 196616 | tf_op jit(solution)/shard_map/ppermute | solution.py:50
  9.9 43.1 %collective-permute-start = (bf16[8,4096]{1,0:T(8,128)(2,1)S(1)}, bf16[8,4096]{1,0:T(8,128)(2,1)S(1)}, u32[]{:S(2)}, u32[]{:S(2)}) collective-permute-start(bf16[8,4096]{1,0:T(8,128)(2,1)S(1)} %get-tuple-element.37), channel_id=1, source_target_pairs={{0,4},{1,5},{2,6},{3,7},{4,8},{5,9},{6,10},{7,11},{8,12},{9,13},{1... | collective-permute-start | bytes 196616 | tf_op jit(solution)/shard_map/ppermute | solution.py:50
  10.6 42.5 %collective-permute-start.1 = (bf16[8,4096]{1,0:T(8,128)(2,1)S(1)}, bf16[8,4096]{1,0:T(8,128)(2,1)S(1)}, u32[]{:S(2)}, u32[]{:S(2)}) collective-permute-start(bf16[8,4096]{1,0:T(8,128)(2,1)S(1)} %get-tuple-element.37), channel_id=1, source_target_pairs={{0,8},{1,9},{2,10},{3,11},{4,12},{5,13},{6,14},{7,15},{8,0},{9,1},... | collective-permute-start | bytes 196616 | tf_op jit(solution)/shard_map/ppermute | solution.py:50
  47.7 5.7 %collective-permute-start.2 = (bf16[8,4096]{1,0:T(8,128)(2,1)S(1)}, bf16[8,4096]{1,0:T(8,128)(2,1)S(1)}, u32[]{:S(2)}, u32[]{:S(2)}) collective-permute-start(bf16[8,4096]{1,0:T(8,128)(2,1)S(1)} %get-tuple-element.37), channel_id=1, source_target_pairs={{0,12},{1,13},{2,14},{3,15},{4,0},{5,1},{6,2},{7,3},{8,4},{9,5},{1... | collective-permute-start | bytes 196616 | tf_op jit(solution)/shard_map/ppermute | solution.py:50
  51.4 9.3 %collective-permute-start.8 = (bf16[32,4096]{1,0:T(8,128)(2,1)S(1)}, bf16[32,4096]{1,0:T(8,128)(2,1)S(1)}, u32[]{:S(2)}, u32[]{:S(2)}) collective-permute-start(bf16[32,4096]{1,0:T(8,128)(2,1)S(1)} %pad_maximum_fusion.2), channel_id=1, source_target_pairs={{0,2},{1,3},{2,0},{3,1},{4,6},{5,7},{6,4},{7,5},{8,10},{9,11},{10,... | collective-permute-start | bytes 786440 | tf_op jit(solution)/shard_map/ppermute | solution.py:50
  53.4 10.4 %collective-permute-start.3 = (bf16[32,4096]{1,0:T(8,128)(2,1)S(1)}, bf16[32,4096]{1,0:T(8,128)(2,1)S(1)}, u32[]{:S(2)}, u32[]{:S(2)}) collective-permute-start(bf16[32,4096]{1,0:T(8,128)(2,1)S(1)} %pad_maximum_fusion.1), channel_id=1, source_target_pairs={{0,2},{1,3},{2,0},{3,1},{4,6},{5,7},{6,4},{7,5},{8,10},{9,11},{10,... | collective-permute-start | bytes 786440 | tf_op jit(solution)/shard_map/ppermute | solution.py:50
  61.5 2.4 %collective-permute-start.9 = (bf16[64,4096]{1,0:T(8,128)(2,1)S(1)}, bf16[64,4096]{1,0:T(8,128)(2,1)S(1)}, u32[]{:S(2)}, u32[]{:S(2)}) collective-permute-start(bf16[64,4096]{1,0:T(8,128)(2,1)S(1)} %get-tuple-element.28), channel_id=1, source_target_pairs={{0,1},{1,0},{2,3},{3,2},{4,5},{5,4},{6,7},{7,6},{8,9},{9,8},{10,11... | collective-permute-start | bytes 1572872 | tf_op jit(solution)/shard_map/ppermute | solution.py:50
  63.8 4.7 %collective-permute-start.4 = (bf16[64,4096]{1,0:T(8,128)(2,1)S(1)}, bf16[64,4096]{1,0:T(8,128)(2,1)S(1)}, u32[]{:S(2)}, u32[]{:S(2)}) collective-permute-start(bf16[64,4096]{1,0:T(8,128)(2,1)S(1)} %get-tuple-element.26), channel_id=1, source_target_pairs={{0,1},{1,0},{2,3},{3,2},{4,5},{5,4},{6,7},{7,6},{8,9},{9,8},{10,11... | collective-permute-start | bytes 1572872 | tf_op jit(solution)/shard_map/ppermute | solution.py:50
  73.0 15.3 %all-to-all-start = ((bf16[16,16,640]{2,1,0:T(8,128)(2,1)}), bf16[16,16,640]{2,1,0:T(8,128)(2,1)S(1)}, u32[]{:S(2)}, u32[]{:S(2)}) async-start(bf16[16,16,640]{2,1,0:T(8,128)(2,1)} %bitcast.36), calls=%async_computation | async-start | bytes 655360 | tf_op jit(solution)/shard_map/all_to_all | solution.py:153
  98.1 13.9 %all-to-all-start.1 = ((bf16[16,16,512]{2,1,0:T(8,128)(2,1)}), bf16[16,16,512]{2,1,0:T(8,128)(2,1)S(1)}, u32[]{:S(2)}, u32[]{:S(2)}) async-start(bf16[16,16,512]{2,1,0:T(8,128)(2,1)} %bitcast.98), calls=%async_computation.1 | async-start | bytes 524288 | tf_op jit(solution)/shard_map/all_to_all | solution.py:206
  115.2 3.6 %collective-permute-start.10 = (bf16[64,4096]{1,0:T(8,128)(2,1)S(1)}, bf16[64,4096]{1,0:T(8,128)(2,1)S(1)}, u32[]{:S(2)}, u32[]{:S(2)}) collective-permute-start(bf16[64,4096]{1,0:T(8,128)(2,1)S(1)} %slice.224), channel_id=1, source_target_pairs={{0,1},{1,0},{2,3},{3,2},{4,5},{5,4},{6,7},{7,6},{8,9},{9,8},{10,11... | collective-permute-start | bytes 1572872 | tf_op jit(solution)/shard_map/ppermute | solution.py:50
  118.2 2.1 %collective-permute-start.15 = (bf16[64,4096]{1,0:T(8,128)(2,1)S(1)}, bf16[64,4096]{1,0:T(8,128)(2,1)S(1)}, u32[]{:S(2)}, u32[]{:S(2)}) collective-permute-start(bf16[64,4096]{1,0:T(8,128)(2,1)S(1)} %slice.223), channel_id=1, source_target_pairs={{0,1},{1,0},{2,3},{3,2},{4,5},{5,4},{6,7},{7,6},{8,9},{9,8},{10,11... | collective-permute-start | bytes 1572872 | tf_op jit(solution)/shard_map/ppermute | solution.py:50
  118.9 22.1 %copy-start.4 = (bf16[8,8192]{1,0:T(8,128)(2,1)S(1)}, bf16[8,8192]{1,0:T(8,128)(2,1)}, u32[]{:S(2)}) copy-start(bf16[8,8192]{1,0:T(8,128)(2,1)} %param.13) | copy-start | bytes 393220
  118.9 9.2 %collective-permute-start.11 = (bf16[32,4096]{1,0:T(8,128)(2,1)S(1)}, bf16[32,4096]{1,0:T(8,128)(2,1)S(1)}, u32[]{:S(2)}, u32[]{:S(2)}) collective-permute-start(bf16[32,4096]{1,0:T(8,128)(2,1)S(1)} %slice.226), channel_id=1, source_target_pairs={{0,2},{1,3},{2,0},{3,1},{4,6},{5,7},{6,4},{7,5},{8,10},{9,11},{10,... | collective-permute-start | bytes 786440 | tf_op jit(solution)/shard_map/ppermute | solution.py:50
  120.5 12.4 %collective-permute-start.16 = (bf16[32,4096]{1,0:T(8,128)(2,1)S(1)}, bf16[32,4096]{1,0:T(8,128)(2,1)S(1)}, u32[]{:S(2)}, u32[]{:S(2)}) collective-permute-start(bf16[32,4096]{1,0:T(8,128)(2,1)S(1)} %slice.225), channel_id=1, source_target_pairs={{0,2},{1,3},{2,0},{3,1},{4,6},{5,7},{6,4},{7,5},{8,10},{9,11},{10,... | collective-permute-start | bytes 786440 | tf_op jit(solution)/shard_map/ppermute | solution.py:50
  128.2 6.6 %collective-permute-start.12 = (bf16[8,4096]{1,0:T(8,128)(2,1)S(1)}, bf16[8,4096]{1,0:T(8,128)(2,1)S(1)}, u32[]{:S(2)}, u32[]{:S(2)}) collective-permute-start(bf16[8,4096]{1,0:T(8,128)(2,1)S(1)} %get-tuple-element.20), channel_id=1, source_target_pairs={{0,4},{1,5},{2,6},{3,7},{4,8},{5,9},{6,10},{7,11},{8,12},{9,13},{1... | collective-permute-start | bytes 196616 | tf_op jit(solution)/shard_map/ppermute | solution.py:50
  128.5 8.8 %collective-permute-start.13 = (bf16[8,4096]{1,0:T(8,128)(2,1)S(1)}, bf16[8,4096]{1,0:T(8,128)(2,1)S(1)}, u32[]{:S(2)}, u32[]{:S(2)}) collective-permute-start(bf16[8,4096]{1,0:T(8,128)(2,1)S(1)} %get-tuple-element.22), channel_id=1, source_target_pairs={{0,8},{1,9},{2,10},{3,11},{4,12},{5,13},{6,14},{7,15},{8,0},{9,1},... | collective-permute-start | bytes 196616 | tf_op jit(solution)/shard_map/ppermute | solution.py:50
  129.8 7.4 %collective-permute-start.14 = (bf16[8,4096]{1,0:T(8,128)(2,1)S(1)}, bf16[8,4096]{1,0:T(8,128)(2,1)S(1)}, u32[]{:S(2)}, u32[]{:S(2)}) collective-permute-start(bf16[8,4096]{1,0:T(8,128)(2,1)S(1)} %get-tuple-element.21), channel_id=1, source_target_pairs={{0,12},{1,13},{2,14},{3,15},{4,0},{5,1},{6,2},{7,3},{8,4},{9,5},{1... | collective-permute-start | bytes 196616 | tf_op jit(solution)/shard_map/ppermute | solution.py:50
  132.9 6.5 %collective-permute-start.17 = (bf16[8,4096]{1,0:T(8,128)(2,1)S(1)}, bf16[8,4096]{1,0:T(8,128)(2,1)S(1)}, u32[]{:S(2)}, u32[]{:S(2)}) collective-permute-start(bf16[8,4096]{1,0:T(8,128)(2,1)S(1)} %get-tuple-element.23), channel_id=1, source_target_pairs={{0,4},{1,5},{2,6},{3,7},{4,8},{5,9},{6,10},{7,11},{8,12},{9,13},{1... | collective-permute-start | bytes 196616 | tf_op jit(solution)/shard_map/ppermute | solution.py:50
  133.7 7.3 %collective-permute-start.18 = (bf16[8,4096]{1,0:T(8,128)(2,1)S(1)}, bf16[8,4096]{1,0:T(8,128)(2,1)S(1)}, u32[]{:S(2)}, u32[]{:S(2)}) collective-permute-start(bf16[8,4096]{1,0:T(8,128)(2,1)S(1)} %get-tuple-element.25), channel_id=1, source_target_pairs={{0,8},{1,9},{2,10},{3,11},{4,12},{5,13},{6,14},{7,15},{8,0},{9,1},... | collective-permute-start | bytes 196616 | tf_op jit(solution)/shard_map/ppermute | solution.py:50
  134.9 6.1 %collective-permute-start.19 = (bf16[8,4096]{1,0:T(8,128)(2,1)S(1)}, bf16[8,4096]{1,0:T(8,128)(2,1)S(1)}, u32[]{:S(2)}, u32[]{:S(2)}) collective-permute-start(bf16[8,4096]{1,0:T(8,128)(2,1)S(1)} %get-tuple-element.24), channel_id=1, source_target_pairs={{0,12},{1,13},{2,14},{3,15},{4,0},{5,1},{6,2},{7,3},{8,4},{9,5},{1... | collective-permute-start | bytes 196616 | tf_op jit(solution)/shard_map/ppermute | solution.py:50
  (9 other events, 89.6 us)

commit v2 on v1

v2 whole, which is shorter than its diff:
```python
import functools

import jax
import jax.numpy as jnp
from jax import lax
from jax.experimental import pallas as pl
from jax.experimental.pallas import tpu as pltpu
from jax.sharding import PartitionSpec as P

HEAD = 128
AXES = ("tp", "attn")

epsilon = 1e-05
rope_base = 500000.0


class Grid:
    def __init__(self):
        tp = lax.axis_size("tp")
        self.core = lax.axis_size("attn")
        self.near = 2 if tp % 2 == 0 else 1
        self.far = tp // self.near
        self.size = tp * self.core

    def index(self, far, near, core):
        return (far * self.near + near) * self.core + core

    def perm(self, far=0, near=0, core=0):
        pairs = []
        for f in range(self.far):
            for n in range(self.near):
                for c in range(self.core):
                    to = self.index(
                        (f + far) % self.far, (n + near) % self.near, (c + core) % self.core
                    )
                    pairs.append((self.index(f, n, c), to))
        return pairs

    def send(self, x, far=0, near=0, core=0):
        return lax.ppermute(x, AXES, self.perm(far, near, core))

    def blocks(self, sign):
        me = lax.axis_index(AXES)
        c = me % self.core
        n = (me // self.core) % self.near
        f = me // (self.core * self.near)
        places = []
        for dc in range(self.core):
            for dn in range(self.near):
                for df in range(self.far):
                    places.append(
                        self.index(
                            (f + sign * df) % self.far,
                            (n + sign * dn) % self.near,
                            (c + sign * dc) % self.core,
                        )
                    )
        return jnp.stack(places)


def gather_rows(grid, x):
    parts = [x] + [grid.send(x, far=d) for d in range(1, grid.far)]
    x = jnp.concatenate(parts, axis=0)
    x = jnp.concatenate([x] + [grid.send(x, near=d) for d in range(1, grid.near)], axis=0)
    return x, grid.send(x, core=1)


def scatter_sum(grid, x):
    for axis, count in (("core", grid.core), ("near", grid.near), ("far", grid.far)):
        rows = x.shape[0] // count
        got = [
            grid.send(x[d * rows : (d + 1) * rows].astype(jnp.bfloat16), **{axis: d})
            for d in range(1, count)
        ]
        x = x[:rows]
        for part in got:
            x = x + part.astype(jnp.float32)
    return x


def project_kernel(first, last, xa, xb, wq, wk, wv, *refs):
    if not first:
        before, refs = refs[0], refs[1:]
    if last:
        place, refs = refs[0], refs[1:]
    out, total = refs
    step = pl.program_id(0)
    per_query = wq.shape[1]

    @pl.when(step == 0)
    def _():
        total[...] = jnp.zeros_like(total) if first else before[...]

    x = jnp.concatenate([xa[...], xb[...]], axis=0)
    pieces = [wk[...], wv[...]]
    spare = total.shape[1] - per_query - 2 * wk.shape[0]
    if spare:
        pieces.append(jnp.zeros((spare, wk.shape[1]), wk.dtype))
    kv = jnp.concatenate(pieces, axis=0)
    total[:, :per_query] += jnp.dot(x, wq[...], preferred_element_type=jnp.float32)
    total[:, per_query:] += lax.dot_general(
        x, kv, (((1,), (1,)), ((), ())), preferred_element_type=jnp.float32
    )

    @pl.when(step == pl.num_programs(0) - 1)
    def _():
        if last:
            rows = lax.broadcasted_iota(jnp.int32, (out.shape[0], place.shape[1]), 0)
            route = jnp.where(rows == place[...], 1.0, 0.0).astype(jnp.bfloat16)
            moved = jnp.dot(
                route, total[...].astype(jnp.bfloat16), preferred_element_type=jnp.float32
            )
            out[...] = moved.astype(jnp.bfloat16)
        else:
            out[...] = total[...]


def project(chunk, chunks, halves, w_query, w_key_t, w_value_t, before, place, slots, row_width):
    xa, xb = halves
    width = xa.shape[1]
    block = min(1024, width)
    steps = width // block
    start = chunk * steps
    rows = xa.shape[0] + xb.shape[0]
    first, last = chunk == 0, chunk == chunks - 1
    whole = lambda i: (0, 0)
    args = [xa, xb, w_query, w_key_t, w_value_t]
    specs = [
        pl.BlockSpec((xa.shape[0], block), lambda i: (0, i)),
        pl.BlockSpec((xb.shape[0], block), lambda i: (0, i)),
        pl.BlockSpec((block, w_query.shape[1]), lambda i: (start + i, 0)),
        pl.BlockSpec((w_key_t.shape[0], block), lambda i: (0, start + i)),
        pl.BlockSpec((w_value_t.shape[0], block), lambda i: (0, start + i)),
    ]
    if not first:
        args.append(before)
        specs.append(pl.BlockSpec(before.shape, whole))
    if last:
        args.append(place.reshape(1, rows))
        specs.append(pl.BlockSpec((1, rows), whole))
        out = jax.ShapeDtypeStruct((slots, row_width), jnp.bfloat16)
    else:
        out = jax.ShapeDtypeStruct((rows, row_width), jnp.float32)
    return pl.pallas_call(
        functools.partial(project_kernel, first, last),
        grid=(steps,),
        in_specs=specs,
        out_specs=pl.BlockSpec(out.shape, whole),
        out_shape=out,
        scratch_shapes=[pltpu.VMEM((rows, row_width), jnp.float32)],
        compiler_params=pltpu.CompilerParams(vmem_limit_bytes=24 * 2**20),
        cost_estimate=pl.CostEstimate(
            flops=2 * rows * width * row_width,
            bytes_accessed=2 * width * row_width,
            transcendentals=0,
        ),
        name="project",
    )(*args)


def attend_kernel(
    batch,
    per_query,
    per_key,
    table,
    lengths,
    inbound,
    cosine,
    sine,
    key_pages,
    value_pages,
    out,
    keys,
    values,
    query_rot,
    key_own,
    value_own,
    mixed,
    key_sems,
    value_sems,
):
    owners, slots, _ = inbound.shape
    pages = table.shape[1]
    page = key_pages.shape[1]
    kv_heads = key_pages.shape[2] // HEAD
    heads_dev = per_query // HEAD
    heads = owners * heads_dev
    group = heads // kv_heads
    span = pages * page
    pieces = owners // kv_heads

    def fetch(slot, carry):
        for j in range(pages):
            number = table[slot, j]
            rows = pl.ds(j * page, page)
            pltpu.make_async_copy(
                key_pages.at[number], keys.at[slot, rows], key_sems.at[slot]
            ).start()
            pltpu.make_async_copy(
                value_pages.at[number], values.at[slot, rows], value_sems.at[slot]
            ).start()
        return carry

    lax.fori_loop(0, slots, fetch, 0)

    cos = cosine[...]
    sin = sine[...]

    def turn(x):
        turned = x * cos + pltpu.roll(x, HEAD // 2, 1) * sin
        return turned.astype(jnp.bfloat16).astype(jnp.float32)

    for source in range(owners):
        for j in range(heads_dev):
            head = source * heads_dev + j
            x = inbound[source, :, j * HEAD : (j + 1) * HEAD].astype(jnp.float32)
            query_rot[head * slots : (head + 1) * slots, :] = turn(x)

    lane = lax.broadcasted_iota(jnp.int32, (slots, HEAD), 1) // per_key
    for g in range(kv_heads):
        key = jnp.zeros((slots, HEAD), jnp.float32)
        value = jnp.zeros((slots, HEAD), jnp.float32)
        for j in range(pieces):
            tile = inbound[g * pieces + j, :, per_query : per_query + HEAD].astype(jnp.float32)
            shift = j * per_key
            back = (shift - per_key) % HEAD
            key = jnp.where(lane == j, pltpu.roll(tile, shift, 1) if shift else tile, key)
            value = jnp.where(lane == j, pltpu.roll(tile, back, 1) if back else tile, value)
        key_own[g * slots : (g + 1) * slots, :] = turn(key)
        value_own[g * slots : (g + 1) * slots, :] = value

    scale = HEAD ** (-0.5)
    position = lax.broadcasted_iota(jnp.int32, (heads, span), 1)
    pair = 2 * group
    upper = lax.broadcasted_iota(jnp.int32, (pair, HEAD), 0) < group
    zero = jnp.zeros((pair, HEAD), jnp.bfloat16)

    def some(step, carry):
        places = [step * batch + b for b in range(batch)]
        scored = []
        for slot in places:
            pltpu.make_async_copy(keys.at[slot], keys.at[slot], key_sems.at[slot]).wait()
            rotated = query_rot[pl.ds(slot, heads, stride=slots), :]
            low = rotated.astype(jnp.bfloat16)
            parts = []
            for p in range(kv_heads // 2):
                mine = low[p * pair : (p + 1) * pair]
                wide = jnp.concatenate(
                    [jnp.where(upper, mine, zero), jnp.where(upper, zero, mine)], axis=1
                )
                parts.append(
                    lax.dot_general(
                        wide,
                        keys[slot, :, p * 2 * HEAD : (p + 1) * 2 * HEAD],
                        (((1,), (1,)), ((), ())),
                        preferred_element_type=jnp.float32,
                    )
                )
            own_key = key_own[pl.ds(slot, kv_heads, stride=slots), :]
            product = rotated.reshape(kv_heads, group, HEAD) * own_key[:, None, :]
            own = jnp.sum(product.reshape(heads, HEAD), axis=1, keepdims=True) * scale
            scored.append((jnp.concatenate(parts, axis=0) * scale, own))
        chances = []
        for slot, (scores, own) in zip(places, scored):
            valid = position < lengths[slot]
            masked = jnp.where(valid, scores, -1e30)
            top = jnp.maximum(jnp.max(masked, axis=1, keepdims=True), own)
            terms = jnp.where(valid, jnp.exp(masked - top), 0.0)
            own_term = jnp.exp(own - top)
            total = jnp.sum(terms, axis=1, keepdims=True) + own_term
            own_chance = (own_term / total).astype(jnp.bfloat16).astype(jnp.float32)
            chances.append(((terms / total).astype(jnp.bfloat16), own_chance))
        for slot, (chance, own_chance) in zip(places, chances):
            pltpu.make_async_copy(values.at[slot], values.at[slot], value_sems.at[slot]).wait()
            parts = []
            for p in range(kv_heads // 2):
                both = jnp.dot(
                    chance[p * pair : (p + 1) * pair],
                    values[slot, :, p * 2 * HEAD : (p + 1) * 2 * HEAD],
                    preferred_element_type=jnp.float32,
                )
                parts.append(both[:group, :HEAD])
                parts.append(both[group:, HEAD:])
            own_value = value_own[pl.ds(slot, kv_heads, stride=slots), :]
            own_value = jnp.broadcast_to(own_value[:, None, :], (kv_heads, group, HEAD))
            result = jnp.concatenate(parts, axis=0) + own_chance * own_value.reshape(heads, HEAD)
            mixed[pl.ds(slot, heads, stride=slots), :] = result
        return carry

    lax.fori_loop(0, slots // batch, some, 0)

    for target in range(owners):
        for j in range(heads_dev):
            head = target * heads_dev + j
            out[target, :, j * HEAD : (j + 1) * HEAD] = mixed[
                head * slots : (head + 1) * slots, :
            ].astype(jnp.bfloat16)


def attend(inbound, lengths, table, cosine, sine, key_pages, value_pages, per_query, per_key):
    owners, slots, _ = inbound.shape
    pages = table.shape[1]
    page, kv_width = key_pages.shape[1:]
    kv_heads = kv_width // HEAD
    heads = owners * (per_query // HEAD)
    held = (slots, pages * page, kv_width)
    smem = pl.BlockSpec(memory_space=pltpu.SMEM)
    vmem = pl.BlockSpec(memory_space=pltpu.VMEM)
    hbm = pl.BlockSpec(memory_space=pl.ANY)
    return pl.pallas_call(
        functools.partial(attend_kernel, 4, per_query, per_key),
        in_specs=[smem, smem, vmem, vmem, vmem, hbm, hbm],
        out_specs=vmem,
        out_shape=jax.ShapeDtypeStruct((owners, slots, per_query), jnp.bfloat16),
        scratch_shapes=[
            pltpu.VMEM(held, jnp.bfloat16),
            pltpu.VMEM(held, jnp.bfloat16),
            pltpu.VMEM((heads * slots, HEAD), jnp.float32),
            pltpu.VMEM((kv_heads * slots, HEAD), jnp.float32),
            pltpu.VMEM((kv_heads * slots, HEAD), jnp.float32),
            pltpu.VMEM((heads * slots, HEAD), jnp.float32),
            pltpu.SemaphoreType.DMA((slots,)),
            pltpu.SemaphoreType.DMA((slots,)),
        ],
        compiler_params=pltpu.CompilerParams(vmem_limit_bytes=24 * 2**20),
        cost_estimate=pl.CostEstimate(
            flops=8 * slots * heads * pages * page * HEAD,
            bytes_accessed=4 * slots * pages * page * kv_width,
            transcendentals=slots * heads * pages * page,
        ),
        name="attend",
    )(table, lengths, inbound, cosine, sine, key_pages, value_pages)


def on_device(
    hidden_in,
    norm_gain,
    w_query,
    w_key,
    w_value,
    w_out,
    key_pages,
    value_pages,
    page_table,
    kv_owner,
    cached,
):
    grid = Grid()
    owners = grid.size
    slot_count = page_table.shape[1]
    per_query = w_query.shape[1]
    per_key = w_key.shape[1]
    row_width = per_query + -(-2 * per_key // HEAD) * HEAD
    requests = kv_owner.shape[0]
    rows_dev = requests // owners
    width = hidden_in.shape[1]
    all_slots = owners * slot_count

    inputs = hidden_in.astype(jnp.float32)
    factor = lax.rsqrt(jnp.mean(inputs * inputs, axis=1, keepdims=True) + epsilon)
    normed = (inputs * factor * norm_gain).astype(jnp.bfloat16)

    order = jnp.arange(requests, dtype=jnp.int32)
    earlier = (kv_owner[:, None] == kv_owner[None, :]) & (order[None, :] < order[:, None])
    slot_index = jnp.sum(earlier.astype(jnp.int32), axis=1)
    place = kv_owner * slot_count + slot_index

    def reordered(blocks):
        pick = blocks[:, None] == jnp.arange(owners, dtype=jnp.int32)[None, :]
        moved = jnp.where(pick[:, :, None], place.reshape(1, owners, rows_dev), 0)
        return jnp.sum(moved, axis=1).reshape(requests)

    slots = jnp.arange(all_slots, dtype=jnp.int32)
    place_in = reordered(grid.blocks(-1))
    place_out = reordered(grid.blocks(1))
    route_out = (place_out[:, None] == slots[None, :]).astype(jnp.bfloat16)

    mine = lax.axis_index(AXES) * slot_count + jnp.arange(slot_count, dtype=jnp.int32)
    lengths = jnp.sum(jnp.where(place[:, None] == mine[None, :], cached[:, None], 0), axis=0)
    halfway = HEAD // 2
    offsets = jnp.arange(halfway, dtype=jnp.float32)
    frequency = rope_base ** (-(2.0 * offsets) / HEAD)
    angles = lengths.astype(jnp.float32)[:, None] * frequency
    cosine_part = jnp.cos(angles)
    sine_part = jnp.sin(angles)
    cosine = jnp.concatenate([cosine_part, cosine_part], axis=1)
    sine = jnp.concatenate([-sine_part, sine_part], axis=1)

    chunks = 2
    step = width // chunks
    total = None
    for i in range(chunks):
        halves = gather_rows(grid, normed[:, i * step : (i + 1) * step])
        total = project(
            i, chunks, halves, w_query, w_key.T, w_value.T, total, place_in, all_slots, row_width
        )
    outbound = total.reshape(owners, slot_count, row_width)
    inbound = lax.all_to_all(outbound, AXES, split_axis=0, concat_axis=0, tiled=True)
    attended = attend(
        inbound,
        lengths,
        page_table[0],
        cosine,
        sine,
        key_pages[0],
        value_pages[0],
        per_query,
        per_key,
    )
    returned = lax.all_to_all(attended, AXES, split_axis=0, concat_axis=0, tiled=True)
    returned = returned.reshape(all_slots, per_query)
    head_rows = jnp.dot(route_out, returned, preferred_element_type=jnp.float32)
    head_rows = head_rows.astype(jnp.bfloat16)
    sums = []
    for i in range(chunks):
        partial = jnp.dot(
            head_rows, w_out[:, i * step : (i + 1) * step], preferred_element_type=jnp.float32
        )
        sums.append(scatter_sum(grid, partial))
    summed = jnp.concatenate(sums, axis=1)
    return (inputs + summed).astype(jnp.bfloat16)


def solution(mesh):
    placed = (
        P(("groups", "tp", "attn"), None),
        P(),
        P(None, ("tp", "attn")),
        P(None, ("tp", "attn")),
        P(None, ("tp", "attn")),
        P(("tp", "attn"), None),
        P(("groups", "tp", "attn"), None, None, None),
        P(("groups", "tp", "attn"), None, None, None),
        P(("groups", "tp", "attn"), None, None),
        P("groups"),
        P("groups"),
    )
    return jax.shard_map(
        on_device,
        mesh=mesh,
        in_specs=placed,
        out_specs=P(("groups", "tp", "attn"), None),
        check_vma=False,
    )
```

time: 142 us -> 130 us (0.915)
  Pallas kernels: 0 us -> 26.9 us
  other arithmetic: 27.6 us -> 6.2 us
  local copies, waits for them, and re-layouts: 30.1 us -> 9.37 us
  matrix products: 20.5 us -> 6.03 us
  waiting for transfers between devices: 31 us -> 45.1 us
  starting transfers between devices: 31.9 us -> 35.6 us
    pallas_call x0 -> x3, Pallas kernels: none -> 26.9 us  [the longest x1 19.3 us: attend(): pl.pallas_call(functools.partial(attend_kernel, 4, per_query, per_key), i...]
    dot_general x5 -> x0, matrix products: 14.5 us -> none  [the longest x1 4.41 us: on_device(): outbound = jnp.dot(route_in, projected, preferred_element_type=jnp.float32)]
    concatenate x2 -> x1, other arithmetic: 12.9 us -> 0.08 us  [on_device(): cosine = jnp.concatenate([cosine_part, cosine_part], axis=1)]
    gather x2 -> x0, local copies, waits for them, and re-layouts: 10 us -> none  [the longest x1 5.05 us: on_device(): jnp.take(key_pages[0], page_table[0], axis=0)]
    all_to_all x1, waiting for transfers between devices: 2.17 us -> 10.6 us  [on_device(): lax.all_to_all(outbound, AXES, split_axis=0, concat_axis=0, tiled=True)]
    unnamed x33 -> x26, local copies, waits for them, and re-layouts: 16.2 us -> 7.88 us
    ppermute x20, waiting for transfers between devices: 18.9 us -> 24.6 us  [send(): return lax.ppermute(x, AXES, self.perm(far, near, core))]
    select_n x2 -> x0, other arithmetic: 4.43 us -> none  [the longest x1 3.75 us: on_device(): jnp.take(key_pages[0], page_table[0], axis=0)]
  transfers between devices with their start and end apart: 22 -> 22, of which waited for: 10 -> 11; matrix products, arithmetic and copies ran while one was open for 40% -> 5% of each run, Pallas kernels for 0% -> 3%
where the time goes in v2:
time: 130 us
  waiting for transfers between devices  45.1 us (35%)
  starting transfers between devices  35.6 us (27%)
  Pallas kernels  26.9 us (21%)
  local copies, waits for them, and re-layouts  9.37 us (7%)
  other arithmetic  6.2 us (5%)
  matrix products  6.03 us (5%)
    ppermute x20, starting transfers between devices, send(): return lax.ppermute(x, AXES, self.perm(far, near, core))  28.1 us
    ppermute x20, waiting for transfers between devices, send(): return lax.ppermute(x, AXES, self.perm(far, near, core))  24.6 us
    pallas_call x1, Pallas kernels, attend(): pl.pallas_call(functools.partial(attend_kernel, 4, per_query, per_key), i...  19.3 us
    all_to_all x1, waiting for transfers between devices, on_device(): lax.all_to_all(outbound, AXES, split_axis=0, concat_axis=0, tiled=True)  10.6 us
    all_to_all x1, waiting for transfers between devices, on_device(): lax.all_to_all(attended, AXES, split_axis=0, concat_axis=0, tiled=True)  9.92 us
    unnamed x26, local copies, waits for them, and re-layouts  7.88 us
    pallas_call x2, Pallas kernels, project(): pl.pallas_call(functools.partial(project_kernel, first, last), grid=(step...  7.59 us
    dot_general x2, matrix products, on_device(): jnp.dot(head_rows, w_out[:, i * step:(i + 1) * step], preferred_element_t...  5.81 us
  transfers between devices with their start and end apart: 22, of which 11 were waited for; matrix products, arithmetic and copies ran while one was open for 5% of the time, Pallas kernels for 3%

profile of v2, /device:TPU:0, one launch (start us, length us, event | category | flops | bytes accessed | tf_op | source)
XLA Modules:
  0.0 129.6 jit_solution(4201064122156769741)
XLA Ops:
  2.9 5.1 %collective-permute-start.7 = (bf16[8,4096]{1,0:T(8,128)(2,1)S(1)}, bf16[8,4096]{1,0:T(8,128)(2,1)S(1)}, u32[]{:S(2)}, u32[]{:S(2)}) collective-permute-start(bf16[8,4096]{1,0:T(8,128)(2,1)S(1)} %get-tuple-element.17), channel_id=1, source_target_pairs={{0,12},{1,13},{2,14},{3,15},{4,0},{5,1},{6,2},{7,3},{8,4},{9,5},{1... | collective-permute-start | bytes 196616 | tf_op jit(solution)/shard_map/ppermute | solution.py:40
  8.4 2.5 %collective-permute-start.1 = (bf16[8,4096]{1,0:T(8,128)(2,1)}, bf16[8,4096]{1,0:T(8,128)(2,1)S(1)}, u32[]{:S(2)}, u32[]{:S(2)}) collective-permute-start(bf16[8,4096]{1,0:T(8,128)(2,1)} %get-tuple-element.20), channel_id=1, source_target_pairs={{0,8},{1,9},{2,10},{3,11},{4,12},{5,13},{6,14},{7,15},{8,0},{9,1},... | collective-permute-start | bytes 196616 | tf_op jit(solution)/shard_map/ppermute | solution.py:40
  10.9 2.0 %collective-permute-start = (bf16[8,4096]{1,0:T(8,128)(2,1)}, bf16[8,4096]{1,0:T(8,128)(2,1)S(1)}, u32[]{:S(2)}, u32[]{:S(2)}) collective-permute-start(bf16[8,4096]{1,0:T(8,128)(2,1)} %get-tuple-element.20), channel_id=1, source_target_pairs={{0,4},{1,5},{2,6},{3,7},{4,8},{5,9},{6,10},{7,11},{8,12},{9,13},{1... | collective-permute-start | bytes 196616 | tf_op jit(solution)/shard_map/ppermute | solution.py:40
  13.8 5.4 %collective-permute-start.5 = (bf16[8,4096]{1,0:T(8,128)(2,1)S(1)}, bf16[8,4096]{1,0:T(8,128)(2,1)S(1)}, u32[]{:S(2)}, u32[]{:S(2)}) collective-permute-start(bf16[8,4096]{1,0:T(8,128)(2,1)S(1)} %get-tuple-element.17), channel_id=1, source_target_pairs={{0,4},{1,5},{2,6},{3,7},{4,8},{5,9},{6,10},{7,11},{8,12},{9,13},{1... | collective-permute-start | bytes 196616 | tf_op jit(solution)/shard_map/ppermute | solution.py:40
  20.2 1.6 %collective-permute-start.3 = (bf16[32,4096]{1,0:T(8,128)(2,1)S(1)}, bf16[32,4096]{1,0:T(8,128)(2,1)S(1)}, u32[]{:S(2)}, u32[]{:S(2)}) collective-permute-start(bf16[32,4096]{1,0:T(8,128)(2,1)S(1)} %pad_maximum_fusion), channel_id=1, source_target_pairs={{0,2},{1,3},{2,0},{3,1},{4,6},{5,7},{6,4},{7,5},{8,10},{9,11},{10,... | collective-permute-start | bytes 786440 | tf_op jit(solution)/shard_map/ppermute | solution.py:40
  22.8 10.3 %collective-permute-done.8 = bf16[32,4096]{1,0:T(8,128)(2,1)S(1)} collective-permute-done((bf16[32,4096]{1,0:T(8,128)(2,1)S(1)}, bf16[32,4096]{1,0:T(8,128)(2,1)S(1)}, u32[]{:S(2)}, u32[]{:S(2)}) %collective-permute-start.8) | collective-permute-done | bytes 262176 | tf_op jit(solution)/shard_map/ppermute | solution.py:40
  35.2 3.4 %copy-done = bf16[8192,512]{1,0:T(8,128)(2,1)S(1)} copy-done((bf16[8192,512]{1,0:T(8,128)(2,1)S(1)}, bf16[8192,512]{1,0:T(8,128)(2,1)}, u32[]{:S(2)}) %copy-start) | copy-done | bytes 8388632
  38.6 3.5 %project.2.refs_0_ = f32[128,640]{1,0:T(8,128)S(1)} custom-call(bf16[64,4096]{1,0:T(8,128)(2,1)S(1)} %constant_dynamic-update-slice_fusion.5.xa, bf16[64,4096]{1,0:T(8,128)(2,1)} %collective-permute-done.9.xb, bf16[8192,512]{1,0:T(8,128)(2,1)S(1)} %copy-done, bf16[64,8192]{1,0:T(8,128)(2,1)S(1)} %bitcast.41, bf16[64,8192]{1,0:T(8,128)(2,1)S(1)} %bitcast.43), custom_call_target="tpu_custom_call" | custom-call | flops 671088640 | bytes 5242880 | tf_op jit(solution)/shard_map/project/pallas_call | solution.py:144
  42.2 4.0 %project.3 = bf16[256,640]{1,0:T(8,128)(2,1)} custom-call(bf16[64,4096]{1,0:T(8,128)(2,1)S(1)} %constant_dynamic-update-slice_fusion.xa, bf16[64,4096]{1,0:T(8,128)(2,1)} %collective-permute-done.4.xb, bf16[8192,512]{1,0:T(8,128)(2,1)S(1)} %copy-done.1, bf16[64,8192]{1,0:T(8,128)(2,1)S(1)} %bitcast.42, bf16[64,8192]{1,0:T(8,128)(2,1)S(1)} %bitcast.44, ...), custom_call_target="tpu_custom_call" | custom-call | flops 671088640 | bytes 5242880 | tf_op jit(solution)/shard_map/project/pallas_call | solution.py:144
  46.3 3.9 %all-to-all-start = ((bf16[16,16,640]{2,1,0:T(8,128)(2,1)}), bf16[16,16,640]{2,1,0:T(8,128)(2,1)S(1)}, u32[]{:S(2)}, u32[]{:S(2)}) async-start(bf16[16,16,640]{2,1,0:T(8,128)(2,1)} %bitcast.34), calls=%async_computation | async-start | bytes 655360 | tf_op jit(solution)/shard_map/all_to_all | solution.py:398
  50.7 10.6 %all-to-all-done.inbound = bf16[16,16,640]{2,1,0:T(8,128)(2,1)S(1)} async-done(((bf16[16,16,640]{2,1,0:T(8,128)(2,1)}), bf16[16,16,640]{2,1,0:T(8,128)(2,1)S(1)}, u32[]{:S(2)}, u32[]{:S(2)}) %all-to-all-start) | async-done | bytes 327712 | tf_op jit(solution)/shard_map/all_to_all | solution.py:398
  61.3 2.2 %copy-done.4 = bf16[1,64,32,1024]{3,2,1,0:T(8,128)(2,1)S(1)} copy-done((bf16[1,64,32,1024]{3,2,1,0:T(8,128)(2,1)S(1)}, bf16[1,64,32,1024]{3,2,1,0:T(8,128)(2,1)}, u32[]{:S(2)}) %copy-start.4) | copy-done | bytes 4194328
  63.5 2.2 %copy-done.5 = bf16[1,64,32,1024]{3,2,1,0:T(8,128)(2,1)S(1)} copy-done((bf16[1,64,32,1024]{3,2,1,0:T(8,128)(2,1)S(1)}, bf16[1,64,32,1024]{3,2,1,0:T(8,128)(2,1)}, u32[]{:S(2)}) %copy-start.5) | copy-done | bytes 4194328
  65.7 19.3 %attend.1 = bf16[16,16,512]{2,1,0:T(8,128)(2,1)} custom-call(s32[16,4]{1,0:T(8,128)S(1)} %copy.15.table, s32[16]{0:T(128)S(1)} %select_reduce_fusion.2.lengths, bf16[16,16,640]{2,1,0:T(8,128)(2,1)S(1)} %all-to-all-done.inbound, f32[16,128]{1,0:T(8,128)S(1)} %get-tuple-element.26.cosine, f32[16,128]{1,0:T(8,128)S(1)} %get-tuple-element.27.sine, ...), custom_call_target="tpu_custom_call" | custom-call | flops 134217728 | bytes 8388608 | tf_op jit(solution)/shard_map/attend/pallas_call | solution.py:310
  85.1 3.5 %all-to-all-start.1 = ((bf16[16,16,512]{2,1,0:T(8,128)(2,1)}), bf16[16,16,512]{2,1,0:T(8,128)(2,1)S(1)}, u32[]{:S(2)}, u32[]{:S(2)}) async-start(bf16[16,16,512]{2,1,0:T(8,128)(2,1)} %attend.1), calls=%async_computation.1 | async-start | bytes 524288 | tf_op jit(solution)/shard_map/all_to_all | solution.py:410
  88.7 9.9 %all-to-all-done.1 = bf16[16,16,512]{2,1,0:T(8,128)(2,1)S(1)} async-done(((bf16[16,16,512]{2,1,0:T(8,128)(2,1)}), bf16[16,16,512]{2,1,0:T(8,128)(2,1)S(1)}, u32[]{:S(2)}, u32[]{:S(2)}) %all-to-all-start.1) | async-done | bytes 262176 | tf_op jit(solution)/shard_map/all_to_all | solution.py:410
  98.8 2.9 %fusion = f32[128,4096]{1,0:T(8,128)S(1)} fusion(bf16[128,512]{1,0:T(8,128)(2,1)S(1)} %convolution_convert_fusion, bf16[512,8192]{1,0:T(8,128)(2,1)} %param.16), kind=kOutput, calls=%fused_computation | convolution fusion | flops 536870912 | bytes 6422528 | tf_op jit(solution)/shard_map/dot_general | solution.py:416
  101.9 2.9 %fusion.2 = f32[128,4096]{1,0:T(8,128)S(1)} fusion(bf16[128,512]{1,0:T(8,128)(2,1)S(1)} %convolution_convert_fusion, bf16[512,8192]{1,0:T(8,128)(2,1)} %param.16), kind=kOutput, calls=%fused_computation.2 | convolution fusion | flops 536870912 | bytes 6422528 | tf_op jit(solution)/shard_map/dot_general | solution.py:416
  105.7 1.3 collective-permute-done.10
  107.9 6.9 %collective-permute-done.16 = bf16[32,4096]{1,0:T(8,128)(2,1)S(1)} collective-permute-done((bf16[32,4096]{1,0:T(8,128)(2,1)S(1)}, bf16[32,4096]{1,0:T(8,128)(2,1)S(1)}, u32[]{:S(2)}, u32[]{:S(2)}) %collective-permute-start.16) | collective-permute-done | bytes 262176 | tf_op jit(solution)/shard_map/ppermute | solution.py:40
  115.1 3.7 %collective-permute-start.19 = (bf16[8,4096]{1,0:T(8,128)(2,1)S(1)}, bf16[8,4096]{1,0:T(8,128)(2,1)S(1)}, u32[]{:S(2)}, u32[]{:S(2)}) collective-permute-start(bf16[8,4096]{1,0:T(8,128)(2,1)S(1)} %get-tuple-element.15), channel_id=1, source_target_pairs={{0,12},{1,13},{2,14},{3,15},{4,0},{5,1},{6,2},{7,3},{8,4},{9,5},{1... | collective-permute-start | bytes 196616 | tf_op jit(solution)/shard_map/ppermute | solution.py:40
  120.3 3.2 %collective-permute-start.14 = (bf16[8,4096]{1,0:T(8,128)(2,1)S(1)}, bf16[8,4096]{1,0:T(8,128)(2,1)S(1)}, u32[]{:S(2)}, u32[]{:S(2)}) collective-permute-start(bf16[8,4096]{1,0:T(8,128)(2,1)S(1)} %get-tuple-element.12), channel_id=1, source_target_pairs={{0,12},{1,13},{2,14},{3,15},{4,0},{5,1},{6,2},{7,3},{8,4},{9,5},{1... | collective-permute-start | bytes 196616 | tf_op jit(solution)/shard_map/ppermute | solution.py:40
  124.7 1.4 %collective-permute-done.12 = bf16[8,4096]{1,0:T(8,128)(2,1)S(1)} collective-permute-done((bf16[8,4096]{1,0:T(8,128)(2,1)S(1)}, bf16[8,4096]{1,0:T(8,128)(2,1)S(1)}, u32[]{:S(2)}, u32[]{:S(2)}) %collective-permute-start.12) | collective-permute-done | bytes 65568 | tf_op jit(solution)/shard_map/ppermute | solution.py:40
  126.1 2.7 %collective-permute-done.13 = bf16[8,4096]{1,0:T(8,128)(2,1)S(1)} collective-permute-done((bf16[8,4096]{1,0:T(8,128)(2,1)S(1)}, bf16[8,4096]{1,0:T(8,128)(2,1)S(1)}, u32[]{:S(2)}, u32[]{:S(2)}) %collective-permute-start.13) | collective-permute-done | bytes 65568 | tf_op jit(solution)/shard_map/ppermute | solution.py:40
  (90 shorter events, 14.8 us)
Async XLA Ops:
  0.0 35.2 %copy-start.3 = (bf16[8192,64]{0,1:T(8,128)(2,1)S(1)}, bf16[8192,64]{0,1:T(8,128)(2,1)}, u32[]{:S(2)}) copy-start(bf16[8192,64]{0,1:T(8,128)(2,1)} %param.15) | copy-start | bytes 3145732
  0.0 35.2 %copy-start.2 = (bf16[8192,64]{0,1:T(8,128)(2,1)S(1)}, bf16[8192,64]{0,1:T(8,128)(2,1)}, u32[]{:S(2)}) copy-start(bf16[8192,64]{0,1:T(8,128)(2,1)} %param.14) | copy-start | bytes 3145732
  2.9 18.9 %collective-permute-start.7 = (bf16[8,4096]{1,0:T(8,128)(2,1)S(1)}, bf16[8,4096]{1,0:T(8,128)(2,1)S(1)}, u32[]{:S(2)}, u32[]{:S(2)}) collective-permute-start(bf16[8,4096]{1,0:T(8,128)(2,1)S(1)} %get-tuple-element.17), channel_id=1, source_target_pairs={{0,12},{1,13},{2,14},{3,15},{4,0},{5,1},{6,2},{7,3},{8,4},{9,5},{1... | collective-permute-start | bytes 196616 | tf_op jit(solution)/shard_map/ppermute | solution.py:40
  8.0 13.9 %collective-permute-start.6 = (bf16[8,4096]{1,0:T(8,128)(2,1)S(1)}, bf16[8,4096]{1,0:T(8,128)(2,1)S(1)}, u32[]{:S(2)}, u32[]{:S(2)}) collective-permute-start(bf16[8,4096]{1,0:T(8,128)(2,1)S(1)} %get-tuple-element.17), channel_id=1, source_target_pairs={{0,8},{1,9},{2,10},{3,11},{4,12},{5,13},{6,14},{7,15},{8,0},{9,1},... | collective-permute-start | bytes 196616 | tf_op jit(solution)/shard_map/ppermute | solution.py:40
  8.0 5.9 %collective-permute-start.2 = (bf16[8,4096]{1,0:T(8,128)(2,1)}, bf16[8,4096]{1,0:T(8,128)(2,1)S(1)}, u32[]{:S(2)}, u32[]{:S(2)}) collective-permute-start(bf16[8,4096]{1,0:T(8,128)(2,1)} %get-tuple-element.20), channel_id=1, source_target_pairs={{0,12},{1,13},{2,14},{3,15},{4,0},{5,1},{6,2},{7,3},{8,4},{9,5},{1... | collective-permute-start | bytes 196616 | tf_op jit(solution)/shard_map/ppermute | solution.py:40
  8.4 10.9 %collective-permute-start.1 = (bf16[8,4096]{1,0:T(8,128)(2,1)}, bf16[8,4096]{1,0:T(8,128)(2,1)S(1)}, u32[]{:S(2)}, u32[]{:S(2)}) collective-permute-start(bf16[8,4096]{1,0:T(8,128)(2,1)} %get-tuple-element.20), channel_id=1, source_target_pairs={{0,8},{1,9},{2,10},{3,11},{4,12},{5,13},{6,14},{7,15},{8,0},{9,1},... | collective-permute-start | bytes 196616 | tf_op jit(solution)/shard_map/ppermute | solution.py:40
  10.9 8.5 %collective-permute-start = (bf16[8,4096]{1,0:T(8,128)(2,1)}, bf16[8,4096]{1,0:T(8,128)(2,1)S(1)}, u32[]{:S(2)}, u32[]{:S(2)}) collective-permute-start(bf16[8,4096]{1,0:T(8,128)(2,1)} %get-tuple-element.20), channel_id=1, source_target_pairs={{0,4},{1,5},{2,6},{3,7},{4,8},{5,9},{6,10},{7,11},{8,12},{9,13},{1... | collective-permute-start | bytes 196616 | tf_op jit(solution)/shard_map/ppermute | solution.py:40
  13.8 8.0 %collective-permute-start.5 = (bf16[8,4096]{1,0:T(8,128)(2,1)S(1)}, bf16[8,4096]{1,0:T(8,128)(2,1)S(1)}, u32[]{:S(2)}, u32[]{:S(2)}) collective-permute-start(bf16[8,4096]{1,0:T(8,128)(2,1)S(1)} %get-tuple-element.17), channel_id=1, source_target_pairs={{0,4},{1,5},{2,6},{3,7},{4,8},{5,9},{6,10},{7,11},{8,12},{9,13},{1... | collective-permute-start | bytes 196616 | tf_op jit(solution)/shard_map/ppermute | solution.py:40
  20.2 12.9 %collective-permute-start.3 = (bf16[32,4096]{1,0:T(8,128)(2,1)S(1)}, bf16[32,4096]{1,0:T(8,128)(2,1)S(1)}, u32[]{:S(2)}, u32[]{:S(2)}) collective-permute-start(bf16[32,4096]{1,0:T(8,128)(2,1)S(1)} %pad_maximum_fusion), channel_id=1, source_target_pairs={{0,2},{1,3},{2,0},{3,1},{4,6},{5,7},{6,4},{7,5},{8,10},{9,11},{10,... | collective-permute-start | bytes 786440 | tf_op jit(solution)/shard_map/ppermute | solution.py:40
  21.9 11.2 %collective-permute-start.8 = (bf16[32,4096]{1,0:T(8,128)(2,1)S(1)}, bf16[32,4096]{1,0:T(8,128)(2,1)S(1)}, u32[]{:S(2)}, u32[]{:S(2)}) collective-permute-start(bf16[32,4096]{1,0:T(8,128)(2,1)S(1)} %pad_maximum_fusion.1), channel_id=1, source_target_pairs={{0,2},{1,3},{2,0},{3,1},{4,6},{5,7},{6,4},{7,5},{8,10},{9,11},{10,... | collective-permute-start | bytes 786440 | tf_op jit(solution)/shard_map/ppermute | solution.py:40
  33.1 2.1 %collective-permute-start.9 = (bf16[64,4096]{1,0:T(8,128)(2,1)S(1)}, bf16[64,4096]{1,0:T(8,128)(2,1)}, u32[]{:S(2)}, u32[]{:S(2)}) collective-permute-start(bf16[64,4096]{1,0:T(8,128)(2,1)S(1)} %constant_dynamic-update-slice_fusion.5.xa), channel_id=1, source_target_pairs={{0,1},{1,0},{2,3},{3,2},{4,5},{5,4},{6,7},{7,6},{8,9},{9,8},{10,11... | collective-permute-start | bytes 1572872 | tf_op jit(solution)/shard_map/ppermute | solution.py:40
  33.2 9.0 %collective-permute-start.4 = (bf16[64,4096]{1,0:T(8,128)(2,1)S(1)}, bf16[64,4096]{1,0:T(8,128)(2,1)}, u32[]{:S(2)}, u32[]{:S(2)}) collective-permute-start(bf16[64,4096]{1,0:T(8,128)(2,1)S(1)} %constant_dynamic-update-slice_fusion.xa), channel_id=1, source_target_pairs={{0,1},{1,0},{2,3},{3,2},{4,5},{5,4},{6,7},{7,6},{8,9},{9,8},{10,11... | collective-permute-start | bytes 1572872 | tf_op jit(solution)/shard_map/ppermute | solution.py:40
  46.3 15.1 %all-to-all-start = ((bf16[16,16,640]{2,1,0:T(8,128)(2,1)}), bf16[16,16,640]{2,1,0:T(8,128)(2,1)S(1)}, u32[]{:S(2)}, u32[]{:S(2)}) async-start(bf16[16,16,640]{2,1,0:T(8,128)(2,1)} %bitcast.34), calls=%async_computation | async-start | bytes 655360 | tf_op jit(solution)/shard_map/all_to_all | solution.py:398
  85.1 13.6 %all-to-all-start.1 = ((bf16[16,16,512]{2,1,0:T(8,128)(2,1)}), bf16[16,16,512]{2,1,0:T(8,128)(2,1)S(1)}, u32[]{:S(2)}, u32[]{:S(2)}) async-start(bf16[16,16,512]{2,1,0:T(8,128)(2,1)} %attend.1), calls=%async_computation.1 | async-start | bytes 524288 | tf_op jit(solution)/shard_map/all_to_all | solution.py:410
  101.8 3.6 %collective-permute-start.15 = (bf16[64,4096]{1,0:T(8,128)(2,1)S(1)}, bf16[64,4096]{1,0:T(8,128)(2,1)S(1)}, u32[]{:S(2)}, u32[]{:S(2)}) collective-permute-start(bf16[64,4096]{1,0:T(8,128)(2,1)S(1)} %slice.132), channel_id=1, source_target_pairs={{0,1},{1,0},{2,3},{3,2},{4,5},{5,4},{6,7},{7,6},{8,9},{9,8},{10,11... | collective-permute-start | bytes 1572872 | tf_op jit(solution)/shard_map/ppermute | solution.py:40
  104.9 2.1 %collective-permute-start.10 = (bf16[64,4096]{1,0:T(8,128)(2,1)S(1)}, bf16[64,4096]{1,0:T(8,128)(2,1)S(1)}, u32[]{:S(2)}, u32[]{:S(2)}) collective-permute-start(bf16[64,4096]{1,0:T(8,128)(2,1)S(1)} %slice.133), channel_id=1, source_target_pairs={{0,1},{1,0},{2,3},{3,2},{4,5},{5,4},{6,7},{7,6},{8,9},{9,8},{10,11... | collective-permute-start | bytes 1572872 | tf_op jit(solution)/shard_map/ppermute | solution.py:40
  105.6 9.2 %collective-permute-start.16 = (bf16[32,4096]{1,0:T(8,128)(2,1)S(1)}, bf16[32,4096]{1,0:T(8,128)(2,1)S(1)}, u32[]{:S(2)}, u32[]{:S(2)}) collective-permute-start(bf16[32,4096]{1,0:T(8,128)(2,1)S(1)} %slice.134), channel_id=1, source_target_pairs={{0,2},{1,3},{2,0},{3,1},{4,6},{5,7},{6,4},{7,5},{8,10},{9,11},{10,... | collective-permute-start | bytes 786440 | tf_op jit(solution)/shard_map/ppermute | solution.py:40
  107.1 12.4 %collective-permute-start.11 = (bf16[32,4096]{1,0:T(8,128)(2,1)S(1)}, bf16[32,4096]{1,0:T(8,128)(2,1)S(1)}, u32[]{:S(2)}, u32[]{:S(2)}) collective-permute-start(bf16[32,4096]{1,0:T(8,128)(2,1)S(1)} %slice.135), channel_id=1, source_target_pairs={{0,2},{1,3},{2,0},{3,1},{4,6},{5,7},{6,4},{7,5},{8,10},{9,11},{10,... | collective-permute-start | bytes 786440 | tf_op jit(solution)/shard_map/ppermute | solution.py:40
  114.9 8.6 %collective-permute-start.17 = (bf16[8,4096]{1,0:T(8,128)(2,1)S(1)}, bf16[8,4096]{1,0:T(8,128)(2,1)S(1)}, u32[]{:S(2)}, u32[]{:S(2)}) collective-permute-start(bf16[8,4096]{1,0:T(8,128)(2,1)S(1)} %get-tuple-element.14), channel_id=1, source_target_pairs={{0,4},{1,5},{2,6},{3,7},{4,8},{5,9},{6,10},{7,11},{8,12},{9,13},{1... | collective-permute-start | bytes 196616 | tf_op jit(solution)/shard_map/ppermute | solution.py:40
  115.1 8.8 %collective-permute-start.19 = (bf16[8,4096]{1,0:T(8,128)(2,1)S(1)}, bf16[8,4096]{1,0:T(8,128)(2,1)S(1)}, u32[]{:S(2)}, u32[]{:S(2)}) collective-permute-start(bf16[8,4096]{1,0:T(8,128)(2,1)S(1)} %get-tuple-element.15), channel_id=1, source_target_pairs={{0,12},{1,13},{2,14},{3,15},{4,0},{5,1},{6,2},{7,3},{8,4},{9,5},{1... | collective-permute-start | bytes 196616 | tf_op jit(solution)/shard_map/ppermute | solution.py:40
  118.8 5.9 %collective-permute-start.18 = (bf16[8,4096]{1,0:T(8,128)(2,1)S(1)}, bf16[8,4096]{1,0:T(8,128)(2,1)S(1)}, u32[]{:S(2)}, u32[]{:S(2)}) collective-permute-start(bf16[8,4096]{1,0:T(8,128)(2,1)S(1)} %get-tuple-element.16), channel_id=1, source_target_pairs={{0,8},{1,9},{2,10},{3,11},{4,12},{5,13},{6,14},{7,15},{8,0},{9,1},... | collective-permute-start | bytes 196616 | tf_op jit(solution)/shard_map/ppermute | solution.py:40
  119.6 6.5 %collective-permute-start.12 = (bf16[8,4096]{1,0:T(8,128)(2,1)S(1)}, bf16[8,4096]{1,0:T(8,128)(2,1)S(1)}, u32[]{:S(2)}, u32[]{:S(2)}) collective-permute-start(bf16[8,4096]{1,0:T(8,128)(2,1)S(1)} %get-tuple-element.11), channel_id=1, source_target_pairs={{0,4},{1,5},{2,6},{3,7},{4,8},{5,9},{6,10},{7,11},{8,12},{9,13},{1... | collective-permute-start | bytes 196616 | tf_op jit(solution)/shard_map/ppermute | solution.py:40
  120.3 5.8 %collective-permute-start.14 = (bf16[8,4096]{1,0:T(8,128)(2,1)S(1)}, bf16[8,4096]{1,0:T(8,128)(2,1)S(1)}, u32[]{:S(2)}, u32[]{:S(2)}) collective-permute-start(bf16[8,4096]{1,0:T(8,128)(2,1)S(1)} %get-tuple-element.12), channel_id=1, source_target_pairs={{0,12},{1,13},{2,14},{3,15},{4,0},{5,1},{6,2},{7,3},{8,4},{9,5},{1... | collective-permute-start | bytes 196616 | tf_op jit(solution)/shard_map/ppermute | solution.py:40
  123.5 5.4 %collective-permute-start.13 = (bf16[8,4096]{1,0:T(8,128)(2,1)S(1)}, bf16[8,4096]{1,0:T(8,128)(2,1)S(1)}, u32[]{:S(2)}, u32[]{:S(2)}) collective-permute-start(bf16[8,4096]{1,0:T(8,128)(2,1)S(1)} %get-tuple-element.13), channel_id=1, source_target_pairs={{0,8},{1,9},{2,10},{3,11},{4,12},{5,13},{6,14},{7,15},{8,0},{9,1},... | collective-permute-start | bytes 196616 | tf_op jit(solution)/shard_map/ppermute | solution.py:40
  (8 other events, 84.9 us)

commit v3 on v2

--- a/solution.py
+++ b/solution.py
@@ -2,6 +2,7 @@
 
 import jax
 import jax.numpy as jnp
+import numpy as np
 from jax import lax
 from jax.experimental import pallas as pl
 from jax.experimental.pallas import tpu as pltpu
@@ -40,22 +41,23 @@
         return lax.ppermute(x, AXES, self.perm(far, near, core))
 
     def blocks(self, sign):
-        me = lax.axis_index(AXES)
-        c = me % self.core
-        n = (me // self.core) % self.near
-        f = me // (self.core * self.near)
-        places = []
-        for dc in range(self.core):
-            for dn in range(self.near):
-                for df in range(self.far):
-                    places.append(
-                        self.index(
-                            (f + sign * df) % self.far,
-                            (n + sign * dn) % self.near,
-                            (c + sign * dc) % self.core,
-                        )
+        rows = []
+        for f in range(self.far):
+            for n in range(self.near):
+                for c in range(self.core):
+                    rows.append(
+                        [
+                            self.index(
+                                (f + sign * df) % self.far,
+                                (n + sign * dn) % self.near,
+                                (c + sign * dc) % self.core,
+                            )
+                            for dc in range(self.core)
+                            for dn in range(self.near)
+                            for df in range(self.far)
+                        ]
                     )
-        return jnp.stack(places)
+        return jnp.asarray(np.array(rows, np.int32))[lax.axis_index(AXES)]
 
 
 def gather_rows(grid, x):
@@ -148,7 +150,7 @@
         out_specs=pl.BlockSpec(out.shape, whole),
         out_shape=out,
         scratch_shapes=[pltpu.VMEM((rows, row_width), jnp.float32)],
-        compiler_params=pltpu.CompilerParams(vmem_limit_bytes=24 * 2**20),
+        compiler_params=pltpu.CompilerParams(vmem_limit_bytes=56 * 2**20),
         cost_estimate=pl.CostEstimate(
             flops=2 * rows * width * row_width,
             bytes_accessed=2 * width * row_width,
@@ -159,7 +161,6 @@
 
 
 def attend_kernel(
-    batch,
     per_query,
     per_key,
     table,
@@ -173,50 +174,60 @@
     keys,
     values,
     query_rot,
-    key_own,
     value_own,
+    chance,
     mixed,
     key_sems,
     value_sems,
 ):
     owners, slots, _ = inbound.shape
     pages = table.shape[1]
-    page = key_pages.shape[1]
-    kv_heads = key_pages.shape[2] // HEAD
+    page, kv_width = key_pages.shape[1:]
+    kv_heads = kv_width // HEAD
     heads_dev = per_query // HEAD
     heads = owners * heads_dev
-    group = heads // kv_heads
+    pair = 2 * heads // kv_heads
+    pairs = kv_heads // 2
     span = pages * page
     pieces = owners // kv_heads
-
-    def fetch(slot, carry):
-        for j in range(pages):
-            number = table[slot, j]
-            rows = pl.ds(j * page, page)
-            pltpu.make_async_copy(
-                key_pages.at[number], keys.at[slot, rows], key_sems.at[slot]
-            ).start()
-            pltpu.make_async_copy(
-                value_pages.at[number], values.at[slot, rows], value_sems.at[slot]
-            ).start()
-        return carry
-
-    lax.fori_loop(0, slots, fetch, 0)
+    batches, held, _ = keys.shape
+    batch = slots // batches
+
+    def fetch(pool, place, sems):
+        def one(slot, carry):
+            for j in range(pages):
+                pltpu.make_async_copy(
+                    pool.at[table[slot, j]], place(slot, j * page), sems.at[slot // batch]
+                ).start()
+            return carry
+
+        lax.fori_loop(0, slots, one, 0)
+
+    def key_place(slot, row):
+        return keys.at[slot // batch, pl.ds((slot % batch) * span + row, page)]
+
+    def value_place(slot, row):
+        return values.at[slot, pl.ds(row, page)]
+
+    fetch(key_pages, key_place, key_sems)
+    fetch(value_pages, value_place, value_sems)
 
     cos = cosine[...]
     sin = sine[...]
 
     def turn(x):
-        turned = x * cos + pltpu.roll(x, HEAD // 2, 1) * sin
-        return turned.astype(jnp.bfloat16).astype(jnp.float32)
+        return (x * cos + pltpu.roll(x, HEAD // 2, 1) * sin).astype(jnp.bfloat16)
 
     for source in range(owners):
         for j in range(heads_dev):
+            x = inbound[source, :, j * HEAD : (j + 1) * HEAD].astype(jnp.float32)
+            x = turn(x).astype(jnp.float32)
             head = source * heads_dev + j
-            x = inbound[source, :, j * HEAD : (j + 1) * HEAD].astype(jnp.float32)
-            query_rot[head * slots : (head + 1) * slots, :] = turn(x)
-
-    lane = lax.broadcasted_iota(jnp.int32, (slots, HEAD), 1) // per_key
+            for b in range(batches):
+                rows = pl.ds(head % pair * batch, batch)
+                query_rot[head // pair, b, rows] = x[b * batch : (b + 1) * batch]
+
+    piece = lax.broadcasted_iota(jnp.int32, (slots, HEAD), 1) // per_key
     for g in range(kv_heads):
         key = jnp.zeros((slots, HEAD), jnp.float32)
         value = jnp.zeros((slots, HEAD), jnp.float32)
@@ -224,77 +235,84 @@
             tile = inbound[g * pieces + j, :, per_query : per_query + HEAD].astype(jnp.float32)
             shift = j * per_key
             back = (shift - per_key) % HEAD
-            key = jnp.where(lane == j, pltpu.roll(tile, shift, 1) if shift else tile, key)
-            value = jnp.where(lane == j, pltpu.roll(tile, back, 1) if back else tile, value)
-        key_own[g * slots : (g + 1) * slots, :] = turn(key)
-        value_own[g * slots : (g + 1) * slots, :] = value
+            key = jnp.where(piece == j, pltpu.roll(tile, shift, 1) if shift else tile, key)
+            value = jnp.where(piece == j, pltpu.roll(tile, back, 1) if back else tile, value)
+        for b in range(batches):
+            keys[b, batch * span :, g * HEAD : (g + 1) * HEAD] = turn(key)
+        value_own[g] = value
 
     scale = HEAD ** (-0.5)
-    position = lax.broadcasted_iota(jnp.int32, (heads, span), 1)
-    pair = 2 * group
-    upper = lax.broadcasted_iota(jnp.int32, (pair, HEAD), 0) < group
-    zero = jnp.zeros((pair, HEAD), jnp.bfloat16)
-
-    def some(step, carry):
-        places = [step * batch + b for b in range(batch)]
-        scored = []
-        for slot in places:
-            pltpu.make_async_copy(keys.at[slot], keys.at[slot], key_sems.at[slot]).wait()
-            rotated = query_rot[pl.ds(slot, heads, stride=slots), :]
-            low = rotated.astype(jnp.bfloat16)
-            parts = []
-            for p in range(kv_heads // 2):
-                mine = low[p * pair : (p + 1) * pair]
-                wide = jnp.concatenate(
-                    [jnp.where(upper, mine, zero), jnp.where(upper, zero, mine)], axis=1
-                )
-                parts.append(
-                    lax.dot_general(
-                        wide,
-                        keys[slot, :, p * 2 * HEAD : (p + 1) * 2 * HEAD],
-                        (((1,), (1,)), ((), ())),
-                        preferred_element_type=jnp.float32,
-                    )
-                )
-            own_key = key_own[pl.ds(slot, kv_heads, stride=slots), :]
-            product = rotated.reshape(kv_heads, group, HEAD) * own_key[:, None, :]
-            own = jnp.sum(product.reshape(heads, HEAD), axis=1, keepdims=True) * scale
-            scored.append((jnp.concatenate(parts, axis=0) * scale, own))
-        chances = []
-        for slot, (scores, own) in zip(places, scored):
-            valid = position < lengths[slot]
-            masked = jnp.where(valid, scores, -1e30)
-            top = jnp.maximum(jnp.max(masked, axis=1, keepdims=True), own)
+    columns = pair * batch
+    row = lax.broadcasted_iota(jnp.int32, (span, columns), 0)
+    place = lax.broadcasted_iota(jnp.int32, (span, columns), 1) % batch
+    own_row = lax.broadcasted_iota(jnp.int32, (slots, columns), 0)
+    own_place = lax.broadcasted_iota(jnp.int32, (slots, columns), 1) % batch
+    first = lax.broadcasted_iota(jnp.int32, (HEAD, columns), 1) < columns // 2
+    same = lax.broadcasted_iota(jnp.int32, (columns, columns), 0) == lax.broadcasted_iota(
+        jnp.int32, (columns, columns), 1
+    )
+
+    own_chances = {}
+    for b in range(batches):
+        whole = keys.at[b, pl.ds(0, batch * span)]
+        pltpu.make_async_copy(whole, whole, key_sems.at[b]).wait()
+        valid = row < lengths[b]
+        for p in range(pairs):
+            turned = query_rot[p, b].T.astype(jnp.bfloat16)
+            none = jnp.zeros_like(turned)
+            wide = jnp.concatenate(
+                [jnp.where(first, turned, none), jnp.where(first, none, turned)], axis=0
+            )
+            products = jnp.dot(
+                keys[b, :, p * 2 * HEAD : (p + 1) * 2 * HEAD],
+                wide,
+                preferred_element_type=jnp.float32,
+            )
+            scores = products[:span]
+            for s in range(1, batch):
+                scores = jnp.where(place == s, products[s * span : (s + 1) * span], scores)
+            own = jnp.where(own_row == own_place + b * batch, products[batch * span :], 0.0)
+            own = jnp.sum(own, axis=0, keepdims=True) * scale
+            masked = jnp.where(valid, scores * scale, -1e30)
+            top = jnp.maximum(jnp.max(masked, axis=0, keepdims=True), own)
             terms = jnp.where(valid, jnp.exp(masked - top), 0.0)
             own_term = jnp.exp(own - top)
-            total = jnp.sum(terms, axis=1, keepdims=True) + own_term
+            total = jnp.sum(terms, axis=0, keepdims=True) + own_term
+            chance[p, b] = (terms / total).T.astype(jnp.bfloat16).astype(jnp.float32)
             own_chance = (own_term / total).astype(jnp.bfloat16).astype(jnp.float32)
-            chances.append(((terms / total).astype(jnp.bfloat16), own_chance))
-        for slot, (chance, own_chance) in zip(places, chances):
-            pltpu.make_async_copy(values.at[slot], values.at[slot], value_sems.at[slot]).wait()
-            parts = []
-            for p in range(kv_heads // 2):
+            own_chances[p, b] = jnp.sum(
+                jnp.where(same, own_chance, 0.0), axis=1, keepdims=True
+            )
+
+    for b in range(batches):
+        whole = values.at[pl.ds(b * batch, batch)]
+        pltpu.make_async_copy(whole, whole, value_sems.at[b]).wait()
+        for s in range(batch):
+            for p in range(pairs):
+                mine = chance[p, b, pl.ds(s, pair, stride=batch)].astype(jnp.bfloat16)
                 both = jnp.dot(
-                    chance[p * pair : (p + 1) * pair],
-                    values[slot, :, p * 2 * HEAD : (p + 1) * 2 * HEAD],
+                    mine,
+                    values[b * batch + s, :, p * 2 * HEAD : (p + 1) * 2 * HEAD],
                     preferred_element_type=jnp.float32,
                 )
-                parts.append(both[:group, :HEAD])
-                parts.append(both[group:, HEAD:])
-            own_value = value_own[pl.ds(slot, kv_heads, stride=slots), :]
-            own_value = jnp.broadcast_to(own_value[:, None, :], (kv_heads, group, HEAD))
-            result = jnp.concatenate(parts, axis=0) + own_chance * own_value.reshape(heads, HEAD)
-            mixed[pl.ds(slot, heads, stride=slots), :] = result
-        return carry
-
-    lax.fori_loop(0, slots // batch, some, 0)
-
-    for target in range(owners):
-        for j in range(heads_dev):
-            head = target * heads_dev + j
-            out[target, :, j * HEAD : (j + 1) * HEAD] = mixed[
-                head * slots : (head + 1) * slots, :
-            ].astype(jnp.bfloat16)
+                result = jnp.concatenate(
+                    [both[: pair // 2, :HEAD], both[pair // 2 :, HEAD:]], axis=0
+                )
+                mixed[p, b, pl.ds(s, pair, stride=batch)] = result
+
+    for p in range(pairs):
+        for j in range(pair):
+            head = p * pair + j
+            g = head * kv_heads // heads
+            halves = []
+            for b in range(batches):
+                rows = slice(j * batch, (j + 1) * batch)
+                own_value = value_own[g, b * batch : (b + 1) * batch]
+                halves.append(mixed[p, b, rows] + own_chances[p, b][rows] * own_value)
+            column = head % heads_dev * HEAD
+            out[head // heads_dev, :, column : column + HEAD] = jnp.concatenate(
+                halves, axis=0
+            ).astype(jnp.bfloat16)
 
 
 def attend(inbound, lengths, table, cosine, sine, key_pages, value_pages, per_query, per_key):
@@ -303,30 +321,36 @@
     page, kv_width = key_pages.shape[1:]
     kv_heads = kv_width // HEAD
     heads = owners * (per_query // HEAD)
-    held = (slots, pages * page, kv_width)
+    span = pages * page
+    pair = 2 * heads // kv_heads
+    pairs = kv_heads // 2
+    batches = slots * pair // HEAD
+    batch = slots // batches
+    columns = pair * batch
+    lengths = jnp.tile(lengths.reshape(batches, 1, batch), (1, 1, pair))
     smem = pl.BlockSpec(memory_space=pltpu.SMEM)
     vmem = pl.BlockSpec(memory_space=pltpu.VMEM)
     hbm = pl.BlockSpec(memory_space=pl.ANY)
     return pl.pallas_call(
-        functools.partial(attend_kernel, 4, per_query, per_key),
-        in_specs=[smem, smem, vmem, vmem, vmem, hbm, hbm],
+        functools.partial(attend_kernel, per_query, per_key),
+        in_specs=[smem, vmem, vmem, vmem, vmem, hbm, hbm],
         out_specs=vmem,
         out_shape=jax.ShapeDtypeStruct((owners, slots, per_query), jnp.bfloat16),
         scratch_shapes=[
-            pltpu.VMEM(held, jnp.bfloat16),
-            pltpu.VMEM(held, jnp.bfloat16),
-            pltpu.VMEM((heads * slots, HEAD), jnp.float32),
-            pltpu.VMEM((kv_heads * slots, HEAD), jnp.float32),
-            pltpu.VMEM((kv_heads * slots, HEAD), jnp.float32),
-            pltpu.VMEM((heads * slots, HEAD), jnp.float32),
-            pltpu.SemaphoreType.DMA((slots,)),
-            pltpu.SemaphoreType.DMA((slots,)),
+            pltpu.VMEM((batches, batch * span + slots, kv_width), jnp.bfloat16),
+            pltpu.VMEM((slots, span, kv_width), jnp.bfloat16),
+            pltpu.VMEM((pairs, batches, columns, HEAD), jnp.float32),
+            pltpu.VMEM((kv_heads, slots, HEAD), jnp.float32),
+            pltpu.VMEM((pairs, batches, columns, span), jnp.float32),
+            pltpu.VMEM((pairs, batches, columns, HEAD), jnp.float32),
+            pltpu.SemaphoreType.DMA((batches,)),
+            pltpu.SemaphoreType.DMA((batches,)),
         ],
-        compiler_params=pltpu.CompilerParams(vmem_limit_bytes=24 * 2**20),
+        compiler_params=pltpu.CompilerParams(vmem_limit_bytes=56 * 2**20),
         cost_estimate=pl.CostEstimate(
-            flops=8 * slots * heads * pages * page * HEAD,
-            bytes_accessed=4 * slots * pages * page * kv_width,
-            transcendentals=slots * heads * pages * page,
+            flops=8 * slots * heads * span * HEAD,
+            bytes_accessed=4 * slots * span * kv_width,
+            transcendentals=slots * heads * span,
         ),
         name="attend",
     )(table, lengths, inbound, cosine, sine, key_pages, value_pages)

time: 130 us -> 113 us (0.87)
  Pallas kernels: 26.9 us -> 16.4 us
  local copies, waits for them, and re-layouts: 9.37 us -> 5.67 us
  waiting for transfers between devices: 45.1 us -> 42.1 us
    pallas_call x1, Pallas kernels: 19.3 us -> 6.12 us  [attend(): pl.pallas_call(functools.partial(attend_kernel, per_query, per_key), in_s...]
    unnamed x26 -> x22, local copies, waits for them, and re-layouts: 7.88 us -> 2.41 us
    pallas_call x2, Pallas kernels: 7.59 us -> 10.3 us  [project(): pl.pallas_call(functools.partial(project_kernel, first, last), grid=(step...]
    all_to_all x1, waiting for transfers between devices: 10.6 us -> 8.62 us  [on_device(): lax.all_to_all(outbound, AXES, split_axis=0, concat_axis=0, tiled=True)]
    ppermute x20, starting transfers between devices: 28.1 us -> 26.6 us  [send(): return lax.ppermute(x, AXES, self.perm(far, near, core))]
  transfers between devices with their start and end apart: 22 -> 22, of which waited for: 11 -> 11; matrix products, arithmetic and copies ran while one was open for 5% -> 9% of each run, Pallas kernels for 3% -> 4%
where the time goes in v3:
time: 113 us; the launch traced here: 112 us
  waiting for transfers between devices  42.1 us (37%)
  starting transfers between devices  34.8 us (31%)
  Pallas kernels  16.4 us (15%)
  other arithmetic  6.56 us (6%)
  matrix products  6.03 us (5%)
  local copies, waits for them, and re-layouts  5.67 us (5%)
    ppermute x20, starting transfers between devices, send(): return lax.ppermute(x, AXES, self.perm(far, near, core))  26.6 us
    ppermute x20, waiting for transfers between devices, send(): return lax.ppermute(x, AXES, self.perm(far, near, core))  23.6 us
    pallas_call x2, Pallas kernels, project(): pl.pallas_call(functools.partial(project_kernel, first, last), grid=(step...  10.3 us
    all_to_all x1, waiting for transfers between devices, on_device(): lax.all_to_all(attended, AXES, split_axis=0, concat_axis=0, tiled=True)  9.92 us
    all_to_all x1, waiting for transfers between devices, on_device(): lax.all_to_all(outbound, AXES, split_axis=0, concat_axis=0, tiled=True)  8.62 us
    pallas_call x1, Pallas kernels, attend(): pl.pallas_call(functools.partial(attend_kernel, per_query, per_key), in_s...  6.12 us
    dot_general x2, matrix products, on_device(): jnp.dot(head_rows, w_out[:, i * step:(i + 1) * step], preferred_element_t...  5.81 us
    all_to_all x1, starting transfers between devices, on_device(): lax.all_to_all(outbound, AXES, split_axis=0, concat_axis=0, tiled=True)  4.66 us
  transfers between devices with their start and end apart: 22, of which 11 were waited for; matrix products, arithmetic and copies ran while one was open for 9% of the time, Pallas kernels for 4%

profile of v3, /device:TPU:0, one launch (start us, length us, event | category | flops | bytes accessed | tf_op | source)
XLA Modules:
  0.0 112.0 jit_solution(7868561262023688324)
XLA Ops:
  0.0 1.1 fusion.4
  1.1 1.0 fusion.6
  2.1 5.1 %collective-permute-start.7 = (bf16[8,4096]{1,0:T(8,128)(2,1)S(1)}, bf16[8,4096]{1,0:T(8,128)(2,1)S(1)}, u32[]{:S(2)}, u32[]{:S(2)}) collective-permute-start(bf16[8,4096]{1,0:T(8,128)(2,1)S(1)} %get-tuple-element.17), channel_id=1, source_target_pairs={{0,12},{1,13},{2,14},{3,15},{4,0},{5,1},{6,2},{7,3},{8,4},{9,5},{1... | collective-permute-start | bytes 196616 | tf_op jit(solution)/shard_map/ppermute | solution.py:41
  7.7 2.5 %collective-permute-start.1 = (bf16[8,4096]{1,0:T(8,128)(2,1)S(1)}, bf16[8,4096]{1,0:T(8,128)(2,1)S(1)}, u32[]{:S(2)}, u32[]{:S(2)}) collective-permute-start(bf16[8,4096]{1,0:T(8,128)(2,1)S(1)} %get-tuple-element.20), channel_id=1, source_target_pairs={{0,8},{1,9},{2,10},{3,11},{4,12},{5,13},{6,14},{7,15},{8,0},{9,1},... | collective-permute-start | bytes 196616 | tf_op jit(solution)/shard_map/ppermute | solution.py:41
  10.2 2.0 %collective-permute-start = (bf16[8,4096]{1,0:T(8,128)(2,1)S(1)}, bf16[8,4096]{1,0:T(8,128)(2,1)S(1)}, u32[]{:S(2)}, u32[]{:S(2)}) collective-permute-start(bf16[8,4096]{1,0:T(8,128)(2,1)S(1)} %get-tuple-element.20), channel_id=1, source_target_pairs={{0,4},{1,5},{2,6},{3,7},{4,8},{5,9},{6,10},{7,11},{8,12},{9,13},{1... | collective-permute-start | bytes 196616 | tf_op jit(solution)/shard_map/ppermute | solution.py:41
  14.6 3.1 %collective-permute-start.5 = (bf16[8,4096]{1,0:T(8,128)(2,1)S(1)}, bf16[8,4096]{1,0:T(8,128)(2,1)S(1)}, u32[]{:S(2)}, u32[]{:S(2)}) collective-permute-start(bf16[8,4096]{1,0:T(8,128)(2,1)S(1)} %get-tuple-element.17), channel_id=1, source_target_pairs={{0,4},{1,5},{2,6},{3,7},{4,8},{5,9},{6,10},{7,11},{8,12},{9,13},{1... | collective-permute-start | bytes 196616 | tf_op jit(solution)/shard_map/ppermute | solution.py:41
  18.6 1.6 %collective-permute-start.3 = (bf16[32,4096]{1,0:T(8,128)(2,1)S(1)}, bf16[32,4096]{1,0:T(8,128)(2,1)S(1)}, u32[]{:S(2)}, u32[]{:S(2)}) collective-permute-start(bf16[32,4096]{1,0:T(8,128)(2,1)S(1)} %pad_maximum_fusion), channel_id=1, source_target_pairs={{0,2},{1,3},{2,0},{3,1},{4,6},{5,7},{6,4},{7,5},{8,10},{9,11},{10,... | collective-permute-start | bytes 786440 | tf_op jit(solution)/shard_map/ppermute | solution.py:41
  20.7 1.6 %collective-permute-start.8 = (bf16[32,4096]{1,0:T(8,128)(2,1)S(1)}, bf16[32,4096]{1,0:T(8,128)(2,1)S(1)}, u32[]{:S(2)}, u32[]{:S(2)}) collective-permute-start(bf16[32,4096]{1,0:T(8,128)(2,1)S(1)} %pad_maximum_fusion.1), channel_id=1, source_target_pairs={{0,2},{1,3},{2,0},{3,1},{4,6},{5,7},{6,4},{7,5},{8,10},{9,11},{10,... | collective-permute-start | bytes 786440 | tf_op jit(solution)/shard_map/ppermute | solution.py:41
  22.4 8.4 %collective-permute-done.8 = bf16[32,4096]{1,0:T(8,128)(2,1)S(1)} collective-permute-done((bf16[32,4096]{1,0:T(8,128)(2,1)S(1)}, bf16[32,4096]{1,0:T(8,128)(2,1)S(1)}, u32[]{:S(2)}, u32[]{:S(2)}) %collective-permute-start.8) | collective-permute-done | bytes 262176 | tf_op jit(solution)/shard_map/ppermute | solution.py:41
  33.7 4.9 %project.2.refs_0_ = f32[128,640]{1,0:T(8,128)} custom-call(bf16[64,4096]{1,0:T(8,128)(2,1)} %copy-done.3, bf16[64,4096]{1,0:T(8,128)(2,1)} %copy-done.4, bf16[8192,512]{1,0:T(8,128)(2,1)} %wq.3, bf16[64,8192]{1,0:T(8,128)(2,1)} %bitcast.15, bf16[64,8192]{1,0:T(8,128)(2,1)} %bitcast.17), custom_call_target="tpu_custom_call" | custom-call | flops 671088640 | bytes 5242880 | tf_op jit(solution)/shard_map/project/pallas_call | solution.py:146
  39.5 5.4 %project.3 = bf16[256,640]{1,0:T(8,128)(2,1)} custom-call(bf16[64,4096]{1,0:T(8,128)(2,1)} %copy-done.2, bf16[64,4096]{1,0:T(8,128)(2,1)} %copy-done.5, bf16[8192,512]{1,0:T(8,128)(2,1)} %wq.3, bf16[64,8192]{1,0:T(8,128)(2,1)} %bitcast.16, bf16[64,8192]{1,0:T(8,128)(2,1)} %bitcast.18, f32[128,640]{1,0:T(8,128)} %project.2.refs_0_, ...), custom_call_target="tpu_custom_call" | custom-call | flops 671088640 | bytes 5242880 | tf_op jit(solution)/shard_map/project/pallas_call | solution.py:146
  44.9 4.7 %all-to-all-start = ((bf16[16,16,640]{2,1,0:T(8,128)(2,1)}), bf16[16,16,640]{2,1,0:T(8,128)(2,1)S(1)}, u32[]{:S(2)}, u32[]{:S(2)}) async-start(bf16[16,16,640]{2,1,0:T(8,128)(2,1)} %bitcast.21), calls=%async_computation | async-start | bytes 655360 | tf_op jit(solution)/shard_map/all_to_all | solution.py:422
  52.0 8.6 %all-to-all-done.inbound = bf16[16,16,640]{2,1,0:T(8,128)(2,1)S(1)} async-done(((bf16[16,16,640]{2,1,0:T(8,128)(2,1)}), bf16[16,16,640]{2,1,0:T(8,128)(2,1)S(1)}, u32[]{:S(2)}, u32[]{:S(2)}) %all-to-all-start) | async-done | bytes 327712 | tf_op jit(solution)/shard_map/all_to_all | solution.py:422
  61.4 6.1 %attend.1 = bf16[16,16,512]{2,1,0:T(8,128)(2,1)} custom-call(s32[16,4]{1,0:T(8,128)} %copy.18.table, s32[2,1,128]{2,1,0:T(1,128)} %bitcast.23, bf16[16,16,640]{2,1,0:T(8,128)(2,1)} %copy-done, f32[16,128]{1,0:T(8,128)} %get-tuple-element.26.cosine, f32[16,128]{1,0:T(8,128)} %get-tuple-element.27.sine, bf16[64,32,1024]{2,1,0:T(8,128)(2,1)} %bitcast.19, ...), custom_call_target="tpu_custom_call" | custom-call | flops 134217728 | bytes 8388608 | tf_op jit(solution)/shard_map/attend/pallas_call | solution.py:334
  67.5 3.5 %all-to-all-start.1 = ((bf16[16,16,512]{2,1,0:T(8,128)(2,1)}), bf16[16,16,512]{2,1,0:T(8,128)(2,1)S(1)}, u32[]{:S(2)}, u32[]{:S(2)}) async-start(bf16[16,16,512]{2,1,0:T(8,128)(2,1)} %attend.1), calls=%async_computation.1 | async-start | bytes 524288 | tf_op jit(solution)/shard_map/all_to_all | solution.py:434
  71.1 9.9 %all-to-all-done.1 = bf16[16,16,512]{2,1,0:T(8,128)(2,1)S(1)} async-done(((bf16[16,16,512]{2,1,0:T(8,128)(2,1)}), bf16[16,16,512]{2,1,0:T(8,128)(2,1)S(1)}, u32[]{:S(2)}, u32[]{:S(2)}) %all-to-all-start.1) | async-done | bytes 262176 | tf_op jit(solution)/shard_map/all_to_all | solution.py:434
  81.3 2.9 %fusion = f32[128,4096]{1,0:T(8,128)S(1)} fusion(bf16[128,512]{1,0:T(8,128)(2,1)S(1)} %convolution_convert_fusion, bf16[512,8192]{1,0:T(8,128)(2,1)} %param.18), kind=kOutput, calls=%fused_computation | convolution fusion | flops 536870912 | bytes 6422528 | tf_op jit(solution)/shard_map/dot_general | solution.py:440
  84.3 2.9 %fusion.2 = f32[128,4096]{1,0:T(8,128)S(1)} fusion(bf16[128,512]{1,0:T(8,128)(2,1)S(1)} %convolution_convert_fusion, bf16[512,8192]{1,0:T(8,128)(2,1)} %param.18), kind=kOutput, calls=%fused_computation.2 | convolution fusion | flops 536870912 | bytes 6422528 | tf_op jit(solution)/shard_map/dot_general | solution.py:440
  88.1 1.3 %collective-permute-done.10 = bf16[64,4096]{1,0:T(8,128)(2,1)S(1)} collective-permute-done((bf16[64,4096]{1,0:T(8,128)(2,1)S(1)}, bf16[64,4096]{1,0:T(8,128)(2,1)S(1)}, u32[]{:S(2)}, u32[]{:S(2)}) %collective-permute-start.10) | collective-permute-done | bytes 524320 | tf_op jit(solution)/shard_map/ppermute | solution.py:41
  90.3 6.9 %collective-permute-done.16 = bf16[32,4096]{1,0:T(8,128)(2,1)S(1)} collective-permute-done((bf16[32,4096]{1,0:T(8,128)(2,1)S(1)}, bf16[32,4096]{1,0:T(8,128)(2,1)S(1)}, u32[]{:S(2)}, u32[]{:S(2)}) %collective-permute-start.16) | collective-permute-done | bytes 262176 | tf_op jit(solution)/shard_map/ppermute | solution.py:41
  97.5 3.7 %collective-permute-start.19 = (bf16[8,4096]{1,0:T(8,128)(2,1)S(1)}, bf16[8,4096]{1,0:T(8,128)(2,1)S(1)}, u32[]{:S(2)}, u32[]{:S(2)}) collective-permute-start(bf16[8,4096]{1,0:T(8,128)(2,1)S(1)} %get-tuple-element.15), channel_id=1, source_target_pairs={{0,12},{1,13},{2,14},{3,15},{4,0},{5,1},{6,2},{7,3},{8,4},{9,5},{1... | collective-permute-start | bytes 196616 | tf_op jit(solution)/shard_map/ppermute | solution.py:41
  102.7 3.2 %collective-permute-start.14 = (bf16[8,4096]{1,0:T(8,128)(2,1)S(1)}, bf16[8,4096]{1,0:T(8,128)(2,1)S(1)}, u32[]{:S(2)}, u32[]{:S(2)}) collective-permute-start(bf16[8,4096]{1,0:T(8,128)(2,1)S(1)} %get-tuple-element.12), channel_id=1, source_target_pairs={{0,12},{1,13},{2,14},{3,15},{4,0},{5,1},{6,2},{7,3},{8,4},{9,5},{1... | collective-permute-start | bytes 196616 | tf_op jit(solution)/shard_map/ppermute | solution.py:41
  107.1 1.4 %collective-permute-done.12 = bf16[8,4096]{1,0:T(8,128)(2,1)S(1)} collective-permute-done((bf16[8,4096]{1,0:T(8,128)(2,1)S(1)}, bf16[8,4096]{1,0:T(8,128)(2,1)S(1)}, u32[]{:S(2)}, u32[]{:S(2)}) %collective-permute-start.12) | collective-permute-done | bytes 65568 | tf_op jit(solution)/shard_map/ppermute | solution.py:41
  108.5 2.7 %collective-permute-done.13 = bf16[8,4096]{1,0:T(8,128)(2,1)S(1)} collective-permute-done((bf16[8,4096]{1,0:T(8,128)(2,1)S(1)}, bf16[8,4096]{1,0:T(8,128)(2,1)S(1)}, u32[]{:S(2)}, u32[]{:S(2)}) %collective-permute-start.13) | collective-permute-done | bytes 65568 | tf_op jit(solution)/shard_map/ppermute | solution.py:41
  (89 shorter events, 17.1 us)
Async XLA Ops:
  2.1 18.1 %collective-permute-start.7 = (bf16[8,4096]{1,0:T(8,128)(2,1)S(1)}, bf16[8,4096]{1,0:T(8,128)(2,1)S(1)}, u32[]{:S(2)}, u32[]{:S(2)}) collective-permute-start(bf16[8,4096]{1,0:T(8,128)(2,1)S(1)} %get-tuple-element.17), channel_id=1, source_target_pairs={{0,12},{1,13},{2,14},{3,15},{4,0},{5,1},{6,2},{7,3},{8,4},{9,5},{1... | collective-permute-start | bytes 196616 | tf_op jit(solution)/shard_map/ppermute | solution.py:41
  7.2 13.0 %collective-permute-start.6 = (bf16[8,4096]{1,0:T(8,128)(2,1)S(1)}, bf16[8,4096]{1,0:T(8,128)(2,1)S(1)}, u32[]{:S(2)}, u32[]{:S(2)}) collective-permute-start(bf16[8,4096]{1,0:T(8,128)(2,1)S(1)} %get-tuple-element.17), channel_id=1, source_target_pairs={{0,8},{1,9},{2,10},{3,11},{4,12},{5,13},{6,14},{7,15},{8,0},{9,1},... | collective-permute-start | bytes 196616 | tf_op jit(solution)/shard_map/ppermute | solution.py:41
  7.2 7.4 %collective-permute-start.2 = (bf16[8,4096]{1,0:T(8,128)(2,1)S(1)}, bf16[8,4096]{1,0:T(8,128)(2,1)S(1)}, u32[]{:S(2)}, u32[]{:S(2)}) collective-permute-start(bf16[8,4096]{1,0:T(8,128)(2,1)S(1)} %get-tuple-element.20), channel_id=1, source_target_pairs={{0,12},{1,13},{2,14},{3,15},{4,0},{5,1},{6,2},{7,3},{8,4},{9,5},{1... | collective-permute-start | bytes 196616 | tf_op jit(solution)/shard_map/ppermute | solution.py:41
  7.7 10.9 %collective-permute-start.1 = (bf16[8,4096]{1,0:T(8,128)(2,1)S(1)}, bf16[8,4096]{1,0:T(8,128)(2,1)S(1)}, u32[]{:S(2)}, u32[]{:S(2)}) collective-permute-start(bf16[8,4096]{1,0:T(8,128)(2,1)S(1)} %get-tuple-element.20), channel_id=1, source_target_pairs={{0,8},{1,9},{2,10},{3,11},{4,12},{5,13},{6,14},{7,15},{8,0},{9,1},... | collective-permute-start | bytes 196616 | tf_op jit(solution)/shard_map/ppermute | solution.py:41
  10.2 8.5 %collective-permute-start = (bf16[8,4096]{1,0:T(8,128)(2,1)S(1)}, bf16[8,4096]{1,0:T(8,128)(2,1)S(1)}, u32[]{:S(2)}, u32[]{:S(2)}) collective-permute-start(bf16[8,4096]{1,0:T(8,128)(2,1)S(1)} %get-tuple-element.20), channel_id=1, source_target_pairs={{0,4},{1,5},{2,6},{3,7},{4,8},{5,9},{6,10},{7,11},{8,12},{9,13},{1... | collective-permute-start | bytes 196616 | tf_op jit(solution)/shard_map/ppermute | solution.py:41
  14.6 6.1 %collective-permute-start.5 = (bf16[8,4096]{1,0:T(8,128)(2,1)S(1)}, bf16[8,4096]{1,0:T(8,128)(2,1)S(1)}, u32[]{:S(2)}, u32[]{:S(2)}) collective-permute-start(bf16[8,4096]{1,0:T(8,128)(2,1)S(1)} %get-tuple-element.17), channel_id=1, source_target_pairs={{0,4},{1,5},{2,6},{3,7},{4,8},{5,9},{6,10},{7,11},{8,12},{9,13},{1... | collective-permute-start | bytes 196616 | tf_op jit(solution)/shard_map/ppermute | solution.py:41
  18.6 12.3 %collective-permute-start.3 = (bf16[32,4096]{1,0:T(8,128)(2,1)S(1)}, bf16[32,4096]{1,0:T(8,128)(2,1)S(1)}, u32[]{:S(2)}, u32[]{:S(2)}) collective-permute-start(bf16[32,4096]{1,0:T(8,128)(2,1)S(1)} %pad_maximum_fusion), channel_id=1, source_target_pairs={{0,2},{1,3},{2,0},{3,1},{4,6},{5,7},{6,4},{7,5},{8,10},{9,11},{10,... | collective-permute-start | bytes 786440 | tf_op jit(solution)/shard_map/ppermute | solution.py:41
  20.7 10.1 %collective-permute-start.8 = (bf16[32,4096]{1,0:T(8,128)(2,1)S(1)}, bf16[32,4096]{1,0:T(8,128)(2,1)S(1)}, u32[]{:S(2)}, u32[]{:S(2)}) collective-permute-start(bf16[32,4096]{1,0:T(8,128)(2,1)S(1)} %pad_maximum_fusion.1), channel_id=1, source_target_pairs={{0,2},{1,3},{2,0},{3,1},{4,6},{5,7},{6,4},{7,5},{8,10},{9,11},{10,... | collective-permute-start | bytes 786440 | tf_op jit(solution)/shard_map/ppermute | solution.py:41
  30.8 2.1 %collective-permute-start.9 = (bf16[64,4096]{1,0:T(8,128)(2,1)S(1)}, bf16[64,4096]{1,0:T(8,128)(2,1)S(1)}, u32[]{:S(2)}, u32[]{:S(2)}) collective-permute-start(bf16[64,4096]{1,0:T(8,128)(2,1)S(1)} %constant_dynamic-update-slice_fusion.5.xa), channel_id=1, source_target_pairs={{0,1},{1,0},{2,3},{3,2},{4,5},{5,4},{6,7},{7,6},{8,9},{9,8},{10,11... | collective-permute-start | bytes 1572872 | tf_op jit(solution)/shard_map/ppermute | solution.py:41
  31.0 7.7 %collective-permute-start.4 = (bf16[64,4096]{1,0:T(8,128)(2,1)S(1)}, bf16[64,4096]{1,0:T(8,128)(2,1)S(1)}, u32[]{:S(2)}, u32[]{:S(2)}) collective-permute-start(bf16[64,4096]{1,0:T(8,128)(2,1)S(1)} %constant_dynamic-update-slice_fusion.xa), channel_id=1, source_target_pairs={{0,1},{1,0},{2,3},{3,2},{4,5},{5,4},{6,7},{7,6},{8,9},{9,8},{10,11... | collective-permute-start | bytes 1572872 | tf_op jit(solution)/shard_map/ppermute | solution.py:41
  38.6 11.2 %copy-start.6 = (s32[1,16,4]{1,2,0:T(4,128)S(1)}, s32[1,16,4]{1,2,0:T(4,128)}, u32[]{:S(2)}) copy-start(s32[1,16,4]{1,2,0:T(4,128)} %param.21) | copy-start | bytes 772
  44.9 15.8 %all-to-all-start = ((bf16[16,16,640]{2,1,0:T(8,128)(2,1)}), bf16[16,16,640]{2,1,0:T(8,128)(2,1)S(1)}, u32[]{:S(2)}, u32[]{:S(2)}) async-start(bf16[16,16,640]{2,1,0:T(8,128)(2,1)} %bitcast.21), calls=%async_computation | async-start | bytes 655360 | tf_op jit(solution)/shard_map/all_to_all | solution.py:422
  67.5 13.6 %all-to-all-start.1 = ((bf16[16,16,512]{2,1,0:T(8,128)(2,1)}), bf16[16,16,512]{2,1,0:T(8,128)(2,1)S(1)}, u32[]{:S(2)}, u32[]{:S(2)}) async-start(bf16[16,16,512]{2,1,0:T(8,128)(2,1)} %attend.1), calls=%async_computation.1 | async-start | bytes 524288 | tf_op jit(solution)/shard_map/all_to_all | solution.py:434
  84.3 3.6 %collective-permute-start.15 = (bf16[64,4096]{1,0:T(8,128)(2,1)S(1)}, bf16[64,4096]{1,0:T(8,128)(2,1)S(1)}, u32[]{:S(2)}, u32[]{:S(2)}) collective-permute-start(bf16[64,4096]{1,0:T(8,128)(2,1)S(1)} %slice.132), channel_id=1, source_target_pairs={{0,1},{1,0},{2,3},{3,2},{4,5},{5,4},{6,7},{7,6},{8,9},{9,8},{10,11... | collective-permute-start | bytes 1572872 | tf_op jit(solution)/shard_map/ppermute | solution.py:41
  87.3 2.1 %collective-permute-start.10 = (bf16[64,4096]{1,0:T(8,128)(2,1)S(1)}, bf16[64,4096]{1,0:T(8,128)(2,1)S(1)}, u32[]{:S(2)}, u32[]{:S(2)}) collective-permute-start(bf16[64,4096]{1,0:T(8,128)(2,1)S(1)} %slice.133), channel_id=1, source_target_pairs={{0,1},{1,0},{2,3},{3,2},{4,5},{5,4},{6,7},{7,6},{8,9},{9,8},{10,11... | collective-permute-start | bytes 1572872 | tf_op jit(solution)/shard_map/ppermute | solution.py:41
  88.0 23.3 %copy-start.1 = (bf16[8,8192]{1,0:T(8,128)(2,1)S(1)}, bf16[8,8192]{1,0:T(8,128)(2,1)}, u32[]{:S(2)}) copy-start(bf16[8,8192]{1,0:T(8,128)(2,1)} %param.13) | copy-start | bytes 393220
  88.0 9.2 %collective-permute-start.16 = (bf16[32,4096]{1,0:T(8,128)(2,1)S(1)}, bf16[32,4096]{1,0:T(8,128)(2,1)S(1)}, u32[]{:S(2)}, u32[]{:S(2)}) collective-permute-start(bf16[32,4096]{1,0:T(8,128)(2,1)S(1)} %slice.134), channel_id=1, source_target_pairs={{0,2},{1,3},{2,0},{3,1},{4,6},{5,7},{6,4},{7,5},{8,10},{9,11},{10,... | collective-permute-start | bytes 786440 | tf_op jit(solution)/shard_map/ppermute | solution.py:41
  89.6 12.4 %collective-permute-start.11 = (bf16[32,4096]{1,0:T(8,128)(2,1)S(1)}, bf16[32,4096]{1,0:T(8,128)(2,1)S(1)}, u32[]{:S(2)}, u32[]{:S(2)}) collective-permute-start(bf16[32,4096]{1,0:T(8,128)(2,1)S(1)} %slice.135), channel_id=1, source_target_pairs={{0,2},{1,3},{2,0},{3,1},{4,6},{5,7},{6,4},{7,5},{8,10},{9,11},{10,... | collective-permute-start | bytes 786440 | tf_op jit(solution)/shard_map/ppermute | solution.py:41
  97.3 8.6 %collective-permute-start.17 = (bf16[8,4096]{1,0:T(8,128)(2,1)S(1)}, bf16[8,4096]{1,0:T(8,128)(2,1)S(1)}, u32[]{:S(2)}, u32[]{:S(2)}) collective-permute-start(bf16[8,4096]{1,0:T(8,128)(2,1)S(1)} %get-tuple-element.14), channel_id=1, source_target_pairs={{0,4},{1,5},{2,6},{3,7},{4,8},{5,9},{6,10},{7,11},{8,12},{9,13},{1... | collective-permute-start | bytes 196616 | tf_op jit(solution)/shard_map/ppermute | solution.py:41
  97.5 8.8 %collective-permute-start.19 = (bf16[8,4096]{1,0:T(8,128)(2,1)S(1)}, bf16[8,4096]{1,0:T(8,128)(2,1)S(1)}, u32[]{:S(2)}, u32[]{:S(2)}) collective-permute-start(bf16[8,4096]{1,0:T(8,128)(2,1)S(1)} %get-tuple-element.15), channel_id=1, source_target_pairs={{0,12},{1,13},{2,14},{3,15},{4,0},{5,1},{6,2},{7,3},{8,4},{9,5},{1... | collective-permute-start | bytes 196616 | tf_op jit(solution)/shard_map/ppermute | solution.py:41
  101.2 5.9 %collective-permute-start.18 = (bf16[8,4096]{1,0:T(8,128)(2,1)S(1)}, bf16[8,4096]{1,0:T(8,128)(2,1)S(1)}, u32[]{:S(2)}, u32[]{:S(2)}) collective-permute-start(bf16[8,4096]{1,0:T(8,128)(2,1)S(1)} %get-tuple-element.16), channel_id=1, source_target_pairs={{0,8},{1,9},{2,10},{3,11},{4,12},{5,13},{6,14},{7,15},{8,0},{9,1},... | collective-permute-start | bytes 196616 | tf_op jit(solution)/shard_map/ppermute | solution.py:41
  102.0 6.5 %collective-permute-start.12 = (bf16[8,4096]{1,0:T(8,128)(2,1)S(1)}, bf16[8,4096]{1,0:T(8,128)(2,1)S(1)}, u32[]{:S(2)}, u32[]{:S(2)}) collective-permute-start(bf16[8,4096]{1,0:T(8,128)(2,1)S(1)} %get-tuple-element.11), channel_id=1, source_target_pairs={{0,4},{1,5},{2,6},{3,7},{4,8},{5,9},{6,10},{7,11},{8,12},{9,13},{1... | collective-permute-start | bytes 196616 | tf_op jit(solution)/shard_map/ppermute | solution.py:41
  102.7 5.8 %collective-permute-start.14 = (bf16[8,4096]{1,0:T(8,128)(2,1)S(1)}, bf16[8,4096]{1,0:T(8,128)(2,1)S(1)}, u32[]{:S(2)}, u32[]{:S(2)}) collective-permute-start(bf16[8,4096]{1,0:T(8,128)(2,1)S(1)} %get-tuple-element.12), channel_id=1, source_target_pairs={{0,12},{1,13},{2,14},{3,15},{4,0},{5,1},{6,2},{7,3},{8,4},{9,5},{1... | collective-permute-start | bytes 196616 | tf_op jit(solution)/shard_map/ppermute | solution.py:41
  105.9 5.4 %collective-permute-start.13 = (bf16[8,4096]{1,0:T(8,128)(2,1)S(1)}, bf16[8,4096]{1,0:T(8,128)(2,1)S(1)}, u32[]{:S(2)}, u32[]{:S(2)}) collective-permute-start(bf16[8,4096]{1,0:T(8,128)(2,1)S(1)} %get-tuple-element.13), channel_id=1, source_target_pairs={{0,8},{1,9},{2,10},{3,11},{4,12},{5,13},{6,14},{7,15},{8,0},{9,1},... | collective-permute-start | bytes 196616 | tf_op jit(solution)/shard_map/ppermute | solution.py:41
  (6 other events, 23.0 us)

commit v4 on v3

--- a/solution.py
+++ b/solution.py
@@ -60,27 +60,46 @@
         return jnp.asarray(np.array(rows, np.int32))[lax.axis_index(AXES)]
 
 
+def after(x, *earlier):
+    return lax.optimization_barrier((x, *earlier))[0]
+
+
 def gather_rows(grid, x):
-    parts = [x] + [grid.send(x, far=d) for d in range(1, grid.far)]
-    x = jnp.concatenate(parts, axis=0)
-    x = jnp.concatenate([x] + [grid.send(x, near=d) for d in range(1, grid.near)], axis=0)
-    return x, grid.send(x, core=1)
-
-
-def scatter_sum(grid, x):
-    for axis, count in (("core", grid.core), ("near", grid.near), ("far", grid.far)):
-        rows = x.shape[0] // count
-        got = [
-            grid.send(x[d * rows : (d + 1) * rows].astype(jnp.bfloat16), **{axis: d})
-            for d in range(1, count)
+    line = jnp.concatenate([x] + [grid.send(x, far=d) for d in range(1, grid.far)], axis=0)
+    beside = grid.send(line, near=1)
+    return line, beside, grid.send(line, core=1), grid.send(beside, core=1)
+
+
+def scatter_sum(grid, rows, w_out, chunks):
+    step = w_out.shape[1] // chunks
+    sums = []
+    sent = got = None
+    for i in range(chunks):
+        if i:
+            rows = after(rows, sent)
+        x = jnp.dot(rows, w_out[:, i * step : (i + 1) * step], preferred_element_type=jnp.float32)
+        half = x.shape[0] // 2
+        x = x[:half] + grid.send(x[half:].astype(jnp.bfloat16), core=1).astype(jnp.float32)
+        half = half // 2
+        sent = x[half:].astype(jnp.bfloat16)
+        if i:
+            sent = after(sent, got)
+        got = grid.send(sent, near=1)
+        x = x[:half] + got.astype(jnp.float32)
+        rows_dev = half // grid.far
+        parts = [
+            grid.send(x[d * rows_dev : (d + 1) * rows_dev].astype(jnp.bfloat16), far=d)
+            for d in range(1, grid.far)
         ]
-        x = x[:rows]
-        for part in got:
+        x = x[:rows_dev]
+        for part in parts:
             x = x + part.astype(jnp.float32)
-    return x
-
-
-def project_kernel(first, last, xa, xb, wq, wk, wv, *refs):
+        sums.append(x)
+    return jnp.concatenate(sums, axis=1)
+
+
+def project_kernel(first, last, count, *refs):
+    parts, (wq, wk, wv), refs = refs[:count], refs[count : count + 3], refs[count + 3 :]
     if not first:
         before, refs = refs[0], refs[1:]
     if last:
@@ -93,7 +112,7 @@
     def _():
         total[...] = jnp.zeros_like(total) if first else before[...]
 
-    x = jnp.concatenate([xa[...], xb[...]], axis=0)
+    x = jnp.concatenate([part[...] for part in parts], axis=0)
     pieces = [wk[...], wv[...]]
     spare = total.shape[1] - per_query - 2 * wk.shape[0]
     if spare:
@@ -117,19 +136,17 @@
             out[...] = total[...]
 
 
-def project(chunk, chunks, halves, w_query, w_key_t, w_value_t, before, place, slots, row_width):
-    xa, xb = halves
-    width = xa.shape[1]
+def project(chunk, chunks, parts, w_query, w_key_t, w_value_t, before, place, slots, row_width):
+    width = parts[0].shape[1]
     block = min(1024, width)
     steps = width // block
     start = chunk * steps
-    rows = xa.shape[0] + xb.shape[0]
+    rows = sum(part.shape[0] for part in parts)
     first, last = chunk == 0, chunk == chunks - 1
     whole = lambda i: (0, 0)
-    args = [xa, xb, w_query, w_key_t, w_value_t]
+    args = [*parts, w_query, w_key_t, w_value_t]
     specs = [
-        pl.BlockSpec((xa.shape[0], block), lambda i: (0, i)),
-        pl.BlockSpec((xb.shape[0], block), lambda i: (0, i)),
+        *[pl.BlockSpec((part.shape[0], block), lambda i: (0, i)) for part in parts],
         pl.BlockSpec((block, w_query.shape[1]), lambda i: (start + i, 0)),
         pl.BlockSpec((w_key_t.shape[0], block), lambda i: (0, start + i)),
         pl.BlockSpec((w_value_t.shape[0], block), lambda i: (0, start + i)),
@@ -144,13 +161,13 @@
     else:
         out = jax.ShapeDtypeStruct((rows, row_width), jnp.float32)
     return pl.pallas_call(
-        functools.partial(project_kernel, first, last),
+        functools.partial(project_kernel, first, last, len(parts)),
         grid=(steps,),
         in_specs=specs,
         out_specs=pl.BlockSpec(out.shape, whole),
         out_shape=out,
         scratch_shapes=[pltpu.VMEM((rows, row_width), jnp.float32)],
-        compiler_params=pltpu.CompilerParams(vmem_limit_bytes=56 * 2**20),
+        compiler_params=pltpu.CompilerParams(vmem_limit_bytes=48 * 2**20),
         cost_estimate=pl.CostEstimate(
             flops=2 * rows * width * row_width,
             bytes_accessed=2 * width * row_width,
@@ -171,14 +188,11 @@
     key_pages,
     value_pages,
     out,
-    keys,
-    values,
+    key_new,
     query_rot,
     value_own,
     chance,
     mixed,
-    key_sems,
-    value_sems,
 ):
     owners, slots, _ = inbound.shape
     pages = table.shape[1]
@@ -190,27 +204,11 @@
     pairs = kv_heads // 2
     span = pages * page
     pieces = owners // kv_heads
-    batches, held, _ = keys.shape
+    batches = query_rot.shape[1]
     batch = slots // batches
 
-    def fetch(pool, place, sems):
-        def one(slot, carry):
-            for j in range(pages):
-                pltpu.make_async_copy(
-                    pool.at[table[slot, j]], place(slot, j * page), sems.at[slot // batch]
-                ).start()
-            return carry
-
-        lax.fori_loop(0, slots, one, 0)
-
-    def key_place(slot, row):
-        return keys.at[slot // batch, pl.ds((slot % batch) * span + row, page)]
-
-    def value_place(slot, row):
-        return values.at[slot, pl.ds(row, page)]
-
-    fetch(key_pages, key_place, key_sems)
-    fetch(value_pages, value_place, value_sems)
+    def held(pool, slot, columns):
+        return [pool[table[slot, j], :, columns] for j in range(pages)]
 
     cos = cosine[...]
     sin = sine[...]
@@ -237,8 +235,7 @@
             back = (shift - per_key) % HEAD
             key = jnp.where(piece == j, pltpu.roll(tile, shift, 1) if shift else tile, key)
             value = jnp.where(piece == j, pltpu.roll(tile, back, 1) if back else tile, value)
-        for b in range(batches):
-            keys[b, batch * span :, g * HEAD : (g + 1) * HEAD] = turn(key)
+        key_new[:, g * HEAD : (g + 1) * HEAD] = turn(key)
         value_own[g] = value
 
     scale = HEAD ** (-0.5)
@@ -254,8 +251,6 @@
 
     own_chances = {}
     for b in range(batches):
-        whole = keys.at[b, pl.ds(0, batch * span)]
-        pltpu.make_async_copy(whole, whole, key_sems.at[b]).wait()
         valid = row < lengths[b]
         for p in range(pairs):
             turned = query_rot[p, b].T.astype(jnp.bfloat16)
@@ -263,10 +258,13 @@
             wide = jnp.concatenate(
                 [jnp.where(first, turned, none), jnp.where(first, none, turned)], axis=0
             )
+            columns_p = slice(p * 2 * HEAD, (p + 1) * 2 * HEAD)
+            keys = []
+            for s in range(batch):
+                keys += held(key_pages, b * batch + s, columns_p)
+            keys.append(key_new[:, columns_p])
             products = jnp.dot(
-                keys[b, :, p * 2 * HEAD : (p + 1) * 2 * HEAD],
-                wide,
-                preferred_element_type=jnp.float32,
+                jnp.concatenate(keys, axis=0), wide, preferred_element_type=jnp.float32
             )
             scores = products[:span]
             for s in range(1, batch):
@@ -285,15 +283,13 @@
             )
 
     for b in range(batches):
-        whole = values.at[pl.ds(b * batch, batch)]
-        pltpu.make_async_copy(whole, whole, value_sems.at[b]).wait()
         for s in range(batch):
             for p in range(pairs):
                 mine = chance[p, b, pl.ds(s, pair, stride=batch)].astype(jnp.bfloat16)
+                columns_p = slice(p * 2 * HEAD, (p + 1) * 2 * HEAD)
+                values = held(value_pages, b * batch + s, columns_p)
                 both = jnp.dot(
-                    mine,
-                    values[b * batch + s, :, p * 2 * HEAD : (p + 1) * 2 * HEAD],
-                    preferred_element_type=jnp.float32,
+                    mine, jnp.concatenate(values, axis=0), preferred_element_type=jnp.float32
                 )
                 result = jnp.concatenate(
                     [both[: pair // 2, :HEAD], both[pair // 2 :, HEAD:]], axis=0
@@ -330,23 +326,19 @@
     lengths = jnp.tile(lengths.reshape(batches, 1, batch), (1, 1, pair))
     smem = pl.BlockSpec(memory_space=pltpu.SMEM)
     vmem = pl.BlockSpec(memory_space=pltpu.VMEM)
-    hbm = pl.BlockSpec(memory_space=pl.ANY)
     return pl.pallas_call(
         functools.partial(attend_kernel, per_query, per_key),
-        in_specs=[smem, vmem, vmem, vmem, vmem, hbm, hbm],
+        in_specs=[smem, vmem, vmem, vmem, vmem, vmem, vmem],
         out_specs=vmem,
         out_shape=jax.ShapeDtypeStruct((owners, slots, per_query), jnp.bfloat16),
         scratch_shapes=[
-            pltpu.VMEM((batches, batch * span + slots, kv_width), jnp.bfloat16),
-            pltpu.VMEM((slots, span, kv_width), jnp.bfloat16),
+            pltpu.VMEM((slots, kv_width), jnp.bfloat16),
             pltpu.VMEM((pairs, batches, columns, HEAD), jnp.float32),
             pltpu.VMEM((kv_heads, slots, HEAD), jnp.float32),
             pltpu.VMEM((pairs, batches, columns, span), jnp.float32),
             pltpu.VMEM((pairs, batches, columns, HEAD), jnp.float32),
-            pltpu.SemaphoreType.DMA((batches,)),
-            pltpu.SemaphoreType.DMA((batches,)),
         ],
-        compiler_params=pltpu.CompilerParams(vmem_limit_bytes=56 * 2**20),
+        compiler_params=pltpu.CompilerParams(vmem_limit_bytes=44 * 2**20),
         cost_estimate=pl.CostEstimate(
             flops=8 * slots * heads * span * HEAD,
             bytes_accessed=4 * slots * span * kv_width,
@@ -412,11 +404,15 @@
 
     chunks = 2
     step = width // chunks
-    total = None
+    total = line = None
     for i in range(chunks):
-        halves = gather_rows(grid, normed[:, i * step : (i + 1) * step])
+        x = normed[:, i * step : (i + 1) * step]
+        if i:
+            x = after(x, line)
+        parts = gather_rows(grid, x)
+        line = parts[0]
         total = project(
-            i, chunks, halves, w_query, w_key.T, w_value.T, total, place_in, all_slots, row_width
+            i, chunks, parts, w_query, w_key.T, w_value.T, total, place_in, all_slots, row_width
         )
     outbound = total.reshape(owners, slot_count, row_width)
     inbound = lax.all_to_all(outbound, AXES, split_axis=0, concat_axis=0, tiled=True)
@@ -435,13 +431,7 @@
     returned = returned.reshape(all_slots, per_query)
     head_rows = jnp.dot(route_out, returned, preferred_element_type=jnp.float32)
     head_rows = head_rows.astype(jnp.bfloat16)
-    sums = []
-    for i in range(chunks):
-        partial = jnp.dot(
-            head_rows, w_out[:, i * step : (i + 1) * step], preferred_element_type=jnp.float32
-        )
-        sums.append(scatter_sum(grid, partial))
-    summed = jnp.concatenate(sums, axis=1)
+    summed = scatter_sum(grid, head_rows, w_out, chunks)
     return (inputs + summed).astype(jnp.bfloat16)
 
 

time: 113 us -> 112 us (level)
  waiting for transfers between devices: 42.1 us -> 48.1 us
  starting transfers between devices: 34.8 us -> 30.4 us
  Pallas kernels: 16.4 us -> 12.2 us
  local copies, waits for them, and re-layouts: 5.67 us -> 8.37 us
    unnamed x22 -> x21, local copies, waits for them, and re-layouts: 2.41 us -> 6.86 us
    ppermute x20 -> x22, starting transfers between devices: 26.6 us -> 22.3 us  [send(): return lax.ppermute(x, AXES, self.perm(far, near, core))]
    ppermute x20 -> x22, waiting for transfers between devices: 23.6 us -> 27.8 us  [send(): return lax.ppermute(x, AXES, self.perm(far, near, core))]
    pallas_call x1, Pallas kernels: 6.12 us -> 3.4 us  [attend(): pl.pallas_call(functools.partial(attend_kernel, per_query, per_key), in_s...]
    all_to_all x1, waiting for transfers between devices: 8.62 us -> 10.4 us  [on_device(): lax.all_to_all(outbound, AXES, split_axis=0, concat_axis=0, tiled=True)]
    pallas_call x2, Pallas kernels: 10.3 us -> 8.81 us  [project(): pl.pallas_call(functools.partial(project_kernel, first, last, len(parts))...]
  transfers between devices with their start and end apart: 22 -> 24, of which waited for: 11 -> 12; matrix products, arithmetic and copies ran while one was open for 9% -> 6% of each run, Pallas kernels for 4% -> 4%
where the time goes in v4:
time: 112 us; the launch traced here: 111 us
  waiting for transfers between devices  48.1 us (43%)
  starting transfers between devices  30.4 us (27%)
  Pallas kernels  12.2 us (11%)
  local copies, waits for them, and re-layouts  8.37 us (7%)
  matrix products  6.02 us (5%)
  other arithmetic  5.99 us (5%)
    ppermute x22, waiting for transfers between devices, send(): return lax.ppermute(x, AXES, self.perm(far, near, core))  27.8 us
    ppermute x22, starting transfers between devices, send(): return lax.ppermute(x, AXES, self.perm(far, near, core))  22.3 us
    all_to_all x1, waiting for transfers between devices, on_device(): lax.all_to_all(outbound, AXES, split_axis=0, concat_axis=0, tiled=True)  10.4 us
    all_to_all x1, waiting for transfers between devices, on_device(): lax.all_to_all(attended, AXES, split_axis=0, concat_axis=0, tiled=True)  9.92 us
    pallas_call x2, Pallas kernels, project(): pl.pallas_call(functools.partial(project_kernel, first, last, len(parts))...  8.81 us
    unnamed x21, local copies, waits for them, and re-layouts  6.86 us
    dot_general x2, matrix products, scatter_sum(): jnp.dot(rows, w_out[:, i * step:(i + 1) * step], preferred_element_type=j...  5.8 us
    all_to_all x1, starting transfers between devices, on_device(): lax.all_to_all(outbound, AXES, split_axis=0, concat_axis=0, tiled=True)  4.61 us
  transfers between devices with their start and end apart: 24, of which 12 were waited for; matrix products, arithmetic and copies ran while one was open for 6% of the time, Pallas kernels for 4%

profile of v4, /device:TPU:0, one launch (start us, length us, event | category | flops | bytes accessed | tf_op | source)
XLA Modules:
  0.0 111.4 jit_solution(15954834366212224372)
XLA Ops:
  2.1 5.1 %collective-permute-start.2 = (bf16[8,4096]{1,0:T(8,128)(2,1)S(1)}, bf16[8,4096]{1,0:T(8,128)(2,1)S(1)}, u32[]{:S(2)}, u32[]{:S(2)}) collective-permute-start(bf16[8,4096]{1,0:T(8,128)(2,1)S(1)} %get-tuple-element.23), channel_id=1, source_target_pairs={{0,12},{1,13},{2,14},{3,15},{4,0},{5,1},{6,2},{7,3},{8,4},{9,5},{1... | collective-permute-start | bytes 196616 | tf_op jit(solution)/shard_map/ppermute | solution.py:41
  9.7 4.0 %collective-permute-done.1 = bf16[8,4096]{1,0:T(8,128)(2,1)S(1)} collective-permute-done((bf16[8,4096]{1,0:T(8,128)(2,1)S(1)}, bf16[8,4096]{1,0:T(8,128)(2,1)S(1)}, u32[]{:S(2)}, u32[]{:S(2)}) %collective-permute-start.1) | collective-permute-done | bytes 65568 | tf_op jit(solution)/shard_map/ppermute | solution.py:41
  13.7 1.9 %collective-permute-start.5 = (bf16[8,4096]{1,0:T(8,128)(2,1)S(1)}, bf16[8,4096]{1,0:T(8,128)(2,1)S(1)}, u32[]{:S(2)}, u32[]{:S(2)}) collective-permute-start(bf16[8,4096]{1,0:T(8,128)(2,1)S(1)} %get-tuple-element.8), channel_id=1, source_target_pairs={{0,12},{1,13},{2,14},{3,15},{4,0},{5,1},{6,2},{7,3},{8,4},{9,5},{1... | collective-permute-start | bytes 196616 | tf_op jit(solution)/shard_map/ppermute | solution.py:41
  15.7 1.9 %collective-permute-start.3 = (bf16[8,4096]{1,0:T(8,128)(2,1)S(1)}, bf16[8,4096]{1,0:T(8,128)(2,1)S(1)}, u32[]{:S(2)}, u32[]{:S(2)}) collective-permute-start(bf16[8,4096]{1,0:T(8,128)(2,1)S(1)} %get-tuple-element.8), channel_id=1, source_target_pairs={{0,4},{1,5},{2,6},{3,7},{4,8},{5,9},{6,10},{7,11},{8,12},{9,13},{1... | collective-permute-start | bytes 196616 | tf_op jit(solution)/shard_map/ppermute | solution.py:41
  19.1 2.7 %collective-permute-done.3 = bf16[8,4096]{1,0:T(8,128)(2,1)S(1)} collective-permute-done((bf16[8,4096]{1,0:T(8,128)(2,1)S(1)}, bf16[8,4096]{1,0:T(8,128)(2,1)S(1)}, u32[]{:S(2)}, u32[]{:S(2)}) %collective-permute-start.3) | collective-permute-done | bytes 65568 | tf_op jit(solution)/shard_map/ppermute | solution.py:41
  25.7 4.4 %collective-permute-done.6.refs_1_ = bf16[32,4096]{1,0:T(8,128)(2,1)S(1)} collective-permute-done((bf16[32,4096]{1,0:T(8,128)(2,1)S(1)}, bf16[32,4096]{1,0:T(8,128)(2,1)S(1)}, u32[]{:S(2)}, u32[]{:S(2)}) %collective-permute-start.6) | collective-permute-done | bytes 262176 | tf_op jit(solution)/shard_map/ppermute | solution.py:41
  34.1 4.0 %project.2.refs_7_ = f32[128,640]{1,0:T(8,128)S(1)} custom-call(bf16[32,4096]{1,0:T(8,128)(2,1)S(1)} %pad_maximum_fusion.refs_0_, bf16[32,4096]{1,0:T(8,128)(2,1)S(1)} %collective-permute-done.9.refs_1_, bf16[32,4096]{1,0:T(8,128)(2,1)S(1)} %collective-permute-done.10.refs_2_, bf16[32,4096]{1,0:T(8,128)(2,1)S(1)} %collective-permute-done.11.refs_3_, ...), custom_call_target="tpu_custom_call" | custom-call | flops 671088640 | bytes 5242880 | tf_op jit(solution)/shard_map/project/pallas_call | solution.py:163
  38.1 4.8 %project.3 = bf16[256,640]{1,0:T(8,128)(2,1)} custom-call(bf16[32,4096]{1,0:T(8,128)(2,1)S(1)} %constant_dynamic-update-slice_fusion.refs_0_, bf16[32,4096]{1,0:T(8,128)(2,1)S(1)} %collective-permute-done.6.refs_1_, bf16[32,4096]{1,0:T(8,128)(2,1)S(1)} %collective-permute-done.7.refs_2_, bf16[32,4096]{1,0:T(8,128)(2,1)S(1)} %collective-permute-done.8.refs_3_, ...), custom_call_target="tpu_custom_call" | custom-call | flops 671088640 | bytes 5242880 | tf_op jit(solution)/shard_map/project/pallas_call | solution.py:163
  43.0 4.6 %all-to-all-start = ((bf16[16,16,640]{2,1,0:T(8,128)(2,1)}), bf16[16,16,640]{2,1,0:T(8,128)(2,1)S(1)}, u32[]{:S(2)}, u32[]{:S(2)}) async-start(bf16[16,16,640]{2,1,0:T(8,128)(2,1)} %bitcast.6), calls=%async_computation | async-start | bytes 655360 | tf_op jit(solution)/shard_map/all_to_all | solution.py:418
  48.3 10.4 %all-to-all-done.inbound = bf16[16,16,640]{2,1,0:T(8,128)(2,1)S(1)} async-done(((bf16[16,16,640]{2,1,0:T(8,128)(2,1)}), bf16[16,16,640]{2,1,0:T(8,128)(2,1)S(1)}, u32[]{:S(2)}, u32[]{:S(2)}) %all-to-all-start) | async-done | bytes 327712 | tf_op jit(solution)/shard_map/all_to_all | solution.py:418
  58.7 2.2 %copy-done.4 = bf16[1,64,32,1024]{3,2,1,0:T(8,128)(2,1)S(1)} copy-done((bf16[1,64,32,1024]{3,2,1,0:T(8,128)(2,1)S(1)}, bf16[1,64,32,1024]{3,2,1,0:T(8,128)(2,1)}, u32[]{:S(2)}) %copy-start.4) | copy-done | bytes 4194328
  60.9 2.2 %copy-done.5 = bf16[1,64,32,1024]{3,2,1,0:T(8,128)(2,1)S(1)} copy-done((bf16[1,64,32,1024]{3,2,1,0:T(8,128)(2,1)S(1)}, bf16[1,64,32,1024]{3,2,1,0:T(8,128)(2,1)}, u32[]{:S(2)}) %copy-start.5) | copy-done | bytes 4194328
  63.1 3.4 %attend.1 = bf16[16,16,512]{2,1,0:T(8,128)(2,1)} custom-call(s32[16,4]{1,0:T(8,128)S(1)} %copy.18.table, s32[2,1,128]{2,1,0:T(1,128)S(1)} %bitcast.21, bf16[16,16,640]{2,1,0:T(8,128)(2,1)S(1)} %all-to-all-done.inbound, f32[16,128]{1,0:T(8,128)S(1)} %get-tuple-element.30.cosine, f32[16,128]{1,0:T(8,128)S(1)} %get-tuple-element.31.sine, ...), custom_call_target="tpu_custom_call" | custom-call | flops 134217728 | bytes 8388608 | tf_op jit(solution)/shard_map/attend/pallas_call | solution.py:329
  66.4 3.5 %all-to-all-start.1 = ((bf16[16,16,512]{2,1,0:T(8,128)(2,1)}), bf16[16,16,512]{2,1,0:T(8,128)(2,1)S(1)}, u32[]{:S(2)}, u32[]{:S(2)}) async-start(bf16[16,16,512]{2,1,0:T(8,128)(2,1)} %attend.1), calls=%async_computation.1 | async-start | bytes 524288 | tf_op jit(solution)/shard_map/all_to_all | solution.py:430
  70.1 9.9 %all-to-all-done.1 = bf16[16,16,512]{2,1,0:T(8,128)(2,1)S(1)} async-done(((bf16[16,16,512]{2,1,0:T(8,128)(2,1)}), bf16[16,16,512]{2,1,0:T(8,128)(2,1)S(1)}, u32[]{:S(2)}, u32[]{:S(2)}) %all-to-all-start.1) | async-done | bytes 262176 | tf_op jit(solution)/shard_map/all_to_all | solution.py:430
  80.2 2.9 %fusion.2 = f32[128,4096]{1,0:T(8,128)S(1)} fusion(bf16[128,512]{1,0:T(8,128)(2,1)S(1)} %convolution_convert_fusion, bf16[512,8192]{1,0:T(8,128)(2,1)} %param.18), kind=kOutput, calls=%fused_computation.2 | convolution fusion | flops 536870912 | bytes 6422528 | tf_op jit(solution)/shard_map/dot_general | solution.py:80
  83.3 1.9 %collective-permute-done.12 = bf16[64,4096]{1,0:T(8,128)(2,1)S(1)} collective-permute-done((bf16[64,4096]{1,0:T(8,128)(2,1)S(1)}, bf16[64,4096]{1,0:T(8,128)(2,1)S(1)}, u32[]{:S(2)}, u32[]{:S(2)}) %collective-permute-start.12) | collective-permute-done | bytes 524320 | tf_op jit(solution)/shard_map/ppermute | solution.py:41
  85.6 2.9 %fusion = f32[128,4096]{1,0:T(8,128)S(1)} fusion(bf16[128,512]{1,0:T(8,128)(2,1)S(1)} %convolution_convert_fusion, bf16[512,8192]{1,0:T(8,128)(2,1)} %param.18), kind=kOutput, calls=%fused_computation | convolution fusion | flops 536870912 | bytes 6422528 | tf_op jit(solution)/shard_map/dot_general | solution.py:80
  88.7 5.1 %collective-permute-done.13 = bf16[32,4096]{1,0:T(8,128)(2,1)S(1)} collective-permute-done((bf16[32,4096]{1,0:T(8,128)(2,1)S(1)}, bf16[32,4096]{1,0:T(8,128)(2,1)S(1)}, u32[]{:S(2)}, u32[]{:S(2)}) %collective-permute-start.13) | collective-permute-done | bytes 262176 | tf_op jit(solution)/shard_map/ppermute | solution.py:41
  95.4 2.9 %collective-permute-start.16 = (bf16[8,4096]{1,0:T(8,128)(2,1)S(1)}, bf16[8,4096]{1,0:T(8,128)(2,1)S(1)}, u32[]{:S(2)}, u32[]{:S(2)}) collective-permute-start(bf16[8,4096]{1,0:T(8,128)(2,1)S(1)} %get-tuple-element.18), channel_id=1, source_target_pairs={{0,12},{1,13},{2,14},{3,15},{4,0},{5,1},{6,2},{7,3},{8,4},{9,5},{1... | collective-permute-start | bytes 196616 | tf_op jit(solution)/shard_map/ppermute | solution.py:41
  98.3 3.2 %collective-permute-done.18 = bf16[32,4096]{1,0:T(8,128)(2,1)S(1)} collective-permute-done((bf16[32,4096]{1,0:T(8,128)(2,1)S(1)}, bf16[32,4096]{1,0:T(8,128)(2,1)S(1)}, u32[]{:S(2)}, u32[]{:S(2)}) %collective-permute-start.18) | collective-permute-done | bytes 262176 | tf_op jit(solution)/shard_map/ppermute | solution.py:41
  102.5 3.0 %collective-permute-start.21 = (bf16[8,4096]{1,0:T(8,128)(2,1)S(1)}, bf16[8,4096]{1,0:T(8,128)(2,1)S(1)}, u32[]{:S(2)}, u32[]{:S(2)}) collective-permute-start(bf16[8,4096]{1,0:T(8,128)(2,1)S(1)} %get-tuple-element.21), channel_id=1, source_target_pairs={{0,12},{1,13},{2,14},{3,15},{4,0},{5,1},{6,2},{7,3},{8,4},{9,5},{1... | collective-permute-start | bytes 196616 | tf_op jit(solution)/shard_map/ppermute | solution.py:41
  105.6 2.3 %collective-permute-done.19 = bf16[8,4096]{1,0:T(8,128)(2,1)S(1)} collective-permute-done((bf16[8,4096]{1,0:T(8,128)(2,1)S(1)}, bf16[8,4096]{1,0:T(8,128)(2,1)S(1)}, u32[]{:S(2)}, u32[]{:S(2)}) %collective-permute-start.19) | collective-permute-done | bytes 65568 | tf_op jit(solution)/shard_map/ppermute | solution.py:41
  107.9 2.8 %collective-permute-done.20 = bf16[8,4096]{1,0:T(8,128)(2,1)S(1)} collective-permute-done((bf16[8,4096]{1,0:T(8,128)(2,1)S(1)}, bf16[8,4096]{1,0:T(8,128)(2,1)S(1)}, u32[]{:S(2)}, u32[]{:S(2)}) %collective-permute-start.20) | collective-permute-done | bytes 65568 | tf_op jit(solution)/shard_map/ppermute | solution.py:41
  (90 shorter events, 19.0 us)
Async XLA Ops:
  2.1 7.6 %collective-permute-start.2 = (bf16[8,4096]{1,0:T(8,128)(2,1)S(1)}, bf16[8,4096]{1,0:T(8,128)(2,1)S(1)}, u32[]{:S(2)}, u32[]{:S(2)}) collective-permute-start(bf16[8,4096]{1,0:T(8,128)(2,1)S(1)} %get-tuple-element.23), channel_id=1, source_target_pairs={{0,12},{1,13},{2,14},{3,15},{4,0},{5,1},{6,2},{7,3},{8,4},{9,5},{1... | collective-permute-start | bytes 196616 | tf_op jit(solution)/shard_map/ppermute | solution.py:41
  7.2 6.5 %collective-permute-start.1 = (bf16[8,4096]{1,0:T(8,128)(2,1)S(1)}, bf16[8,4096]{1,0:T(8,128)(2,1)S(1)}, u32[]{:S(2)}, u32[]{:S(2)}) collective-permute-start(bf16[8,4096]{1,0:T(8,128)(2,1)S(1)} %get-tuple-element.23), channel_id=1, source_target_pairs={{0,8},{1,9},{2,10},{3,11},{4,12},{5,13},{6,14},{7,15},{8,0},{9,1},... | collective-permute-start | bytes 196616 | tf_op jit(solution)/shard_map/ppermute | solution.py:41
  7.2 6.5 %collective-permute-start = (bf16[8,4096]{1,0:T(8,128)(2,1)S(1)}, bf16[8,4096]{1,0:T(8,128)(2,1)S(1)}, u32[]{:S(2)}, u32[]{:S(2)}) collective-permute-start(bf16[8,4096]{1,0:T(8,128)(2,1)S(1)} %get-tuple-element.23), channel_id=1, source_target_pairs={{0,4},{1,5},{2,6},{3,7},{4,8},{5,9},{6,10},{7,11},{8,12},{9,13},{1... | collective-permute-start | bytes 196616 | tf_op jit(solution)/shard_map/ppermute | solution.py:41
  13.7 8.8 %collective-permute-start.5 = (bf16[8,4096]{1,0:T(8,128)(2,1)S(1)}, bf16[8,4096]{1,0:T(8,128)(2,1)S(1)}, u32[]{:S(2)}, u32[]{:S(2)}) collective-permute-start(bf16[8,4096]{1,0:T(8,128)(2,1)S(1)} %get-tuple-element.8), channel_id=1, source_target_pairs={{0,12},{1,13},{2,14},{3,15},{4,0},{5,1},{6,2},{7,3},{8,4},{9,5},{1... | collective-permute-start | bytes 196616 | tf_op jit(solution)/shard_map/ppermute | solution.py:41
  15.7 6.8 %collective-permute-start.4 = (bf16[8,4096]{1,0:T(8,128)(2,1)S(1)}, bf16[8,4096]{1,0:T(8,128)(2,1)S(1)}, u32[]{:S(2)}, u32[]{:S(2)}) collective-permute-start(bf16[8,4096]{1,0:T(8,128)(2,1)S(1)} %get-tuple-element.8), channel_id=1, source_target_pairs={{0,8},{1,9},{2,10},{3,11},{4,12},{5,13},{6,14},{7,15},{8,0},{9,1},... | collective-permute-start | bytes 196616 | tf_op jit(solution)/shard_map/ppermute | solution.py:41
  15.7 6.1 %collective-permute-start.3 = (bf16[8,4096]{1,0:T(8,128)(2,1)S(1)}, bf16[8,4096]{1,0:T(8,128)(2,1)S(1)}, u32[]{:S(2)}, u32[]{:S(2)}) collective-permute-start(bf16[8,4096]{1,0:T(8,128)(2,1)S(1)} %get-tuple-element.8), channel_id=1, source_target_pairs={{0,4},{1,5},{2,6},{3,7},{4,8},{5,9},{6,10},{7,11},{8,12},{9,13},{1... | collective-permute-start | bytes 196616 | tf_op jit(solution)/shard_map/ppermute | solution.py:41
  17.6 8.0 %collective-permute-start.9 = (bf16[32,4096]{1,0:T(8,128)(2,1)S(1)}, bf16[32,4096]{1,0:T(8,128)(2,1)S(1)}, u32[]{:S(2)}, u32[]{:S(2)}) collective-permute-start(bf16[32,4096]{1,0:T(8,128)(2,1)S(1)} %pad_maximum_fusion.refs_0_), channel_id=1, source_target_pairs={{0,2},{1,3},{2,0},{3,1},{4,6},{5,7},{6,4},{7,5},{8,10},{9,11},{10,... | collective-permute-start | bytes 786440 | tf_op jit(solution)/shard_map/ppermute | solution.py:41
  22.5 7.5 %collective-permute-start.6 = (bf16[32,4096]{1,0:T(8,128)(2,1)S(1)}, bf16[32,4096]{1,0:T(8,128)(2,1)S(1)}, u32[]{:S(2)}, u32[]{:S(2)}) collective-permute-start(bf16[32,4096]{1,0:T(8,128)(2,1)S(1)} %constant_dynamic-update-slice_fusion.refs_0_), channel_id=1, source_target_pairs={{0,2},{1,3},{2,0},{3,1},{4,6},{5,7},{6,4},{7,5},{8,10},{9,11},{10,... | collective-permute-start | bytes 786440 | tf_op jit(solution)/shard_map/ppermute | solution.py:41
  25.1 6.5 %collective-permute-start.10 = (bf16[32,4096]{1,0:T(8,128)(2,1)S(1)}, bf16[32,4096]{1,0:T(8,128)(2,1)S(1)}, u32[]{:S(2)}, u32[]{:S(2)}) collective-permute-start(bf16[32,4096]{1,0:T(8,128)(2,1)S(1)} %pad_maximum_fusion.refs_0_), channel_id=1, source_target_pairs={{0,1},{1,0},{2,3},{3,2},{4,5},{5,4},{6,7},{7,6},{8,9},{9,8},{10,11... | collective-permute-start | bytes 786440 | tf_op jit(solution)/shard_map/ppermute | solution.py:41
  25.1 13.0 %collective-permute-start.7 = (bf16[32,4096]{1,0:T(8,128)(2,1)S(1)}, bf16[32,4096]{1,0:T(8,128)(2,1)S(1)}, u32[]{:S(2)}, u32[]{:S(2)}) collective-permute-start(bf16[32,4096]{1,0:T(8,128)(2,1)S(1)} %constant_dynamic-update-slice_fusion.refs_0_), channel_id=1, source_target_pairs={{0,1},{1,0},{2,3},{3,2},{4,5},{5,4},{6,7},{7,6},{8,9},{9,8},{10,11... | collective-permute-start | bytes 786440 | tf_op jit(solution)/shard_map/ppermute | solution.py:41
  25.6 6.0 %collective-permute-start.11 = (bf16[32,4096]{1,0:T(8,128)(2,1)S(1)}, bf16[32,4096]{1,0:T(8,128)(2,1)S(1)}, u32[]{:S(2)}, u32[]{:S(2)}) collective-permute-start(bf16[32,4096]{1,0:T(8,128)(2,1)S(1)} %collective-permute-done.9.refs_1_), channel_id=1, source_target_pairs={{0,1},{1,0},{2,3},{3,2},{4,5},{5,4},{6,7},{7,6},{8,9},{9,8},{10,11... | collective-permute-start | bytes 786440 | tf_op jit(solution)/shard_map/ppermute | solution.py:41
  30.1 8.0 %collective-permute-start.8 = (bf16[32,4096]{1,0:T(8,128)(2,1)S(1)}, bf16[32,4096]{1,0:T(8,128)(2,1)S(1)}, u32[]{:S(2)}, u32[]{:S(2)}) collective-permute-start(bf16[32,4096]{1,0:T(8,128)(2,1)S(1)} %collective-permute-done.6.refs_1_), channel_id=1, source_target_pairs={{0,1},{1,0},{2,3},{3,2},{4,5},{5,4},{6,7},{7,6},{8,9},{9,8},{10,11... | collective-permute-start | bytes 786440 | tf_op jit(solution)/shard_map/ppermute | solution.py:41
  43.0 15.7 %all-to-all-start = ((bf16[16,16,640]{2,1,0:T(8,128)(2,1)}), bf16[16,16,640]{2,1,0:T(8,128)(2,1)S(1)}, u32[]{:S(2)}, u32[]{:S(2)}) async-start(bf16[16,16,640]{2,1,0:T(8,128)(2,1)} %bitcast.6), calls=%async_computation | async-start | bytes 655360 | tf_op jit(solution)/shard_map/all_to_all | solution.py:418
  66.4 13.5 %all-to-all-start.1 = ((bf16[16,16,512]{2,1,0:T(8,128)(2,1)}), bf16[16,16,512]{2,1,0:T(8,128)(2,1)S(1)}, u32[]{:S(2)}, u32[]{:S(2)}) async-start(bf16[16,16,512]{2,1,0:T(8,128)(2,1)} %attend.1), calls=%async_computation.1 | async-start | bytes 524288 | tf_op jit(solution)/shard_map/all_to_all | solution.py:430
  83.2 2.0 %collective-permute-start.12 = (bf16[64,4096]{1,0:T(8,128)(2,1)S(1)}, bf16[64,4096]{1,0:T(8,128)(2,1)S(1)}, u32[]{:S(2)}, u32[]{:S(2)}) collective-permute-start(bf16[64,4096]{1,0:T(8,128)(2,1)S(1)} %slice.131), channel_id=1, source_target_pairs={{0,1},{1,0},{2,3},{3,2},{4,5},{5,4},{6,7},{7,6},{8,9},{9,8},{10,11... | collective-permute-start | bytes 1572872 | tf_op jit(solution)/shard_map/ppermute | solution.py:41
  85.3 8.4 %collective-permute-start.13 = (bf16[32,4096]{1,0:T(8,128)(2,1)S(1)}, bf16[32,4096]{1,0:T(8,128)(2,1)S(1)}, u32[]{:S(2)}, u32[]{:S(2)}) collective-permute-start(bf16[32,4096]{1,0:T(8,128)(2,1)S(1)} %slice.133), channel_id=1, source_target_pairs={{0,2},{1,3},{2,0},{3,1},{4,6},{5,7},{6,4},{7,5},{8,10},{9,11},{10,... | collective-permute-start | bytes 786440 | tf_op jit(solution)/shard_map/ppermute | solution.py:41
  88.5 5.3 %collective-permute-start.17 = (bf16[64,4096]{1,0:T(8,128)(2,1)S(1)}, bf16[64,4096]{1,0:T(8,128)(2,1)S(1)}, u32[]{:S(2)}, u32[]{:S(2)}) collective-permute-start(bf16[64,4096]{1,0:T(8,128)(2,1)S(1)} %slice.130), channel_id=1, source_target_pairs={{0,1},{1,0},{2,3},{3,2},{4,5},{5,4},{6,7},{7,6},{8,9},{9,8},{10,11... | collective-permute-start | bytes 1572872 | tf_op jit(solution)/shard_map/ppermute | solution.py:41
  94.0 7.6 %collective-permute-start.18 = (bf16[32,4096]{1,0:T(8,128)(2,1)S(1)}, bf16[32,4096]{1,0:T(8,128)(2,1)S(1)}, u32[]{:S(2)}, u32[]{:S(2)}) collective-permute-start(bf16[32,4096]{1,0:T(8,128)(2,1)S(1)} %slice.132), channel_id=1, source_target_pairs={{0,2},{1,3},{2,0},{3,1},{4,6},{5,7},{6,4},{7,5},{8,10},{9,11},{10,... | collective-permute-start | bytes 786440 | tf_op jit(solution)/shard_map/ppermute | solution.py:41
  94.4 11.1 %collective-permute-start.14 = (bf16[8,4096]{1,0:T(8,128)(2,1)S(1)}, bf16[8,4096]{1,0:T(8,128)(2,1)S(1)}, u32[]{:S(2)}, u32[]{:S(2)}) collective-permute-start(bf16[8,4096]{1,0:T(8,128)(2,1)S(1)} %get-tuple-element.17), channel_id=1, source_target_pairs={{0,4},{1,5},{2,6},{3,7},{4,8},{5,9},{6,10},{7,11},{8,12},{9,13},{1... | collective-permute-start | bytes 196616 | tf_op jit(solution)/shard_map/ppermute | solution.py:41
  95.4 10.1 %collective-permute-start.16 = (bf16[8,4096]{1,0:T(8,128)(2,1)S(1)}, bf16[8,4096]{1,0:T(8,128)(2,1)S(1)}, u32[]{:S(2)}, u32[]{:S(2)}) collective-permute-start(bf16[8,4096]{1,0:T(8,128)(2,1)S(1)} %get-tuple-element.18), channel_id=1, source_target_pairs={{0,12},{1,13},{2,14},{3,15},{4,0},{5,1},{6,2},{7,3},{8,4},{9,5},{1... | collective-permute-start | bytes 196616 | tf_op jit(solution)/shard_map/ppermute | solution.py:41
  98.3 7.2 %collective-permute-start.15 = (bf16[8,4096]{1,0:T(8,128)(2,1)S(1)}, bf16[8,4096]{1,0:T(8,128)(2,1)S(1)}, u32[]{:S(2)}, u32[]{:S(2)}) collective-permute-start(bf16[8,4096]{1,0:T(8,128)(2,1)S(1)} %get-tuple-element.19), channel_id=1, source_target_pairs={{0,8},{1,9},{2,10},{3,11},{4,12},{5,13},{6,14},{7,15},{8,0},{9,1},... | collective-permute-start | bytes 196616 | tf_op jit(solution)/shard_map/ppermute | solution.py:41
  101.7 6.2 %collective-permute-start.19 = (bf16[8,4096]{1,0:T(8,128)(2,1)S(1)}, bf16[8,4096]{1,0:T(8,128)(2,1)S(1)}, u32[]{:S(2)}, u32[]{:S(2)}) collective-permute-start(bf16[8,4096]{1,0:T(8,128)(2,1)S(1)} %get-tuple-element.20), channel_id=1, source_target_pairs={{0,4},{1,5},{2,6},{3,7},{4,8},{5,9},{6,10},{7,11},{8,12},{9,13},{1... | collective-permute-start | bytes 196616 | tf_op jit(solution)/shard_map/ppermute | solution.py:41
  102.5 5.4 %collective-permute-start.21 = (bf16[8,4096]{1,0:T(8,128)(2,1)S(1)}, bf16[8,4096]{1,0:T(8,128)(2,1)S(1)}, u32[]{:S(2)}, u32[]{:S(2)}) collective-permute-start(bf16[8,4096]{1,0:T(8,128)(2,1)S(1)} %get-tuple-element.21), channel_id=1, source_target_pairs={{0,12},{1,13},{2,14},{3,15},{4,0},{5,1},{6,2},{7,3},{8,4},{9,5},{1... | collective-permute-start | bytes 196616 | tf_op jit(solution)/shard_map/ppermute | solution.py:41
  105.5 5.2 %collective-permute-start.20 = (bf16[8,4096]{1,0:T(8,128)(2,1)S(1)}, bf16[8,4096]{1,0:T(8,128)(2,1)S(1)}, u32[]{:S(2)}, u32[]{:S(2)}) collective-permute-start(bf16[8,4096]{1,0:T(8,128)(2,1)S(1)} %get-tuple-element.22), channel_id=1, source_target_pairs={{0,8},{1,9},{2,10},{3,11},{4,12},{5,13},{6,14},{7,15},{8,0},{9,1},... | collective-permute-start | bytes 196616 | tf_op jit(solution)/shard_map/ppermute | solution.py:41
  (9 other events, 56.5 us)

commit v5 on v4

--- a/solution.py
+++ b/solution.py
@@ -59,69 +59,121 @@
                     )
         return jnp.asarray(np.array(rows, np.int32))[lax.axis_index(AXES)]
 
+    def crossed(self):
+        return [
+            (dc * self.near + dn) * self.far + df
+            for dc in range(self.core)
+            for df in range(self.far)
+            for dn in range(self.near)
+        ]
+
 
 def after(x, *earlier):
     return lax.optimization_barrier((x, *earlier))[0]
 
 
-def gather_rows(grid, x):
-    line = jnp.concatenate([x] + [grid.send(x, far=d) for d in range(1, grid.far)], axis=0)
-    beside = grid.send(line, near=1)
-    return line, beside, grid.send(line, core=1), grid.send(beside, core=1)
-
-
-def scatter_sum(grid, rows, w_out, chunks):
-    step = w_out.shape[1] // chunks
-    sums = []
-    sent = got = None
-    for i in range(chunks):
-        if i:
-            rows = after(rows, sent)
-        x = jnp.dot(rows, w_out[:, i * step : (i + 1) * step], preferred_element_type=jnp.float32)
-        half = x.shape[0] // 2
-        x = x[:half] + grid.send(x[half:].astype(jnp.bfloat16), core=1).astype(jnp.float32)
-        half = half // 2
-        sent = x[half:].astype(jnp.bfloat16)
-        if i:
-            sent = after(sent, got)
-        got = grid.send(sent, near=1)
-        x = x[:half] + got.astype(jnp.float32)
-        rows_dev = half // grid.far
+def gather_rows(grid, xa, xb, meanwhile):
+    beside_b = grid.send(xb, near=1)
+    line_a = jnp.concatenate([xa] + [grid.send(xa, far=d) for d in range(1, grid.far)], axis=0)
+    pair_b = jnp.concatenate([xb, beside_b], axis=0)
+    line_a, pair_b = lax.optimization_barrier((line_a, pair_b))
+    beside_a = grid.send(line_a, near=1)
+    line_b = [grid.send(pair_b, far=d) for d in range(1, grid.far)]
+    beside_a, line_b, meanwhile = lax.optimization_barrier((beside_a, line_b, meanwhile))
+    parts_a = [line_a, beside_a]
+    parts_b = [pair_b, *line_b]
+    parts_a += [grid.send(part, core=1) for part in parts_a]
+    parts_b += [grid.send(part, core=1) for part in parts_b]
+    return parts_a, parts_b, meanwhile
+
+
+def narrow(x):
+    return x.astype(jnp.bfloat16)
+
+
+def wide(x):
+    return x.astype(jnp.float32)
+
+
+def scatter_sum(grid, rows_a, rows_b, w_out):
+    half = w_out.shape[1] // 2
+
+    def start(rows, w):
+        x = jnp.dot(rows, w, preferred_element_type=jnp.float32)
+        middle = x.shape[0] // 2
+        away = narrow(x[middle:])
+        return away, x[:middle] + wide(grid.send(away, core=1))
+
+    def along_near(x):
+        middle = x.shape[0] // 2
+        return x[:middle] + wide(grid.send(narrow(x[middle:]), near=1))
+
+    def along_far(x):
+        size = x.shape[0] // grid.far
         parts = [
-            grid.send(x[d * rows_dev : (d + 1) * rows_dev].astype(jnp.bfloat16), far=d)
-            for d in range(1, grid.far)
+            grid.send(narrow(x[d * size : (d + 1) * size]), far=d) for d in range(1, grid.far)
         ]
-        x = x[:rows_dev]
+        x = x[:size]
         for part in parts:
-            x = x + part.astype(jnp.float32)
-        sums.append(x)
-    return jnp.concatenate(sums, axis=1)
-
-
-def project_kernel(first, last, count, *refs):
-    parts, (wq, wk, wv), refs = refs[:count], refs[count : count + 3], refs[count + 3 :]
+            x = x + wide(part)
+        return x
+
+    away, xb = start(rows_b, w_out[:, half:])
+    _, xa = start(after(rows_a, away), w_out[:, :half])
+    xb = along_near(along_far(xb))
+    xa = along_far(along_near(xa))
+    return jnp.concatenate([xa, xb], axis=1)
+
+
+def norm_kernel(x, gain, *outs):
+    inputs = x[...].astype(jnp.float32)
+    factor = lax.rsqrt(jnp.mean(inputs * inputs, axis=1, keepdims=True) + epsilon)
+    normed = (inputs * factor * gain[...]).astype(jnp.bfloat16)
+    start = 0
+    for out in outs:
+        out[...] = normed[:, start : start + out.shape[1]]
+        start += out.shape[1]
+
+
+def norm(x, gain, widths):
+    vmem = pl.BlockSpec(memory_space=pltpu.VMEM)
+    return pl.pallas_call(
+        norm_kernel,
+        in_specs=[vmem, vmem],
+        out_specs=[vmem] * len(widths),
+        out_shape=[jax.ShapeDtypeStruct((x.shape[0], w), jnp.bfloat16) for w in widths],
+        compiler_params=pltpu.CompilerParams(vmem_limit_bytes=16 * 2**20),
+        name="norm",
+    )(x, gain.reshape(1, -1))
+
+
+def project_kernel(first, last, order, *refs):
+    count = len(refs) - 4 - (not first) - last
+    parts, (wq, w_kv), refs = refs[:count], refs[count : count + 2], refs[count + 2 :]
     if not first:
         before, refs = refs[0], refs[1:]
     if last:
         place, refs = refs[0], refs[1:]
     out, total = refs
     step = pl.program_id(0)
-    per_query = wq.shape[1]
+    block, per_query = wq.shape
 
     @pl.when(step == 0)
     def _():
         total[...] = jnp.zeros_like(total) if first else before[...]
 
-    x = jnp.concatenate([part[...] for part in parts], axis=0)
-    pieces = [wk[...], wv[...]]
-    spare = total.shape[1] - per_query - 2 * wk.shape[0]
-    if spare:
-        pieces.append(jnp.zeros((spare, wk.shape[1]), wk.dtype))
-    kv = jnp.concatenate(pieces, axis=0)
-    total[:, :per_query] += jnp.dot(x, wq[...], preferred_element_type=jnp.float32)
-    total[:, per_query:] += lax.dot_general(
-        x, kv, (((1,), (1,)), ((), ())), preferred_element_type=jnp.float32
-    )
+    here = pl.ds(pl.multiple_of(step * block, block), block)
+    x = jnp.concatenate([part[:, here] for part in parts], axis=0)
+    products = [
+        jnp.dot(x, wq[...], preferred_element_type=jnp.float32),
+        lax.dot_general(x, w_kv[...], (((1,), (1,)), ((), ())), preferred_element_type=jnp.float32),
+    ]
+    size = x.shape[0] // len(order)
+    for product, columns in zip(products, (slice(0, per_query), slice(per_query, None))):
+        for i, place_i in enumerate(order):
+            total[place_i * size : (place_i + 1) * size, columns] += product[
+                i * size : (i + 1) * size
+            ]
 
     @pl.when(step == pl.num_programs(0) - 1)
     def _():
@@ -136,35 +188,33 @@
             out[...] = total[...]
 
 
-def project(chunk, chunks, parts, w_query, w_key_t, w_value_t, before, place, slots, row_width):
+def project(start, parts, order, w_query, w_kv_t, before, place, slots):
+    row_width = w_query.shape[1] + w_kv_t.shape[0]
     width = parts[0].shape[1]
-    block = min(1024, width)
-    steps = width // block
-    start = chunk * steps
+    block = 1024
     rows = sum(part.shape[0] for part in parts)
-    first, last = chunk == 0, chunk == chunks - 1
-    whole = lambda i: (0, 0)
-    args = [*parts, w_query, w_key_t, w_value_t]
-    specs = [
-        *[pl.BlockSpec((part.shape[0], block), lambda i: (0, i)) for part in parts],
-        pl.BlockSpec((block, w_query.shape[1]), lambda i: (start + i, 0)),
-        pl.BlockSpec((w_key_t.shape[0], block), lambda i: (0, start + i)),
-        pl.BlockSpec((w_value_t.shape[0], block), lambda i: (0, start + i)),
+    first, last = before is None, place is not None
+    vmem = pl.BlockSpec(memory_space=pltpu.VMEM)
+    args = [*parts, w_query, w_kv_t]
+    specs = [vmem] * len(parts)
+    specs += [
+        pl.BlockSpec((block, w_query.shape[1]), lambda i: (start // block + i, 0)),
+        pl.BlockSpec((w_kv_t.shape[0], block), lambda i: (0, start // block + i)),
     ]
     if not first:
         args.append(before)
-        specs.append(pl.BlockSpec(before.shape, whole))
+        specs.append(vmem)
     if last:
         args.append(place.reshape(1, rows))
-        specs.append(pl.BlockSpec((1, rows), whole))
+        specs.append(vmem)
         out = jax.ShapeDtypeStruct((slots, row_width), jnp.bfloat16)
     else:
         out = jax.ShapeDtypeStruct((rows, row_width), jnp.float32)
     return pl.pallas_call(
-        functools.partial(project_kernel, first, last, len(parts)),
-        grid=(steps,),
+        functools.partial(project_kernel, first, last, order),
+        grid=(width // block,),
         in_specs=specs,
-        out_specs=pl.BlockSpec(out.shape, whole),
+        out_specs=vmem,
         out_shape=out,
         scratch_shapes=[pltpu.VMEM((rows, row_width), jnp.float32)],
         compiler_params=pltpu.CompilerParams(vmem_limit_bytes=48 * 2**20),
@@ -188,6 +238,9 @@
     key_pages,
     value_pages,
     out,
+    key_pool,
+    value_pool,
+    sems,
     key_new,
     query_rot,
     value_own,
@@ -207,6 +260,13 @@
     batches = query_rot.shape[1]
     batch = slots // batches
 
+    cuts = 4
+    size = key_pages.shape[0] // cuts
+    for i, (pool, on_chip) in enumerate(((key_pages, key_pool), (value_pages, value_pool))):
+        for cut in range(cuts):
+            part = pl.ds(cut * size, size)
+            pltpu.make_async_copy(pool.at[part], on_chip.at[part], sems.at[i]).start()
+
     def held(pool, slot, columns):
         return [pool[table[slot, j], :, columns] for j in range(pages)]
 
@@ -249,6 +309,7 @@
         jnp.int32, (columns, columns), 1
     )
 
+    pltpu.make_async_copy(key_pool, key_pool, sems.at[0]).wait()
     own_chances = {}
     for b in range(batches):
         valid = row < lengths[b]
@@ -261,7 +322,7 @@
             columns_p = slice(p * 2 * HEAD, (p + 1) * 2 * HEAD)
             keys = []
             for s in range(batch):
-                keys += held(key_pages, b * batch + s, columns_p)
+                keys += held(key_pool, b * batch + s, columns_p)
             keys.append(key_new[:, columns_p])
             products = jnp.dot(
                 jnp.concatenate(keys, axis=0), wide, preferred_element_type=jnp.float32
@@ -282,12 +343,13 @@
                 jnp.where(same, own_chance, 0.0), axis=1, keepdims=True
             )
 
+    pltpu.make_async_copy(value_pool, value_pool, sems.at[1]).wait()
     for b in range(batches):
         for s in range(batch):
             for p in range(pairs):
                 mine = chance[p, b, pl.ds(s, pair, stride=batch)].astype(jnp.bfloat16)
                 columns_p = slice(p * 2 * HEAD, (p + 1) * 2 * HEAD)
-                values = held(value_pages, b * batch + s, columns_p)
+                values = held(value_pool, b * batch + s, columns_p)
                 both = jnp.dot(
                     mine, jnp.concatenate(values, axis=0), preferred_element_type=jnp.float32
                 )
@@ -326,19 +388,23 @@
     lengths = jnp.tile(lengths.reshape(batches, 1, batch), (1, 1, pair))
     smem = pl.BlockSpec(memory_space=pltpu.SMEM)
     vmem = pl.BlockSpec(memory_space=pltpu.VMEM)
+    hbm = pl.BlockSpec(memory_space=pl.ANY)
     return pl.pallas_call(
         functools.partial(attend_kernel, per_query, per_key),
-        in_specs=[smem, vmem, vmem, vmem, vmem, vmem, vmem],
+        in_specs=[smem, vmem, vmem, vmem, vmem, hbm, hbm],
         out_specs=vmem,
         out_shape=jax.ShapeDtypeStruct((owners, slots, per_query), jnp.bfloat16),
         scratch_shapes=[
+            pltpu.VMEM(key_pages.shape, jnp.bfloat16),
+            pltpu.VMEM(value_pages.shape, jnp.bfloat16),
+            pltpu.SemaphoreType.DMA((2,)),
             pltpu.VMEM((slots, kv_width), jnp.bfloat16),
             pltpu.VMEM((pairs, batches, columns, HEAD), jnp.float32),
             pltpu.VMEM((kv_heads, slots, HEAD), jnp.float32),
             pltpu.VMEM((pairs, batches, columns, span), jnp.float32),
             pltpu.VMEM((pairs, batches, columns, HEAD), jnp.float32),
         ],
-        compiler_params=pltpu.CompilerParams(vmem_limit_bytes=44 * 2**20),
+        compiler_params=pltpu.CompilerParams(vmem_limit_bytes=52 * 2**20),
         cost_estimate=pl.CostEstimate(
             flops=8 * slots * heads * span * HEAD,
             bytes_accessed=4 * slots * span * kv_width,
@@ -372,9 +438,8 @@
     width = hidden_in.shape[1]
     all_slots = owners * slot_count
 
-    inputs = hidden_in.astype(jnp.float32)
-    factor = lax.rsqrt(jnp.mean(inputs * inputs, axis=1, keepdims=True) + epsilon)
-    normed = (inputs * factor * norm_gain).astype(jnp.bfloat16)
+    unit = width // 8
+    xa, xb = norm(hidden_in, norm_gain, (5 * unit, 3 * unit))
 
     order = jnp.arange(requests, dtype=jnp.int32)
     earlier = (kv_owner[:, None] == kv_owner[None, :]) & (order[None, :] < order[:, None])
@@ -390,6 +455,9 @@
     place_in = reordered(grid.blocks(-1))
     place_out = reordered(grid.blocks(1))
     route_out = (place_out[:, None] == slots[None, :]).astype(jnp.bfloat16)
+    crossed = grid.crossed()
+    crossed_out = place_out.reshape(owners, rows_dev)[np.array(crossed)].reshape(requests)
+    route_crossed = (crossed_out[:, None] == slots[None, :]).astype(jnp.bfloat16)
 
     mine = lax.axis_index(AXES) * slot_count + jnp.arange(slot_count, dtype=jnp.int32)
     lengths = jnp.sum(jnp.where(place[:, None] == mine[None, :], cached[:, None], 0), axis=0)
@@ -402,18 +470,17 @@
     cosine = jnp.concatenate([cosine_part, cosine_part], axis=1)
     sine = jnp.concatenate([-sine_part, sine_part], axis=1)
 
-    chunks = 2
-    step = width // chunks
-    total = line = None
-    for i in range(chunks):
-        x = normed[:, i * step : (i + 1) * step]
-        if i:
-            x = after(x, line)
-        parts = gather_rows(grid, x)
-        line = parts[0]
-        total = project(
-            i, chunks, parts, w_query, w_key.T, w_value.T, total, place_in, all_slots, row_width
-        )
+    pieces = [w_key.T, w_value.T]
+    spare = row_width - per_query - 2 * per_key
+    if spare:
+        pieces.append(jnp.zeros((spare, width), w_key.dtype))
+    w_kv_t = jnp.concatenate(pieces, axis=0)
+    parts_a, parts_b, (w_kv_t, place_in, place_out, cosine, sine) = gather_rows(
+        grid, xa, xb, (w_kv_t, place_in, place_out, cosine, sine)
+    )
+    plain = list(range(owners))
+    total = project(0, parts_a, plain, w_query, w_kv_t, None, None, all_slots)
+    total = project(5 * unit, parts_b, crossed, w_query, w_kv_t, total, place_in, all_slots)
     outbound = total.reshape(owners, slot_count, row_width)
     inbound = lax.all_to_all(outbound, AXES, split_axis=0, concat_axis=0, tiled=True)
     attended = attend(
@@ -429,10 +496,10 @@
     )
     returned = lax.all_to_all(attended, AXES, split_axis=0, concat_axis=0, tiled=True)
     returned = returned.reshape(all_slots, per_query)
-    head_rows = jnp.dot(route_out, returned, preferred_element_type=jnp.float32)
-    head_rows = head_rows.astype(jnp.bfloat16)
-    summed = scatter_sum(grid, head_rows, w_out, chunks)
-    return (inputs + summed).astype(jnp.bfloat16)
+    rows_a = narrow(jnp.dot(route_out, returned, preferred_element_type=jnp.float32))
+    rows_b = narrow(jnp.dot(route_crossed, returned, preferred_element_type=jnp.float32))
+    summed = scatter_sum(grid, rows_a, rows_b, w_out)
+    return narrow(wide(hidden_in) + summed)
 
 
 def solution(mesh):

time: 112 us -> 105 us (0.938)
  waiting for transfers between devices: 48.1 us -> 43.4 us
  local copies, waits for them, and re-layouts: 8.37 us -> 3.8 us
  Pallas kernels: 12.2 us -> 15.3 us
    unnamed x21 -> x10, local copies, waits for them, and re-layouts: 6.86 us -> 1.68 us
    ppermute x22 -> x24, waiting for transfers between devices: 27.8 us -> 23.4 us  [send(): return lax.ppermute(x, AXES, self.perm(far, near, core))]
    pallas_call x1, Pallas kernels: 3.4 us -> 5.98 us  [attend(): pl.pallas_call(functools.partial(attend_kernel, per_query, per_key), in_s...]
    concatenate x1 -> x3, other arithmetic: 0.02 us -> 1.71 us  [the longest x1 1.68 us: on_device(): w_kv_t = jnp.concatenate(pieces, axis=0)]
    pallas_call x2 -> x3, Pallas kernels: 8.81 us -> 9.32 us  [the longest x2 9.14 us: project(): pl.pallas_call(functools.partial(project_kernel, first, last, order), gri...]
    ppermute x22 -> x24, starting transfers between devices: 22.3 us -> 22.3 us  [send(): return lax.ppermute(x, AXES, self.perm(far, near, core))]
  transfers between devices with their start and end apart: 24 -> 26, of which waited for: 12 -> 11; matrix products, arithmetic and copies ran while one was open for 6% -> 10% of each run, Pallas kernels for 4% -> 5%
where the time goes in v5:
time: 105 us
  waiting for transfers between devices  43.4 us (41%)
  starting transfers between devices  29.4 us (28%)
  Pallas kernels  15.3 us (15%)
  other arithmetic  6.23 us (6%)
  matrix products  6.2 us (6%)
  local copies, waits for them, and re-layouts  3.8 us (4%)
    ppermute x24, waiting for transfers between devices, send(): return lax.ppermute(x, AXES, self.perm(far, near, core))  23.4 us
    ppermute x24, starting transfers between devices, send(): return lax.ppermute(x, AXES, self.perm(far, near, core))  22.3 us
    all_to_all x1, waiting for transfers between devices, on_device(): lax.all_to_all(outbound, AXES, split_axis=0, concat_axis=0, tiled=True)  10.8 us
    all_to_all x1, waiting for transfers between devices, on_device(): lax.all_to_all(attended, AXES, split_axis=0, concat_axis=0, tiled=True)  9.24 us
    pallas_call x2, Pallas kernels, project(): pl.pallas_call(functools.partial(project_kernel, first, last, order), gri...  9.14 us
    pallas_call x1, Pallas kernels, attend(): pl.pallas_call(functools.partial(attend_kernel, per_query, per_key), in_s...  5.98 us
    dot_general x2, matrix products, start(): x = jnp.dot(rows, w, preferred_element_type=jnp.float32)  5.97 us
    all_to_all x1, starting transfers between devices, on_device(): lax.all_to_all(attended, AXES, split_axis=0, concat_axis=0, tiled=True)  3.54 us
  transfers between devices with their start and end apart: 26, of which 11 were waited for; matrix products, arithmetic and copies ran while one was open for 10% of the time, Pallas kernels for 5%

profile of v5, /device:TPU:0, one launch (start us, length us, event | category | flops | bytes accessed | tf_op | source)
XLA Modules:
  0.0 104.8 jit_solution(4860143042494858170)
XLA Ops:
  1.9 5.1 %collective-permute-start.2 = (bf16[8,5120]{1,0:T(8,128)(2,1)S(1)}, bf16[8,5120]{1,0:T(8,128)(2,1)S(1)}, u32[]{:S(2)}, u32[]{:S(2)}) collective-permute-start(bf16[8,5120]{1,0:T(8,128)(2,1)S(1)} %get-tuple-element.18), channel_id=1, source_target_pairs={{0,12},{1,13},{2,14},{3,15},{4,0},{5,1},{6,2},{7,3},{8,4},{9,5},{1... | collective-permute-start | bytes 245768 | tf_op jit(solution)/shard_map/ppermute | solution.py:41
  7.0 1.0 collective-permute-start
  8.0 1.5 %collective-permute-start.3 = (bf16[8,3072]{1,0:T(8,128)(2,1)S(1)}, bf16[8,3072]{1,0:T(8,128)(2,1)S(1)}, u32[]{:S(2)}, u32[]{:S(2)}) collective-permute-start(bf16[8,3072]{1,0:T(8,128)(2,1)S(1)} %get-tuple-element.19), channel_id=1, source_target_pairs={{0,2},{1,3},{2,0},{3,1},{4,6},{5,7},{6,4},{7,5},{8,10},{9,11},{10,... | collective-permute-start | bytes 147464 | tf_op jit(solution)/shard_map/ppermute | solution.py:41
  12.9 1.7 %pad_maximum_fusion.refs_5_.refs_9_ = bf16[128,8192]{1,0:T(8,128)(2,1)S(1)} fusion(bf16[64,8192]{1,0:T(8,128)(2,1)} %bitcast.24, bf16[64,8192]{1,0:T(8,128)(2,1)} %bitcast.25), kind=kLoop, calls=%fused_computation.5 | loop fusion | flops 4194304 | bytes 4194304 | tf_op jit(solution)/shard_map/concatenate | solution.py:477
  16.2 2.7 %collective-permute-start.7 = (bf16[16,3072]{1,0:T(8,128)(2,1)S(1)}, bf16[16,3072]{1,0:T(8,128)(2,1)S(1)}, u32[]{:S(2)}, u32[]{:S(2)}) collective-permute-start(bf16[16,3072]{1,0:T(8,128)(2,1)S(1)} %pad_maximum_fusion.2.refs_0_), channel_id=1, source_target_pairs={{0,12},{1,13},{2,14},{3,15},{4,0},{5,1},{6,2},{7,3},{8,4},{9,5},{1... | collective-permute-start | bytes 294920 | tf_op jit(solution)/shard_map/ppermute | solution.py:41
  18.9 1.1 %collective-permute-start.6 = (bf16[16,3072]{1,0:T(8,128)(2,1)S(1)}, bf16[16,3072]{1,0:T(8,128)(2,1)S(1)}, u32[]{:S(2)}, u32[]{:S(2)}) collective-permute-start(bf16[16,3072]{1,0:T(8,128)(2,1)S(1)} %pad_maximum_fusion.2.refs_0_), channel_id=1, source_target_pairs={{0,8},{1,9},{2,10},{3,11},{4,12},{5,13},{6,14},{7,15},{8,0},{9,1},... | collective-permute-start | bytes 294920 | tf_op jit(solution)/shard_map/ppermute | solution.py:41
  20.6 1.4 %collective-permute-done.7.refs_3_ = bf16[16,3072]{1,0:T(8,128)(2,1)S(1)} collective-permute-done((bf16[16,3072]{1,0:T(8,128)(2,1)S(1)}, bf16[16,3072]{1,0:T(8,128)(2,1)S(1)}, u32[]{:S(2)}, u32[]{:S(2)}) %collective-permute-start.7) | collective-permute-done | bytes 98336 | tf_op jit(solution)/shard_map/ppermute | solution.py:41
  22.0 5.7 %collective-permute-done.6.refs_2_ = bf16[16,3072]{1,0:T(8,128)(2,1)S(1)} collective-permute-done((bf16[16,3072]{1,0:T(8,128)(2,1)S(1)}, bf16[16,3072]{1,0:T(8,128)(2,1)S(1)}, u32[]{:S(2)}, u32[]{:S(2)}) %collective-permute-start.6) | collective-permute-done | bytes 98336 | tf_op jit(solution)/shard_map/ppermute | solution.py:41
  29.4 4.9 %project.2.refs_10_ = f32[128,640]{1,0:T(8,128)S(1)} custom-call(bf16[32,5120]{1,0:T(8,128)(2,1)S(1)} %pad_maximum_fusion.1.refs_0_, bf16[32,5120]{1,0:T(8,128)(2,1)S(1)} %collective-permute-done.4.refs_1_, bf16[32,5120]{1,0:T(8,128)(2,1)S(1)} %collective-permute-done.12.refs_2_, bf16[32,5120]{1,0:T(8,128)(2,1)S(1)} %collective-permute-done.13.refs_3_, ...), custom_call_target="tpu_custom_call" | custom-call | flops 838860800 | bytes 6553600 | tf_op jit(solution)/shard_map/project/pallas_call | solution.py:213
  34.4 4.2 %project.3 = bf16[256,640]{1,0:T(8,128)(2,1)} custom-call(bf16[16,3072]{1,0:T(8,128)(2,1)S(1)} %pad_maximum_fusion.2.refs_0_, bf16[16,3072]{1,0:T(8,128)(2,1)S(1)} %collective-permute-done.5.refs_1_, bf16[16,3072]{1,0:T(8,128)(2,1)S(1)} %collective-permute-done.6.refs_2_, bf16[16,3072]{1,0:T(8,128)(2,1)S(1)} %collective-permute-done.7.refs_3_, ...), custom_call_target="tpu_custom_call" | custom-call | flops 503316480 | bytes 3932160 | tf_op jit(solution)/shard_map/project/pallas_call | solution.py:213
  38.6 3.5 %all-to-all-start = ((bf16[16,16,640]{2,1,0:T(8,128)(2,1)}), bf16[16,16,640]{2,1,0:T(8,128)(2,1)S(1)}, u32[]{:S(2)}, u32[]{:S(2)}) async-start(bf16[16,16,640]{2,1,0:T(8,128)(2,1)} %bitcast.8), calls=%async_computation | async-start | bytes 655360 | tf_op jit(solution)/shard_map/all_to_all | solution.py:485
  42.4 10.8 %all-to-all-done.inbound = bf16[16,16,640]{2,1,0:T(8,128)(2,1)S(1)} async-done(((bf16[16,16,640]{2,1,0:T(8,128)(2,1)}), bf16[16,16,640]{2,1,0:T(8,128)(2,1)S(1)}, u32[]{:S(2)}, u32[]{:S(2)}) %all-to-all-start) | async-done | bytes 327712 | tf_op jit(solution)/shard_map/all_to_all | solution.py:485
  53.2 6.0 %attend.1 = bf16[16,16,512]{2,1,0:T(8,128)(2,1)} custom-call(s32[16,4]{1,0:T(8,128)S(1)} %copy.20.table, s32[2,1,128]{2,1,0:T(1,128)S(1)} %bitcast.18, bf16[16,16,640]{2,1,0:T(8,128)(2,1)S(1)} %all-to-all-done.inbound, f32[16,128]{1,0:T(8,128)S(1)} %get-tuple-element.28.cosine, f32[16,128]{1,0:T(8,128)S(1)} %get-tuple-element.29.sine, ...), custom_call_target="tpu_custom_call" | custom-call | flops 134217728 | bytes 8388608 | tf_op jit(solution)/shard_map/attend/pallas_call | solution.py:392
  59.2 3.5 %all-to-all-start.1 = ((bf16[16,16,512]{2,1,0:T(8,128)(2,1)}), bf16[16,16,512]{2,1,0:T(8,128)(2,1)S(1)}, u32[]{:S(2)}, u32[]{:S(2)}) async-start(bf16[16,16,512]{2,1,0:T(8,128)(2,1)} %attend.1), calls=%async_computation.1 | async-start | bytes 524288 | tf_op jit(solution)/shard_map/all_to_all | solution.py:497
  63.5 9.2 %all-to-all-done.1 = bf16[16,16,512]{2,1,0:T(8,128)(2,1)S(1)} async-done(((bf16[16,16,512]{2,1,0:T(8,128)(2,1)}), bf16[16,16,512]{2,1,0:T(8,128)(2,1)S(1)}, u32[]{:S(2)}, u32[]{:S(2)}) %all-to-all-start.1) | async-done | bytes 262176 | tf_op jit(solution)/shard_map/all_to_all | solution.py:497
  72.7 3.1 %fusion.2 = f32[128,4096]{1,0:T(8,128)S(1)} fusion(bf16[512,8192]{1,0:T(8,128)(2,1)} %param.20, bf16[256,512]{1,0:T(8,128)(2,1)S(1)} %bitcast.22, s32[128]{0:T(128)S(1)} %eq.112), kind=kOutput, calls=%fused_computation.3 | convolution fusion | flops 570523648 | bytes 6554112 | tf_op jit(solution)/shard_map/dot_general | solution.py:102
  76.2 2.9 %fusion = f32[128,4096]{1,0:T(8,128)S(1)} fusion(bf16[128,512]{1,0:T(8,128)(2,1)S(1)} %convolution_convert_fusion.1, bf16[512,8192]{1,0:T(8,128)(2,1)} %param.20), kind=kOutput, calls=%fused_computation.1 | convolution fusion | flops 536870912 | bytes 6422528 | tf_op jit(solution)/shard_map/dot_general | solution.py:102
  80.2 3.6 %collective-permute-start.22 = (bf16[16,4096]{1,0:T(8,128)(2,1)S(1)}, bf16[16,4096]{1,0:T(8,128)(2,1)S(1)}, u32[]{:S(2)}, u32[]{:S(2)}) collective-permute-start(bf16[16,4096]{1,0:T(8,128)(2,1)S(1)} %get-tuple-element.38), channel_id=1, source_target_pairs={{0,12},{1,13},{2,14},{3,15},{4,0},{5,1},{6,2},{7,3},{8,4},{9,5},{1... | collective-permute-start | bytes 393224 | tf_op jit(solution)/shard_map/ppermute | solution.py:41
  84.1 4.1 %collective-permute-done.20 = bf16[16,4096]{1,0:T(8,128)(2,1)S(1)} collective-permute-done((bf16[16,4096]{1,0:T(8,128)(2,1)S(1)}, bf16[16,4096]{1,0:T(8,128)(2,1)S(1)}, u32[]{:S(2)}, u32[]{:S(2)}) %collective-permute-start.20) | collective-permute-done | bytes 131104 | tf_op jit(solution)/shard_map/ppermute | solution.py:41
  88.2 1.2 %collective-permute-done.22 = bf16[16,4096]{1,0:T(8,128)(2,1)S(1)} collective-permute-done((bf16[16,4096]{1,0:T(8,128)(2,1)S(1)}, bf16[16,4096]{1,0:T(8,128)(2,1)S(1)}, u32[]{:S(2)}, u32[]{:S(2)}) %collective-permute-start.22) | collective-permute-done | bytes 131104 | tf_op jit(solution)/shard_map/ppermute | solution.py:41
  89.3 5.2 %collective-permute-done.21 = bf16[16,4096]{1,0:T(8,128)(2,1)S(1)} collective-permute-done((bf16[16,4096]{1,0:T(8,128)(2,1)S(1)}, bf16[16,4096]{1,0:T(8,128)(2,1)S(1)}, u32[]{:S(2)}, u32[]{:S(2)}) %collective-permute-start.21) | collective-permute-done | bytes 131104 | tf_op jit(solution)/shard_map/ppermute | solution.py:41
  95.0 3.8 %collective-permute-start.18 = (bf16[8,4096]{1,0:T(8,128)(2,1)S(1)}, bf16[8,4096]{1,0:T(8,128)(2,1)S(1)}, u32[]{:S(2)}, u32[]{:S(2)}) collective-permute-start(bf16[8,4096]{1,0:T(8,128)(2,1)S(1)} %get-tuple-element.41), channel_id=1, source_target_pairs={{0,12},{1,13},{2,14},{3,15},{4,0},{5,1},{6,2},{7,3},{8,4},{9,5},{1... | collective-permute-start | bytes 196616 | tf_op jit(solution)/shard_map/ppermute | solution.py:41
  99.0 2.4 %collective-permute-done.16 = bf16[8,4096]{1,0:T(8,128)(2,1)S(1)} collective-permute-done((bf16[8,4096]{1,0:T(8,128)(2,1)S(1)}, bf16[8,4096]{1,0:T(8,128)(2,1)S(1)}, u32[]{:S(2)}, u32[]{:S(2)}) %collective-permute-start.16) | collective-permute-done | bytes 65568 | tf_op jit(solution)/shard_map/ppermute | solution.py:41
  101.4 2.6 %collective-permute-done.17 = bf16[8,4096]{1,0:T(8,128)(2,1)S(1)} collective-permute-done((bf16[8,4096]{1,0:T(8,128)(2,1)S(1)}, bf16[8,4096]{1,0:T(8,128)(2,1)S(1)}, u32[]{:S(2)}, u32[]{:S(2)}) %collective-permute-start.17) | collective-permute-done | bytes 65568 | tf_op jit(solution)/shard_map/ppermute | solution.py:41
  (84 shorter events, 12.9 us)
Async XLA Ops:
  1.9 13.4 %collective-permute-start.2 = (bf16[8,5120]{1,0:T(8,128)(2,1)S(1)}, bf16[8,5120]{1,0:T(8,128)(2,1)S(1)}, u32[]{:S(2)}, u32[]{:S(2)}) collective-permute-start(bf16[8,5120]{1,0:T(8,128)(2,1)S(1)} %get-tuple-element.18), channel_id=1, source_target_pairs={{0,12},{1,13},{2,14},{3,15},{4,0},{5,1},{6,2},{7,3},{8,4},{9,5},{1... | collective-permute-start | bytes 245768 | tf_op jit(solution)/shard_map/ppermute | solution.py:41
  7.0 8.3 %collective-permute-start.1 = (bf16[8,5120]{1,0:T(8,128)(2,1)S(1)}, bf16[8,5120]{1,0:T(8,128)(2,1)S(1)}, u32[]{:S(2)}, u32[]{:S(2)}) collective-permute-start(bf16[8,5120]{1,0:T(8,128)(2,1)S(1)} %get-tuple-element.18), channel_id=1, source_target_pairs={{0,8},{1,9},{2,10},{3,11},{4,12},{5,13},{6,14},{7,15},{8,0},{9,1},... | collective-permute-start | bytes 245768 | tf_op jit(solution)/shard_map/ppermute | solution.py:41
  7.0 8.3 %collective-permute-start = (bf16[8,5120]{1,0:T(8,128)(2,1)S(1)}, bf16[8,5120]{1,0:T(8,128)(2,1)S(1)}, u32[]{:S(2)}, u32[]{:S(2)}) collective-permute-start(bf16[8,5120]{1,0:T(8,128)(2,1)S(1)} %get-tuple-element.18), channel_id=1, source_target_pairs={{0,4},{1,5},{2,6},{3,7},{4,8},{5,9},{6,10},{7,11},{8,12},{9,13},{1... | collective-permute-start | bytes 245768 | tf_op jit(solution)/shard_map/ppermute | solution.py:41
  8.0 7.3 %collective-permute-start.3 = (bf16[8,3072]{1,0:T(8,128)(2,1)S(1)}, bf16[8,3072]{1,0:T(8,128)(2,1)S(1)}, u32[]{:S(2)}, u32[]{:S(2)}) collective-permute-start(bf16[8,3072]{1,0:T(8,128)(2,1)S(1)} %get-tuple-element.19), channel_id=1, source_target_pairs={{0,2},{1,3},{2,0},{3,1},{4,6},{5,7},{6,4},{7,5},{8,10},{9,11},{10,... | collective-permute-start | bytes 147464 | tf_op jit(solution)/shard_map/ppermute | solution.py:41
  15.4 12.4 %collective-permute-start.4 = (bf16[32,5120]{1,0:T(8,128)(2,1)S(1)}, bf16[32,5120]{1,0:T(8,128)(2,1)S(1)}, u32[]{:S(2)}, u32[]{:S(2)}) collective-permute-start(bf16[32,5120]{1,0:T(8,128)(2,1)S(1)} %pad_maximum_fusion.1.refs_0_), channel_id=1, source_target_pairs={{0,2},{1,3},{2,0},{3,1},{4,6},{5,7},{6,4},{7,5},{8,10},{9,11},{10,... | collective-permute-start | bytes 983048 | tf_op jit(solution)/shard_map/ppermute | solution.py:41
  16.2 5.8 %collective-permute-start.7 = (bf16[16,3072]{1,0:T(8,128)(2,1)S(1)}, bf16[16,3072]{1,0:T(8,128)(2,1)S(1)}, u32[]{:S(2)}, u32[]{:S(2)}) collective-permute-start(bf16[16,3072]{1,0:T(8,128)(2,1)S(1)} %pad_maximum_fusion.2.refs_0_), channel_id=1, source_target_pairs={{0,12},{1,13},{2,14},{3,15},{4,0},{5,1},{6,2},{7,3},{8,4},{9,5},{1... | collective-permute-start | bytes 294920 | tf_op jit(solution)/shard_map/ppermute | solution.py:41
  18.9 8.8 %collective-permute-start.6 = (bf16[16,3072]{1,0:T(8,128)(2,1)S(1)}, bf16[16,3072]{1,0:T(8,128)(2,1)S(1)}, u32[]{:S(2)}, u32[]{:S(2)}) collective-permute-start(bf16[16,3072]{1,0:T(8,128)(2,1)S(1)} %pad_maximum_fusion.2.refs_0_), channel_id=1, source_target_pairs={{0,8},{1,9},{2,10},{3,11},{4,12},{5,13},{6,14},{7,15},{8,0},{9,1},... | collective-permute-start | bytes 294920 | tf_op jit(solution)/shard_map/ppermute | solution.py:41
  20.0 7.7 %collective-permute-start.5 = (bf16[16,3072]{1,0:T(8,128)(2,1)S(1)}, bf16[16,3072]{1,0:T(8,128)(2,1)S(1)}, u32[]{:S(2)}, u32[]{:S(2)}) collective-permute-start(bf16[16,3072]{1,0:T(8,128)(2,1)S(1)} %pad_maximum_fusion.2.refs_0_), channel_id=1, source_target_pairs={{0,4},{1,5},{2,6},{3,7},{4,8},{5,9},{6,10},{7,11},{8,12},{9,13},{1... | collective-permute-start | bytes 294920 | tf_op jit(solution)/shard_map/ppermute | solution.py:41
  20.4 8.4 %collective-permute-start.12 = (bf16[32,5120]{1,0:T(8,128)(2,1)S(1)}, bf16[32,5120]{1,0:T(8,128)(2,1)S(1)}, u32[]{:S(2)}, u32[]{:S(2)}) collective-permute-start(bf16[32,5120]{1,0:T(8,128)(2,1)S(1)} %pad_maximum_fusion.1.refs_0_), channel_id=1, source_target_pairs={{0,1},{1,0},{2,3},{3,2},{4,5},{5,4},{6,7},{7,6},{8,9},{9,8},{10,11... | collective-permute-start | bytes 983048 | tf_op jit(solution)/shard_map/ppermute | solution.py:41
  27.8 6.5 %collective-permute-start.8 = (bf16[16,3072]{1,0:T(8,128)(2,1)S(1)}, bf16[16,3072]{1,0:T(8,128)(2,1)S(1)}, u32[]{:S(2)}, u32[]{:S(2)}) collective-permute-start(bf16[16,3072]{1,0:T(8,128)(2,1)S(1)} %pad_maximum_fusion.2.refs_0_), channel_id=1, source_target_pairs={{0,1},{1,0},{2,3},{3,2},{4,5},{5,4},{6,7},{7,6},{8,9},{9,8},{10,11... | collective-permute-start | bytes 294920 | tf_op jit(solution)/shard_map/ppermute | solution.py:41
  28.3 6.1 %collective-permute-start.9 = (bf16[16,3072]{1,0:T(8,128)(2,1)S(1)}, bf16[16,3072]{1,0:T(8,128)(2,1)S(1)}, u32[]{:S(2)}, u32[]{:S(2)}) collective-permute-start(bf16[16,3072]{1,0:T(8,128)(2,1)S(1)} %collective-permute-done.5.refs_1_), channel_id=1, source_target_pairs={{0,1},{1,0},{2,3},{3,2},{4,5},{5,4},{6,7},{7,6},{8,9},{9,8},{10,11... | collective-permute-start | bytes 294920 | tf_op jit(solution)/shard_map/ppermute | solution.py:41
  28.3 6.0 %collective-permute-start.10 = (bf16[16,3072]{1,0:T(8,128)(2,1)S(1)}, bf16[16,3072]{1,0:T(8,128)(2,1)S(1)}, u32[]{:S(2)}, u32[]{:S(2)}) collective-permute-start(bf16[16,3072]{1,0:T(8,128)(2,1)S(1)} %collective-permute-done.6.refs_2_), channel_id=1, source_target_pairs={{0,1},{1,0},{2,3},{3,2},{4,5},{5,4},{6,7},{7,6},{8,9},{9,8},{10,11... | collective-permute-start | bytes 294920 | tf_op jit(solution)/shard_map/ppermute | solution.py:41
  28.8 5.6 %collective-permute-start.11 = (bf16[16,3072]{1,0:T(8,128)(2,1)S(1)}, bf16[16,3072]{1,0:T(8,128)(2,1)S(1)}, u32[]{:S(2)}, u32[]{:S(2)}) collective-permute-start(bf16[16,3072]{1,0:T(8,128)(2,1)S(1)} %collective-permute-done.7.refs_3_), channel_id=1, source_target_pairs={{0,1},{1,0},{2,3},{3,2},{4,5},{5,4},{6,7},{7,6},{8,9},{9,8},{10,11... | collective-permute-start | bytes 294920 | tf_op jit(solution)/shard_map/ppermute | solution.py:41
  38.6 14.6 %all-to-all-start = ((bf16[16,16,640]{2,1,0:T(8,128)(2,1)}), bf16[16,16,640]{2,1,0:T(8,128)(2,1)S(1)}, u32[]{:S(2)}, u32[]{:S(2)}) async-start(bf16[16,16,640]{2,1,0:T(8,128)(2,1)} %bitcast.8), calls=%async_computation | async-start | bytes 655360 | tf_op jit(solution)/shard_map/all_to_all | solution.py:485
  59.2 13.6 %all-to-all-start.1 = ((bf16[16,16,512]{2,1,0:T(8,128)(2,1)}), bf16[16,16,512]{2,1,0:T(8,128)(2,1)S(1)}, u32[]{:S(2)}, u32[]{:S(2)}) async-start(bf16[16,16,512]{2,1,0:T(8,128)(2,1)} %attend.1), calls=%async_computation.1 | async-start | bytes 524288 | tf_op jit(solution)/shard_map/all_to_all | solution.py:497
  79.2 4.6 %collective-permute-start.14 = (bf16[64,4096]{1,0:T(8,128)(2,1)S(1)}, bf16[64,4096]{1,0:T(8,128)(2,1)S(1)}, u32[]{:S(2)}, u32[]{:S(2)}) collective-permute-start(bf16[64,4096]{1,0:T(8,128)(2,1)S(1)} %slice.122), channel_id=1, source_target_pairs={{0,1},{1,0},{2,3},{3,2},{4,5},{5,4},{6,7},{7,6},{8,9},{9,8},{10,11... | collective-permute-start | bytes 1572872 | tf_op jit(solution)/shard_map/ppermute | solution.py:41
  79.9 8.3 %collective-permute-start.20 = (bf16[16,4096]{1,0:T(8,128)(2,1)S(1)}, bf16[16,4096]{1,0:T(8,128)(2,1)S(1)}, u32[]{:S(2)}, u32[]{:S(2)}) collective-permute-start(bf16[16,4096]{1,0:T(8,128)(2,1)S(1)} %get-tuple-element.37), channel_id=1, source_target_pairs={{0,4},{1,5},{2,6},{3,7},{4,8},{5,9},{6,10},{7,11},{8,12},{9,13},{1... | collective-permute-start | bytes 393224 | tf_op jit(solution)/shard_map/ppermute | solution.py:41
  80.2 9.2 %collective-permute-start.22 = (bf16[16,4096]{1,0:T(8,128)(2,1)S(1)}, bf16[16,4096]{1,0:T(8,128)(2,1)S(1)}, u32[]{:S(2)}, u32[]{:S(2)}) collective-permute-start(bf16[16,4096]{1,0:T(8,128)(2,1)S(1)} %get-tuple-element.38), channel_id=1, source_target_pairs={{0,12},{1,13},{2,14},{3,15},{4,0},{5,1},{6,2},{7,3},{8,4},{9,5},{1... | collective-permute-start | bytes 393224 | tf_op jit(solution)/shard_map/ppermute | solution.py:41
  83.8 10.8 %collective-permute-start.21 = (bf16[16,4096]{1,0:T(8,128)(2,1)S(1)}, bf16[16,4096]{1,0:T(8,128)(2,1)S(1)}, u32[]{:S(2)}, u32[]{:S(2)}) collective-permute-start(bf16[16,4096]{1,0:T(8,128)(2,1)S(1)} %get-tuple-element.39), channel_id=1, source_target_pairs={{0,8},{1,9},{2,10},{3,11},{4,12},{5,13},{6,14},{7,15},{8,0},{9,1},... | collective-permute-start | bytes 393224 | tf_op jit(solution)/shard_map/ppermute | solution.py:41
  84.0 10.9 %collective-permute-start.15 = (bf16[32,4096]{1,0:T(8,128)(2,1)S(1)}, bf16[32,4096]{1,0:T(8,128)(2,1)S(1)}, u32[]{:S(2)}, u32[]{:S(2)}) collective-permute-start(bf16[32,4096]{1,0:T(8,128)(2,1)S(1)} %slice.124), channel_id=1, source_target_pairs={{0,2},{1,3},{2,0},{3,1},{4,6},{5,7},{6,4},{7,5},{8,10},{9,11},{10,... | collective-permute-start | bytes 786440 | tf_op jit(solution)/shard_map/ppermute | solution.py:41
  94.6 4.3 %collective-permute-start.23 = (bf16[8,4096]{1,0:T(8,128)(2,1)S(1)}, bf16[8,4096]{1,0:T(8,128)(2,1)S(1)}, u32[]{:S(2)}, u32[]{:S(2)}) collective-permute-start(bf16[8,4096]{1,0:T(8,128)(2,1)S(1)} %slice.125), channel_id=1, source_target_pairs={{0,2},{1,3},{2,0},{3,1},{4,6},{5,7},{6,4},{7,5},{8,10},{9,11},{10,... | collective-permute-start | bytes 196616 | tf_op jit(solution)/shard_map/ppermute | solution.py:41
  95.0 6.4 %collective-permute-start.16 = (bf16[8,4096]{1,0:T(8,128)(2,1)S(1)}, bf16[8,4096]{1,0:T(8,128)(2,1)S(1)}, u32[]{:S(2)}, u32[]{:S(2)}) collective-permute-start(bf16[8,4096]{1,0:T(8,128)(2,1)S(1)} %get-tuple-element.40), channel_id=1, source_target_pairs={{0,4},{1,5},{2,6},{3,7},{4,8},{5,9},{6,10},{7,11},{8,12},{9,13},{1... | collective-permute-start | bytes 196616 | tf_op jit(solution)/shard_map/ppermute | solution.py:41
  95.0 6.4 %collective-permute-start.18 = (bf16[8,4096]{1,0:T(8,128)(2,1)S(1)}, bf16[8,4096]{1,0:T(8,128)(2,1)S(1)}, u32[]{:S(2)}, u32[]{:S(2)}) collective-permute-start(bf16[8,4096]{1,0:T(8,128)(2,1)S(1)} %get-tuple-element.41), channel_id=1, source_target_pairs={{0,12},{1,13},{2,14},{3,15},{4,0},{5,1},{6,2},{7,3},{8,4},{9,5},{1... | collective-permute-start | bytes 196616 | tf_op jit(solution)/shard_map/ppermute | solution.py:41
  98.8 5.2 %collective-permute-start.17 = (bf16[8,4096]{1,0:T(8,128)(2,1)S(1)}, bf16[8,4096]{1,0:T(8,128)(2,1)S(1)}, u32[]{:S(2)}, u32[]{:S(2)}) collective-permute-start(bf16[8,4096]{1,0:T(8,128)(2,1)S(1)} %get-tuple-element.42), channel_id=1, source_target_pairs={{0,8},{1,9},{2,10},{3,11},{4,12},{5,13},{6,14},{7,15},{8,0},{9,1},... | collective-permute-start | bytes 196616 | tf_op jit(solution)/shard_map/ppermute | solution.py:41
  (7 other events, 48.8 us)

commit v6 on v5

--- a/solution.py
+++ b/solution.py
@@ -79,7 +79,7 @@
     line_a, pair_b = lax.optimization_barrier((line_a, pair_b))
     beside_a = grid.send(line_a, near=1)
     line_b = [grid.send(pair_b, far=d) for d in range(1, grid.far)]
-    beside_a, line_b, meanwhile = lax.optimization_barrier((beside_a, line_b, meanwhile))
+    beside_a, line_b, meanwhile = lax.optimization_barrier((beside_a, line_b, meanwhile(pair_b)))
     parts_a = [line_a, beside_a]
     parts_b = [pair_b, *line_b]
     parts_a += [grid.send(part, core=1) for part in parts_a]
@@ -95,9 +95,7 @@
     return x.astype(jnp.float32)
 
 
-def scatter_sum(grid, rows_a, rows_b, w_out):
-    half = w_out.shape[1] // 2
-
+def scatter_sum(grid, rows_a, rows_b, w_out, cut):
     def start(rows, w):
         x = jnp.dot(rows, w, preferred_element_type=jnp.float32)
         middle = x.shape[0] // 2
@@ -118,8 +116,8 @@
             x = x + wide(part)
         return x
 
-    away, xb = start(rows_b, w_out[:, half:])
-    _, xa = start(after(rows_a, away), w_out[:, :half])
+    away, xb = start(rows_b, w_out[:, cut:])
+    _, xa = start(after(rows_a, away), w_out[:, :cut])
     xb = along_near(along_far(xb))
     xa = along_far(along_near(xa))
     return jnp.concatenate([xa, xb], axis=1)
@@ -147,7 +145,34 @@
     )(x, gain.reshape(1, -1))
 
 
-def project_kernel(first, last, order, *refs):
+def fetch_kernel(*refs):
+    count = len(refs) // 2
+    sems = refs[-1]
+    copies = [
+        pltpu.make_async_copy(refs[i], refs[count + i], sems.at[i]) for i in range(count)
+    ]
+    for copy in copies:
+        copy.start()
+    for copy in copies:
+        copy.wait()
+
+
+def fetch(*arrays, limit):
+    return pl.pallas_call(
+        fetch_kernel,
+        in_specs=[pl.BlockSpec(memory_space=pl.ANY)] * len(arrays),
+        out_specs=[pl.BlockSpec(memory_space=pltpu.VMEM)] * len(arrays),
+        out_shape=[jax.ShapeDtypeStruct(x.shape, x.dtype) for x in arrays],
+        scratch_shapes=[pltpu.SemaphoreType.DMA((len(arrays),))],
+        compiler_params=pltpu.CompilerParams(vmem_limit_bytes=limit * 2**20),
+        cost_estimate=pl.CostEstimate(
+            flops=0, bytes_accessed=sum(x.size * 4 for x in arrays), transcendentals=0
+        ),
+        name="fetch",
+    )(*arrays)
+
+
+def project_kernel(first, last, order, start, block, *refs):
     count = len(refs) - 4 - (not first) - last
     parts, (wq, w_kv), refs = refs[:count], refs[count : count + 2], refs[count + 2 :]
     if not first:
@@ -156,17 +181,18 @@
         place, refs = refs[0], refs[1:]
     out, total = refs
     step = pl.program_id(0)
-    block, per_query = wq.shape
+    per_query = wq.shape[1]
 
     @pl.when(step == 0)
     def _():
         total[...] = jnp.zeros_like(total) if first else before[...]
 
     here = pl.ds(pl.multiple_of(step * block, block), block)
+    there = pl.ds(pl.multiple_of(start + step * block, block), block)
     x = jnp.concatenate([part[:, here] for part in parts], axis=0)
     products = [
-        jnp.dot(x, wq[...], preferred_element_type=jnp.float32),
-        lax.dot_general(x, w_kv[...], (((1,), (1,)), ((), ())), preferred_element_type=jnp.float32),
+        jnp.dot(x, wq[there, :], preferred_element_type=jnp.float32),
+        lax.dot_general(x, w_kv[:, there], (((1,), (1,)), ((), ())), preferred_element_type=jnp.float32),
     ]
     size = x.shape[0] // len(order)
     for product, columns in zip(products, (slice(0, per_query), slice(per_query, None))):
@@ -198,8 +224,8 @@
     args = [*parts, w_query, w_kv_t]
     specs = [vmem] * len(parts)
     specs += [
-        pl.BlockSpec((block, w_query.shape[1]), lambda i: (start // block + i, 0)),
-        pl.BlockSpec((w_kv_t.shape[0], block), lambda i: (0, start // block + i)),
+        vmem,
+        vmem,
     ]
     if not first:
         args.append(before)
@@ -211,13 +237,13 @@
     else:
         out = jax.ShapeDtypeStruct((rows, row_width), jnp.float32)
     return pl.pallas_call(
-        functools.partial(project_kernel, first, last, order),
+        functools.partial(project_kernel, first, last, order, start, block),
         grid=(width // block,),
         in_specs=specs,
         out_specs=vmem,
         out_shape=out,
         scratch_shapes=[pltpu.VMEM((rows, row_width), jnp.float32)],
-        compiler_params=pltpu.CompilerParams(vmem_limit_bytes=48 * 2**20),
+        compiler_params=pltpu.CompilerParams(vmem_limit_bytes=24 * 2**20),
         cost_estimate=pl.CostEstimate(
             flops=2 * rows * width * row_width,
             bytes_accessed=2 * width * row_width,
@@ -238,9 +264,6 @@
     key_pages,
     value_pages,
     out,
-    key_pool,
-    value_pool,
-    sems,
     key_new,
     query_rot,
     value_own,
@@ -260,13 +283,6 @@
     batches = query_rot.shape[1]
     batch = slots // batches
 
-    cuts = 4
-    size = key_pages.shape[0] // cuts
-    for i, (pool, on_chip) in enumerate(((key_pages, key_pool), (value_pages, value_pool))):
-        for cut in range(cuts):
-            part = pl.ds(cut * size, size)
-            pltpu.make_async_copy(pool.at[part], on_chip.at[part], sems.at[i]).start()
-
     def held(pool, slot, columns):
         return [pool[table[slot, j], :, columns] for j in range(pages)]
 
@@ -309,7 +325,6 @@
         jnp.int32, (columns, columns), 1
     )
 
-    pltpu.make_async_copy(key_pool, key_pool, sems.at[0]).wait()
     own_chances = {}
     for b in range(batches):
         valid = row < lengths[b]
@@ -322,7 +337,7 @@
             columns_p = slice(p * 2 * HEAD, (p + 1) * 2 * HEAD)
             keys = []
             for s in range(batch):
-                keys += held(key_pool, b * batch + s, columns_p)
+                keys += held(key_pages, b * batch + s, columns_p)
             keys.append(key_new[:, columns_p])
             products = jnp.dot(
                 jnp.concatenate(keys, axis=0), wide, preferred_element_type=jnp.float32
@@ -343,13 +358,12 @@
                 jnp.where(same, own_chance, 0.0), axis=1, keepdims=True
             )
 
-    pltpu.make_async_copy(value_pool, value_pool, sems.at[1]).wait()
     for b in range(batches):
         for s in range(batch):
             for p in range(pairs):
                 mine = chance[p, b, pl.ds(s, pair, stride=batch)].astype(jnp.bfloat16)
                 columns_p = slice(p * 2 * HEAD, (p + 1) * 2 * HEAD)
-                values = held(value_pool, b * batch + s, columns_p)
+                values = held(value_pages, b * batch + s, columns_p)
                 both = jnp.dot(
                     mine, jnp.concatenate(values, axis=0), preferred_element_type=jnp.float32
                 )
@@ -388,23 +402,19 @@
     lengths = jnp.tile(lengths.reshape(batches, 1, batch), (1, 1, pair))
     smem = pl.BlockSpec(memory_space=pltpu.SMEM)
     vmem = pl.BlockSpec(memory_space=pltpu.VMEM)
-    hbm = pl.BlockSpec(memory_space=pl.ANY)
     return pl.pallas_call(
         functools.partial(attend_kernel, per_query, per_key),
-        in_specs=[smem, vmem, vmem, vmem, vmem, hbm, hbm],
+        in_specs=[smem, vmem, vmem, vmem, vmem, vmem, vmem],
         out_specs=vmem,
         out_shape=jax.ShapeDtypeStruct((owners, slots, per_query), jnp.bfloat16),
         scratch_shapes=[
-            pltpu.VMEM(key_pages.shape, jnp.bfloat16),
-            pltpu.VMEM(value_pages.shape, jnp.bfloat16),
-            pltpu.SemaphoreType.DMA((2,)),
             pltpu.VMEM((slots, kv_width), jnp.bfloat16),
             pltpu.VMEM((pairs, batches, columns, HEAD), jnp.float32),
             pltpu.VMEM((kv_heads, slots, HEAD), jnp.float32),
             pltpu.VMEM((pairs, batches, columns, span), jnp.float32),
             pltpu.VMEM((pairs, batches, columns, HEAD), jnp.float32),
         ],
-        compiler_params=pltpu.CompilerParams(vmem_limit_bytes=52 * 2**20),
+        compiler_params=pltpu.CompilerParams(vmem_limit_bytes=24 * 2**20),
         cost_estimate=pl.CostEstimate(
             flops=8 * slots * heads * span * HEAD,
             bytes_accessed=4 * slots * span * kv_width,
@@ -475,30 +485,36 @@
     if spare:
         pieces.append(jnp.zeros((spare, width), w_key.dtype))
     w_kv_t = jnp.concatenate(pieces, axis=0)
-    parts_a, parts_b, (w_kv_t, place_in, place_out, cosine, sine) = gather_rows(
-        grid, xa, xb, (w_kv_t, place_in, place_out, cosine, sine)
-    )
+
+    def beside_gather(x):
+        (w,) = fetch(after(w_query, x), limit=44)
+        return w, w_kv_t, place_in, place_out, cosine, sine
+
+    parts_a, parts_b, others = gather_rows(grid, xa, xb, beside_gather)
+    w_query, w_kv_t, place_in, place_out, cosine, sine = others
     plain = list(range(owners))
     total = project(0, parts_a, plain, w_query, w_kv_t, None, None, all_slots)
     total = project(5 * unit, parts_b, crossed, w_query, w_kv_t, total, place_in, all_slots)
     outbound = total.reshape(owners, slot_count, row_width)
     inbound = lax.all_to_all(outbound, AXES, split_axis=0, concat_axis=0, tiled=True)
+    keys, values = fetch(after(key_pages, outbound)[0], value_pages[0], limit=44)
     attended = attend(
         inbound,
         lengths,
         page_table[0],
         cosine,
         sine,
-        key_pages[0],
-        value_pages[0],
+        keys,
+        values,
         per_query,
         per_key,
     )
+    (w_out,) = fetch(after(w_out, attended), limit=44)
     returned = lax.all_to_all(attended, AXES, split_axis=0, concat_axis=0, tiled=True)
     returned = returned.reshape(all_slots, per_query)
     rows_a = narrow(jnp.dot(route_out, returned, preferred_element_type=jnp.float32))
     rows_b = narrow(jnp.dot(route_crossed, returned, preferred_element_type=jnp.float32))
-    summed = scatter_sum(grid, rows_a, rows_b, w_out)
+    summed = scatter_sum(grid, rows_a, rows_b, w_out, 5 * unit)
     return narrow(wide(hidden_in) + summed)
 
 

time: 105 us -> 101 us (0.962)
  waiting for transfers between devices: 43.4 us -> 21.9 us
  local copies, waits for them, and re-layouts: 3.8 us -> 15.5 us
  Pallas kernels: 15.3 us -> 18 us
  starting transfers between devices: 29.4 us -> 31.9 us
    unnamed x10 -> x22, local copies, waits for them, and re-layouts: 1.68 us -> 13.3 us
    all_to_all x1, waiting for transfers between devices: 10.8 us -> 3.34 us  [on_device(): lax.all_to_all(outbound, AXES, split_axis=0, concat_axis=0, tiled=True)]
    ppermute x24, waiting for transfers between devices: 23.4 us -> 16 us  [send(): return lax.ppermute(x, AXES, self.perm(far, near, core))]
    all_to_all x1, waiting for transfers between devices: 9.24 us -> 2.56 us  [on_device(): lax.all_to_all(attended, AXES, split_axis=0, concat_axis=0, tiled=True)]
    pallas_call x2 -> x5, Pallas kernels: 9.14 us -> 14.5 us  [the longest x3 10.3 us: fetch(): pl.pallas_call(fetch_kernel, in_specs=[pl.BlockSpec(memory_space=pl.ANY)]...]
    pallas_call x1, Pallas kernels: 5.98 us -> 3.41 us  [attend(): pl.pallas_call(functools.partial(attend_kernel, per_query, per_key), in_s...]
    ppermute x24, starting transfers between devices: 22.3 us -> 23.7 us  [send(): return lax.ppermute(x, AXES, self.perm(far, near, core))]
    all_to_all x1, starting transfers between devices: 3.54 us -> 4.71 us  [on_device(): lax.all_to_all(outbound, AXES, split_axis=0, concat_axis=0, tiled=True)]
  transfers between devices with their start and end apart: 26 -> 26, of which waited for: 11 -> 9; matrix products, arithmetic and copies ran while one was open for 10% -> 11% of each run, Pallas kernels for 5% -> 12%
where the time goes in v6:
time: 101 us
  starting transfers between devices  31.9 us (32%)
  waiting for transfers between devices  21.9 us (22%)
  Pallas kernels  18 us (18%)
  local copies, waits for them, and re-layouts  15.5 us (15%)
  other arithmetic  6.54 us (6%)
  matrix products  6.27 us (6%)
    ppermute x24, starting transfers between devices, send(): return lax.ppermute(x, AXES, self.perm(far, near, core))  23.7 us
    ppermute x24, waiting for transfers between devices, send(): return lax.ppermute(x, AXES, self.perm(far, near, core))  16 us
    unnamed x22, local copies, waits for them, and re-layouts  13.3 us
    pallas_call x3, Pallas kernels, fetch(): pl.pallas_call(fetch_kernel, in_specs=[pl.BlockSpec(memory_space=pl.ANY)]...  10.3 us
    dot_general x2, matrix products, start(): x = jnp.dot(rows, w, preferred_element_type=jnp.float32)  6.04 us
    all_to_all x1, starting transfers between devices, on_device(): lax.all_to_all(outbound, AXES, split_axis=0, concat_axis=0, tiled=True)  4.71 us
    pallas_call x2, Pallas kernels, project(): pl.pallas_call(functools.partial(project_kernel, first, last, order, star...  4.18 us
    all_to_all x1, starting transfers between devices, on_device(): lax.all_to_all(attended, AXES, split_axis=0, concat_axis=0, tiled=True)  3.53 us
  transfers between devices with their start and end apart: 26, of which 9 were waited for; matrix products, arithmetic and copies ran while one was open for 11% of the time, Pallas kernels for 12%

profile of v6, /device:TPU:0, one launch (start us, length us, event | category | flops | bytes accessed | tf_op | source)
XLA Modules:
  0.0 100.5 jit_solution(4241815767162851742)
XLA Ops:
  1.9 5.1 %collective-permute-start.2 = (bf16[8,5120]{1,0:T(8,128)(2,1)S(1)}, bf16[8,5120]{1,0:T(8,128)(2,1)S(1)}, u32[]{:S(2)}, u32[]{:S(2)}) collective-permute-start(bf16[8,5120]{1,0:T(8,128)(2,1)S(1)} %get-tuple-element.24), channel_id=1, source_target_pairs={{0,12},{1,13},{2,14},{3,15},{4,0},{5,1},{6,2},{7,3},{8,4},{9,5},{1... | collective-permute-start | bytes 245768 | tf_op jit(solution)/shard_map/ppermute | solution.py:41
  12.9 1.7 %pad_maximum_fusion.refs_5_.refs_9_ = bf16[128,8192]{1,0:T(8,128)(2,1)S(1)} fusion(bf16[64,8192]{1,0:T(8,128)(2,1)} %bitcast.24, bf16[64,8192]{1,0:T(8,128)(2,1)} %bitcast.25), kind=kLoop, calls=%fused_computation.5 | loop fusion | flops 4194304 | bytes 4194304 | tf_op jit(solution)/shard_map/concatenate | solution.py:487
  16.4 2.5 %collective-permute-start.5 = (bf16[16,3072]{1,0:T(8,128)(2,1)S(1)}, bf16[16,3072]{1,0:T(8,128)(2,1)S(1)}, u32[]{:S(2)}, u32[]{:S(2)}) collective-permute-start(bf16[16,3072]{1,0:T(8,128)(2,1)S(1)} %pad_maximum_fusion.2.refs_0_), channel_id=1, source_target_pairs={{0,4},{1,5},{2,6},{3,7},{4,8},{5,9},{6,10},{7,11},{8,12},{9,13},{1... | collective-permute-start | bytes 294920 | tf_op jit(solution)/shard_map/ppermute | solution.py:41
  21.5 3.4 %fetch.3.refs_4_.refs_8_ = bf16[8192,512]{1,0:T(8,128)(2,1)S(1)} custom-call(bf16[8192,512]{1,0:T(8,128)(2,1)} %refs_0_), custom_call_target="tpu_custom_call" | custom-call | bytes 16777216 | tf_op jit(solution)/shard_map/fetch/pallas_call | solution.py:161
  24.9 2.0 %collective-permute-done.6.refs_2_ = bf16[16,3072]{1,0:T(8,128)(2,1)S(1)} collective-permute-done((bf16[16,3072]{1,0:T(8,128)(2,1)S(1)}, bf16[16,3072]{1,0:T(8,128)(2,1)S(1)}, u32[]{:S(2)}, u32[]{:S(2)}) %collective-permute-start.6) | collective-permute-done | bytes 98336 | tf_op jit(solution)/shard_map/ppermute | solution.py:41
  28.5 2.0 %project.2.refs_10_ = f32[128,640]{1,0:T(8,128)S(1)} custom-call(bf16[32,5120]{1,0:T(8,128)(2,1)S(1)} %pad_maximum_fusion.1.refs_0_, bf16[32,5120]{1,0:T(8,128)(2,1)S(1)} %collective-permute-done.4.refs_1_, bf16[32,5120]{1,0:T(8,128)(2,1)S(1)} %collective-permute-done.12.refs_2_, bf16[32,5120]{1,0:T(8,128)(2,1)S(1)} %collective-permute-done.13.refs_3_, ...), custom_call_target="tpu_custom_call" | custom-call | flops 838860800 | bytes 6553600 | tf_op jit(solution)/shard_map/project/pallas_call | solution.py:239
  30.6 2.2 %project.3 = bf16[256,640]{1,0:T(8,128)(2,1)} custom-call(bf16[16,3072]{1,0:T(8,128)(2,1)S(1)} %pad_maximum_fusion.2.refs_0_, bf16[16,3072]{1,0:T(8,128)(2,1)S(1)} %collective-permute-done.5.refs_1_, bf16[16,3072]{1,0:T(8,128)(2,1)S(1)} %collective-permute-done.6.refs_2_, bf16[16,3072]{1,0:T(8,128)(2,1)S(1)} %collective-permute-done.7.refs_3_, ...), custom_call_target="tpu_custom_call" | custom-call | flops 503316480 | bytes 3932160 | tf_op jit(solution)/shard_map/project/pallas_call | solution.py:239
  32.8 4.7 %all-to-all-start = ((bf16[16,16,640]{2,1,0:T(8,128)(2,1)}), bf16[16,16,640]{2,1,0:T(8,128)(2,1)S(1)}, u32[]{:S(2)}, u32[]{:S(2)}) async-start(bf16[16,16,640]{2,1,0:T(8,128)(2,1)} %bitcast.8), calls=%async_computation | async-start | bytes 655360 | tf_op jit(solution)/shard_map/all_to_all | solution.py:499
  37.8 3.5 %fetch.4 = (bf16[64,32,1024]{2,1,0:T(8,128)(2,1)S(1)}, bf16[64,32,1024]{2,1,0:T(8,128)(2,1)S(1)}) custom-call(bf16[64,32,1024]{2,1,0:T(8,128)(2,1)} %bitcast.20, bf16[64,32,1024]{2,1,0:T(8,128)(2,1)} %bitcast.21), custom_call_target="tpu_custom_call" | custom-call | bytes 16777216 | tf_op jit(solution)/shard_map/fetch/pallas_call | solution.py:161
  41.3 2.0 %copy-done.1 = bf16[64,32,1024]{2,1,0:T(8,128)(2,1)} copy-done((bf16[64,32,1024]{2,1,0:T(8,128)(2,1)}, bf16[64,32,1024]{2,1,0:T(8,128)(2,1)S(1)}, u32[]{:S(2)}) %copy-start.1) | copy-done | bytes 4194328
  43.2 2.0 %copy-done.3 = bf16[64,32,1024]{2,1,0:T(8,128)(2,1)} copy-done((bf16[64,32,1024]{2,1,0:T(8,128)(2,1)}, bf16[64,32,1024]{2,1,0:T(8,128)(2,1)S(1)}, u32[]{:S(2)}) %copy-start.3) | copy-done | bytes 4194328
  45.2 3.3 %all-to-all-done.inbound = bf16[16,16,640]{2,1,0:T(8,128)(2,1)S(1)} async-done(((bf16[16,16,640]{2,1,0:T(8,128)(2,1)}), bf16[16,16,640]{2,1,0:T(8,128)(2,1)S(1)}, u32[]{:S(2)}, u32[]{:S(2)}) %all-to-all-start) | async-done | bytes 327712 | tf_op jit(solution)/shard_map/all_to_all | solution.py:499
  48.6 2.2 %copy-done.2 = bf16[64,32,1024]{2,1,0:T(8,128)(2,1)S(1)} copy-done((bf16[64,32,1024]{2,1,0:T(8,128)(2,1)S(1)}, bf16[64,32,1024]{2,1,0:T(8,128)(2,1)}, u32[]{:S(2)}) %copy-start.2) | copy-done | bytes 4194328
  50.8 2.2 %copy-done.4 = bf16[64,32,1024]{2,1,0:T(8,128)(2,1)S(1)} copy-done((bf16[64,32,1024]{2,1,0:T(8,128)(2,1)S(1)}, bf16[64,32,1024]{2,1,0:T(8,128)(2,1)}, u32[]{:S(2)}) %copy-start.4) | copy-done | bytes 4194328
  53.0 3.4 %attend.1 = bf16[16,16,512]{2,1,0:T(8,128)(2,1)} custom-call(s32[16,4]{1,0:T(8,128)S(1)} %copy.20.table, s32[2,1,128]{2,1,0:T(1,128)S(1)} %bitcast.18, bf16[16,16,640]{2,1,0:T(8,128)(2,1)S(1)} %all-to-all-done.inbound, f32[16,128]{1,0:T(8,128)S(1)} %get-tuple-element.36.cosine, f32[16,128]{1,0:T(8,128)S(1)} %get-tuple-element.37.sine, ...), custom_call_target="tpu_custom_call" | custom-call | flops 134217728 | bytes 8388608 | tf_op jit(solution)/shard_map/attend/pallas_call | solution.py:405
  56.4 3.5 %all-to-all-start.1 = ((bf16[16,16,512]{2,1,0:T(8,128)(2,1)}), bf16[16,16,512]{2,1,0:T(8,128)(2,1)S(1)}, u32[]{:S(2)}, u32[]{:S(2)}) async-start(bf16[16,16,512]{2,1,0:T(8,128)(2,1)} %attend.1), calls=%async_computation.1 | async-start | bytes 524288 | tf_op jit(solution)/shard_map/all_to_all | solution.py:513
  60.7 3.4 %fetch.5 = bf16[512,8192]{1,0:T(8,128)(2,1)S(1)} custom-call(bf16[512,8192]{1,0:T(8,128)(2,1)} %refs_0_.1), custom_call_target="tpu_custom_call" | custom-call | bytes 16777216 | tf_op jit(solution)/shard_map/fetch/pallas_call | solution.py:161
  64.1 3.3 %copy-done = bf16[512,8192]{1,0:T(8,128)(2,1)} copy-done((bf16[512,8192]{1,0:T(8,128)(2,1)}, bf16[512,8192]{1,0:T(8,128)(2,1)S(1)}, u32[]{:S(2)}) %copy-start) | copy-done | bytes 8388632
  67.4 2.6 %all-to-all-done.1 = bf16[16,16,512]{2,1,0:T(8,128)(2,1)S(1)} async-done(((bf16[16,16,512]{2,1,0:T(8,128)(2,1)}), bf16[16,16,512]{2,1,0:T(8,128)(2,1)S(1)}, u32[]{:S(2)}, u32[]{:S(2)}) %all-to-all-start.1) | async-done | bytes 262176 | tf_op jit(solution)/shard_map/all_to_all | solution.py:513
  69.9 2.6 %fusion.2 = f32[128,3072]{1,0:T(8,128)S(1)} fusion(bf16[512,8192]{1,0:T(8,128)(2,1)} %copy-done, bf16[256,512]{1,0:T(8,128)(2,1)S(1)} %bitcast.22, s32[128]{0:T(128)S(1)} %eq.112), kind=kOutput, calls=%fused_computation.3 | convolution fusion | flops 436305920 | bytes 4981248 | tf_op jit(solution)/shard_map/dot_general | solution.py:100
  72.9 3.4 %fusion = f32[128,5120]{1,0:T(8,128)S(1)} fusion(bf16[128,512]{1,0:T(8,128)(2,1)S(1)} %convolution_convert_fusion.1, bf16[512,8192]{1,0:T(8,128)(2,1)} %copy-done), kind=kOutput, calls=%fused_computation.1 | convolution fusion | flops 671088640 | bytes 7995392 | tf_op jit(solution)/shard_map/dot_general | solution.py:100
  82.1 6.3 %collective-permute-done.21 = bf16[16,3072]{1,0:T(8,128)(2,1)S(1)} collective-permute-done((bf16[16,3072]{1,0:T(8,128)(2,1)S(1)}, bf16[16,3072]{1,0:T(8,128)(2,1)S(1)}, u32[]{:S(2)}, u32[]{:S(2)}) %collective-permute-start.21) | collective-permute-done | bytes 98336 | tf_op jit(solution)/shard_map/ppermute | solution.py:41
  89.4 3.2 %collective-permute-start.18 = (bf16[8,5120]{1,0:T(8,128)(2,1)S(1)}, bf16[8,5120]{1,0:T(8,128)(2,1)S(1)}, u32[]{:S(2)}, u32[]{:S(2)}) collective-permute-start(bf16[8,5120]{1,0:T(8,128)(2,1)S(1)} %get-tuple-element.53), channel_id=1, source_target_pairs={{0,12},{1,13},{2,14},{3,15},{4,0},{5,1},{6,2},{7,3},{8,4},{9,5},{1... | collective-permute-start | bytes 245768 | tf_op jit(solution)/shard_map/ppermute | solution.py:41
  94.8 5.0 %collective-permute-done.17 = bf16[8,5120]{1,0:T(8,128)(2,1)S(1)} collective-permute-done((bf16[8,5120]{1,0:T(8,128)(2,1)S(1)}, bf16[8,5120]{1,0:T(8,128)(2,1)S(1)}, u32[]{:S(2)}, u32[]{:S(2)}) %collective-permute-start.17) | collective-permute-done | bytes 81952 | tf_op jit(solution)/shard_map/ppermute | solution.py:41
  (99 shorter events, 24.7 us)
Async XLA Ops:
  1.9 13.7 %collective-permute-start.2 = (bf16[8,5120]{1,0:T(8,128)(2,1)S(1)}, bf16[8,5120]{1,0:T(8,128)(2,1)S(1)}, u32[]{:S(2)}, u32[]{:S(2)}) collective-permute-start(bf16[8,5120]{1,0:T(8,128)(2,1)S(1)} %get-tuple-element.24), channel_id=1, source_target_pairs={{0,12},{1,13},{2,14},{3,15},{4,0},{5,1},{6,2},{7,3},{8,4},{9,5},{1... | collective-permute-start | bytes 245768 | tf_op jit(solution)/shard_map/ppermute | solution.py:41
  7.0 8.7 %collective-permute-start.1 = (bf16[8,5120]{1,0:T(8,128)(2,1)S(1)}, bf16[8,5120]{1,0:T(8,128)(2,1)S(1)}, u32[]{:S(2)}, u32[]{:S(2)}) collective-permute-start(bf16[8,5120]{1,0:T(8,128)(2,1)S(1)} %get-tuple-element.24), channel_id=1, source_target_pairs={{0,8},{1,9},{2,10},{3,11},{4,12},{5,13},{6,14},{7,15},{8,0},{9,1},... | collective-permute-start | bytes 245768 | tf_op jit(solution)/shard_map/ppermute | solution.py:41
  7.0 8.7 %collective-permute-start = (bf16[8,5120]{1,0:T(8,128)(2,1)S(1)}, bf16[8,5120]{1,0:T(8,128)(2,1)S(1)}, u32[]{:S(2)}, u32[]{:S(2)}) collective-permute-start(bf16[8,5120]{1,0:T(8,128)(2,1)S(1)} %get-tuple-element.24), channel_id=1, source_target_pairs={{0,4},{1,5},{2,6},{3,7},{4,8},{5,9},{6,10},{7,11},{8,12},{9,13},{1... | collective-permute-start | bytes 245768 | tf_op jit(solution)/shard_map/ppermute | solution.py:41
  8.0 7.6 %collective-permute-start.3 = (bf16[8,3072]{1,0:T(8,128)(2,1)S(1)}, bf16[8,3072]{1,0:T(8,128)(2,1)S(1)}, u32[]{:S(2)}, u32[]{:S(2)}) collective-permute-start(bf16[8,3072]{1,0:T(8,128)(2,1)S(1)} %get-tuple-element.25), channel_id=1, source_target_pairs={{0,2},{1,3},{2,0},{3,1},{4,6},{5,7},{6,4},{7,5},{8,10},{9,11},{10,... | collective-permute-start | bytes 147464 | tf_op jit(solution)/shard_map/ppermute | solution.py:41
  15.7 11.2 %collective-permute-start.4 = (bf16[32,5120]{1,0:T(8,128)(2,1)S(1)}, bf16[32,5120]{1,0:T(8,128)(2,1)S(1)}, u32[]{:S(2)}, u32[]{:S(2)}) collective-permute-start(bf16[32,5120]{1,0:T(8,128)(2,1)S(1)} %pad_maximum_fusion.1.refs_0_), channel_id=1, source_target_pairs={{0,2},{1,3},{2,0},{3,1},{4,6},{5,7},{6,4},{7,5},{8,10},{9,11},{10,... | collective-permute-start | bytes 983048 | tf_op jit(solution)/shard_map/ppermute | solution.py:41
  16.4 8.5 %collective-permute-start.5 = (bf16[16,3072]{1,0:T(8,128)(2,1)S(1)}, bf16[16,3072]{1,0:T(8,128)(2,1)S(1)}, u32[]{:S(2)}, u32[]{:S(2)}) collective-permute-start(bf16[16,3072]{1,0:T(8,128)(2,1)S(1)} %pad_maximum_fusion.2.refs_0_), channel_id=1, source_target_pairs={{0,4},{1,5},{2,6},{3,7},{4,8},{5,9},{6,10},{7,11},{8,12},{9,13},{1... | collective-permute-start | bytes 294920 | tf_op jit(solution)/shard_map/ppermute | solution.py:41
  18.9 8.0 %collective-permute-start.6 = (bf16[16,3072]{1,0:T(8,128)(2,1)S(1)}, bf16[16,3072]{1,0:T(8,128)(2,1)S(1)}, u32[]{:S(2)}, u32[]{:S(2)}) collective-permute-start(bf16[16,3072]{1,0:T(8,128)(2,1)S(1)} %pad_maximum_fusion.2.refs_0_), channel_id=1, source_target_pairs={{0,8},{1,9},{2,10},{3,11},{4,12},{5,13},{6,14},{7,15},{8,0},{9,1},... | collective-permute-start | bytes 294920 | tf_op jit(solution)/shard_map/ppermute | solution.py:41
  19.8 7.1 %collective-permute-start.7 = (bf16[16,3072]{1,0:T(8,128)(2,1)S(1)}, bf16[16,3072]{1,0:T(8,128)(2,1)S(1)}, u32[]{:S(2)}, u32[]{:S(2)}) collective-permute-start(bf16[16,3072]{1,0:T(8,128)(2,1)S(1)} %pad_maximum_fusion.2.refs_0_), channel_id=1, source_target_pairs={{0,12},{1,13},{2,14},{3,15},{4,0},{5,1},{6,2},{7,3},{8,4},{9,5},{1... | collective-permute-start | bytes 294920 | tf_op jit(solution)/shard_map/ppermute | solution.py:41
  21.3 6.6 %collective-permute-start.12 = (bf16[32,5120]{1,0:T(8,128)(2,1)S(1)}, bf16[32,5120]{1,0:T(8,128)(2,1)S(1)}, u32[]{:S(2)}, u32[]{:S(2)}) collective-permute-start(bf16[32,5120]{1,0:T(8,128)(2,1)S(1)} %pad_maximum_fusion.1.refs_0_), channel_id=1, source_target_pairs={{0,1},{1,0},{2,3},{3,2},{4,5},{5,4},{6,7},{7,6},{8,9},{9,8},{10,11... | collective-permute-start | bytes 983048 | tf_op jit(solution)/shard_map/ppermute | solution.py:41
  26.9 3.6 %collective-permute-start.8 = (bf16[16,3072]{1,0:T(8,128)(2,1)S(1)}, bf16[16,3072]{1,0:T(8,128)(2,1)S(1)}, u32[]{:S(2)}, u32[]{:S(2)}) collective-permute-start(bf16[16,3072]{1,0:T(8,128)(2,1)S(1)} %pad_maximum_fusion.2.refs_0_), channel_id=1, source_target_pairs={{0,1},{1,0},{2,3},{3,2},{4,5},{5,4},{6,7},{7,6},{8,9},{9,8},{10,11... | collective-permute-start | bytes 294920 | tf_op jit(solution)/shard_map/ppermute | solution.py:41
  27.4 3.1 %collective-permute-start.9 = (bf16[16,3072]{1,0:T(8,128)(2,1)S(1)}, bf16[16,3072]{1,0:T(8,128)(2,1)S(1)}, u32[]{:S(2)}, u32[]{:S(2)}) collective-permute-start(bf16[16,3072]{1,0:T(8,128)(2,1)S(1)} %collective-permute-done.5.refs_1_), channel_id=1, source_target_pairs={{0,1},{1,0},{2,3},{3,2},{4,5},{5,4},{6,7},{7,6},{8,9},{9,8},{10,11... | collective-permute-start | bytes 294920 | tf_op jit(solution)/shard_map/ppermute | solution.py:41
  27.5 3.1 %collective-permute-start.10 = (bf16[16,3072]{1,0:T(8,128)(2,1)S(1)}, bf16[16,3072]{1,0:T(8,128)(2,1)S(1)}, u32[]{:S(2)}, u32[]{:S(2)}) collective-permute-start(bf16[16,3072]{1,0:T(8,128)(2,1)S(1)} %collective-permute-done.6.refs_2_), channel_id=1, source_target_pairs={{0,1},{1,0},{2,3},{3,2},{4,5},{5,4},{6,7},{7,6},{8,9},{9,8},{10,11... | collective-permute-start | bytes 294920 | tf_op jit(solution)/shard_map/ppermute | solution.py:41
  32.8 15.8 %all-to-all-start = ((bf16[16,16,640]{2,1,0:T(8,128)(2,1)}), bf16[16,16,640]{2,1,0:T(8,128)(2,1)S(1)}, u32[]{:S(2)}, u32[]{:S(2)}) async-start(bf16[16,16,640]{2,1,0:T(8,128)(2,1)} %bitcast.8), calls=%async_computation | async-start | bytes 655360 | tf_op jit(solution)/shard_map/all_to_all | solution.py:499
  56.4 13.5 %all-to-all-start.1 = ((bf16[16,16,512]{2,1,0:T(8,128)(2,1)}), bf16[16,16,512]{2,1,0:T(8,128)(2,1)S(1)}, u32[]{:S(2)}, u32[]{:S(2)}) async-start(bf16[16,16,512]{2,1,0:T(8,128)(2,1)} %attend.1), calls=%async_computation.1 | async-start | bytes 524288 | tf_op jit(solution)/shard_map/all_to_all | solution.py:513
  72.6 4.4 %collective-permute-start.19 = (bf16[64,3072]{1,0:T(8,128)(2,1)S(1)}, bf16[64,3072]{1,0:T(8,128)(2,1)S(1)}, u32[]{:S(2)}, u32[]{:S(2)}) collective-permute-start(bf16[64,3072]{1,0:T(8,128)(2,1)S(1)} %slice.125), channel_id=1, source_target_pairs={{0,1},{1,0},{2,3},{3,2},{4,5},{5,4},{6,7},{7,6},{8,9},{9,8},{10,11... | collective-permute-start | bytes 1179656 | tf_op jit(solution)/shard_map/ppermute | solution.py:41
  76.4 3.8 %collective-permute-start.14 = (bf16[64,5120]{1,0:T(8,128)(2,1)S(1)}, bf16[64,5120]{1,0:T(8,128)(2,1)S(1)}, u32[]{:S(2)}, u32[]{:S(2)}) collective-permute-start(bf16[64,5120]{1,0:T(8,128)(2,1)S(1)} %slice.124), channel_id=1, source_target_pairs={{0,1},{1,0},{2,3},{3,2},{4,5},{5,4},{6,7},{7,6},{8,9},{9,8},{10,11... | collective-permute-start | bytes 1966088 | tf_op jit(solution)/shard_map/ppermute | solution.py:41
  77.1 4.9 %collective-permute-start.22 = (bf16[16,3072]{1,0:T(8,128)(2,1)S(1)}, bf16[16,3072]{1,0:T(8,128)(2,1)S(1)}, u32[]{:S(2)}, u32[]{:S(2)}) collective-permute-start(bf16[16,3072]{1,0:T(8,128)(2,1)S(1)} %get-tuple-element.50), channel_id=1, source_target_pairs={{0,12},{1,13},{2,14},{3,15},{4,0},{5,1},{6,2},{7,3},{8,4},{9,5},{1... | collective-permute-start | bytes 294920 | tf_op jit(solution)/shard_map/ppermute | solution.py:41
  78.3 10.0 %collective-permute-start.21 = (bf16[16,3072]{1,0:T(8,128)(2,1)S(1)}, bf16[16,3072]{1,0:T(8,128)(2,1)S(1)}, u32[]{:S(2)}, u32[]{:S(2)}) collective-permute-start(bf16[16,3072]{1,0:T(8,128)(2,1)S(1)} %get-tuple-element.51), channel_id=1, source_target_pairs={{0,8},{1,9},{2,10},{3,11},{4,12},{5,13},{6,14},{7,15},{8,0},{9,1},... | collective-permute-start | bytes 294920 | tf_op jit(solution)/shard_map/ppermute | solution.py:41
  78.9 9.5 %collective-permute-start.20 = (bf16[16,3072]{1,0:T(8,128)(2,1)S(1)}, bf16[16,3072]{1,0:T(8,128)(2,1)S(1)}, u32[]{:S(2)}, u32[]{:S(2)}) collective-permute-start(bf16[16,3072]{1,0:T(8,128)(2,1)S(1)} %get-tuple-element.49), channel_id=1, source_target_pairs={{0,4},{1,5},{2,6},{3,7},{4,8},{5,9},{6,10},{7,11},{8,12},{9,13},{1... | collective-permute-start | bytes 294920 | tf_op jit(solution)/shard_map/ppermute | solution.py:41
  80.4 8.9 %collective-permute-start.15 = (bf16[32,5120]{1,0:T(8,128)(2,1)S(1)}, bf16[32,5120]{1,0:T(8,128)(2,1)S(1)}, u32[]{:S(2)}, u32[]{:S(2)}) collective-permute-start(bf16[32,5120]{1,0:T(8,128)(2,1)S(1)} %slice.126), channel_id=1, source_target_pairs={{0,2},{1,3},{2,0},{3,1},{4,6},{5,7},{6,4},{7,5},{8,10},{9,11},{10,... | collective-permute-start | bytes 983048 | tf_op jit(solution)/shard_map/ppermute | solution.py:41
  88.4 5.1 %collective-permute-start.23 = (bf16[8,3072]{1,0:T(8,128)(2,1)S(1)}, bf16[8,3072]{1,0:T(8,128)(2,1)S(1)}, u32[]{:S(2)}, u32[]{:S(2)}) collective-permute-start(bf16[8,3072]{1,0:T(8,128)(2,1)S(1)} %slice.127), channel_id=1, source_target_pairs={{0,2},{1,3},{2,0},{3,1},{4,6},{5,7},{6,4},{7,5},{8,10},{9,11},{10,... | collective-permute-start | bytes 147464 | tf_op jit(solution)/shard_map/ppermute | solution.py:41
  89.4 5.4 %collective-permute-start.18 = (bf16[8,5120]{1,0:T(8,128)(2,1)S(1)}, bf16[8,5120]{1,0:T(8,128)(2,1)S(1)}, u32[]{:S(2)}, u32[]{:S(2)}) collective-permute-start(bf16[8,5120]{1,0:T(8,128)(2,1)S(1)} %get-tuple-element.53), channel_id=1, source_target_pairs={{0,12},{1,13},{2,14},{3,15},{4,0},{5,1},{6,2},{7,3},{8,4},{9,5},{1... | collective-permute-start | bytes 245768 | tf_op jit(solution)/shard_map/ppermute | solution.py:41
  92.6 7.2 %collective-permute-start.17 = (bf16[8,5120]{1,0:T(8,128)(2,1)S(1)}, bf16[8,5120]{1,0:T(8,128)(2,1)S(1)}, u32[]{:S(2)}, u32[]{:S(2)}) collective-permute-start(bf16[8,5120]{1,0:T(8,128)(2,1)S(1)} %get-tuple-element.54), channel_id=1, source_target_pairs={{0,8},{1,9},{2,10},{3,11},{4,12},{5,13},{6,14},{7,15},{8,0},{9,1},... | collective-permute-start | bytes 245768 | tf_op jit(solution)/shard_map/ppermute | solution.py:41
  92.6 7.2 %collective-permute-start.16 = (bf16[8,5120]{1,0:T(8,128)(2,1)S(1)}, bf16[8,5120]{1,0:T(8,128)(2,1)S(1)}, u32[]{:S(2)}, u32[]{:S(2)}) collective-permute-start(bf16[8,5120]{1,0:T(8,128)(2,1)S(1)} %get-tuple-element.52), channel_id=1, source_target_pairs={{0,4},{1,5},{2,6},{3,7},{4,8},{5,9},{6,10},{7,11},{8,12},{9,13},{1... | collective-permute-start | bytes 245768 | tf_op jit(solution)/shard_map/ppermute | solution.py:41
  (13 other events, 61.3 us)

commit v7 on v6

--- a/solution.py
+++ b/solution.py
@@ -40,23 +40,22 @@
     def send(self, x, far=0, near=0, core=0):
         return lax.ppermute(x, AXES, self.perm(far, near, core))
 
-    def blocks(self, sign):
+    def blocks(self, sign, order=None):
         rows = []
         for f in range(self.far):
             for n in range(self.near):
                 for c in range(self.core):
-                    rows.append(
-                        [
-                            self.index(
-                                (f + sign * df) % self.far,
-                                (n + sign * dn) % self.near,
-                                (c + sign * dc) % self.core,
-                            )
-                            for dc in range(self.core)
-                            for dn in range(self.near)
-                            for df in range(self.far)
-                        ]
-                    )
+                    row = [
+                        self.index(
+                            (f + sign * df) % self.far,
+                            (n + sign * dn) % self.near,
+                            (c + sign * dc) % self.core,
+                        )
+                        for dc in range(self.core)
+                        for dn in range(self.near)
+                        for df in range(self.far)
+                    ]
+                    rows.append([row[i] for i in order] if order else row)
         return jnp.asarray(np.array(rows, np.int32))[lax.axis_index(AXES)]
 
     def crossed(self):
@@ -95,17 +94,57 @@
     return x.astype(jnp.float32)
 
 
-def scatter_sum(grid, rows_a, rows_b, w_out, cut):
-    def start(rows, w):
-        x = jnp.dot(rows, w, preferred_element_type=jnp.float32)
-        middle = x.shape[0] // 2
-        away = narrow(x[middle:])
-        return away, x[:middle] + wide(grid.send(away, core=1))
-
-    def along_near(x):
-        middle = x.shape[0] // 2
-        return x[:middle] + wide(grid.send(narrow(x[middle:]), near=1))
-
+def product_kernel(start, step, place, returned, w_out, away, keep, held, sems):
+    copies = []
+    for i in range(held.shape[1] // step):
+        here = pl.ds(i * step, step)
+        copies.append(
+            pltpu.make_async_copy(
+                w_out.at[:, pl.ds(start + i * step, step)], held.at[:, here], sems.at[i]
+            )
+        )
+        copies[-1].start()
+    slots = lax.broadcasted_iota(jnp.int32, (returned.shape[0], place.shape[1]), 0)
+    route = jnp.where(slots == place[...], 1.0, 0.0).astype(jnp.bfloat16)
+    rows = lax.dot_general(
+        route, returned[...], (((0,), (0,)), ((), ())), preferred_element_type=jnp.float32
+    ).astype(jnp.bfloat16)
+    half = keep.shape[0]
+    for i, copy in enumerate(copies):
+        copy.wait()
+        here = slice(i * step, (i + 1) * step)
+        x = jnp.dot(rows, held[:, here], preferred_element_type=jnp.float32)
+        keep[:, here] = x[:half]
+        away[:, here] = x[half:].astype(jnp.bfloat16)
+
+
+def product(place, returned, w_out, start, width):
+    rows = place.shape[0]
+    step = 512
+    vmem = pl.BlockSpec(memory_space=pltpu.VMEM)
+    return pl.pallas_call(
+        functools.partial(product_kernel, start, step),
+        in_specs=[vmem, vmem, pl.BlockSpec(memory_space=pl.ANY)],
+        out_specs=[vmem, vmem],
+        out_shape=[
+            jax.ShapeDtypeStruct((rows // 2, width), jnp.bfloat16),
+            jax.ShapeDtypeStruct((rows // 2, width), jnp.float32),
+        ],
+        scratch_shapes=[
+            pltpu.VMEM((w_out.shape[0], width), jnp.bfloat16),
+            pltpu.SemaphoreType.DMA((width // step,)),
+        ],
+        compiler_params=pltpu.CompilerParams(vmem_limit_bytes=48 * 2**20),
+        cost_estimate=pl.CostEstimate(
+            flops=2 * rows * w_out.shape[0] * width,
+            bytes_accessed=2 * w_out.shape[0] * width,
+            transcendentals=0,
+        ),
+        name="product",
+    )(place.reshape(1, rows), returned, w_out)
+
+
+def scatter_sum(grid, place_a, place_b, returned, w_out, cut):
     def along_far(x):
         size = x.shape[0] // grid.far
         parts = [
@@ -116,10 +155,19 @@
             x = x + wide(part)
         return x
 
-    away, xb = start(rows_b, w_out[:, cut:])
-    _, xa = start(after(rows_a, away), w_out[:, :cut])
-    xb = along_near(along_far(xb))
-    xa = along_far(along_near(xa))
+    away_a, keep_a = product(place_a, returned, w_out, 0, cut)
+    xa = keep_a + wide(grid.send(away_a, core=1))
+    middle = xa.shape[0] // 2
+    sent_a = narrow(xa[middle:])
+    xa = xa[:middle] + wide(grid.send(sent_a, near=1))
+    away_b, keep_b = product(
+        place_b, after(returned, sent_a), w_out, cut, w_out.shape[1] - cut
+    )
+    xb = keep_b + wide(grid.send(away_b, core=1))
+    xb = along_far(xb)
+    middle = xb.shape[0] // 2
+    xb = xb[:middle] + wide(grid.send(narrow(xb[middle:]), near=1))
+    xa = along_far(xa)
     return jnp.concatenate([xa, xb], axis=1)
 
 
@@ -217,7 +265,7 @@
 def project(start, parts, order, w_query, w_kv_t, before, place, slots):
     row_width = w_query.shape[1] + w_kv_t.shape[0]
     width = parts[0].shape[1]
-    block = 1024
+    block = next(b for b in (2816, 2560, 1024, 512) if width % b == 0)
     rows = sum(part.shape[0] for part in parts)
     first, last = before is None, place is not None
     vmem = pl.BlockSpec(memory_space=pltpu.VMEM)
@@ -264,6 +312,9 @@
     key_pages,
     value_pages,
     out,
+    key_pool,
+    value_pool,
+    sems,
     key_new,
     query_rot,
     value_own,
@@ -283,6 +334,13 @@
     batches = query_rot.shape[1]
     batch = slots // batches
 
+    cuts = 4
+    size = key_pages.shape[0] // cuts
+    for i, (pool, on_chip) in enumerate(((key_pages, key_pool), (value_pages, value_pool))):
+        for cut in range(cuts):
+            part = pl.ds(cut * size, size)
+            pltpu.make_async_copy(pool.at[part], on_chip.at[part], sems.at[i]).start()
+
     def held(pool, slot, columns):
         return [pool[table[slot, j], :, columns] for j in range(pages)]
 
@@ -325,6 +383,7 @@
         jnp.int32, (columns, columns), 1
     )
 
+    pltpu.make_async_copy(key_pool, key_pool, sems.at[0]).wait()
     own_chances = {}
     for b in range(batches):
         valid = row < lengths[b]
@@ -337,7 +396,7 @@
             columns_p = slice(p * 2 * HEAD, (p + 1) * 2 * HEAD)
             keys = []
             for s in range(batch):
-                keys += held(key_pages, b * batch + s, columns_p)
+                keys += held(key_pool, b * batch + s, columns_p)
             keys.append(key_new[:, columns_p])
             products = jnp.dot(
                 jnp.concatenate(keys, axis=0), wide, preferred_element_type=jnp.float32
@@ -358,12 +417,13 @@
                 jnp.where(same, own_chance, 0.0), axis=1, keepdims=True
             )
 
+    pltpu.make_async_copy(value_pool, value_pool, sems.at[1]).wait()
     for b in range(batches):
         for s in range(batch):
             for p in range(pairs):
                 mine = chance[p, b, pl.ds(s, pair, stride=batch)].astype(jnp.bfloat16)
                 columns_p = slice(p * 2 * HEAD, (p + 1) * 2 * HEAD)
-                values = held(value_pages, b * batch + s, columns_p)
+                values = held(value_pool, b * batch + s, columns_p)
                 both = jnp.dot(
                     mine, jnp.concatenate(values, axis=0), preferred_element_type=jnp.float32
                 )
@@ -402,19 +462,23 @@
     lengths = jnp.tile(lengths.reshape(batches, 1, batch), (1, 1, pair))
     smem = pl.BlockSpec(memory_space=pltpu.SMEM)
     vmem = pl.BlockSpec(memory_space=pltpu.VMEM)
+    hbm = pl.BlockSpec(memory_space=pl.ANY)
     return pl.pallas_call(
         functools.partial(attend_kernel, per_query, per_key),
-        in_specs=[smem, vmem, vmem, vmem, vmem, vmem, vmem],
+        in_specs=[smem, vmem, vmem, vmem, vmem, hbm, hbm],
         out_specs=vmem,
         out_shape=jax.ShapeDtypeStruct((owners, slots, per_query), jnp.bfloat16),
         scratch_shapes=[
+            pltpu.VMEM(key_pages.shape, jnp.bfloat16),
+            pltpu.VMEM(value_pages.shape, jnp.bfloat16),
+            pltpu.SemaphoreType.DMA((2,)),
             pltpu.VMEM((slots, kv_width), jnp.bfloat16),
             pltpu.VMEM((pairs, batches, columns, HEAD), jnp.float32),
             pltpu.VMEM((kv_heads, slots, HEAD), jnp.float32),
             pltpu.VMEM((pairs, batches, columns, span), jnp.float32),
             pltpu.VMEM((pairs, batches, columns, HEAD), jnp.float32),
         ],
-        compiler_params=pltpu.CompilerParams(vmem_limit_bytes=24 * 2**20),
+        compiler_params=pltpu.CompilerParams(vmem_limit_bytes=52 * 2**20),
         cost_estimate=pl.CostEstimate(
             flops=8 * slots * heads * span * HEAD,
             bytes_accessed=4 * slots * span * kv_width,
@@ -448,27 +512,38 @@
     width = hidden_in.shape[1]
     all_slots = owners * slot_count
 
-    unit = width // 8
-    xa, xb = norm(hidden_in, norm_gain, (5 * unit, 3 * unit))
-
-    order = jnp.arange(requests, dtype=jnp.int32)
-    earlier = (kv_owner[:, None] == kv_owner[None, :]) & (order[None, :] < order[:, None])
-    slot_index = jnp.sum(earlier.astype(jnp.int32), axis=1)
-    place = kv_owner * slot_count + slot_index
-
-    def reordered(blocks):
+    crossed = grid.crossed()
+    cut = width // 16 * 11
+    xa, xb = norm(hidden_in, norm_gain, (cut, width - cut))
+
+    def placed(kv_owner):
+        order = jnp.arange(requests, dtype=jnp.int32)
+        earlier = (kv_owner[:, None] == kv_owner[None, :]) & (order[None, :] < order[:, None])
+        return kv_owner * slot_count + jnp.sum(earlier.astype(jnp.int32), axis=1)
+
+    def reordered(place, blocks):
         pick = blocks[:, None] == jnp.arange(owners, dtype=jnp.int32)[None, :]
         moved = jnp.where(pick[:, :, None], place.reshape(1, owners, rows_dev), 0)
         return jnp.sum(moved, axis=1).reshape(requests)
 
-    slots = jnp.arange(all_slots, dtype=jnp.int32)
-    place_in = reordered(grid.blocks(-1))
-    place_out = reordered(grid.blocks(1))
-    route_out = (place_out[:, None] == slots[None, :]).astype(jnp.bfloat16)
-    crossed = grid.crossed()
-    crossed_out = place_out.reshape(owners, rows_dev)[np.array(crossed)].reshape(requests)
-    route_crossed = (crossed_out[:, None] == slots[None, :]).astype(jnp.bfloat16)
-
+    def beside_gather(x):
+        (w,) = fetch(after(w_query, x), limit=44)
+        pieces = [after(w_key, x).T, w_value.T]
+        spare = row_width - per_query - 2 * per_key
+        if spare:
+            pieces.append(jnp.zeros((spare, width), w_key.dtype))
+        place = placed(after(kv_owner, x))
+        return w, jnp.concatenate(pieces, axis=0), place, reordered(place, grid.blocks(-1))
+
+    parts_a, parts_b, others = gather_rows(grid, xa, xb, beside_gather)
+    w_query, w_kv_t, place, place_in = others
+    plain = list(range(owners))
+    total = project(0, parts_a, plain, w_query, w_kv_t, None, None, all_slots)
+    total = project(cut, parts_b, crossed, w_query, w_kv_t, total, place_in, all_slots)
+    outbound = total.reshape(owners, slot_count, row_width)
+    place = after(place, outbound)
+    place_out = reordered(place, grid.blocks(1))
+    crossed_out = reordered(place, grid.blocks(1, crossed))
     mine = lax.axis_index(AXES) * slot_count + jnp.arange(slot_count, dtype=jnp.int32)
     lengths = jnp.sum(jnp.where(place[:, None] == mine[None, :], cached[:, None], 0), axis=0)
     halfway = HEAD // 2
@@ -479,42 +554,21 @@
     sine_part = jnp.sin(angles)
     cosine = jnp.concatenate([cosine_part, cosine_part], axis=1)
     sine = jnp.concatenate([-sine_part, sine_part], axis=1)
-
-    pieces = [w_key.T, w_value.T]
-    spare = row_width - per_query - 2 * per_key
-    if spare:
-        pieces.append(jnp.zeros((spare, width), w_key.dtype))
-    w_kv_t = jnp.concatenate(pieces, axis=0)
-
-    def beside_gather(x):
-        (w,) = fetch(after(w_query, x), limit=44)
-        return w, w_kv_t, place_in, place_out, cosine, sine
-
-    parts_a, parts_b, others = gather_rows(grid, xa, xb, beside_gather)
-    w_query, w_kv_t, place_in, place_out, cosine, sine = others
-    plain = list(range(owners))
-    total = project(0, parts_a, plain, w_query, w_kv_t, None, None, all_slots)
-    total = project(5 * unit, parts_b, crossed, w_query, w_kv_t, total, place_in, all_slots)
-    outbound = total.reshape(owners, slot_count, row_width)
     inbound = lax.all_to_all(outbound, AXES, split_axis=0, concat_axis=0, tiled=True)
-    keys, values = fetch(after(key_pages, outbound)[0], value_pages[0], limit=44)
     attended = attend(
         inbound,
         lengths,
         page_table[0],
         cosine,
         sine,
-        keys,
-        values,
+        key_pages[0],
+        value_pages[0],
         per_query,
         per_key,
     )
-    (w_out,) = fetch(after(w_out, attended), limit=44)
     returned = lax.all_to_all(attended, AXES, split_axis=0, concat_axis=0, tiled=True)
     returned = returned.reshape(all_slots, per_query)
-    rows_a = narrow(jnp.dot(route_out, returned, preferred_element_type=jnp.float32))
-    rows_b = narrow(jnp.dot(route_crossed, returned, preferred_element_type=jnp.float32))
-    summed = scatter_sum(grid, rows_a, rows_b, w_out, 5 * unit)
+    summed = scatter_sum(grid, place_out, crossed_out, returned, w_out, cut)
     return narrow(wide(hidden_in) + summed)
 
 

time: 101 us -> 105 us (1.040)
  waiting for transfers between devices: 21.9 us -> 35.8 us
  matrix products: 6.27 us -> 0 us
  local copies, waits for them, and re-layouts: 15.5 us -> 11.9 us
  other arithmetic: 6.54 us -> 4.71 us
    all_to_all x1, waiting for transfers between devices: 3.34 us -> 10.3 us  [on_device(): lax.all_to_all(outbound, AXES, split_axis=0, concat_axis=0, tiled=True)]
    pallas_call x3 -> x1, Pallas kernels: 10.3 us -> 3.39 us  [fetch(): pl.pallas_call(fetch_kernel, in_specs=[pl.BlockSpec(memory_space=pl.ANY)]...]
    dot_general x3 -> x0, matrix products: 6.27 us -> none  [the longest x2 6.04 us: start(): x = jnp.dot(rows, w, preferred_element_type=jnp.float32)]
    pallas_call x0 -> x2, Pallas kernels: none -> 6.03 us  [product(): pl.pallas_call(functools.partial(product_kernel, start, step), in_specs=[...]
    all_to_all x1, waiting for transfers between devices: 2.56 us -> 8.29 us  [on_device(): lax.all_to_all(attended, AXES, split_axis=0, concat_axis=0, tiled=True)]
    unnamed x22 -> x32, local copies, waits for them, and re-layouts: 13.3 us -> 9.63 us
    pallas_call x1, Pallas kernels: 3.41 us -> 5.97 us  [attend(): pl.pallas_call(functools.partial(attend_kernel, per_query, per_key), in_s...]
    ppermute x24, starting transfers between devices: 23.7 us -> 25.8 us  [send(): return lax.ppermute(x, AXES, self.perm(far, near, core))]
  transfers between devices with their start and end apart: 26 -> 26, of which waited for: 9 -> 12; matrix products, arithmetic and copies ran while one was open for 11% -> 6% of each run, Pallas kernels for 12% -> 5%
where the time goes in v7:
time: 105 us; the launch traced here: 104 us
  waiting for transfers between devices  35.8 us (34%)
  starting transfers between devices  32.9 us (31%)
  Pallas kernels  18.7 us (18%)
  local copies, waits for them, and re-layouts  11.9 us (11%)
  other arithmetic  4.71 us (4%)
    ppermute x24, starting transfers between devices, send(): return lax.ppermute(x, AXES, self.perm(far, near, core))  25.8 us
    ppermute x24, waiting for transfers between devices, send(): return lax.ppermute(x, AXES, self.perm(far, near, core))  17.2 us
    all_to_all x1, waiting for transfers between devices, on_device(): lax.all_to_all(outbound, AXES, split_axis=0, concat_axis=0, tiled=True)  10.3 us
    unnamed x32, local copies, waits for them, and re-layouts  9.63 us
    all_to_all x1, waiting for transfers between devices, on_device(): lax.all_to_all(attended, AXES, split_axis=0, concat_axis=0, tiled=True)  8.29 us
    pallas_call x2, Pallas kernels, product(): pl.pallas_call(functools.partial(product_kernel, start, step), in_specs=[...  6.03 us
    pallas_call x1, Pallas kernels, attend(): pl.pallas_call(functools.partial(attend_kernel, per_query, per_key), in_s...  5.97 us
    all_to_all x1, starting transfers between devices, on_device(): lax.all_to_all(attended, AXES, split_axis=0, concat_axis=0, tiled=True)  3.54 us
  transfers between devices with their start and end apart: 26, of which 12 were waited for; matrix products, arithmetic and copies ran while one was open for 6% of the time, Pallas kernels for 5%

profile of v7, /device:TPU:0, one launch (start us, length us, event | category | flops | bytes accessed | tf_op | source)
XLA Modules:
  0.0 104.5 jit_solution(18367769342193751513)
XLA Ops:
  1.9 3.1 %collective-permute-start = (bf16[8,5632]{1,0:T(8,128)(2,1)S(1)}, bf16[8,5632]{1,0:T(8,128)(2,1)S(1)}, u32[]{:S(2)}, u32[]{:S(2)}) collective-permute-start(bf16[8,5632]{1,0:T(8,128)(2,1)S(1)} %get-tuple-element.26), channel_id=1, source_target_pairs={{0,4},{1,5},{2,6},{3,7},{4,8},{5,9},{6,10},{7,11},{8,12},{9,13},{1... | collective-permute-start | bytes 270344 | tf_op jit(solution)/shard_map/ppermute | solution.py:41
  4.9 2.6 %collective-permute-start.1 = (bf16[8,5632]{1,0:T(8,128)(2,1)S(1)}, bf16[8,5632]{1,0:T(8,128)(2,1)S(1)}, u32[]{:S(2)}, u32[]{:S(2)}) collective-permute-start(bf16[8,5632]{1,0:T(8,128)(2,1)S(1)} %get-tuple-element.26), channel_id=1, source_target_pairs={{0,8},{1,9},{2,10},{3,11},{4,12},{5,13},{6,14},{7,15},{8,0},{9,1},... | collective-permute-start | bytes 270344 | tf_op jit(solution)/shard_map/ppermute | solution.py:41
  11.2 1.7 %collective-permute-done.3 = bf16[8,2560]{1,0:T(8,128)(2,1)S(1)} collective-permute-done((bf16[8,2560]{1,0:T(8,128)(2,1)S(1)}, bf16[8,2560]{1,0:T(8,128)(2,1)S(1)}, u32[]{:S(2)}, u32[]{:S(2)}) %collective-permute-start.3) | collective-permute-done | bytes 40992 | tf_op jit(solution)/shard_map/ppermute | solution.py:41
  13.8 2.3 %collective-permute-start.5 = (bf16[16,2560]{1,0:T(8,128)(2,1)S(1)}, bf16[16,2560]{1,0:T(8,128)(2,1)S(1)}, u32[]{:S(2)}, u32[]{:S(2)}) collective-permute-start(bf16[16,2560]{1,0:T(8,128)(2,1)S(1)} %pad_maximum_fusion.2.refs_0_), channel_id=1, source_target_pairs={{0,4},{1,5},{2,6},{3,7},{4,8},{5,9},{6,10},{7,11},{8,12},{9,13},{1... | collective-permute-start | bytes 245768 | tf_op jit(solution)/shard_map/ppermute | solution.py:41
  16.0 1.7 %collective-permute-start.6 = (bf16[16,2560]{1,0:T(8,128)(2,1)S(1)}, bf16[16,2560]{1,0:T(8,128)(2,1)S(1)}, u32[]{:S(2)}, u32[]{:S(2)}) collective-permute-start(bf16[16,2560]{1,0:T(8,128)(2,1)S(1)} %pad_maximum_fusion.2.refs_0_), channel_id=1, source_target_pairs={{0,8},{1,9},{2,10},{3,11},{4,12},{5,13},{6,14},{7,15},{8,0},{9,1},... | collective-permute-start | bytes 245768 | tf_op jit(solution)/shard_map/ppermute | solution.py:41
  20.0 1.7 %pad_maximum_fusion.refs_5_.refs_9_ = bf16[128,8192]{1,0:T(8,128)(2,1)S(1)} fusion(bf16[64,8192]{1,0:T(8,128)(2,1)} %bitcast.23, bf16[64,8192]{1,0:T(8,128)(2,1)} %bitcast.24), kind=kLoop, calls=%fused_computation | loop fusion | flops 4194304 | bytes 4194304 | tf_op jit(solution)/shard_map/concatenate | solution.py:536
  22.5 3.4 %fetch.1.refs_4_.refs_8_ = bf16[8192,512]{1,0:T(8,128)(2,1)S(1)} custom-call(bf16[8192,512]{1,0:T(8,128)(2,1)} %refs_0_), custom_call_target="tpu_custom_call" | custom-call | bytes 16777216 | tf_op jit(solution)/shard_map/fetch/pallas_call | solution.py:209
  25.9 3.3 %copy-done = bf16[8192,512]{1,0:T(8,128)(2,1)} copy-done((bf16[8192,512]{1,0:T(8,128)(2,1)}, bf16[8192,512]{1,0:T(8,128)(2,1)S(1)}, u32[]{:S(2)}) %copy-start) | copy-done | bytes 8388632
  32.3 3.4 %copy-done.1 = bf16[8192,512]{1,0:T(8,128)(2,1)S(1)} copy-done((bf16[8192,512]{1,0:T(8,128)(2,1)S(1)}, bf16[8192,512]{1,0:T(8,128)(2,1)}, u32[]{:S(2)}) %copy-start.1) | copy-done | bytes 8388632
  35.7 1.6 %project.2.refs_10_ = f32[128,640]{1,0:T(8,128)S(1)} custom-call(bf16[32,5632]{1,0:T(8,128)(2,1)S(1)} %pad_maximum_fusion.1.refs_0_, bf16[32,5632]{1,0:T(8,128)(2,1)S(1)} %collective-permute-done.4.refs_1_, bf16[32,5632]{1,0:T(8,128)(2,1)S(1)} %collective-permute-done.12.refs_2_, bf16[32,5632]{1,0:T(8,128)(2,1)S(1)} %collective-permute-done.13.refs_3_, ...), custom_call_target="tpu_custom_call" | custom-call | flops 922746880 | bytes 7208960 | tf_op jit(solution)/shard_map/project/pallas_call | solution.py:287
  37.4 1.6 %project.3 = bf16[256,640]{1,0:T(8,128)(2,1)} custom-call(bf16[16,2560]{1,0:T(8,128)(2,1)S(1)} %copy-done.5, bf16[16,2560]{1,0:T(8,128)(2,1)S(1)} %copy-done.7, bf16[16,2560]{1,0:T(8,128)(2,1)S(1)} %copy-done.9, bf16[16,2560]{1,0:T(8,128)(2,1)S(1)} %copy-done.11, bf16[16,2560]{1,0:T(8,128)(2,1)S(1)} %collective-permute-done.8.refs_4_, ...), custom_call_target="tpu_custom_call" | custom-call | flops 419430400 | bytes 3276800 | tf_op jit(solution)/shard_map/project/pallas_call | solution.py:287
  39.0 3.5 %all-to-all-start = ((bf16[16,16,640]{2,1,0:T(8,128)(2,1)}), bf16[16,16,640]{2,1,0:T(8,128)(2,1)S(1)}, u32[]{:S(2)}, u32[]{:S(2)}) async-start(bf16[16,16,640]{2,1,0:T(8,128)(2,1)} %bitcast.6), calls=%async_computation | async-start | bytes 655360 | tf_op jit(solution)/shard_map/all_to_all | solution.py:557
  43.3 10.3 %all-to-all-done.inbound = bf16[16,16,640]{2,1,0:T(8,128)(2,1)S(1)} async-done(((bf16[16,16,640]{2,1,0:T(8,128)(2,1)}), bf16[16,16,640]{2,1,0:T(8,128)(2,1)S(1)}, u32[]{:S(2)}, u32[]{:S(2)}) %all-to-all-start) | async-done | bytes 327712 | tf_op jit(solution)/shard_map/all_to_all | solution.py:557
  53.6 6.0 %attend.1 = bf16[16,16,512]{2,1,0:T(8,128)(2,1)} custom-call(s32[16,4]{1,0:T(8,128)S(1)} %copy.20.table, s32[2,1,128]{2,1,0:T(1,128)S(1)} %bitcast.19, bf16[16,16,640]{2,1,0:T(8,128)(2,1)S(1)} %all-to-all-done.inbound, f32[16,128]{1,0:T(8,128)S(1)} %pad_maximum_fusion.3.cosine, f32[16,128]{1,0:T(8,128)S(1)} %pad_maximum_fusion.4.sine, ...), custom_call_target="tpu_custom_call" | custom-call | flops 134217728 | bytes 8388608 | tf_op jit(solution)/shard_map/attend/pallas_call | solution.py:466
  59.6 3.5 %all-to-all-start.1 = ((bf16[16,16,512]{2,1,0:T(8,128)(2,1)}), bf16[16,16,512]{2,1,0:T(8,128)(2,1)S(1)}, u32[]{:S(2)}, u32[]{:S(2)}) async-start(bf16[16,16,512]{2,1,0:T(8,128)(2,1)} %attend.1), calls=%async_computation.1 | async-start | bytes 524288 | tf_op jit(solution)/shard_map/all_to_all | solution.py:569
  64.8 8.3 %all-to-all-done.1 = bf16[16,16,512]{2,1,0:T(8,128)(2,1)S(1)} async-done(((bf16[16,16,512]{2,1,0:T(8,128)(2,1)}), bf16[16,16,512]{2,1,0:T(8,128)(2,1)S(1)}, u32[]{:S(2)}, u32[]{:S(2)}) %all-to-all-start.1) | async-done | bytes 262176 | tf_op jit(solution)/shard_map/all_to_all | solution.py:569
  73.1 3.7 %product.2 = (bf16[64,5632]{1,0:T(8,128)(2,1)S(1)}, f32[64,5632]{1,0:T(8,128)S(1)}) custom-call(s32[1,128]{1,0:T(1,128)S(1)} %reshape_reshape.6.place, bf16[256,512]{1,0:T(8,128)(2,1)S(1)} %bitcast.16, bf16[512,8192]{1,0:T(8,128)(2,1)} %w_out.3), custom_call_target="tpu_custom_call" | custom-call | flops 738197504 | bytes 5767168 | tf_op jit(solution)/shard_map/product/pallas_call | solution.py:125
  77.0 2.1 %collective-permute-done.14 = bf16[64,5632]{1,0:T(8,128)(2,1)S(1)} collective-permute-done((bf16[64,5632]{1,0:T(8,128)(2,1)S(1)}, bf16[64,5632]{1,0:T(8,128)(2,1)S(1)}, u32[]{:S(2)}, u32[]{:S(2)}) %collective-permute-start.14) | collective-permute-done | bytes 720928 | tf_op jit(solution)/shard_map/ppermute | solution.py:41
  79.3 2.3 %product.3 = (bf16[64,2560]{1,0:T(8,128)(2,1)S(1)}, f32[64,2560]{1,0:T(8,128)S(1)}) custom-call(s32[1,128]{1,0:T(1,128)S(1)} %reshape_reshape.7.place, bf16[256,512]{1,0:T(8,128)(2,1)S(1)} %bitcast.17, bf16[512,8192]{1,0:T(8,128)(2,1)} %w_out.3), custom_call_target="tpu_custom_call" | custom-call | flops 335544320 | bytes 2621440 | tf_op jit(solution)/shard_map/product/pallas_call | solution.py:125
  85.0 2.4 %collective-permute-start.22 = (bf16[16,2560]{1,0:T(8,128)(2,1)S(1)}, bf16[16,2560]{1,0:T(8,128)(2,1)S(1)}, u32[]{:S(2)}, u32[]{:S(2)}) collective-permute-start(bf16[16,2560]{1,0:T(8,128)(2,1)S(1)} %get-tuple-element.57), channel_id=1, source_target_pairs={{0,12},{1,13},{2,14},{3,15},{4,0},{5,1},{6,2},{7,3},{8,4},{9,5},{1... | collective-permute-start | bytes 245768 | tf_op jit(solution)/shard_map/ppermute | solution.py:41
  87.4 5.1 %collective-permute-done.15 = bf16[32,5632]{1,0:T(8,128)(2,1)S(1)} collective-permute-done((bf16[32,5632]{1,0:T(8,128)(2,1)S(1)}, bf16[32,5632]{1,0:T(8,128)(2,1)S(1)}, u32[]{:S(2)}, u32[]{:S(2)}) %collective-permute-start.15) | collective-permute-done | bytes 360480 | tf_op jit(solution)/shard_map/ppermute | solution.py:41
  94.0 1.9 %collective-permute-start.16 = (bf16[8,5632]{1,0:T(8,128)(2,1)S(1)}, bf16[8,5632]{1,0:T(8,128)(2,1)S(1)}, u32[]{:S(2)}, u32[]{:S(2)}) collective-permute-start(bf16[8,5632]{1,0:T(8,128)(2,1)S(1)} %get-tuple-element.53), channel_id=1, source_target_pairs={{0,4},{1,5},{2,6},{3,7},{4,8},{5,9},{6,10},{7,11},{8,12},{9,13},{1... | collective-permute-start | bytes 270344 | tf_op jit(solution)/shard_map/ppermute | solution.py:41
  98.4 2.9 %collective-permute-done.16 = bf16[8,5632]{1,0:T(8,128)(2,1)S(1)} collective-permute-done((bf16[8,5632]{1,0:T(8,128)(2,1)S(1)}, bf16[8,5632]{1,0:T(8,128)(2,1)S(1)}, u32[]{:S(2)}, u32[]{:S(2)}) %collective-permute-start.16) | collective-permute-done | bytes 90144 | tf_op jit(solution)/shard_map/ppermute | solution.py:41
  101.2 2.5 %collective-permute-done.17 = bf16[8,5632]{1,0:T(8,128)(2,1)S(1)} collective-permute-done((bf16[8,5632]{1,0:T(8,128)(2,1)S(1)}, bf16[8,5632]{1,0:T(8,128)(2,1)S(1)}, u32[]{:S(2)}, u32[]{:S(2)}) %collective-permute-start.17) | collective-permute-done | bytes 90144 | tf_op jit(solution)/shard_map/ppermute | solution.py:41
  (108 shorter events, 23.4 us)
Async XLA Ops:
  1.9 11.0 %collective-permute-start = (bf16[8,5632]{1,0:T(8,128)(2,1)S(1)}, bf16[8,5632]{1,0:T(8,128)(2,1)S(1)}, u32[]{:S(2)}, u32[]{:S(2)}) collective-permute-start(bf16[8,5632]{1,0:T(8,128)(2,1)S(1)} %get-tuple-element.26), channel_id=1, source_target_pairs={{0,4},{1,5},{2,6},{3,7},{4,8},{5,9},{6,10},{7,11},{8,12},{9,13},{1... | collective-permute-start | bytes 270344 | tf_op jit(solution)/shard_map/ppermute | solution.py:41
  4.9 8.6 %collective-permute-start.1 = (bf16[8,5632]{1,0:T(8,128)(2,1)S(1)}, bf16[8,5632]{1,0:T(8,128)(2,1)S(1)}, u32[]{:S(2)}, u32[]{:S(2)}) collective-permute-start(bf16[8,5632]{1,0:T(8,128)(2,1)S(1)} %get-tuple-element.26), channel_id=1, source_target_pairs={{0,8},{1,9},{2,10},{3,11},{4,12},{5,13},{6,14},{7,15},{8,0},{9,1},... | collective-permute-start | bytes 270344 | tf_op jit(solution)/shard_map/ppermute | solution.py:41
  7.5 6.2 %collective-permute-start.2 = (bf16[8,5632]{1,0:T(8,128)(2,1)S(1)}, bf16[8,5632]{1,0:T(8,128)(2,1)S(1)}, u32[]{:S(2)}, u32[]{:S(2)}) collective-permute-start(bf16[8,5632]{1,0:T(8,128)(2,1)S(1)} %get-tuple-element.26), channel_id=1, source_target_pairs={{0,12},{1,13},{2,14},{3,15},{4,0},{5,1},{6,2},{7,3},{8,4},{9,5},{1... | collective-permute-start | bytes 270344 | tf_op jit(solution)/shard_map/ppermute | solution.py:41
  8.9 4.0 %collective-permute-start.3 = (bf16[8,2560]{1,0:T(8,128)(2,1)S(1)}, bf16[8,2560]{1,0:T(8,128)(2,1)S(1)}, u32[]{:S(2)}, u32[]{:S(2)}) collective-permute-start(bf16[8,2560]{1,0:T(8,128)(2,1)S(1)} %get-tuple-element.27), channel_id=1, source_target_pairs={{0,2},{1,3},{2,0},{3,1},{4,6},{5,7},{6,4},{7,5},{8,10},{9,11},{10,... | collective-permute-start | bytes 122888 | tf_op jit(solution)/shard_map/ppermute | solution.py:41
  13.8 15.4 %collective-permute-start.5 = (bf16[16,2560]{1,0:T(8,128)(2,1)S(1)}, bf16[16,2560]{1,0:T(8,128)(2,1)S(1)}, u32[]{:S(2)}, u32[]{:S(2)}) collective-permute-start(bf16[16,2560]{1,0:T(8,128)(2,1)S(1)} %pad_maximum_fusion.2.refs_0_), channel_id=1, source_target_pairs={{0,4},{1,5},{2,6},{3,7},{4,8},{5,9},{6,10},{7,11},{8,12},{9,13},{1... | collective-permute-start | bytes 245768 | tf_op jit(solution)/shard_map/ppermute | solution.py:41
  16.0 13.2 %collective-permute-start.6 = (bf16[16,2560]{1,0:T(8,128)(2,1)S(1)}, bf16[16,2560]{1,0:T(8,128)(2,1)S(1)}, u32[]{:S(2)}, u32[]{:S(2)}) collective-permute-start(bf16[16,2560]{1,0:T(8,128)(2,1)S(1)} %pad_maximum_fusion.2.refs_0_), channel_id=1, source_target_pairs={{0,8},{1,9},{2,10},{3,11},{4,12},{5,13},{6,14},{7,15},{8,0},{9,1},... | collective-permute-start | bytes 245768 | tf_op jit(solution)/shard_map/ppermute | solution.py:41
  17.8 11.4 %collective-permute-start.7 = (bf16[16,2560]{1,0:T(8,128)(2,1)S(1)}, bf16[16,2560]{1,0:T(8,128)(2,1)S(1)}, u32[]{:S(2)}, u32[]{:S(2)}) collective-permute-start(bf16[16,2560]{1,0:T(8,128)(2,1)S(1)} %pad_maximum_fusion.2.refs_0_), channel_id=1, source_target_pairs={{0,12},{1,13},{2,14},{3,15},{4,0},{5,1},{6,2},{7,3},{8,4},{9,5},{1... | collective-permute-start | bytes 245768 | tf_op jit(solution)/shard_map/ppermute | solution.py:41
  18.5 12.0 %collective-permute-start.4 = (bf16[32,5632]{1,0:T(8,128)(2,1)S(1)}, bf16[32,5632]{1,0:T(8,128)(2,1)S(1)}, u32[]{:S(2)}, u32[]{:S(2)}) collective-permute-start(bf16[32,5632]{1,0:T(8,128)(2,1)S(1)} %pad_maximum_fusion.1.refs_0_), channel_id=1, source_target_pairs={{0,2},{1,3},{2,0},{3,1},{4,6},{5,7},{6,4},{7,5},{8,10},{9,11},{10,... | collective-permute-start | bytes 1081352 | tf_op jit(solution)/shard_map/ppermute | solution.py:41
  20.0 11.6 %collective-permute-start.12 = (bf16[32,5632]{1,0:T(8,128)(2,1)S(1)}, bf16[32,5632]{1,0:T(8,128)(2,1)S(1)}, u32[]{:S(2)}, u32[]{:S(2)}) collective-permute-start(bf16[32,5632]{1,0:T(8,128)(2,1)S(1)} %pad_maximum_fusion.1.refs_0_), channel_id=1, source_target_pairs={{0,1},{1,0},{2,3},{3,2},{4,5},{5,4},{6,7},{7,6},{8,9},{9,8},{10,11... | collective-permute-start | bytes 1081352 | tf_op jit(solution)/shard_map/ppermute | solution.py:41
  31.0 6.2 %collective-permute-start.8 = (bf16[16,2560]{1,0:T(8,128)(2,1)}, bf16[16,2560]{1,0:T(8,128)(2,1)S(1)}, u32[]{:S(2)}, u32[]{:S(2)}) collective-permute-start(bf16[16,2560]{1,0:T(8,128)(2,1)} %copy-done.4), channel_id=1, source_target_pairs={{0,1},{1,0},{2,3},{3,2},{4,5},{5,4},{6,7},{7,6},{8,9},{9,8},{10,11... | collective-permute-start | bytes 245768 | tf_op jit(solution)/shard_map/ppermute | solution.py:41
  31.1 6.2 %collective-permute-start.10 = (bf16[16,2560]{1,0:T(8,128)(2,1)}, bf16[16,2560]{1,0:T(8,128)(2,1)S(1)}, u32[]{:S(2)}, u32[]{:S(2)}) collective-permute-start(bf16[16,2560]{1,0:T(8,128)(2,1)} %copy-done.8), channel_id=1, source_target_pairs={{0,1},{1,0},{2,3},{3,2},{4,5},{5,4},{6,7},{7,6},{8,9},{9,8},{10,11... | collective-permute-start | bytes 245768 | tf_op jit(solution)/shard_map/ppermute | solution.py:41
  31.5 5.8 %collective-permute-start.11 = (bf16[16,2560]{1,0:T(8,128)(2,1)}, bf16[16,2560]{1,0:T(8,128)(2,1)S(1)}, u32[]{:S(2)}, u32[]{:S(2)}) collective-permute-start(bf16[16,2560]{1,0:T(8,128)(2,1)} %copy-done.10), channel_id=1, source_target_pairs={{0,1},{1,0},{2,3},{3,2},{4,5},{5,4},{6,7},{7,6},{8,9},{9,8},{10,11... | collective-permute-start | bytes 245768 | tf_op jit(solution)/shard_map/ppermute | solution.py:41
  31.6 5.7 %collective-permute-start.9 = (bf16[16,2560]{1,0:T(8,128)(2,1)}, bf16[16,2560]{1,0:T(8,128)(2,1)S(1)}, u32[]{:S(2)}, u32[]{:S(2)}) collective-permute-start(bf16[16,2560]{1,0:T(8,128)(2,1)} %copy-done.6), channel_id=1, source_target_pairs={{0,1},{1,0},{2,3},{3,2},{4,5},{5,4},{6,7},{7,6},{8,9},{9,8},{10,11... | collective-permute-start | bytes 245768 | tf_op jit(solution)/shard_map/ppermute | solution.py:41
  39.0 14.6 %all-to-all-start = ((bf16[16,16,640]{2,1,0:T(8,128)(2,1)}), bf16[16,16,640]{2,1,0:T(8,128)(2,1)S(1)}, u32[]{:S(2)}, u32[]{:S(2)}) async-start(bf16[16,16,640]{2,1,0:T(8,128)(2,1)} %bitcast.6), calls=%async_computation | async-start | bytes 655360 | tf_op jit(solution)/shard_map/all_to_all | solution.py:557
  59.6 13.6 %all-to-all-start.1 = ((bf16[16,16,512]{2,1,0:T(8,128)(2,1)}), bf16[16,16,512]{2,1,0:T(8,128)(2,1)S(1)}, u32[]{:S(2)}, u32[]{:S(2)}) async-start(bf16[16,16,512]{2,1,0:T(8,128)(2,1)} %attend.1), calls=%async_computation.1 | async-start | bytes 524288 | tf_op jit(solution)/shard_map/all_to_all | solution.py:569
  76.9 2.3 %collective-permute-start.14 = (bf16[64,5632]{1,0:T(8,128)(2,1)S(1)}, bf16[64,5632]{1,0:T(8,128)(2,1)S(1)}, u32[]{:S(2)}, u32[]{:S(2)}) collective-permute-start(bf16[64,5632]{1,0:T(8,128)(2,1)S(1)} %get-tuple-element.43), channel_id=1, source_target_pairs={{0,1},{1,0},{2,3},{3,2},{4,5},{5,4},{6,7},{7,6},{8,9},{9,8},{10,11... | collective-permute-start | bytes 2162696 | tf_op jit(solution)/shard_map/ppermute | solution.py:41
  81.8 10.7 %collective-permute-start.15 = (bf16[32,5632]{1,0:T(8,128)(2,1)S(1)}, bf16[32,5632]{1,0:T(8,128)(2,1)S(1)}, u32[]{:S(2)}, u32[]{:S(2)}) collective-permute-start(bf16[32,5632]{1,0:T(8,128)(2,1)S(1)} %slice.82), channel_id=1, source_target_pairs={{0,2},{1,3},{2,0},{3,1},{4,6},{5,7},{6,4},{7,5},{8,10},{9,11},{10,... | collective-permute-start | bytes 1081352 | tf_op jit(solution)/shard_map/ppermute | solution.py:41
  83.4 9.2 %collective-permute-start.20 = (bf16[16,2560]{1,0:T(8,128)(2,1)S(1)}, bf16[16,2560]{1,0:T(8,128)(2,1)S(1)}, u32[]{:S(2)}, u32[]{:S(2)}) collective-permute-start(bf16[16,2560]{1,0:T(8,128)(2,1)S(1)} %get-tuple-element.56), channel_id=1, source_target_pairs={{0,4},{1,5},{2,6},{3,7},{4,8},{5,9},{6,10},{7,11},{8,12},{9,13},{1... | collective-permute-start | bytes 245768 | tf_op jit(solution)/shard_map/ppermute | solution.py:41
  83.8 9.5 %collective-permute-start.21 = (bf16[16,2560]{1,0:T(8,128)(2,1)S(1)}, bf16[16,2560]{1,0:T(8,128)(2,1)S(1)}, u32[]{:S(2)}, u32[]{:S(2)}) collective-permute-start(bf16[16,2560]{1,0:T(8,128)(2,1)S(1)} %get-tuple-element.58), channel_id=1, source_target_pairs={{0,8},{1,9},{2,10},{3,11},{4,12},{5,13},{6,14},{7,15},{8,0},{9,1},... | collective-permute-start | bytes 245768 | tf_op jit(solution)/shard_map/ppermute | solution.py:41
  85.0 8.4 %collective-permute-start.22 = (bf16[16,2560]{1,0:T(8,128)(2,1)S(1)}, bf16[16,2560]{1,0:T(8,128)(2,1)S(1)}, u32[]{:S(2)}, u32[]{:S(2)}) collective-permute-start(bf16[16,2560]{1,0:T(8,128)(2,1)S(1)} %get-tuple-element.57), channel_id=1, source_target_pairs={{0,12},{1,13},{2,14},{3,15},{4,0},{5,1},{6,2},{7,3},{8,4},{9,5},{1... | collective-permute-start | bytes 245768 | tf_op jit(solution)/shard_map/ppermute | solution.py:41
  93.4 4.9 %collective-permute-start.23 = (bf16[8,2560]{1,0:T(8,128)(2,1)S(1)}, bf16[8,2560]{1,0:T(8,128)(2,1)S(1)}, u32[]{:S(2)}, u32[]{:S(2)}) collective-permute-start(bf16[8,2560]{1,0:T(8,128)(2,1)S(1)} %slice.83), channel_id=1, source_target_pairs={{0,2},{1,3},{2,0},{3,1},{4,6},{5,7},{6,4},{7,5},{8,10},{9,11},{10,... | collective-permute-start | bytes 122888 | tf_op jit(solution)/shard_map/ppermute | solution.py:41
  94.0 7.2 %collective-permute-start.16 = (bf16[8,5632]{1,0:T(8,128)(2,1)S(1)}, bf16[8,5632]{1,0:T(8,128)(2,1)S(1)}, u32[]{:S(2)}, u32[]{:S(2)}) collective-permute-start(bf16[8,5632]{1,0:T(8,128)(2,1)S(1)} %get-tuple-element.53), channel_id=1, source_target_pairs={{0,4},{1,5},{2,6},{3,7},{4,8},{5,9},{6,10},{7,11},{8,12},{9,13},{1... | collective-permute-start | bytes 270344 | tf_op jit(solution)/shard_map/ppermute | solution.py:41
  95.9 7.8 %collective-permute-start.17 = (bf16[8,5632]{1,0:T(8,128)(2,1)S(1)}, bf16[8,5632]{1,0:T(8,128)(2,1)S(1)}, u32[]{:S(2)}, u32[]{:S(2)}) collective-permute-start(bf16[8,5632]{1,0:T(8,128)(2,1)S(1)} %get-tuple-element.55), channel_id=1, source_target_pairs={{0,8},{1,9},{2,10},{3,11},{4,12},{5,13},{6,14},{7,15},{8,0},{9,1},... | collective-permute-start | bytes 270344 | tf_op jit(solution)/shard_map/ppermute | solution.py:41
  96.8 6.9 %collective-permute-start.18 = (bf16[8,5632]{1,0:T(8,128)(2,1)S(1)}, bf16[8,5632]{1,0:T(8,128)(2,1)S(1)}, u32[]{:S(2)}, u32[]{:S(2)}) collective-permute-start(bf16[8,5632]{1,0:T(8,128)(2,1)S(1)} %get-tuple-element.54), channel_id=1, source_target_pairs={{0,12},{1,13},{2,14},{3,15},{4,0},{5,1},{6,2},{7,3},{8,4},{9,5},{1... | collective-permute-start | bytes 270344 | tf_op jit(solution)/shard_map/ppermute | solution.py:41
  (18 other events, 60.0 us)

commit v8 on v7

--- a/solution.py
+++ b/solution.py
@@ -94,80 +94,89 @@
     return x.astype(jnp.float32)
 
 
-def product_kernel(start, step, place, returned, w_out, away, keep, held, sems):
+def product_kernel(cuts, place_a, place_b, returned, w_out, away_a, keep_a, away_b, keep_b, held, sems):
     copies = []
-    for i in range(held.shape[1] // step):
-        here = pl.ds(i * step, step)
-        copies.append(
-            pltpu.make_async_copy(
-                w_out.at[:, pl.ds(start + i * step, step)], held.at[:, here], sems.at[i]
-            )
+    for i, (start, stop) in enumerate(cuts):
+        here = pl.ds(start, stop - start)
+        copies.append(pltpu.make_async_copy(w_out.at[:, here], held.at[:, here], sems.at[i]))
+        copies[-1].start()
+    slots = lax.broadcasted_iota(jnp.int32, (returned.shape[0], place_a.shape[1]), 0)
+
+    def picked(place):
+        route = jnp.where(slots == place[...], 1.0, 0.0).astype(jnp.bfloat16)
+        rows = lax.dot_general(
+            route, returned[...], (((0,), (0,)), ((), ())), preferred_element_type=jnp.float32
         )
-        copies[-1].start()
-    slots = lax.broadcasted_iota(jnp.int32, (returned.shape[0], place.shape[1]), 0)
-    route = jnp.where(slots == place[...], 1.0, 0.0).astype(jnp.bfloat16)
-    rows = lax.dot_general(
-        route, returned[...], (((0,), (0,)), ((), ())), preferred_element_type=jnp.float32
-    ).astype(jnp.bfloat16)
-    half = keep.shape[0]
-    for i, copy in enumerate(copies):
+        return rows.astype(jnp.bfloat16)
+
+    rows_a, rows_b = picked(place_a), picked(place_b)
+    half = keep_a.shape[0]
+    middle = keep_a.shape[1]
+    for copy, (start, stop) in zip(copies, cuts):
         copy.wait()
-        here = slice(i * step, (i + 1) * step)
-        x = jnp.dot(rows, held[:, here], preferred_element_type=jnp.float32)
+        rows, away, keep = (rows_a, away_a, keep_a) if start < middle else (rows_b, away_b, keep_b)
+        x = jnp.dot(rows, held[:, start:stop], preferred_element_type=jnp.float32)
+        begin = start if start < middle else start - middle
+        here = slice(begin, begin + stop - start)
         keep[:, here] = x[:half]
         away[:, here] = x[half:].astype(jnp.bfloat16)
 
 
-def product(place, returned, w_out, start, width):
-    rows = place.shape[0]
-    step = 512
+def product(place_a, place_b, returned, w_out, cut):
+    rows = place_a.shape[0]
+    depth, width = w_out.shape
+    cuts = []
+    for start, stop in ((0, cut), (cut, width)):
+        while start < stop:
+            cuts.append((start, min(start + 1024, stop)))
+            start = cuts[-1][1]
     vmem = pl.BlockSpec(memory_space=pltpu.VMEM)
+    out = []
+    for size in (cut, width - cut):
+        out.append(jax.ShapeDtypeStruct((rows // 2, size), jnp.bfloat16))
+        out.append(jax.ShapeDtypeStruct((rows // 2, size), jnp.float32))
     return pl.pallas_call(
-        functools.partial(product_kernel, start, step),
-        in_specs=[vmem, vmem, pl.BlockSpec(memory_space=pl.ANY)],
-        out_specs=[vmem, vmem],
-        out_shape=[
-            jax.ShapeDtypeStruct((rows // 2, width), jnp.bfloat16),
-            jax.ShapeDtypeStruct((rows // 2, width), jnp.float32),
-        ],
+        functools.partial(product_kernel, tuple(cuts)),
+        in_specs=[vmem, vmem, vmem, pl.BlockSpec(memory_space=pl.ANY)],
+        out_specs=[vmem] * 4,
+        out_shape=out,
         scratch_shapes=[
-            pltpu.VMEM((w_out.shape[0], width), jnp.bfloat16),
-            pltpu.SemaphoreType.DMA((width // step,)),
+            pltpu.VMEM(w_out.shape, jnp.bfloat16),
+            pltpu.SemaphoreType.DMA((len(cuts),)),
         ],
         compiler_params=pltpu.CompilerParams(vmem_limit_bytes=48 * 2**20),
         cost_estimate=pl.CostEstimate(
-            flops=2 * rows * w_out.shape[0] * width,
-            bytes_accessed=2 * w_out.shape[0] * width,
-            transcendentals=0,
+            flops=2 * rows * depth * width, bytes_accessed=2 * depth * width, transcendentals=0
         ),
         name="product",
-    )(place.reshape(1, rows), returned, w_out)
+    )(place_a.reshape(1, rows), place_b.reshape(1, rows), returned, w_out)
 
 
 def scatter_sum(grid, place_a, place_b, returned, w_out, cut):
-    def along_far(x):
+    def send_far(x):
         size = x.shape[0] // grid.far
-        parts = [
+        return x[:size], [
             grid.send(narrow(x[d * size : (d + 1) * size]), far=d) for d in range(1, grid.far)
         ]
-        x = x[:size]
+
+    def total(x, parts):
         for part in parts:
             x = x + wide(part)
         return x
 
-    away_a, keep_a = product(place_a, returned, w_out, 0, cut)
+    away_a, keep_a, away_b, keep_b = product(place_a, place_b, returned, w_out, cut)
     xa = keep_a + wide(grid.send(away_a, core=1))
     middle = xa.shape[0] // 2
     sent_a = narrow(xa[middle:])
-    xa = xa[:middle] + wide(grid.send(sent_a, near=1))
-    away_b, keep_b = product(
-        place_b, after(returned, sent_a), w_out, cut, w_out.shape[1] - cut
-    )
-    xb = keep_b + wide(grid.send(away_b, core=1))
-    xb = along_far(xb)
+    got_a = grid.send(sent_a, near=1)
+    xb = keep_b + wide(grid.send(after(away_b, sent_a), core=1))
+    xb, got_b = send_far(xb)
+    got_a, got_b = lax.optimization_barrier((got_a, got_b))
+    xa, parts_a = send_far(xa[:middle] + wide(got_a))
+    xb = total(xb, got_b)
     middle = xb.shape[0] // 2
     xb = xb[:middle] + wide(grid.send(narrow(xb[middle:]), near=1))
-    xa = along_far(xa)
+    xa = total(xa, parts_a)
     return jnp.concatenate([xa, xb], axis=1)
 
 
@@ -265,7 +274,7 @@
 def project(start, parts, order, w_query, w_kv_t, before, place, slots):
     row_width = w_query.shape[1] + w_kv_t.shape[0]
     width = parts[0].shape[1]
-    block = next(b for b in (2816, 2560, 1024, 512) if width % b == 0)
+    block = next(b for b in (2816, 2688, 1024, 512) if width % b == 0)
     rows = sum(part.shape[0] for part in parts)
     first, last = before is None, place is not None
     vmem = pl.BlockSpec(memory_space=pltpu.VMEM)
@@ -513,7 +522,7 @@
     all_slots = owners * slot_count
 
     crossed = grid.crossed()
-    cut = width // 16 * 11
+    cut = width // 32 * 21
     xa, xb = norm(hidden_in, norm_gain, (cut, width - cut))
 
     def placed(kv_owner):
@@ -544,7 +553,8 @@
     place = after(place, outbound)
     place_out = reordered(place, grid.blocks(1))
     crossed_out = reordered(place, grid.blocks(1, crossed))
-    mine = lax.axis_index(AXES) * slot_count + jnp.arange(slot_count, dtype=jnp.int32)
+    mine = jnp.asarray(np.arange(all_slots, dtype=np.int32).reshape(owners, slot_count))
+    mine = mine[lax.axis_index(AXES)]
     lengths = jnp.sum(jnp.where(place[:, None] == mine[None, :], cached[:, None], 0), axis=0)
     halfway = HEAD // 2
     offsets = jnp.arange(halfway, dtype=jnp.float32)
@@ -558,7 +568,7 @@
     attended = attend(
         inbound,
         lengths,
-        page_table[0],
+        after(page_table, outbound)[0],
         cosine,
         sine,
         key_pages[0],

time: 105 us -> 97.6 us (0.930)
  local copies, waits for them, and re-layouts: 11.9 us -> 4.01 us
  waiting for transfers between devices: 35.8 us -> 38.2 us
  Pallas kernels: 18.7 us -> 16.9 us
    unnamed x32 -> x12, local copies, waits for them, and re-layouts: 9.63 us -> 1.68 us
    pallas_call x2 -> x1, Pallas kernels: 6.03 us -> 4.08 us  [product(): pl.pallas_call(functools.partial(product_kernel, tuple(cuts)), in_specs=[...]
    ppermute x24, waiting for transfers between devices: 17.2 us -> 19 us  [send(): return lax.ppermute(x, AXES, self.perm(far, near, core))]
where the time goes in v8:
time: 97.6 us; the launch traced here: 97.1 us
  waiting for transfers between devices  38.2 us (39%)
  starting transfers between devices  33 us (34%)
  Pallas kernels  16.9 us (17%)
  other arithmetic  4.72 us (5%)
  local copies, waits for them, and re-layouts  4.01 us (4%)
    ppermute x24, starting transfers between devices, send(): return lax.ppermute(x, AXES, self.perm(far, near, core))  25.4 us
    ppermute x24, waiting for transfers between devices, send(): return lax.ppermute(x, AXES, self.perm(far, near, core))  19 us
    all_to_all x1, waiting for transfers between devices, on_device(): lax.all_to_all(outbound, AXES, split_axis=0, concat_axis=0, tiled=True)  10.3 us
    all_to_all x1, waiting for transfers between devices, on_device(): lax.all_to_all(attended, AXES, split_axis=0, concat_axis=0, tiled=True)  8.89 us
    pallas_call x1, Pallas kernels, attend(): pl.pallas_call(functools.partial(attend_kernel, per_query, per_key), in_s...  5.98 us
    pallas_call x1, Pallas kernels, product(): pl.pallas_call(functools.partial(product_kernel, tuple(cuts)), in_specs=[...  4.08 us
    all_to_all x1, starting transfers between devices, on_device(): lax.all_to_all(outbound, AXES, split_axis=0, concat_axis=0, tiled=True)  4.06 us
    all_to_all x1, starting transfers between devices, on_device(): lax.all_to_all(attended, AXES, split_axis=0, concat_axis=0, tiled=True)  3.54 us
  transfers between devices with their start and end apart: 26, of which 12 were waited for; matrix products, arithmetic and copies ran while one was open for 6% of the time, Pallas kernels for 5%

profile of v8, /device:TPU:0, one launch (start us, length us, event | category | flops | bytes accessed | tf_op | source)
XLA Modules:
  0.0 97.1 jit_solution(6224751290987571010)
XLA Ops:
  1.9 3.1 %collective-permute-start = (bf16[8,5376]{1,0:T(8,128)(2,1)S(1)}, bf16[8,5376]{1,0:T(8,128)(2,1)S(1)}, u32[]{:S(2)}, u32[]{:S(2)}) collective-permute-start(bf16[8,5376]{1,0:T(8,128)(2,1)S(1)} %get-tuple-element.31), channel_id=1, source_target_pairs={{0,4},{1,5},{2,6},{3,7},{4,8},{5,9},{6,10},{7,11},{8,12},{9,13},{1... | collective-permute-start | bytes 258056 | tf_op jit(solution)/shard_map/ppermute | solution.py:41
  4.9 2.6 %collective-permute-start.1 = (bf16[8,5376]{1,0:T(8,128)(2,1)S(1)}, bf16[8,5376]{1,0:T(8,128)(2,1)S(1)}, u32[]{:S(2)}, u32[]{:S(2)}) collective-permute-start(bf16[8,5376]{1,0:T(8,128)(2,1)S(1)} %get-tuple-element.31), channel_id=1, source_target_pairs={{0,8},{1,9},{2,10},{3,11},{4,12},{5,13},{6,14},{7,15},{8,0},{9,1},... | collective-permute-start | bytes 258056 | tf_op jit(solution)/shard_map/ppermute | solution.py:41
  11.2 1.7 %collective-permute-done.3 = bf16[8,2816]{1,0:T(8,128)(2,1)S(1)} collective-permute-done((bf16[8,2816]{1,0:T(8,128)(2,1)S(1)}, bf16[8,2816]{1,0:T(8,128)(2,1)S(1)}, u32[]{:S(2)}, u32[]{:S(2)}) %collective-permute-start.3) | collective-permute-done | bytes 45088 | tf_op jit(solution)/shard_map/ppermute | solution.py:41
  13.5 2.1 %collective-permute-start.5 = (bf16[16,2816]{1,0:T(8,128)(2,1)S(1)}, bf16[16,2816]{1,0:T(8,128)(2,1)S(1)}, u32[]{:S(2)}, u32[]{:S(2)}) collective-permute-start(bf16[16,2816]{1,0:T(8,128)(2,1)S(1)} %pad_maximum_fusion.2.refs_0_), channel_id=1, source_target_pairs={{0,4},{1,5},{2,6},{3,7},{4,8},{5,9},{6,10},{7,11},{8,12},{9,13},{1... | collective-permute-start | bytes 270344 | tf_op jit(solution)/shard_map/ppermute | solution.py:41
  15.7 1.8 %collective-permute-start.6 = (bf16[16,2816]{1,0:T(8,128)(2,1)S(1)}, bf16[16,2816]{1,0:T(8,128)(2,1)S(1)}, u32[]{:S(2)}, u32[]{:S(2)}) collective-permute-start(bf16[16,2816]{1,0:T(8,128)(2,1)S(1)} %pad_maximum_fusion.2.refs_0_), channel_id=1, source_target_pairs={{0,8},{1,9},{2,10},{3,11},{4,12},{5,13},{6,14},{7,15},{8,0},{9,1},... | collective-permute-start | bytes 270344 | tf_op jit(solution)/shard_map/ppermute | solution.py:41
  19.6 1.7 %pad_maximum_fusion.refs_5_.refs_9_ = bf16[128,8192]{1,0:T(8,128)(2,1)S(1)} fusion(bf16[64,8192]{1,0:T(8,128)(2,1)} %bitcast.24, bf16[64,8192]{1,0:T(8,128)(2,1)} %bitcast.25), kind=kLoop, calls=%fused_computation | loop fusion | flops 4194304 | bytes 4194304 | tf_op jit(solution)/shard_map/concatenate | solution.py:545
  22.2 3.4 %fetch.1.refs_4_.refs_8_ = bf16[8192,512]{1,0:T(8,128)(2,1)S(1)} custom-call(bf16[8192,512]{1,0:T(8,128)(2,1)} %refs_0_), custom_call_target="tpu_custom_call" | custom-call | bytes 16777216 | tf_op jit(solution)/shard_map/fetch/pallas_call | solution.py:218
  25.6 1.9 %collective-permute-done.4.refs_1_ = bf16[32,5376]{1,0:T(8,128)(2,1)S(1)} collective-permute-done((bf16[32,5376]{1,0:T(8,128)(2,1)S(1)}, bf16[32,5376]{1,0:T(8,128)(2,1)S(1)}, u32[]{:S(2)}, u32[]{:S(2)}) %collective-permute-start.4) | collective-permute-done | bytes 344096 | tf_op jit(solution)/shard_map/ppermute | solution.py:41
  29.3 1.6 %project.2.refs_10_ = f32[128,640]{1,0:T(8,128)S(1)} custom-call(bf16[32,5376]{1,0:T(8,128)(2,1)S(1)} %pad_maximum_fusion.1.refs_0_, bf16[32,5376]{1,0:T(8,128)(2,1)S(1)} %collective-permute-done.4.refs_1_, bf16[32,5376]{1,0:T(8,128)(2,1)S(1)} %collective-permute-done.12.refs_2_, bf16[32,5376]{1,0:T(8,128)(2,1)S(1)} %collective-permute-done.13.refs_3_, ...), custom_call_target="tpu_custom_call" | custom-call | flops 880803840 | bytes 6881280 | tf_op jit(solution)/shard_map/project/pallas_call | solution.py:296
  30.9 1.6 %project.3 = bf16[256,640]{1,0:T(8,128)(2,1)} custom-call(bf16[16,2816]{1,0:T(8,128)(2,1)S(1)} %pad_maximum_fusion.2.refs_0_, bf16[16,2816]{1,0:T(8,128)(2,1)S(1)} %collective-permute-done.5.refs_1_, bf16[16,2816]{1,0:T(8,128)(2,1)S(1)} %collective-permute-done.6.refs_2_, bf16[16,2816]{1,0:T(8,128)(2,1)S(1)} %collective-permute-done.7.refs_3_, ...), custom_call_target="tpu_custom_call" | custom-call | flops 461373440 | bytes 3604480 | tf_op jit(solution)/shard_map/project/pallas_call | solution.py:296
  32.6 4.1 %all-to-all-start = ((bf16[16,16,640]{2,1,0:T(8,128)(2,1)}), bf16[16,16,640]{2,1,0:T(8,128)(2,1)S(1)}, u32[]{:S(2)}, u32[]{:S(2)}) async-start(bf16[16,16,640]{2,1,0:T(8,128)(2,1)} %bitcast.6), calls=%async_computation | async-start | bytes 655360 | tf_op jit(solution)/shard_map/all_to_all | solution.py:567
  37.4 10.3 %all-to-all-done.inbound = bf16[16,16,640]{2,1,0:T(8,128)(2,1)S(1)} async-done(((bf16[16,16,640]{2,1,0:T(8,128)(2,1)}), bf16[16,16,640]{2,1,0:T(8,128)(2,1)S(1)}, u32[]{:S(2)}, u32[]{:S(2)}) %all-to-all-start) | async-done | bytes 327712 | tf_op jit(solution)/shard_map/all_to_all | solution.py:567
  47.8 6.0 %attend.1 = bf16[16,16,512]{2,1,0:T(8,128)(2,1)} custom-call(s32[16,4]{1,0:T(8,128)S(1)} %copy.21.table, s32[2,1,128]{2,1,0:T(1,128)S(1)} %bitcast.20, bf16[16,16,640]{2,1,0:T(8,128)(2,1)S(1)} %all-to-all-done.inbound, f32[16,128]{1,0:T(8,128)S(1)} %pad_maximum_fusion.3.cosine, f32[16,128]{1,0:T(8,128)S(1)} %pad_maximum_fusion.4.sine, ...), custom_call_target="tpu_custom_call" | custom-call | flops 134217728 | bytes 8388608 | tf_op jit(solution)/shard_map/attend/pallas_call | solution.py:475
  53.7 3.5 %all-to-all-start.1 = ((bf16[16,16,512]{2,1,0:T(8,128)(2,1)}), bf16[16,16,512]{2,1,0:T(8,128)(2,1)S(1)}, u32[]{:S(2)}, u32[]{:S(2)}) async-start(bf16[16,16,512]{2,1,0:T(8,128)(2,1)} %attend.1), calls=%async_computation.1 | async-start | bytes 524288 | tf_op jit(solution)/shard_map/all_to_all | solution.py:579
  58.4 8.9 %all-to-all-done.1 = bf16[16,16,512]{2,1,0:T(8,128)(2,1)S(1)} async-done(((bf16[16,16,512]{2,1,0:T(8,128)(2,1)}), bf16[16,16,512]{2,1,0:T(8,128)(2,1)S(1)}, u32[]{:S(2)}, u32[]{:S(2)}) %all-to-all-start.1) | async-done | bytes 262176 | tf_op jit(solution)/shard_map/all_to_all | solution.py:579
  67.3 4.1 %product.1 = (bf16[64,5376]{1,0:T(8,128)(2,1)S(1)}, f32[64,5376]{1,0:T(8,128)S(1)}, bf16[64,2816]{1,0:T(8,128)(2,1)S(1)}, f32[64,2816]{1,0:T(8,128)S(1)}) custom-call(s32[1,128]{1,0:T(1,128)S(1)} %reshape_reshape.6.place_a, s32[1,128]{1,0:T(1,128)S(1)} %reshape_reshape.7.place_b, bf16[256,512]{1,0:T(8,128)(2,1)S(1)} %bitcast.18, bf16[512,8192]{1,0:T(8,128)(2,1)} %w_out.1), custom_call_target="tpu_custom_call" | custom-call | flops 1073741824 | bytes 8388608 | tf_op jit(solution)/shard_map/product/pallas_call | solution.py:138
  71.5 2.1 %collective-permute-done.14 = bf16[64,5376]{1,0:T(8,128)(2,1)S(1)} collective-permute-done((bf16[64,5376]{1,0:T(8,128)(2,1)S(1)}, bf16[64,5376]{1,0:T(8,128)(2,1)S(1)}, u32[]{:S(2)}, u32[]{:S(2)}) %collective-permute-start.14) | collective-permute-done | bytes 688160 | tf_op jit(solution)/shard_map/ppermute | solution.py:41
  77.2 2.4 %collective-permute-start.19 = (bf16[16,2816]{1,0:T(8,128)(2,1)S(1)}, bf16[16,2816]{1,0:T(8,128)(2,1)S(1)}, u32[]{:S(2)}, u32[]{:S(2)}) collective-permute-start(bf16[16,2816]{1,0:T(8,128)(2,1)S(1)} %get-tuple-element.63), channel_id=1, source_target_pairs={{0,12},{1,13},{2,14},{3,15},{4,0},{5,1},{6,2},{7,3},{8,4},{9,5},{1... | collective-permute-start | bytes 270344 | tf_op jit(solution)/shard_map/ppermute | solution.py:41
  79.6 4.7 %collective-permute-done.15 = bf16[32,5376]{1,0:T(8,128)(2,1)S(1)} collective-permute-done((bf16[32,5376]{1,0:T(8,128)(2,1)S(1)}, bf16[32,5376]{1,0:T(8,128)(2,1)S(1)}, u32[]{:S(2)}, u32[]{:S(2)}) %collective-permute-start.15) | collective-permute-done | bytes 344096 | tf_op jit(solution)/shard_map/ppermute | solution.py:41
  84.3 1.8 %collective-permute-done.18 = bf16[16,2816]{1,0:T(8,128)(2,1)S(1)} collective-permute-done((bf16[16,2816]{1,0:T(8,128)(2,1)S(1)}, bf16[16,2816]{1,0:T(8,128)(2,1)S(1)}, u32[]{:S(2)}, u32[]{:S(2)}) %collective-permute-start.18) | collective-permute-done | bytes 90144 | tf_op jit(solution)/shard_map/ppermute | solution.py:41
  86.8 2.1 %collective-permute-start.20 = (bf16[8,5376]{1,0:T(8,128)(2,1)S(1)}, bf16[8,5376]{1,0:T(8,128)(2,1)S(1)}, u32[]{:S(2)}, u32[]{:S(2)}) collective-permute-start(bf16[8,5376]{1,0:T(8,128)(2,1)S(1)} %get-tuple-element.66), channel_id=1, source_target_pairs={{0,4},{1,5},{2,6},{3,7},{4,8},{5,9},{6,10},{7,11},{8,12},{9,13},{1... | collective-permute-start | bytes 258056 | tf_op jit(solution)/shard_map/ppermute | solution.py:41
  89.7 1.6 %collective-permute-start.22 = (bf16[8,5376]{1,0:T(8,128)(2,1)S(1)}, bf16[8,5376]{1,0:T(8,128)(2,1)S(1)}, u32[]{:S(2)}, u32[]{:S(2)}) collective-permute-start(bf16[8,5376]{1,0:T(8,128)(2,1)S(1)} %get-tuple-element.67), channel_id=1, source_target_pairs={{0,12},{1,13},{2,14},{3,15},{4,0},{5,1},{6,2},{7,3},{8,4},{9,5},{1... | collective-permute-start | bytes 258056 | tf_op jit(solution)/shard_map/ppermute | solution.py:41
  91.4 2.4 %collective-permute-done.20 = bf16[8,5376]{1,0:T(8,128)(2,1)S(1)} collective-permute-done((bf16[8,5376]{1,0:T(8,128)(2,1)S(1)}, bf16[8,5376]{1,0:T(8,128)(2,1)S(1)}, u32[]{:S(2)}, u32[]{:S(2)}) %collective-permute-start.20) | collective-permute-done | bytes 86048 | tf_op jit(solution)/shard_map/ppermute | solution.py:41
  93.7 2.6 %collective-permute-done.21 = bf16[8,5376]{1,0:T(8,128)(2,1)S(1)} collective-permute-done((bf16[8,5376]{1,0:T(8,128)(2,1)S(1)}, bf16[8,5376]{1,0:T(8,128)(2,1)S(1)}, u32[]{:S(2)}, u32[]{:S(2)}) %collective-permute-start.21) | collective-permute-done | bytes 86048 | tf_op jit(solution)/shard_map/ppermute | solution.py:41
  (86 shorter events, 18.5 us)
Async XLA Ops:
  1.9 11.1 %collective-permute-start = (bf16[8,5376]{1,0:T(8,128)(2,1)S(1)}, bf16[8,5376]{1,0:T(8,128)(2,1)S(1)}, u32[]{:S(2)}, u32[]{:S(2)}) collective-permute-start(bf16[8,5376]{1,0:T(8,128)(2,1)S(1)} %get-tuple-element.31), channel_id=1, source_target_pairs={{0,4},{1,5},{2,6},{3,7},{4,8},{5,9},{6,10},{7,11},{8,12},{9,13},{1... | collective-permute-start | bytes 258056 | tf_op jit(solution)/shard_map/ppermute | solution.py:41
  4.9 8.4 %collective-permute-start.1 = (bf16[8,5376]{1,0:T(8,128)(2,1)S(1)}, bf16[8,5376]{1,0:T(8,128)(2,1)S(1)}, u32[]{:S(2)}, u32[]{:S(2)}) collective-permute-start(bf16[8,5376]{1,0:T(8,128)(2,1)S(1)} %get-tuple-element.31), channel_id=1, source_target_pairs={{0,8},{1,9},{2,10},{3,11},{4,12},{5,13},{6,14},{7,15},{8,0},{9,1},... | collective-permute-start | bytes 258056 | tf_op jit(solution)/shard_map/ppermute | solution.py:41
  7.5 6.0 %collective-permute-start.2 = (bf16[8,5376]{1,0:T(8,128)(2,1)S(1)}, bf16[8,5376]{1,0:T(8,128)(2,1)S(1)}, u32[]{:S(2)}, u32[]{:S(2)}) collective-permute-start(bf16[8,5376]{1,0:T(8,128)(2,1)S(1)} %get-tuple-element.31), channel_id=1, source_target_pairs={{0,12},{1,13},{2,14},{3,15},{4,0},{5,1},{6,2},{7,3},{8,4},{9,5},{1... | collective-permute-start | bytes 258056 | tf_op jit(solution)/shard_map/ppermute | solution.py:41
  8.9 4.0 %collective-permute-start.3 = (bf16[8,2816]{1,0:T(8,128)(2,1)S(1)}, bf16[8,2816]{1,0:T(8,128)(2,1)S(1)}, u32[]{:S(2)}, u32[]{:S(2)}) collective-permute-start(bf16[8,2816]{1,0:T(8,128)(2,1)S(1)} %get-tuple-element.32), channel_id=1, source_target_pairs={{0,2},{1,3},{2,0},{3,1},{4,6},{5,7},{6,4},{7,5},{8,10},{9,11},{10,... | collective-permute-start | bytes 135176 | tf_op jit(solution)/shard_map/ppermute | solution.py:41
  13.5 12.1 %collective-permute-start.5 = (bf16[16,2816]{1,0:T(8,128)(2,1)S(1)}, bf16[16,2816]{1,0:T(8,128)(2,1)S(1)}, u32[]{:S(2)}, u32[]{:S(2)}) collective-permute-start(bf16[16,2816]{1,0:T(8,128)(2,1)S(1)} %pad_maximum_fusion.2.refs_0_), channel_id=1, source_target_pairs={{0,4},{1,5},{2,6},{3,7},{4,8},{5,9},{6,10},{7,11},{8,12},{9,13},{1... | collective-permute-start | bytes 270344 | tf_op jit(solution)/shard_map/ppermute | solution.py:41
  15.7 9.9 %collective-permute-start.6 = (bf16[16,2816]{1,0:T(8,128)(2,1)S(1)}, bf16[16,2816]{1,0:T(8,128)(2,1)S(1)}, u32[]{:S(2)}, u32[]{:S(2)}) collective-permute-start(bf16[16,2816]{1,0:T(8,128)(2,1)S(1)} %pad_maximum_fusion.2.refs_0_), channel_id=1, source_target_pairs={{0,8},{1,9},{2,10},{3,11},{4,12},{5,13},{6,14},{7,15},{8,0},{9,1},... | collective-permute-start | bytes 270344 | tf_op jit(solution)/shard_map/ppermute | solution.py:41
  17.5 8.1 %collective-permute-start.7 = (bf16[16,2816]{1,0:T(8,128)(2,1)S(1)}, bf16[16,2816]{1,0:T(8,128)(2,1)S(1)}, u32[]{:S(2)}, u32[]{:S(2)}) collective-permute-start(bf16[16,2816]{1,0:T(8,128)(2,1)S(1)} %pad_maximum_fusion.2.refs_0_), channel_id=1, source_target_pairs={{0,12},{1,13},{2,14},{3,15},{4,0},{5,1},{6,2},{7,3},{8,4},{9,5},{1... | collective-permute-start | bytes 270344 | tf_op jit(solution)/shard_map/ppermute | solution.py:41
  18.1 9.4 %collective-permute-start.4 = (bf16[32,5376]{1,0:T(8,128)(2,1)S(1)}, bf16[32,5376]{1,0:T(8,128)(2,1)S(1)}, u32[]{:S(2)}, u32[]{:S(2)}) collective-permute-start(bf16[32,5376]{1,0:T(8,128)(2,1)S(1)} %pad_maximum_fusion.1.refs_0_), channel_id=1, source_target_pairs={{0,2},{1,3},{2,0},{3,1},{4,6},{5,7},{6,4},{7,5},{8,10},{9,11},{10,... | collective-permute-start | bytes 1032200 | tf_op jit(solution)/shard_map/ppermute | solution.py:41
  19.6 8.9 %collective-permute-start.12 = (bf16[32,5376]{1,0:T(8,128)(2,1)S(1)}, bf16[32,5376]{1,0:T(8,128)(2,1)S(1)}, u32[]{:S(2)}, u32[]{:S(2)}) collective-permute-start(bf16[32,5376]{1,0:T(8,128)(2,1)S(1)} %pad_maximum_fusion.1.refs_0_), channel_id=1, source_target_pairs={{0,1},{1,0},{2,3},{3,2},{4,5},{5,4},{6,7},{7,6},{8,9},{9,8},{10,11... | collective-permute-start | bytes 1032200 | tf_op jit(solution)/shard_map/ppermute | solution.py:41
  27.5 3.3 %collective-permute-start.8 = (bf16[16,2816]{1,0:T(8,128)(2,1)S(1)}, bf16[16,2816]{1,0:T(8,128)(2,1)S(1)}, u32[]{:S(2)}, u32[]{:S(2)}) collective-permute-start(bf16[16,2816]{1,0:T(8,128)(2,1)S(1)} %pad_maximum_fusion.2.refs_0_), channel_id=1, source_target_pairs={{0,1},{1,0},{2,3},{3,2},{4,5},{5,4},{6,7},{7,6},{8,9},{9,8},{10,11... | collective-permute-start | bytes 270344 | tf_op jit(solution)/shard_map/ppermute | solution.py:41
  28.0 2.9 %collective-permute-start.10 = (bf16[16,2816]{1,0:T(8,128)(2,1)S(1)}, bf16[16,2816]{1,0:T(8,128)(2,1)S(1)}, u32[]{:S(2)}, u32[]{:S(2)}) collective-permute-start(bf16[16,2816]{1,0:T(8,128)(2,1)S(1)} %collective-permute-done.6.refs_2_), channel_id=1, source_target_pairs={{0,1},{1,0},{2,3},{3,2},{4,5},{5,4},{6,7},{7,6},{8,9},{9,8},{10,11... | collective-permute-start | bytes 270344 | tf_op jit(solution)/shard_map/ppermute | solution.py:41
  28.0 2.9 %collective-permute-start.11 = (bf16[16,2816]{1,0:T(8,128)(2,1)S(1)}, bf16[16,2816]{1,0:T(8,128)(2,1)S(1)}, u32[]{:S(2)}, u32[]{:S(2)}) collective-permute-start(bf16[16,2816]{1,0:T(8,128)(2,1)S(1)} %collective-permute-done.7.refs_3_), channel_id=1, source_target_pairs={{0,1},{1,0},{2,3},{3,2},{4,5},{5,4},{6,7},{7,6},{8,9},{9,8},{10,11... | collective-permute-start | bytes 270344 | tf_op jit(solution)/shard_map/ppermute | solution.py:41
  28.6 2.4 %collective-permute-start.9 = (bf16[16,2816]{1,0:T(8,128)(2,1)S(1)}, bf16[16,2816]{1,0:T(8,128)(2,1)S(1)}, u32[]{:S(2)}, u32[]{:S(2)}) collective-permute-start(bf16[16,2816]{1,0:T(8,128)(2,1)S(1)} %collective-permute-done.5.refs_1_), channel_id=1, source_target_pairs={{0,1},{1,0},{2,3},{3,2},{4,5},{5,4},{6,7},{7,6},{8,9},{9,8},{10,11... | collective-permute-start | bytes 270344 | tf_op jit(solution)/shard_map/ppermute | solution.py:41
  32.6 15.2 %all-to-all-start = ((bf16[16,16,640]{2,1,0:T(8,128)(2,1)}), bf16[16,16,640]{2,1,0:T(8,128)(2,1)S(1)}, u32[]{:S(2)}, u32[]{:S(2)}) async-start(bf16[16,16,640]{2,1,0:T(8,128)(2,1)} %bitcast.6), calls=%async_computation | async-start | bytes 655360 | tf_op jit(solution)/shard_map/all_to_all | solution.py:567
  53.7 13.6 %all-to-all-start.1 = ((bf16[16,16,512]{2,1,0:T(8,128)(2,1)}), bf16[16,16,512]{2,1,0:T(8,128)(2,1)S(1)}, u32[]{:S(2)}, u32[]{:S(2)}) async-start(bf16[16,16,512]{2,1,0:T(8,128)(2,1)} %attend.1), calls=%async_computation.1 | async-start | bytes 524288 | tf_op jit(solution)/shard_map/all_to_all | solution.py:579
  71.4 2.2 %collective-permute-start.14 = (bf16[64,5376]{1,0:T(8,128)(2,1)S(1)}, bf16[64,5376]{1,0:T(8,128)(2,1)S(1)}, u32[]{:S(2)}, u32[]{:S(2)}) collective-permute-start(bf16[64,5376]{1,0:T(8,128)(2,1)S(1)} %get-tuple-element.49), channel_id=1, source_target_pairs={{0,1},{1,0},{2,3},{3,2},{4,5},{5,4},{6,7},{7,6},{8,9},{9,8},{10,11... | collective-permute-start | bytes 2064392 | tf_op jit(solution)/shard_map/ppermute | solution.py:41
  74.0 10.3 %collective-permute-start.15 = (bf16[32,5376]{1,0:T(8,128)(2,1)S(1)}, bf16[32,5376]{1,0:T(8,128)(2,1)S(1)}, u32[]{:S(2)}, u32[]{:S(2)}) collective-permute-start(bf16[32,5376]{1,0:T(8,128)(2,1)S(1)} %slice.82), channel_id=1, source_target_pairs={{0,2},{1,3},{2,0},{3,1},{4,6},{5,7},{6,4},{7,5},{8,10},{9,11},{10,... | collective-permute-start | bytes 1032200 | tf_op jit(solution)/shard_map/ppermute | solution.py:41
  75.6 8.7 %collective-permute-start.17 = (bf16[16,2816]{1,0:T(8,128)(2,1)S(1)}, bf16[16,2816]{1,0:T(8,128)(2,1)S(1)}, u32[]{:S(2)}, u32[]{:S(2)}) collective-permute-start(bf16[16,2816]{1,0:T(8,128)(2,1)S(1)} %get-tuple-element.65), channel_id=1, source_target_pairs={{0,4},{1,5},{2,6},{3,7},{4,8},{5,9},{6,10},{7,11},{8,12},{9,13},{1... | collective-permute-start | bytes 270344 | tf_op jit(solution)/shard_map/ppermute | solution.py:41
  76.0 10.1 %collective-permute-start.18 = (bf16[16,2816]{1,0:T(8,128)(2,1)S(1)}, bf16[16,2816]{1,0:T(8,128)(2,1)S(1)}, u32[]{:S(2)}, u32[]{:S(2)}) collective-permute-start(bf16[16,2816]{1,0:T(8,128)(2,1)S(1)} %get-tuple-element.64), channel_id=1, source_target_pairs={{0,8},{1,9},{2,10},{3,11},{4,12},{5,13},{6,14},{7,15},{8,0},{9,1},... | collective-permute-start | bytes 270344 | tf_op jit(solution)/shard_map/ppermute | solution.py:41
  77.2 8.9 %collective-permute-start.19 = (bf16[16,2816]{1,0:T(8,128)(2,1)S(1)}, bf16[16,2816]{1,0:T(8,128)(2,1)S(1)}, u32[]{:S(2)}, u32[]{:S(2)}) collective-permute-start(bf16[16,2816]{1,0:T(8,128)(2,1)S(1)} %get-tuple-element.63), channel_id=1, source_target_pairs={{0,12},{1,13},{2,14},{3,15},{4,0},{5,1},{6,2},{7,3},{8,4},{9,5},{1... | collective-permute-start | bytes 270344 | tf_op jit(solution)/shard_map/ppermute | solution.py:41
  86.2 5.1 %collective-permute-start.23 = (bf16[8,2816]{1,0:T(8,128)(2,1)S(1)}, bf16[8,2816]{1,0:T(8,128)(2,1)S(1)}, u32[]{:S(2)}, u32[]{:S(2)}) collective-permute-start(bf16[8,2816]{1,0:T(8,128)(2,1)S(1)} %slice.83), channel_id=1, source_target_pairs={{0,2},{1,3},{2,0},{3,1},{4,6},{5,7},{6,4},{7,5},{8,10},{9,11},{10,... | collective-permute-start | bytes 135176 | tf_op jit(solution)/shard_map/ppermute | solution.py:41
  86.8 6.9 %collective-permute-start.20 = (bf16[8,5376]{1,0:T(8,128)(2,1)S(1)}, bf16[8,5376]{1,0:T(8,128)(2,1)S(1)}, u32[]{:S(2)}, u32[]{:S(2)}) collective-permute-start(bf16[8,5376]{1,0:T(8,128)(2,1)S(1)} %get-tuple-element.66), channel_id=1, source_target_pairs={{0,4},{1,5},{2,6},{3,7},{4,8},{5,9},{6,10},{7,11},{8,12},{9,13},{1... | collective-permute-start | bytes 258056 | tf_op jit(solution)/shard_map/ppermute | solution.py:41
  88.9 7.5 %collective-permute-start.21 = (bf16[8,5376]{1,0:T(8,128)(2,1)S(1)}, bf16[8,5376]{1,0:T(8,128)(2,1)S(1)}, u32[]{:S(2)}, u32[]{:S(2)}) collective-permute-start(bf16[8,5376]{1,0:T(8,128)(2,1)S(1)} %get-tuple-element.68), channel_id=1, source_target_pairs={{0,8},{1,9},{2,10},{3,11},{4,12},{5,13},{6,14},{7,15},{8,0},{9,1},... | collective-permute-start | bytes 258056 | tf_op jit(solution)/shard_map/ppermute | solution.py:41
  89.7 6.6 %collective-permute-start.22 = (bf16[8,5376]{1,0:T(8,128)(2,1)S(1)}, bf16[8,5376]{1,0:T(8,128)(2,1)S(1)}, u32[]{:S(2)}, u32[]{:S(2)}) collective-permute-start(bf16[8,5376]{1,0:T(8,128)(2,1)S(1)} %get-tuple-element.67), channel_id=1, source_target_pairs={{0,12},{1,13},{2,14},{3,15},{4,0},{5,1},{6,2},{7,3},{8,4},{9,5},{1... | collective-permute-start | bytes 258056 | tf_op jit(solution)/shard_map/ppermute | solution.py:41
  (8 other events, 39.5 us)

commit v9 on v8

--- a/solution.py
+++ b/solution.py
@@ -17,70 +17,69 @@
 
 class Grid:
     def __init__(self):
-        tp = lax.axis_size("tp")
-        self.core = lax.axis_size("attn")
-        self.near = 2 if tp % 2 == 0 else 1
-        self.far = tp // self.near
-        self.size = tp * self.core
-
-    def index(self, far, near, core):
-        return (far * self.near + near) * self.core + core
-
-    def perm(self, far=0, near=0, core=0):
-        pairs = []
-        for f in range(self.far):
-            for n in range(self.near):
-                for c in range(self.core):
-                    to = self.index(
-                        (f + far) % self.far, (n + near) % self.near, (c + core) % self.core
-                    )
-                    pairs.append((self.index(f, n, c), to))
-        return pairs
-
-    def send(self, x, far=0, near=0, core=0):
-        return lax.ppermute(x, AXES, self.perm(far, near, core))
-
-    def blocks(self, sign, order=None):
-        rows = []
-        for f in range(self.far):
-            for n in range(self.near):
-                for c in range(self.core):
-                    row = [
-                        self.index(
-                            (f + sign * df) % self.far,
-                            (n + sign * dn) % self.near,
-                            (c + sign * dc) % self.core,
-                        )
-                        for dc in range(self.core)
-                        for dn in range(self.near)
-                        for df in range(self.far)
-                    ]
-                    rows.append([row[i] for i in order] if order else row)
+        self.half = lax.axis_size("tp") // 4
+        self.sizes = (self.half, 2, 2, lax.axis_size("attn"))
+        self.size = int(np.prod(self.sizes))
+
+    def shifted(self, place, moves):
+        return np.ravel_multi_index(
+            tuple((p + m) % n for p, m, n in zip(place, moves, self.sizes)), self.sizes
+        )
+
+    def send(self, x, half=0, pair=0, near=0, core=0):
+        pairs = [
+            (i, int(self.shifted(np.unravel_index(i, self.sizes), (half, pair, near, core))))
+            for i in range(self.size)
+        ]
+        return lax.ppermute(x, AXES, pairs)
+
+    def moves(self, order):
+        counts = [self.sizes[axis] for axis in order]
+        places = []
+        for steps in np.ndindex(*counts):
+            move = [0, 0, 0, 0]
+            for axis, step in zip(order, steps):
+                move[axis] = step
+            places.append(tuple(move))
+        return places
+
+    def blocks(self, sign, order):
+        rows = [
+            [
+                int(self.shifted(np.unravel_index(i, self.sizes), [sign * m for m in move]))
+                for move in self.moves(order)
+            ]
+            for i in range(self.size)
+        ]
         return jnp.asarray(np.array(rows, np.int32))[lax.axis_index(AXES)]
 
-    def crossed(self):
-        return [
-            (dc * self.near + dn) * self.far + df
-            for dc in range(self.core)
-            for df in range(self.far)
-            for dn in range(self.near)
-        ]
+
+HALF, PAIR, NEAR, CORE = range(4)
+ORDER_A = (CORE, NEAR, PAIR, HALF)
+ORDER_B = (CORE, PAIR, HALF, NEAR)
 
 
 def after(x, *earlier):
     return lax.optimization_barrier((x, *earlier))[0]
 
 
+def gather_line(grid, x):
+    crossed = [grid.send(x, half=d) for d in range(1, grid.half)]
+    crossed = crossed[0] if len(crossed) == 1 else jnp.concatenate(crossed, axis=0)
+    return [x, crossed, grid.send(x, pair=1), grid.send(crossed, pair=1)]
+
+
 def gather_rows(grid, xa, xb, meanwhile):
     beside_b = grid.send(xb, near=1)
-    line_a = jnp.concatenate([xa] + [grid.send(xa, far=d) for d in range(1, grid.far)], axis=0)
+    line_a = jnp.concatenate(gather_line(grid, xa), axis=0)
     pair_b = jnp.concatenate([xb, beside_b], axis=0)
     line_a, pair_b = lax.optimization_barrier((line_a, pair_b))
     beside_a = grid.send(line_a, near=1)
-    line_b = [grid.send(pair_b, far=d) for d in range(1, grid.far)]
-    beside_a, line_b, meanwhile = lax.optimization_barrier((beside_a, line_b, meanwhile(pair_b)))
+    parts_b = gather_line(grid, pair_b)
+    beside_a, parts_b, meanwhile = lax.optimization_barrier(
+        (beside_a, parts_b, meanwhile(pair_b))
+    )
     parts_a = [line_a, beside_a]
-    parts_b = [pair_b, *line_b]
     parts_a += [grid.send(part, core=1) for part in parts_a]
     parts_b += [grid.send(part, core=1) for part in parts_b]
     return parts_a, parts_b, meanwhile
@@ -153,11 +152,17 @@
 
 
 def scatter_sum(grid, place_a, place_b, returned, w_out, cut):
-    def send_far(x):
-        size = x.shape[0] // grid.far
-        return x[:size], [
-            grid.send(narrow(x[d * size : (d + 1) * size]), far=d) for d in range(1, grid.far)
+    def along_line(x):
+        size = x.shape[0] // 2 // grid.half
+        middle = x.shape[0] // 2
+        first = grid.send(narrow(x[middle + size :]), pair=1)
+        second = grid.send(narrow(x[middle : middle + size]), pair=1)
+        far = x[size:middle] + wide(first)
+        third = [
+            grid.send(narrow(far[d * size : (d + 1) * size]), half=d + 1)
+            for d in range(grid.half - 1)
         ]
+        return x[:size], [second] + third
 
     def total(x, parts):
         for part in parts:
@@ -170,9 +175,9 @@
     sent_a = narrow(xa[middle:])
     got_a = grid.send(sent_a, near=1)
     xb = keep_b + wide(grid.send(after(away_b, sent_a), core=1))
-    xb, got_b = send_far(xb)
+    xb, got_b = along_line(xb)
     got_a, got_b = lax.optimization_barrier((got_a, got_b))
-    xa, parts_a = send_far(xa[:middle] + wide(got_a))
+    xa, parts_a = along_line(xa[:middle] + wide(got_a))
     xb = total(xb, got_b)
     middle = xb.shape[0] // 2
     xb = xb[:middle] + wide(grid.send(narrow(xb[middle:]), near=1))
@@ -274,7 +279,7 @@
 def project(start, parts, order, w_query, w_kv_t, before, place, slots):
     row_width = w_query.shape[1] + w_kv_t.shape[0]
     width = parts[0].shape[1]
-    block = next(b for b in (2816, 2688, 1024, 512) if width % b == 0)
+    block = width
     rows = sum(part.shape[0] for part in parts)
     first, last = before is None, place is not None
     vmem = pl.BlockSpec(memory_space=pltpu.VMEM)
@@ -521,8 +526,9 @@
     width = hidden_in.shape[1]
     all_slots = owners * slot_count
 
-    crossed = grid.crossed()
-    cut = width // 32 * 21
+    moves_a = grid.moves(ORDER_A)
+    order_b = [moves_a.index(move) for move in grid.moves(ORDER_B)]
+    cut = width // 8 * 5
     xa, xb = norm(hidden_in, norm_gain, (cut, width - cut))
 
     def placed(kv_owner):
@@ -542,17 +548,17 @@
         if spare:
             pieces.append(jnp.zeros((spare, width), w_key.dtype))
         place = placed(after(kv_owner, x))
-        return w, jnp.concatenate(pieces, axis=0), place, reordered(place, grid.blocks(-1))
+        return w, jnp.concatenate(pieces, axis=0), place, reordered(place, grid.blocks(-1, ORDER_A))
 
     parts_a, parts_b, others = gather_rows(grid, xa, xb, beside_gather)
     w_query, w_kv_t, place, place_in = others
     plain = list(range(owners))
     total = project(0, parts_a, plain, w_query, w_kv_t, None, None, all_slots)
-    total = project(cut, parts_b, crossed, w_query, w_kv_t, total, place_in, all_slots)
+    total = project(cut, parts_b, order_b, w_query, w_kv_t, total, place_in, all_slots)
     outbound = total.reshape(owners, slot_count, row_width)
     place = after(place, outbound)
-    place_out = reordered(place, grid.blocks(1))
-    crossed_out = reordered(place, grid.blocks(1, crossed))
+    place_a = reordered(place, grid.blocks(1, ORDER_A))
+    place_b = reordered(place, grid.blocks(1, ORDER_B))
     mine = jnp.asarray(np.arange(all_slots, dtype=np.int32).reshape(owners, slot_count))
     mine = mine[lax.axis_index(AXES)]
     lengths = jnp.sum(jnp.where(place[:, None] == mine[None, :], cached[:, None], 0), axis=0)
@@ -578,7 +584,7 @@
     )
     returned = lax.all_to_all(attended, AXES, split_axis=0, concat_axis=0, tiled=True)
     returned = returned.reshape(all_slots, per_query)
-    summed = scatter_sum(grid, place_out, crossed_out, returned, w_out, cut)
+    summed = scatter_sum(grid, place_a, place_b, returned, w_out, cut)
     return narrow(wide(hidden_in) + summed)
 
 

time: 97.6 us -> 99 us (1.014)
  waiting for transfers between devices: 38.2 us -> 43.5 us
  starting transfers between devices: 33 us -> 29 us
    ppermute x24, waiting for transfers between devices: 19 us -> 24.9 us  [send(): return lax.ppermute(x, AXES, pairs)]
    ppermute x24, starting transfers between devices: 25.4 us -> 22 us  [send(): return lax.ppermute(x, AXES, pairs)]
  transfers between devices with their start and end apart: 26 -> 26, of which waited for: 12 -> 14; matrix products, arithmetic and copies ran while one was open for 6% -> 7% of each run, Pallas kernels for 5% -> 5%
where the time goes in v9:
time: 99 us; the launch traced here: 98.4 us
  waiting for transfers between devices  43.5 us (44%)
  starting transfers between devices  29 us (29%)
  Pallas kernels  16.3 us (16%)
  other arithmetic  5.33 us (5%)
  local copies, waits for them, and re-layouts  3.99 us (4%)
    ppermute x24, waiting for transfers between devices, send(): return lax.ppermute(x, AXES, pairs)  24.9 us
    ppermute x24, starting transfers between devices, send(): return lax.ppermute(x, AXES, pairs)  22 us
    all_to_all x1, waiting for transfers between devices, on_device(): lax.all_to_all(outbound, AXES, split_axis=0, concat_axis=0, tiled=True)  10.3 us
    all_to_all x1, waiting for transfers between devices, on_device(): lax.all_to_all(attended, AXES, split_axis=0, concat_axis=0, tiled=True)  8.26 us
    pallas_call x1, Pallas kernels, attend(): pl.pallas_call(functools.partial(attend_kernel, per_query, per_key), in_s...  5.99 us
    pallas_call x1, Pallas kernels, product(): pl.pallas_call(functools.partial(product_kernel, tuple(cuts)), in_specs=[...  3.86 us
    all_to_all x1, starting transfers between devices, on_device(): lax.all_to_all(attended, AXES, split_axis=0, concat_axis=0, tiled=True)  3.54 us
    all_to_all x1, starting transfers between devices, on_device(): lax.all_to_all(outbound, AXES, split_axis=0, concat_axis=0, tiled=True)  3.54 us
  transfers between devices with their start and end apart: 26, of which 14 were waited for; matrix products, arithmetic and copies ran while one was open for 7% of the time, Pallas kernels for 5%

profile of v9, /device:TPU:0, one launch (start us, length us, event | category | flops | bytes accessed | tf_op | source)
XLA Modules:
  0.0 98.4 jit_solution(9680487818383626967)
XLA Ops:
  1.9 4.1 %collective-permute-start = (bf16[8,5120]{1,0:T(8,128)(2,1)S(1)}, bf16[8,5120]{1,0:T(8,128)(2,1)S(1)}, u32[]{:S(2)}, u32[]{:S(2)}) collective-permute-start(bf16[8,5120]{1,0:T(8,128)(2,1)S(1)} %get-tuple-element.31), channel_id=1, source_target_pairs={{0,8},{1,9},{2,10},{3,11},{4,12},{5,13},{6,14},{7,15},{8,0},{9,1},... | collective-permute-start | bytes 245768 | tf_op jit(solution)/shard_map/ppermute | solution.py:34
  6.0 1.6 %collective-permute-start.1 = (bf16[8,5120]{1,0:T(8,128)(2,1)S(1)}, bf16[8,5120]{1,0:T(8,128)(2,1)S(1)}, u32[]{:S(2)}, u32[]{:S(2)}) collective-permute-start(bf16[8,5120]{1,0:T(8,128)(2,1)S(1)} %get-tuple-element.31), channel_id=1, source_target_pairs={{0,4},{1,5},{2,6},{3,7},{4,0},{5,1},{6,2},{7,3},{8,12},{9,13},{10,... | collective-permute-start | bytes 245768 | tf_op jit(solution)/shard_map/ppermute | solution.py:34
  7.5 1.5 %collective-permute-start.3 = (bf16[8,3072]{1,0:T(8,128)(2,1)S(1)}, bf16[8,3072]{1,0:T(8,128)(2,1)S(1)}, u32[]{:S(2)}, u32[]{:S(2)}) collective-permute-start(bf16[8,3072]{1,0:T(8,128)(2,1)S(1)} %get-tuple-element.32), channel_id=1, source_target_pairs={{0,2},{1,3},{2,0},{3,1},{4,6},{5,7},{6,4},{7,5},{8,10},{9,11},{10,... | collective-permute-start | bytes 147464 | tf_op jit(solution)/shard_map/ppermute | solution.py:34
  11.6 2.7 %collective-permute-done.2 = bf16[8,5120]{1,0:T(8,128)(2,1)S(1)} collective-permute-done((bf16[8,5120]{1,0:T(8,128)(2,1)S(1)}, bf16[8,5120]{1,0:T(8,128)(2,1)S(1)}, u32[]{:S(2)}, u32[]{:S(2)}) %collective-permute-start.2) | collective-permute-done | bytes 81952 | tf_op jit(solution)/shard_map/ppermute | solution.py:34
  14.3 2.5 %collective-permute-start.5 = (bf16[16,3072]{1,0:T(8,128)(2,1)S(1)}, bf16[16,3072]{1,0:T(8,128)(2,1)S(1)}, u32[]{:S(2)}, u32[]{:S(2)}) collective-permute-start(bf16[16,3072]{1,0:T(8,128)(2,1)S(1)} %pad_maximum_fusion.2.refs_0_), channel_id=1, source_target_pairs={{0,8},{1,9},{2,10},{3,11},{4,12},{5,13},{6,14},{7,15},{8,0},{9,1},... | collective-permute-start | bytes 294920 | tf_op jit(solution)/shard_map/ppermute | solution.py:34
  16.8 2.0 %collective-permute-start.6 = (bf16[16,3072]{1,0:T(8,128)(2,1)S(1)}, bf16[16,3072]{1,0:T(8,128)(2,1)S(1)}, u32[]{:S(2)}, u32[]{:S(2)}) collective-permute-start(bf16[16,3072]{1,0:T(8,128)(2,1)S(1)} %pad_maximum_fusion.2.refs_0_), channel_id=1, source_target_pairs={{0,4},{1,5},{2,6},{3,7},{4,0},{5,1},{6,2},{7,3},{8,12},{9,13},{10,... | collective-permute-start | bytes 294920 | tf_op jit(solution)/shard_map/ppermute | solution.py:34
  18.8 1.5 %collective-permute-start.4 = (bf16[32,5120]{1,0:T(8,128)(2,1)S(1)}, bf16[32,5120]{1,0:T(8,128)(2,1)S(1)}, u32[]{:S(2)}, u32[]{:S(2)}) collective-permute-start(bf16[32,5120]{1,0:T(8,128)(2,1)S(1)} %pad_maximum_fusion.1.refs_0_), channel_id=1, source_target_pairs={{0,2},{1,3},{2,0},{3,1},{4,6},{5,7},{6,4},{7,5},{8,10},{9,11},{10,... | collective-permute-start | bytes 983048 | tf_op jit(solution)/shard_map/ppermute | solution.py:34
  21.2 1.7 %pad_maximum_fusion.refs_5_.refs_9_ = bf16[128,8192]{1,0:T(8,128)(2,1)S(1)} fusion(bf16[64,8192]{1,0:T(8,128)(2,1)} %bitcast.22, bf16[64,8192]{1,0:T(8,128)(2,1)} %bitcast.23), kind=kLoop, calls=%fused_computation | loop fusion | flops 4194304 | bytes 4194304 | tf_op jit(solution)/shard_map/concatenate | solution.py:551
  23.6 3.4 %fetch.1.refs_4_.refs_8_ = bf16[8192,512]{1,0:T(8,128)(2,1)S(1)} custom-call(bf16[8192,512]{1,0:T(8,128)(2,1)} %refs_0_), custom_call_target="tpu_custom_call" | custom-call | bytes 16777216 | tf_op jit(solution)/shard_map/fetch/pallas_call | solution.py:223
  31.2 1.7 %project.3 = bf16[256,640]{1,0:T(8,128)(2,1)} custom-call(bf16[16,3072]{1,0:T(8,128)(2,1)S(1)} %pad_maximum_fusion.2.refs_0_, bf16[16,3072]{1,0:T(8,128)(2,1)S(1)} %collective-permute-done.5.refs_1_, bf16[16,3072]{1,0:T(8,128)(2,1)S(1)} %collective-permute-done.6.refs_2_, bf16[16,3072]{1,0:T(8,128)(2,1)S(1)} %collective-permute-done.7.refs_3_, ...), custom_call_target="tpu_custom_call" | custom-call | flops 503316480 | bytes 3932160 | tf_op jit(solution)/shard_map/project/pallas_call | solution.py:301
  32.9 3.5 %all-to-all-start = ((bf16[16,16,640]{2,1,0:T(8,128)(2,1)}), bf16[16,16,640]{2,1,0:T(8,128)(2,1)S(1)}, u32[]{:S(2)}, u32[]{:S(2)}) async-start(bf16[16,16,640]{2,1,0:T(8,128)(2,1)} %bitcast.5), calls=%async_computation | async-start | bytes 655360 | tf_op jit(solution)/shard_map/all_to_all | solution.py:573
  37.2 10.3 %all-to-all-done.inbound = bf16[16,16,640]{2,1,0:T(8,128)(2,1)S(1)} async-done(((bf16[16,16,640]{2,1,0:T(8,128)(2,1)}), bf16[16,16,640]{2,1,0:T(8,128)(2,1)S(1)}, u32[]{:S(2)}, u32[]{:S(2)}) %all-to-all-start) | async-done | bytes 327712 | tf_op jit(solution)/shard_map/all_to_all | solution.py:573
  47.5 6.0 %attend.1 = bf16[16,16,512]{2,1,0:T(8,128)(2,1)} custom-call(s32[16,4]{1,0:T(8,128)S(1)} %copy.21.table, s32[2,1,128]{2,1,0:T(1,128)S(1)} %bitcast.18, bf16[16,16,640]{2,1,0:T(8,128)(2,1)S(1)} %all-to-all-done.inbound, f32[16,128]{1,0:T(8,128)S(1)} %pad_maximum_fusion.3.cosine, f32[16,128]{1,0:T(8,128)S(1)} %pad_maximum_fusion.4.sine, ...), custom_call_target="tpu_custom_call" | custom-call | flops 134217728 | bytes 8388608 | tf_op jit(solution)/shard_map/attend/pallas_call | solution.py:480
  53.5 3.5 %all-to-all-start.1 = ((bf16[16,16,512]{2,1,0:T(8,128)(2,1)}), bf16[16,16,512]{2,1,0:T(8,128)(2,1)S(1)}, u32[]{:S(2)}, u32[]{:S(2)}) async-start(bf16[16,16,512]{2,1,0:T(8,128)(2,1)} %attend.1), calls=%async_computation.1 | async-start | bytes 524288 | tf_op jit(solution)/shard_map/all_to_all | solution.py:585
  58.8 8.3 %all-to-all-done.1 = bf16[16,16,512]{2,1,0:T(8,128)(2,1)S(1)} async-done(((bf16[16,16,512]{2,1,0:T(8,128)(2,1)}), bf16[16,16,512]{2,1,0:T(8,128)(2,1)S(1)}, u32[]{:S(2)}, u32[]{:S(2)}) %all-to-all-start.1) | async-done | bytes 262176 | tf_op jit(solution)/shard_map/all_to_all | solution.py:585
  67.1 3.9 %product.1 = (bf16[64,5120]{1,0:T(8,128)(2,1)S(1)}, f32[64,5120]{1,0:T(8,128)S(1)}, bf16[64,3072]{1,0:T(8,128)(2,1)S(1)}, f32[64,3072]{1,0:T(8,128)S(1)}) custom-call(s32[1,128]{1,0:T(1,128)S(1)} %reshape_reshape.6.place_a, s32[1,128]{1,0:T(1,128)S(1)} %reshape_reshape.7.place_b, bf16[256,512]{1,0:T(8,128)(2,1)S(1)} %bitcast.16, bf16[512,8192]{1,0:T(8,128)(2,1)} %w_out.1), custom_call_target="tpu_custom_call" | custom-call | flops 1073741824 | bytes 8388608 | tf_op jit(solution)/shard_map/product/pallas_call | solution.py:137
  71.0 2.1 %collective-permute-done.14 = bf16[64,5120]{1,0:T(8,128)(2,1)S(1)} collective-permute-done((bf16[64,5120]{1,0:T(8,128)(2,1)S(1)}, bf16[64,5120]{1,0:T(8,128)(2,1)S(1)}, u32[]{:S(2)}, u32[]{:S(2)}) %collective-permute-start.14) | collective-permute-done | bytes 655392 | tf_op jit(solution)/shard_map/ppermute | solution.py:34
  73.5 1.6 %collective-permute-done.16 = bf16[64,3072]{1,0:T(8,128)(2,1)S(1)} collective-permute-done((bf16[64,3072]{1,0:T(8,128)(2,1)S(1)}, bf16[64,3072]{1,0:T(8,128)(2,1)S(1)}, u32[]{:S(2)}, u32[]{:S(2)}) %collective-permute-start.16) | collective-permute-done | bytes 393248 | tf_op jit(solution)/shard_map/ppermute | solution.py:34
  77.4 3.5 %collective-permute-done.18 = bf16[16,3072]{1,0:T(8,128)(2,1)S(1)} collective-permute-done((bf16[16,3072]{1,0:T(8,128)(2,1)S(1)}, bf16[16,3072]{1,0:T(8,128)(2,1)S(1)}, u32[]{:S(2)}, u32[]{:S(2)}) %collective-permute-start.18) | collective-permute-done | bytes 98336 | tf_op jit(solution)/shard_map/ppermute | solution.py:34
  82.0 3.3 %collective-permute-done.15 = bf16[32,5120]{1,0:T(8,128)(2,1)S(1)} collective-permute-done((bf16[32,5120]{1,0:T(8,128)(2,1)S(1)}, bf16[32,5120]{1,0:T(8,128)(2,1)S(1)}, u32[]{:S(2)}, u32[]{:S(2)}) %collective-permute-start.15) | collective-permute-done | bytes 327712 | tf_op jit(solution)/shard_map/ppermute | solution.py:34
  85.3 2.0 %collective-permute-done.19 = bf16[16,3072]{1,0:T(8,128)(2,1)S(1)} collective-permute-done((bf16[16,3072]{1,0:T(8,128)(2,1)S(1)}, bf16[16,3072]{1,0:T(8,128)(2,1)S(1)}, u32[]{:S(2)}, u32[]{:S(2)}) %collective-permute-start.19) | collective-permute-done | bytes 98336 | tf_op jit(solution)/shard_map/ppermute | solution.py:34
  87.5 2.0 %collective-permute-start.20 = (bf16[8,5120]{1,0:T(8,128)(2,1)S(1)}, bf16[8,5120]{1,0:T(8,128)(2,1)S(1)}, u32[]{:S(2)}, u32[]{:S(2)}) collective-permute-start(bf16[8,5120]{1,0:T(8,128)(2,1)S(1)} %get-tuple-element.65), channel_id=1, source_target_pairs={{0,4},{1,5},{2,6},{3,7},{4,0},{5,1},{6,2},{7,3},{8,12},{9,13},{10,... | collective-permute-start | bytes 245768 | tf_op jit(solution)/shard_map/ppermute | solution.py:34
  90.1 1.8 %collective-permute-done.21 = bf16[8,5120]{1,0:T(8,128)(2,1)S(1)} collective-permute-done((bf16[8,5120]{1,0:T(8,128)(2,1)S(1)}, bf16[8,5120]{1,0:T(8,128)(2,1)S(1)}, u32[]{:S(2)}, u32[]{:S(2)}) %collective-permute-start.21) | collective-permute-done | bytes 81952 | tf_op jit(solution)/shard_map/ppermute | solution.py:34
  93.7 4.0 %collective-permute-done.22 = bf16[8,5120]{1,0:T(8,128)(2,1)S(1)} collective-permute-done((bf16[8,5120]{1,0:T(8,128)(2,1)S(1)}, bf16[8,5120]{1,0:T(8,128)(2,1)S(1)}, u32[]{:S(2)}, u32[]{:S(2)}) %collective-permute-start.22) | collective-permute-done | bytes 81952 | tf_op jit(solution)/shard_map/ppermute | solution.py:34
  (87 shorter events, 19.8 us)
Async XLA Ops:
  1.9 8.0 %collective-permute-start = (bf16[8,5120]{1,0:T(8,128)(2,1)S(1)}, bf16[8,5120]{1,0:T(8,128)(2,1)S(1)}, u32[]{:S(2)}, u32[]{:S(2)}) collective-permute-start(bf16[8,5120]{1,0:T(8,128)(2,1)S(1)} %get-tuple-element.31), channel_id=1, source_target_pairs={{0,8},{1,9},{2,10},{3,11},{4,12},{5,13},{6,14},{7,15},{8,0},{9,1},... | collective-permute-start | bytes 245768 | tf_op jit(solution)/shard_map/ppermute | solution.py:34
  6.0 5.7 %collective-permute-start.1 = (bf16[8,5120]{1,0:T(8,128)(2,1)S(1)}, bf16[8,5120]{1,0:T(8,128)(2,1)S(1)}, u32[]{:S(2)}, u32[]{:S(2)}) collective-permute-start(bf16[8,5120]{1,0:T(8,128)(2,1)S(1)} %get-tuple-element.31), channel_id=1, source_target_pairs={{0,4},{1,5},{2,6},{3,7},{4,0},{5,1},{6,2},{7,3},{8,12},{9,13},{10,... | collective-permute-start | bytes 245768 | tf_op jit(solution)/shard_map/ppermute | solution.py:34
  7.5 4.1 %collective-permute-start.3 = (bf16[8,3072]{1,0:T(8,128)(2,1)S(1)}, bf16[8,3072]{1,0:T(8,128)(2,1)S(1)}, u32[]{:S(2)}, u32[]{:S(2)}) collective-permute-start(bf16[8,3072]{1,0:T(8,128)(2,1)S(1)} %get-tuple-element.32), channel_id=1, source_target_pairs={{0,2},{1,3},{2,0},{3,1},{4,6},{5,7},{6,4},{7,5},{8,10},{9,11},{10,... | collective-permute-start | bytes 147464 | tf_op jit(solution)/shard_map/ppermute | solution.py:34
  9.8 4.5 %collective-permute-start.2 = (bf16[8,5120]{1,0:T(8,128)(2,1)S(1)}, bf16[8,5120]{1,0:T(8,128)(2,1)S(1)}, u32[]{:S(2)}, u32[]{:S(2)}) collective-permute-start(bf16[8,5120]{1,0:T(8,128)(2,1)S(1)} %collective-permute-done), channel_id=1, source_target_pairs={{0,4},{1,5},{2,6},{3,7},{4,0},{5,1},{6,2},{7,3},{8,12},{9,13},{10,... | collective-permute-start | bytes 245768 | tf_op jit(solution)/shard_map/ppermute | solution.py:34
  14.3 8.8 %collective-permute-start.5 = (bf16[16,3072]{1,0:T(8,128)(2,1)S(1)}, bf16[16,3072]{1,0:T(8,128)(2,1)S(1)}, u32[]{:S(2)}, u32[]{:S(2)}) collective-permute-start(bf16[16,3072]{1,0:T(8,128)(2,1)S(1)} %pad_maximum_fusion.2.refs_0_), channel_id=1, source_target_pairs={{0,8},{1,9},{2,10},{3,11},{4,12},{5,13},{6,14},{7,15},{8,0},{9,1},... | collective-permute-start | bytes 294920 | tf_op jit(solution)/shard_map/ppermute | solution.py:34
  16.8 10.2 %collective-permute-start.6 = (bf16[16,3072]{1,0:T(8,128)(2,1)S(1)}, bf16[16,3072]{1,0:T(8,128)(2,1)S(1)}, u32[]{:S(2)}, u32[]{:S(2)}) collective-permute-start(bf16[16,3072]{1,0:T(8,128)(2,1)S(1)} %pad_maximum_fusion.2.refs_0_), channel_id=1, source_target_pairs={{0,4},{1,5},{2,6},{3,7},{4,0},{5,1},{6,2},{7,3},{8,12},{9,13},{10,... | collective-permute-start | bytes 294920 | tf_op jit(solution)/shard_map/ppermute | solution.py:34
  18.8 9.5 %collective-permute-start.4 = (bf16[32,5120]{1,0:T(8,128)(2,1)S(1)}, bf16[32,5120]{1,0:T(8,128)(2,1)S(1)}, u32[]{:S(2)}, u32[]{:S(2)}) collective-permute-start(bf16[32,5120]{1,0:T(8,128)(2,1)S(1)} %pad_maximum_fusion.1.refs_0_), channel_id=1, source_target_pairs={{0,2},{1,3},{2,0},{3,1},{4,6},{5,7},{6,4},{7,5},{8,10},{9,11},{10,... | collective-permute-start | bytes 983048 | tf_op jit(solution)/shard_map/ppermute | solution.py:34
  20.3 9.0 %collective-permute-start.12 = (bf16[32,5120]{1,0:T(8,128)(2,1)S(1)}, bf16[32,5120]{1,0:T(8,128)(2,1)S(1)}, u32[]{:S(2)}, u32[]{:S(2)}) collective-permute-start(bf16[32,5120]{1,0:T(8,128)(2,1)S(1)} %pad_maximum_fusion.1.refs_0_), channel_id=1, source_target_pairs={{0,1},{1,0},{2,3},{3,2},{4,5},{5,4},{6,7},{7,6},{8,9},{9,8},{10,11... | collective-permute-start | bytes 983048 | tf_op jit(solution)/shard_map/ppermute | solution.py:34
  23.1 5.2 %collective-permute-start.7 = (bf16[16,3072]{1,0:T(8,128)(2,1)S(1)}, bf16[16,3072]{1,0:T(8,128)(2,1)S(1)}, u32[]{:S(2)}, u32[]{:S(2)}) collective-permute-start(bf16[16,3072]{1,0:T(8,128)(2,1)S(1)} %collective-permute-done.5.refs_1_), channel_id=1, source_target_pairs={{0,4},{1,5},{2,6},{3,7},{4,0},{5,1},{6,2},{7,3},{8,12},{9,13},{10,... | collective-permute-start | bytes 294920 | tf_op jit(solution)/shard_map/ppermute | solution.py:34
  28.3 2.8 %collective-permute-start.10 = (bf16[16,3072]{1,0:T(8,128)(2,1)S(1)}, bf16[16,3072]{1,0:T(8,128)(2,1)S(1)}, u32[]{:S(2)}, u32[]{:S(2)}) collective-permute-start(bf16[16,3072]{1,0:T(8,128)(2,1)S(1)} %collective-permute-done.6.refs_2_), channel_id=1, source_target_pairs={{0,1},{1,0},{2,3},{3,2},{4,5},{5,4},{6,7},{7,6},{8,9},{9,8},{10,11... | collective-permute-start | bytes 294920 | tf_op jit(solution)/shard_map/ppermute | solution.py:34
  28.8 2.3 %collective-permute-start.11 = (bf16[16,3072]{1,0:T(8,128)(2,1)S(1)}, bf16[16,3072]{1,0:T(8,128)(2,1)S(1)}, u32[]{:S(2)}, u32[]{:S(2)}) collective-permute-start(bf16[16,3072]{1,0:T(8,128)(2,1)S(1)} %collective-permute-done.7.refs_3_), channel_id=1, source_target_pairs={{0,1},{1,0},{2,3},{3,2},{4,5},{5,4},{6,7},{7,6},{8,9},{9,8},{10,11... | collective-permute-start | bytes 294920 | tf_op jit(solution)/shard_map/ppermute | solution.py:34
  28.8 2.3 %collective-permute-start.8 = (bf16[16,3072]{1,0:T(8,128)(2,1)S(1)}, bf16[16,3072]{1,0:T(8,128)(2,1)S(1)}, u32[]{:S(2)}, u32[]{:S(2)}) collective-permute-start(bf16[16,3072]{1,0:T(8,128)(2,1)S(1)} %pad_maximum_fusion.2.refs_0_), channel_id=1, source_target_pairs={{0,1},{1,0},{2,3},{3,2},{4,5},{5,4},{6,7},{7,6},{8,9},{9,8},{10,11... | collective-permute-start | bytes 294920 | tf_op jit(solution)/shard_map/ppermute | solution.py:34
  29.4 1.8 %collective-permute-start.9 = (bf16[16,3072]{1,0:T(8,128)(2,1)S(1)}, bf16[16,3072]{1,0:T(8,128)(2,1)S(1)}, u32[]{:S(2)}, u32[]{:S(2)}) collective-permute-start(bf16[16,3072]{1,0:T(8,128)(2,1)S(1)} %collective-permute-done.5.refs_1_), channel_id=1, source_target_pairs={{0,1},{1,0},{2,3},{3,2},{4,5},{5,4},{6,7},{7,6},{8,9},{9,8},{10,11... | collective-permute-start | bytes 294920 | tf_op jit(solution)/shard_map/ppermute | solution.py:34
  32.9 14.6 %all-to-all-start = ((bf16[16,16,640]{2,1,0:T(8,128)(2,1)}), bf16[16,16,640]{2,1,0:T(8,128)(2,1)S(1)}, u32[]{:S(2)}, u32[]{:S(2)}) async-start(bf16[16,16,640]{2,1,0:T(8,128)(2,1)} %bitcast.5), calls=%async_computation | async-start | bytes 655360 | tf_op jit(solution)/shard_map/all_to_all | solution.py:573
  53.5 13.6 %all-to-all-start.1 = ((bf16[16,16,512]{2,1,0:T(8,128)(2,1)}), bf16[16,16,512]{2,1,0:T(8,128)(2,1)S(1)}, u32[]{:S(2)}, u32[]{:S(2)}) async-start(bf16[16,16,512]{2,1,0:T(8,128)(2,1)} %attend.1), calls=%async_computation.1 | async-start | bytes 524288 | tf_op jit(solution)/shard_map/all_to_all | solution.py:585
  70.9 2.2 %collective-permute-start.14 = (bf16[64,5120]{1,0:T(8,128)(2,1)S(1)}, bf16[64,5120]{1,0:T(8,128)(2,1)S(1)}, u32[]{:S(2)}, u32[]{:S(2)}) collective-permute-start(bf16[64,5120]{1,0:T(8,128)(2,1)S(1)} %get-tuple-element.50), channel_id=1, source_target_pairs={{0,1},{1,0},{2,3},{3,2},{4,5},{5,4},{6,7},{7,6},{8,9},{9,8},{10,11... | collective-permute-start | bytes 1966088 | tf_op jit(solution)/shard_map/ppermute | solution.py:34
  75.2 5.7 %collective-permute-start.18 = (bf16[16,3072]{1,0:T(8,128)(2,1)S(1)}, bf16[16,3072]{1,0:T(8,128)(2,1)S(1)}, u32[]{:S(2)}, u32[]{:S(2)}) collective-permute-start(bf16[16,3072]{1,0:T(8,128)(2,1)S(1)} %get-tuple-element.63), channel_id=1, source_target_pairs={{0,4},{1,5},{2,6},{3,7},{4,0},{5,1},{6,2},{7,3},{8,12},{9,13},{10,... | collective-permute-start | bytes 294920 | tf_op jit(solution)/shard_map/ppermute | solution.py:34
  75.6 9.7 %collective-permute-start.15 = (bf16[32,5120]{1,0:T(8,128)(2,1)S(1)}, bf16[32,5120]{1,0:T(8,128)(2,1)S(1)}, u32[]{:S(2)}, u32[]{:S(2)}) collective-permute-start(bf16[32,5120]{1,0:T(8,128)(2,1)S(1)} %slice.82), channel_id=1, source_target_pairs={{0,2},{1,3},{2,0},{3,1},{4,6},{5,7},{6,4},{7,5},{8,10},{9,11},{10,... | collective-permute-start | bytes 983048 | tf_op jit(solution)/shard_map/ppermute | solution.py:34
  76.4 8.9 %collective-permute-start.17 = (bf16[16,3072]{1,0:T(8,128)(2,1)S(1)}, bf16[16,3072]{1,0:T(8,128)(2,1)S(1)}, u32[]{:S(2)}, u32[]{:S(2)}) collective-permute-start(bf16[16,3072]{1,0:T(8,128)(2,1)S(1)} %get-tuple-element.64), channel_id=1, source_target_pairs={{0,4},{1,5},{2,6},{3,7},{4,0},{5,1},{6,2},{7,3},{8,12},{9,13},{10,... | collective-permute-start | bytes 294920 | tf_op jit(solution)/shard_map/ppermute | solution.py:34
  80.9 6.4 %collective-permute-start.19 = (bf16[16,3072]{1,0:T(8,128)(2,1)S(1)}, bf16[16,3072]{1,0:T(8,128)(2,1)S(1)}, u32[]{:S(2)}, u32[]{:S(2)}) collective-permute-start(bf16[16,3072]{1,0:T(8,128)(2,1)S(1)} %fusion.2), channel_id=1, source_target_pairs={{0,8},{1,9},{2,10},{3,11},{4,12},{5,13},{6,14},{7,15},{8,0},{9,1},... | collective-permute-start | bytes 294920 | tf_op jit(solution)/shard_map/ppermute | solution.py:34
  87.4 4.5 %collective-permute-start.21 = (bf16[8,5120]{1,0:T(8,128)(2,1)S(1)}, bf16[8,5120]{1,0:T(8,128)(2,1)S(1)}, u32[]{:S(2)}, u32[]{:S(2)}) collective-permute-start(bf16[8,5120]{1,0:T(8,128)(2,1)S(1)} %get-tuple-element.66), channel_id=1, source_target_pairs={{0,4},{1,5},{2,6},{3,7},{4,0},{5,1},{6,2},{7,3},{8,12},{9,13},{10,... | collective-permute-start | bytes 245768 | tf_op jit(solution)/shard_map/ppermute | solution.py:34
  87.5 6.2 %collective-permute-start.20 = (bf16[8,5120]{1,0:T(8,128)(2,1)S(1)}, bf16[8,5120]{1,0:T(8,128)(2,1)S(1)}, u32[]{:S(2)}, u32[]{:S(2)}) collective-permute-start(bf16[8,5120]{1,0:T(8,128)(2,1)S(1)} %get-tuple-element.65), channel_id=1, source_target_pairs={{0,4},{1,5},{2,6},{3,7},{4,0},{5,1},{6,2},{7,3},{8,12},{9,13},{10,... | collective-permute-start | bytes 245768 | tf_op jit(solution)/shard_map/ppermute | solution.py:34
  89.6 4.2 %collective-permute-start.23 = (bf16[8,3072]{1,0:T(8,128)(2,1)S(1)}, bf16[8,3072]{1,0:T(8,128)(2,1)S(1)}, u32[]{:S(2)}, u32[]{:S(2)}) collective-permute-start(bf16[8,3072]{1,0:T(8,128)(2,1)S(1)} %slice.83), channel_id=1, source_target_pairs={{0,2},{1,3},{2,0},{3,1},{4,6},{5,7},{6,4},{7,5},{8,10},{9,11},{10,... | collective-permute-start | bytes 147464 | tf_op jit(solution)/shard_map/ppermute | solution.py:34
  92.0 5.8 %collective-permute-start.22 = (bf16[8,5120]{1,0:T(8,128)(2,1)S(1)}, bf16[8,5120]{1,0:T(8,128)(2,1)S(1)}, u32[]{:S(2)}, u32[]{:S(2)}) collective-permute-start(bf16[8,5120]{1,0:T(8,128)(2,1)S(1)} %fusion.3), channel_id=1, source_target_pairs={{0,8},{1,9},{2,10},{3,11},{4,12},{5,13},{6,14},{7,15},{8,0},{9,1},... | collective-permute-start | bytes 245768 | tf_op jit(solution)/shard_map/ppermute | solution.py:34
  (8 other events, 34.5 us)

commit v10 on v9

--- a/solution.py
+++ b/solution.py
@@ -69,20 +69,27 @@
     return [x, crossed, grid.send(x, pair=1), grid.send(crossed, pair=1)]
 
 
-def gather_rows(grid, xa, xb, meanwhile):
+def gather_rows(grid, xa, xb, first, second):
     beside_b = grid.send(xb, near=1)
-    line_a = jnp.concatenate(gather_line(grid, xa), axis=0)
+    line_a = jnp.concatenate(
+        [xa]
+        + [
+            grid.send(xa, half=half, pair=pair)
+            for pair in range(2)
+            for half in range(grid.half)
+            if half or pair
+        ],
+        axis=0,
+    )
     pair_b = jnp.concatenate([xb, beside_b], axis=0)
-    line_a, pair_b = lax.optimization_barrier((line_a, pair_b))
+    line_a, pair_b, first = lax.optimization_barrier((line_a, pair_b, first(xa)))
     beside_a = grid.send(line_a, near=1)
     parts_b = gather_line(grid, pair_b)
-    beside_a, parts_b, meanwhile = lax.optimization_barrier(
-        (beside_a, parts_b, meanwhile(pair_b))
-    )
+    beside_a, parts_b, second = lax.optimization_barrier((beside_a, parts_b, second(pair_b)))
     parts_a = [line_a, beside_a]
     parts_a += [grid.send(part, core=1) for part in parts_a]
     parts_b += [grid.send(part, core=1) for part in parts_b]
-    return parts_a, parts_b, meanwhile
+    return parts_a, parts_b, first, second
 
 
 def narrow(x):
@@ -93,12 +100,31 @@
     return x.astype(jnp.float32)
 
 
-def product_kernel(cuts, place_a, place_b, returned, w_out, away_a, keep_a, away_b, keep_b, held, sems):
+def product_kernel(
+    cuts,
+    place_a,
+    place_b,
+    returned,
+    w_out,
+    w_front,
+    away_a,
+    keep_a,
+    away_b,
+    keep_b,
+    held,
+    sems,
+):
+    front = w_front.shape[1]
     copies = []
     for i, (start, stop) in enumerate(cuts):
-        here = pl.ds(start, stop - start)
-        copies.append(pltpu.make_async_copy(w_out.at[:, here], held.at[:, here], sems.at[i]))
-        copies[-1].start()
+        copy = None
+        if start >= front:
+            size = pl.ds(start, stop - start), pl.ds(start - front, stop - start)
+            copy = pltpu.make_async_copy(
+                w_out.at[:, size[0]], held.at[:, size[1]], sems.at[i]
+            )
+            copy.start()
+        copies.append(copy)
     slots = lax.broadcasted_iota(jnp.int32, (returned.shape[0], place_a.shape[1]), 0)
 
     def picked(place):
@@ -112,20 +138,23 @@
     half = keep_a.shape[0]
     middle = keep_a.shape[1]
     for copy, (start, stop) in zip(copies, cuts):
-        copy.wait()
+        if copy is not None:
+            copy.wait()
         rows, away, keep = (rows_a, away_a, keep_a) if start < middle else (rows_b, away_b, keep_b)
-        x = jnp.dot(rows, held[:, start:stop], preferred_element_type=jnp.float32)
+        w = w_front[:, start:stop] if copy is None else held[:, start - front : stop - front]
+        x = jnp.dot(rows, w, preferred_element_type=jnp.float32)
         begin = start if start < middle else start - middle
         here = slice(begin, begin + stop - start)
         keep[:, here] = x[:half]
         away[:, here] = x[half:].astype(jnp.bfloat16)
 
 
-def product(place_a, place_b, returned, w_out, cut):
+def product(place_a, place_b, returned, w_out, w_front, cut):
     rows = place_a.shape[0]
     depth, width = w_out.shape
     cuts = []
-    for start, stop in ((0, cut), (cut, width)):
+    front = w_front.shape[1]
+    for start, stop in ((0, front), (front, cut), (cut, width)):
         while start < stop:
             cuts.append((start, min(start + 1024, stop)))
             start = cuts[-1][1]
@@ -136,11 +165,11 @@
         out.append(jax.ShapeDtypeStruct((rows // 2, size), jnp.float32))
     return pl.pallas_call(
         functools.partial(product_kernel, tuple(cuts)),
-        in_specs=[vmem, vmem, vmem, pl.BlockSpec(memory_space=pl.ANY)],
+        in_specs=[vmem, vmem, vmem, pl.BlockSpec(memory_space=pl.ANY), vmem],
         out_specs=[vmem] * 4,
         out_shape=out,
         scratch_shapes=[
-            pltpu.VMEM(w_out.shape, jnp.bfloat16),
+            pltpu.VMEM((depth, width - front), jnp.bfloat16),
             pltpu.SemaphoreType.DMA((len(cuts),)),
         ],
         compiler_params=pltpu.CompilerParams(vmem_limit_bytes=48 * 2**20),
@@ -148,10 +177,10 @@
             flops=2 * rows * depth * width, bytes_accessed=2 * depth * width, transcendentals=0
         ),
         name="product",
-    )(place_a.reshape(1, rows), place_b.reshape(1, rows), returned, w_out)
-
-
-def scatter_sum(grid, place_a, place_b, returned, w_out, cut):
+    )(place_a.reshape(1, rows), place_b.reshape(1, rows), returned, w_out, w_front)
+
+
+def scatter_sum(grid, place_a, place_b, returned, w_out, w_front, cut):
     def along_line(x):
         size = x.shape[0] // 2 // grid.half
         middle = x.shape[0] // 2
@@ -164,12 +193,23 @@
         ]
         return x[:size], [second] + third
 
+    def direct(x):
+        size = x.shape[0] // 2 // grid.half
+        parts = []
+        for pair in range(2):
+            for half in range(grid.half):
+                begin = (pair * grid.half + half) * size
+                if begin:
+                    sent = narrow(x[begin : begin + size])
+                    parts.append(grid.send(sent, half=half, pair=pair))
+        return x[:size], parts
+
     def total(x, parts):
         for part in parts:
             x = x + wide(part)
         return x
 
-    away_a, keep_a, away_b, keep_b = product(place_a, place_b, returned, w_out, cut)
+    away_a, keep_a, away_b, keep_b = product(place_a, place_b, returned, w_out, w_front, cut)
     xa = keep_a + wide(grid.send(away_a, core=1))
     middle = xa.shape[0] // 2
     sent_a = narrow(xa[middle:])
@@ -177,7 +217,7 @@
     xb = keep_b + wide(grid.send(after(away_b, sent_a), core=1))
     xb, got_b = along_line(xb)
     got_a, got_b = lax.optimization_barrier((got_a, got_b))
-    xa, parts_a = along_line(xa[:middle] + wide(got_a))
+    xa, parts_a = direct(xa[:middle] + wide(got_a))
     xb = total(xb, got_b)
     middle = xb.shape[0] // 2
     xb = xb[:middle] + wide(grid.send(narrow(xb[middle:]), near=1))
@@ -207,28 +247,37 @@
     )(x, gain.reshape(1, -1))
 
 
-def fetch_kernel(*refs):
-    count = len(refs) // 2
+def fetch_kernel(starts, *refs):
+    count = len(starts)
     sems = refs[-1]
-    copies = [
-        pltpu.make_async_copy(refs[i], refs[count + i], sems.at[i]) for i in range(count)
-    ]
-    for copy in copies:
-        copy.start()
+    copies = []
+    for i, start in enumerate(starts):
+        source, target = refs[i], refs[count + i]
+        if start is not None:
+            columns = pl.ds(start, target.shape[-1])
+            source = source.at[(slice(None),) * (len(target.shape) - 1) + (columns,)]
+        copies.append(pltpu.make_async_copy(source, target, sems.at[i]))
+        copies[-1].start()
     for copy in copies:
         copy.wait()
 
 
-def fetch(*arrays, limit):
+def fetch(*wanted, limit):
+    arrays = [x for x, _ in wanted]
+    starts = [columns and columns[0] for _, columns in wanted]
+    out = [
+        jax.ShapeDtypeStruct(x.shape[:-1] + (columns[1],) if columns else x.shape, x.dtype)
+        for x, columns in wanted
+    ]
     return pl.pallas_call(
-        fetch_kernel,
+        functools.partial(fetch_kernel, starts),
         in_specs=[pl.BlockSpec(memory_space=pl.ANY)] * len(arrays),
         out_specs=[pl.BlockSpec(memory_space=pltpu.VMEM)] * len(arrays),
-        out_shape=[jax.ShapeDtypeStruct(x.shape, x.dtype) for x in arrays],
+        out_shape=out,
         scratch_shapes=[pltpu.SemaphoreType.DMA((len(arrays),))],
         compiler_params=pltpu.CompilerParams(vmem_limit_bytes=limit * 2**20),
         cost_estimate=pl.CostEstimate(
-            flops=0, bytes_accessed=sum(x.size * 4 for x in arrays), transcendentals=0
+            flops=0, bytes_accessed=sum(x.size * 4 for x in out), transcendentals=0
         ),
         name="fetch",
     )(*arrays)
@@ -325,6 +374,7 @@
     sine,
     key_pages,
     value_pages,
+    key_front,
     out,
     key_pool,
     value_pool,
@@ -350,7 +400,9 @@
 
     cuts = 4
     size = key_pages.shape[0] // cuts
-    for i, (pool, on_chip) in enumerate(((key_pages, key_pool), (value_pages, value_pool))):
+    front = key_front.shape[2]
+    back = key_pages.at[:, :, pl.ds(front, kv_width - front)]
+    for i, (pool, on_chip) in enumerate(((back, key_pool), (value_pages, value_pool))):
         for cut in range(cuts):
             part = pl.ds(cut * size, size)
             pltpu.make_async_copy(pool.at[part], on_chip.at[part], sems.at[i]).start()
@@ -397,11 +449,15 @@
         jnp.int32, (columns, columns), 1
     )
 
-    pltpu.make_async_copy(key_pool, key_pool, sems.at[0]).wait()
     own_chances = {}
-    for b in range(batches):
-        valid = row < lengths[b]
-        for p in range(pairs):
+    for p in range(pairs):
+        begin = p * 2 * HEAD
+        if begin == front:
+            pltpu.make_async_copy(key_pool, key_pool, sems.at[0]).wait()
+        source = key_front if begin < front else key_pool
+        inside = begin if begin < front else begin - front
+        for b in range(batches):
+            valid = row < lengths[b]
             turned = query_rot[p, b].T.astype(jnp.bfloat16)
             none = jnp.zeros_like(turned)
             wide = jnp.concatenate(
@@ -410,7 +466,7 @@
             columns_p = slice(p * 2 * HEAD, (p + 1) * 2 * HEAD)
             keys = []
             for s in range(batch):
-                keys += held(key_pool, b * batch + s, columns_p)
+                keys += held(source, b * batch + s, slice(inside, inside + 2 * HEAD))
             keys.append(key_new[:, columns_p])
             products = jnp.dot(
                 jnp.concatenate(keys, axis=0), wide, preferred_element_type=jnp.float32
@@ -461,7 +517,9 @@
             ).astype(jnp.bfloat16)
 
 
-def attend(inbound, lengths, table, cosine, sine, key_pages, value_pages, per_query, per_key):
+def attend(
+    inbound, lengths, table, cosine, sine, key_pages, value_pages, key_front, per_query, per_key
+):
     owners, slots, _ = inbound.shape
     pages = table.shape[1]
     page, kv_width = key_pages.shape[1:]
@@ -479,11 +537,11 @@
     hbm = pl.BlockSpec(memory_space=pl.ANY)
     return pl.pallas_call(
         functools.partial(attend_kernel, per_query, per_key),
-        in_specs=[smem, vmem, vmem, vmem, vmem, hbm, hbm],
+        in_specs=[smem, vmem, vmem, vmem, vmem, hbm, hbm, vmem],
         out_specs=vmem,
         out_shape=jax.ShapeDtypeStruct((owners, slots, per_query), jnp.bfloat16),
         scratch_shapes=[
-            pltpu.VMEM(key_pages.shape, jnp.bfloat16),
+            pltpu.VMEM(key_pages.shape[:2] + (kv_width - key_front.shape[2],), jnp.bfloat16),
             pltpu.VMEM(value_pages.shape, jnp.bfloat16),
             pltpu.SemaphoreType.DMA((2,)),
             pltpu.VMEM((slots, kv_width), jnp.bfloat16),
@@ -499,7 +557,7 @@
             transcendentals=slots * heads * span,
         ),
         name="attend",
-    )(table, lengths, inbound, cosine, sine, key_pages, value_pages)
+    )(table, lengths, inbound, cosine, sine, key_pages, value_pages, key_front)
 
 
 def on_device(
@@ -541,17 +599,21 @@
         moved = jnp.where(pick[:, :, None], place.reshape(1, owners, rows_dev), 0)
         return jnp.sum(moved, axis=1).reshape(requests)
 
-    def beside_gather(x):
-        (w,) = fetch(after(w_query, x), limit=44)
+    def first(x):
+        place = placed(after(kv_owner, x))
+        place_in = reordered(place, grid.blocks(-1, ORDER_A))
+        (w,) = fetch((after(w_query, place_in), None), limit=44)
+        return w, place, place_in
+
+    def second(x):
         pieces = [after(w_key, x).T, w_value.T]
         spare = row_width - per_query - 2 * per_key
         if spare:
             pieces.append(jnp.zeros((spare, width), w_key.dtype))
-        place = placed(after(kv_owner, x))
-        return w, jnp.concatenate(pieces, axis=0), place, reordered(place, grid.blocks(-1, ORDER_A))
-
-    parts_a, parts_b, others = gather_rows(grid, xa, xb, beside_gather)
-    w_query, w_kv_t, place, place_in = others
+        return jnp.concatenate(pieces, axis=0)
+
+    parts_a, parts_b, others, w_kv_t = gather_rows(grid, xa, xb, first, second)
+    w_query, place, place_in = others
     plain = list(range(owners))
     total = project(0, parts_a, plain, w_query, w_kv_t, None, None, all_slots)
     total = project(cut, parts_b, order_b, w_query, w_kv_t, total, place_in, all_slots)
@@ -571,6 +633,8 @@
     cosine = jnp.concatenate([cosine_part, cosine_part], axis=1)
     sine = jnp.concatenate([-sine_part, sine_part], axis=1)
     inbound = lax.all_to_all(outbound, AXES, split_axis=0, concat_axis=0, tiled=True)
+    kv_half = key_pages.shape[3] // 2
+    (key_front,) = fetch((after(key_pages, outbound)[0], (0, kv_half)), limit=51)
     attended = attend(
         inbound,
         lengths,
@@ -579,12 +643,14 @@
         sine,
         key_pages[0],
         value_pages[0],
+        key_front,
         per_query,
         per_key,
     )
+    (w_front,) = fetch((after(w_out, attended), (0, width // 32 * 10)), limit=48)
     returned = lax.all_to_all(attended, AXES, split_axis=0, concat_axis=0, tiled=True)
     returned = returned.reshape(all_slots, per_query)
-    summed = scatter_sum(grid, place_a, place_b, returned, w_out, cut)
+    summed = scatter_sum(grid, place_a, place_b, returned, w_out, w_front, width // 32 * 19)
     return narrow(wide(hidden_in) + summed)
 
 

time: 99 us -> 98.6 us (level)
  waiting for transfers between devices: 43.5 us -> 38 us
  Pallas kernels: 16.3 us -> 20 us
  local copies, waits for them, and re-layouts: 3.99 us -> 5.33 us
    pallas_call x1 -> x3, Pallas kernels: 3.39 us -> 6.91 us  [fetch(): pl.pallas_call(functools.partial(fetch_kernel, starts), in_specs=[pl.Bloc...]
    all_to_all x1, waiting for transfers between devices: 10.3 us -> 7.37 us  [on_device(): lax.all_to_all(outbound, AXES, split_axis=0, concat_axis=0, tiled=True)]
    all_to_all x1, waiting for transfers between devices: 8.26 us -> 6.5 us  [on_device(): lax.all_to_all(attended, AXES, split_axis=0, concat_axis=0, tiled=True)]
    concatenate x2, other arithmetic: 1.72 us -> 0.21 us  [the longest x1 0.18 us: second(): return jnp.concatenate(pieces, axis=0)]
    unnamed x12 -> x16, local copies, waits for them, and re-layouts: 1.69 us -> 3.03 us
  transfers between devices with their start and end apart: 26 -> 26, of which waited for: 14 -> 13; matrix products, arithmetic and copies ran while one was open for 7% -> 6% of each run, Pallas kernels for 5% -> 8%
where the time goes in v10:
time: 98.6 us; the launch traced here: 98 us
  waiting for transfers between devices  38 us (39%)
  starting transfers between devices  29.8 us (30%)
  Pallas kernels  20 us (20%)
  local copies, waits for them, and re-layouts  5.33 us (5%)
  other arithmetic  4.48 us (5%)
    ppermute x24, waiting for transfers between devices, send(): return lax.ppermute(x, AXES, pairs)  24.2 us
    ppermute x24, starting transfers between devices, send(): return lax.ppermute(x, AXES, pairs)  22.3 us
    all_to_all x1, waiting for transfers between devices, on_device(): lax.all_to_all(outbound, AXES, split_axis=0, concat_axis=0, tiled=True)  7.37 us
    pallas_call x3, Pallas kernels, fetch(): pl.pallas_call(functools.partial(fetch_kernel, starts), in_specs=[pl.Bloc...  6.91 us
    pallas_call x1, Pallas kernels, attend(): pl.pallas_call(functools.partial(attend_kernel, per_query, per_key), in_s...  6.58 us
    all_to_all x1, waiting for transfers between devices, on_device(): lax.all_to_all(attended, AXES, split_axis=0, concat_axis=0, tiled=True)  6.5 us
    all_to_all x1, starting transfers between devices, on_device(): lax.all_to_all(outbound, AXES, split_axis=0, concat_axis=0, tiled=True)  4.02 us
    all_to_all x1, starting transfers between devices, on_device(): lax.all_to_all(attended, AXES, split_axis=0, concat_axis=0, tiled=True)  3.54 us
  transfers between devices with their start and end apart: 26, of which 13 were waited for; matrix products, arithmetic and copies ran while one was open for 6% of the time, Pallas kernels for 8%

profile of v10, /device:TPU:0, one launch (start us, length us, event | category | flops | bytes accessed | tf_op | source)
XLA Modules:
  0.0 98.0 jit_solution(5021864633797033240)
XLA Ops:
  1.9 4.1 %collective-permute-start = (bf16[8,5120]{1,0:T(8,128)(2,1)S(1)}, bf16[8,5120]{1,0:T(8,128)(2,1)S(1)}, u32[]{:S(2)}, u32[]{:S(2)}) collective-permute-start(bf16[8,5120]{1,0:T(8,128)(2,1)S(1)} %get-tuple-element.33), channel_id=1, source_target_pairs={{0,8},{1,9},{2,10},{3,11},{4,12},{5,13},{6,14},{7,15},{8,0},{9,1},... | collective-permute-start | bytes 245768 | tf_op jit(solution)/shard_map/ppermute | solution.py:34
  7.5 1.7 %collective-permute-start.3 = (bf16[8,3072]{1,0:T(8,128)(2,1)S(1)}, bf16[8,3072]{1,0:T(8,128)(2,1)S(1)}, u32[]{:S(2)}, u32[]{:S(2)}) collective-permute-start(bf16[8,3072]{1,0:T(8,128)(2,1)S(1)} %get-tuple-element.34), channel_id=1, source_target_pairs={{0,2},{1,3},{2,0},{3,1},{4,6},{5,7},{6,4},{7,5},{8,10},{9,11},{10,... | collective-permute-start | bytes 147464 | tf_op jit(solution)/shard_map/ppermute | solution.py:34
  12.3 3.5 %fetch.3.refs_4_.refs_8_ = bf16[8192,512]{1,0:T(8,128)(2,1)S(1)} custom-call(bf16[8192,512]{1,0:T(8,128)(2,1)} %refs_0_), custom_call_target="tpu_custom_call" | custom-call | bytes 16777216 | tf_op jit(solution)/shard_map/fetch/pallas_call | solution.py:272
  15.9 1.8 %collective-permute-start.5 = (bf16[16,3072]{1,0:T(8,128)(2,1)S(1)}, bf16[16,3072]{1,0:T(8,128)(2,1)S(1)}, u32[]{:S(2)}, u32[]{:S(2)}) collective-permute-start(bf16[16,3072]{1,0:T(8,128)(2,1)S(1)} %pad_maximum_fusion.2.refs_0_), channel_id=1, source_target_pairs={{0,8},{1,9},{2,10},{3,11},{4,12},{5,13},{6,14},{7,15},{8,0},{9,1},... | collective-permute-start | bytes 294920 | tf_op jit(solution)/shard_map/ppermute | solution.py:34
  17.7 2.5 %collective-permute-start.6 = (bf16[16,3072]{1,0:T(8,128)(2,1)S(1)}, bf16[16,3072]{1,0:T(8,128)(2,1)S(1)}, u32[]{:S(2)}, u32[]{:S(2)}) collective-permute-start(bf16[16,3072]{1,0:T(8,128)(2,1)S(1)} %pad_maximum_fusion.2.refs_0_), channel_id=1, source_target_pairs={{0,4},{1,5},{2,6},{3,7},{4,0},{5,1},{6,2},{7,3},{8,12},{9,13},{10,... | collective-permute-start | bytes 294920 | tf_op jit(solution)/shard_map/ppermute | solution.py:34
  20.6 2.0 %collective-permute-done.5.refs_1_ = bf16[16,3072]{1,0:T(8,128)(2,1)S(1)} collective-permute-done((bf16[16,3072]{1,0:T(8,128)(2,1)S(1)}, bf16[16,3072]{1,0:T(8,128)(2,1)S(1)}, u32[]{:S(2)}, u32[]{:S(2)}) %collective-permute-start.5) | collective-permute-done | bytes 98336 | tf_op jit(solution)/shard_map/ppermute | solution.py:34
  23.2 4.1 %collective-permute-done.7.refs_3_ = bf16[16,3072]{1,0:T(8,128)(2,1)S(1)} collective-permute-done((bf16[16,3072]{1,0:T(8,128)(2,1)S(1)}, bf16[16,3072]{1,0:T(8,128)(2,1)S(1)}, u32[]{:S(2)}, u32[]{:S(2)}) %collective-permute-start.7) | collective-permute-done | bytes 98336 | tf_op jit(solution)/shard_map/ppermute | solution.py:34
  30.9 1.7 %project.3 = bf16[256,640]{1,0:T(8,128)(2,1)} custom-call(bf16[16,3072]{1,0:T(8,128)(2,1)S(1)} %pad_maximum_fusion.2.refs_0_, bf16[16,3072]{1,0:T(8,128)(2,1)S(1)} %collective-permute-done.5.refs_1_, bf16[16,3072]{1,0:T(8,128)(2,1)S(1)} %collective-permute-done.6.refs_2_, bf16[16,3072]{1,0:T(8,128)(2,1)S(1)} %collective-permute-done.7.refs_3_, ...), custom_call_target="tpu_custom_call" | custom-call | flops 503316480 | bytes 3932160 | tf_op jit(solution)/shard_map/project/pallas_call | solution.py:350
  32.5 4.0 %all-to-all-start = ((bf16[16,16,640]{2,1,0:T(8,128)(2,1)}), bf16[16,16,640]{2,1,0:T(8,128)(2,1)S(1)}, u32[]{:S(2)}, u32[]{:S(2)}) async-start(bf16[16,16,640]{2,1,0:T(8,128)(2,1)} %bitcast.5), calls=%async_computation | async-start | bytes 655360 | tf_op jit(solution)/shard_map/all_to_all | solution.py:635
  36.9 1.6 %fetch.4.key_front = bf16[64,32,512]{2,1,0:T(8,128)(2,1)S(1)} custom-call(bf16[64,32,1024]{2,1,0:T(8,128)(2,1)} %bitcast.21), custom_call_target="tpu_custom_call" | custom-call | bytes 4194304 | tf_op jit(solution)/shard_map/fetch/pallas_call | solution.py:272
  40.3 7.4 %all-to-all-done.inbound = bf16[16,16,640]{2,1,0:T(8,128)(2,1)S(1)} async-done(((bf16[16,16,640]{2,1,0:T(8,128)(2,1)}), bf16[16,16,640]{2,1,0:T(8,128)(2,1)S(1)}, u32[]{:S(2)}, u32[]{:S(2)}) %all-to-all-start) | async-done | bytes 327712 | tf_op jit(solution)/shard_map/all_to_all | solution.py:635
  47.7 6.6 %attend.1 = bf16[16,16,512]{2,1,0:T(8,128)(2,1)} custom-call(s32[16,4]{1,0:T(8,128)S(1)} %copy.21.table, s32[2,1,128]{2,1,0:T(1,128)S(1)} %bitcast.19, bf16[16,16,640]{2,1,0:T(8,128)(2,1)S(1)} %all-to-all-done.inbound, f32[16,128]{1,0:T(8,128)S(1)} %pad_maximum_fusion.3.cosine, f32[16,128]{1,0:T(8,128)S(1)} %pad_maximum_fusion.4.sine, ...), custom_call_target="tpu_custom_call" | custom-call | flops 134217728 | bytes 8388608 | tf_op jit(solution)/shard_map/attend/pallas_call | solution.py:538
  54.3 3.5 %all-to-all-start.1 = ((bf16[16,16,512]{2,1,0:T(8,128)(2,1)}), bf16[16,16,512]{2,1,0:T(8,128)(2,1)S(1)}, u32[]{:S(2)}, u32[]{:S(2)}) async-start(bf16[16,16,512]{2,1,0:T(8,128)(2,1)} %attend.1), calls=%async_computation.1 | async-start | bytes 524288 | tf_op jit(solution)/shard_map/all_to_all | solution.py:651
  59.6 1.8 %fetch.5.w_front = bf16[512,2560]{1,0:T(8,128)(2,1)S(1)} custom-call(bf16[512,8192]{1,0:T(8,128)(2,1)} %w_out.1), custom_call_target="tpu_custom_call" | custom-call | bytes 5242880 | tf_op jit(solution)/shard_map/fetch/pallas_call | solution.py:272
  61.3 6.5 %all-to-all-done.1 = bf16[16,16,512]{2,1,0:T(8,128)(2,1)S(1)} async-done(((bf16[16,16,512]{2,1,0:T(8,128)(2,1)}), bf16[16,16,512]{2,1,0:T(8,128)(2,1)S(1)}, u32[]{:S(2)}, u32[]{:S(2)}) %all-to-all-start.1) | async-done | bytes 262176 | tf_op jit(solution)/shard_map/all_to_all | solution.py:651
  67.8 3.3 %product.1 = (bf16[64,4864]{1,0:T(8,128)(2,1)S(1)}, f32[64,4864]{1,0:T(8,128)S(1)}, bf16[64,3328]{1,0:T(8,128)(2,1)S(1)}, f32[64,3328]{1,0:T(8,128)S(1)}) custom-call(s32[1,128]{1,0:T(1,128)S(1)} %reshape_reshape.6.place_a, s32[1,128]{1,0:T(1,128)S(1)} %reshape_reshape.7.place_b, bf16[256,512]{1,0:T(8,128)(2,1)S(1)} %bitcast.17, bf16[512,8192]{1,0:T(8,128)(2,1)} %w_out.1, ...), custom_call_target="tpu_custom_call" | custom-call | flops 1073741824 | bytes 8388608 | tf_op jit(solution)/shard_map/product/pallas_call | solution.py:166
  71.2 2.0 %collective-permute-done.14 = bf16[64,4864]{1,0:T(8,128)(2,1)S(1)} collective-permute-done((bf16[64,4864]{1,0:T(8,128)(2,1)S(1)}, bf16[64,4864]{1,0:T(8,128)(2,1)S(1)}, u32[]{:S(2)}, u32[]{:S(2)}) %collective-permute-start.14) | collective-permute-done | bytes 622624 | tf_op jit(solution)/shard_map/ppermute | solution.py:34
  73.7 1.6 %collective-permute-done.16 = bf16[64,3328]{1,0:T(8,128)(2,1)S(1)} collective-permute-done((bf16[64,3328]{1,0:T(8,128)(2,1)S(1)}, bf16[64,3328]{1,0:T(8,128)(2,1)S(1)}, u32[]{:S(2)}, u32[]{:S(2)}) %collective-permute-start.16) | collective-permute-done | bytes 426016 | tf_op jit(solution)/shard_map/ppermute | solution.py:34
  77.7 3.6 %collective-permute-done.18 = bf16[16,3328]{1,0:T(8,128)(2,1)S(1)} collective-permute-done((bf16[16,3328]{1,0:T(8,128)(2,1)S(1)}, bf16[16,3328]{1,0:T(8,128)(2,1)S(1)}, u32[]{:S(2)}, u32[]{:S(2)}) %collective-permute-start.18) | collective-permute-done | bytes 106528 | tf_op jit(solution)/shard_map/ppermute | solution.py:34
  82.4 2.8 %collective-permute-done.15 = bf16[32,4864]{1,0:T(8,128)(2,1)S(1)} collective-permute-done((bf16[32,4864]{1,0:T(8,128)(2,1)S(1)}, bf16[32,4864]{1,0:T(8,128)(2,1)S(1)}, u32[]{:S(2)}, u32[]{:S(2)}) %collective-permute-start.15) | collective-permute-done | bytes 311328 | tf_op jit(solution)/shard_map/ppermute | solution.py:34
  85.1 2.8 %collective-permute-done.19 = bf16[16,3328]{1,0:T(8,128)(2,1)S(1)} collective-permute-done((bf16[16,3328]{1,0:T(8,128)(2,1)S(1)}, bf16[16,3328]{1,0:T(8,128)(2,1)S(1)}, u32[]{:S(2)}, u32[]{:S(2)}) %collective-permute-start.19) | collective-permute-done | bytes 106528 | tf_op jit(solution)/shard_map/ppermute | solution.py:34
  88.9 2.1 %collective-permute-start.21 = (bf16[8,4864]{1,0:T(8,128)(2,1)S(1)}, bf16[8,4864]{1,0:T(8,128)(2,1)S(1)}, u32[]{:S(2)}, u32[]{:S(2)}) collective-permute-start(bf16[8,4864]{1,0:T(8,128)(2,1)S(1)} %get-tuple-element.71), channel_id=1, source_target_pairs={{0,4},{1,5},{2,6},{3,7},{4,0},{5,1},{6,2},{7,3},{8,12},{9,13},{10,... | collective-permute-start | bytes 233480 | tf_op jit(solution)/shard_map/ppermute | solution.py:34
  90.9 2.3 %collective-permute-start.22 = (bf16[8,4864]{1,0:T(8,128)(2,1)S(1)}, bf16[8,4864]{1,0:T(8,128)(2,1)S(1)}, u32[]{:S(2)}, u32[]{:S(2)}) collective-permute-start(bf16[8,4864]{1,0:T(8,128)(2,1)S(1)} %get-tuple-element.70), channel_id=1, source_target_pairs={{0,12},{1,13},{2,14},{3,15},{4,8},{5,9},{6,10},{7,11},{8,4},{9,5},... | collective-permute-start | bytes 233480 | tf_op jit(solution)/shard_map/ppermute | solution.py:34
  93.2 2.4 %collective-permute-done.20 = bf16[8,4864]{1,0:T(8,128)(2,1)S(1)} collective-permute-done((bf16[8,4864]{1,0:T(8,128)(2,1)S(1)}, bf16[8,4864]{1,0:T(8,128)(2,1)S(1)}, u32[]{:S(2)}, u32[]{:S(2)}) %collective-permute-start.20) | collective-permute-done | bytes 77856 | tf_op jit(solution)/shard_map/ppermute | solution.py:34
  (92 shorter events, 21.9 us)
Async XLA Ops:
  1.9 14.0 %collective-permute-start = (bf16[8,5120]{1,0:T(8,128)(2,1)S(1)}, bf16[8,5120]{1,0:T(8,128)(2,1)S(1)}, u32[]{:S(2)}, u32[]{:S(2)}) collective-permute-start(bf16[8,5120]{1,0:T(8,128)(2,1)S(1)} %get-tuple-element.33), channel_id=1, source_target_pairs={{0,8},{1,9},{2,10},{3,11},{4,12},{5,13},{6,14},{7,15},{8,0},{9,1},... | collective-permute-start | bytes 245768 | tf_op jit(solution)/shard_map/ppermute | solution.py:34
  6.0 9.9 %collective-permute-start.1 = (bf16[8,5120]{1,0:T(8,128)(2,1)S(1)}, bf16[8,5120]{1,0:T(8,128)(2,1)S(1)}, u32[]{:S(2)}, u32[]{:S(2)}) collective-permute-start(bf16[8,5120]{1,0:T(8,128)(2,1)S(1)} %get-tuple-element.33), channel_id=1, source_target_pairs={{0,4},{1,5},{2,6},{3,7},{4,0},{5,1},{6,2},{7,3},{8,12},{9,13},{10,... | collective-permute-start | bytes 245768 | tf_op jit(solution)/shard_map/ppermute | solution.py:34
  7.5 8.3 %collective-permute-start.2 = (bf16[8,5120]{1,0:T(8,128)(2,1)S(1)}, bf16[8,5120]{1,0:T(8,128)(2,1)S(1)}, u32[]{:S(2)}, u32[]{:S(2)}) collective-permute-start(bf16[8,5120]{1,0:T(8,128)(2,1)S(1)} %get-tuple-element.33), channel_id=1, source_target_pairs={{0,12},{1,13},{2,14},{3,15},{4,8},{5,9},{6,10},{7,11},{8,4},{9,5},... | collective-permute-start | bytes 245768 | tf_op jit(solution)/shard_map/ppermute | solution.py:34
  7.5 8.3 %collective-permute-start.3 = (bf16[8,3072]{1,0:T(8,128)(2,1)S(1)}, bf16[8,3072]{1,0:T(8,128)(2,1)S(1)}, u32[]{:S(2)}, u32[]{:S(2)}) collective-permute-start(bf16[8,3072]{1,0:T(8,128)(2,1)S(1)} %get-tuple-element.34), channel_id=1, source_target_pairs={{0,2},{1,3},{2,0},{3,1},{4,6},{5,7},{6,4},{7,5},{8,10},{9,11},{10,... | collective-permute-start | bytes 147464 | tf_op jit(solution)/shard_map/ppermute | solution.py:34
  15.9 6.7 %collective-permute-start.5 = (bf16[16,3072]{1,0:T(8,128)(2,1)S(1)}, bf16[16,3072]{1,0:T(8,128)(2,1)S(1)}, u32[]{:S(2)}, u32[]{:S(2)}) collective-permute-start(bf16[16,3072]{1,0:T(8,128)(2,1)S(1)} %pad_maximum_fusion.2.refs_0_), channel_id=1, source_target_pairs={{0,8},{1,9},{2,10},{3,11},{4,12},{5,13},{6,14},{7,15},{8,0},{9,1},... | collective-permute-start | bytes 294920 | tf_op jit(solution)/shard_map/ppermute | solution.py:34
  17.7 5.5 %collective-permute-start.6 = (bf16[16,3072]{1,0:T(8,128)(2,1)S(1)}, bf16[16,3072]{1,0:T(8,128)(2,1)S(1)}, u32[]{:S(2)}, u32[]{:S(2)}) collective-permute-start(bf16[16,3072]{1,0:T(8,128)(2,1)S(1)} %pad_maximum_fusion.2.refs_0_), channel_id=1, source_target_pairs={{0,4},{1,5},{2,6},{3,7},{4,0},{5,1},{6,2},{7,3},{8,12},{9,13},{10,... | collective-permute-start | bytes 294920 | tf_op jit(solution)/shard_map/ppermute | solution.py:34
  20.1 7.8 %collective-permute-start.4 = (bf16[32,5120]{1,0:T(8,128)(2,1)S(1)}, bf16[32,5120]{1,0:T(8,128)(2,1)S(1)}, u32[]{:S(2)}, u32[]{:S(2)}) collective-permute-start(bf16[32,5120]{1,0:T(8,128)(2,1)S(1)} %pad_maximum_fusion.1.refs_0_), channel_id=1, source_target_pairs={{0,2},{1,3},{2,0},{3,1},{4,6},{5,7},{6,4},{7,5},{8,10},{9,11},{10,... | collective-permute-start | bytes 983048 | tf_op jit(solution)/shard_map/ppermute | solution.py:34
  20.6 8.3 %collective-permute-start.12 = (bf16[32,5120]{1,0:T(8,128)(2,1)S(1)}, bf16[32,5120]{1,0:T(8,128)(2,1)S(1)}, u32[]{:S(2)}, u32[]{:S(2)}) collective-permute-start(bf16[32,5120]{1,0:T(8,128)(2,1)S(1)} %pad_maximum_fusion.1.refs_0_), channel_id=1, source_target_pairs={{0,1},{1,0},{2,3},{3,2},{4,5},{5,4},{6,7},{7,6},{8,9},{9,8},{10,11... | collective-permute-start | bytes 983048 | tf_op jit(solution)/shard_map/ppermute | solution.py:34
  22.6 4.6 %collective-permute-start.7 = (bf16[16,3072]{1,0:T(8,128)(2,1)S(1)}, bf16[16,3072]{1,0:T(8,128)(2,1)S(1)}, u32[]{:S(2)}, u32[]{:S(2)}) collective-permute-start(bf16[16,3072]{1,0:T(8,128)(2,1)S(1)} %collective-permute-done.5.refs_1_), channel_id=1, source_target_pairs={{0,4},{1,5},{2,6},{3,7},{4,0},{5,1},{6,2},{7,3},{8,12},{9,13},{10,... | collective-permute-start | bytes 294920 | tf_op jit(solution)/shard_map/ppermute | solution.py:34
  27.9 2.9 %collective-permute-start.10 = (bf16[16,3072]{1,0:T(8,128)(2,1)S(1)}, bf16[16,3072]{1,0:T(8,128)(2,1)S(1)}, u32[]{:S(2)}, u32[]{:S(2)}) collective-permute-start(bf16[16,3072]{1,0:T(8,128)(2,1)S(1)} %collective-permute-done.6.refs_2_), channel_id=1, source_target_pairs={{0,1},{1,0},{2,3},{3,2},{4,5},{5,4},{6,7},{7,6},{8,9},{9,8},{10,11... | collective-permute-start | bytes 294920 | tf_op jit(solution)/shard_map/ppermute | solution.py:34
  28.4 2.4 %collective-permute-start.11 = (bf16[16,3072]{1,0:T(8,128)(2,1)S(1)}, bf16[16,3072]{1,0:T(8,128)(2,1)S(1)}, u32[]{:S(2)}, u32[]{:S(2)}) collective-permute-start(bf16[16,3072]{1,0:T(8,128)(2,1)S(1)} %collective-permute-done.7.refs_3_), channel_id=1, source_target_pairs={{0,1},{1,0},{2,3},{3,2},{4,5},{5,4},{6,7},{7,6},{8,9},{9,8},{10,11... | collective-permute-start | bytes 294920 | tf_op jit(solution)/shard_map/ppermute | solution.py:34
  28.4 2.4 %collective-permute-start.8 = (bf16[16,3072]{1,0:T(8,128)(2,1)S(1)}, bf16[16,3072]{1,0:T(8,128)(2,1)S(1)}, u32[]{:S(2)}, u32[]{:S(2)}) collective-permute-start(bf16[16,3072]{1,0:T(8,128)(2,1)S(1)} %pad_maximum_fusion.2.refs_0_), channel_id=1, source_target_pairs={{0,1},{1,0},{2,3},{3,2},{4,5},{5,4},{6,7},{7,6},{8,9},{9,8},{10,11... | collective-permute-start | bytes 294920 | tf_op jit(solution)/shard_map/ppermute | solution.py:34
  28.9 1.9 %collective-permute-start.9 = (bf16[16,3072]{1,0:T(8,128)(2,1)S(1)}, bf16[16,3072]{1,0:T(8,128)(2,1)S(1)}, u32[]{:S(2)}, u32[]{:S(2)}) collective-permute-start(bf16[16,3072]{1,0:T(8,128)(2,1)S(1)} %collective-permute-done.5.refs_1_), channel_id=1, source_target_pairs={{0,1},{1,0},{2,3},{3,2},{4,5},{5,4},{6,7},{7,6},{8,9},{9,8},{10,11... | collective-permute-start | bytes 294920 | tf_op jit(solution)/shard_map/ppermute | solution.py:34
  32.5 15.1 %all-to-all-start = ((bf16[16,16,640]{2,1,0:T(8,128)(2,1)}), bf16[16,16,640]{2,1,0:T(8,128)(2,1)S(1)}, u32[]{:S(2)}, u32[]{:S(2)}) async-start(bf16[16,16,640]{2,1,0:T(8,128)(2,1)} %bitcast.5), calls=%async_computation | async-start | bytes 655360 | tf_op jit(solution)/shard_map/all_to_all | solution.py:635
  54.3 13.6 %all-to-all-start.1 = ((bf16[16,16,512]{2,1,0:T(8,128)(2,1)}), bf16[16,16,512]{2,1,0:T(8,128)(2,1)S(1)}, u32[]{:S(2)}, u32[]{:S(2)}) async-start(bf16[16,16,512]{2,1,0:T(8,128)(2,1)} %attend.1), calls=%async_computation.1 | async-start | bytes 524288 | tf_op jit(solution)/shard_map/all_to_all | solution.py:651
  71.2 2.1 %collective-permute-start.14 = (bf16[64,4864]{1,0:T(8,128)(2,1)S(1)}, bf16[64,4864]{1,0:T(8,128)(2,1)S(1)}, u32[]{:S(2)}, u32[]{:S(2)}) collective-permute-start(bf16[64,4864]{1,0:T(8,128)(2,1)S(1)} %get-tuple-element.54), channel_id=1, source_target_pairs={{0,1},{1,0},{2,3},{3,2},{4,5},{5,4},{6,7},{7,6},{8,9},{9,8},{10,11... | collective-permute-start | bytes 1867784 | tf_op jit(solution)/shard_map/ppermute | solution.py:34
  75.4 5.9 %collective-permute-start.18 = (bf16[16,3328]{1,0:T(8,128)(2,1)S(1)}, bf16[16,3328]{1,0:T(8,128)(2,1)S(1)}, u32[]{:S(2)}, u32[]{:S(2)}) collective-permute-start(bf16[16,3328]{1,0:T(8,128)(2,1)S(1)} %get-tuple-element.67), channel_id=1, source_target_pairs={{0,4},{1,5},{2,6},{3,7},{4,0},{5,1},{6,2},{7,3},{8,12},{9,13},{10,... | collective-permute-start | bytes 319496 | tf_op jit(solution)/shard_map/ppermute | solution.py:34
  75.8 9.3 %collective-permute-start.15 = (bf16[32,4864]{1,0:T(8,128)(2,1)S(1)}, bf16[32,4864]{1,0:T(8,128)(2,1)S(1)}, u32[]{:S(2)}, u32[]{:S(2)}) collective-permute-start(bf16[32,4864]{1,0:T(8,128)(2,1)S(1)} %slice.82), channel_id=1, source_target_pairs={{0,2},{1,3},{2,0},{3,1},{4,6},{5,7},{6,4},{7,5},{8,10},{9,11},{10,... | collective-permute-start | bytes 933896 | tf_op jit(solution)/shard_map/ppermute | solution.py:34
  76.6 8.6 %collective-permute-start.17 = (bf16[16,3328]{1,0:T(8,128)(2,1)S(1)}, bf16[16,3328]{1,0:T(8,128)(2,1)S(1)}, u32[]{:S(2)}, u32[]{:S(2)}) collective-permute-start(bf16[16,3328]{1,0:T(8,128)(2,1)S(1)} %get-tuple-element.68), channel_id=1, source_target_pairs={{0,4},{1,5},{2,6},{3,7},{4,0},{5,1},{6,2},{7,3},{8,12},{9,13},{10,... | collective-permute-start | bytes 319496 | tf_op jit(solution)/shard_map/ppermute | solution.py:34
  81.3 6.6 %collective-permute-start.19 = (bf16[16,3328]{1,0:T(8,128)(2,1)S(1)}, bf16[16,3328]{1,0:T(8,128)(2,1)S(1)}, u32[]{:S(2)}, u32[]{:S(2)}) collective-permute-start(bf16[16,3328]{1,0:T(8,128)(2,1)S(1)} %fusion.2), channel_id=1, source_target_pairs={{0,8},{1,9},{2,10},{3,11},{4,12},{5,13},{6,14},{7,15},{8,0},{9,1},... | collective-permute-start | bytes 319496 | tf_op jit(solution)/shard_map/ppermute | solution.py:34
  88.1 5.2 %collective-permute-start.23 = (bf16[8,3328]{1,0:T(8,128)(2,1)S(1)}, bf16[8,3328]{1,0:T(8,128)(2,1)S(1)}, u32[]{:S(2)}, u32[]{:S(2)}) collective-permute-start(bf16[8,3328]{1,0:T(8,128)(2,1)S(1)} %slice.83), channel_id=1, source_target_pairs={{0,2},{1,3},{2,0},{3,1},{4,6},{5,7},{6,4},{7,5},{8,10},{9,11},{10,... | collective-permute-start | bytes 159752 | tf_op jit(solution)/shard_map/ppermute | solution.py:34
  88.8 6.9 %collective-permute-start.20 = (bf16[8,4864]{1,0:T(8,128)(2,1)S(1)}, bf16[8,4864]{1,0:T(8,128)(2,1)S(1)}, u32[]{:S(2)}, u32[]{:S(2)}) collective-permute-start(bf16[8,4864]{1,0:T(8,128)(2,1)S(1)} %get-tuple-element.69), channel_id=1, source_target_pairs={{0,8},{1,9},{2,10},{3,11},{4,12},{5,13},{6,14},{7,15},{8,0},{9,1},... | collective-permute-start | bytes 233480 | tf_op jit(solution)/shard_map/ppermute | solution.py:34
  88.9 6.8 %collective-permute-start.21 = (bf16[8,4864]{1,0:T(8,128)(2,1)S(1)}, bf16[8,4864]{1,0:T(8,128)(2,1)S(1)}, u32[]{:S(2)}, u32[]{:S(2)}) collective-permute-start(bf16[8,4864]{1,0:T(8,128)(2,1)S(1)} %get-tuple-element.71), channel_id=1, source_target_pairs={{0,4},{1,5},{2,6},{3,7},{4,0},{5,1},{6,2},{7,3},{8,12},{9,13},{10,... | collective-permute-start | bytes 233480 | tf_op jit(solution)/shard_map/ppermute | solution.py:34
  90.9 6.3 %collective-permute-start.22 = (bf16[8,4864]{1,0:T(8,128)(2,1)S(1)}, bf16[8,4864]{1,0:T(8,128)(2,1)S(1)}, u32[]{:S(2)}, u32[]{:S(2)}) collective-permute-start(bf16[8,4864]{1,0:T(8,128)(2,1)S(1)} %get-tuple-element.70), channel_id=1, source_target_pairs={{0,12},{1,13},{2,14},{3,15},{4,8},{5,9},{6,10},{7,11},{8,4},{9,5},... | collective-permute-start | bytes 233480 | tf_op jit(solution)/shard_map/ppermute | solution.py:34
  (10 other events, 52.8 us)

commit v11 on v10

--- a/solution.py
+++ b/solution.py
@@ -61,12 +61,6 @@
 
 def after(x, *earlier):
     return lax.optimization_barrier((x, *earlier))[0]
-
-
-def gather_line(grid, x):
-    crossed = [grid.send(x, half=d) for d in range(1, grid.half)]
-    crossed = crossed[0] if len(crossed) == 1 else jnp.concatenate(crossed, axis=0)
-    return [x, crossed, grid.send(x, pair=1), grid.send(crossed, pair=1)]
 
 
 def gather_rows(grid, xa, xb, first, second):
@@ -84,8 +78,13 @@
     pair_b = jnp.concatenate([xb, beside_b], axis=0)
     line_a, pair_b, first = lax.optimization_barrier((line_a, pair_b, first(xa)))
     beside_a = grid.send(line_a, near=1)
-    parts_b = gather_line(grid, pair_b)
-    beside_a, parts_b, second = lax.optimization_barrier((beside_a, parts_b, second(pair_b)))
+    parts_b = [pair_b] + [
+        grid.send(pair_b, half=half, pair=pair)
+        for pair in range(2)
+        for half in range(grid.half)
+        if half or pair
+    ]
+    beside_a, parts_b[1], second = lax.optimization_barrier((beside_a, parts_b[1], second(pair_b)))
     parts_a = [line_a, beside_a]
     parts_a += [grid.send(part, core=1) for part in parts_a]
     parts_b += [grid.send(part, core=1) for part in parts_b]
@@ -181,18 +180,6 @@
 
 
 def scatter_sum(grid, place_a, place_b, returned, w_out, w_front, cut):
-    def along_line(x):
-        size = x.shape[0] // 2 // grid.half
-        middle = x.shape[0] // 2
-        first = grid.send(narrow(x[middle + size :]), pair=1)
-        second = grid.send(narrow(x[middle : middle + size]), pair=1)
-        far = x[size:middle] + wide(first)
-        third = [
-            grid.send(narrow(far[d * size : (d + 1) * size]), half=d + 1)
-            for d in range(grid.half - 1)
-        ]
-        return x[:size], [second] + third
-
     def direct(x):
         size = x.shape[0] // 2 // grid.half
         parts = []
@@ -215,12 +202,13 @@
     sent_a = narrow(xa[middle:])
     got_a = grid.send(sent_a, near=1)
     xb = keep_b + wide(grid.send(after(away_b, sent_a), core=1))
-    xb, got_b = along_line(xb)
-    got_a, got_b = lax.optimization_barrier((got_a, got_b))
+    xb, got_b = direct(xb)
+    got_a, got_b[0] = lax.optimization_barrier((got_a, got_b[0]))
     xa, parts_a = direct(xa[:middle] + wide(got_a))
     xb = total(xb, got_b)
     middle = xb.shape[0] // 2
-    xb = xb[:middle] + wide(grid.send(narrow(xb[middle:]), near=1))
+    sent_b = after(narrow(xb[middle:]), parts_a[0])
+    xb = xb[:middle] + wide(grid.send(sent_b, near=1))
     xa = total(xa, parts_a)
     return jnp.concatenate([xa, xb], axis=1)
 
@@ -374,7 +362,6 @@
     sine,
     key_pages,
     value_pages,
-    key_front,
     out,
     key_pool,
     value_pool,
@@ -400,9 +387,7 @@
 
     cuts = 4
     size = key_pages.shape[0] // cuts
-    front = key_front.shape[2]
-    back = key_pages.at[:, :, pl.ds(front, kv_width - front)]
-    for i, (pool, on_chip) in enumerate(((back, key_pool), (value_pages, value_pool))):
+    for i, (pool, on_chip) in enumerate(((key_pages, key_pool), (value_pages, value_pool))):
         for cut in range(cuts):
             part = pl.ds(cut * size, size)
             pltpu.make_async_copy(pool.at[part], on_chip.at[part], sems.at[i]).start()
@@ -449,15 +434,11 @@
         jnp.int32, (columns, columns), 1
     )
 
+    pltpu.make_async_copy(key_pool, key_pool, sems.at[0]).wait()
     own_chances = {}
-    for p in range(pairs):
-        begin = p * 2 * HEAD
-        if begin == front:
-            pltpu.make_async_copy(key_pool, key_pool, sems.at[0]).wait()
-        source = key_front if begin < front else key_pool
-        inside = begin if begin < front else begin - front
-        for b in range(batches):
-            valid = row < lengths[b]
+    for b in range(batches):
+        valid = row < lengths[b]
+        for p in range(pairs):
             turned = query_rot[p, b].T.astype(jnp.bfloat16)
             none = jnp.zeros_like(turned)
             wide = jnp.concatenate(
@@ -466,7 +447,7 @@
             columns_p = slice(p * 2 * HEAD, (p + 1) * 2 * HEAD)
             keys = []
             for s in range(batch):
-                keys += held(source, b * batch + s, slice(inside, inside + 2 * HEAD))
+                keys += held(key_pool, b * batch + s, columns_p)
             keys.append(key_new[:, columns_p])
             products = jnp.dot(
                 jnp.concatenate(keys, axis=0), wide, preferred_element_type=jnp.float32
@@ -517,9 +498,7 @@
             ).astype(jnp.bfloat16)
 
 
-def attend(
-    inbound, lengths, table, cosine, sine, key_pages, value_pages, key_front, per_query, per_key
-):
+def attend(inbound, lengths, table, cosine, sine, key_pages, value_pages, per_query, per_key):
     owners, slots, _ = inbound.shape
     pages = table.shape[1]
     page, kv_width = key_pages.shape[1:]
@@ -537,11 +516,11 @@
     hbm = pl.BlockSpec(memory_space=pl.ANY)
     return pl.pallas_call(
         functools.partial(attend_kernel, per_query, per_key),
-        in_specs=[smem, vmem, vmem, vmem, vmem, hbm, hbm, vmem],
+        in_specs=[smem, vmem, vmem, vmem, vmem, hbm, hbm],
         out_specs=vmem,
         out_shape=jax.ShapeDtypeStruct((owners, slots, per_query), jnp.bfloat16),
         scratch_shapes=[
-            pltpu.VMEM(key_pages.shape[:2] + (kv_width - key_front.shape[2],), jnp.bfloat16),
+            pltpu.VMEM(key_pages.shape, jnp.bfloat16),
             pltpu.VMEM(value_pages.shape, jnp.bfloat16),
             pltpu.SemaphoreType.DMA((2,)),
             pltpu.VMEM((slots, kv_width), jnp.bfloat16),
@@ -557,7 +536,7 @@
             transcendentals=slots * heads * span,
         ),
         name="attend",
-    )(table, lengths, inbound, cosine, sine, key_pages, value_pages, key_front)
+    )(table, lengths, inbound, cosine, sine, key_pages, value_pages)
 
 
 def on_device(
@@ -601,19 +580,17 @@
 
     def first(x):
         place = placed(after(kv_owner, x))
-        place_in = reordered(place, grid.blocks(-1, ORDER_A))
-        (w,) = fetch((after(w_query, place_in), None), limit=44)
-        return w, place, place_in
-
-    def second(x):
         pieces = [after(w_key, x).T, w_value.T]
         spare = row_width - per_query - 2 * per_key
         if spare:
             pieces.append(jnp.zeros((spare, width), w_key.dtype))
-        return jnp.concatenate(pieces, axis=0)
-
-    parts_a, parts_b, others, w_kv_t = gather_rows(grid, xa, xb, first, second)
-    w_query, place, place_in = others
+        return place, reordered(place, grid.blocks(-1, ORDER_A)), jnp.concatenate(pieces, axis=0)
+
+    def second(x):
+        return fetch((after(w_query, x), None), limit=44)[0]
+
+    parts_a, parts_b, others, w_query = gather_rows(grid, xa, xb, first, second)
+    place, place_in, w_kv_t = others
     plain = list(range(owners))
     total = project(0, parts_a, plain, w_query, w_kv_t, None, None, all_slots)
     total = project(cut, parts_b, order_b, w_query, w_kv_t, total, place_in, all_slots)
@@ -633,8 +610,6 @@
     cosine = jnp.concatenate([cosine_part, cosine_part], axis=1)
     sine = jnp.concatenate([-sine_part, sine_part], axis=1)
     inbound = lax.all_to_all(outbound, AXES, split_axis=0, concat_axis=0, tiled=True)
-    kv_half = key_pages.shape[3] // 2
-    (key_front,) = fetch((after(key_pages, outbound)[0], (0, kv_half)), limit=51)
     attended = attend(
         inbound,
         lengths,
@@ -643,14 +618,13 @@
         sine,
         key_pages[0],
         value_pages[0],
-        key_front,
         per_query,
         per_key,
     )
     (w_front,) = fetch((after(w_out, attended), (0, width // 32 * 10)), limit=48)
     returned = lax.all_to_all(attended, AXES, split_axis=0, concat_axis=0, tiled=True)
     returned = returned.reshape(all_slots, per_query)
-    summed = scatter_sum(grid, place_a, place_b, returned, w_out, w_front, width // 32 * 19)
+    summed = scatter_sum(grid, place_a, place_b, returned, w_out, w_front, width // 32 * 21)
     return narrow(wide(hidden_in) + summed)
 
 

time: 98.6 us -> 101 us (1.024)
  starting transfers between devices: 29.8 us -> 33.6 us
  Pallas kernels: 20 us -> 17.3 us
  other arithmetic: 4.48 us -> 5.97 us
  waiting for transfers between devices: 38 us -> 39.4 us
  local copies, waits for them, and re-layouts: 5.33 us -> 4.01 us
    ppermute x24, starting transfers between devices: 22.3 us -> 26.2 us  [send(): return lax.ppermute(x, AXES, pairs)]
    all_to_all x1, waiting for transfers between devices: 7.37 us -> 10.3 us  [on_device(): lax.all_to_all(outbound, AXES, split_axis=0, concat_axis=0, tiled=True)]
    pallas_call x3 -> x2, Pallas kernels: 6.91 us -> 5.14 us  [fetch(): pl.pallas_call(functools.partial(fetch_kernel, starts), in_specs=[pl.Bloc...]
    ppermute x24, waiting for transfers between devices: 24.2 us -> 22.5 us  [send(): return lax.ppermute(x, AXES, pairs)]
    concatenate x1, other arithmetic: 0.18 us -> 1.68 us  [first(): jnp.concatenate(pieces, axis=0)]
    unnamed x16 -> x10, local copies, waits for them, and re-layouts: 3.03 us -> 1.68 us
  transfers between devices with their start and end apart: 26 -> 26, of which waited for: 13 -> 10; matrix products, arithmetic and copies ran while one was open for 6% -> 7% of each run, Pallas kernels for 8% -> 6%
where the time goes in v11:
time: 101 us
  waiting for transfers between devices  39.4 us (39%)
  starting transfers between devices  33.6 us (33%)
  Pallas kernels  17.3 us (17%)
  other arithmetic  5.97 us (6%)
  local copies, waits for them, and re-layouts  4.01 us (4%)
    ppermute x24, starting transfers between devices, send(): return lax.ppermute(x, AXES, pairs)  26.2 us
    ppermute x24, waiting for transfers between devices, send(): return lax.ppermute(x, AXES, pairs)  22.5 us
    all_to_all x1, waiting for transfers between devices, on_device(): lax.all_to_all(outbound, AXES, split_axis=0, concat_axis=0, tiled=True)  10.3 us
    all_to_all x1, waiting for transfers between devices, on_device(): lax.all_to_all(attended, AXES, split_axis=0, concat_axis=0, tiled=True)  6.5 us
    pallas_call x1, Pallas kernels, attend(): pl.pallas_call(functools.partial(attend_kernel, per_query, per_key), in_s...  5.97 us
    pallas_call x2, Pallas kernels, fetch(): pl.pallas_call(functools.partial(fetch_kernel, starts), in_specs=[pl.Bloc...  5.14 us
    all_to_all x1, starting transfers between devices, on_device(): lax.all_to_all(outbound, AXES, split_axis=0, concat_axis=0, tiled=True)  3.8 us
    all_to_all x1, starting transfers between devices, on_device(): lax.all_to_all(attended, AXES, split_axis=0, concat_axis=0, tiled=True)  3.54 us
  transfers between devices with their start and end apart: 26, of which 10 were waited for; matrix products, arithmetic and copies ran while one was open for 7% of the time, Pallas kernels for 6%

profile of v11, /device:TPU:0, one launch (start us, length us, event | category | flops | bytes accessed | tf_op | source)
XLA Modules:
  0.0 100.6 jit_solution(11602829346359304369)
XLA Ops:
  1.9 4.1 %collective-permute-start = (bf16[8,5120]{1,0:T(8,128)(2,1)S(1)}, bf16[8,5120]{1,0:T(8,128)(2,1)S(1)}, u32[]{:S(2)}, u32[]{:S(2)}) collective-permute-start(bf16[8,5120]{1,0:T(8,128)(2,1)S(1)} %get-tuple-element.29), channel_id=1, source_target_pairs={{0,8},{1,9},{2,10},{3,11},{4,12},{5,13},{6,14},{7,15},{8,0},{9,1},... | collective-permute-start | bytes 245768 | tf_op jit(solution)/shard_map/ppermute | solution.py:34
  6.0 1.6 %collective-permute-start.1 = (bf16[8,5120]{1,0:T(8,128)(2,1)S(1)}, bf16[8,5120]{1,0:T(8,128)(2,1)S(1)}, u32[]{:S(2)}, u32[]{:S(2)}) collective-permute-start(bf16[8,5120]{1,0:T(8,128)(2,1)S(1)} %get-tuple-element.29), channel_id=1, source_target_pairs={{0,4},{1,5},{2,6},{3,7},{4,0},{5,1},{6,2},{7,3},{8,12},{9,13},{10,... | collective-permute-start | bytes 245768 | tf_op jit(solution)/shard_map/ppermute | solution.py:34
  7.5 1.7 %collective-permute-start.3 = (bf16[8,3072]{1,0:T(8,128)(2,1)S(1)}, bf16[8,3072]{1,0:T(8,128)(2,1)S(1)}, u32[]{:S(2)}, u32[]{:S(2)}) collective-permute-start(bf16[8,3072]{1,0:T(8,128)(2,1)S(1)} %get-tuple-element.30), channel_id=1, source_target_pairs={{0,2},{1,3},{2,0},{3,1},{4,6},{5,7},{6,4},{7,5},{8,10},{9,11},{10,... | collective-permute-start | bytes 147464 | tf_op jit(solution)/shard_map/ppermute | solution.py:34
  11.8 1.7 %pad_maximum_fusion.refs_5_.refs_9_ = bf16[128,8192]{1,0:T(8,128)(2,1)S(1)} fusion(bf16[64,8192]{1,0:T(8,128)(2,1)} %bitcast.22, bf16[64,8192]{1,0:T(8,128)(2,1)} %bitcast.23), kind=kLoop, calls=%fused_computation | loop fusion | flops 4194304 | bytes 4194304 | tf_op jit(solution)/shard_map/concatenate | solution.py:587
  14.0 1.5 %collective-permute-start.4 = (bf16[32,5120]{1,0:T(8,128)(2,1)S(1)}, bf16[32,5120]{1,0:T(8,128)(2,1)S(1)}, u32[]{:S(2)}, u32[]{:S(2)}) collective-permute-start(bf16[32,5120]{1,0:T(8,128)(2,1)S(1)} %pad_maximum_fusion.1.refs_0_), channel_id=1, source_target_pairs={{0,2},{1,3},{2,0},{3,1},{4,6},{5,7},{6,4},{7,5},{8,10},{9,11},{10,... | collective-permute-start | bytes 983048 | tf_op jit(solution)/shard_map/ppermute | solution.py:34
  15.5 2.5 %collective-permute-start.5 = (bf16[16,3072]{1,0:T(8,128)(2,1)S(1)}, bf16[16,3072]{1,0:T(8,128)(2,1)S(1)}, u32[]{:S(2)}, u32[]{:S(2)}) collective-permute-start(bf16[16,3072]{1,0:T(8,128)(2,1)S(1)} %pad_maximum_fusion.2.refs_0_), channel_id=1, source_target_pairs={{0,8},{1,9},{2,10},{3,11},{4,12},{5,13},{6,14},{7,15},{8,0},{9,1},... | collective-permute-start | bytes 294920 | tf_op jit(solution)/shard_map/ppermute | solution.py:34
  17.9 3.4 %fetch.2.refs_4_.refs_8_ = bf16[8192,512]{1,0:T(8,128)(2,1)S(1)} custom-call(bf16[8192,512]{1,0:T(8,128)(2,1)} %refs_0_), custom_call_target="tpu_custom_call" | custom-call | bytes 16777216 | tf_op jit(solution)/shard_map/fetch/pallas_call | solution.py:260
  22.6 1.4 %collective-permute-start.6 = (bf16[16,3072]{1,0:T(8,128)(2,1)S(1)}, bf16[16,3072]{1,0:T(8,128)(2,1)S(1)}, u32[]{:S(2)}, u32[]{:S(2)}) collective-permute-start(bf16[16,3072]{1,0:T(8,128)(2,1)S(1)} %pad_maximum_fusion.2.refs_0_), channel_id=1, source_target_pairs={{0,4},{1,5},{2,6},{3,7},{4,0},{5,1},{6,2},{7,3},{8,12},{9,13},{10,... | collective-permute-start | bytes 294920 | tf_op jit(solution)/shard_map/ppermute | solution.py:34
  24.0 3.4 %collective-permute-start.7 = (bf16[16,3072]{1,0:T(8,128)(2,1)S(1)}, bf16[16,3072]{1,0:T(8,128)(2,1)S(1)}, u32[]{:S(2)}, u32[]{:S(2)}) collective-permute-start(bf16[16,3072]{1,0:T(8,128)(2,1)S(1)} %pad_maximum_fusion.2.refs_0_), channel_id=1, source_target_pairs={{0,12},{1,13},{2,14},{3,15},{4,8},{5,9},{6,10},{7,11},{8,4},{9,5},... | collective-permute-start | bytes 294920 | tf_op jit(solution)/shard_map/ppermute | solution.py:34
  27.9 4.8 %collective-permute-done.7.refs_3_ = bf16[16,3072]{1,0:T(8,128)(2,1)S(1)} collective-permute-done((bf16[16,3072]{1,0:T(8,128)(2,1)S(1)}, bf16[16,3072]{1,0:T(8,128)(2,1)S(1)}, u32[]{:S(2)}, u32[]{:S(2)}) %collective-permute-start.7) | collective-permute-done | bytes 98336 | tf_op jit(solution)/shard_map/ppermute | solution.py:34
  34.4 1.7 %project.3 = bf16[256,640]{1,0:T(8,128)(2,1)} custom-call(bf16[16,3072]{1,0:T(8,128)(2,1)S(1)} %pad_maximum_fusion.2.refs_0_, bf16[16,3072]{1,0:T(8,128)(2,1)S(1)} %collective-permute-done.5.refs_1_, bf16[16,3072]{1,0:T(8,128)(2,1)S(1)} %collective-permute-done.6.refs_2_, bf16[16,3072]{1,0:T(8,128)(2,1)S(1)} %collective-permute-done.7.refs_3_, ...), custom_call_target="tpu_custom_call" | custom-call | flops 503316480 | bytes 3932160 | tf_op jit(solution)/shard_map/project/pallas_call | solution.py:338
  36.1 3.8 %all-to-all-start = ((bf16[16,16,640]{2,1,0:T(8,128)(2,1)}), bf16[16,16,640]{2,1,0:T(8,128)(2,1)S(1)}, u32[]{:S(2)}, u32[]{:S(2)}) async-start(bf16[16,16,640]{2,1,0:T(8,128)(2,1)} %bitcast.5), calls=%async_computation | async-start | bytes 655360 | tf_op jit(solution)/shard_map/all_to_all | solution.py:612
  40.7 10.3 %all-to-all-done.inbound = bf16[16,16,640]{2,1,0:T(8,128)(2,1)S(1)} async-done(((bf16[16,16,640]{2,1,0:T(8,128)(2,1)}), bf16[16,16,640]{2,1,0:T(8,128)(2,1)S(1)}, u32[]{:S(2)}, u32[]{:S(2)}) %all-to-all-start) | async-done | bytes 327712 | tf_op jit(solution)/shard_map/all_to_all | solution.py:612
  51.0 6.0 %attend.1 = bf16[16,16,512]{2,1,0:T(8,128)(2,1)} custom-call(s32[16,4]{1,0:T(8,128)S(1)} %copy.21.table, s32[2,1,128]{2,1,0:T(1,128)S(1)} %bitcast.18, bf16[16,16,640]{2,1,0:T(8,128)(2,1)S(1)} %all-to-all-done.inbound, f32[16,128]{1,0:T(8,128)S(1)} %pad_maximum_fusion.3.cosine, f32[16,128]{1,0:T(8,128)S(1)} %pad_maximum_fusion.4.sine, ...), custom_call_target="tpu_custom_call" | custom-call | flops 134217728 | bytes 8388608 | tf_op jit(solution)/shard_map/attend/pallas_call | solution.py:517
  57.0 3.5 %all-to-all-start.1 = ((bf16[16,16,512]{2,1,0:T(8,128)(2,1)}), bf16[16,16,512]{2,1,0:T(8,128)(2,1)S(1)}, u32[]{:S(2)}, u32[]{:S(2)}) async-start(bf16[16,16,512]{2,1,0:T(8,128)(2,1)} %attend.1), calls=%async_computation.1 | async-start | bytes 524288 | tf_op jit(solution)/shard_map/all_to_all | solution.py:625
  62.3 1.8 %fetch.3.w_front = bf16[512,2560]{1,0:T(8,128)(2,1)S(1)} custom-call(bf16[512,8192]{1,0:T(8,128)(2,1)} %w_out.1), custom_call_target="tpu_custom_call" | custom-call | bytes 5242880 | tf_op jit(solution)/shard_map/fetch/pallas_call | solution.py:260
  64.0 6.5 %all-to-all-done.1 = bf16[16,16,512]{2,1,0:T(8,128)(2,1)S(1)} async-done(((bf16[16,16,512]{2,1,0:T(8,128)(2,1)}), bf16[16,16,512]{2,1,0:T(8,128)(2,1)S(1)}, u32[]{:S(2)}, u32[]{:S(2)}) %all-to-all-start.1) | async-done | bytes 262176 | tf_op jit(solution)/shard_map/all_to_all | solution.py:625
  70.5 3.2 %product.1 = (bf16[64,5376]{1,0:T(8,128)(2,1)S(1)}, f32[64,5376]{1,0:T(8,128)S(1)}, bf16[64,2816]{1,0:T(8,128)(2,1)S(1)}, f32[64,2816]{1,0:T(8,128)S(1)}) custom-call(s32[1,128]{1,0:T(1,128)S(1)} %reshape_reshape.6.place_a, s32[1,128]{1,0:T(1,128)S(1)} %reshape_reshape.7.place_b, bf16[256,512]{1,0:T(8,128)(2,1)S(1)} %bitcast.16, bf16[512,8192]{1,0:T(8,128)(2,1)} %w_out.1, ...), custom_call_target="tpu_custom_call" | custom-call | flops 1073741824 | bytes 8388608 | tf_op jit(solution)/shard_map/product/pallas_call | solution.py:165
  73.8 2.1 %collective-permute-done.14 = bf16[64,5376]{1,0:T(8,128)(2,1)S(1)} collective-permute-done((bf16[64,5376]{1,0:T(8,128)(2,1)S(1)}, bf16[64,5376]{1,0:T(8,128)(2,1)S(1)}, u32[]{:S(2)}, u32[]{:S(2)}) %collective-permute-start.14) | collective-permute-done | bytes 688160 | tf_op jit(solution)/shard_map/ppermute | solution.py:34
  79.6 2.9 %collective-permute-start.22 = (bf16[16,2816]{1,0:T(8,128)(2,1)S(1)}, bf16[16,2816]{1,0:T(8,128)(2,1)S(1)}, u32[]{:S(2)}, u32[]{:S(2)}) collective-permute-start(bf16[16,2816]{1,0:T(8,128)(2,1)S(1)} %get-tuple-element.60), channel_id=1, source_target_pairs={{0,12},{1,13},{2,14},{3,15},{4,8},{5,9},{6,10},{7,11},{8,4},{9,5},... | collective-permute-start | bytes 270344 | tf_op jit(solution)/shard_map/ppermute | solution.py:34
  82.4 4.2 %collective-permute-done.15 = bf16[32,5376]{1,0:T(8,128)(2,1)S(1)} collective-permute-done((bf16[32,5376]{1,0:T(8,128)(2,1)S(1)}, bf16[32,5376]{1,0:T(8,128)(2,1)S(1)}, u32[]{:S(2)}, u32[]{:S(2)}) %collective-permute-start.15) | collective-permute-done | bytes 344096 | tf_op jit(solution)/shard_map/ppermute | solution.py:34
  88.6 2.6 %collective-permute-start.20 = (bf16[8,5376]{1,0:T(8,128)(2,1)S(1)}, bf16[8,5376]{1,0:T(8,128)(2,1)S(1)}, u32[]{:S(2)}, u32[]{:S(2)}) collective-permute-start(bf16[8,5376]{1,0:T(8,128)(2,1)S(1)} %get-tuple-element.63), channel_id=1, source_target_pairs={{0,12},{1,13},{2,14},{3,15},{4,8},{5,9},{6,10},{7,11},{8,4},{9,5},... | collective-permute-start | bytes 258056 | tf_op jit(solution)/shard_map/ppermute | solution.py:34
  91.3 4.5 %collective-permute-done.18 = bf16[8,5376]{1,0:T(8,128)(2,1)S(1)} collective-permute-done((bf16[8,5376]{1,0:T(8,128)(2,1)S(1)}, bf16[8,5376]{1,0:T(8,128)(2,1)S(1)}, u32[]{:S(2)}, u32[]{:S(2)}) %collective-permute-start.18) | collective-permute-done | bytes 86048 | tf_op jit(solution)/shard_map/ppermute | solution.py:34
  95.9 4.0 %collective-permute-done.23 = bf16[8,2816]{1,0:T(8,128)(2,1)S(1)} collective-permute-done((bf16[8,2816]{1,0:T(8,128)(2,1)S(1)}, bf16[8,2816]{1,0:T(8,128)(2,1)S(1)}, u32[]{:S(2)}, u32[]{:S(2)}) %collective-permute-start.23) | collective-permute-done | bytes 45088 | tf_op jit(solution)/shard_map/ppermute | solution.py:34
  (84 shorter events, 17.2 us)
Async XLA Ops:
  1.9 12.1 %collective-permute-start = (bf16[8,5120]{1,0:T(8,128)(2,1)S(1)}, bf16[8,5120]{1,0:T(8,128)(2,1)S(1)}, u32[]{:S(2)}, u32[]{:S(2)}) collective-permute-start(bf16[8,5120]{1,0:T(8,128)(2,1)S(1)} %get-tuple-element.29), channel_id=1, source_target_pairs={{0,8},{1,9},{2,10},{3,11},{4,12},{5,13},{6,14},{7,15},{8,0},{9,1},... | collective-permute-start | bytes 245768 | tf_op jit(solution)/shard_map/ppermute | solution.py:34
  6.0 8.0 %collective-permute-start.1 = (bf16[8,5120]{1,0:T(8,128)(2,1)S(1)}, bf16[8,5120]{1,0:T(8,128)(2,1)S(1)}, u32[]{:S(2)}, u32[]{:S(2)}) collective-permute-start(bf16[8,5120]{1,0:T(8,128)(2,1)S(1)} %get-tuple-element.29), channel_id=1, source_target_pairs={{0,4},{1,5},{2,6},{3,7},{4,0},{5,1},{6,2},{7,3},{8,12},{9,13},{10,... | collective-permute-start | bytes 245768 | tf_op jit(solution)/shard_map/ppermute | solution.py:34
  7.5 6.4 %collective-permute-start.2 = (bf16[8,5120]{1,0:T(8,128)(2,1)S(1)}, bf16[8,5120]{1,0:T(8,128)(2,1)S(1)}, u32[]{:S(2)}, u32[]{:S(2)}) collective-permute-start(bf16[8,5120]{1,0:T(8,128)(2,1)S(1)} %get-tuple-element.29), channel_id=1, source_target_pairs={{0,12},{1,13},{2,14},{3,15},{4,8},{5,9},{6,10},{7,11},{8,4},{9,5},... | collective-permute-start | bytes 245768 | tf_op jit(solution)/shard_map/ppermute | solution.py:34
  7.5 6.4 %collective-permute-start.3 = (bf16[8,3072]{1,0:T(8,128)(2,1)S(1)}, bf16[8,3072]{1,0:T(8,128)(2,1)S(1)}, u32[]{:S(2)}, u32[]{:S(2)}) collective-permute-start(bf16[8,3072]{1,0:T(8,128)(2,1)S(1)} %get-tuple-element.30), channel_id=1, source_target_pairs={{0,2},{1,3},{2,0},{3,1},{4,6},{5,7},{6,4},{7,5},{8,10},{9,11},{10,... | collective-permute-start | bytes 147464 | tf_op jit(solution)/shard_map/ppermute | solution.py:34
  14.0 8.6 %collective-permute-start.4 = (bf16[32,5120]{1,0:T(8,128)(2,1)S(1)}, bf16[32,5120]{1,0:T(8,128)(2,1)S(1)}, u32[]{:S(2)}, u32[]{:S(2)}) collective-permute-start(bf16[32,5120]{1,0:T(8,128)(2,1)S(1)} %pad_maximum_fusion.1.refs_0_), channel_id=1, source_target_pairs={{0,2},{1,3},{2,0},{3,1},{4,6},{5,7},{6,4},{7,5},{8,10},{9,11},{10,... | collective-permute-start | bytes 983048 | tf_op jit(solution)/shard_map/ppermute | solution.py:34
  15.5 7.1 %collective-permute-start.5 = (bf16[16,3072]{1,0:T(8,128)(2,1)S(1)}, bf16[16,3072]{1,0:T(8,128)(2,1)S(1)}, u32[]{:S(2)}, u32[]{:S(2)}) collective-permute-start(bf16[16,3072]{1,0:T(8,128)(2,1)S(1)} %pad_maximum_fusion.2.refs_0_), channel_id=1, source_target_pairs={{0,8},{1,9},{2,10},{3,11},{4,12},{5,13},{6,14},{7,15},{8,0},{9,1},... | collective-permute-start | bytes 294920 | tf_op jit(solution)/shard_map/ppermute | solution.py:34
  17.9 14.7 %collective-permute-start.12 = (bf16[32,5120]{1,0:T(8,128)(2,1)S(1)}, bf16[32,5120]{1,0:T(8,128)(2,1)S(1)}, u32[]{:S(2)}, u32[]{:S(2)}) collective-permute-start(bf16[32,5120]{1,0:T(8,128)(2,1)S(1)} %pad_maximum_fusion.1.refs_0_), channel_id=1, source_target_pairs={{0,1},{1,0},{2,3},{3,2},{4,5},{5,4},{6,7},{7,6},{8,9},{9,8},{10,11... | collective-permute-start | bytes 983048 | tf_op jit(solution)/shard_map/ppermute | solution.py:34
  22.6 10.6 %collective-permute-start.13 = (bf16[32,5120]{1,0:T(8,128)(2,1)S(1)}, bf16[32,5120]{1,0:T(8,128)(2,1)S(1)}, u32[]{:S(2)}, u32[]{:S(2)}) collective-permute-start(bf16[32,5120]{1,0:T(8,128)(2,1)S(1)} %collective-permute-done.4.refs_1_), channel_id=1, source_target_pairs={{0,1},{1,0},{2,3},{3,2},{4,5},{5,4},{6,7},{7,6},{8,9},{9,8},{10,11... | collective-permute-start | bytes 983048 | tf_op jit(solution)/shard_map/ppermute | solution.py:34
  22.6 5.2 %collective-permute-start.6 = (bf16[16,3072]{1,0:T(8,128)(2,1)S(1)}, bf16[16,3072]{1,0:T(8,128)(2,1)S(1)}, u32[]{:S(2)}, u32[]{:S(2)}) collective-permute-start(bf16[16,3072]{1,0:T(8,128)(2,1)S(1)} %pad_maximum_fusion.2.refs_0_), channel_id=1, source_target_pairs={{0,4},{1,5},{2,6},{3,7},{4,0},{5,1},{6,2},{7,3},{8,12},{9,13},{10,... | collective-permute-start | bytes 294920 | tf_op jit(solution)/shard_map/ppermute | solution.py:34
  24.0 8.7 %collective-permute-start.7 = (bf16[16,3072]{1,0:T(8,128)(2,1)S(1)}, bf16[16,3072]{1,0:T(8,128)(2,1)S(1)}, u32[]{:S(2)}, u32[]{:S(2)}) collective-permute-start(bf16[16,3072]{1,0:T(8,128)(2,1)S(1)} %pad_maximum_fusion.2.refs_0_), channel_id=1, source_target_pairs={{0,12},{1,13},{2,14},{3,15},{4,8},{5,9},{6,10},{7,11},{8,4},{9,5},... | collective-permute-start | bytes 294920 | tf_op jit(solution)/shard_map/ppermute | solution.py:34
  27.3 7.0 %collective-permute-start.8 = (bf16[16,3072]{1,0:T(8,128)(2,1)S(1)}, bf16[16,3072]{1,0:T(8,128)(2,1)S(1)}, u32[]{:S(2)}, u32[]{:S(2)}) collective-permute-start(bf16[16,3072]{1,0:T(8,128)(2,1)S(1)} %pad_maximum_fusion.2.refs_0_), channel_id=1, source_target_pairs={{0,1},{1,0},{2,3},{3,2},{4,5},{5,4},{6,7},{7,6},{8,9},{9,8},{10,11... | collective-permute-start | bytes 294920 | tf_op jit(solution)/shard_map/ppermute | solution.py:34
  27.8 6.6 %collective-permute-start.10 = (bf16[16,3072]{1,0:T(8,128)(2,1)S(1)}, bf16[16,3072]{1,0:T(8,128)(2,1)S(1)}, u32[]{:S(2)}, u32[]{:S(2)}) collective-permute-start(bf16[16,3072]{1,0:T(8,128)(2,1)S(1)} %collective-permute-done.6.refs_2_), channel_id=1, source_target_pairs={{0,1},{1,0},{2,3},{3,2},{4,5},{5,4},{6,7},{7,6},{8,9},{9,8},{10,11... | collective-permute-start | bytes 294920 | tf_op jit(solution)/shard_map/ppermute | solution.py:34
  36.1 14.9 %all-to-all-start = ((bf16[16,16,640]{2,1,0:T(8,128)(2,1)}), bf16[16,16,640]{2,1,0:T(8,128)(2,1)S(1)}, u32[]{:S(2)}, u32[]{:S(2)}) async-start(bf16[16,16,640]{2,1,0:T(8,128)(2,1)} %bitcast.5), calls=%async_computation | async-start | bytes 655360 | tf_op jit(solution)/shard_map/all_to_all | solution.py:612
  57.0 13.6 %all-to-all-start.1 = ((bf16[16,16,512]{2,1,0:T(8,128)(2,1)}), bf16[16,16,512]{2,1,0:T(8,128)(2,1)S(1)}, u32[]{:S(2)}, u32[]{:S(2)}) async-start(bf16[16,16,512]{2,1,0:T(8,128)(2,1)} %attend.1), calls=%async_computation.1 | async-start | bytes 524288 | tf_op jit(solution)/shard_map/all_to_all | solution.py:625
  73.7 2.2 %collective-permute-start.14 = (bf16[64,5376]{1,0:T(8,128)(2,1)S(1)}, bf16[64,5376]{1,0:T(8,128)(2,1)S(1)}, u32[]{:S(2)}, u32[]{:S(2)}) collective-permute-start(bf16[64,5376]{1,0:T(8,128)(2,1)S(1)} %get-tuple-element.46), channel_id=1, source_target_pairs={{0,1},{1,0},{2,3},{3,2},{4,5},{5,4},{6,7},{7,6},{8,9},{9,8},{10,11... | collective-permute-start | bytes 2064392 | tf_op jit(solution)/shard_map/ppermute | solution.py:34
  76.1 1.7 %collective-permute-start.16 = (bf16[64,2816]{1,0:T(8,128)(2,1)S(1)}, bf16[64,2816]{1,0:T(8,128)(2,1)S(1)}, u32[]{:S(2)}, u32[]{:S(2)}) collective-permute-start(bf16[64,2816]{1,0:T(8,128)(2,1)S(1)} %get-tuple-element.49), channel_id=1, source_target_pairs={{0,1},{1,0},{2,3},{3,2},{4,5},{5,4},{6,7},{7,6},{8,9},{9,8},{10,11... | collective-permute-start | bytes 1081352 | tf_op jit(solution)/shard_map/ppermute | solution.py:34
  76.3 10.3 %collective-permute-start.15 = (bf16[32,5376]{1,0:T(8,128)(2,1)S(1)}, bf16[32,5376]{1,0:T(8,128)(2,1)S(1)}, u32[]{:S(2)}, u32[]{:S(2)}) collective-permute-start(bf16[32,5376]{1,0:T(8,128)(2,1)S(1)} %slice.82), channel_id=1, source_target_pairs={{0,2},{1,3},{2,0},{3,1},{4,6},{5,7},{6,4},{7,5},{8,10},{9,11},{10,... | collective-permute-start | bytes 1032200 | tf_op jit(solution)/shard_map/ppermute | solution.py:34
  78.0 8.7 %collective-permute-start.17 = (bf16[16,2816]{1,0:T(8,128)(2,1)S(1)}, bf16[16,2816]{1,0:T(8,128)(2,1)S(1)}, u32[]{:S(2)}, u32[]{:S(2)}) collective-permute-start(bf16[16,2816]{1,0:T(8,128)(2,1)S(1)} %get-tuple-element.59), channel_id=1, source_target_pairs={{0,8},{1,9},{2,10},{3,11},{4,12},{5,13},{6,14},{7,15},{8,0},{9,1},... | collective-permute-start | bytes 270344 | tf_op jit(solution)/shard_map/ppermute | solution.py:34
  79.1 12.2 %collective-permute-start.21 = (bf16[16,2816]{1,0:T(8,128)(2,1)S(1)}, bf16[16,2816]{1,0:T(8,128)(2,1)S(1)}, u32[]{:S(2)}, u32[]{:S(2)}) collective-permute-start(bf16[16,2816]{1,0:T(8,128)(2,1)S(1)} %get-tuple-element.61), channel_id=1, source_target_pairs={{0,4},{1,5},{2,6},{3,7},{4,0},{5,1},{6,2},{7,3},{8,12},{9,13},{10,... | collective-permute-start | bytes 270344 | tf_op jit(solution)/shard_map/ppermute | solution.py:34
  79.6 11.7 %collective-permute-start.22 = (bf16[16,2816]{1,0:T(8,128)(2,1)S(1)}, bf16[16,2816]{1,0:T(8,128)(2,1)S(1)}, u32[]{:S(2)}, u32[]{:S(2)}) collective-permute-start(bf16[16,2816]{1,0:T(8,128)(2,1)S(1)} %get-tuple-element.60), channel_id=1, source_target_pairs={{0,12},{1,13},{2,14},{3,15},{4,8},{5,9},{6,10},{7,11},{8,4},{9,5},... | collective-permute-start | bytes 270344 | tf_op jit(solution)/shard_map/ppermute | solution.py:34
  86.8 9.0 %collective-permute-start.18 = (bf16[8,5376]{1,0:T(8,128)(2,1)S(1)}, bf16[8,5376]{1,0:T(8,128)(2,1)S(1)}, u32[]{:S(2)}, u32[]{:S(2)}) collective-permute-start(bf16[8,5376]{1,0:T(8,128)(2,1)S(1)} %get-tuple-element.64), channel_id=1, source_target_pairs={{0,8},{1,9},{2,10},{3,11},{4,12},{5,13},{6,14},{7,15},{8,0},{9,1},... | collective-permute-start | bytes 258056 | tf_op jit(solution)/shard_map/ppermute | solution.py:34
  87.9 8.0 %collective-permute-start.19 = (bf16[8,5376]{1,0:T(8,128)(2,1)S(1)}, bf16[8,5376]{1,0:T(8,128)(2,1)S(1)}, u32[]{:S(2)}, u32[]{:S(2)}) collective-permute-start(bf16[8,5376]{1,0:T(8,128)(2,1)S(1)} %get-tuple-element.62), channel_id=1, source_target_pairs={{0,4},{1,5},{2,6},{3,7},{4,0},{5,1},{6,2},{7,3},{8,12},{9,13},{10,... | collective-permute-start | bytes 258056 | tf_op jit(solution)/shard_map/ppermute | solution.py:34
  88.6 7.2 %collective-permute-start.20 = (bf16[8,5376]{1,0:T(8,128)(2,1)S(1)}, bf16[8,5376]{1,0:T(8,128)(2,1)S(1)}, u32[]{:S(2)}, u32[]{:S(2)}) collective-permute-start(bf16[8,5376]{1,0:T(8,128)(2,1)S(1)} %get-tuple-element.63), channel_id=1, source_target_pairs={{0,12},{1,13},{2,14},{3,15},{4,8},{5,9},{6,10},{7,11},{8,4},{9,5},... | collective-permute-start | bytes 258056 | tf_op jit(solution)/shard_map/ppermute | solution.py:34
  95.8 4.0 %collective-permute-start.23 = (bf16[8,2816]{1,0:T(8,128)(2,1)S(1)}, bf16[8,2816]{1,0:T(8,128)(2,1)S(1)}, u32[]{:S(2)}, u32[]{:S(2)}) collective-permute-start(bf16[8,2816]{1,0:T(8,128)(2,1)S(1)} %slice.83), channel_id=1, source_target_pairs={{0,2},{1,3},{2,0},{3,1},{4,6},{5,7},{6,4},{7,5},{8,10},{9,11},{10,... | collective-permute-start | bytes 135176 | tf_op jit(solution)/shard_map/ppermute | solution.py:34
  (7 other events, 38.5 us)

commit v12 on v11

--- a/solution.py
+++ b/solution.py
@@ -84,7 +84,7 @@
         for half in range(grid.half)
         if half or pair
     ]
-    beside_a, parts_b[1], second = lax.optimization_barrier((beside_a, parts_b[1], second(pair_b)))
+    beside_a, parts_b, second = lax.optimization_barrier((beside_a, parts_b, second(pair_b)))
     parts_a = [line_a, beside_a]
     parts_a += [grid.send(part, core=1) for part in parts_a]
     parts_b += [grid.send(part, core=1) for part in parts_b]
@@ -180,6 +180,18 @@
 
 
 def scatter_sum(grid, place_a, place_b, returned, w_out, w_front, cut):
+    def along_line(x):
+        size = x.shape[0] // 2 // grid.half
+        middle = x.shape[0] // 2
+        first = grid.send(narrow(x[middle + size :]), pair=1)
+        second = grid.send(after(narrow(x[middle : middle + size]), first), pair=1)
+        far = x[size:middle] + wide(first)
+        third = [
+            grid.send(narrow(far[d * size : (d + 1) * size]), half=d + 1)
+            for d in range(grid.half - 1)
+        ]
+        return x[:size], [second] + third
+
     def direct(x):
         size = x.shape[0] // 2 // grid.half
         parts = []
@@ -202,13 +214,12 @@
     sent_a = narrow(xa[middle:])
     got_a = grid.send(sent_a, near=1)
     xb = keep_b + wide(grid.send(after(away_b, sent_a), core=1))
-    xb, got_b = direct(xb)
-    got_a, got_b[0] = lax.optimization_barrier((got_a, got_b[0]))
+    xb, got_b = along_line(xb)
+    got_a, got_b = lax.optimization_barrier((got_a, got_b))
     xa, parts_a = direct(xa[:middle] + wide(got_a))
     xb = total(xb, got_b)
     middle = xb.shape[0] // 2
-    sent_b = after(narrow(xb[middle:]), parts_a[0])
-    xb = xb[:middle] + wide(grid.send(sent_b, near=1))
+    xb = xb[:middle] + wide(grid.send(narrow(xb[middle:]), near=1))
     xa = total(xa, parts_a)
     return jnp.concatenate([xa, xb], axis=1)
 
@@ -385,12 +396,13 @@
     batches = query_rot.shape[1]
     batch = slots // batches
 
-    cuts = 4
-    size = key_pages.shape[0] // cuts
+    width = kv_width // 2
+    copies = []
     for i, (pool, on_chip) in enumerate(((key_pages, key_pool), (value_pages, value_pool))):
-        for cut in range(cuts):
-            part = pl.ds(cut * size, size)
-            pltpu.make_async_copy(pool.at[part], on_chip.at[part], sems.at[i]).start()
+        for half in range(2):
+            part = pool.at[:, :, pl.ds(half * width, width)]
+            copies.append(pltpu.make_async_copy(part, on_chip.at[half], sems.at[i, half]))
+            copies[-1].start()
 
     def held(pool, slot, columns):
         return [pool[table[slot, j], :, columns] for j in range(pages)]
@@ -434,21 +446,23 @@
         jnp.int32, (columns, columns), 1
     )
 
-    pltpu.make_async_copy(key_pool, key_pool, sems.at[0]).wait()
     own_chances = {}
-    for b in range(batches):
-        valid = row < lengths[b]
-        for p in range(pairs):
+    for p in range(pairs):
+        half, inside = divmod(p * 2 * HEAD, width)
+        columns_p = slice(inside, inside + 2 * HEAD)
+        if inside == 0:
+            copies[half].wait()
+        for b in range(batches):
+            valid = row < lengths[b]
             turned = query_rot[p, b].T.astype(jnp.bfloat16)
             none = jnp.zeros_like(turned)
             wide = jnp.concatenate(
                 [jnp.where(first, turned, none), jnp.where(first, none, turned)], axis=0
             )
-            columns_p = slice(p * 2 * HEAD, (p + 1) * 2 * HEAD)
             keys = []
             for s in range(batch):
-                keys += held(key_pool, b * batch + s, columns_p)
-            keys.append(key_new[:, columns_p])
+                keys += held(key_pool.at[half], b * batch + s, columns_p)
+            keys.append(key_new[:, p * 2 * HEAD : (p + 1) * 2 * HEAD])
             products = jnp.dot(
                 jnp.concatenate(keys, axis=0), wide, preferred_element_type=jnp.float32
             )
@@ -468,13 +482,15 @@
                 jnp.where(same, own_chance, 0.0), axis=1, keepdims=True
             )
 
-    pltpu.make_async_copy(value_pool, value_pool, sems.at[1]).wait()
-    for b in range(batches):
-        for s in range(batch):
-            for p in range(pairs):
+    for p in range(pairs):
+        half, inside = divmod(p * 2 * HEAD, width)
+        columns_p = slice(inside, inside + 2 * HEAD)
+        if inside == 0:
+            copies[2 + half].wait()
+        for b in range(batches):
+            for s in range(batch):
                 mine = chance[p, b, pl.ds(s, pair, stride=batch)].astype(jnp.bfloat16)
-                columns_p = slice(p * 2 * HEAD, (p + 1) * 2 * HEAD)
-                values = held(value_pool, b * batch + s, columns_p)
+                values = held(value_pool.at[half], b * batch + s, columns_p)
                 both = jnp.dot(
                     mine, jnp.concatenate(values, axis=0), preferred_element_type=jnp.float32
                 )
@@ -482,8 +498,6 @@
                     [both[: pair // 2, :HEAD], both[pair // 2 :, HEAD:]], axis=0
                 )
                 mixed[p, b, pl.ds(s, pair, stride=batch)] = result
-
-    for p in range(pairs):
         for j in range(pair):
             head = p * pair + j
             g = head * kv_heads // heads
@@ -520,9 +534,9 @@
         out_specs=vmem,
         out_shape=jax.ShapeDtypeStruct((owners, slots, per_query), jnp.bfloat16),
         scratch_shapes=[
-            pltpu.VMEM(key_pages.shape, jnp.bfloat16),
-            pltpu.VMEM(value_pages.shape, jnp.bfloat16),
-            pltpu.SemaphoreType.DMA((2,)),
+            pltpu.VMEM((2, *key_pages.shape[:2], kv_width // 2), jnp.bfloat16),
+            pltpu.VMEM((2, *key_pages.shape[:2], kv_width // 2), jnp.bfloat16),
+            pltpu.SemaphoreType.DMA((2, 2)),
             pltpu.VMEM((slots, kv_width), jnp.bfloat16),
             pltpu.VMEM((pairs, batches, columns, HEAD), jnp.float32),
             pltpu.VMEM((kv_heads, slots, HEAD), jnp.float32),
@@ -624,7 +638,7 @@
     (w_front,) = fetch((after(w_out, attended), (0, width // 32 * 10)), limit=48)
     returned = lax.all_to_all(attended, AXES, split_axis=0, concat_axis=0, tiled=True)
     returned = returned.reshape(all_slots, per_query)
-    summed = scatter_sum(grid, place_a, place_b, returned, w_out, w_front, width // 32 * 21)
+    summed = scatter_sum(grid, place_a, place_b, returned, w_out, w_front, width // 32 * 19)
     return narrow(wide(hidden_in) + summed)
 
 

time: 101 us -> 96.3 us (0.953)
  starting transfers between devices: 33.6 us -> 30.5 us
  waiting for transfers between devices: 39.4 us -> 37.4 us
    ppermute x24, starting transfers between devices: 26.2 us -> 22.7 us  [send(): return lax.ppermute(x, AXES, pairs)]
    ppermute x24, waiting for transfers between devices: 22.5 us -> 20.6 us  [send(): return lax.ppermute(x, AXES, pairs)]
  transfers between devices with their start and end apart: 26 -> 26, of which waited for: 10 -> 12; matrix products, arithmetic and copies ran while one was open for 7% -> 7% of each run, Pallas kernels for 6% -> 7%
where the time goes in v12:
time: 96.3 us; the launch traced here: 95.7 us
  waiting for transfers between devices  37.4 us (39%)
  starting transfers between devices  30.5 us (32%)
  Pallas kernels  17.5 us (18%)
  other arithmetic  5.96 us (6%)
  local copies, waits for them, and re-layouts  4 us (4%)
    ppermute x24, starting transfers between devices, send(): return lax.ppermute(x, AXES, pairs)  22.7 us
    ppermute x24, waiting for transfers between devices, send(): return lax.ppermute(x, AXES, pairs)  20.6 us
    all_to_all x1, waiting for transfers between devices, on_device(): lax.all_to_all(outbound, AXES, split_axis=0, concat_axis=0, tiled=True)  10.3 us
    all_to_all x1, waiting for transfers between devices, on_device(): lax.all_to_all(attended, AXES, split_axis=0, concat_axis=0, tiled=True)  6.5 us
    pallas_call x1, Pallas kernels, attend(): pl.pallas_call(functools.partial(attend_kernel, per_query, per_key), in_s...  5.97 us
    pallas_call x2, Pallas kernels, fetch(): pl.pallas_call(functools.partial(fetch_kernel, starts), in_specs=[pl.Bloc...  5.14 us
    all_to_all x1, starting transfers between devices, on_device(): lax.all_to_all(outbound, AXES, split_axis=0, concat_axis=0, tiled=True)  4.25 us
    all_to_all x1, starting transfers between devices, on_device(): lax.all_to_all(attended, AXES, split_axis=0, concat_axis=0, tiled=True)  3.54 us
  transfers between devices with their start and end apart: 26, of which 12 were waited for; matrix products, arithmetic and copies ran while one was open for 7% of the time, Pallas kernels for 7%

profile of v12, /device:TPU:0, one launch (start us, length us, event | category | flops | bytes accessed | tf_op | source)
XLA Modules:
  0.0 95.7 jit_solution(677998801221690239)
XLA Ops:
  1.9 4.1 %collective-permute-start = (bf16[8,5120]{1,0:T(8,128)(2,1)S(1)}, bf16[8,5120]{1,0:T(8,128)(2,1)S(1)}, u32[]{:S(2)}, u32[]{:S(2)}) collective-permute-start(bf16[8,5120]{1,0:T(8,128)(2,1)S(1)} %get-tuple-element.33), channel_id=1, source_target_pairs={{0,8},{1,9},{2,10},{3,11},{4,12},{5,13},{6,14},{7,15},{8,0},{9,1},... | collective-permute-start | bytes 245768 | tf_op jit(solution)/shard_map/ppermute | solution.py:34
  6.0 1.6 %collective-permute-start.1 = (bf16[8,5120]{1,0:T(8,128)(2,1)S(1)}, bf16[8,5120]{1,0:T(8,128)(2,1)S(1)}, u32[]{:S(2)}, u32[]{:S(2)}) collective-permute-start(bf16[8,5120]{1,0:T(8,128)(2,1)S(1)} %get-tuple-element.33), channel_id=1, source_target_pairs={{0,4},{1,5},{2,6},{3,7},{4,0},{5,1},{6,2},{7,3},{8,12},{9,13},{10,... | collective-permute-start | bytes 245768 | tf_op jit(solution)/shard_map/ppermute | solution.py:34
  7.5 1.7 %collective-permute-start.3 = (bf16[8,3072]{1,0:T(8,128)(2,1)S(1)}, bf16[8,3072]{1,0:T(8,128)(2,1)S(1)}, u32[]{:S(2)}, u32[]{:S(2)}) collective-permute-start(bf16[8,3072]{1,0:T(8,128)(2,1)S(1)} %get-tuple-element.34), channel_id=1, source_target_pairs={{0,2},{1,3},{2,0},{3,1},{4,6},{5,7},{6,4},{7,5},{8,10},{9,11},{10,... | collective-permute-start | bytes 147464 | tf_op jit(solution)/shard_map/ppermute | solution.py:34
  11.8 1.7 %pad_maximum_fusion.refs_5_.refs_9_ = bf16[128,8192]{1,0:T(8,128)(2,1)S(1)} fusion(bf16[64,8192]{1,0:T(8,128)(2,1)} %bitcast.22, bf16[64,8192]{1,0:T(8,128)(2,1)} %bitcast.23), kind=kLoop, calls=%fused_computation | loop fusion | flops 4194304 | bytes 4194304 | tf_op jit(solution)/shard_map/concatenate | solution.py:601
  15.5 2.5 %collective-permute-start.5 = (bf16[16,3072]{1,0:T(8,128)(2,1)S(1)}, bf16[16,3072]{1,0:T(8,128)(2,1)S(1)}, u32[]{:S(2)}, u32[]{:S(2)}) collective-permute-start(bf16[16,3072]{1,0:T(8,128)(2,1)S(1)} %pad_maximum_fusion.2.refs_0_), channel_id=1, source_target_pairs={{0,8},{1,9},{2,10},{3,11},{4,12},{5,13},{6,14},{7,15},{8,0},{9,1},... | collective-permute-start | bytes 294920 | tf_op jit(solution)/shard_map/ppermute | solution.py:34
  19.9 3.4 %fetch.2.refs_4_.refs_8_ = bf16[8192,512]{1,0:T(8,128)(2,1)S(1)} custom-call(bf16[8192,512]{1,0:T(8,128)(2,1)} %refs_0_), custom_call_target="tpu_custom_call" | custom-call | bytes 16777216 | tf_op jit(solution)/shard_map/fetch/pallas_call | solution.py:271
  23.3 2.0 %collective-permute-done.5.refs_1_ = bf16[16,3072]{1,0:T(8,128)(2,1)S(1)} collective-permute-done((bf16[16,3072]{1,0:T(8,128)(2,1)S(1)}, bf16[16,3072]{1,0:T(8,128)(2,1)S(1)}, u32[]{:S(2)}, u32[]{:S(2)}) %collective-permute-start.5) | collective-permute-done | bytes 98336 | tf_op jit(solution)/shard_map/ppermute | solution.py:34
  28.6 1.7 %project.3 = bf16[256,640]{1,0:T(8,128)(2,1)} custom-call(bf16[16,3072]{1,0:T(8,128)(2,1)S(1)} %pad_maximum_fusion.2.refs_0_, bf16[16,3072]{1,0:T(8,128)(2,1)S(1)} %collective-permute-done.5.refs_1_, bf16[16,3072]{1,0:T(8,128)(2,1)S(1)} %collective-permute-done.6.refs_2_, bf16[16,3072]{1,0:T(8,128)(2,1)S(1)} %collective-permute-done.7.refs_3_, ...), custom_call_target="tpu_custom_call" | custom-call | flops 503316480 | bytes 3932160 | tf_op jit(solution)/shard_map/project/pallas_call | solution.py:349
  30.3 4.3 %all-to-all-start = ((bf16[16,16,640]{2,1,0:T(8,128)(2,1)}), bf16[16,16,640]{2,1,0:T(8,128)(2,1)S(1)}, u32[]{:S(2)}, u32[]{:S(2)}) async-start(bf16[16,16,640]{2,1,0:T(8,128)(2,1)} %bitcast.5), calls=%async_computation | async-start | bytes 655360 | tf_op jit(solution)/shard_map/all_to_all | solution.py:626
  35.3 10.3 %all-to-all-done.inbound = bf16[16,16,640]{2,1,0:T(8,128)(2,1)S(1)} async-done(((bf16[16,16,640]{2,1,0:T(8,128)(2,1)}), bf16[16,16,640]{2,1,0:T(8,128)(2,1)S(1)}, u32[]{:S(2)}, u32[]{:S(2)}) %all-to-all-start) | async-done | bytes 327712 | tf_op jit(solution)/shard_map/all_to_all | solution.py:626
  45.7 6.0 %attend.1 = bf16[16,16,512]{2,1,0:T(8,128)(2,1)} custom-call(s32[16,4]{1,0:T(8,128)S(1)} %copy.21.table, s32[2,1,128]{2,1,0:T(1,128)S(1)} %bitcast.18, bf16[16,16,640]{2,1,0:T(8,128)(2,1)S(1)} %all-to-all-done.inbound, f32[16,128]{1,0:T(8,128)S(1)} %pad_maximum_fusion.3.cosine, f32[16,128]{1,0:T(8,128)S(1)} %pad_maximum_fusion.4.sine, ...), custom_call_target="tpu_custom_call" | custom-call | flops 134217728 | bytes 8388608 | tf_op jit(solution)/shard_map/attend/pallas_call | solution.py:531
  51.6 3.5 %all-to-all-start.1 = ((bf16[16,16,512]{2,1,0:T(8,128)(2,1)}), bf16[16,16,512]{2,1,0:T(8,128)(2,1)S(1)}, u32[]{:S(2)}, u32[]{:S(2)}) async-start(bf16[16,16,512]{2,1,0:T(8,128)(2,1)} %attend.1), calls=%async_computation.1 | async-start | bytes 524288 | tf_op jit(solution)/shard_map/all_to_all | solution.py:639
  56.9 1.8 %fetch.3.w_front = bf16[512,2560]{1,0:T(8,128)(2,1)S(1)} custom-call(bf16[512,8192]{1,0:T(8,128)(2,1)} %w_out.1), custom_call_target="tpu_custom_call" | custom-call | bytes 5242880 | tf_op jit(solution)/shard_map/fetch/pallas_call | solution.py:271
  58.7 6.5 %all-to-all-done.1 = bf16[16,16,512]{2,1,0:T(8,128)(2,1)S(1)} async-done(((bf16[16,16,512]{2,1,0:T(8,128)(2,1)}), bf16[16,16,512]{2,1,0:T(8,128)(2,1)S(1)}, u32[]{:S(2)}, u32[]{:S(2)}) %all-to-all-start.1) | async-done | bytes 262176 | tf_op jit(solution)/shard_map/all_to_all | solution.py:639
  65.2 3.3 %product.1 = (bf16[64,4864]{1,0:T(8,128)(2,1)S(1)}, f32[64,4864]{1,0:T(8,128)S(1)}, bf16[64,3328]{1,0:T(8,128)(2,1)S(1)}, f32[64,3328]{1,0:T(8,128)S(1)}) custom-call(s32[1,128]{1,0:T(1,128)S(1)} %reshape_reshape.6.place_a, s32[1,128]{1,0:T(1,128)S(1)} %reshape_reshape.7.place_b, bf16[256,512]{1,0:T(8,128)(2,1)S(1)} %bitcast.16, bf16[512,8192]{1,0:T(8,128)(2,1)} %w_out.1, ...), custom_call_target="tpu_custom_call" | custom-call | flops 1073741824 | bytes 8388608 | tf_op jit(solution)/shard_map/product/pallas_call | solution.py:165
  68.6 2.0 %collective-permute-done.14 = bf16[64,4864]{1,0:T(8,128)(2,1)S(1)} collective-permute-done((bf16[64,4864]{1,0:T(8,128)(2,1)S(1)}, bf16[64,4864]{1,0:T(8,128)(2,1)S(1)}, u32[]{:S(2)}, u32[]{:S(2)}) %collective-permute-start.14) | collective-permute-done | bytes 622624 | tf_op jit(solution)/shard_map/ppermute | solution.py:34
  71.0 1.6 %collective-permute-done.16 = bf16[64,3328]{1,0:T(8,128)(2,1)S(1)} collective-permute-done((bf16[64,3328]{1,0:T(8,128)(2,1)S(1)}, bf16[64,3328]{1,0:T(8,128)(2,1)S(1)}, u32[]{:S(2)}, u32[]{:S(2)}) %collective-permute-start.16) | collective-permute-done | bytes 426016 | tf_op jit(solution)/shard_map/ppermute | solution.py:34
  74.0 3.9 %collective-permute-done.17 = bf16[16,3328]{1,0:T(8,128)(2,1)S(1)} collective-permute-done((bf16[16,3328]{1,0:T(8,128)(2,1)S(1)}, bf16[16,3328]{1,0:T(8,128)(2,1)S(1)}, u32[]{:S(2)}, u32[]{:S(2)}) %collective-permute-start.17) | collective-permute-done | bytes 106528 | tf_op jit(solution)/shard_map/ppermute | solution.py:34
  79.7 2.9 %collective-permute-done.15 = bf16[32,4864]{1,0:T(8,128)(2,1)S(1)} collective-permute-done((bf16[32,4864]{1,0:T(8,128)(2,1)S(1)}, bf16[32,4864]{1,0:T(8,128)(2,1)S(1)}, u32[]{:S(2)}, u32[]{:S(2)}) %collective-permute-start.15) | collective-permute-done | bytes 311328 | tf_op jit(solution)/shard_map/ppermute | solution.py:34
  82.5 2.8 %collective-permute-done.19 = bf16[16,3328]{1,0:T(8,128)(2,1)S(1)} collective-permute-done((bf16[16,3328]{1,0:T(8,128)(2,1)S(1)}, bf16[16,3328]{1,0:T(8,128)(2,1)S(1)}, u32[]{:S(2)}, u32[]{:S(2)}) %collective-permute-start.19) | collective-permute-done | bytes 106528 | tf_op jit(solution)/shard_map/ppermute | solution.py:34
  87.1 1.6 %collective-permute-start.21 = (bf16[8,4864]{1,0:T(8,128)(2,1)S(1)}, bf16[8,4864]{1,0:T(8,128)(2,1)S(1)}, u32[]{:S(2)}, u32[]{:S(2)}) collective-permute-start(bf16[8,4864]{1,0:T(8,128)(2,1)S(1)} %get-tuple-element.71), channel_id=1, source_target_pairs={{0,4},{1,5},{2,6},{3,7},{4,0},{5,1},{6,2},{7,3},{8,12},{9,13},{10,... | collective-permute-start | bytes 233480 | tf_op jit(solution)/shard_map/ppermute | solution.py:34
  88.7 1.9 %collective-permute-start.22 = (bf16[8,4864]{1,0:T(8,128)(2,1)S(1)}, bf16[8,4864]{1,0:T(8,128)(2,1)S(1)}, u32[]{:S(2)}, u32[]{:S(2)}) collective-permute-start(bf16[8,4864]{1,0:T(8,128)(2,1)S(1)} %get-tuple-element.70), channel_id=1, source_target_pairs={{0,12},{1,13},{2,14},{3,15},{4,8},{5,9},{6,10},{7,11},{8,4},{9,5},... | collective-permute-start | bytes 233480 | tf_op jit(solution)/shard_map/ppermute | solution.py:34
  90.6 2.6 %collective-permute-done.20 = bf16[8,4864]{1,0:T(8,128)(2,1)S(1)} collective-permute-done((bf16[8,4864]{1,0:T(8,128)(2,1)S(1)}, bf16[8,4864]{1,0:T(8,128)(2,1)S(1)}, u32[]{:S(2)}, u32[]{:S(2)}) %collective-permute-start.20) | collective-permute-done | bytes 77856 | tf_op jit(solution)/shard_map/ppermute | solution.py:34
  93.3 1.7 %collective-permute-done.22 = bf16[8,4864]{1,0:T(8,128)(2,1)S(1)} collective-permute-done((bf16[8,4864]{1,0:T(8,128)(2,1)S(1)}, bf16[8,4864]{1,0:T(8,128)(2,1)S(1)}, u32[]{:S(2)}, u32[]{:S(2)}) %collective-permute-start.22) | collective-permute-done | bytes 77856 | tf_op jit(solution)/shard_map/ppermute | solution.py:34
  (85 shorter events, 20.0 us)
Async XLA Ops:
  1.9 12.1 %collective-permute-start = (bf16[8,5120]{1,0:T(8,128)(2,1)S(1)}, bf16[8,5120]{1,0:T(8,128)(2,1)S(1)}, u32[]{:S(2)}, u32[]{:S(2)}) collective-permute-start(bf16[8,5120]{1,0:T(8,128)(2,1)S(1)} %get-tuple-element.33), channel_id=1, source_target_pairs={{0,8},{1,9},{2,10},{3,11},{4,12},{5,13},{6,14},{7,15},{8,0},{9,1},... | collective-permute-start | bytes 245768 | tf_op jit(solution)/shard_map/ppermute | solution.py:34
  6.0 8.0 %collective-permute-start.1 = (bf16[8,5120]{1,0:T(8,128)(2,1)S(1)}, bf16[8,5120]{1,0:T(8,128)(2,1)S(1)}, u32[]{:S(2)}, u32[]{:S(2)}) collective-permute-start(bf16[8,5120]{1,0:T(8,128)(2,1)S(1)} %get-tuple-element.33), channel_id=1, source_target_pairs={{0,4},{1,5},{2,6},{3,7},{4,0},{5,1},{6,2},{7,3},{8,12},{9,13},{10,... | collective-permute-start | bytes 245768 | tf_op jit(solution)/shard_map/ppermute | solution.py:34
  7.5 6.4 %collective-permute-start.2 = (bf16[8,5120]{1,0:T(8,128)(2,1)S(1)}, bf16[8,5120]{1,0:T(8,128)(2,1)S(1)}, u32[]{:S(2)}, u32[]{:S(2)}) collective-permute-start(bf16[8,5120]{1,0:T(8,128)(2,1)S(1)} %get-tuple-element.33), channel_id=1, source_target_pairs={{0,12},{1,13},{2,14},{3,15},{4,8},{5,9},{6,10},{7,11},{8,4},{9,5},... | collective-permute-start | bytes 245768 | tf_op jit(solution)/shard_map/ppermute | solution.py:34
  7.5 6.4 %collective-permute-start.3 = (bf16[8,3072]{1,0:T(8,128)(2,1)S(1)}, bf16[8,3072]{1,0:T(8,128)(2,1)S(1)}, u32[]{:S(2)}, u32[]{:S(2)}) collective-permute-start(bf16[8,3072]{1,0:T(8,128)(2,1)S(1)} %get-tuple-element.34), channel_id=1, source_target_pairs={{0,2},{1,3},{2,0},{3,1},{4,6},{5,7},{6,4},{7,5},{8,10},{9,11},{10,... | collective-permute-start | bytes 147464 | tf_op jit(solution)/shard_map/ppermute | solution.py:34
  14.0 11.7 %collective-permute-start.4 = (bf16[32,5120]{1,0:T(8,128)(2,1)S(1)}, bf16[32,5120]{1,0:T(8,128)(2,1)S(1)}, u32[]{:S(2)}, u32[]{:S(2)}) collective-permute-start(bf16[32,5120]{1,0:T(8,128)(2,1)S(1)} %pad_maximum_fusion.1.refs_0_), channel_id=1, source_target_pairs={{0,2},{1,3},{2,0},{3,1},{4,6},{5,7},{6,4},{7,5},{8,10},{9,11},{10,... | collective-permute-start | bytes 983048 | tf_op jit(solution)/shard_map/ppermute | solution.py:34
  15.5 9.8 %collective-permute-start.5 = (bf16[16,3072]{1,0:T(8,128)(2,1)S(1)}, bf16[16,3072]{1,0:T(8,128)(2,1)S(1)}, u32[]{:S(2)}, u32[]{:S(2)}) collective-permute-start(bf16[16,3072]{1,0:T(8,128)(2,1)S(1)} %pad_maximum_fusion.2.refs_0_), channel_id=1, source_target_pairs={{0,8},{1,9},{2,10},{3,11},{4,12},{5,13},{6,14},{7,15},{8,0},{9,1},... | collective-permute-start | bytes 294920 | tf_op jit(solution)/shard_map/ppermute | solution.py:34
  17.9 7.8 %collective-permute-start.6 = (bf16[16,3072]{1,0:T(8,128)(2,1)S(1)}, bf16[16,3072]{1,0:T(8,128)(2,1)S(1)}, u32[]{:S(2)}, u32[]{:S(2)}) collective-permute-start(bf16[16,3072]{1,0:T(8,128)(2,1)S(1)} %pad_maximum_fusion.2.refs_0_), channel_id=1, source_target_pairs={{0,4},{1,5},{2,6},{3,7},{4,0},{5,1},{6,2},{7,3},{8,12},{9,13},{10,... | collective-permute-start | bytes 294920 | tf_op jit(solution)/shard_map/ppermute | solution.py:34
  18.8 7.0 %collective-permute-start.7 = (bf16[16,3072]{1,0:T(8,128)(2,1)S(1)}, bf16[16,3072]{1,0:T(8,128)(2,1)S(1)}, u32[]{:S(2)}, u32[]{:S(2)}) collective-permute-start(bf16[16,3072]{1,0:T(8,128)(2,1)S(1)} %pad_maximum_fusion.2.refs_0_), channel_id=1, source_target_pairs={{0,12},{1,13},{2,14},{3,15},{4,8},{5,9},{6,10},{7,11},{8,4},{9,5},... | collective-permute-start | bytes 294920 | tf_op jit(solution)/shard_map/ppermute | solution.py:34
  19.9 6.9 %collective-permute-start.12 = (bf16[32,5120]{1,0:T(8,128)(2,1)S(1)}, bf16[32,5120]{1,0:T(8,128)(2,1)S(1)}, u32[]{:S(2)}, u32[]{:S(2)}) collective-permute-start(bf16[32,5120]{1,0:T(8,128)(2,1)S(1)} %pad_maximum_fusion.1.refs_0_), channel_id=1, source_target_pairs={{0,1},{1,0},{2,3},{3,2},{4,5},{5,4},{6,7},{7,6},{8,9},{9,8},{10,11... | collective-permute-start | bytes 983048 | tf_op jit(solution)/shard_map/ppermute | solution.py:34
  25.7 2.8 %collective-permute-start.10 = (bf16[16,3072]{1,0:T(8,128)(2,1)S(1)}, bf16[16,3072]{1,0:T(8,128)(2,1)S(1)}, u32[]{:S(2)}, u32[]{:S(2)}) collective-permute-start(bf16[16,3072]{1,0:T(8,128)(2,1)S(1)} %collective-permute-done.6.refs_2_), channel_id=1, source_target_pairs={{0,1},{1,0},{2,3},{3,2},{4,5},{5,4},{6,7},{7,6},{8,9},{9,8},{10,11... | collective-permute-start | bytes 294920 | tf_op jit(solution)/shard_map/ppermute | solution.py:34
  26.2 2.3 %collective-permute-start.11 = (bf16[16,3072]{1,0:T(8,128)(2,1)S(1)}, bf16[16,3072]{1,0:T(8,128)(2,1)S(1)}, u32[]{:S(2)}, u32[]{:S(2)}) collective-permute-start(bf16[16,3072]{1,0:T(8,128)(2,1)S(1)} %collective-permute-done.7.refs_3_), channel_id=1, source_target_pairs={{0,1},{1,0},{2,3},{3,2},{4,5},{5,4},{6,7},{7,6},{8,9},{9,8},{10,11... | collective-permute-start | bytes 294920 | tf_op jit(solution)/shard_map/ppermute | solution.py:34
  26.3 2.3 %collective-permute-start.8 = (bf16[16,3072]{1,0:T(8,128)(2,1)S(1)}, bf16[16,3072]{1,0:T(8,128)(2,1)S(1)}, u32[]{:S(2)}, u32[]{:S(2)}) collective-permute-start(bf16[16,3072]{1,0:T(8,128)(2,1)S(1)} %pad_maximum_fusion.2.refs_0_), channel_id=1, source_target_pairs={{0,1},{1,0},{2,3},{3,2},{4,5},{5,4},{6,7},{7,6},{8,9},{9,8},{10,11... | collective-permute-start | bytes 294920 | tf_op jit(solution)/shard_map/ppermute | solution.py:34
  30.3 15.4 %all-to-all-start = ((bf16[16,16,640]{2,1,0:T(8,128)(2,1)}), bf16[16,16,640]{2,1,0:T(8,128)(2,1)S(1)}, u32[]{:S(2)}, u32[]{:S(2)}) async-start(bf16[16,16,640]{2,1,0:T(8,128)(2,1)} %bitcast.5), calls=%async_computation | async-start | bytes 655360 | tf_op jit(solution)/shard_map/all_to_all | solution.py:626
  51.6 13.6 %all-to-all-start.1 = ((bf16[16,16,512]{2,1,0:T(8,128)(2,1)}), bf16[16,16,512]{2,1,0:T(8,128)(2,1)S(1)}, u32[]{:S(2)}, u32[]{:S(2)}) async-start(bf16[16,16,512]{2,1,0:T(8,128)(2,1)} %attend.1), calls=%async_computation.1 | async-start | bytes 524288 | tf_op jit(solution)/shard_map/all_to_all | solution.py:639
  68.5 2.1 %collective-permute-start.14 = (bf16[64,4864]{1,0:T(8,128)(2,1)S(1)}, bf16[64,4864]{1,0:T(8,128)(2,1)S(1)}, u32[]{:S(2)}, u32[]{:S(2)}) collective-permute-start(bf16[64,4864]{1,0:T(8,128)(2,1)S(1)} %get-tuple-element.53), channel_id=1, source_target_pairs={{0,1},{1,0},{2,3},{3,2},{4,5},{5,4},{6,7},{7,6},{8,9},{9,8},{10,11... | collective-permute-start | bytes 1867784 | tf_op jit(solution)/shard_map/ppermute | solution.py:34
  70.8 1.8 %collective-permute-start.16 = (bf16[64,3328]{1,0:T(8,128)(2,1)S(1)}, bf16[64,3328]{1,0:T(8,128)(2,1)S(1)}, u32[]{:S(2)}, u32[]{:S(2)}) collective-permute-start(bf16[64,3328]{1,0:T(8,128)(2,1)S(1)} %get-tuple-element.56), channel_id=1, source_target_pairs={{0,1},{1,0},{2,3},{3,2},{4,5},{5,4},{6,7},{7,6},{8,9},{9,8},{10,11... | collective-permute-start | bytes 1277960 | tf_op jit(solution)/shard_map/ppermute | solution.py:34
  72.8 5.1 %collective-permute-start.17 = (bf16[16,3328]{1,0:T(8,128)(2,1)S(1)}, bf16[16,3328]{1,0:T(8,128)(2,1)S(1)}, u32[]{:S(2)}, u32[]{:S(2)}) collective-permute-start(bf16[16,3328]{1,0:T(8,128)(2,1)S(1)} %get-tuple-element.67), channel_id=1, source_target_pairs={{0,4},{1,5},{2,6},{3,7},{4,0},{5,1},{6,2},{7,3},{8,12},{9,13},{10,... | collective-permute-start | bytes 319496 | tf_op jit(solution)/shard_map/ppermute | solution.py:34
  73.2 9.3 %collective-permute-start.15 = (bf16[32,4864]{1,0:T(8,128)(2,1)S(1)}, bf16[32,4864]{1,0:T(8,128)(2,1)S(1)}, u32[]{:S(2)}, u32[]{:S(2)}) collective-permute-start(bf16[32,4864]{1,0:T(8,128)(2,1)S(1)} %slice.82), channel_id=1, source_target_pairs={{0,2},{1,3},{2,0},{3,1},{4,6},{5,7},{6,4},{7,5},{8,10},{9,11},{10,... | collective-permute-start | bytes 933896 | tf_op jit(solution)/shard_map/ppermute | solution.py:34
  77.9 7.5 %collective-permute-start.19 = (bf16[16,3328]{1,0:T(8,128)(2,1)S(1)}, bf16[16,3328]{1,0:T(8,128)(2,1)S(1)}, u32[]{:S(2)}, u32[]{:S(2)}) collective-permute-start(bf16[16,3328]{1,0:T(8,128)(2,1)S(1)} %fusion.2), channel_id=1, source_target_pairs={{0,8},{1,9},{2,10},{3,11},{4,12},{5,13},{6,14},{7,15},{8,0},{9,1},... | collective-permute-start | bytes 319496 | tf_op jit(solution)/shard_map/ppermute | solution.py:34
  79.0 6.4 %collective-permute-start.18 = (bf16[16,3328]{1,0:T(8,128)(2,1)S(1)}, bf16[16,3328]{1,0:T(8,128)(2,1)S(1)}, u32[]{:S(2)}, u32[]{:S(2)}) collective-permute-start(bf16[16,3328]{1,0:T(8,128)(2,1)S(1)} %get-tuple-element.57), channel_id=1, source_target_pairs={{0,4},{1,5},{2,6},{3,7},{4,0},{5,1},{6,2},{7,3},{8,12},{9,13},{10,... | collective-permute-start | bytes 319496 | tf_op jit(solution)/shard_map/ppermute | solution.py:34
  85.5 5.1 %collective-permute-start.23 = (bf16[8,3328]{1,0:T(8,128)(2,1)S(1)}, bf16[8,3328]{1,0:T(8,128)(2,1)S(1)}, u32[]{:S(2)}, u32[]{:S(2)}) collective-permute-start(bf16[8,3328]{1,0:T(8,128)(2,1)S(1)} %slice.83), channel_id=1, source_target_pairs={{0,2},{1,3},{2,0},{3,1},{4,6},{5,7},{6,4},{7,5},{8,10},{9,11},{10,... | collective-permute-start | bytes 159752 | tf_op jit(solution)/shard_map/ppermute | solution.py:34
  86.1 7.1 %collective-permute-start.20 = (bf16[8,4864]{1,0:T(8,128)(2,1)S(1)}, bf16[8,4864]{1,0:T(8,128)(2,1)S(1)}, u32[]{:S(2)}, u32[]{:S(2)}) collective-permute-start(bf16[8,4864]{1,0:T(8,128)(2,1)S(1)} %get-tuple-element.69), channel_id=1, source_target_pairs={{0,8},{1,9},{2,10},{3,11},{4,12},{5,13},{6,14},{7,15},{8,0},{9,1},... | collective-permute-start | bytes 233480 | tf_op jit(solution)/shard_map/ppermute | solution.py:34
  87.1 6.2 %collective-permute-start.21 = (bf16[8,4864]{1,0:T(8,128)(2,1)S(1)}, bf16[8,4864]{1,0:T(8,128)(2,1)S(1)}, u32[]{:S(2)}, u32[]{:S(2)}) collective-permute-start(bf16[8,4864]{1,0:T(8,128)(2,1)S(1)} %get-tuple-element.71), channel_id=1, source_target_pairs={{0,4},{1,5},{2,6},{3,7},{4,0},{5,1},{6,2},{7,3},{8,12},{9,13},{10,... | collective-permute-start | bytes 233480 | tf_op jit(solution)/shard_map/ppermute | solution.py:34
  88.7 6.2 %collective-permute-start.22 = (bf16[8,4864]{1,0:T(8,128)(2,1)S(1)}, bf16[8,4864]{1,0:T(8,128)(2,1)S(1)}, u32[]{:S(2)}, u32[]{:S(2)}) collective-permute-start(bf16[8,4864]{1,0:T(8,128)(2,1)S(1)} %get-tuple-element.70), channel_id=1, source_target_pairs={{0,12},{1,13},{2,14},{3,15},{4,8},{5,9},{6,10},{7,11},{8,4},{9,5},... | collective-permute-start | bytes 233480 | tf_op jit(solution)/shard_map/ppermute | solution.py:34
  (7 other events, 34.6 us)

commit v13 on v12

--- a/solution.py
+++ b/solution.py
@@ -99,99 +99,74 @@
     return x.astype(jnp.float32)
 
 
-def product_kernel(
-    cuts,
-    place_a,
-    place_b,
-    returned,
-    w_out,
-    w_front,
-    away_a,
-    keep_a,
-    away_b,
-    keep_b,
-    held,
-    sems,
-):
-    front = w_front.shape[1]
+def product_kernel(start, cuts, place, returned, w_out, *refs):
+    front = refs[0].shape[1] if len(refs) == 5 else 0
+    away, keep, held, sems = refs[-4:]
     copies = []
-    for i, (start, stop) in enumerate(cuts):
+    for i, (begin, end) in enumerate(cuts):
         copy = None
-        if start >= front:
-            size = pl.ds(start, stop - start), pl.ds(start - front, stop - start)
+        if begin >= front:
+            source = w_out.at[:, pl.ds(start + begin, end - begin)]
             copy = pltpu.make_async_copy(
-                w_out.at[:, size[0]], held.at[:, size[1]], sems.at[i]
+                source, held.at[:, pl.ds(begin - front, end - begin)], sems.at[i]
             )
             copy.start()
         copies.append(copy)
-    slots = lax.broadcasted_iota(jnp.int32, (returned.shape[0], place_a.shape[1]), 0)
-
-    def picked(place):
-        route = jnp.where(slots == place[...], 1.0, 0.0).astype(jnp.bfloat16)
-        rows = lax.dot_general(
-            route, returned[...], (((0,), (0,)), ((), ())), preferred_element_type=jnp.float32
-        )
-        return rows.astype(jnp.bfloat16)
-
-    rows_a, rows_b = picked(place_a), picked(place_b)
-    half = keep_a.shape[0]
-    middle = keep_a.shape[1]
-    for copy, (start, stop) in zip(copies, cuts):
-        if copy is not None:
+    slots = lax.broadcasted_iota(jnp.int32, (returned.shape[0], place.shape[1]), 0)
+    route = jnp.where(slots == place[...], 1.0, 0.0).astype(jnp.bfloat16)
+    rows = lax.dot_general(
+        route, returned[...], (((0,), (0,)), ((), ())), preferred_element_type=jnp.float32
+    ).astype(jnp.bfloat16)
+    half = keep.shape[0]
+    for copy, (begin, end) in zip(copies, cuts):
+        if copy is None:
+            w = refs[0][:, begin:end]
+        else:
             copy.wait()
-        rows, away, keep = (rows_a, away_a, keep_a) if start < middle else (rows_b, away_b, keep_b)
-        w = w_front[:, start:stop] if copy is None else held[:, start - front : stop - front]
+            w = held[:, begin - front : end - front]
         x = jnp.dot(rows, w, preferred_element_type=jnp.float32)
-        begin = start if start < middle else start - middle
-        here = slice(begin, begin + stop - start)
-        keep[:, here] = x[:half]
-        away[:, here] = x[half:].astype(jnp.bfloat16)
-
-
-def product(place_a, place_b, returned, w_out, w_front, cut):
-    rows = place_a.shape[0]
-    depth, width = w_out.shape
+        keep[:, begin:end] = x[:half]
+        away[:, begin:end] = x[half:].astype(jnp.bfloat16)
+
+
+def product(place, returned, w_out, start, width, w_front=None):
+    rows = place.shape[0]
+    depth = w_out.shape[0]
+    front = 0 if w_front is None else w_front.shape[1]
     cuts = []
-    front = w_front.shape[1]
-    for start, stop in ((0, front), (front, cut), (cut, width)):
-        while start < stop:
-            cuts.append((start, min(start + 1024, stop)))
-            start = cuts[-1][1]
+    for begin, end in ((0, front), (front, width)):
+        while begin < end:
+            cuts.append((begin, min(begin + 1024, end)))
+            begin = cuts[-1][1]
     vmem = pl.BlockSpec(memory_space=pltpu.VMEM)
-    out = []
-    for size in (cut, width - cut):
-        out.append(jax.ShapeDtypeStruct((rows // 2, size), jnp.bfloat16))
-        out.append(jax.ShapeDtypeStruct((rows // 2, size), jnp.float32))
+    args = [place.reshape(1, rows), returned, w_out]
+    specs = [vmem, vmem, pl.BlockSpec(memory_space=pl.ANY)]
+    if front:
+        args.append(w_front)
+        specs.append(vmem)
     return pl.pallas_call(
-        functools.partial(product_kernel, tuple(cuts)),
-        in_specs=[vmem, vmem, vmem, pl.BlockSpec(memory_space=pl.ANY), vmem],
-        out_specs=[vmem] * 4,
-        out_shape=out,
+        functools.partial(product_kernel, start, tuple(cuts)),
+        in_specs=specs,
+        out_specs=[vmem, vmem],
+        out_shape=[
+            jax.ShapeDtypeStruct((rows // 2, width), jnp.bfloat16),
+            jax.ShapeDtypeStruct((rows // 2, width), jnp.float32),
+        ],
         scratch_shapes=[
             pltpu.VMEM((depth, width - front), jnp.bfloat16),
             pltpu.SemaphoreType.DMA((len(cuts),)),
         ],
         compiler_params=pltpu.CompilerParams(vmem_limit_bytes=48 * 2**20),
         cost_estimate=pl.CostEstimate(
-            flops=2 * rows * depth * width, bytes_accessed=2 * depth * width, transcendentals=0
+            flops=2 * rows * depth * width,
+            bytes_accessed=2 * depth * (width - front),
+            transcendentals=0,
         ),
         name="product",
-    )(place_a.reshape(1, rows), place_b.reshape(1, rows), returned, w_out, w_front)
+    )(*args)
 
 
 def scatter_sum(grid, place_a, place_b, returned, w_out, w_front, cut):
-    def along_line(x):
-        size = x.shape[0] // 2 // grid.half
-        middle = x.shape[0] // 2
-        first = grid.send(narrow(x[middle + size :]), pair=1)
-        second = grid.send(after(narrow(x[middle : middle + size]), first), pair=1)
-        far = x[size:middle] + wide(first)
-        third = [
-            grid.send(narrow(far[d * size : (d + 1) * size]), half=d + 1)
-            for d in range(grid.half - 1)
-        ]
-        return x[:size], [second] + third
-
     def direct(x):
         size = x.shape[0] // 2 // grid.half
         parts = []
@@ -208,13 +183,16 @@
             x = x + wide(part)
         return x
 
-    away_a, keep_a, away_b, keep_b = product(place_a, place_b, returned, w_out, w_front, cut)
+    away_a, keep_a = product(place_a, returned, w_out, 0, cut, w_front)
+    away_b, keep_b = product(
+        place_b, after(returned, away_a), w_out, cut, w_out.shape[1] - cut
+    )
     xa = keep_a + wide(grid.send(away_a, core=1))
     middle = xa.shape[0] // 2
     sent_a = narrow(xa[middle:])
     got_a = grid.send(sent_a, near=1)
     xb = keep_b + wide(grid.send(after(away_b, sent_a), core=1))
-    xb, got_b = along_line(xb)
+    xb, got_b = direct(xb)
     got_a, got_b = lax.optimization_barrier((got_a, got_b))
     xa, parts_a = direct(xa[:middle] + wide(got_a))
     xb = total(xb, got_b)
@@ -396,16 +374,23 @@
     batches = query_rot.shape[1]
     batch = slots // batches
 
-    width = kv_width // 2
+    width = 2 * HEAD
     copies = []
     for i, (pool, on_chip) in enumerate(((key_pages, key_pool), (value_pages, value_pool))):
-        for half in range(2):
-            part = pool.at[:, :, pl.ds(half * width, width)]
-            copies.append(pltpu.make_async_copy(part, on_chip.at[half], sems.at[i, half]))
-            copies[-1].start()
-
-    def held(pool, slot, columns):
-        return [pool[table[slot, j], :, columns] for j in range(pages)]
+        for p in range(pairs):
+            part = pool.at[:, :, pl.ds(p * width, width)]
+            copies.append(pltpu.make_async_copy(part, on_chip.at[p], sems.at[i, p]))
+    ahead = 2
+    for copy in copies[:ahead]:
+        copy.start()
+
+    def arrived(i):
+        copies[i].wait()
+        if i + ahead < len(copies):
+            copies[i + ahead].start()
+
+    def held(pool, slot):
+        return [pool[table[slot, j]] for j in range(pages)]
 
     cos = cosine[...]
     sin = sine[...]
@@ -448,10 +433,7 @@
 
     own_chances = {}
     for p in range(pairs):
-        half, inside = divmod(p * 2 * HEAD, width)
-        columns_p = slice(inside, inside + 2 * HEAD)
-        if inside == 0:
-            copies[half].wait()
+        arrived(p)
         for b in range(batches):
             valid = row < lengths[b]
             turned = query_rot[p, b].T.astype(jnp.bfloat16)
@@ -461,7 +443,7 @@
             )
             keys = []
             for s in range(batch):
-                keys += held(key_pool.at[half], b * batch + s, columns_p)
+                keys += held(key_pool.at[p], b * batch + s)
             keys.append(key_new[:, p * 2 * HEAD : (p + 1) * 2 * HEAD])
             products = jnp.dot(
                 jnp.concatenate(keys, axis=0), wide, preferred_element_type=jnp.float32
@@ -483,14 +465,11 @@
             )
 
     for p in range(pairs):
-        half, inside = divmod(p * 2 * HEAD, width)
-        columns_p = slice(inside, inside + 2 * HEAD)
-        if inside == 0:
-            copies[2 + half].wait()
+        arrived(pairs + p)
         for b in range(batches):
             for s in range(batch):
                 mine = chance[p, b, pl.ds(s, pair, stride=batch)].astype(jnp.bfloat16)
-                values = held(value_pool.at[half], b * batch + s, columns_p)
+                values = held(value_pool.at[p], b * batch + s)
                 both = jnp.dot(
                     mine, jnp.concatenate(values, axis=0), preferred_element_type=jnp.float32
                 )
@@ -534,9 +513,9 @@
         out_specs=vmem,
         out_shape=jax.ShapeDtypeStruct((owners, slots, per_query), jnp.bfloat16),
         scratch_shapes=[
-            pltpu.VMEM((2, *key_pages.shape[:2], kv_width // 2), jnp.bfloat16),
-            pltpu.VMEM((2, *key_pages.shape[:2], kv_width // 2), jnp.bfloat16),
-            pltpu.SemaphoreType.DMA((2, 2)),
+            pltpu.VMEM((pairs, *key_pages.shape[:2], 2 * HEAD), jnp.bfloat16),
+            pltpu.VMEM((pairs, *key_pages.shape[:2], 2 * HEAD), jnp.bfloat16),
+            pltpu.SemaphoreType.DMA((2, pairs)),
             pltpu.VMEM((slots, kv_width), jnp.bfloat16),
             pltpu.VMEM((pairs, batches, columns, HEAD), jnp.float32),
             pltpu.VMEM((kv_heads, slots, HEAD), jnp.float32),
@@ -638,7 +617,7 @@
     (w_front,) = fetch((after(w_out, attended), (0, width // 32 * 10)), limit=48)
     returned = lax.all_to_all(attended, AXES, split_axis=0, concat_axis=0, tiled=True)
     returned = returned.reshape(all_slots, per_query)
-    summed = scatter_sum(grid, place_a, place_b, returned, w_out, w_front, width // 32 * 19)
+    summed = scatter_sum(grid, place_a, place_b, returned, w_out, w_front, width // 32 * 21)
     return narrow(wide(hidden_in) + summed)
 
 

time: 96.3 us -> 100 us (1.038)
  Pallas kernels: 17.5 us -> 22.1 us
  waiting for transfers between devices: 37.4 us -> 33.2 us
  starting transfers between devices: 30.5 us -> 33.2 us
  local copies, waits for them, and re-layouts: 4 us -> 5.1 us
    ppermute x24, waiting for transfers between devices: 20.6 us -> 16.3 us  [send(): return lax.ppermute(x, AXES, pairs)]
    pallas_call x1, Pallas kernels: 5.97 us -> 8.37 us  [attend(): pl.pallas_call(functools.partial(attend_kernel, per_query, per_key), in_s...]
    ppermute x24, starting transfers between devices: 22.7 us -> 24.8 us  [send(): return lax.ppermute(x, AXES, pairs)]
    pallas_call x1 -> x2, Pallas kernels: 3.34 us -> 5.51 us  [product(): pl.pallas_call(functools.partial(product_kernel, start, tuple(cuts)), in_...]
    unnamed x10 -> x14, local copies, waits for them, and re-layouts: 1.68 us -> 2.78 us
  transfers between devices with their start and end apart: 26 -> 26, of which waited for: 12 -> 10; matrix products, arithmetic and copies ran while one was open for 7% -> 7% of each run, Pallas kernels for 7% -> 9%
where the time goes in v13:
time: 100 us; the launch traced here: 99.8 us
  starting transfers between devices  33.2 us (33%)
  waiting for transfers between devices  33.2 us (33%)
  Pallas kernels  22.1 us (22%)
  other arithmetic  5.94 us (6%)
  local copies, waits for them, and re-layouts  5.1 us (5%)
    ppermute x24, starting transfers between devices, send(): return lax.ppermute(x, AXES, pairs)  24.8 us
    ppermute x24, waiting for transfers between devices, send(): return lax.ppermute(x, AXES, pairs)  16.3 us
    all_to_all x1, waiting for transfers between devices, on_device(): lax.all_to_all(outbound, AXES, split_axis=0, concat_axis=0, tiled=True)  9.66 us
    pallas_call x1, Pallas kernels, attend(): pl.pallas_call(functools.partial(attend_kernel, per_query, per_key), in_s...  8.37 us
    all_to_all x1, waiting for transfers between devices, on_device(): lax.all_to_all(attended, AXES, split_axis=0, concat_axis=0, tiled=True)  7.29 us
    pallas_call x2, Pallas kernels, product(): pl.pallas_call(functools.partial(product_kernel, start, tuple(cuts)), in_...  5.51 us
    pallas_call x2, Pallas kernels, fetch(): pl.pallas_call(functools.partial(fetch_kernel, starts), in_specs=[pl.Bloc...  5.14 us
    all_to_all x1, starting transfers between devices, on_device(): lax.all_to_all(outbound, AXES, split_axis=0, concat_axis=0, tiled=True)  4.78 us
  transfers between devices with their start and end apart: 26, of which 10 were waited for; matrix products, arithmetic and copies ran while one was open for 7% of the time, Pallas kernels for 9%

profile of v13, /device:TPU:0, one launch (start us, length us, event | category | flops | bytes accessed | tf_op | source)
XLA Modules:
  0.0 99.8 jit_solution(6690991544818268812)
XLA Ops:
  1.9 4.1 %collective-permute-start = (bf16[8,5120]{1,0:T(8,128)(2,1)S(1)}, bf16[8,5120]{1,0:T(8,128)(2,1)S(1)}, u32[]{:S(2)}, u32[]{:S(2)}) collective-permute-start(bf16[8,5120]{1,0:T(8,128)(2,1)S(1)} %get-tuple-element.34), channel_id=1, source_target_pairs={{0,8},{1,9},{2,10},{3,11},{4,12},{5,13},{6,14},{7,15},{8,0},{9,1},... | collective-permute-start | bytes 245768 | tf_op jit(solution)/shard_map/ppermute | solution.py:34
  6.0 1.6 %collective-permute-start.1 = (bf16[8,5120]{1,0:T(8,128)(2,1)S(1)}, bf16[8,5120]{1,0:T(8,128)(2,1)S(1)}, u32[]{:S(2)}, u32[]{:S(2)}) collective-permute-start(bf16[8,5120]{1,0:T(8,128)(2,1)S(1)} %get-tuple-element.34), channel_id=1, source_target_pairs={{0,4},{1,5},{2,6},{3,7},{4,0},{5,1},{6,2},{7,3},{8,12},{9,13},{10,... | collective-permute-start | bytes 245768 | tf_op jit(solution)/shard_map/ppermute | solution.py:34
  7.5 1.7 %collective-permute-start.3 = (bf16[8,3072]{1,0:T(8,128)(2,1)S(1)}, bf16[8,3072]{1,0:T(8,128)(2,1)S(1)}, u32[]{:S(2)}, u32[]{:S(2)}) collective-permute-start(bf16[8,3072]{1,0:T(8,128)(2,1)S(1)} %get-tuple-element.35), channel_id=1, source_target_pairs={{0,2},{1,3},{2,0},{3,1},{4,6},{5,7},{6,4},{7,5},{8,10},{9,11},{10,... | collective-permute-start | bytes 147464 | tf_op jit(solution)/shard_map/ppermute | solution.py:34
  11.8 1.7 %pad_maximum_fusion.refs_5_.refs_9_ = bf16[128,8192]{1,0:T(8,128)(2,1)S(1)} fusion(bf16[64,8192]{1,0:T(8,128)(2,1)} %bitcast.23, bf16[64,8192]{1,0:T(8,128)(2,1)} %bitcast.24), kind=kLoop, calls=%fused_computation | loop fusion | flops 4194304 | bytes 4194304 | tf_op jit(solution)/shard_map/concatenate | solution.py:580
  14.0 1.5 %collective-permute-start.4 = (bf16[32,5120]{1,0:T(8,128)(2,1)S(1)}, bf16[32,5120]{1,0:T(8,128)(2,1)S(1)}, u32[]{:S(2)}, u32[]{:S(2)}) collective-permute-start(bf16[32,5120]{1,0:T(8,128)(2,1)S(1)} %pad_maximum_fusion.1.refs_0_), channel_id=1, source_target_pairs={{0,2},{1,3},{2,0},{3,1},{4,6},{5,7},{6,4},{7,5},{8,10},{9,11},{10,... | collective-permute-start | bytes 983048 | tf_op jit(solution)/shard_map/ppermute | solution.py:34
  15.5 2.5 %collective-permute-start.5 = (bf16[16,3072]{1,0:T(8,128)(2,1)S(1)}, bf16[16,3072]{1,0:T(8,128)(2,1)S(1)}, u32[]{:S(2)}, u32[]{:S(2)}) collective-permute-start(bf16[16,3072]{1,0:T(8,128)(2,1)S(1)} %pad_maximum_fusion.2.refs_0_), channel_id=1, source_target_pairs={{0,8},{1,9},{2,10},{3,11},{4,12},{5,13},{6,14},{7,15},{8,0},{9,1},... | collective-permute-start | bytes 294920 | tf_op jit(solution)/shard_map/ppermute | solution.py:34
  19.9 3.4 %fetch.2.refs_4_.refs_8_ = bf16[8192,512]{1,0:T(8,128)(2,1)S(1)} custom-call(bf16[8192,512]{1,0:T(8,128)(2,1)} %refs_0_), custom_call_target="tpu_custom_call" | custom-call | bytes 16777216 | tf_op jit(solution)/shard_map/fetch/pallas_call | solution.py:249
  24.2 2.7 %collective-permute-done.6.refs_2_ = bf16[16,3072]{1,0:T(8,128)(2,1)S(1)} collective-permute-done((bf16[16,3072]{1,0:T(8,128)(2,1)S(1)}, bf16[16,3072]{1,0:T(8,128)(2,1)S(1)}, u32[]{:S(2)}, u32[]{:S(2)}) %collective-permute-start.6) | collective-permute-done | bytes 98336 | tf_op jit(solution)/shard_map/ppermute | solution.py:34
  29.8 1.7 %project.3 = bf16[256,640]{1,0:T(8,128)(2,1)} custom-call(bf16[16,3072]{1,0:T(8,128)(2,1)S(1)} %pad_maximum_fusion.2.refs_0_, bf16[16,3072]{1,0:T(8,128)(2,1)S(1)} %collective-permute-done.5.refs_1_, bf16[16,3072]{1,0:T(8,128)(2,1)S(1)} %collective-permute-done.6.refs_2_, bf16[16,3072]{1,0:T(8,128)(2,1)S(1)} %collective-permute-done.7.refs_3_, ...), custom_call_target="tpu_custom_call" | custom-call | flops 503316480 | bytes 3932160 | tf_op jit(solution)/shard_map/project/pallas_call | solution.py:327
  31.5 4.8 %all-to-all-start = ((bf16[16,16,640]{2,1,0:T(8,128)(2,1)}), bf16[16,16,640]{2,1,0:T(8,128)(2,1)S(1)}, u32[]{:S(2)}, u32[]{:S(2)}) async-start(bf16[16,16,640]{2,1,0:T(8,128)(2,1)} %bitcast.5), calls=%async_computation | async-start | bytes 655360 | tf_op jit(solution)/shard_map/all_to_all | solution.py:605
  37.7 9.7 %all-to-all-done.inbound = bf16[16,16,640]{2,1,0:T(8,128)(2,1)S(1)} async-done(((bf16[16,16,640]{2,1,0:T(8,128)(2,1)}), bf16[16,16,640]{2,1,0:T(8,128)(2,1)S(1)}, u32[]{:S(2)}, u32[]{:S(2)}) %all-to-all-start) | async-done | bytes 327712 | tf_op jit(solution)/shard_map/all_to_all | solution.py:605
  47.3 8.4 %attend.1 = bf16[16,16,512]{2,1,0:T(8,128)(2,1)} custom-call(s32[16,4]{1,0:T(8,128)S(1)} %copy.21.table, s32[2,1,128]{2,1,0:T(1,128)S(1)} %bitcast.19, bf16[16,16,640]{2,1,0:T(8,128)(2,1)S(1)} %all-to-all-done.inbound, f32[16,128]{1,0:T(8,128)S(1)} %pad_maximum_fusion.3.cosine, f32[16,128]{1,0:T(8,128)S(1)} %pad_maximum_fusion.4.sine, ...), custom_call_target="tpu_custom_call" | custom-call | flops 134217728 | bytes 8388608 | tf_op jit(solution)/shard_map/attend/pallas_call | solution.py:510
  55.7 3.5 %all-to-all-start.1 = ((bf16[16,16,512]{2,1,0:T(8,128)(2,1)}), bf16[16,16,512]{2,1,0:T(8,128)(2,1)S(1)}, u32[]{:S(2)}, u32[]{:S(2)}) async-start(bf16[16,16,512]{2,1,0:T(8,128)(2,1)} %attend.1), calls=%async_computation.1 | async-start | bytes 524288 | tf_op jit(solution)/shard_map/all_to_all | solution.py:618
  60.2 1.8 %fetch.3.refs_0_ = bf16[512,2560]{1,0:T(8,128)(2,1)S(1)} custom-call(bf16[512,8192]{1,0:T(8,128)(2,1)} %w_out.3), custom_call_target="tpu_custom_call" | custom-call | bytes 5242880 | tf_op jit(solution)/shard_map/fetch/pallas_call | solution.py:249
  62.0 7.3 %all-to-all-done.1 = bf16[16,16,512]{2,1,0:T(8,128)(2,1)S(1)} async-done(((bf16[16,16,512]{2,1,0:T(8,128)(2,1)}), bf16[16,16,512]{2,1,0:T(8,128)(2,1)S(1)}, u32[]{:S(2)}, u32[]{:S(2)}) %all-to-all-start.1) | async-done | bytes 262176 | tf_op jit(solution)/shard_map/all_to_all | solution.py:618
  69.3 3.2 %product.2 = (bf16[64,5376]{1,0:T(8,128)(2,1)}, f32[64,5376]{1,0:T(8,128)S(1)}) custom-call(s32[1,128]{1,0:T(1,128)S(1)} %reshape_reshape.6.place, bf16[256,512]{1,0:T(8,128)(2,1)S(1)} %bitcast.16, bf16[512,8192]{1,0:T(8,128)(2,1)} %w_out.3, bf16[512,2560]{1,0:T(8,128)(2,1)S(1)} %fetch.3.refs_0_), custom_call_target="tpu_custom_call" | custom-call | flops 704643072 | bytes 2883584 | tf_op jit(solution)/shard_map/product/pallas_call | solution.py:147
  73.7 2.3 %product.3 = (bf16[64,2816]{1,0:T(8,128)(2,1)S(1)}, f32[64,2816]{1,0:T(8,128)S(1)}) custom-call(s32[1,128]{1,0:T(1,128)S(1)} %reshape_reshape.7.place, bf16[256,512]{1,0:T(8,128)(2,1)S(1)} %bitcast.17, bf16[512,8192]{1,0:T(8,128)(2,1)} %w_out.3), custom_call_target="tpu_custom_call" | custom-call | flops 369098752 | bytes 2883584 | tf_op jit(solution)/shard_map/product/pallas_call | solution.py:147
  76.8 1.2 %collective-permute-done.16 = bf16[64,2816]{1,0:T(8,128)(2,1)S(1)} collective-permute-done((bf16[64,2816]{1,0:T(8,128)(2,1)S(1)}, bf16[64,2816]{1,0:T(8,128)(2,1)S(1)}, u32[]{:S(2)}, u32[]{:S(2)}) %collective-permute-start.16) | collective-permute-done | bytes 360480 | tf_op jit(solution)/shard_map/ppermute | solution.py:34
  80.0 2.7 %collective-permute-start.19 = (bf16[16,2816]{1,0:T(8,128)(2,1)S(1)}, bf16[16,2816]{1,0:T(8,128)(2,1)S(1)}, u32[]{:S(2)}, u32[]{:S(2)}) collective-permute-start(bf16[16,2816]{1,0:T(8,128)(2,1)S(1)} %get-tuple-element.69), channel_id=1, source_target_pairs={{0,12},{1,13},{2,14},{3,15},{4,8},{5,9},{6,10},{7,11},{8,4},{9,5},... | collective-permute-start | bytes 270344 | tf_op jit(solution)/shard_map/ppermute | solution.py:34
  82.7 4.2 %collective-permute-done.15 = bf16[32,5376]{1,0:T(8,128)(2,1)S(1)} collective-permute-done((bf16[32,5376]{1,0:T(8,128)(2,1)S(1)}, bf16[32,5376]{1,0:T(8,128)(2,1)S(1)}, u32[]{:S(2)}, u32[]{:S(2)}) %collective-permute-start.15) | collective-permute-done | bytes 344096 | tf_op jit(solution)/shard_map/ppermute | solution.py:34
  88.8 2.5 %collective-permute-start.20 = (bf16[8,5376]{1,0:T(8,128)(2,1)S(1)}, bf16[8,5376]{1,0:T(8,128)(2,1)S(1)}, u32[]{:S(2)}, u32[]{:S(2)}) collective-permute-start(bf16[8,5376]{1,0:T(8,128)(2,1)S(1)} %get-tuple-element.72), channel_id=1, source_target_pairs={{0,8},{1,9},{2,10},{3,11},{4,12},{5,13},{6,14},{7,15},{8,0},{9,1},... | collective-permute-start | bytes 258056 | tf_op jit(solution)/shard_map/ppermute | solution.py:34
  91.3 2.0 %collective-permute-start.22 = (bf16[8,5376]{1,0:T(8,128)(2,1)S(1)}, bf16[8,5376]{1,0:T(8,128)(2,1)S(1)}, u32[]{:S(2)}, u32[]{:S(2)}) collective-permute-start(bf16[8,5376]{1,0:T(8,128)(2,1)S(1)} %get-tuple-element.73), channel_id=1, source_target_pairs={{0,12},{1,13},{2,14},{3,15},{4,8},{5,9},{6,10},{7,11},{8,4},{9,5},... | collective-permute-start | bytes 258056 | tf_op jit(solution)/shard_map/ppermute | solution.py:34
  93.3 4.4 %collective-permute-done.20 = bf16[8,5376]{1,0:T(8,128)(2,1)S(1)} collective-permute-done((bf16[8,5376]{1,0:T(8,128)(2,1)S(1)}, bf16[8,5376]{1,0:T(8,128)(2,1)S(1)}, u32[]{:S(2)}, u32[]{:S(2)}) %collective-permute-start.20) | collective-permute-done | bytes 86048 | tf_op jit(solution)/shard_map/ppermute | solution.py:34
  97.7 1.4 %collective-permute-done.22 = bf16[8,5376]{1,0:T(8,128)(2,1)S(1)} collective-permute-done((bf16[8,5376]{1,0:T(8,128)(2,1)S(1)}, bf16[8,5376]{1,0:T(8,128)(2,1)S(1)}, u32[]{:S(2)}, u32[]{:S(2)}) %collective-permute-start.22) | collective-permute-done | bytes 86048 | tf_op jit(solution)/shard_map/ppermute | solution.py:34
  (89 shorter events, 19.5 us)
Async XLA Ops:
  1.9 12.1 %collective-permute-start = (bf16[8,5120]{1,0:T(8,128)(2,1)S(1)}, bf16[8,5120]{1,0:T(8,128)(2,1)S(1)}, u32[]{:S(2)}, u32[]{:S(2)}) collective-permute-start(bf16[8,5120]{1,0:T(8,128)(2,1)S(1)} %get-tuple-element.34), channel_id=1, source_target_pairs={{0,8},{1,9},{2,10},{3,11},{4,12},{5,13},{6,14},{7,15},{8,0},{9,1},... | collective-permute-start | bytes 245768 | tf_op jit(solution)/shard_map/ppermute | solution.py:34
  6.0 8.0 %collective-permute-start.1 = (bf16[8,5120]{1,0:T(8,128)(2,1)S(1)}, bf16[8,5120]{1,0:T(8,128)(2,1)S(1)}, u32[]{:S(2)}, u32[]{:S(2)}) collective-permute-start(bf16[8,5120]{1,0:T(8,128)(2,1)S(1)} %get-tuple-element.34), channel_id=1, source_target_pairs={{0,4},{1,5},{2,6},{3,7},{4,0},{5,1},{6,2},{7,3},{8,12},{9,13},{10,... | collective-permute-start | bytes 245768 | tf_op jit(solution)/shard_map/ppermute | solution.py:34
  7.5 6.4 %collective-permute-start.2 = (bf16[8,5120]{1,0:T(8,128)(2,1)S(1)}, bf16[8,5120]{1,0:T(8,128)(2,1)S(1)}, u32[]{:S(2)}, u32[]{:S(2)}) collective-permute-start(bf16[8,5120]{1,0:T(8,128)(2,1)S(1)} %get-tuple-element.34), channel_id=1, source_target_pairs={{0,12},{1,13},{2,14},{3,15},{4,8},{5,9},{6,10},{7,11},{8,4},{9,5},... | collective-permute-start | bytes 245768 | tf_op jit(solution)/shard_map/ppermute | solution.py:34
  7.5 6.4 %collective-permute-start.3 = (bf16[8,3072]{1,0:T(8,128)(2,1)S(1)}, bf16[8,3072]{1,0:T(8,128)(2,1)S(1)}, u32[]{:S(2)}, u32[]{:S(2)}) collective-permute-start(bf16[8,3072]{1,0:T(8,128)(2,1)S(1)} %get-tuple-element.35), channel_id=1, source_target_pairs={{0,2},{1,3},{2,0},{3,1},{4,6},{5,7},{6,4},{7,5},{8,10},{9,11},{10,... | collective-permute-start | bytes 147464 | tf_op jit(solution)/shard_map/ppermute | solution.py:34
  14.0 12.9 %collective-permute-start.4 = (bf16[32,5120]{1,0:T(8,128)(2,1)S(1)}, bf16[32,5120]{1,0:T(8,128)(2,1)S(1)}, u32[]{:S(2)}, u32[]{:S(2)}) collective-permute-start(bf16[32,5120]{1,0:T(8,128)(2,1)S(1)} %pad_maximum_fusion.1.refs_0_), channel_id=1, source_target_pairs={{0,2},{1,3},{2,0},{3,1},{4,6},{5,7},{6,4},{7,5},{8,10},{9,11},{10,... | collective-permute-start | bytes 983048 | tf_op jit(solution)/shard_map/ppermute | solution.py:34
  15.5 12.5 %collective-permute-start.12 = (bf16[32,5120]{1,0:T(8,128)(2,1)S(1)}, bf16[32,5120]{1,0:T(8,128)(2,1)S(1)}, u32[]{:S(2)}, u32[]{:S(2)}) collective-permute-start(bf16[32,5120]{1,0:T(8,128)(2,1)S(1)} %pad_maximum_fusion.1.refs_0_), channel_id=1, source_target_pairs={{0,1},{1,0},{2,3},{3,2},{4,5},{5,4},{6,7},{7,6},{8,9},{9,8},{10,11... | collective-permute-start | bytes 983048 | tf_op jit(solution)/shard_map/ppermute | solution.py:34
  15.5 8.7 %collective-permute-start.5 = (bf16[16,3072]{1,0:T(8,128)(2,1)S(1)}, bf16[16,3072]{1,0:T(8,128)(2,1)S(1)}, u32[]{:S(2)}, u32[]{:S(2)}) collective-permute-start(bf16[16,3072]{1,0:T(8,128)(2,1)S(1)} %pad_maximum_fusion.2.refs_0_), channel_id=1, source_target_pairs={{0,8},{1,9},{2,10},{3,11},{4,12},{5,13},{6,14},{7,15},{8,0},{9,1},... | collective-permute-start | bytes 294920 | tf_op jit(solution)/shard_map/ppermute | solution.py:34
  17.9 9.0 %collective-permute-start.6 = (bf16[16,3072]{1,0:T(8,128)(2,1)S(1)}, bf16[16,3072]{1,0:T(8,128)(2,1)S(1)}, u32[]{:S(2)}, u32[]{:S(2)}) collective-permute-start(bf16[16,3072]{1,0:T(8,128)(2,1)S(1)} %pad_maximum_fusion.2.refs_0_), channel_id=1, source_target_pairs={{0,4},{1,5},{2,6},{3,7},{4,0},{5,1},{6,2},{7,3},{8,12},{9,13},{10,... | collective-permute-start | bytes 294920 | tf_op jit(solution)/shard_map/ppermute | solution.py:34
  18.8 8.1 %collective-permute-start.7 = (bf16[16,3072]{1,0:T(8,128)(2,1)S(1)}, bf16[16,3072]{1,0:T(8,128)(2,1)S(1)}, u32[]{:S(2)}, u32[]{:S(2)}) collective-permute-start(bf16[16,3072]{1,0:T(8,128)(2,1)S(1)} %pad_maximum_fusion.2.refs_0_), channel_id=1, source_target_pairs={{0,12},{1,13},{2,14},{3,15},{4,8},{5,9},{6,10},{7,11},{8,4},{9,5},... | collective-permute-start | bytes 294920 | tf_op jit(solution)/shard_map/ppermute | solution.py:34
  26.9 2.8 %collective-permute-start.10 = (bf16[16,3072]{1,0:T(8,128)(2,1)S(1)}, bf16[16,3072]{1,0:T(8,128)(2,1)S(1)}, u32[]{:S(2)}, u32[]{:S(2)}) collective-permute-start(bf16[16,3072]{1,0:T(8,128)(2,1)S(1)} %collective-permute-done.6.refs_2_), channel_id=1, source_target_pairs={{0,1},{1,0},{2,3},{3,2},{4,5},{5,4},{6,7},{7,6},{8,9},{9,8},{10,11... | collective-permute-start | bytes 294920 | tf_op jit(solution)/shard_map/ppermute | solution.py:34
  27.4 2.3 %collective-permute-start.11 = (bf16[16,3072]{1,0:T(8,128)(2,1)S(1)}, bf16[16,3072]{1,0:T(8,128)(2,1)S(1)}, u32[]{:S(2)}, u32[]{:S(2)}) collective-permute-start(bf16[16,3072]{1,0:T(8,128)(2,1)S(1)} %collective-permute-done.7.refs_3_), channel_id=1, source_target_pairs={{0,1},{1,0},{2,3},{3,2},{4,5},{5,4},{6,7},{7,6},{8,9},{9,8},{10,11... | collective-permute-start | bytes 294920 | tf_op jit(solution)/shard_map/ppermute | solution.py:34
  27.5 2.3 %collective-permute-start.8 = (bf16[16,3072]{1,0:T(8,128)(2,1)S(1)}, bf16[16,3072]{1,0:T(8,128)(2,1)S(1)}, u32[]{:S(2)}, u32[]{:S(2)}) collective-permute-start(bf16[16,3072]{1,0:T(8,128)(2,1)S(1)} %pad_maximum_fusion.2.refs_0_), channel_id=1, source_target_pairs={{0,1},{1,0},{2,3},{3,2},{4,5},{5,4},{6,7},{7,6},{8,9},{9,8},{10,11... | collective-permute-start | bytes 294920 | tf_op jit(solution)/shard_map/ppermute | solution.py:34
  31.5 15.9 %all-to-all-start = ((bf16[16,16,640]{2,1,0:T(8,128)(2,1)}), bf16[16,16,640]{2,1,0:T(8,128)(2,1)S(1)}, u32[]{:S(2)}, u32[]{:S(2)}) async-start(bf16[16,16,640]{2,1,0:T(8,128)(2,1)} %bitcast.5), calls=%async_computation | async-start | bytes 655360 | tf_op jit(solution)/shard_map/all_to_all | solution.py:605
  55.7 13.6 %all-to-all-start.1 = ((bf16[16,16,512]{2,1,0:T(8,128)(2,1)}), bf16[16,16,512]{2,1,0:T(8,128)(2,1)S(1)}, u32[]{:S(2)}, u32[]{:S(2)}) async-start(bf16[16,16,512]{2,1,0:T(8,128)(2,1)} %attend.1), calls=%async_computation.1 | async-start | bytes 524288 | tf_op jit(solution)/shard_map/all_to_all | solution.py:618
  73.6 2.4 %collective-permute-start.14 = (bf16[64,5376]{1,0:T(8,128)(2,1)}, bf16[64,5376]{1,0:T(8,128)(2,1)S(1)}, u32[]{:S(2)}, u32[]{:S(2)}) collective-permute-start(bf16[64,5376]{1,0:T(8,128)(2,1)} %get-tuple-element.54), channel_id=1, source_target_pairs={{0,1},{1,0},{2,3},{3,2},{4,5},{5,4},{6,7},{7,6},{8,9},{9,8},{10,11... | collective-permute-start | bytes 2064392 | tf_op jit(solution)/shard_map/ppermute | solution.py:34
  76.2 1.9 %collective-permute-start.16 = (bf16[64,2816]{1,0:T(8,128)(2,1)S(1)}, bf16[64,2816]{1,0:T(8,128)(2,1)S(1)}, u32[]{:S(2)}, u32[]{:S(2)}) collective-permute-start(bf16[64,2816]{1,0:T(8,128)(2,1)S(1)} %get-tuple-element.58), channel_id=1, source_target_pairs={{0,1},{1,0},{2,3},{3,2},{4,5},{5,4},{6,7},{7,6},{8,9},{9,8},{10,11... | collective-permute-start | bytes 1081352 | tf_op jit(solution)/shard_map/ppermute | solution.py:34
  76.8 10.0 %collective-permute-start.15 = (bf16[32,5376]{1,0:T(8,128)(2,1)S(1)}, bf16[32,5376]{1,0:T(8,128)(2,1)S(1)}, u32[]{:S(2)}, u32[]{:S(2)}) collective-permute-start(bf16[32,5376]{1,0:T(8,128)(2,1)S(1)} %slice.82), channel_id=1, source_target_pairs={{0,2},{1,3},{2,0},{3,1},{4,6},{5,7},{6,4},{7,5},{8,10},{9,11},{10,... | collective-permute-start | bytes 1032200 | tf_op jit(solution)/shard_map/ppermute | solution.py:34
  78.2 9.6 %collective-permute-start.17 = (bf16[16,2816]{1,0:T(8,128)(2,1)S(1)}, bf16[16,2816]{1,0:T(8,128)(2,1)S(1)}, u32[]{:S(2)}, u32[]{:S(2)}) collective-permute-start(bf16[16,2816]{1,0:T(8,128)(2,1)S(1)} %get-tuple-element.71), channel_id=1, source_target_pairs={{0,8},{1,9},{2,10},{3,11},{4,12},{5,13},{6,14},{7,15},{8,0},{9,1},... | collective-permute-start | bytes 270344 | tf_op jit(solution)/shard_map/ppermute | solution.py:34
  79.3 8.5 %collective-permute-start.18 = (bf16[16,2816]{1,0:T(8,128)(2,1)S(1)}, bf16[16,2816]{1,0:T(8,128)(2,1)S(1)}, u32[]{:S(2)}, u32[]{:S(2)}) collective-permute-start(bf16[16,2816]{1,0:T(8,128)(2,1)S(1)} %get-tuple-element.70), channel_id=1, source_target_pairs={{0,4},{1,5},{2,6},{3,7},{4,0},{5,1},{6,2},{7,3},{8,12},{9,13},{10,... | collective-permute-start | bytes 270344 | tf_op jit(solution)/shard_map/ppermute | solution.py:34
  80.0 7.8 %collective-permute-start.19 = (bf16[16,2816]{1,0:T(8,128)(2,1)S(1)}, bf16[16,2816]{1,0:T(8,128)(2,1)S(1)}, u32[]{:S(2)}, u32[]{:S(2)}) collective-permute-start(bf16[16,2816]{1,0:T(8,128)(2,1)S(1)} %get-tuple-element.69), channel_id=1, source_target_pairs={{0,12},{1,13},{2,14},{3,15},{4,8},{5,9},{6,10},{7,11},{8,4},{9,5},... | collective-permute-start | bytes 270344 | tf_op jit(solution)/shard_map/ppermute | solution.py:34
  87.9 5.4 %collective-permute-start.23 = (bf16[8,2816]{1,0:T(8,128)(2,1)S(1)}, bf16[8,2816]{1,0:T(8,128)(2,1)S(1)}, u32[]{:S(2)}, u32[]{:S(2)}) collective-permute-start(bf16[8,2816]{1,0:T(8,128)(2,1)S(1)} %slice.83), channel_id=1, source_target_pairs={{0,2},{1,3},{2,0},{3,1},{4,6},{5,7},{6,4},{7,5},{8,10},{9,11},{10,... | collective-permute-start | bytes 135176 | tf_op jit(solution)/shard_map/ppermute | solution.py:34
  88.8 8.8 %collective-permute-start.20 = (bf16[8,5376]{1,0:T(8,128)(2,1)S(1)}, bf16[8,5376]{1,0:T(8,128)(2,1)S(1)}, u32[]{:S(2)}, u32[]{:S(2)}) collective-permute-start(bf16[8,5376]{1,0:T(8,128)(2,1)S(1)} %get-tuple-element.72), channel_id=1, source_target_pairs={{0,8},{1,9},{2,10},{3,11},{4,12},{5,13},{6,14},{7,15},{8,0},{9,1},... | collective-permute-start | bytes 258056 | tf_op jit(solution)/shard_map/ppermute | solution.py:34
  91.3 6.4 %collective-permute-start.21 = (bf16[8,5376]{1,0:T(8,128)(2,1)S(1)}, bf16[8,5376]{1,0:T(8,128)(2,1)S(1)}, u32[]{:S(2)}, u32[]{:S(2)}) collective-permute-start(bf16[8,5376]{1,0:T(8,128)(2,1)S(1)} %get-tuple-element.74), channel_id=1, source_target_pairs={{0,4},{1,5},{2,6},{3,7},{4,0},{5,1},{6,2},{7,3},{8,12},{9,13},{10,... | collective-permute-start | bytes 258056 | tf_op jit(solution)/shard_map/ppermute | solution.py:34
  91.3 7.8 %collective-permute-start.22 = (bf16[8,5376]{1,0:T(8,128)(2,1)S(1)}, bf16[8,5376]{1,0:T(8,128)(2,1)S(1)}, u32[]{:S(2)}, u32[]{:S(2)}) collective-permute-start(bf16[8,5376]{1,0:T(8,128)(2,1)S(1)} %get-tuple-element.73), channel_id=1, source_target_pairs={{0,12},{1,13},{2,14},{3,15},{4,8},{5,9},{6,10},{7,11},{8,4},{9,5},... | collective-permute-start | bytes 258056 | tf_op jit(solution)/shard_map/ppermute | solution.py:34
  (9 other events, 44.2 us)

commit v14 on v11

--- a/solution.py
+++ b/solution.py
@@ -84,7 +84,7 @@
         for half in range(grid.half)
         if half or pair
     ]
-    beside_a, parts_b[1], second = lax.optimization_barrier((beside_a, parts_b[1], second(pair_b)))
+    beside_a, parts_b, second = lax.optimization_barrier((beside_a, parts_b, second(pair_b)))
     parts_a = [line_a, beside_a]
     parts_a += [grid.send(part, core=1) for part in parts_a]
     parts_b += [grid.send(part, core=1) for part in parts_b]
@@ -203,12 +203,11 @@
     got_a = grid.send(sent_a, near=1)
     xb = keep_b + wide(grid.send(after(away_b, sent_a), core=1))
     xb, got_b = direct(xb)
-    got_a, got_b[0] = lax.optimization_barrier((got_a, got_b[0]))
+    got_a, got_b = lax.optimization_barrier((got_a, got_b))
     xa, parts_a = direct(xa[:middle] + wide(got_a))
     xb = total(xb, got_b)
     middle = xb.shape[0] // 2
-    sent_b = after(narrow(xb[middle:]), parts_a[0])
-    xb = xb[:middle] + wide(grid.send(sent_b, near=1))
+    xb = xb[:middle] + wide(grid.send(narrow(xb[middle:]), near=1))
     xa = total(xa, parts_a)
     return jnp.concatenate([xa, xb], axis=1)
 
@@ -387,10 +386,13 @@
 
     cuts = 4
     size = key_pages.shape[0] // cuts
-    for i, (pool, on_chip) in enumerate(((key_pages, key_pool), (value_pages, value_pool))):
+
+    def fetch_pool(pool, on_chip, sem):
         for cut in range(cuts):
             part = pl.ds(cut * size, size)
-            pltpu.make_async_copy(pool.at[part], on_chip.at[part], sems.at[i]).start()
+            pltpu.make_async_copy(pool.at[part], on_chip.at[part], sem).start()
+
+    fetch_pool(key_pages, key_pool, sems.at[0])
 
     def held(pool, slot, columns):
         return [pool[table[slot, j], :, columns] for j in range(pages)]
@@ -434,17 +436,18 @@
         jnp.int32, (columns, columns), 1
     )
 
+    own_chances = {}
     pltpu.make_async_copy(key_pool, key_pool, sems.at[0]).wait()
-    own_chances = {}
-    for b in range(batches):
-        valid = row < lengths[b]
-        for p in range(pairs):
+    fetch_pool(value_pages, value_pool, sems.at[1])
+    for p in range(pairs):
+        columns_p = slice(p * 2 * HEAD, (p + 1) * 2 * HEAD)
+        for b in range(batches):
+            valid = row < lengths[b]
             turned = query_rot[p, b].T.astype(jnp.bfloat16)
             none = jnp.zeros_like(turned)
             wide = jnp.concatenate(
                 [jnp.where(first, turned, none), jnp.where(first, none, turned)], axis=0
             )
-            columns_p = slice(p * 2 * HEAD, (p + 1) * 2 * HEAD)
             keys = []
             for s in range(batch):
                 keys += held(key_pool, b * batch + s, columns_p)
@@ -469,11 +472,11 @@
             )
 
     pltpu.make_async_copy(value_pool, value_pool, sems.at[1]).wait()
-    for b in range(batches):
-        for s in range(batch):
-            for p in range(pairs):
+    for p in range(pairs):
+        columns_p = slice(p * 2 * HEAD, (p + 1) * 2 * HEAD)
+        for b in range(batches):
+            for s in range(batch):
                 mine = chance[p, b, pl.ds(s, pair, stride=batch)].astype(jnp.bfloat16)
-                columns_p = slice(p * 2 * HEAD, (p + 1) * 2 * HEAD)
                 values = held(value_pool, b * batch + s, columns_p)
                 both = jnp.dot(
                     mine, jnp.concatenate(values, axis=0), preferred_element_type=jnp.float32
@@ -482,8 +485,6 @@
                     [both[: pair // 2, :HEAD], both[pair // 2 :, HEAD:]], axis=0
                 )
                 mixed[p, b, pl.ds(s, pair, stride=batch)] = result
-
-    for p in range(pairs):
         for j in range(pair):
             head = p * pair + j
             g = head * kv_heads // heads

time: 101 us -> 96.7 us (0.957)
  waiting for transfers between devices: 39.4 us -> 34.1 us
  Pallas kernels: 17.3 us -> 19.2 us
    ppermute x24, waiting for transfers between devices: 22.5 us -> 17.2 us  [send(): return lax.ppermute(x, AXES, pairs)]
    pallas_call x1, Pallas kernels: 5.97 us -> 7.83 us  [attend(): pl.pallas_call(functools.partial(attend_kernel, per_query, per_key), in_s...]
    ppermute x24, starting transfers between devices: 26.2 us -> 24.8 us  [send(): return lax.ppermute(x, AXES, pairs)]
  transfers between devices with their start and end apart: 26 -> 26, of which waited for: 10 -> 11; matrix products, arithmetic and copies ran while one was open for 7% -> 8% of each run, Pallas kernels for 6% -> 7%
where the time goes in v14:
time: 96.7 us; the launch traced here: 96.1 us
  waiting for transfers between devices  34.1 us (35%)
  starting transfers between devices  32.6 us (34%)
  Pallas kernels  19.2 us (20%)
  other arithmetic  5.98 us (6%)
  local copies, waits for them, and re-layouts  4.01 us (4%)
    ppermute x24, starting transfers between devices, send(): return lax.ppermute(x, AXES, pairs)  24.8 us
    ppermute x24, waiting for transfers between devices, send(): return lax.ppermute(x, AXES, pairs)  17.2 us
    all_to_all x1, waiting for transfers between devices, on_device(): lax.all_to_all(outbound, AXES, split_axis=0, concat_axis=0, tiled=True)  10.3 us
    pallas_call x1, Pallas kernels, attend(): pl.pallas_call(functools.partial(attend_kernel, per_query, per_key), in_s...  7.83 us
    all_to_all x1, waiting for transfers between devices, on_device(): lax.all_to_all(attended, AXES, split_axis=0, concat_axis=0, tiled=True)  6.5 us
    pallas_call x2, Pallas kernels, fetch(): pl.pallas_call(functools.partial(fetch_kernel, starts), in_specs=[pl.Bloc...  5.14 us
    all_to_all x1, starting transfers between devices, on_device(): lax.all_to_all(outbound, AXES, split_axis=0, concat_axis=0, tiled=True)  4.25 us
    all_to_all x1, starting transfers between devices, on_device(): lax.all_to_all(attended, AXES, split_axis=0, concat_axis=0, tiled=True)  3.54 us
  transfers between devices with their start and end apart: 26, of which 11 were waited for; matrix products, arithmetic and copies ran while one was open for 8% of the time, Pallas kernels for 7%

profile of v14, /device:TPU:0, one launch (start us, length us, event | category | flops | bytes accessed | tf_op | source)
XLA Modules:
  0.0 96.1 jit_solution(17109084530461728769)
XLA Ops:
  1.9 4.1 %collective-permute-start = (bf16[8,5120]{1,0:T(8,128)(2,1)S(1)}, bf16[8,5120]{1,0:T(8,128)(2,1)S(1)}, u32[]{:S(2)}, u32[]{:S(2)}) collective-permute-start(bf16[8,5120]{1,0:T(8,128)(2,1)S(1)} %get-tuple-element.33), channel_id=1, source_target_pairs={{0,8},{1,9},{2,10},{3,11},{4,12},{5,13},{6,14},{7,15},{8,0},{9,1},... | collective-permute-start | bytes 245768 | tf_op jit(solution)/shard_map/ppermute | solution.py:34
  6.0 1.6 %collective-permute-start.1 = (bf16[8,5120]{1,0:T(8,128)(2,1)S(1)}, bf16[8,5120]{1,0:T(8,128)(2,1)S(1)}, u32[]{:S(2)}, u32[]{:S(2)}) collective-permute-start(bf16[8,5120]{1,0:T(8,128)(2,1)S(1)} %get-tuple-element.33), channel_id=1, source_target_pairs={{0,4},{1,5},{2,6},{3,7},{4,0},{5,1},{6,2},{7,3},{8,12},{9,13},{10,... | collective-permute-start | bytes 245768 | tf_op jit(solution)/shard_map/ppermute | solution.py:34
  7.5 1.7 %collective-permute-start.3 = (bf16[8,3072]{1,0:T(8,128)(2,1)S(1)}, bf16[8,3072]{1,0:T(8,128)(2,1)S(1)}, u32[]{:S(2)}, u32[]{:S(2)}) collective-permute-start(bf16[8,3072]{1,0:T(8,128)(2,1)S(1)} %get-tuple-element.34), channel_id=1, source_target_pairs={{0,2},{1,3},{2,0},{3,1},{4,6},{5,7},{6,4},{7,5},{8,10},{9,11},{10,... | collective-permute-start | bytes 147464 | tf_op jit(solution)/shard_map/ppermute | solution.py:34
  11.8 1.7 %pad_maximum_fusion.refs_5_.refs_9_ = bf16[128,8192]{1,0:T(8,128)(2,1)S(1)} fusion(bf16[64,8192]{1,0:T(8,128)(2,1)} %bitcast.22, bf16[64,8192]{1,0:T(8,128)(2,1)} %bitcast.23), kind=kLoop, calls=%fused_computation | loop fusion | flops 4194304 | bytes 4194304 | tf_op jit(solution)/shard_map/concatenate | solution.py:588
  14.0 1.5 %collective-permute-start.4 = (bf16[32,5120]{1,0:T(8,128)(2,1)S(1)}, bf16[32,5120]{1,0:T(8,128)(2,1)S(1)}, u32[]{:S(2)}, u32[]{:S(2)}) collective-permute-start(bf16[32,5120]{1,0:T(8,128)(2,1)S(1)} %pad_maximum_fusion.1.refs_0_), channel_id=1, source_target_pairs={{0,2},{1,3},{2,0},{3,1},{4,6},{5,7},{6,4},{7,5},{8,10},{9,11},{10,... | collective-permute-start | bytes 983048 | tf_op jit(solution)/shard_map/ppermute | solution.py:34
  15.5 2.5 %collective-permute-start.5 = (bf16[16,3072]{1,0:T(8,128)(2,1)S(1)}, bf16[16,3072]{1,0:T(8,128)(2,1)S(1)}, u32[]{:S(2)}, u32[]{:S(2)}) collective-permute-start(bf16[16,3072]{1,0:T(8,128)(2,1)S(1)} %pad_maximum_fusion.2.refs_0_), channel_id=1, source_target_pairs={{0,8},{1,9},{2,10},{3,11},{4,12},{5,13},{6,14},{7,15},{8,0},{9,1},... | collective-permute-start | bytes 294920 | tf_op jit(solution)/shard_map/ppermute | solution.py:34
  19.9 3.4 %fetch.2.refs_4_.refs_8_ = bf16[8192,512]{1,0:T(8,128)(2,1)S(1)} custom-call(bf16[8192,512]{1,0:T(8,128)(2,1)} %refs_0_), custom_call_target="tpu_custom_call" | custom-call | bytes 16777216 | tf_op jit(solution)/shard_map/fetch/pallas_call | solution.py:259
  23.3 2.0 %collective-permute-done.5.refs_1_ = bf16[16,3072]{1,0:T(8,128)(2,1)S(1)} collective-permute-done((bf16[16,3072]{1,0:T(8,128)(2,1)S(1)}, bf16[16,3072]{1,0:T(8,128)(2,1)S(1)}, u32[]{:S(2)}, u32[]{:S(2)}) %collective-permute-start.5) | collective-permute-done | bytes 98336 | tf_op jit(solution)/shard_map/ppermute | solution.py:34
  27.4 1.2 %project.2.refs_10_ = f32[128,640]{1,0:T(8,128)S(1)} custom-call(bf16[32,5120]{1,0:T(8,128)(2,1)S(1)} %pad_maximum_fusion.1.refs_0_, bf16[32,5120]{1,0:T(8,128)(2,1)S(1)} %collective-permute-done.4.refs_1_, bf16[32,5120]{1,0:T(8,128)(2,1)S(1)} %collective-permute-done.12.refs_2_, bf16[32,5120]{1,0:T(8,128)(2,1)S(1)} %collective-permute-done.13.refs_3_, ...), custom_call_target="tpu_custom_call" | custom-call | flops 838860800 | bytes 6553600 | tf_op jit(solution)/shard_map/project/pallas_call | solution.py:337
  28.6 1.7 %project.3 = bf16[256,640]{1,0:T(8,128)(2,1)} custom-call(bf16[16,3072]{1,0:T(8,128)(2,1)S(1)} %pad_maximum_fusion.2.refs_0_, bf16[16,3072]{1,0:T(8,128)(2,1)S(1)} %collective-permute-done.5.refs_1_, bf16[16,3072]{1,0:T(8,128)(2,1)S(1)} %collective-permute-done.6.refs_2_, bf16[16,3072]{1,0:T(8,128)(2,1)S(1)} %collective-permute-done.7.refs_3_, ...), custom_call_target="tpu_custom_call" | custom-call | flops 503316480 | bytes 3932160 | tf_op jit(solution)/shard_map/project/pallas_call | solution.py:337
  30.3 4.3 %all-to-all-start = ((bf16[16,16,640]{2,1,0:T(8,128)(2,1)}), bf16[16,16,640]{2,1,0:T(8,128)(2,1)S(1)}, u32[]{:S(2)}, u32[]{:S(2)}) async-start(bf16[16,16,640]{2,1,0:T(8,128)(2,1)} %bitcast.5), calls=%async_computation | async-start | bytes 655360 | tf_op jit(solution)/shard_map/all_to_all | solution.py:613
  35.3 10.3 %all-to-all-done.inbound = bf16[16,16,640]{2,1,0:T(8,128)(2,1)S(1)} async-done(((bf16[16,16,640]{2,1,0:T(8,128)(2,1)}), bf16[16,16,640]{2,1,0:T(8,128)(2,1)S(1)}, u32[]{:S(2)}, u32[]{:S(2)}) %all-to-all-start) | async-done | bytes 327712 | tf_op jit(solution)/shard_map/all_to_all | solution.py:613
  45.7 7.8 %attend.1 = bf16[16,16,512]{2,1,0:T(8,128)(2,1)} custom-call(s32[16,4]{1,0:T(8,128)S(1)} %copy.21.table, s32[2,1,128]{2,1,0:T(1,128)S(1)} %bitcast.18, bf16[16,16,640]{2,1,0:T(8,128)(2,1)S(1)} %all-to-all-done.inbound, f32[16,128]{1,0:T(8,128)S(1)} %pad_maximum_fusion.3.cosine, f32[16,128]{1,0:T(8,128)S(1)} %pad_maximum_fusion.4.sine, ...), custom_call_target="tpu_custom_call" | custom-call | flops 134217728 | bytes 8388608 | tf_op jit(solution)/shard_map/attend/pallas_call | solution.py:518
  53.5 3.5 %all-to-all-start.1 = ((bf16[16,16,512]{2,1,0:T(8,128)(2,1)}), bf16[16,16,512]{2,1,0:T(8,128)(2,1)S(1)}, u32[]{:S(2)}, u32[]{:S(2)}) async-start(bf16[16,16,512]{2,1,0:T(8,128)(2,1)} %attend.1), calls=%async_computation.1 | async-start | bytes 524288 | tf_op jit(solution)/shard_map/all_to_all | solution.py:626
  58.8 1.8 %fetch.3.w_front = bf16[512,2560]{1,0:T(8,128)(2,1)S(1)} custom-call(bf16[512,8192]{1,0:T(8,128)(2,1)} %w_out.1), custom_call_target="tpu_custom_call" | custom-call | bytes 5242880 | tf_op jit(solution)/shard_map/fetch/pallas_call | solution.py:259
  60.6 6.5 %all-to-all-done.1 = bf16[16,16,512]{2,1,0:T(8,128)(2,1)S(1)} async-done(((bf16[16,16,512]{2,1,0:T(8,128)(2,1)}), bf16[16,16,512]{2,1,0:T(8,128)(2,1)S(1)}, u32[]{:S(2)}, u32[]{:S(2)}) %all-to-all-start.1) | async-done | bytes 262176 | tf_op jit(solution)/shard_map/all_to_all | solution.py:626
  67.1 3.2 %product.1 = (bf16[64,5376]{1,0:T(8,128)(2,1)S(1)}, f32[64,5376]{1,0:T(8,128)S(1)}, bf16[64,2816]{1,0:T(8,128)(2,1)S(1)}, f32[64,2816]{1,0:T(8,128)S(1)}) custom-call(s32[1,128]{1,0:T(1,128)S(1)} %reshape_reshape.6.place_a, s32[1,128]{1,0:T(1,128)S(1)} %reshape_reshape.7.place_b, bf16[256,512]{1,0:T(8,128)(2,1)S(1)} %bitcast.16, bf16[512,8192]{1,0:T(8,128)(2,1)} %w_out.1, ...), custom_call_target="tpu_custom_call" | custom-call | flops 1073741824 | bytes 8388608 | tf_op jit(solution)/shard_map/product/pallas_call | solution.py:165
  70.3 2.1 %collective-permute-done.14 = bf16[64,5376]{1,0:T(8,128)(2,1)S(1)} collective-permute-done((bf16[64,5376]{1,0:T(8,128)(2,1)S(1)}, bf16[64,5376]{1,0:T(8,128)(2,1)S(1)}, u32[]{:S(2)}, u32[]{:S(2)}) %collective-permute-start.14) | collective-permute-done | bytes 688160 | tf_op jit(solution)/shard_map/ppermute | solution.py:34
  76.1 2.9 %collective-permute-start.19 = (bf16[16,2816]{1,0:T(8,128)(2,1)S(1)}, bf16[16,2816]{1,0:T(8,128)(2,1)S(1)}, u32[]{:S(2)}, u32[]{:S(2)}) collective-permute-start(bf16[16,2816]{1,0:T(8,128)(2,1)S(1)} %get-tuple-element.67), channel_id=1, source_target_pairs={{0,12},{1,13},{2,14},{3,15},{4,8},{5,9},{6,10},{7,11},{8,4},{9,5},... | collective-permute-start | bytes 270344 | tf_op jit(solution)/shard_map/ppermute | solution.py:34
  79.0 4.2 %collective-permute-done.15 = bf16[32,5376]{1,0:T(8,128)(2,1)S(1)} collective-permute-done((bf16[32,5376]{1,0:T(8,128)(2,1)S(1)}, bf16[32,5376]{1,0:T(8,128)(2,1)S(1)}, u32[]{:S(2)}, u32[]{:S(2)}) %collective-permute-start.15) | collective-permute-done | bytes 344096 | tf_op jit(solution)/shard_map/ppermute | solution.py:34
  85.1 2.4 %collective-permute-start.20 = (bf16[8,5376]{1,0:T(8,128)(2,1)S(1)}, bf16[8,5376]{1,0:T(8,128)(2,1)S(1)}, u32[]{:S(2)}, u32[]{:S(2)}) collective-permute-start(bf16[8,5376]{1,0:T(8,128)(2,1)S(1)} %get-tuple-element.70), channel_id=1, source_target_pairs={{0,8},{1,9},{2,10},{3,11},{4,12},{5,13},{6,14},{7,15},{8,0},{9,1},... | collective-permute-start | bytes 258056 | tf_op jit(solution)/shard_map/ppermute | solution.py:34
  87.5 2.1 %collective-permute-start.22 = (bf16[8,5376]{1,0:T(8,128)(2,1)S(1)}, bf16[8,5376]{1,0:T(8,128)(2,1)S(1)}, u32[]{:S(2)}, u32[]{:S(2)}) collective-permute-start(bf16[8,5376]{1,0:T(8,128)(2,1)S(1)} %get-tuple-element.71), channel_id=1, source_target_pairs={{0,12},{1,13},{2,14},{3,15},{4,8},{5,9},{6,10},{7,11},{8,4},{9,5},... | collective-permute-start | bytes 258056 | tf_op jit(solution)/shard_map/ppermute | solution.py:34
  89.6 4.4 %collective-permute-done.20 = bf16[8,5376]{1,0:T(8,128)(2,1)S(1)} collective-permute-done((bf16[8,5376]{1,0:T(8,128)(2,1)S(1)}, bf16[8,5376]{1,0:T(8,128)(2,1)S(1)}, u32[]{:S(2)}, u32[]{:S(2)}) %collective-permute-start.20) | collective-permute-done | bytes 86048 | tf_op jit(solution)/shard_map/ppermute | solution.py:34
  94.0 1.4 %collective-permute-done.22 = bf16[8,5376]{1,0:T(8,128)(2,1)S(1)} collective-permute-done((bf16[8,5376]{1,0:T(8,128)(2,1)S(1)}, bf16[8,5376]{1,0:T(8,128)(2,1)S(1)}, u32[]{:S(2)}, u32[]{:S(2)}) %collective-permute-start.22) | collective-permute-done | bytes 86048 | tf_op jit(solution)/shard_map/ppermute | solution.py:34
  (84 shorter events, 17.7 us)
Async XLA Ops:
  1.9 12.1 %collective-permute-start = (bf16[8,5120]{1,0:T(8,128)(2,1)S(1)}, bf16[8,5120]{1,0:T(8,128)(2,1)S(1)}, u32[]{:S(2)}, u32[]{:S(2)}) collective-permute-start(bf16[8,5120]{1,0:T(8,128)(2,1)S(1)} %get-tuple-element.33), channel_id=1, source_target_pairs={{0,8},{1,9},{2,10},{3,11},{4,12},{5,13},{6,14},{7,15},{8,0},{9,1},... | collective-permute-start | bytes 245768 | tf_op jit(solution)/shard_map/ppermute | solution.py:34
  6.0 8.0 %collective-permute-start.1 = (bf16[8,5120]{1,0:T(8,128)(2,1)S(1)}, bf16[8,5120]{1,0:T(8,128)(2,1)S(1)}, u32[]{:S(2)}, u32[]{:S(2)}) collective-permute-start(bf16[8,5120]{1,0:T(8,128)(2,1)S(1)} %get-tuple-element.33), channel_id=1, source_target_pairs={{0,4},{1,5},{2,6},{3,7},{4,0},{5,1},{6,2},{7,3},{8,12},{9,13},{10,... | collective-permute-start | bytes 245768 | tf_op jit(solution)/shard_map/ppermute | solution.py:34
  7.5 6.4 %collective-permute-start.2 = (bf16[8,5120]{1,0:T(8,128)(2,1)S(1)}, bf16[8,5120]{1,0:T(8,128)(2,1)S(1)}, u32[]{:S(2)}, u32[]{:S(2)}) collective-permute-start(bf16[8,5120]{1,0:T(8,128)(2,1)S(1)} %get-tuple-element.33), channel_id=1, source_target_pairs={{0,12},{1,13},{2,14},{3,15},{4,8},{5,9},{6,10},{7,11},{8,4},{9,5},... | collective-permute-start | bytes 245768 | tf_op jit(solution)/shard_map/ppermute | solution.py:34
  7.5 6.4 %collective-permute-start.3 = (bf16[8,3072]{1,0:T(8,128)(2,1)S(1)}, bf16[8,3072]{1,0:T(8,128)(2,1)S(1)}, u32[]{:S(2)}, u32[]{:S(2)}) collective-permute-start(bf16[8,3072]{1,0:T(8,128)(2,1)S(1)} %get-tuple-element.34), channel_id=1, source_target_pairs={{0,2},{1,3},{2,0},{3,1},{4,6},{5,7},{6,4},{7,5},{8,10},{9,11},{10,... | collective-permute-start | bytes 147464 | tf_op jit(solution)/shard_map/ppermute | solution.py:34
  14.0 11.7 %collective-permute-start.4 = (bf16[32,5120]{1,0:T(8,128)(2,1)S(1)}, bf16[32,5120]{1,0:T(8,128)(2,1)S(1)}, u32[]{:S(2)}, u32[]{:S(2)}) collective-permute-start(bf16[32,5120]{1,0:T(8,128)(2,1)S(1)} %pad_maximum_fusion.1.refs_0_), channel_id=1, source_target_pairs={{0,2},{1,3},{2,0},{3,1},{4,6},{5,7},{6,4},{7,5},{8,10},{9,11},{10,... | collective-permute-start | bytes 983048 | tf_op jit(solution)/shard_map/ppermute | solution.py:34
  15.5 9.8 %collective-permute-start.5 = (bf16[16,3072]{1,0:T(8,128)(2,1)S(1)}, bf16[16,3072]{1,0:T(8,128)(2,1)S(1)}, u32[]{:S(2)}, u32[]{:S(2)}) collective-permute-start(bf16[16,3072]{1,0:T(8,128)(2,1)S(1)} %pad_maximum_fusion.2.refs_0_), channel_id=1, source_target_pairs={{0,8},{1,9},{2,10},{3,11},{4,12},{5,13},{6,14},{7,15},{8,0},{9,1},... | collective-permute-start | bytes 294920 | tf_op jit(solution)/shard_map/ppermute | solution.py:34
  17.9 7.8 %collective-permute-start.6 = (bf16[16,3072]{1,0:T(8,128)(2,1)S(1)}, bf16[16,3072]{1,0:T(8,128)(2,1)S(1)}, u32[]{:S(2)}, u32[]{:S(2)}) collective-permute-start(bf16[16,3072]{1,0:T(8,128)(2,1)S(1)} %pad_maximum_fusion.2.refs_0_), channel_id=1, source_target_pairs={{0,4},{1,5},{2,6},{3,7},{4,0},{5,1},{6,2},{7,3},{8,12},{9,13},{10,... | collective-permute-start | bytes 294920 | tf_op jit(solution)/shard_map/ppermute | solution.py:34
  18.8 7.0 %collective-permute-start.7 = (bf16[16,3072]{1,0:T(8,128)(2,1)S(1)}, bf16[16,3072]{1,0:T(8,128)(2,1)S(1)}, u32[]{:S(2)}, u32[]{:S(2)}) collective-permute-start(bf16[16,3072]{1,0:T(8,128)(2,1)S(1)} %pad_maximum_fusion.2.refs_0_), channel_id=1, source_target_pairs={{0,12},{1,13},{2,14},{3,15},{4,8},{5,9},{6,10},{7,11},{8,4},{9,5},... | collective-permute-start | bytes 294920 | tf_op jit(solution)/shard_map/ppermute | solution.py:34
  19.9 6.9 %collective-permute-start.12 = (bf16[32,5120]{1,0:T(8,128)(2,1)S(1)}, bf16[32,5120]{1,0:T(8,128)(2,1)S(1)}, u32[]{:S(2)}, u32[]{:S(2)}) collective-permute-start(bf16[32,5120]{1,0:T(8,128)(2,1)S(1)} %pad_maximum_fusion.1.refs_0_), channel_id=1, source_target_pairs={{0,1},{1,0},{2,3},{3,2},{4,5},{5,4},{6,7},{7,6},{8,9},{9,8},{10,11... | collective-permute-start | bytes 983048 | tf_op jit(solution)/shard_map/ppermute | solution.py:34
  25.7 2.8 %collective-permute-start.10 = (bf16[16,3072]{1,0:T(8,128)(2,1)S(1)}, bf16[16,3072]{1,0:T(8,128)(2,1)S(1)}, u32[]{:S(2)}, u32[]{:S(2)}) collective-permute-start(bf16[16,3072]{1,0:T(8,128)(2,1)S(1)} %collective-permute-done.6.refs_2_), channel_id=1, source_target_pairs={{0,1},{1,0},{2,3},{3,2},{4,5},{5,4},{6,7},{7,6},{8,9},{9,8},{10,11... | collective-permute-start | bytes 294920 | tf_op jit(solution)/shard_map/ppermute | solution.py:34
  26.2 2.3 %collective-permute-start.11 = (bf16[16,3072]{1,0:T(8,128)(2,1)S(1)}, bf16[16,3072]{1,0:T(8,128)(2,1)S(1)}, u32[]{:S(2)}, u32[]{:S(2)}) collective-permute-start(bf16[16,3072]{1,0:T(8,128)(2,1)S(1)} %collective-permute-done.7.refs_3_), channel_id=1, source_target_pairs={{0,1},{1,0},{2,3},{3,2},{4,5},{5,4},{6,7},{7,6},{8,9},{9,8},{10,11... | collective-permute-start | bytes 294920 | tf_op jit(solution)/shard_map/ppermute | solution.py:34
  26.3 2.3 %collective-permute-start.8 = (bf16[16,3072]{1,0:T(8,128)(2,1)S(1)}, bf16[16,3072]{1,0:T(8,128)(2,1)S(1)}, u32[]{:S(2)}, u32[]{:S(2)}) collective-permute-start(bf16[16,3072]{1,0:T(8,128)(2,1)S(1)} %pad_maximum_fusion.2.refs_0_), channel_id=1, source_target_pairs={{0,1},{1,0},{2,3},{3,2},{4,5},{5,4},{6,7},{7,6},{8,9},{9,8},{10,11... | collective-permute-start | bytes 294920 | tf_op jit(solution)/shard_map/ppermute | solution.py:34
  26.8 1.8 %collective-permute-start.9 = (bf16[16,3072]{1,0:T(8,128)(2,1)S(1)}, bf16[16,3072]{1,0:T(8,128)(2,1)S(1)}, u32[]{:S(2)}, u32[]{:S(2)}) collective-permute-start(bf16[16,3072]{1,0:T(8,128)(2,1)S(1)} %collective-permute-done.5.refs_1_), channel_id=1, source_target_pairs={{0,1},{1,0},{2,3},{3,2},{4,5},{5,4},{6,7},{7,6},{8,9},{9,8},{10,11... | collective-permute-start | bytes 294920 | tf_op jit(solution)/shard_map/ppermute | solution.py:34
  30.3 15.4 %all-to-all-start = ((bf16[16,16,640]{2,1,0:T(8,128)(2,1)}), bf16[16,16,640]{2,1,0:T(8,128)(2,1)S(1)}, u32[]{:S(2)}, u32[]{:S(2)}) async-start(bf16[16,16,640]{2,1,0:T(8,128)(2,1)} %bitcast.5), calls=%async_computation | async-start | bytes 655360 | tf_op jit(solution)/shard_map/all_to_all | solution.py:613
  53.5 13.6 %all-to-all-start.1 = ((bf16[16,16,512]{2,1,0:T(8,128)(2,1)}), bf16[16,16,512]{2,1,0:T(8,128)(2,1)S(1)}, u32[]{:S(2)}, u32[]{:S(2)}) async-start(bf16[16,16,512]{2,1,0:T(8,128)(2,1)} %attend.1), calls=%async_computation.1 | async-start | bytes 524288 | tf_op jit(solution)/shard_map/all_to_all | solution.py:626
  70.2 2.2 %collective-permute-start.14 = (bf16[64,5376]{1,0:T(8,128)(2,1)S(1)}, bf16[64,5376]{1,0:T(8,128)(2,1)S(1)}, u32[]{:S(2)}, u32[]{:S(2)}) collective-permute-start(bf16[64,5376]{1,0:T(8,128)(2,1)S(1)} %get-tuple-element.53), channel_id=1, source_target_pairs={{0,1},{1,0},{2,3},{3,2},{4,5},{5,4},{6,7},{7,6},{8,9},{9,8},{10,11... | collective-permute-start | bytes 2064392 | tf_op jit(solution)/shard_map/ppermute | solution.py:34
  72.8 10.3 %collective-permute-start.15 = (bf16[32,5376]{1,0:T(8,128)(2,1)S(1)}, bf16[32,5376]{1,0:T(8,128)(2,1)S(1)}, u32[]{:S(2)}, u32[]{:S(2)}) collective-permute-start(bf16[32,5376]{1,0:T(8,128)(2,1)S(1)} %slice.82), channel_id=1, source_target_pairs={{0,2},{1,3},{2,0},{3,1},{4,6},{5,7},{6,4},{7,5},{8,10},{9,11},{10,... | collective-permute-start | bytes 1032200 | tf_op jit(solution)/shard_map/ppermute | solution.py:34
  74.5 8.7 %collective-permute-start.17 = (bf16[16,2816]{1,0:T(8,128)(2,1)S(1)}, bf16[16,2816]{1,0:T(8,128)(2,1)S(1)}, u32[]{:S(2)}, u32[]{:S(2)}) collective-permute-start(bf16[16,2816]{1,0:T(8,128)(2,1)S(1)} %get-tuple-element.69), channel_id=1, source_target_pairs={{0,8},{1,9},{2,10},{3,11},{4,12},{5,13},{6,14},{7,15},{8,0},{9,1},... | collective-permute-start | bytes 270344 | tf_op jit(solution)/shard_map/ppermute | solution.py:34
  75.6 7.6 %collective-permute-start.18 = (bf16[16,2816]{1,0:T(8,128)(2,1)S(1)}, bf16[16,2816]{1,0:T(8,128)(2,1)S(1)}, u32[]{:S(2)}, u32[]{:S(2)}) collective-permute-start(bf16[16,2816]{1,0:T(8,128)(2,1)S(1)} %get-tuple-element.68), channel_id=1, source_target_pairs={{0,4},{1,5},{2,6},{3,7},{4,0},{5,1},{6,2},{7,3},{8,12},{9,13},{10,... | collective-permute-start | bytes 270344 | tf_op jit(solution)/shard_map/ppermute | solution.py:34
  76.1 8.0 %collective-permute-start.19 = (bf16[16,2816]{1,0:T(8,128)(2,1)S(1)}, bf16[16,2816]{1,0:T(8,128)(2,1)S(1)}, u32[]{:S(2)}, u32[]{:S(2)}) collective-permute-start(bf16[16,2816]{1,0:T(8,128)(2,1)S(1)} %get-tuple-element.67), channel_id=1, source_target_pairs={{0,12},{1,13},{2,14},{3,15},{4,8},{5,9},{6,10},{7,11},{8,4},{9,5},... | collective-permute-start | bytes 270344 | tf_op jit(solution)/shard_map/ppermute | solution.py:34
  84.2 5.4 %collective-permute-start.23 = (bf16[8,2816]{1,0:T(8,128)(2,1)S(1)}, bf16[8,2816]{1,0:T(8,128)(2,1)S(1)}, u32[]{:S(2)}, u32[]{:S(2)}) collective-permute-start(bf16[8,2816]{1,0:T(8,128)(2,1)S(1)} %slice.83), channel_id=1, source_target_pairs={{0,2},{1,3},{2,0},{3,1},{4,6},{5,7},{6,4},{7,5},{8,10},{9,11},{10,... | collective-permute-start | bytes 135176 | tf_op jit(solution)/shard_map/ppermute | solution.py:34
  85.1 8.9 %collective-permute-start.20 = (bf16[8,5376]{1,0:T(8,128)(2,1)S(1)}, bf16[8,5376]{1,0:T(8,128)(2,1)S(1)}, u32[]{:S(2)}, u32[]{:S(2)}) collective-permute-start(bf16[8,5376]{1,0:T(8,128)(2,1)S(1)} %get-tuple-element.70), channel_id=1, source_target_pairs={{0,8},{1,9},{2,10},{3,11},{4,12},{5,13},{6,14},{7,15},{8,0},{9,1},... | collective-permute-start | bytes 258056 | tf_op jit(solution)/shard_map/ppermute | solution.py:34
  87.5 6.5 %collective-permute-start.21 = (bf16[8,5376]{1,0:T(8,128)(2,1)S(1)}, bf16[8,5376]{1,0:T(8,128)(2,1)S(1)}, u32[]{:S(2)}, u32[]{:S(2)}) collective-permute-start(bf16[8,5376]{1,0:T(8,128)(2,1)S(1)} %get-tuple-element.72), channel_id=1, source_target_pairs={{0,4},{1,5},{2,6},{3,7},{4,0},{5,1},{6,2},{7,3},{8,12},{9,13},{10,... | collective-permute-start | bytes 258056 | tf_op jit(solution)/shard_map/ppermute | solution.py:34
  87.5 7.9 %collective-permute-start.22 = (bf16[8,5376]{1,0:T(8,128)(2,1)S(1)}, bf16[8,5376]{1,0:T(8,128)(2,1)S(1)}, u32[]{:S(2)}, u32[]{:S(2)}) collective-permute-start(bf16[8,5376]{1,0:T(8,128)(2,1)S(1)} %get-tuple-element.71), channel_id=1, source_target_pairs={{0,12},{1,13},{2,14},{3,15},{4,8},{5,9},{6,10},{7,11},{8,4},{9,5},... | collective-permute-start | bytes 258056 | tf_op jit(solution)/shard_map/ppermute | solution.py:34
  (7 other events, 38.3 us)

commit v15 on v14

--- a/solution.py
+++ b/solution.py
@@ -42,16 +42,6 @@
                 move[axis] = step
             places.append(tuple(move))
         return places
-
-    def blocks(self, sign, order):
-        rows = [
-            [
-                int(self.shifted(np.unravel_index(i, self.sizes), [sign * m for m in move]))
-                for move in self.moves(order)
-            ]
-            for i in range(self.size)
-        ]
-        return jnp.asarray(np.array(rows, np.int32))[lax.axis_index(AXES)]
 
 
 HALF, PAIR, NEAR, CORE = range(4)
@@ -149,7 +139,7 @@
 
 
 def product(place_a, place_b, returned, w_out, w_front, cut):
-    rows = place_a.shape[0]
+    rows = place_a.shape[1]
     depth, width = w_out.shape
     cuts = []
     front = w_front.shape[1]
@@ -176,7 +166,7 @@
             flops=2 * rows * depth * width, bytes_accessed=2 * depth * width, transcendentals=0
         ),
         name="product",
-    )(place_a.reshape(1, rows), place_b.reshape(1, rows), returned, w_out, w_front)
+    )(place_a, place_b, returned, w_out, w_front)
 
 
 def scatter_sum(grid, place_a, place_b, returned, w_out, w_front, cut):
@@ -229,9 +219,62 @@
         in_specs=[vmem, vmem],
         out_specs=[vmem] * len(widths),
         out_shape=[jax.ShapeDtypeStruct((x.shape[0], w), jnp.bfloat16) for w in widths],
-        compiler_params=pltpu.CompilerParams(vmem_limit_bytes=16 * 2**20),
+        compiler_params=pltpu.CompilerParams(vmem_limit_bytes=60 * 2**20),
         name="norm",
     )(x, gain.reshape(1, -1))
+
+
+def placing_kernel(sizes, slots, orders, kv_owner, *outs):
+    requests = kv_owner.shape[1]
+    row = lax.broadcasted_iota(jnp.int32, (requests, requests), 0)
+    column = lax.broadcasted_iota(jnp.int32, (requests, requests), 1)
+
+    def upright(x):
+        return jnp.sum(jnp.where(row == column, x, 0.0), axis=1, keepdims=True)
+
+    owner = kv_owner[...].astype(jnp.float32)
+    earlier = (upright(owner) == owner) & (row < column)
+    slot = jnp.sum(jnp.where(earlier, 1.0, 0.0), axis=0, keepdims=True)
+    place = owner * slots + slot
+    upright_place = upright(place)
+
+    tp = lax.axis_index("tp")
+    me = (lax.div(tp, 4), lax.rem(lax.div(tp, 2), 2), lax.rem(tp, 2), lax.axis_index("attn"))
+    rows_dev = requests // int(np.prod(sizes))
+    lane = lax.broadcasted_iota(jnp.int32, (1, requests), 1)
+    for order, out in zip(orders, outs):
+        if order is None:
+            out[...] = place.astype(jnp.int32)
+            continue
+        if not order:
+            out[...] = (tp * sizes[CORE] + me[CORE]) * slots + lane
+            continue
+        sign, axes = order
+        rest = lax.div(lane, rows_dev)
+        where = [None] * len(sizes)
+        for axis in reversed(axes):
+            move = lax.rem(rest, sizes[axis])
+            rest = lax.div(rest, sizes[axis])
+            where[axis] = lax.rem(me[axis] + sizes[axis] + sign * move, sizes[axis])
+        block = where[0]
+        for axis in range(1, len(sizes)):
+            block = block * sizes[axis] + where[axis]
+        source = block * rows_dev + lax.rem(lane, rows_dev)
+        moved = jnp.sum(jnp.where(row == source, upright_place, 0.0), axis=0, keepdims=True)
+        out[...] = moved.astype(jnp.int32)
+
+
+def placing(kv_owner, sizes, slots, orders):
+    requests = kv_owner.shape[0]
+    vmem = pl.BlockSpec(memory_space=pltpu.VMEM)
+    return pl.pallas_call(
+        functools.partial(placing_kernel, sizes, slots, orders),
+        in_specs=[vmem],
+        out_specs=[vmem] * len(orders),
+        out_shape=[jax.ShapeDtypeStruct((1, requests), jnp.int32)] * len(orders),
+        compiler_params=pltpu.CompilerParams(vmem_limit_bytes=16 * 2**20),
+        name="placing",
+    )(kv_owner.reshape(1, requests))
 
 
 def fetch_kernel(starts, *refs):
@@ -329,7 +372,7 @@
         args.append(before)
         specs.append(vmem)
     if last:
-        args.append(place.reshape(1, rows))
+        args.append(place)
         specs.append(vmem)
         out = jax.ShapeDtypeStruct((slots, row_width), jnp.bfloat16)
     else:
@@ -384,7 +427,7 @@
     batches = query_rot.shape[1]
     batch = slots // batches
 
-    cuts = 4
+    cuts = 16
     size = key_pages.shape[0] // cuts
 
     def fetch_pool(pool, on_chip, sem):
@@ -393,6 +436,7 @@
             pltpu.make_async_copy(pool.at[part], on_chip.at[part], sem).start()
 
     fetch_pool(key_pages, key_pool, sems.at[0])
+    fetch_pool(value_pages, value_pool, sems.at[1])
 
     def held(pool, slot, columns):
         return [pool[table[slot, j], :, columns] for j in range(pages)]
@@ -438,7 +482,6 @@
 
     own_chances = {}
     pltpu.make_async_copy(key_pool, key_pool, sems.at[0]).wait()
-    fetch_pool(value_pages, value_pool, sems.at[1])
     for p in range(pairs):
         columns_p = slice(p * 2 * HEAD, (p + 1) * 2 * HEAD)
         for b in range(batches):
@@ -569,38 +612,26 @@
     cut = width // 8 * 5
     xa, xb = norm(hidden_in, norm_gain, (cut, width - cut))
 
-    def placed(kv_owner):
-        order = jnp.arange(requests, dtype=jnp.int32)
-        earlier = (kv_owner[:, None] == kv_owner[None, :]) & (order[None, :] < order[:, None])
-        return kv_owner * slot_count + jnp.sum(earlier.astype(jnp.int32), axis=1)
-
-    def reordered(place, blocks):
-        pick = blocks[:, None] == jnp.arange(owners, dtype=jnp.int32)[None, :]
-        moved = jnp.where(pick[:, :, None], place.reshape(1, owners, rows_dev), 0)
-        return jnp.sum(moved, axis=1).reshape(requests)
-
     def first(x):
-        place = placed(after(kv_owner, x))
+        orders = (None, (-1, ORDER_A), (1, ORDER_A), (1, ORDER_B), ())
+        places = placing(after(kv_owner, x), grid.sizes, slot_count, orders)
         pieces = [after(w_key, x).T, w_value.T]
         spare = row_width - per_query - 2 * per_key
         if spare:
             pieces.append(jnp.zeros((spare, width), w_key.dtype))
-        return place, reordered(place, grid.blocks(-1, ORDER_A)), jnp.concatenate(pieces, axis=0)
+        return places, jnp.concatenate(pieces, axis=0)
 
     def second(x):
         return fetch((after(w_query, x), None), limit=44)[0]
 
     parts_a, parts_b, others, w_query = gather_rows(grid, xa, xb, first, second)
-    place, place_in, w_kv_t = others
+    (place, place_in, place_a, place_b, mine), w_kv_t = others
     plain = list(range(owners))
     total = project(0, parts_a, plain, w_query, w_kv_t, None, None, all_slots)
     total = project(cut, parts_b, order_b, w_query, w_kv_t, total, place_in, all_slots)
     outbound = total.reshape(owners, slot_count, row_width)
-    place = after(place, outbound)
-    place_a = reordered(place, grid.blocks(1, ORDER_A))
-    place_b = reordered(place, grid.blocks(1, ORDER_B))
-    mine = jnp.asarray(np.arange(all_slots, dtype=np.int32).reshape(owners, slot_count))
-    mine = mine[lax.axis_index(AXES)]
+    place = after(place, outbound).reshape(requests)
+    mine = mine[0, :slot_count]
     lengths = jnp.sum(jnp.where(place[:, None] == mine[None, :], cached[:, None], 0), axis=0)
     halfway = HEAD // 2
     offsets = jnp.arange(halfway, dtype=jnp.float32)

time: 96.7 us -> 95.3 us (0.986)
  waiting for transfers between devices: 34.1 us -> 39.7 us
  local copies, waits for them, and re-layouts: 4.01 us -> 0.37 us
  other arithmetic: 5.98 us -> 3.29 us
    ppermute x24, waiting for transfers between devices: 17.2 us -> 21 us  [send(): return lax.ppermute(x, AXES, pairs)]
    pallas_call x1, Pallas kernels: 7.83 us -> 5.88 us  [attend(): pl.pallas_call(functools.partial(attend_kernel, per_query, per_key), in_s...]
    reduce_sum x3 -> x0, other arithmetic: 1.88 us -> none  [the longest x2 0.98 us: reordered(): return jnp.sum(moved, axis=1).reshape(requests)]
    all_to_all x1, waiting for transfers between devices: 6.5 us -> 8.25 us  [on_device(): lax.all_to_all(attended, AXES, split_axis=0, concat_axis=0, tiled=True)]
    unnamed x10 -> x12, local copies, waits for them, and re-layouts: 1.68 us -> 0.03 us
    pallas_call x1, Pallas kernels: 0.18 us -> 1.74 us  [norm(): pl.pallas_call(norm_kernel, in_specs=[vmem, vmem], out_specs=[vmem] * len...]
    eq x2 -> x1, local copies, waits for them, and re-layouts: 1.42 us -> 0.01 us  [on_device(): place[:, None] == mine[None, :]]
  transfers between devices with their start and end apart: 26 -> 26, of which waited for: 11 -> 13; matrix products, arithmetic and copies ran while one was open for 8% -> 3% of each run, Pallas kernels for 7% -> 7%
where the time goes in v15:
time: 95.3 us; the launch traced here: 94.9 us
  waiting for transfers between devices  39.7 us (42%)
  starting transfers between devices  32.3 us (34%)
  Pallas kernels  19 us (20%)
  other arithmetic  3.29 us (3%)
    ppermute x24, starting transfers between devices, send(): return lax.ppermute(x, AXES, pairs)  24.9 us
    ppermute x24, waiting for transfers between devices, send(): return lax.ppermute(x, AXES, pairs)  21 us
    all_to_all x1, waiting for transfers between devices, on_device(): lax.all_to_all(outbound, AXES, split_axis=0, concat_axis=0, tiled=True)  10.4 us
    all_to_all x1, waiting for transfers between devices, on_device(): lax.all_to_all(attended, AXES, split_axis=0, concat_axis=0, tiled=True)  8.25 us
    pallas_call x1, Pallas kernels, attend(): pl.pallas_call(functools.partial(attend_kernel, per_query, per_key), in_s...  5.88 us
    pallas_call x2, Pallas kernels, fetch(): pl.pallas_call(functools.partial(fetch_kernel, starts), in_specs=[pl.Bloc...  5.14 us
    all_to_all x1, starting transfers between devices, on_device(): lax.all_to_all(outbound, AXES, split_axis=0, concat_axis=0, tiled=True)  3.78 us
    all_to_all x1, starting transfers between devices, on_device(): lax.all_to_all(attended, AXES, split_axis=0, concat_axis=0, tiled=True)  3.54 us
  transfers between devices with their start and end apart: 26, of which 13 were waited for; matrix products, arithmetic and copies ran while one was open for 3% of the time, Pallas kernels for 7%

profile of v15, /device:TPU:0, one launch (start us, length us, event | category | flops | bytes accessed | tf_op | source)
XLA Modules:
  0.0 94.9 jit_solution(16075018255976165042)
XLA Ops:
  0.0 1.7 %norm.1 = (bf16[8,5120]{1,0:T(8,128)(2,1)}, bf16[8,3072]{1,0:T(8,128)(2,1)}) custom-call(bf16[8,8192]{1,0:T(8,128)(2,1)} %x.1, f32[1,8192]{1,0:T(1,128)} %bitcast.21), custom_call_target="tpu_custom_call" | custom-call | tf_op jit(solution)/shard_map/norm/pallas_call | solution.py:217
  1.7 4.0 %collective-permute-start = (bf16[8,5120]{1,0:T(8,128)(2,1)}, bf16[8,5120]{1,0:T(8,128)(2,1)S(1)}, u32[]{:S(2)}, u32[]{:S(2)}) collective-permute-start(bf16[8,5120]{1,0:T(8,128)(2,1)} %get-tuple-element.41), channel_id=1, source_target_pairs={{0,8},{1,9},{2,10},{3,11},{4,12},{5,13},{6,14},{7,15},{8,0},{9,1},... | collective-permute-start | bytes 245768 | tf_op jit(solution)/shard_map/ppermute | solution.py:34
  7.4 1.7 %collective-permute-start.3 = (bf16[8,3072]{1,0:T(8,128)(2,1)}, bf16[8,3072]{1,0:T(8,128)(2,1)S(1)}, u32[]{:S(2)}, u32[]{:S(2)}) collective-permute-start(bf16[8,3072]{1,0:T(8,128)(2,1)} %get-tuple-element.42), channel_id=1, source_target_pairs={{0,2},{1,3},{2,0},{3,1},{4,6},{5,7},{6,4},{7,5},{8,10},{9,11},{10,... | collective-permute-start | bytes 147464 | tf_op jit(solution)/shard_map/ppermute | solution.py:34
  9.1 1.8 %pad_maximum_fusion.refs_5_.refs_9_ = bf16[128,8192]{1,0:T(8,128)(2,1)S(1)} fusion(bf16[64,8192]{1,0:T(8,128)(2,1)} %bitcast.19, bf16[64,8192]{1,0:T(8,128)(2,1)} %bitcast.20), kind=kLoop, calls=%fused_computation | loop fusion | flops 4194304 | bytes 4194304 | tf_op jit(solution)/shard_map/concatenate | solution.py:622
  11.7 2.1 %collective-permute-done.2 = bf16[8,5120]{1,0:T(8,128)(2,1)S(1)} collective-permute-done((bf16[8,5120]{1,0:T(8,128)(2,1)}, bf16[8,5120]{1,0:T(8,128)(2,1)S(1)}, u32[]{:S(2)}, u32[]{:S(2)}) %collective-permute-start.2) | collective-permute-done | bytes 81952 | tf_op jit(solution)/shard_map/ppermute | solution.py:34
  13.8 1.7 %collective-permute-start.4 = (bf16[32,5120]{1,0:T(8,128)(2,1)S(1)}, bf16[32,5120]{1,0:T(8,128)(2,1)S(1)}, u32[]{:S(2)}, u32[]{:S(2)}) collective-permute-start(bf16[32,5120]{1,0:T(8,128)(2,1)S(1)} %pad_maximum_fusion.1.refs_0_), channel_id=1, source_target_pairs={{0,2},{1,3},{2,0},{3,1},{4,6},{5,7},{6,4},{7,5},{8,10},{9,11},{10,... | collective-permute-start | bytes 983048 | tf_op jit(solution)/shard_map/ppermute | solution.py:34
  15.5 2.5 %collective-permute-start.5 = (bf16[16,3072]{1,0:T(8,128)(2,1)S(1)}, bf16[16,3072]{1,0:T(8,128)(2,1)S(1)}, u32[]{:S(2)}, u32[]{:S(2)}) collective-permute-start(bf16[16,3072]{1,0:T(8,128)(2,1)S(1)} %pad_maximum_fusion.2.refs_0_), channel_id=1, source_target_pairs={{0,8},{1,9},{2,10},{3,11},{4,12},{5,13},{6,14},{7,15},{8,0},{9,1},... | collective-permute-start | bytes 294920 | tf_op jit(solution)/shard_map/ppermute | solution.py:34
  18.0 1.9 %collective-permute-start.7 = (bf16[16,3072]{1,0:T(8,128)(2,1)S(1)}, bf16[16,3072]{1,0:T(8,128)(2,1)S(1)}, u32[]{:S(2)}, u32[]{:S(2)}) collective-permute-start(bf16[16,3072]{1,0:T(8,128)(2,1)S(1)} %pad_maximum_fusion.2.refs_0_), channel_id=1, source_target_pairs={{0,12},{1,13},{2,14},{3,15},{4,8},{5,9},{6,10},{7,11},{8,4},{9,5},... | collective-permute-start | bytes 294920 | tf_op jit(solution)/shard_map/ppermute | solution.py:34
  19.9 3.4 %fetch.2.refs_4_.refs_8_ = bf16[8192,512]{1,0:T(8,128)(2,1)S(1)} custom-call(bf16[8192,512]{1,0:T(8,128)(2,1)} %refs_0_), custom_call_target="tpu_custom_call" | custom-call | bytes 16777216 | tf_op jit(solution)/shard_map/fetch/pallas_call | solution.py:302
  24.3 2.6 %collective-permute-done.6.refs_2_ = bf16[16,3072]{1,0:T(8,128)(2,1)S(1)} collective-permute-done((bf16[16,3072]{1,0:T(8,128)(2,1)S(1)}, bf16[16,3072]{1,0:T(8,128)(2,1)S(1)}, u32[]{:S(2)}, u32[]{:S(2)}) %collective-permute-start.6) | collective-permute-done | bytes 98336 | tf_op jit(solution)/shard_map/ppermute | solution.py:34
  29.8 1.7 %project.3 = bf16[256,640]{1,0:T(8,128)(2,1)} custom-call(bf16[16,3072]{1,0:T(8,128)(2,1)S(1)} %pad_maximum_fusion.2.refs_0_, bf16[16,3072]{1,0:T(8,128)(2,1)S(1)} %collective-permute-done.5.refs_1_, bf16[16,3072]{1,0:T(8,128)(2,1)S(1)} %collective-permute-done.6.refs_2_, bf16[16,3072]{1,0:T(8,128)(2,1)S(1)} %collective-permute-done.7.refs_3_, ...), custom_call_target="tpu_custom_call" | custom-call | flops 503316480 | bytes 3932160 | tf_op jit(solution)/shard_map/project/pallas_call | solution.py:380
  31.5 3.8 %all-to-all-start = ((bf16[16,16,640]{2,1,0:T(8,128)(2,1)}), bf16[16,16,640]{2,1,0:T(8,128)(2,1)S(1)}, u32[]{:S(2)}, u32[]{:S(2)}) async-start(bf16[16,16,640]{2,1,0:T(8,128)(2,1)} %bitcast.4), calls=%async_computation | async-start | bytes 655360 | tf_op jit(solution)/shard_map/all_to_all | solution.py:644
  36.0 10.4 %all-to-all-done.inbound = bf16[16,16,640]{2,1,0:T(8,128)(2,1)S(1)} async-done(((bf16[16,16,640]{2,1,0:T(8,128)(2,1)}), bf16[16,16,640]{2,1,0:T(8,128)(2,1)S(1)}, u32[]{:S(2)}, u32[]{:S(2)}) %all-to-all-start) | async-done | bytes 327712 | tf_op jit(solution)/shard_map/all_to_all | solution.py:644
  46.4 5.9 %attend.1 = bf16[16,16,512]{2,1,0:T(8,128)(2,1)} custom-call(s32[16,4]{1,0:T(8,128)S(1)} %copy.15.table, s32[2,1,128]{2,1,0:T(1,128)S(1)} %bitcast.14, bf16[16,16,640]{2,1,0:T(8,128)(2,1)S(1)} %all-to-all-done.inbound, f32[16,128]{1,0:T(8,128)S(1)} %get-tuple-element.90.cosine, f32[16,128]{1,0:T(8,128)S(1)} %get-tuple-element.91.sine, ...), custom_call_target="tpu_custom_call" | custom-call | flops 134217728 | bytes 8388608 | tf_op jit(solution)/shard_map/attend/pallas_call | solution.py:561
  52.3 3.5 %all-to-all-start.1 = ((bf16[16,16,512]{2,1,0:T(8,128)(2,1)}), bf16[16,16,512]{2,1,0:T(8,128)(2,1)S(1)}, u32[]{:S(2)}, u32[]{:S(2)}) async-start(bf16[16,16,512]{2,1,0:T(8,128)(2,1)} %attend.1), calls=%async_computation.1 | async-start | bytes 524288 | tf_op jit(solution)/shard_map/all_to_all | solution.py:657
  55.8 1.8 %fetch.3.w_front = bf16[512,2560]{1,0:T(8,128)(2,1)S(1)} custom-call(bf16[512,8192]{1,0:T(8,128)(2,1)} %w_out.1), custom_call_target="tpu_custom_call" | custom-call | bytes 5242880 | tf_op jit(solution)/shard_map/fetch/pallas_call | solution.py:302
  57.6 8.2 %all-to-all-done.1 = bf16[16,16,512]{2,1,0:T(8,128)(2,1)S(1)} async-done(((bf16[16,16,512]{2,1,0:T(8,128)(2,1)}), bf16[16,16,512]{2,1,0:T(8,128)(2,1)S(1)}, u32[]{:S(2)}, u32[]{:S(2)}) %all-to-all-start.1) | async-done | bytes 262176 | tf_op jit(solution)/shard_map/all_to_all | solution.py:657
  65.8 3.2 %product.1 = (bf16[64,5376]{1,0:T(8,128)(2,1)S(1)}, f32[64,5376]{1,0:T(8,128)S(1)}, bf16[64,2816]{1,0:T(8,128)(2,1)S(1)}, f32[64,2816]{1,0:T(8,128)S(1)}) custom-call(s32[1,128]{1,0:T(1,128)S(1)} %get-tuple-element.50.place_a, s32[1,128]{1,0:T(1,128)S(1)} %get-tuple-element.51.place_b, bf16[256,512]{1,0:T(8,128)(2,1)S(1)} %bitcast.13, ...), custom_call_target="tpu_custom_call" | custom-call | flops 1073741824 | bytes 8388608 | tf_op jit(solution)/shard_map/product/pallas_call | solution.py:155
  69.1 2.1 %collective-permute-done.14 = bf16[64,5376]{1,0:T(8,128)(2,1)S(1)} collective-permute-done((bf16[64,5376]{1,0:T(8,128)(2,1)S(1)}, bf16[64,5376]{1,0:T(8,128)(2,1)S(1)}, u32[]{:S(2)}, u32[]{:S(2)}) %collective-permute-start.14) | collective-permute-done | bytes 688160 | tf_op jit(solution)/shard_map/ppermute | solution.py:34
  74.9 2.9 %collective-permute-start.19 = (bf16[16,2816]{1,0:T(8,128)(2,1)S(1)}, bf16[16,2816]{1,0:T(8,128)(2,1)S(1)}, u32[]{:S(2)}, u32[]{:S(2)}) collective-permute-start(bf16[16,2816]{1,0:T(8,128)(2,1)S(1)} %get-tuple-element.81), channel_id=1, source_target_pairs={{0,12},{1,13},{2,14},{3,15},{4,8},{5,9},{6,10},{7,11},{8,4},{9,5},... | collective-permute-start | bytes 270344 | tf_op jit(solution)/shard_map/ppermute | solution.py:34
  77.7 4.2 %collective-permute-done.15 = bf16[32,5376]{1,0:T(8,128)(2,1)S(1)} collective-permute-done((bf16[32,5376]{1,0:T(8,128)(2,1)S(1)}, bf16[32,5376]{1,0:T(8,128)(2,1)S(1)}, u32[]{:S(2)}, u32[]{:S(2)}) %collective-permute-start.15) | collective-permute-done | bytes 344096 | tf_op jit(solution)/shard_map/ppermute | solution.py:34
  83.9 2.4 %collective-permute-start.20 = (bf16[8,5376]{1,0:T(8,128)(2,1)S(1)}, bf16[8,5376]{1,0:T(8,128)(2,1)S(1)}, u32[]{:S(2)}, u32[]{:S(2)}) collective-permute-start(bf16[8,5376]{1,0:T(8,128)(2,1)S(1)} %get-tuple-element.84), channel_id=1, source_target_pairs={{0,8},{1,9},{2,10},{3,11},{4,12},{5,13},{6,14},{7,15},{8,0},{9,1},... | collective-permute-start | bytes 258056 | tf_op jit(solution)/shard_map/ppermute | solution.py:34
  86.3 2.1 %collective-permute-start.22 = (bf16[8,5376]{1,0:T(8,128)(2,1)S(1)}, bf16[8,5376]{1,0:T(8,128)(2,1)S(1)}, u32[]{:S(2)}, u32[]{:S(2)}) collective-permute-start(bf16[8,5376]{1,0:T(8,128)(2,1)S(1)} %get-tuple-element.85), channel_id=1, source_target_pairs={{0,12},{1,13},{2,14},{3,15},{4,8},{5,9},{6,10},{7,11},{8,4},{9,5},... | collective-permute-start | bytes 258056 | tf_op jit(solution)/shard_map/ppermute | solution.py:34
  88.4 4.4 %collective-permute-done.20 = bf16[8,5376]{1,0:T(8,128)(2,1)S(1)} collective-permute-done((bf16[8,5376]{1,0:T(8,128)(2,1)S(1)}, bf16[8,5376]{1,0:T(8,128)(2,1)S(1)}, u32[]{:S(2)}, u32[]{:S(2)}) %collective-permute-start.20) | collective-permute-done | bytes 86048 | tf_op jit(solution)/shard_map/ppermute | solution.py:34
  (72 shorter events, 14.7 us)
Async XLA Ops:
  1.7 9.9 %collective-permute-start = (bf16[8,5120]{1,0:T(8,128)(2,1)}, bf16[8,5120]{1,0:T(8,128)(2,1)S(1)}, u32[]{:S(2)}, u32[]{:S(2)}) collective-permute-start(bf16[8,5120]{1,0:T(8,128)(2,1)} %get-tuple-element.41), channel_id=1, source_target_pairs={{0,8},{1,9},{2,10},{3,11},{4,12},{5,13},{6,14},{7,15},{8,0},{9,1},... | collective-permute-start | bytes 245768 | tf_op jit(solution)/shard_map/ppermute | solution.py:34
  5.8 5.9 %collective-permute-start.1 = (bf16[8,5120]{1,0:T(8,128)(2,1)}, bf16[8,5120]{1,0:T(8,128)(2,1)S(1)}, u32[]{:S(2)}, u32[]{:S(2)}) collective-permute-start(bf16[8,5120]{1,0:T(8,128)(2,1)} %get-tuple-element.41), channel_id=1, source_target_pairs={{0,4},{1,5},{2,6},{3,7},{4,0},{5,1},{6,2},{7,3},{8,12},{9,13},{10,... | collective-permute-start | bytes 245768 | tf_op jit(solution)/shard_map/ppermute | solution.py:34
  7.3 6.4 %collective-permute-start.2 = (bf16[8,5120]{1,0:T(8,128)(2,1)}, bf16[8,5120]{1,0:T(8,128)(2,1)S(1)}, u32[]{:S(2)}, u32[]{:S(2)}) collective-permute-start(bf16[8,5120]{1,0:T(8,128)(2,1)} %get-tuple-element.41), channel_id=1, source_target_pairs={{0,12},{1,13},{2,14},{3,15},{4,8},{5,9},{6,10},{7,11},{8,4},{9,5},... | collective-permute-start | bytes 245768 | tf_op jit(solution)/shard_map/ppermute | solution.py:34
  7.4 4.3 %collective-permute-start.3 = (bf16[8,3072]{1,0:T(8,128)(2,1)}, bf16[8,3072]{1,0:T(8,128)(2,1)S(1)}, u32[]{:S(2)}, u32[]{:S(2)}) collective-permute-start(bf16[8,3072]{1,0:T(8,128)(2,1)} %get-tuple-element.42), channel_id=1, source_target_pairs={{0,2},{1,3},{2,0},{3,1},{4,6},{5,7},{6,4},{7,5},{8,10},{9,11},{10,... | collective-permute-start | bytes 147464 | tf_op jit(solution)/shard_map/ppermute | solution.py:34
  13.8 13.1 %collective-permute-start.4 = (bf16[32,5120]{1,0:T(8,128)(2,1)S(1)}, bf16[32,5120]{1,0:T(8,128)(2,1)S(1)}, u32[]{:S(2)}, u32[]{:S(2)}) collective-permute-start(bf16[32,5120]{1,0:T(8,128)(2,1)S(1)} %pad_maximum_fusion.1.refs_0_), channel_id=1, source_target_pairs={{0,2},{1,3},{2,0},{3,1},{4,6},{5,7},{6,4},{7,5},{8,10},{9,11},{10,... | collective-permute-start | bytes 983048 | tf_op jit(solution)/shard_map/ppermute | solution.py:34
  15.5 12.5 %collective-permute-start.12 = (bf16[32,5120]{1,0:T(8,128)(2,1)S(1)}, bf16[32,5120]{1,0:T(8,128)(2,1)S(1)}, u32[]{:S(2)}, u32[]{:S(2)}) collective-permute-start(bf16[32,5120]{1,0:T(8,128)(2,1)S(1)} %pad_maximum_fusion.1.refs_0_), channel_id=1, source_target_pairs={{0,1},{1,0},{2,3},{3,2},{4,5},{5,4},{6,7},{7,6},{8,9},{9,8},{10,11... | collective-permute-start | bytes 983048 | tf_op jit(solution)/shard_map/ppermute | solution.py:34
  15.5 8.8 %collective-permute-start.5 = (bf16[16,3072]{1,0:T(8,128)(2,1)S(1)}, bf16[16,3072]{1,0:T(8,128)(2,1)S(1)}, u32[]{:S(2)}, u32[]{:S(2)}) collective-permute-start(bf16[16,3072]{1,0:T(8,128)(2,1)S(1)} %pad_maximum_fusion.2.refs_0_), channel_id=1, source_target_pairs={{0,8},{1,9},{2,10},{3,11},{4,12},{5,13},{6,14},{7,15},{8,0},{9,1},... | collective-permute-start | bytes 294920 | tf_op jit(solution)/shard_map/ppermute | solution.py:34
  18.0 9.0 %collective-permute-start.6 = (bf16[16,3072]{1,0:T(8,128)(2,1)S(1)}, bf16[16,3072]{1,0:T(8,128)(2,1)S(1)}, u32[]{:S(2)}, u32[]{:S(2)}) collective-permute-start(bf16[16,3072]{1,0:T(8,128)(2,1)S(1)} %pad_maximum_fusion.2.refs_0_), channel_id=1, source_target_pairs={{0,4},{1,5},{2,6},{3,7},{4,0},{5,1},{6,2},{7,3},{8,12},{9,13},{10,... | collective-permute-start | bytes 294920 | tf_op jit(solution)/shard_map/ppermute | solution.py:34
  18.0 8.9 %collective-permute-start.7 = (bf16[16,3072]{1,0:T(8,128)(2,1)S(1)}, bf16[16,3072]{1,0:T(8,128)(2,1)S(1)}, u32[]{:S(2)}, u32[]{:S(2)}) collective-permute-start(bf16[16,3072]{1,0:T(8,128)(2,1)S(1)} %pad_maximum_fusion.2.refs_0_), channel_id=1, source_target_pairs={{0,12},{1,13},{2,14},{3,15},{4,8},{5,9},{6,10},{7,11},{8,4},{9,5},... | collective-permute-start | bytes 294920 | tf_op jit(solution)/shard_map/ppermute | solution.py:34
  26.9 2.8 %collective-permute-start.10 = (bf16[16,3072]{1,0:T(8,128)(2,1)S(1)}, bf16[16,3072]{1,0:T(8,128)(2,1)S(1)}, u32[]{:S(2)}, u32[]{:S(2)}) collective-permute-start(bf16[16,3072]{1,0:T(8,128)(2,1)S(1)} %collective-permute-done.6.refs_2_), channel_id=1, source_target_pairs={{0,1},{1,0},{2,3},{3,2},{4,5},{5,4},{6,7},{7,6},{8,9},{9,8},{10,11... | collective-permute-start | bytes 294920 | tf_op jit(solution)/shard_map/ppermute | solution.py:34
  27.4 2.3 %collective-permute-start.11 = (bf16[16,3072]{1,0:T(8,128)(2,1)S(1)}, bf16[16,3072]{1,0:T(8,128)(2,1)S(1)}, u32[]{:S(2)}, u32[]{:S(2)}) collective-permute-start(bf16[16,3072]{1,0:T(8,128)(2,1)S(1)} %collective-permute-done.7.refs_3_), channel_id=1, source_target_pairs={{0,1},{1,0},{2,3},{3,2},{4,5},{5,4},{6,7},{7,6},{8,9},{9,8},{10,11... | collective-permute-start | bytes 294920 | tf_op jit(solution)/shard_map/ppermute | solution.py:34
  27.5 2.3 %collective-permute-start.8 = (bf16[16,3072]{1,0:T(8,128)(2,1)S(1)}, bf16[16,3072]{1,0:T(8,128)(2,1)S(1)}, u32[]{:S(2)}, u32[]{:S(2)}) collective-permute-start(bf16[16,3072]{1,0:T(8,128)(2,1)S(1)} %pad_maximum_fusion.2.refs_0_), channel_id=1, source_target_pairs={{0,1},{1,0},{2,3},{3,2},{4,5},{5,4},{6,7},{7,6},{8,9},{9,8},{10,11... | collective-permute-start | bytes 294920 | tf_op jit(solution)/shard_map/ppermute | solution.py:34
  27.9 1.9 %collective-permute-start.9 = (bf16[16,3072]{1,0:T(8,128)(2,1)S(1)}, bf16[16,3072]{1,0:T(8,128)(2,1)S(1)}, u32[]{:S(2)}, u32[]{:S(2)}) collective-permute-start(bf16[16,3072]{1,0:T(8,128)(2,1)S(1)} %collective-permute-done.5.refs_1_), channel_id=1, source_target_pairs={{0,1},{1,0},{2,3},{3,2},{4,5},{5,4},{6,7},{7,6},{8,9},{9,8},{10,11... | collective-permute-start | bytes 294920 | tf_op jit(solution)/shard_map/ppermute | solution.py:34
  31.5 14.9 %all-to-all-start = ((bf16[16,16,640]{2,1,0:T(8,128)(2,1)}), bf16[16,16,640]{2,1,0:T(8,128)(2,1)S(1)}, u32[]{:S(2)}, u32[]{:S(2)}) async-start(bf16[16,16,640]{2,1,0:T(8,128)(2,1)} %bitcast.4), calls=%async_computation | async-start | bytes 655360 | tf_op jit(solution)/shard_map/all_to_all | solution.py:644
  52.3 13.6 %all-to-all-start.1 = ((bf16[16,16,512]{2,1,0:T(8,128)(2,1)}), bf16[16,16,512]{2,1,0:T(8,128)(2,1)S(1)}, u32[]{:S(2)}, u32[]{:S(2)}) async-start(bf16[16,16,512]{2,1,0:T(8,128)(2,1)} %attend.1), calls=%async_computation.1 | async-start | bytes 524288 | tf_op jit(solution)/shard_map/all_to_all | solution.py:657
  69.0 2.2 %collective-permute-start.14 = (bf16[64,5376]{1,0:T(8,128)(2,1)S(1)}, bf16[64,5376]{1,0:T(8,128)(2,1)S(1)}, u32[]{:S(2)}, u32[]{:S(2)}) collective-permute-start(bf16[64,5376]{1,0:T(8,128)(2,1)S(1)} %get-tuple-element.69), channel_id=1, source_target_pairs={{0,1},{1,0},{2,3},{3,2},{4,5},{5,4},{6,7},{7,6},{8,9},{9,8},{10,11... | collective-permute-start | bytes 2064392 | tf_op jit(solution)/shard_map/ppermute | solution.py:34
  71.6 10.3 %collective-permute-start.15 = (bf16[32,5376]{1,0:T(8,128)(2,1)S(1)}, bf16[32,5376]{1,0:T(8,128)(2,1)S(1)}, u32[]{:S(2)}, u32[]{:S(2)}) collective-permute-start(bf16[32,5376]{1,0:T(8,128)(2,1)S(1)} %slice.87), channel_id=1, source_target_pairs={{0,2},{1,3},{2,0},{3,1},{4,6},{5,7},{6,4},{7,5},{8,10},{9,11},{10,... | collective-permute-start | bytes 1032200 | tf_op jit(solution)/shard_map/ppermute | solution.py:34
  73.3 8.7 %collective-permute-start.17 = (bf16[16,2816]{1,0:T(8,128)(2,1)S(1)}, bf16[16,2816]{1,0:T(8,128)(2,1)S(1)}, u32[]{:S(2)}, u32[]{:S(2)}) collective-permute-start(bf16[16,2816]{1,0:T(8,128)(2,1)S(1)} %get-tuple-element.83), channel_id=1, source_target_pairs={{0,8},{1,9},{2,10},{3,11},{4,12},{5,13},{6,14},{7,15},{8,0},{9,1},... | collective-permute-start | bytes 270344 | tf_op jit(solution)/shard_map/ppermute | solution.py:34
  74.4 7.6 %collective-permute-start.18 = (bf16[16,2816]{1,0:T(8,128)(2,1)S(1)}, bf16[16,2816]{1,0:T(8,128)(2,1)S(1)}, u32[]{:S(2)}, u32[]{:S(2)}) collective-permute-start(bf16[16,2816]{1,0:T(8,128)(2,1)S(1)} %get-tuple-element.82), channel_id=1, source_target_pairs={{0,4},{1,5},{2,6},{3,7},{4,0},{5,1},{6,2},{7,3},{8,12},{9,13},{10,... | collective-permute-start | bytes 270344 | tf_op jit(solution)/shard_map/ppermute | solution.py:34
  74.9 8.0 %collective-permute-start.19 = (bf16[16,2816]{1,0:T(8,128)(2,1)S(1)}, bf16[16,2816]{1,0:T(8,128)(2,1)S(1)}, u32[]{:S(2)}, u32[]{:S(2)}) collective-permute-start(bf16[16,2816]{1,0:T(8,128)(2,1)S(1)} %get-tuple-element.81), channel_id=1, source_target_pairs={{0,12},{1,13},{2,14},{3,15},{4,8},{5,9},{6,10},{7,11},{8,4},{9,5},... | collective-permute-start | bytes 270344 | tf_op jit(solution)/shard_map/ppermute | solution.py:34
  83.0 5.4 %collective-permute-start.23 = (bf16[8,2816]{1,0:T(8,128)(2,1)S(1)}, bf16[8,2816]{1,0:T(8,128)(2,1)S(1)}, u32[]{:S(2)}, u32[]{:S(2)}) collective-permute-start(bf16[8,2816]{1,0:T(8,128)(2,1)S(1)} %slice.88), channel_id=1, source_target_pairs={{0,2},{1,3},{2,0},{3,1},{4,6},{5,7},{6,4},{7,5},{8,10},{9,11},{10,... | collective-permute-start | bytes 135176 | tf_op jit(solution)/shard_map/ppermute | solution.py:34
  83.9 8.9 %collective-permute-start.20 = (bf16[8,5376]{1,0:T(8,128)(2,1)S(1)}, bf16[8,5376]{1,0:T(8,128)(2,1)S(1)}, u32[]{:S(2)}, u32[]{:S(2)}) collective-permute-start(bf16[8,5376]{1,0:T(8,128)(2,1)S(1)} %get-tuple-element.84), channel_id=1, source_target_pairs={{0,8},{1,9},{2,10},{3,11},{4,12},{5,13},{6,14},{7,15},{8,0},{9,1},... | collective-permute-start | bytes 258056 | tf_op jit(solution)/shard_map/ppermute | solution.py:34
  86.3 6.5 %collective-permute-start.21 = (bf16[8,5376]{1,0:T(8,128)(2,1)S(1)}, bf16[8,5376]{1,0:T(8,128)(2,1)S(1)}, u32[]{:S(2)}, u32[]{:S(2)}) collective-permute-start(bf16[8,5376]{1,0:T(8,128)(2,1)S(1)} %get-tuple-element.86), channel_id=1, source_target_pairs={{0,4},{1,5},{2,6},{3,7},{4,0},{5,1},{6,2},{7,3},{8,12},{9,13},{10,... | collective-permute-start | bytes 258056 | tf_op jit(solution)/shard_map/ppermute | solution.py:34
  86.3 7.9 %collective-permute-start.22 = (bf16[8,5376]{1,0:T(8,128)(2,1)S(1)}, bf16[8,5376]{1,0:T(8,128)(2,1)S(1)}, u32[]{:S(2)}, u32[]{:S(2)}) collective-permute-start(bf16[8,5376]{1,0:T(8,128)(2,1)S(1)} %get-tuple-element.85), channel_id=1, source_target_pairs={{0,12},{1,13},{2,14},{3,15},{4,8},{5,9},{6,10},{7,11},{8,4},{9,5},... | collective-permute-start | bytes 258056 | tf_op jit(solution)/shard_map/ppermute | solution.py:34
  (8 other events, 44.8 us)

commit v16 on v15

--- a/solution.py
+++ b/solution.py
@@ -202,10 +202,19 @@
     return jnp.concatenate([xa, xb], axis=1)
 
 
-def norm_kernel(x, gain, *outs):
-    inputs = x[...].astype(jnp.float32)
+def norm_kernel(x, gain, *refs):
+    outs, (rows, gains, sems) = refs[:-3], refs[-3:]
+    copies = [
+        pltpu.make_async_copy(x, rows, sems.at[0]),
+        pltpu.make_async_copy(gain, gains, sems.at[1]),
+    ]
+    for copy in copies:
+        copy.start()
+    copies[0].wait()
+    inputs = rows[...].astype(jnp.float32)
     factor = lax.rsqrt(jnp.mean(inputs * inputs, axis=1, keepdims=True) + epsilon)
-    normed = (inputs * factor * gain[...]).astype(jnp.bfloat16)
+    copies[1].wait()
+    normed = (inputs * factor * gains[...]).astype(jnp.bfloat16)
     start = 0
     for out in outs:
         out[...] = normed[:, start : start + out.shape[1]]
@@ -214,11 +223,17 @@
 
 def norm(x, gain, widths):
     vmem = pl.BlockSpec(memory_space=pltpu.VMEM)
+    hbm = pl.BlockSpec(memory_space=pl.ANY)
     return pl.pallas_call(
         norm_kernel,
-        in_specs=[vmem, vmem],
+        in_specs=[hbm, hbm],
         out_specs=[vmem] * len(widths),
         out_shape=[jax.ShapeDtypeStruct((x.shape[0], w), jnp.bfloat16) for w in widths],
+        scratch_shapes=[
+            pltpu.VMEM(x.shape, jnp.bfloat16),
+            pltpu.VMEM((1, x.shape[1]), jnp.float32),
+            pltpu.SemaphoreType.DMA((2,)),
+        ],
         compiler_params=pltpu.CompilerParams(vmem_limit_bytes=60 * 2**20),
         name="norm",
     )(x, gain.reshape(1, -1))
@@ -398,6 +413,7 @@
     per_query,
     per_key,
     table,
+    counts,
     lengths,
     inbound,
     cosine,
@@ -407,7 +423,8 @@
     out,
     key_pool,
     value_pool,
-    sems,
+    key_sems,
+    value_sems,
     key_new,
     query_rot,
     value_own,
@@ -427,19 +444,36 @@
     batches = query_rot.shape[1]
     batch = slots // batches
 
-    cuts = 16
-    size = key_pages.shape[0] // cuts
-
-    def fetch_pool(pool, on_chip, sem):
-        for cut in range(cuts):
-            part = pl.ds(cut * size, size)
-            pltpu.make_async_copy(pool.at[part], on_chip.at[part], sem).start()
-
-    fetch_pool(key_pages, key_pool, sems.at[0])
-    fetch_pool(value_pages, value_pool, sems.at[1])
-
-    def held(pool, slot, columns):
-        return [pool[table[slot, j], :, columns] for j in range(pages)]
+    def page_copy(pool, on_chip, sems, slot, j):
+        rows = pl.ds(j * page, page)
+        return pltpu.make_async_copy(
+            pool.at[table[slot, j]], on_chip.at[slot, rows], sems.at[slot, j]
+        )
+
+    def each_page(act, otherwise=None):
+        def one(slot, carry):
+            for j in range(pages):
+                needed = counts[slot] > j * page
+
+                @pl.when(needed)
+                def _():
+                    act(slot, j)
+
+                if otherwise is not None:
+
+                    @pl.when(jnp.logical_not(needed))
+                    def _():
+                        otherwise(slot, j)
+
+            return carry
+
+        lax.fori_loop(0, slots, one, 0)
+
+    def clear(slot, j):
+        value_pool[slot, pl.ds(j * page, page)] = jnp.zeros((page, kv_width), jnp.bfloat16)
+
+    each_page(lambda slot, j: page_copy(key_pages, key_pool, key_sems, slot, j).start())
+    each_page(lambda slot, j: page_copy(value_pages, value_pool, value_sems, slot, j).start(), clear)
 
     cos = cosine[...]
     sin = sine[...]
@@ -481,7 +515,7 @@
     )
 
     own_chances = {}
-    pltpu.make_async_copy(key_pool, key_pool, sems.at[0]).wait()
+    each_page(lambda slot, j: page_copy(key_pages, key_pool, key_sems, slot, j).wait())
     for p in range(pairs):
         columns_p = slice(p * 2 * HEAD, (p + 1) * 2 * HEAD)
         for b in range(batches):
@@ -491,10 +525,8 @@
             wide = jnp.concatenate(
                 [jnp.where(first, turned, none), jnp.where(first, none, turned)], axis=0
             )
-            keys = []
-            for s in range(batch):
-                keys += held(key_pool, b * batch + s, columns_p)
-            keys.append(key_new[:, columns_p])
+            keys = key_pool[b * batch : (b + 1) * batch, :, columns_p]
+            keys = [keys.reshape(batch * span, 2 * HEAD), key_new[:, columns_p]]
             products = jnp.dot(
                 jnp.concatenate(keys, axis=0), wide, preferred_element_type=jnp.float32
             )
@@ -514,15 +546,16 @@
                 jnp.where(same, own_chance, 0.0), axis=1, keepdims=True
             )
 
-    pltpu.make_async_copy(value_pool, value_pool, sems.at[1]).wait()
+    each_page(lambda slot, j: page_copy(value_pages, value_pool, value_sems, slot, j).wait())
     for p in range(pairs):
         columns_p = slice(p * 2 * HEAD, (p + 1) * 2 * HEAD)
         for b in range(batches):
             for s in range(batch):
                 mine = chance[p, b, pl.ds(s, pair, stride=batch)].astype(jnp.bfloat16)
-                values = held(value_pool, b * batch + s, columns_p)
                 both = jnp.dot(
-                    mine, jnp.concatenate(values, axis=0), preferred_element_type=jnp.float32
+                    mine,
+                    value_pool[b * batch + s, :, columns_p],
+                    preferred_element_type=jnp.float32,
                 )
                 result = jnp.concatenate(
                     [both[: pair // 2, :HEAD], both[pair // 2 :, HEAD:]], axis=0
@@ -554,19 +587,21 @@
     batches = slots * pair // HEAD
     batch = slots // batches
     columns = pair * batch
+    counts = lengths
     lengths = jnp.tile(lengths.reshape(batches, 1, batch), (1, 1, pair))
     smem = pl.BlockSpec(memory_space=pltpu.SMEM)
     vmem = pl.BlockSpec(memory_space=pltpu.VMEM)
     hbm = pl.BlockSpec(memory_space=pl.ANY)
     return pl.pallas_call(
         functools.partial(attend_kernel, per_query, per_key),
-        in_specs=[smem, vmem, vmem, vmem, vmem, hbm, hbm],
+        in_specs=[smem, smem, vmem, vmem, vmem, vmem, hbm, hbm],
         out_specs=vmem,
         out_shape=jax.ShapeDtypeStruct((owners, slots, per_query), jnp.bfloat16),
         scratch_shapes=[
-            pltpu.VMEM(key_pages.shape, jnp.bfloat16),
-            pltpu.VMEM(value_pages.shape, jnp.bfloat16),
-            pltpu.SemaphoreType.DMA((2,)),
+            pltpu.VMEM((slots, span, kv_width), jnp.bfloat16),
+            pltpu.VMEM((slots, span, kv_width), jnp.bfloat16),
+            pltpu.SemaphoreType.DMA((slots, pages)),
+            pltpu.SemaphoreType.DMA((slots, pages)),
             pltpu.VMEM((slots, kv_width), jnp.bfloat16),
             pltpu.VMEM((pairs, batches, columns, HEAD), jnp.float32),
             pltpu.VMEM((kv_heads, slots, HEAD), jnp.float32),
@@ -580,7 +615,7 @@
             transcendentals=slots * heads * span,
         ),
         name="attend",
-    )(table, lengths, inbound, cosine, sine, key_pages, value_pages)
+    )(table, counts, lengths, inbound, cosine, sine, key_pages, value_pages)
 
 
 def on_device(
@@ -609,7 +644,7 @@
 
     moves_a = grid.moves(ORDER_A)
     order_b = [moves_a.index(move) for move in grid.moves(ORDER_B)]
-    cut = width // 8 * 5
+    cut = width // 16 * 11
     xa, xb = norm(hidden_in, norm_gain, (cut, width - cut))
 
     def first(x):

time: 95.3 us -> 95.6 us (level)
  waiting for transfers between devices: 39.7 us -> 38.1 us
  Pallas kernels: 19 us -> 20.1 us
    ppermute x24, waiting for transfers between devices: 21 us -> 19.4 us  [send(): return lax.ppermute(x, AXES, pairs)]
    pallas_call x1, Pallas kernels: 5.88 us -> 6.95 us  [attend(): pl.pallas_call(functools.partial(attend_kernel, per_query, per_key), in_s...]
where the time goes in v16:
time: 95.6 us; the launch traced here: 95.2 us
  waiting for transfers between devices  38.1 us (40%)
  starting transfers between devices  33 us (35%)
  Pallas kernels  20.1 us (21%)
  other arithmetic  3.3 us (3%)
    ppermute x24, starting transfers between devices, send(): return lax.ppermute(x, AXES, pairs)  25.1 us
    ppermute x24, waiting for transfers between devices, send(): return lax.ppermute(x, AXES, pairs)  19.4 us
    all_to_all x1, waiting for transfers between devices, on_device(): lax.all_to_all(outbound, AXES, split_axis=0, concat_axis=0, tiled=True)  10.4 us
    all_to_all x1, waiting for transfers between devices, on_device(): lax.all_to_all(attended, AXES, split_axis=0, concat_axis=0, tiled=True)  8.25 us
    pallas_call x1, Pallas kernels, attend(): pl.pallas_call(functools.partial(attend_kernel, per_query, per_key), in_s...  6.95 us
    pallas_call x2, Pallas kernels, fetch(): pl.pallas_call(functools.partial(fetch_kernel, starts), in_specs=[pl.Bloc...  5.14 us
    all_to_all x1, starting transfers between devices, on_device(): lax.all_to_all(outbound, AXES, split_axis=0, concat_axis=0, tiled=True)  4.41 us
    all_to_all x1, starting transfers between devices, on_device(): lax.all_to_all(attended, AXES, split_axis=0, concat_axis=0, tiled=True)  3.54 us
  transfers between devices with their start and end apart: 26, of which 13 were waited for; matrix products, arithmetic and copies ran while one was open for 3% of the time, Pallas kernels for 7%

profile of v16, /device:TPU:0, one launch (start us, length us, event | category | flops | bytes accessed | tf_op | source)
XLA Modules:
  0.0 95.2 jit_solution(2444974993091461397)
XLA Ops:
  0.0 1.7 %norm.1 = (bf16[8,5632]{1,0:T(8,128)(2,1)}, bf16[8,2560]{1,0:T(8,128)(2,1)}) custom-call(bf16[8,8192]{1,0:T(8,128)(2,1)} %x.1, f32[1,8192]{1,0:T(1,128)} %bitcast.21), custom_call_target="tpu_custom_call" | custom-call | tf_op jit(solution)/shard_map/norm/pallas_call | solution.py:227
  1.7 4.1 %collective-permute-start = (bf16[8,5632]{1,0:T(8,128)(2,1)}, bf16[8,5632]{1,0:T(8,128)(2,1)S(1)}, u32[]{:S(2)}, u32[]{:S(2)}) collective-permute-start(bf16[8,5632]{1,0:T(8,128)(2,1)} %get-tuple-element.41), channel_id=1, source_target_pairs={{0,8},{1,9},{2,10},{3,11},{4,12},{5,13},{6,14},{7,15},{8,0},{9,1},... | collective-permute-start | bytes 270344 | tf_op jit(solution)/shard_map/ppermute | solution.py:34
  5.8 1.6 %collective-permute-start.1 = (bf16[8,5632]{1,0:T(8,128)(2,1)}, bf16[8,5632]{1,0:T(8,128)(2,1)S(1)}, u32[]{:S(2)}, u32[]{:S(2)}) collective-permute-start(bf16[8,5632]{1,0:T(8,128)(2,1)} %get-tuple-element.41), channel_id=1, source_target_pairs={{0,4},{1,5},{2,6},{3,7},{4,0},{5,1},{6,2},{7,3},{8,12},{9,13},{10,... | collective-permute-start | bytes 270344 | tf_op jit(solution)/shard_map/ppermute | solution.py:34
  7.4 1.7 %collective-permute-start.3 = (bf16[8,2560]{1,0:T(8,128)(2,1)}, bf16[8,2560]{1,0:T(8,128)(2,1)S(1)}, u32[]{:S(2)}, u32[]{:S(2)}) collective-permute-start(bf16[8,2560]{1,0:T(8,128)(2,1)} %get-tuple-element.42), channel_id=1, source_target_pairs={{0,2},{1,3},{2,0},{3,1},{4,6},{5,7},{6,4},{7,5},{8,10},{9,11},{10,... | collective-permute-start | bytes 122888 | tf_op jit(solution)/shard_map/ppermute | solution.py:34
  9.2 1.8 %pad_maximum_fusion.refs_5_.refs_9_ = bf16[128,8192]{1,0:T(8,128)(2,1)S(1)} fusion(bf16[64,8192]{1,0:T(8,128)(2,1)} %bitcast.19, bf16[64,8192]{1,0:T(8,128)(2,1)} %bitcast.20), kind=kLoop, calls=%fused_computation | loop fusion | flops 4194304 | bytes 4194304 | tf_op jit(solution)/shard_map/concatenate | solution.py:657
  11.7 2.3 %collective-permute-done.2 = bf16[8,5632]{1,0:T(8,128)(2,1)S(1)} collective-permute-done((bf16[8,5632]{1,0:T(8,128)(2,1)}, bf16[8,5632]{1,0:T(8,128)(2,1)S(1)}, u32[]{:S(2)}, u32[]{:S(2)}) %collective-permute-start.2) | collective-permute-done | bytes 90144 | tf_op jit(solution)/shard_map/ppermute | solution.py:34
  14.1 1.6 %collective-permute-start.4 = (bf16[32,5632]{1,0:T(8,128)(2,1)S(1)}, bf16[32,5632]{1,0:T(8,128)(2,1)S(1)}, u32[]{:S(2)}, u32[]{:S(2)}) collective-permute-start(bf16[32,5632]{1,0:T(8,128)(2,1)S(1)} %pad_maximum_fusion.1.refs_0_), channel_id=1, source_target_pairs={{0,2},{1,3},{2,0},{3,1},{4,6},{5,7},{6,4},{7,5},{8,10},{9,11},{10,... | collective-permute-start | bytes 1081352 | tf_op jit(solution)/shard_map/ppermute | solution.py:34
  15.6 3.1 %collective-permute-start.5 = (bf16[16,2560]{1,0:T(8,128)(2,1)S(1)}, bf16[16,2560]{1,0:T(8,128)(2,1)S(1)}, u32[]{:S(2)}, u32[]{:S(2)}) collective-permute-start(bf16[16,2560]{1,0:T(8,128)(2,1)S(1)} %pad_maximum_fusion.2.refs_0_), channel_id=1, source_target_pairs={{0,8},{1,9},{2,10},{3,11},{4,12},{5,13},{6,14},{7,15},{8,0},{9,1},... | collective-permute-start | bytes 245768 | tf_op jit(solution)/shard_map/ppermute | solution.py:34
  18.7 1.5 %collective-permute-start.7 = (bf16[16,2560]{1,0:T(8,128)(2,1)S(1)}, bf16[16,2560]{1,0:T(8,128)(2,1)S(1)}, u32[]{:S(2)}, u32[]{:S(2)}) collective-permute-start(bf16[16,2560]{1,0:T(8,128)(2,1)S(1)} %pad_maximum_fusion.2.refs_0_), channel_id=1, source_target_pairs={{0,12},{1,13},{2,14},{3,15},{4,8},{5,9},{6,10},{7,11},{8,4},{9,5},... | collective-permute-start | bytes 245768 | tf_op jit(solution)/shard_map/ppermute | solution.py:34
  20.2 3.4 %fetch.2.refs_4_.refs_8_ = bf16[8192,512]{1,0:T(8,128)(2,1)S(1)} custom-call(bf16[8192,512]{1,0:T(8,128)(2,1)} %refs_0_), custom_call_target="tpu_custom_call" | custom-call | bytes 16777216 | tf_op jit(solution)/shard_map/fetch/pallas_call | solution.py:317
  28.4 1.6 %project.3 = bf16[256,640]{1,0:T(8,128)(2,1)} custom-call(bf16[16,2560]{1,0:T(8,128)(2,1)S(1)} %pad_maximum_fusion.2.refs_0_, bf16[16,2560]{1,0:T(8,128)(2,1)S(1)} %collective-permute-done.5.refs_1_, bf16[16,2560]{1,0:T(8,128)(2,1)S(1)} %collective-permute-done.6.refs_2_, bf16[16,2560]{1,0:T(8,128)(2,1)S(1)} %collective-permute-done.7.refs_3_, ...), custom_call_target="tpu_custom_call" | custom-call | flops 419430400 | bytes 3276800 | tf_op jit(solution)/shard_map/project/pallas_call | solution.py:395
  30.0 4.4 %all-to-all-start = ((bf16[16,16,640]{2,1,0:T(8,128)(2,1)}), bf16[16,16,640]{2,1,0:T(8,128)(2,1)S(1)}, u32[]{:S(2)}, u32[]{:S(2)}) async-start(bf16[16,16,640]{2,1,0:T(8,128)(2,1)} %bitcast.4), calls=%async_computation | async-start | bytes 655360 | tf_op jit(solution)/shard_map/all_to_all | solution.py:679
  35.1 10.4 %all-to-all-done.inbound = bf16[16,16,640]{2,1,0:T(8,128)(2,1)S(1)} async-done(((bf16[16,16,640]{2,1,0:T(8,128)(2,1)}), bf16[16,16,640]{2,1,0:T(8,128)(2,1)S(1)}, u32[]{:S(2)}, u32[]{:S(2)}) %all-to-all-start) | async-done | bytes 327712 | tf_op jit(solution)/shard_map/all_to_all | solution.py:679
  45.5 7.0 %attend.1 = bf16[16,16,512]{2,1,0:T(8,128)(2,1)} custom-call(s32[16,4]{1,0:T(8,128)S(1)} %copy.15.table, s32[16]{0:T(128)S(1)} %select_reduce_fusion.counts, s32[2,1,128]{2,1,0:T(1,128)S(1)} %bitcast.14, bf16[16,16,640]{2,1,0:T(8,128)(2,1)S(1)} %all-to-all-done.inbound, f32[16,128]{1,0:T(8,128)S(1)} %get-tuple-element.90.cosine, ...), custom_call_target="tpu_custom_call" | custom-call | flops 134217728 | bytes 8388608 | tf_op jit(solution)/shard_map/attend/pallas_call | solution.py:595
  52.5 3.5 %all-to-all-start.1 = ((bf16[16,16,512]{2,1,0:T(8,128)(2,1)}), bf16[16,16,512]{2,1,0:T(8,128)(2,1)S(1)}, u32[]{:S(2)}, u32[]{:S(2)}) async-start(bf16[16,16,512]{2,1,0:T(8,128)(2,1)} %attend.1), calls=%async_computation.1 | async-start | bytes 524288 | tf_op jit(solution)/shard_map/all_to_all | solution.py:692
  56.0 1.8 %fetch.3.w_front = bf16[512,2560]{1,0:T(8,128)(2,1)S(1)} custom-call(bf16[512,8192]{1,0:T(8,128)(2,1)} %w_out.1), custom_call_target="tpu_custom_call" | custom-call | bytes 5242880 | tf_op jit(solution)/shard_map/fetch/pallas_call | solution.py:317
  57.8 8.2 %all-to-all-done.1 = bf16[16,16,512]{2,1,0:T(8,128)(2,1)S(1)} async-done(((bf16[16,16,512]{2,1,0:T(8,128)(2,1)}), bf16[16,16,512]{2,1,0:T(8,128)(2,1)S(1)}, u32[]{:S(2)}, u32[]{:S(2)}) %all-to-all-start.1) | async-done | bytes 262176 | tf_op jit(solution)/shard_map/all_to_all | solution.py:692
  66.0 3.2 %product.1 = (bf16[64,5376]{1,0:T(8,128)(2,1)S(1)}, f32[64,5376]{1,0:T(8,128)S(1)}, bf16[64,2816]{1,0:T(8,128)(2,1)S(1)}, f32[64,2816]{1,0:T(8,128)S(1)}) custom-call(s32[1,128]{1,0:T(1,128)S(1)} %get-tuple-element.50.place_a, s32[1,128]{1,0:T(1,128)S(1)} %get-tuple-element.51.place_b, bf16[256,512]{1,0:T(8,128)(2,1)S(1)} %bitcast.13, ...), custom_call_target="tpu_custom_call" | custom-call | flops 1073741824 | bytes 8388608 | tf_op jit(solution)/shard_map/product/pallas_call | solution.py:155
  69.3 2.1 %collective-permute-done.14 = bf16[64,5376]{1,0:T(8,128)(2,1)S(1)} collective-permute-done((bf16[64,5376]{1,0:T(8,128)(2,1)S(1)}, bf16[64,5376]{1,0:T(8,128)(2,1)S(1)}, u32[]{:S(2)}, u32[]{:S(2)}) %collective-permute-start.14) | collective-permute-done | bytes 688160 | tf_op jit(solution)/shard_map/ppermute | solution.py:34
  75.1 2.9 %collective-permute-start.19 = (bf16[16,2816]{1,0:T(8,128)(2,1)S(1)}, bf16[16,2816]{1,0:T(8,128)(2,1)S(1)}, u32[]{:S(2)}, u32[]{:S(2)}) collective-permute-start(bf16[16,2816]{1,0:T(8,128)(2,1)S(1)} %get-tuple-element.81), channel_id=1, source_target_pairs={{0,12},{1,13},{2,14},{3,15},{4,8},{5,9},{6,10},{7,11},{8,4},{9,5},... | collective-permute-start | bytes 270344 | tf_op jit(solution)/shard_map/ppermute | solution.py:34
  78.0 4.2 %collective-permute-done.15 = bf16[32,5376]{1,0:T(8,128)(2,1)S(1)} collective-permute-done((bf16[32,5376]{1,0:T(8,128)(2,1)S(1)}, bf16[32,5376]{1,0:T(8,128)(2,1)S(1)}, u32[]{:S(2)}, u32[]{:S(2)}) %collective-permute-start.15) | collective-permute-done | bytes 344096 | tf_op jit(solution)/shard_map/ppermute | solution.py:34
  84.1 2.4 %collective-permute-start.20 = (bf16[8,5376]{1,0:T(8,128)(2,1)S(1)}, bf16[8,5376]{1,0:T(8,128)(2,1)S(1)}, u32[]{:S(2)}, u32[]{:S(2)}) collective-permute-start(bf16[8,5376]{1,0:T(8,128)(2,1)S(1)} %get-tuple-element.84), channel_id=1, source_target_pairs={{0,8},{1,9},{2,10},{3,11},{4,12},{5,13},{6,14},{7,15},{8,0},{9,1},... | collective-permute-start | bytes 258056 | tf_op jit(solution)/shard_map/ppermute | solution.py:34
  86.5 2.1 %collective-permute-start.22 = (bf16[8,5376]{1,0:T(8,128)(2,1)S(1)}, bf16[8,5376]{1,0:T(8,128)(2,1)S(1)}, u32[]{:S(2)}, u32[]{:S(2)}) collective-permute-start(bf16[8,5376]{1,0:T(8,128)(2,1)S(1)} %get-tuple-element.85), channel_id=1, source_target_pairs={{0,12},{1,13},{2,14},{3,15},{4,8},{5,9},{6,10},{7,11},{8,4},{9,5},... | collective-permute-start | bytes 258056 | tf_op jit(solution)/shard_map/ppermute | solution.py:34
  88.6 4.4 %collective-permute-done.20 = bf16[8,5376]{1,0:T(8,128)(2,1)S(1)} collective-permute-done((bf16[8,5376]{1,0:T(8,128)(2,1)S(1)}, bf16[8,5376]{1,0:T(8,128)(2,1)S(1)}, u32[]{:S(2)}, u32[]{:S(2)}) %collective-permute-start.20) | collective-permute-done | bytes 86048 | tf_op jit(solution)/shard_map/ppermute | solution.py:34
  (72 shorter events, 13.9 us)
Async XLA Ops:
  1.7 9.9 %collective-permute-start = (bf16[8,5632]{1,0:T(8,128)(2,1)}, bf16[8,5632]{1,0:T(8,128)(2,1)S(1)}, u32[]{:S(2)}, u32[]{:S(2)}) collective-permute-start(bf16[8,5632]{1,0:T(8,128)(2,1)} %get-tuple-element.41), channel_id=1, source_target_pairs={{0,8},{1,9},{2,10},{3,11},{4,12},{5,13},{6,14},{7,15},{8,0},{9,1},... | collective-permute-start | bytes 270344 | tf_op jit(solution)/shard_map/ppermute | solution.py:34
  5.8 5.8 %collective-permute-start.1 = (bf16[8,5632]{1,0:T(8,128)(2,1)}, bf16[8,5632]{1,0:T(8,128)(2,1)S(1)}, u32[]{:S(2)}, u32[]{:S(2)}) collective-permute-start(bf16[8,5632]{1,0:T(8,128)(2,1)} %get-tuple-element.41), channel_id=1, source_target_pairs={{0,4},{1,5},{2,6},{3,7},{4,0},{5,1},{6,2},{7,3},{8,12},{9,13},{10,... | collective-permute-start | bytes 270344 | tf_op jit(solution)/shard_map/ppermute | solution.py:34
  7.4 6.6 %collective-permute-start.2 = (bf16[8,5632]{1,0:T(8,128)(2,1)}, bf16[8,5632]{1,0:T(8,128)(2,1)S(1)}, u32[]{:S(2)}, u32[]{:S(2)}) collective-permute-start(bf16[8,5632]{1,0:T(8,128)(2,1)} %get-tuple-element.41), channel_id=1, source_target_pairs={{0,12},{1,13},{2,14},{3,15},{4,8},{5,9},{6,10},{7,11},{8,4},{9,5},... | collective-permute-start | bytes 270344 | tf_op jit(solution)/shard_map/ppermute | solution.py:34
  7.4 4.2 %collective-permute-start.3 = (bf16[8,2560]{1,0:T(8,128)(2,1)}, bf16[8,2560]{1,0:T(8,128)(2,1)S(1)}, u32[]{:S(2)}, u32[]{:S(2)}) collective-permute-start(bf16[8,2560]{1,0:T(8,128)(2,1)} %get-tuple-element.42), channel_id=1, source_target_pairs={{0,2},{1,3},{2,0},{3,1},{4,6},{5,7},{6,4},{7,5},{8,10},{9,11},{10,... | collective-permute-start | bytes 122888 | tf_op jit(solution)/shard_map/ppermute | solution.py:34
  14.1 11.3 %collective-permute-start.4 = (bf16[32,5632]{1,0:T(8,128)(2,1)S(1)}, bf16[32,5632]{1,0:T(8,128)(2,1)S(1)}, u32[]{:S(2)}, u32[]{:S(2)}) collective-permute-start(bf16[32,5632]{1,0:T(8,128)(2,1)S(1)} %pad_maximum_fusion.1.refs_0_), channel_id=1, source_target_pairs={{0,2},{1,3},{2,0},{3,1},{4,6},{5,7},{6,4},{7,5},{8,10},{9,11},{10,... | collective-permute-start | bytes 1081352 | tf_op jit(solution)/shard_map/ppermute | solution.py:34
  15.6 8.4 %collective-permute-start.5 = (bf16[16,2560]{1,0:T(8,128)(2,1)S(1)}, bf16[16,2560]{1,0:T(8,128)(2,1)S(1)}, u32[]{:S(2)}, u32[]{:S(2)}) collective-permute-start(bf16[16,2560]{1,0:T(8,128)(2,1)S(1)} %pad_maximum_fusion.2.refs_0_), channel_id=1, source_target_pairs={{0,8},{1,9},{2,10},{3,11},{4,12},{5,13},{6,14},{7,15},{8,0},{9,1},... | collective-permute-start | bytes 245768 | tf_op jit(solution)/shard_map/ppermute | solution.py:34
  18.7 6.7 %collective-permute-start.6 = (bf16[16,2560]{1,0:T(8,128)(2,1)S(1)}, bf16[16,2560]{1,0:T(8,128)(2,1)S(1)}, u32[]{:S(2)}, u32[]{:S(2)}) collective-permute-start(bf16[16,2560]{1,0:T(8,128)(2,1)S(1)} %pad_maximum_fusion.2.refs_0_), channel_id=1, source_target_pairs={{0,4},{1,5},{2,6},{3,7},{4,0},{5,1},{6,2},{7,3},{8,12},{9,13},{10,... | collective-permute-start | bytes 245768 | tf_op jit(solution)/shard_map/ppermute | solution.py:34
  18.7 6.7 %collective-permute-start.7 = (bf16[16,2560]{1,0:T(8,128)(2,1)S(1)}, bf16[16,2560]{1,0:T(8,128)(2,1)S(1)}, u32[]{:S(2)}, u32[]{:S(2)}) collective-permute-start(bf16[16,2560]{1,0:T(8,128)(2,1)S(1)} %pad_maximum_fusion.2.refs_0_), channel_id=1, source_target_pairs={{0,12},{1,13},{2,14},{3,15},{4,8},{5,9},{6,10},{7,11},{8,4},{9,5},... | collective-permute-start | bytes 245768 | tf_op jit(solution)/shard_map/ppermute | solution.py:34
  20.2 6.2 %collective-permute-start.12 = (bf16[32,5632]{1,0:T(8,128)(2,1)S(1)}, bf16[32,5632]{1,0:T(8,128)(2,1)S(1)}, u32[]{:S(2)}, u32[]{:S(2)}) collective-permute-start(bf16[32,5632]{1,0:T(8,128)(2,1)S(1)} %pad_maximum_fusion.1.refs_0_), channel_id=1, source_target_pairs={{0,1},{1,0},{2,3},{3,2},{4,5},{5,4},{6,7},{7,6},{8,9},{9,8},{10,11... | collective-permute-start | bytes 1081352 | tf_op jit(solution)/shard_map/ppermute | solution.py:34
  25.4 3.0 %collective-permute-start.10 = (bf16[16,2560]{1,0:T(8,128)(2,1)S(1)}, bf16[16,2560]{1,0:T(8,128)(2,1)S(1)}, u32[]{:S(2)}, u32[]{:S(2)}) collective-permute-start(bf16[16,2560]{1,0:T(8,128)(2,1)S(1)} %collective-permute-done.6.refs_2_), channel_id=1, source_target_pairs={{0,1},{1,0},{2,3},{3,2},{4,5},{5,4},{6,7},{7,6},{8,9},{9,8},{10,11... | collective-permute-start | bytes 245768 | tf_op jit(solution)/shard_map/ppermute | solution.py:34
  25.9 2.5 %collective-permute-start.11 = (bf16[16,2560]{1,0:T(8,128)(2,1)S(1)}, bf16[16,2560]{1,0:T(8,128)(2,1)S(1)}, u32[]{:S(2)}, u32[]{:S(2)}) collective-permute-start(bf16[16,2560]{1,0:T(8,128)(2,1)S(1)} %collective-permute-done.7.refs_3_), channel_id=1, source_target_pairs={{0,1},{1,0},{2,3},{3,2},{4,5},{5,4},{6,7},{7,6},{8,9},{9,8},{10,11... | collective-permute-start | bytes 245768 | tf_op jit(solution)/shard_map/ppermute | solution.py:34
  26.0 2.4 %collective-permute-start.8 = (bf16[16,2560]{1,0:T(8,128)(2,1)S(1)}, bf16[16,2560]{1,0:T(8,128)(2,1)S(1)}, u32[]{:S(2)}, u32[]{:S(2)}) collective-permute-start(bf16[16,2560]{1,0:T(8,128)(2,1)S(1)} %pad_maximum_fusion.2.refs_0_), channel_id=1, source_target_pairs={{0,1},{1,0},{2,3},{3,2},{4,5},{5,4},{6,7},{7,6},{8,9},{9,8},{10,11... | collective-permute-start | bytes 245768 | tf_op jit(solution)/shard_map/ppermute | solution.py:34
  26.4 2.0 %collective-permute-start.9 = (bf16[16,2560]{1,0:T(8,128)(2,1)S(1)}, bf16[16,2560]{1,0:T(8,128)(2,1)S(1)}, u32[]{:S(2)}, u32[]{:S(2)}) collective-permute-start(bf16[16,2560]{1,0:T(8,128)(2,1)S(1)} %collective-permute-done.5.refs_1_), channel_id=1, source_target_pairs={{0,1},{1,0},{2,3},{3,2},{4,5},{5,4},{6,7},{7,6},{8,9},{9,8},{10,11... | collective-permute-start | bytes 245768 | tf_op jit(solution)/shard_map/ppermute | solution.py:34
  30.0 15.5 %all-to-all-start = ((bf16[16,16,640]{2,1,0:T(8,128)(2,1)}), bf16[16,16,640]{2,1,0:T(8,128)(2,1)S(1)}, u32[]{:S(2)}, u32[]{:S(2)}) async-start(bf16[16,16,640]{2,1,0:T(8,128)(2,1)} %bitcast.4), calls=%async_computation | async-start | bytes 655360 | tf_op jit(solution)/shard_map/all_to_all | solution.py:679
  52.5 13.6 %all-to-all-start.1 = ((bf16[16,16,512]{2,1,0:T(8,128)(2,1)}), bf16[16,16,512]{2,1,0:T(8,128)(2,1)S(1)}, u32[]{:S(2)}, u32[]{:S(2)}) async-start(bf16[16,16,512]{2,1,0:T(8,128)(2,1)} %attend.1), calls=%async_computation.1 | async-start | bytes 524288 | tf_op jit(solution)/shard_map/all_to_all | solution.py:692
  69.2 2.2 %collective-permute-start.14 = (bf16[64,5376]{1,0:T(8,128)(2,1)S(1)}, bf16[64,5376]{1,0:T(8,128)(2,1)S(1)}, u32[]{:S(2)}, u32[]{:S(2)}) collective-permute-start(bf16[64,5376]{1,0:T(8,128)(2,1)S(1)} %get-tuple-element.69), channel_id=1, source_target_pairs={{0,1},{1,0},{2,3},{3,2},{4,5},{5,4},{6,7},{7,6},{8,9},{9,8},{10,11... | collective-permute-start | bytes 2064392 | tf_op jit(solution)/shard_map/ppermute | solution.py:34
  71.8 10.3 %collective-permute-start.15 = (bf16[32,5376]{1,0:T(8,128)(2,1)S(1)}, bf16[32,5376]{1,0:T(8,128)(2,1)S(1)}, u32[]{:S(2)}, u32[]{:S(2)}) collective-permute-start(bf16[32,5376]{1,0:T(8,128)(2,1)S(1)} %slice.87), channel_id=1, source_target_pairs={{0,2},{1,3},{2,0},{3,1},{4,6},{5,7},{6,4},{7,5},{8,10},{9,11},{10,... | collective-permute-start | bytes 1032200 | tf_op jit(solution)/shard_map/ppermute | solution.py:34
  73.5 8.7 %collective-permute-start.17 = (bf16[16,2816]{1,0:T(8,128)(2,1)S(1)}, bf16[16,2816]{1,0:T(8,128)(2,1)S(1)}, u32[]{:S(2)}, u32[]{:S(2)}) collective-permute-start(bf16[16,2816]{1,0:T(8,128)(2,1)S(1)} %get-tuple-element.83), channel_id=1, source_target_pairs={{0,8},{1,9},{2,10},{3,11},{4,12},{5,13},{6,14},{7,15},{8,0},{9,1},... | collective-permute-start | bytes 270344 | tf_op jit(solution)/shard_map/ppermute | solution.py:34
  74.6 7.6 %collective-permute-start.18 = (bf16[16,2816]{1,0:T(8,128)(2,1)S(1)}, bf16[16,2816]{1,0:T(8,128)(2,1)S(1)}, u32[]{:S(2)}, u32[]{:S(2)}) collective-permute-start(bf16[16,2816]{1,0:T(8,128)(2,1)S(1)} %get-tuple-element.82), channel_id=1, source_target_pairs={{0,4},{1,5},{2,6},{3,7},{4,0},{5,1},{6,2},{7,3},{8,12},{9,13},{10,... | collective-permute-start | bytes 270344 | tf_op jit(solution)/shard_map/ppermute | solution.py:34
  75.1 8.0 %collective-permute-start.19 = (bf16[16,2816]{1,0:T(8,128)(2,1)S(1)}, bf16[16,2816]{1,0:T(8,128)(2,1)S(1)}, u32[]{:S(2)}, u32[]{:S(2)}) collective-permute-start(bf16[16,2816]{1,0:T(8,128)(2,1)S(1)} %get-tuple-element.81), channel_id=1, source_target_pairs={{0,12},{1,13},{2,14},{3,15},{4,8},{5,9},{6,10},{7,11},{8,4},{9,5},... | collective-permute-start | bytes 270344 | tf_op jit(solution)/shard_map/ppermute | solution.py:34
  83.2 5.4 %collective-permute-start.23 = (bf16[8,2816]{1,0:T(8,128)(2,1)S(1)}, bf16[8,2816]{1,0:T(8,128)(2,1)S(1)}, u32[]{:S(2)}, u32[]{:S(2)}) collective-permute-start(bf16[8,2816]{1,0:T(8,128)(2,1)S(1)} %slice.88), channel_id=1, source_target_pairs={{0,2},{1,3},{2,0},{3,1},{4,6},{5,7},{6,4},{7,5},{8,10},{9,11},{10,... | collective-permute-start | bytes 135176 | tf_op jit(solution)/shard_map/ppermute | solution.py:34
  84.1 8.9 %collective-permute-start.20 = (bf16[8,5376]{1,0:T(8,128)(2,1)S(1)}, bf16[8,5376]{1,0:T(8,128)(2,1)S(1)}, u32[]{:S(2)}, u32[]{:S(2)}) collective-permute-start(bf16[8,5376]{1,0:T(8,128)(2,1)S(1)} %get-tuple-element.84), channel_id=1, source_target_pairs={{0,8},{1,9},{2,10},{3,11},{4,12},{5,13},{6,14},{7,15},{8,0},{9,1},... | collective-permute-start | bytes 258056 | tf_op jit(solution)/shard_map/ppermute | solution.py:34
  86.5 6.5 %collective-permute-start.21 = (bf16[8,5376]{1,0:T(8,128)(2,1)S(1)}, bf16[8,5376]{1,0:T(8,128)(2,1)S(1)}, u32[]{:S(2)}, u32[]{:S(2)}) collective-permute-start(bf16[8,5376]{1,0:T(8,128)(2,1)S(1)} %get-tuple-element.86), channel_id=1, source_target_pairs={{0,4},{1,5},{2,6},{3,7},{4,0},{5,1},{6,2},{7,3},{8,12},{9,13},{10,... | collective-permute-start | bytes 258056 | tf_op jit(solution)/shard_map/ppermute | solution.py:34
  86.5 7.9 %collective-permute-start.22 = (bf16[8,5376]{1,0:T(8,128)(2,1)S(1)}, bf16[8,5376]{1,0:T(8,128)(2,1)S(1)}, u32[]{:S(2)}, u32[]{:S(2)}) collective-permute-start(bf16[8,5376]{1,0:T(8,128)(2,1)S(1)} %get-tuple-element.85), channel_id=1, source_target_pairs={{0,12},{1,13},{2,14},{3,15},{4,8},{5,9},{6,10},{7,11},{8,4},{9,5},... | collective-permute-start | bytes 258056 | tf_op jit(solution)/shard_map/ppermute | solution.py:34
  (8 other events, 46.0 us)

commit v17 on v15

--- a/solution.py
+++ b/solution.py
@@ -170,16 +170,15 @@
 
 
 def scatter_sum(grid, place_a, place_b, returned, w_out, w_front, cut):
-    def direct(x):
+    def pieces(x):
         size = x.shape[0] // 2 // grid.half
-        parts = []
-        for pair in range(2):
-            for half in range(grid.half):
-                begin = (pair * grid.half + half) * size
-                if begin:
-                    sent = narrow(x[begin : begin + size])
-                    parts.append(grid.send(sent, half=half, pair=pair))
-        return x[:size], parts
+        return x[:size], [narrow(x[i * size : (i + 1) * size]) for i in range(1, 2 * grid.half)]
+
+    def direct(sent):
+        return [
+            grid.send(x, half=i % grid.half, pair=i // grid.half)
+            for i, x in enumerate(sent, start=1)
+        ]
 
     def total(x, parts):
         for part in parts:
@@ -192,20 +191,32 @@
     sent_a = narrow(xa[middle:])
     got_a = grid.send(sent_a, near=1)
     xb = keep_b + wide(grid.send(after(away_b, sent_a), core=1))
-    xb, got_b = direct(xb)
-    got_a, got_b = lax.optimization_barrier((got_a, got_b))
-    xa, parts_a = direct(xa[:middle] + wide(got_a))
+    xb, sent = pieces(xb)
+    got_b = direct(sent)
+    got_a, got_b[0] = lax.optimization_barrier((got_a, got_b[0]))
+    xa, sent = pieces(xa[:middle] + wide(got_a))
+    parts_a = direct(sent)
     xb = total(xb, got_b)
     middle = xb.shape[0] // 2
-    xb = xb[:middle] + wide(grid.send(narrow(xb[middle:]), near=1))
+    sent_b = after(narrow(xb[middle:]), *sent)
     xa = total(xa, parts_a)
+    xb = xb[:middle] + wide(after(grid.send(sent_b, near=1), xa))
     return jnp.concatenate([xa, xb], axis=1)
 
 
-def norm_kernel(x, gain, *outs):
-    inputs = x[...].astype(jnp.float32)
+def norm_kernel(x, gain, *refs):
+    outs, (rows, gains, sems) = refs[:-3], refs[-3:]
+    copies = [
+        pltpu.make_async_copy(x, rows, sems.at[0]),
+        pltpu.make_async_copy(gain, gains, sems.at[1]),
+    ]
+    for copy in copies:
+        copy.start()
+    copies[0].wait()
+    inputs = rows[...].astype(jnp.float32)
     factor = lax.rsqrt(jnp.mean(inputs * inputs, axis=1, keepdims=True) + epsilon)
-    normed = (inputs * factor * gain[...]).astype(jnp.bfloat16)
+    copies[1].wait()
+    normed = (inputs * factor * gains[...]).astype(jnp.bfloat16)
     start = 0
     for out in outs:
         out[...] = normed[:, start : start + out.shape[1]]
@@ -214,11 +225,17 @@
 
 def norm(x, gain, widths):
     vmem = pl.BlockSpec(memory_space=pltpu.VMEM)
+    hbm = pl.BlockSpec(memory_space=pl.ANY)
     return pl.pallas_call(
         norm_kernel,
-        in_specs=[vmem, vmem],
+        in_specs=[hbm, hbm],
         out_specs=[vmem] * len(widths),
         out_shape=[jax.ShapeDtypeStruct((x.shape[0], w), jnp.bfloat16) for w in widths],
+        scratch_shapes=[
+            pltpu.VMEM(x.shape, jnp.bfloat16),
+            pltpu.VMEM((1, x.shape[1]), jnp.float32),
+            pltpu.SemaphoreType.DMA((2,)),
+        ],
         compiler_params=pltpu.CompilerParams(vmem_limit_bytes=60 * 2**20),
         name="norm",
     )(x, gain.reshape(1, -1))
@@ -609,7 +626,7 @@
 
     moves_a = grid.moves(ORDER_A)
     order_b = [moves_a.index(move) for move in grid.moves(ORDER_B)]
-    cut = width // 8 * 5
+    cut = width // 16 * 11
     xa, xb = norm(hidden_in, norm_gain, (cut, width - cut))
 
     def first(x):

time: 95.3 us -> 91.5 us (0.960)
  waiting for transfers between devices: 39.7 us -> 35.5 us
    ppermute x24, waiting for transfers between devices: 21 us -> 16.9 us  [send(): return lax.ppermute(x, AXES, pairs)]
  transfers between devices with their start and end apart: 26 -> 26, of which waited for: 13 -> 11; matrix products, arithmetic and copies ran while one was open for 3% -> 3% of each run, Pallas kernels for 7% -> 7%
where the time goes in v17:
time: 91.5 us; the launch traced here: 91.1 us
  waiting for transfers between devices  35.5 us (39%)
  starting transfers between devices  32.5 us (36%)
  Pallas kernels  19 us (21%)
  other arithmetic  3.29 us (4%)
    ppermute x24, starting transfers between devices, send(): return lax.ppermute(x, AXES, pairs)  24.6 us
    ppermute x24, waiting for transfers between devices, send(): return lax.ppermute(x, AXES, pairs)  16.9 us
    all_to_all x1, waiting for transfers between devices, on_device(): lax.all_to_all(outbound, AXES, split_axis=0, concat_axis=0, tiled=True)  10.4 us
    all_to_all x1, waiting for transfers between devices, on_device(): lax.all_to_all(attended, AXES, split_axis=0, concat_axis=0, tiled=True)  8.25 us
    pallas_call x1, Pallas kernels, attend(): pl.pallas_call(functools.partial(attend_kernel, per_query, per_key), in_s...  5.88 us
    pallas_call x2, Pallas kernels, fetch(): pl.pallas_call(functools.partial(fetch_kernel, starts), in_specs=[pl.Bloc...  5.14 us
    all_to_all x1, starting transfers between devices, on_device(): lax.all_to_all(outbound, AXES, split_axis=0, concat_axis=0, tiled=True)  4.41 us
    all_to_all x1, starting transfers between devices, on_device(): lax.all_to_all(attended, AXES, split_axis=0, concat_axis=0, tiled=True)  3.54 us
  transfers between devices with their start and end apart: 26, of which 11 were waited for; matrix products, arithmetic and copies ran while one was open for 3% of the time, Pallas kernels for 7%

profile of v17, /device:TPU:0, one launch (start us, length us, event | category | flops | bytes accessed | tf_op | source)
XLA Modules:
  0.0 91.1 jit_solution(7344675349112803567)
XLA Ops:
  0.0 1.7 %norm.1 = (bf16[8,5632]{1,0:T(8,128)(2,1)}, bf16[8,2560]{1,0:T(8,128)(2,1)}) custom-call(bf16[8,8192]{1,0:T(8,128)(2,1)} %x.1, f32[1,8192]{1,0:T(1,128)} %bitcast.21), custom_call_target="tpu_custom_call" | custom-call | tf_op jit(solution)/shard_map/norm/pallas_call | solution.py:229
  1.7 4.1 %collective-permute-start = (bf16[8,5632]{1,0:T(8,128)(2,1)}, bf16[8,5632]{1,0:T(8,128)(2,1)S(1)}, u32[]{:S(2)}, u32[]{:S(2)}) collective-permute-start(bf16[8,5632]{1,0:T(8,128)(2,1)} %get-tuple-element.41), channel_id=1, source_target_pairs={{0,8},{1,9},{2,10},{3,11},{4,12},{5,13},{6,14},{7,15},{8,0},{9,1},... | collective-permute-start | bytes 270344 | tf_op jit(solution)/shard_map/ppermute | solution.py:34
  5.8 1.6 %collective-permute-start.1 = (bf16[8,5632]{1,0:T(8,128)(2,1)}, bf16[8,5632]{1,0:T(8,128)(2,1)S(1)}, u32[]{:S(2)}, u32[]{:S(2)}) collective-permute-start(bf16[8,5632]{1,0:T(8,128)(2,1)} %get-tuple-element.41), channel_id=1, source_target_pairs={{0,4},{1,5},{2,6},{3,7},{4,0},{5,1},{6,2},{7,3},{8,12},{9,13},{10,... | collective-permute-start | bytes 270344 | tf_op jit(solution)/shard_map/ppermute | solution.py:34
  7.4 1.7 %collective-permute-start.3 = (bf16[8,2560]{1,0:T(8,128)(2,1)}, bf16[8,2560]{1,0:T(8,128)(2,1)S(1)}, u32[]{:S(2)}, u32[]{:S(2)}) collective-permute-start(bf16[8,2560]{1,0:T(8,128)(2,1)} %get-tuple-element.42), channel_id=1, source_target_pairs={{0,2},{1,3},{2,0},{3,1},{4,6},{5,7},{6,4},{7,5},{8,10},{9,11},{10,... | collective-permute-start | bytes 122888 | tf_op jit(solution)/shard_map/ppermute | solution.py:34
  9.2 1.8 %pad_maximum_fusion.refs_5_.refs_9_ = bf16[128,8192]{1,0:T(8,128)(2,1)S(1)} fusion(bf16[64,8192]{1,0:T(8,128)(2,1)} %bitcast.19, bf16[64,8192]{1,0:T(8,128)(2,1)} %bitcast.20), kind=kLoop, calls=%fused_computation | loop fusion | flops 4194304 | bytes 4194304 | tf_op jit(solution)/shard_map/concatenate | solution.py:639
  11.7 2.3 %collective-permute-done.2 = bf16[8,5632]{1,0:T(8,128)(2,1)S(1)} collective-permute-done((bf16[8,5632]{1,0:T(8,128)(2,1)}, bf16[8,5632]{1,0:T(8,128)(2,1)S(1)}, u32[]{:S(2)}, u32[]{:S(2)}) %collective-permute-start.2) | collective-permute-done | bytes 90144 | tf_op jit(solution)/shard_map/ppermute | solution.py:34
  14.1 1.6 %collective-permute-start.4 = (bf16[32,5632]{1,0:T(8,128)(2,1)S(1)}, bf16[32,5632]{1,0:T(8,128)(2,1)S(1)}, u32[]{:S(2)}, u32[]{:S(2)}) collective-permute-start(bf16[32,5632]{1,0:T(8,128)(2,1)S(1)} %pad_maximum_fusion.1.refs_0_), channel_id=1, source_target_pairs={{0,2},{1,3},{2,0},{3,1},{4,6},{5,7},{6,4},{7,5},{8,10},{9,11},{10,... | collective-permute-start | bytes 1081352 | tf_op jit(solution)/shard_map/ppermute | solution.py:34
  15.6 3.1 %collective-permute-start.5 = (bf16[16,2560]{1,0:T(8,128)(2,1)S(1)}, bf16[16,2560]{1,0:T(8,128)(2,1)S(1)}, u32[]{:S(2)}, u32[]{:S(2)}) collective-permute-start(bf16[16,2560]{1,0:T(8,128)(2,1)S(1)} %pad_maximum_fusion.2.refs_0_), channel_id=1, source_target_pairs={{0,8},{1,9},{2,10},{3,11},{4,12},{5,13},{6,14},{7,15},{8,0},{9,1},... | collective-permute-start | bytes 245768 | tf_op jit(solution)/shard_map/ppermute | solution.py:34
  18.7 1.5 %collective-permute-start.7 = (bf16[16,2560]{1,0:T(8,128)(2,1)S(1)}, bf16[16,2560]{1,0:T(8,128)(2,1)S(1)}, u32[]{:S(2)}, u32[]{:S(2)}) collective-permute-start(bf16[16,2560]{1,0:T(8,128)(2,1)S(1)} %pad_maximum_fusion.2.refs_0_), channel_id=1, source_target_pairs={{0,12},{1,13},{2,14},{3,15},{4,8},{5,9},{6,10},{7,11},{8,4},{9,5},... | collective-permute-start | bytes 245768 | tf_op jit(solution)/shard_map/ppermute | solution.py:34
  20.2 3.4 %fetch.2.refs_4_.refs_8_ = bf16[8192,512]{1,0:T(8,128)(2,1)S(1)} custom-call(bf16[8192,512]{1,0:T(8,128)(2,1)} %refs_0_), custom_call_target="tpu_custom_call" | custom-call | bytes 16777216 | tf_op jit(solution)/shard_map/fetch/pallas_call | solution.py:319
  24.0 1.4 %collective-permute-done.6.refs_2_ = bf16[16,2560]{1,0:T(8,128)(2,1)S(1)} collective-permute-done((bf16[16,2560]{1,0:T(8,128)(2,1)S(1)}, bf16[16,2560]{1,0:T(8,128)(2,1)S(1)}, u32[]{:S(2)}, u32[]{:S(2)}) %collective-permute-start.6) | collective-permute-done | bytes 81952 | tf_op jit(solution)/shard_map/ppermute | solution.py:34
  28.4 1.6 %project.3 = bf16[256,640]{1,0:T(8,128)(2,1)} custom-call(bf16[16,2560]{1,0:T(8,128)(2,1)S(1)} %pad_maximum_fusion.2.refs_0_, bf16[16,2560]{1,0:T(8,128)(2,1)S(1)} %collective-permute-done.5.refs_1_, bf16[16,2560]{1,0:T(8,128)(2,1)S(1)} %collective-permute-done.6.refs_2_, bf16[16,2560]{1,0:T(8,128)(2,1)S(1)} %collective-permute-done.7.refs_3_, ...), custom_call_target="tpu_custom_call" | custom-call | flops 419430400 | bytes 3276800 | tf_op jit(solution)/shard_map/project/pallas_call | solution.py:397
  30.0 4.4 %all-to-all-start = ((bf16[16,16,640]{2,1,0:T(8,128)(2,1)}), bf16[16,16,640]{2,1,0:T(8,128)(2,1)S(1)}, u32[]{:S(2)}, u32[]{:S(2)}) async-start(bf16[16,16,640]{2,1,0:T(8,128)(2,1)} %bitcast.4), calls=%async_computation | async-start | bytes 655360 | tf_op jit(solution)/shard_map/all_to_all | solution.py:661
  35.1 10.4 %all-to-all-done.inbound = bf16[16,16,640]{2,1,0:T(8,128)(2,1)S(1)} async-done(((bf16[16,16,640]{2,1,0:T(8,128)(2,1)}), bf16[16,16,640]{2,1,0:T(8,128)(2,1)S(1)}, u32[]{:S(2)}, u32[]{:S(2)}) %all-to-all-start) | async-done | bytes 327712 | tf_op jit(solution)/shard_map/all_to_all | solution.py:661
  45.5 5.9 %attend.1 = bf16[16,16,512]{2,1,0:T(8,128)(2,1)} custom-call(s32[16,4]{1,0:T(8,128)S(1)} %copy.15.table, s32[2,1,128]{2,1,0:T(1,128)S(1)} %bitcast.14, bf16[16,16,640]{2,1,0:T(8,128)(2,1)S(1)} %all-to-all-done.inbound, f32[16,128]{1,0:T(8,128)S(1)} %get-tuple-element.90.cosine, f32[16,128]{1,0:T(8,128)S(1)} %get-tuple-element.91.sine, ...), custom_call_target="tpu_custom_call" | custom-call | flops 134217728 | bytes 8388608 | tf_op jit(solution)/shard_map/attend/pallas_call | solution.py:578
  51.4 3.5 %all-to-all-start.1 = ((bf16[16,16,512]{2,1,0:T(8,128)(2,1)}), bf16[16,16,512]{2,1,0:T(8,128)(2,1)S(1)}, u32[]{:S(2)}, u32[]{:S(2)}) async-start(bf16[16,16,512]{2,1,0:T(8,128)(2,1)} %attend.1), calls=%async_computation.1 | async-start | bytes 524288 | tf_op jit(solution)/shard_map/all_to_all | solution.py:674
  55.0 1.8 %fetch.3.w_front = bf16[512,2560]{1,0:T(8,128)(2,1)S(1)} custom-call(bf16[512,8192]{1,0:T(8,128)(2,1)} %w_out.1), custom_call_target="tpu_custom_call" | custom-call | bytes 5242880 | tf_op jit(solution)/shard_map/fetch/pallas_call | solution.py:319
  56.7 8.2 %all-to-all-done.1 = bf16[16,16,512]{2,1,0:T(8,128)(2,1)S(1)} async-done(((bf16[16,16,512]{2,1,0:T(8,128)(2,1)}), bf16[16,16,512]{2,1,0:T(8,128)(2,1)S(1)}, u32[]{:S(2)}, u32[]{:S(2)}) %all-to-all-start.1) | async-done | bytes 262176 | tf_op jit(solution)/shard_map/all_to_all | solution.py:674
  65.0 3.2 %product.1 = (bf16[64,5376]{1,0:T(8,128)(2,1)S(1)}, f32[64,5376]{1,0:T(8,128)S(1)}, bf16[64,2816]{1,0:T(8,128)(2,1)S(1)}, f32[64,2816]{1,0:T(8,128)S(1)}) custom-call(s32[1,128]{1,0:T(1,128)S(1)} %get-tuple-element.50.place_a, s32[1,128]{1,0:T(1,128)S(1)} %get-tuple-element.51.place_b, bf16[256,512]{1,0:T(8,128)(2,1)S(1)} %bitcast.13, ...), custom_call_target="tpu_custom_call" | custom-call | flops 1073741824 | bytes 8388608 | tf_op jit(solution)/shard_map/product/pallas_call | solution.py:155
  68.2 2.1 %collective-permute-done.14 = bf16[64,5376]{1,0:T(8,128)(2,1)S(1)} collective-permute-done((bf16[64,5376]{1,0:T(8,128)(2,1)S(1)}, bf16[64,5376]{1,0:T(8,128)(2,1)S(1)}, u32[]{:S(2)}, u32[]{:S(2)}) %collective-permute-start.14) | collective-permute-done | bytes 688160 | tf_op jit(solution)/shard_map/ppermute | solution.py:34
  74.0 2.9 %collective-permute-start.22 = (bf16[16,2816]{1,0:T(8,128)(2,1)S(1)}, bf16[16,2816]{1,0:T(8,128)(2,1)S(1)}, u32[]{:S(2)}, u32[]{:S(2)}) collective-permute-start(bf16[16,2816]{1,0:T(8,128)(2,1)S(1)} %get-tuple-element.82), channel_id=1, source_target_pairs={{0,12},{1,13},{2,14},{3,15},{4,8},{5,9},{6,10},{7,11},{8,4},{9,5},... | collective-permute-start | bytes 270344 | tf_op jit(solution)/shard_map/ppermute | solution.py:34
  76.9 4.2 %collective-permute-done.15 = bf16[32,5376]{1,0:T(8,128)(2,1)S(1)} collective-permute-done((bf16[32,5376]{1,0:T(8,128)(2,1)S(1)}, bf16[32,5376]{1,0:T(8,128)(2,1)S(1)}, u32[]{:S(2)}, u32[]{:S(2)}) %collective-permute-start.15) | collective-permute-done | bytes 344096 | tf_op jit(solution)/shard_map/ppermute | solution.py:34
  83.1 2.6 %collective-permute-start.20 = (bf16[8,5376]{1,0:T(8,128)(2,1)S(1)}, bf16[8,5376]{1,0:T(8,128)(2,1)S(1)}, u32[]{:S(2)}, u32[]{:S(2)}) collective-permute-start(bf16[8,5376]{1,0:T(8,128)(2,1)S(1)} %get-tuple-element.84), channel_id=1, source_target_pairs={{0,12},{1,13},{2,14},{3,15},{4,8},{5,9},{6,10},{7,11},{8,4},{9,5},... | collective-permute-start | bytes 258056 | tf_op jit(solution)/shard_map/ppermute | solution.py:34
  86.1 4.2 %collective-permute-done.18 = bf16[8,5376]{1,0:T(8,128)(2,1)S(1)} collective-permute-done((bf16[8,5376]{1,0:T(8,128)(2,1)S(1)}, bf16[8,5376]{1,0:T(8,128)(2,1)S(1)}, u32[]{:S(2)}, u32[]{:S(2)}) %collective-permute-start.18) | collective-permute-done | bytes 86048 | tf_op jit(solution)/shard_map/ppermute | solution.py:34
  (72 shorter events, 11.6 us)
Async XLA Ops:
  1.7 9.9 %collective-permute-start = (bf16[8,5632]{1,0:T(8,128)(2,1)}, bf16[8,5632]{1,0:T(8,128)(2,1)S(1)}, u32[]{:S(2)}, u32[]{:S(2)}) collective-permute-start(bf16[8,5632]{1,0:T(8,128)(2,1)} %get-tuple-element.41), channel_id=1, source_target_pairs={{0,8},{1,9},{2,10},{3,11},{4,12},{5,13},{6,14},{7,15},{8,0},{9,1},... | collective-permute-start | bytes 270344 | tf_op jit(solution)/shard_map/ppermute | solution.py:34
  5.8 5.8 %collective-permute-start.1 = (bf16[8,5632]{1,0:T(8,128)(2,1)}, bf16[8,5632]{1,0:T(8,128)(2,1)S(1)}, u32[]{:S(2)}, u32[]{:S(2)}) collective-permute-start(bf16[8,5632]{1,0:T(8,128)(2,1)} %get-tuple-element.41), channel_id=1, source_target_pairs={{0,4},{1,5},{2,6},{3,7},{4,0},{5,1},{6,2},{7,3},{8,12},{9,13},{10,... | collective-permute-start | bytes 270344 | tf_op jit(solution)/shard_map/ppermute | solution.py:34
  7.4 6.6 %collective-permute-start.2 = (bf16[8,5632]{1,0:T(8,128)(2,1)}, bf16[8,5632]{1,0:T(8,128)(2,1)S(1)}, u32[]{:S(2)}, u32[]{:S(2)}) collective-permute-start(bf16[8,5632]{1,0:T(8,128)(2,1)} %get-tuple-element.41), channel_id=1, source_target_pairs={{0,12},{1,13},{2,14},{3,15},{4,8},{5,9},{6,10},{7,11},{8,4},{9,5},... | collective-permute-start | bytes 270344 | tf_op jit(solution)/shard_map/ppermute | solution.py:34
  7.4 4.2 %collective-permute-start.3 = (bf16[8,2560]{1,0:T(8,128)(2,1)}, bf16[8,2560]{1,0:T(8,128)(2,1)S(1)}, u32[]{:S(2)}, u32[]{:S(2)}) collective-permute-start(bf16[8,2560]{1,0:T(8,128)(2,1)} %get-tuple-element.42), channel_id=1, source_target_pairs={{0,2},{1,3},{2,0},{3,1},{4,6},{5,7},{6,4},{7,5},{8,10},{9,11},{10,... | collective-permute-start | bytes 122888 | tf_op jit(solution)/shard_map/ppermute | solution.py:34
  14.1 11.3 %collective-permute-start.4 = (bf16[32,5632]{1,0:T(8,128)(2,1)S(1)}, bf16[32,5632]{1,0:T(8,128)(2,1)S(1)}, u32[]{:S(2)}, u32[]{:S(2)}) collective-permute-start(bf16[32,5632]{1,0:T(8,128)(2,1)S(1)} %pad_maximum_fusion.1.refs_0_), channel_id=1, source_target_pairs={{0,2},{1,3},{2,0},{3,1},{4,6},{5,7},{6,4},{7,5},{8,10},{9,11},{10,... | collective-permute-start | bytes 1081352 | tf_op jit(solution)/shard_map/ppermute | solution.py:34
  15.6 8.4 %collective-permute-start.5 = (bf16[16,2560]{1,0:T(8,128)(2,1)S(1)}, bf16[16,2560]{1,0:T(8,128)(2,1)S(1)}, u32[]{:S(2)}, u32[]{:S(2)}) collective-permute-start(bf16[16,2560]{1,0:T(8,128)(2,1)S(1)} %pad_maximum_fusion.2.refs_0_), channel_id=1, source_target_pairs={{0,8},{1,9},{2,10},{3,11},{4,12},{5,13},{6,14},{7,15},{8,0},{9,1},... | collective-permute-start | bytes 245768 | tf_op jit(solution)/shard_map/ppermute | solution.py:34
  18.7 6.7 %collective-permute-start.6 = (bf16[16,2560]{1,0:T(8,128)(2,1)S(1)}, bf16[16,2560]{1,0:T(8,128)(2,1)S(1)}, u32[]{:S(2)}, u32[]{:S(2)}) collective-permute-start(bf16[16,2560]{1,0:T(8,128)(2,1)S(1)} %pad_maximum_fusion.2.refs_0_), channel_id=1, source_target_pairs={{0,4},{1,5},{2,6},{3,7},{4,0},{5,1},{6,2},{7,3},{8,12},{9,13},{10,... | collective-permute-start | bytes 245768 | tf_op jit(solution)/shard_map/ppermute | solution.py:34
  18.7 6.7 %collective-permute-start.7 = (bf16[16,2560]{1,0:T(8,128)(2,1)S(1)}, bf16[16,2560]{1,0:T(8,128)(2,1)S(1)}, u32[]{:S(2)}, u32[]{:S(2)}) collective-permute-start(bf16[16,2560]{1,0:T(8,128)(2,1)S(1)} %pad_maximum_fusion.2.refs_0_), channel_id=1, source_target_pairs={{0,12},{1,13},{2,14},{3,15},{4,8},{5,9},{6,10},{7,11},{8,4},{9,5},... | collective-permute-start | bytes 245768 | tf_op jit(solution)/shard_map/ppermute | solution.py:34
  20.2 6.2 %collective-permute-start.12 = (bf16[32,5632]{1,0:T(8,128)(2,1)S(1)}, bf16[32,5632]{1,0:T(8,128)(2,1)S(1)}, u32[]{:S(2)}, u32[]{:S(2)}) collective-permute-start(bf16[32,5632]{1,0:T(8,128)(2,1)S(1)} %pad_maximum_fusion.1.refs_0_), channel_id=1, source_target_pairs={{0,1},{1,0},{2,3},{3,2},{4,5},{5,4},{6,7},{7,6},{8,9},{9,8},{10,11... | collective-permute-start | bytes 1081352 | tf_op jit(solution)/shard_map/ppermute | solution.py:34
  25.4 3.0 %collective-permute-start.10 = (bf16[16,2560]{1,0:T(8,128)(2,1)S(1)}, bf16[16,2560]{1,0:T(8,128)(2,1)S(1)}, u32[]{:S(2)}, u32[]{:S(2)}) collective-permute-start(bf16[16,2560]{1,0:T(8,128)(2,1)S(1)} %collective-permute-done.6.refs_2_), channel_id=1, source_target_pairs={{0,1},{1,0},{2,3},{3,2},{4,5},{5,4},{6,7},{7,6},{8,9},{9,8},{10,11... | collective-permute-start | bytes 245768 | tf_op jit(solution)/shard_map/ppermute | solution.py:34
  25.9 2.5 %collective-permute-start.11 = (bf16[16,2560]{1,0:T(8,128)(2,1)S(1)}, bf16[16,2560]{1,0:T(8,128)(2,1)S(1)}, u32[]{:S(2)}, u32[]{:S(2)}) collective-permute-start(bf16[16,2560]{1,0:T(8,128)(2,1)S(1)} %collective-permute-done.7.refs_3_), channel_id=1, source_target_pairs={{0,1},{1,0},{2,3},{3,2},{4,5},{5,4},{6,7},{7,6},{8,9},{9,8},{10,11... | collective-permute-start | bytes 245768 | tf_op jit(solution)/shard_map/ppermute | solution.py:34
  26.0 2.4 %collective-permute-start.8 = (bf16[16,2560]{1,0:T(8,128)(2,1)S(1)}, bf16[16,2560]{1,0:T(8,128)(2,1)S(1)}, u32[]{:S(2)}, u32[]{:S(2)}) collective-permute-start(bf16[16,2560]{1,0:T(8,128)(2,1)S(1)} %pad_maximum_fusion.2.refs_0_), channel_id=1, source_target_pairs={{0,1},{1,0},{2,3},{3,2},{4,5},{5,4},{6,7},{7,6},{8,9},{9,8},{10,11... | collective-permute-start | bytes 245768 | tf_op jit(solution)/shard_map/ppermute | solution.py:34
  26.4 2.0 %collective-permute-start.9 = (bf16[16,2560]{1,0:T(8,128)(2,1)S(1)}, bf16[16,2560]{1,0:T(8,128)(2,1)S(1)}, u32[]{:S(2)}, u32[]{:S(2)}) collective-permute-start(bf16[16,2560]{1,0:T(8,128)(2,1)S(1)} %collective-permute-done.5.refs_1_), channel_id=1, source_target_pairs={{0,1},{1,0},{2,3},{3,2},{4,5},{5,4},{6,7},{7,6},{8,9},{9,8},{10,11... | collective-permute-start | bytes 245768 | tf_op jit(solution)/shard_map/ppermute | solution.py:34
  30.0 15.5 %all-to-all-start = ((bf16[16,16,640]{2,1,0:T(8,128)(2,1)}), bf16[16,16,640]{2,1,0:T(8,128)(2,1)S(1)}, u32[]{:S(2)}, u32[]{:S(2)}) async-start(bf16[16,16,640]{2,1,0:T(8,128)(2,1)} %bitcast.4), calls=%async_computation | async-start | bytes 655360 | tf_op jit(solution)/shard_map/all_to_all | solution.py:661
  51.4 13.6 %all-to-all-start.1 = ((bf16[16,16,512]{2,1,0:T(8,128)(2,1)}), bf16[16,16,512]{2,1,0:T(8,128)(2,1)S(1)}, u32[]{:S(2)}, u32[]{:S(2)}) async-start(bf16[16,16,512]{2,1,0:T(8,128)(2,1)} %attend.1), calls=%async_computation.1 | async-start | bytes 524288 | tf_op jit(solution)/shard_map/all_to_all | solution.py:674
  68.2 2.2 %collective-permute-start.14 = (bf16[64,5376]{1,0:T(8,128)(2,1)S(1)}, bf16[64,5376]{1,0:T(8,128)(2,1)S(1)}, u32[]{:S(2)}, u32[]{:S(2)}) collective-permute-start(bf16[64,5376]{1,0:T(8,128)(2,1)S(1)} %get-tuple-element.69), channel_id=1, source_target_pairs={{0,1},{1,0},{2,3},{3,2},{4,5},{5,4},{6,7},{7,6},{8,9},{9,8},{10,11... | collective-permute-start | bytes 2064392 | tf_op jit(solution)/shard_map/ppermute | solution.py:34
  70.8 10.3 %collective-permute-start.15 = (bf16[32,5376]{1,0:T(8,128)(2,1)S(1)}, bf16[32,5376]{1,0:T(8,128)(2,1)S(1)}, u32[]{:S(2)}, u32[]{:S(2)}) collective-permute-start(bf16[32,5376]{1,0:T(8,128)(2,1)S(1)} %slice.87), channel_id=1, source_target_pairs={{0,2},{1,3},{2,0},{3,1},{4,6},{5,7},{6,4},{7,5},{8,10},{9,11},{10,... | collective-permute-start | bytes 1032200 | tf_op jit(solution)/shard_map/ppermute | solution.py:34
  72.4 8.7 %collective-permute-start.17 = (bf16[16,2816]{1,0:T(8,128)(2,1)S(1)}, bf16[16,2816]{1,0:T(8,128)(2,1)S(1)}, u32[]{:S(2)}, u32[]{:S(2)}) collective-permute-start(bf16[16,2816]{1,0:T(8,128)(2,1)S(1)} %get-tuple-element.81), channel_id=1, source_target_pairs={{0,8},{1,9},{2,10},{3,11},{4,12},{5,13},{6,14},{7,15},{8,0},{9,1},... | collective-permute-start | bytes 270344 | tf_op jit(solution)/shard_map/ppermute | solution.py:34
  73.5 12.2 %collective-permute-start.21 = (bf16[16,2816]{1,0:T(8,128)(2,1)S(1)}, bf16[16,2816]{1,0:T(8,128)(2,1)S(1)}, u32[]{:S(2)}, u32[]{:S(2)}) collective-permute-start(bf16[16,2816]{1,0:T(8,128)(2,1)S(1)} %get-tuple-element.83), channel_id=1, source_target_pairs={{0,4},{1,5},{2,6},{3,7},{4,0},{5,1},{6,2},{7,3},{8,12},{9,13},{10,... | collective-permute-start | bytes 270344 | tf_op jit(solution)/shard_map/ppermute | solution.py:34
  74.0 11.7 %collective-permute-start.22 = (bf16[16,2816]{1,0:T(8,128)(2,1)S(1)}, bf16[16,2816]{1,0:T(8,128)(2,1)S(1)}, u32[]{:S(2)}, u32[]{:S(2)}) collective-permute-start(bf16[16,2816]{1,0:T(8,128)(2,1)S(1)} %get-tuple-element.82), channel_id=1, source_target_pairs={{0,12},{1,13},{2,14},{3,15},{4,8},{5,9},{6,10},{7,11},{8,4},{9,5},... | collective-permute-start | bytes 270344 | tf_op jit(solution)/shard_map/ppermute | solution.py:34
  81.2 9.1 %collective-permute-start.18 = (bf16[8,5376]{1,0:T(8,128)(2,1)S(1)}, bf16[8,5376]{1,0:T(8,128)(2,1)S(1)}, u32[]{:S(2)}, u32[]{:S(2)}) collective-permute-start(bf16[8,5376]{1,0:T(8,128)(2,1)S(1)} %get-tuple-element.86), channel_id=1, source_target_pairs={{0,8},{1,9},{2,10},{3,11},{4,12},{5,13},{6,14},{7,15},{8,0},{9,1},... | collective-permute-start | bytes 258056 | tf_op jit(solution)/shard_map/ppermute | solution.py:34
  82.3 8.0 %collective-permute-start.19 = (bf16[8,5376]{1,0:T(8,128)(2,1)S(1)}, bf16[8,5376]{1,0:T(8,128)(2,1)S(1)}, u32[]{:S(2)}, u32[]{:S(2)}) collective-permute-start(bf16[8,5376]{1,0:T(8,128)(2,1)S(1)} %get-tuple-element.85), channel_id=1, source_target_pairs={{0,4},{1,5},{2,6},{3,7},{4,0},{5,1},{6,2},{7,3},{8,12},{9,13},{10,... | collective-permute-start | bytes 258056 | tf_op jit(solution)/shard_map/ppermute | solution.py:34
  83.1 7.2 %collective-permute-start.20 = (bf16[8,5376]{1,0:T(8,128)(2,1)S(1)}, bf16[8,5376]{1,0:T(8,128)(2,1)S(1)}, u32[]{:S(2)}, u32[]{:S(2)}) collective-permute-start(bf16[8,5376]{1,0:T(8,128)(2,1)S(1)} %get-tuple-element.84), channel_id=1, source_target_pairs={{0,12},{1,13},{2,14},{3,15},{4,8},{5,9},{6,10},{7,11},{8,4},{9,5},... | collective-permute-start | bytes 258056 | tf_op jit(solution)/shard_map/ppermute | solution.py:34
  85.7 4.6 %collective-permute-start.23 = (bf16[8,2816]{1,0:T(8,128)(2,1)S(1)}, bf16[8,2816]{1,0:T(8,128)(2,1)S(1)}, u32[]{:S(2)}, u32[]{:S(2)}) collective-permute-start(bf16[8,2816]{1,0:T(8,128)(2,1)S(1)} %slice.88), channel_id=1, source_target_pairs={{0,2},{1,3},{2,0},{3,1},{4,6},{5,7},{6,4},{7,5},{8,10},{9,11},{10,... | collective-permute-start | bytes 135176 | tf_op jit(solution)/shard_map/ppermute | solution.py:34
  (8 other events, 43.0 us)

commit v18 on v17

--- a/solution.py
+++ b/solution.py
@@ -444,16 +444,24 @@
     batches = query_rot.shape[1]
     batch = slots // batches
 
-    cuts = 16
+    cuts = 8
     size = key_pages.shape[0] // cuts
-
-    def fetch_pool(pool, on_chip, sem):
-        for cut in range(cuts):
-            part = pl.ds(cut * size, size)
-            pltpu.make_async_copy(pool.at[part], on_chip.at[part], sem).start()
-
-    fetch_pool(key_pages, key_pool, sems.at[0])
-    fetch_pool(value_pages, value_pool, sems.at[1])
+    width = kv_width // 2
+    for i, (pool, on_chip) in enumerate(((key_pages, key_pool), (value_pages, value_pool))):
+        for half in range(2):
+            for cut in range(cuts):
+                part = pl.ds(cut * size, size)
+                pltpu.make_async_copy(
+                    pool.at[part, :, pl.ds(half * width, width)],
+                    on_chip.at[half, part],
+                    sems.at[i, half],
+                ).start()
+
+    def arrived(on_chip, i, p):
+        half, inside = divmod(p * 2 * HEAD, width)
+        if inside == 0:
+            pltpu.make_async_copy(on_chip.at[half], on_chip.at[half], sems.at[i, half]).wait()
+        return on_chip.at[half], slice(inside, inside + 2 * HEAD)
 
     def held(pool, slot, columns):
         return [pool[table[slot, j], :, columns] for j in range(pages)]
@@ -498,9 +506,8 @@
     )
 
     own_chances = {}
-    pltpu.make_async_copy(key_pool, key_pool, sems.at[0]).wait()
     for p in range(pairs):
-        columns_p = slice(p * 2 * HEAD, (p + 1) * 2 * HEAD)
+        key_half, columns_p = arrived(key_pool, 0, p)
         for b in range(batches):
             valid = row < lengths[b]
             turned = query_rot[p, b].T.astype(jnp.bfloat16)
@@ -510,8 +517,8 @@
             )
             keys = []
             for s in range(batch):
-                keys += held(key_pool, b * batch + s, columns_p)
-            keys.append(key_new[:, columns_p])
+                keys += held(key_half, b * batch + s, columns_p)
+            keys.append(key_new[:, p * 2 * HEAD : (p + 1) * 2 * HEAD])
             products = jnp.dot(
                 jnp.concatenate(keys, axis=0), wide, preferred_element_type=jnp.float32
             )
@@ -531,13 +538,12 @@
                 jnp.where(same, own_chance, 0.0), axis=1, keepdims=True
             )
 
-    pltpu.make_async_copy(value_pool, value_pool, sems.at[1]).wait()
     for p in range(pairs):
-        columns_p = slice(p * 2 * HEAD, (p + 1) * 2 * HEAD)
+        value_half, columns_p = arrived(value_pool, 1, p)
         for b in range(batches):
             for s in range(batch):
                 mine = chance[p, b, pl.ds(s, pair, stride=batch)].astype(jnp.bfloat16)
-                values = held(value_pool, b * batch + s, columns_p)
+                values = held(value_half, b * batch + s, columns_p)
                 both = jnp.dot(
                     mine, jnp.concatenate(values, axis=0), preferred_element_type=jnp.float32
                 )
@@ -581,9 +587,9 @@
         out_specs=vmem,
         out_shape=jax.ShapeDtypeStruct((owners, slots, per_query), jnp.bfloat16),
         scratch_shapes=[
-            pltpu.VMEM(key_pages.shape, jnp.bfloat16),
-            pltpu.VMEM(value_pages.shape, jnp.bfloat16),
-            pltpu.SemaphoreType.DMA((2,)),
+            pltpu.VMEM((2, *key_pages.shape[:2], kv_width // 2), jnp.bfloat16),
+            pltpu.VMEM((2, *key_pages.shape[:2], kv_width // 2), jnp.bfloat16),
+            pltpu.SemaphoreType.DMA((2, 2)),
             pltpu.VMEM((slots, kv_width), jnp.bfloat16),
             pltpu.VMEM((pairs, batches, columns, HEAD), jnp.float32),
             pltpu.VMEM((kv_heads, slots, HEAD), jnp.float32),

time: 91.5 us -> 91.5 us (level)
  no operation moved by 1% of the time
where the time goes in v18:
time: 91.5 us; the launch traced here: 91.1 us
  waiting for transfers between devices  35.6 us (39%)
  starting transfers between devices  32.5 us (36%)
  Pallas kernels  19 us (21%)
  other arithmetic  3.29 us (4%)
    ppermute x24, starting transfers between devices, send(): return lax.ppermute(x, AXES, pairs)  24.6 us
    ppermute x24, waiting for transfers between devices, send(): return lax.ppermute(x, AXES, pairs)  16.9 us
    all_to_all x1, waiting for transfers between devices, on_device(): lax.all_to_all(outbound, AXES, split_axis=0, concat_axis=0, tiled=True)  10.4 us
    all_to_all x1, waiting for transfers between devices, on_device(): lax.all_to_all(attended, AXES, split_axis=0, concat_axis=0, tiled=True)  8.25 us
    pallas_call x1, Pallas kernels, attend(): pl.pallas_call(functools.partial(attend_kernel, per_query, per_key), in_s...  5.88 us
    pallas_call x2, Pallas kernels, fetch(): pl.pallas_call(functools.partial(fetch_kernel, starts), in_specs=[pl.Bloc...  5.14 us
    all_to_all x1, starting transfers between devices, on_device(): lax.all_to_all(outbound, AXES, split_axis=0, concat_axis=0, tiled=True)  4.41 us
    all_to_all x1, starting transfers between devices, on_device(): lax.all_to_all(attended, AXES, split_axis=0, concat_axis=0, tiled=True)  3.54 us
  transfers between devices with their start and end apart: 26, of which 11 were waited for; matrix products, arithmetic and copies ran while one was open for 3% of the time, Pallas kernels for 7%

profile of v18, /device:TPU:0, one launch (start us, length us, event | category | flops | bytes accessed | tf_op | source)
XLA Modules:
  0.0 91.1 jit_solution(9533205938860530678)
XLA Ops:
  0.0 1.7 %norm.1 = (bf16[8,5632]{1,0:T(8,128)(2,1)}, bf16[8,2560]{1,0:T(8,128)(2,1)}) custom-call(bf16[8,8192]{1,0:T(8,128)(2,1)} %x.1, f32[1,8192]{1,0:T(1,128)} %bitcast.21), custom_call_target="tpu_custom_call" | custom-call | tf_op jit(solution)/shard_map/norm/pallas_call | solution.py:229
  1.7 4.1 %collective-permute-start = (bf16[8,5632]{1,0:T(8,128)(2,1)}, bf16[8,5632]{1,0:T(8,128)(2,1)S(1)}, u32[]{:S(2)}, u32[]{:S(2)}) collective-permute-start(bf16[8,5632]{1,0:T(8,128)(2,1)} %get-tuple-element.41), channel_id=1, source_target_pairs={{0,8},{1,9},{2,10},{3,11},{4,12},{5,13},{6,14},{7,15},{8,0},{9,1},... | collective-permute-start | bytes 270344 | tf_op jit(solution)/shard_map/ppermute | solution.py:34
  5.8 1.6 %collective-permute-start.1 = (bf16[8,5632]{1,0:T(8,128)(2,1)}, bf16[8,5632]{1,0:T(8,128)(2,1)S(1)}, u32[]{:S(2)}, u32[]{:S(2)}) collective-permute-start(bf16[8,5632]{1,0:T(8,128)(2,1)} %get-tuple-element.41), channel_id=1, source_target_pairs={{0,4},{1,5},{2,6},{3,7},{4,0},{5,1},{6,2},{7,3},{8,12},{9,13},{10,... | collective-permute-start | bytes 270344 | tf_op jit(solution)/shard_map/ppermute | solution.py:34
  7.4 1.7 %collective-permute-start.3 = (bf16[8,2560]{1,0:T(8,128)(2,1)}, bf16[8,2560]{1,0:T(8,128)(2,1)S(1)}, u32[]{:S(2)}, u32[]{:S(2)}) collective-permute-start(bf16[8,2560]{1,0:T(8,128)(2,1)} %get-tuple-element.42), channel_id=1, source_target_pairs={{0,2},{1,3},{2,0},{3,1},{4,6},{5,7},{6,4},{7,5},{8,10},{9,11},{10,... | collective-permute-start | bytes 122888 | tf_op jit(solution)/shard_map/ppermute | solution.py:34
  9.2 1.8 %pad_maximum_fusion.refs_5_.refs_9_ = bf16[128,8192]{1,0:T(8,128)(2,1)S(1)} fusion(bf16[64,8192]{1,0:T(8,128)(2,1)} %bitcast.19, bf16[64,8192]{1,0:T(8,128)(2,1)} %bitcast.20), kind=kLoop, calls=%fused_computation | loop fusion | flops 4194304 | bytes 4194304 | tf_op jit(solution)/shard_map/concatenate | solution.py:645
  11.7 2.3 %collective-permute-done.2 = bf16[8,5632]{1,0:T(8,128)(2,1)S(1)} collective-permute-done((bf16[8,5632]{1,0:T(8,128)(2,1)}, bf16[8,5632]{1,0:T(8,128)(2,1)S(1)}, u32[]{:S(2)}, u32[]{:S(2)}) %collective-permute-start.2) | collective-permute-done | bytes 90144 | tf_op jit(solution)/shard_map/ppermute | solution.py:34
  14.1 1.6 %collective-permute-start.4 = (bf16[32,5632]{1,0:T(8,128)(2,1)S(1)}, bf16[32,5632]{1,0:T(8,128)(2,1)S(1)}, u32[]{:S(2)}, u32[]{:S(2)}) collective-permute-start(bf16[32,5632]{1,0:T(8,128)(2,1)S(1)} %pad_maximum_fusion.1.refs_0_), channel_id=1, source_target_pairs={{0,2},{1,3},{2,0},{3,1},{4,6},{5,7},{6,4},{7,5},{8,10},{9,11},{10,... | collective-permute-start | bytes 1081352 | tf_op jit(solution)/shard_map/ppermute | solution.py:34
  15.6 3.1 %collective-permute-start.5 = (bf16[16,2560]{1,0:T(8,128)(2,1)S(1)}, bf16[16,2560]{1,0:T(8,128)(2,1)S(1)}, u32[]{:S(2)}, u32[]{:S(2)}) collective-permute-start(bf16[16,2560]{1,0:T(8,128)(2,1)S(1)} %pad_maximum_fusion.2.refs_0_), channel_id=1, source_target_pairs={{0,8},{1,9},{2,10},{3,11},{4,12},{5,13},{6,14},{7,15},{8,0},{9,1},... | collective-permute-start | bytes 245768 | tf_op jit(solution)/shard_map/ppermute | solution.py:34
  18.7 1.5 %collective-permute-start.7 = (bf16[16,2560]{1,0:T(8,128)(2,1)S(1)}, bf16[16,2560]{1,0:T(8,128)(2,1)S(1)}, u32[]{:S(2)}, u32[]{:S(2)}) collective-permute-start(bf16[16,2560]{1,0:T(8,128)(2,1)S(1)} %pad_maximum_fusion.2.refs_0_), channel_id=1, source_target_pairs={{0,12},{1,13},{2,14},{3,15},{4,8},{5,9},{6,10},{7,11},{8,4},{9,5},... | collective-permute-start | bytes 245768 | tf_op jit(solution)/shard_map/ppermute | solution.py:34
  20.2 3.4 %fetch.2.refs_4_.refs_8_ = bf16[8192,512]{1,0:T(8,128)(2,1)S(1)} custom-call(bf16[8192,512]{1,0:T(8,128)(2,1)} %refs_0_), custom_call_target="tpu_custom_call" | custom-call | bytes 16777216 | tf_op jit(solution)/shard_map/fetch/pallas_call | solution.py:319
  24.0 1.4 %collective-permute-done.6.refs_2_ = bf16[16,2560]{1,0:T(8,128)(2,1)S(1)} collective-permute-done((bf16[16,2560]{1,0:T(8,128)(2,1)S(1)}, bf16[16,2560]{1,0:T(8,128)(2,1)S(1)}, u32[]{:S(2)}, u32[]{:S(2)}) %collective-permute-start.6) | collective-permute-done | bytes 81952 | tf_op jit(solution)/shard_map/ppermute | solution.py:34
  28.4 1.6 %project.3 = bf16[256,640]{1,0:T(8,128)(2,1)} custom-call(bf16[16,2560]{1,0:T(8,128)(2,1)S(1)} %pad_maximum_fusion.2.refs_0_, bf16[16,2560]{1,0:T(8,128)(2,1)S(1)} %collective-permute-done.5.refs_1_, bf16[16,2560]{1,0:T(8,128)(2,1)S(1)} %collective-permute-done.6.refs_2_, bf16[16,2560]{1,0:T(8,128)(2,1)S(1)} %collective-permute-done.7.refs_3_, ...), custom_call_target="tpu_custom_call" | custom-call | flops 419430400 | bytes 3276800 | tf_op jit(solution)/shard_map/project/pallas_call | solution.py:397
  30.0 4.4 %all-to-all-start = ((bf16[16,16,640]{2,1,0:T(8,128)(2,1)}), bf16[16,16,640]{2,1,0:T(8,128)(2,1)S(1)}, u32[]{:S(2)}, u32[]{:S(2)}) async-start(bf16[16,16,640]{2,1,0:T(8,128)(2,1)} %bitcast.4), calls=%async_computation | async-start | bytes 655360 | tf_op jit(solution)/shard_map/all_to_all | solution.py:667
  35.1 10.4 %all-to-all-done.inbound = bf16[16,16,640]{2,1,0:T(8,128)(2,1)S(1)} async-done(((bf16[16,16,640]{2,1,0:T(8,128)(2,1)}), bf16[16,16,640]{2,1,0:T(8,128)(2,1)S(1)}, u32[]{:S(2)}, u32[]{:S(2)}) %all-to-all-start) | async-done | bytes 327712 | tf_op jit(solution)/shard_map/all_to_all | solution.py:667
  45.5 5.9 %attend.1 = bf16[16,16,512]{2,1,0:T(8,128)(2,1)} custom-call(s32[16,4]{1,0:T(8,128)S(1)} %copy.15.table, s32[2,1,128]{2,1,0:T(1,128)S(1)} %bitcast.14, bf16[16,16,640]{2,1,0:T(8,128)(2,1)S(1)} %all-to-all-done.inbound, f32[16,128]{1,0:T(8,128)S(1)} %get-tuple-element.90.cosine, f32[16,128]{1,0:T(8,128)S(1)} %get-tuple-element.91.sine, ...), custom_call_target="tpu_custom_call" | custom-call | flops 134217728 | bytes 8388608 | tf_op jit(solution)/shard_map/attend/pallas_call | solution.py:584
  51.4 3.5 %all-to-all-start.1 = ((bf16[16,16,512]{2,1,0:T(8,128)(2,1)}), bf16[16,16,512]{2,1,0:T(8,128)(2,1)S(1)}, u32[]{:S(2)}, u32[]{:S(2)}) async-start(bf16[16,16,512]{2,1,0:T(8,128)(2,1)} %attend.1), calls=%async_computation.1 | async-start | bytes 524288 | tf_op jit(solution)/shard_map/all_to_all | solution.py:680
  55.0 1.8 %fetch.3.w_front = bf16[512,2560]{1,0:T(8,128)(2,1)S(1)} custom-call(bf16[512,8192]{1,0:T(8,128)(2,1)} %w_out.1), custom_call_target="tpu_custom_call" | custom-call | bytes 5242880 | tf_op jit(solution)/shard_map/fetch/pallas_call | solution.py:319
  56.7 8.2 %all-to-all-done.1 = bf16[16,16,512]{2,1,0:T(8,128)(2,1)S(1)} async-done(((bf16[16,16,512]{2,1,0:T(8,128)(2,1)}), bf16[16,16,512]{2,1,0:T(8,128)(2,1)S(1)}, u32[]{:S(2)}, u32[]{:S(2)}) %all-to-all-start.1) | async-done | bytes 262176 | tf_op jit(solution)/shard_map/all_to_all | solution.py:680
  65.0 3.2 %product.1 = (bf16[64,5376]{1,0:T(8,128)(2,1)S(1)}, f32[64,5376]{1,0:T(8,128)S(1)}, bf16[64,2816]{1,0:T(8,128)(2,1)S(1)}, f32[64,2816]{1,0:T(8,128)S(1)}) custom-call(s32[1,128]{1,0:T(1,128)S(1)} %get-tuple-element.50.place_a, s32[1,128]{1,0:T(1,128)S(1)} %get-tuple-element.51.place_b, bf16[256,512]{1,0:T(8,128)(2,1)S(1)} %bitcast.13, ...), custom_call_target="tpu_custom_call" | custom-call | flops 1073741824 | bytes 8388608 | tf_op jit(solution)/shard_map/product/pallas_call | solution.py:155
  68.2 2.1 %collective-permute-done.14 = bf16[64,5376]{1,0:T(8,128)(2,1)S(1)} collective-permute-done((bf16[64,5376]{1,0:T(8,128)(2,1)S(1)}, bf16[64,5376]{1,0:T(8,128)(2,1)S(1)}, u32[]{:S(2)}, u32[]{:S(2)}) %collective-permute-start.14) | collective-permute-done | bytes 688160 | tf_op jit(solution)/shard_map/ppermute | solution.py:34
  74.0 2.9 %collective-permute-start.22 = (bf16[16,2816]{1,0:T(8,128)(2,1)S(1)}, bf16[16,2816]{1,0:T(8,128)(2,1)S(1)}, u32[]{:S(2)}, u32[]{:S(2)}) collective-permute-start(bf16[16,2816]{1,0:T(8,128)(2,1)S(1)} %get-tuple-element.82), channel_id=1, source_target_pairs={{0,12},{1,13},{2,14},{3,15},{4,8},{5,9},{6,10},{7,11},{8,4},{9,5},... | collective-permute-start | bytes 270344 | tf_op jit(solution)/shard_map/ppermute | solution.py:34
  76.9 4.2 %collective-permute-done.15 = bf16[32,5376]{1,0:T(8,128)(2,1)S(1)} collective-permute-done((bf16[32,5376]{1,0:T(8,128)(2,1)S(1)}, bf16[32,5376]{1,0:T(8,128)(2,1)S(1)}, u32[]{:S(2)}, u32[]{:S(2)}) %collective-permute-start.15) | collective-permute-done | bytes 344096 | tf_op jit(solution)/shard_map/ppermute | solution.py:34
  83.1 2.6 %collective-permute-start.20 = (bf16[8,5376]{1,0:T(8,128)(2,1)S(1)}, bf16[8,5376]{1,0:T(8,128)(2,1)S(1)}, u32[]{:S(2)}, u32[]{:S(2)}) collective-permute-start(bf16[8,5376]{1,0:T(8,128)(2,1)S(1)} %get-tuple-element.84), channel_id=1, source_target_pairs={{0,12},{1,13},{2,14},{3,15},{4,8},{5,9},{6,10},{7,11},{8,4},{9,5},... | collective-permute-start | bytes 258056 | tf_op jit(solution)/shard_map/ppermute | solution.py:34
  86.1 4.2 %collective-permute-done.18 = bf16[8,5376]{1,0:T(8,128)(2,1)S(1)} collective-permute-done((bf16[8,5376]{1,0:T(8,128)(2,1)S(1)}, bf16[8,5376]{1,0:T(8,128)(2,1)S(1)}, u32[]{:S(2)}, u32[]{:S(2)}) %collective-permute-start.18) | collective-permute-done | bytes 86048 | tf_op jit(solution)/shard_map/ppermute | solution.py:34
  (72 shorter events, 11.6 us)
Async XLA Ops:
  1.7 9.9 %collective-permute-start = (bf16[8,5632]{1,0:T(8,128)(2,1)}, bf16[8,5632]{1,0:T(8,128)(2,1)S(1)}, u32[]{:S(2)}, u32[]{:S(2)}) collective-permute-start(bf16[8,5632]{1,0:T(8,128)(2,1)} %get-tuple-element.41), channel_id=1, source_target_pairs={{0,8},{1,9},{2,10},{3,11},{4,12},{5,13},{6,14},{7,15},{8,0},{9,1},... | collective-permute-start | bytes 270344 | tf_op jit(solution)/shard_map/ppermute | solution.py:34
  5.8 5.8 %collective-permute-start.1 = (bf16[8,5632]{1,0:T(8,128)(2,1)}, bf16[8,5632]{1,0:T(8,128)(2,1)S(1)}, u32[]{:S(2)}, u32[]{:S(2)}) collective-permute-start(bf16[8,5632]{1,0:T(8,128)(2,1)} %get-tuple-element.41), channel_id=1, source_target_pairs={{0,4},{1,5},{2,6},{3,7},{4,0},{5,1},{6,2},{7,3},{8,12},{9,13},{10,... | collective-permute-start | bytes 270344 | tf_op jit(solution)/shard_map/ppermute | solution.py:34
  7.4 6.6 %collective-permute-start.2 = (bf16[8,5632]{1,0:T(8,128)(2,1)}, bf16[8,5632]{1,0:T(8,128)(2,1)S(1)}, u32[]{:S(2)}, u32[]{:S(2)}) collective-permute-start(bf16[8,5632]{1,0:T(8,128)(2,1)} %get-tuple-element.41), channel_id=1, source_target_pairs={{0,12},{1,13},{2,14},{3,15},{4,8},{5,9},{6,10},{7,11},{8,4},{9,5},... | collective-permute-start | bytes 270344 | tf_op jit(solution)/shard_map/ppermute | solution.py:34
  7.4 4.2 %collective-permute-start.3 = (bf16[8,2560]{1,0:T(8,128)(2,1)}, bf16[8,2560]{1,0:T(8,128)(2,1)S(1)}, u32[]{:S(2)}, u32[]{:S(2)}) collective-permute-start(bf16[8,2560]{1,0:T(8,128)(2,1)} %get-tuple-element.42), channel_id=1, source_target_pairs={{0,2},{1,3},{2,0},{3,1},{4,6},{5,7},{6,4},{7,5},{8,10},{9,11},{10,... | collective-permute-start | bytes 122888 | tf_op jit(solution)/shard_map/ppermute | solution.py:34
  14.1 11.3 %collective-permute-start.4 = (bf16[32,5632]{1,0:T(8,128)(2,1)S(1)}, bf16[32,5632]{1,0:T(8,128)(2,1)S(1)}, u32[]{:S(2)}, u32[]{:S(2)}) collective-permute-start(bf16[32,5632]{1,0:T(8,128)(2,1)S(1)} %pad_maximum_fusion.1.refs_0_), channel_id=1, source_target_pairs={{0,2},{1,3},{2,0},{3,1},{4,6},{5,7},{6,4},{7,5},{8,10},{9,11},{10,... | collective-permute-start | bytes 1081352 | tf_op jit(solution)/shard_map/ppermute | solution.py:34
  15.6 8.4 %collective-permute-start.5 = (bf16[16,2560]{1,0:T(8,128)(2,1)S(1)}, bf16[16,2560]{1,0:T(8,128)(2,1)S(1)}, u32[]{:S(2)}, u32[]{:S(2)}) collective-permute-start(bf16[16,2560]{1,0:T(8,128)(2,1)S(1)} %pad_maximum_fusion.2.refs_0_), channel_id=1, source_target_pairs={{0,8},{1,9},{2,10},{3,11},{4,12},{5,13},{6,14},{7,15},{8,0},{9,1},... | collective-permute-start | bytes 245768 | tf_op jit(solution)/shard_map/ppermute | solution.py:34
  18.7 6.7 %collective-permute-start.6 = (bf16[16,2560]{1,0:T(8,128)(2,1)S(1)}, bf16[16,2560]{1,0:T(8,128)(2,1)S(1)}, u32[]{:S(2)}, u32[]{:S(2)}) collective-permute-start(bf16[16,2560]{1,0:T(8,128)(2,1)S(1)} %pad_maximum_fusion.2.refs_0_), channel_id=1, source_target_pairs={{0,4},{1,5},{2,6},{3,7},{4,0},{5,1},{6,2},{7,3},{8,12},{9,13},{10,... | collective-permute-start | bytes 245768 | tf_op jit(solution)/shard_map/ppermute | solution.py:34
  18.7 6.7 %collective-permute-start.7 = (bf16[16,2560]{1,0:T(8,128)(2,1)S(1)}, bf16[16,2560]{1,0:T(8,128)(2,1)S(1)}, u32[]{:S(2)}, u32[]{:S(2)}) collective-permute-start(bf16[16,2560]{1,0:T(8,128)(2,1)S(1)} %pad_maximum_fusion.2.refs_0_), channel_id=1, source_target_pairs={{0,12},{1,13},{2,14},{3,15},{4,8},{5,9},{6,10},{7,11},{8,4},{9,5},... | collective-permute-start | bytes 245768 | tf_op jit(solution)/shard_map/ppermute | solution.py:34
  20.2 6.2 %collective-permute-start.12 = (bf16[32,5632]{1,0:T(8,128)(2,1)S(1)}, bf16[32,5632]{1,0:T(8,128)(2,1)S(1)}, u32[]{:S(2)}, u32[]{:S(2)}) collective-permute-start(bf16[32,5632]{1,0:T(8,128)(2,1)S(1)} %pad_maximum_fusion.1.refs_0_), channel_id=1, source_target_pairs={{0,1},{1,0},{2,3},{3,2},{4,5},{5,4},{6,7},{7,6},{8,9},{9,8},{10,11... | collective-permute-start | bytes 1081352 | tf_op jit(solution)/shard_map/ppermute | solution.py:34
  25.4 3.0 %collective-permute-start.10 = (bf16[16,2560]{1,0:T(8,128)(2,1)S(1)}, bf16[16,2560]{1,0:T(8,128)(2,1)S(1)}, u32[]{:S(2)}, u32[]{:S(2)}) collective-permute-start(bf16[16,2560]{1,0:T(8,128)(2,1)S(1)} %collective-permute-done.6.refs_2_), channel_id=1, source_target_pairs={{0,1},{1,0},{2,3},{3,2},{4,5},{5,4},{6,7},{7,6},{8,9},{9,8},{10,11... | collective-permute-start | bytes 245768 | tf_op jit(solution)/shard_map/ppermute | solution.py:34
  25.9 2.5 %collective-permute-start.11 = (bf16[16,2560]{1,0:T(8,128)(2,1)S(1)}, bf16[16,2560]{1,0:T(8,128)(2,1)S(1)}, u32[]{:S(2)}, u32[]{:S(2)}) collective-permute-start(bf16[16,2560]{1,0:T(8,128)(2,1)S(1)} %collective-permute-done.7.refs_3_), channel_id=1, source_target_pairs={{0,1},{1,0},{2,3},{3,2},{4,5},{5,4},{6,7},{7,6},{8,9},{9,8},{10,11... | collective-permute-start | bytes 245768 | tf_op jit(solution)/shard_map/ppermute | solution.py:34
  26.0 2.4 %collective-permute-start.8 = (bf16[16,2560]{1,0:T(8,128)(2,1)S(1)}, bf16[16,2560]{1,0:T(8,128)(2,1)S(1)}, u32[]{:S(2)}, u32[]{:S(2)}) collective-permute-start(bf16[16,2560]{1,0:T(8,128)(2,1)S(1)} %pad_maximum_fusion.2.refs_0_), channel_id=1, source_target_pairs={{0,1},{1,0},{2,3},{3,2},{4,5},{5,4},{6,7},{7,6},{8,9},{9,8},{10,11... | collective-permute-start | bytes 245768 | tf_op jit(solution)/shard_map/ppermute | solution.py:34
  26.4 2.0 %collective-permute-start.9 = (bf16[16,2560]{1,0:T(8,128)(2,1)S(1)}, bf16[16,2560]{1,0:T(8,128)(2,1)S(1)}, u32[]{:S(2)}, u32[]{:S(2)}) collective-permute-start(bf16[16,2560]{1,0:T(8,128)(2,1)S(1)} %collective-permute-done.5.refs_1_), channel_id=1, source_target_pairs={{0,1},{1,0},{2,3},{3,2},{4,5},{5,4},{6,7},{7,6},{8,9},{9,8},{10,11... | collective-permute-start | bytes 245768 | tf_op jit(solution)/shard_map/ppermute | solution.py:34
  30.0 15.5 %all-to-all-start = ((bf16[16,16,640]{2,1,0:T(8,128)(2,1)}), bf16[16,16,640]{2,1,0:T(8,128)(2,1)S(1)}, u32[]{:S(2)}, u32[]{:S(2)}) async-start(bf16[16,16,640]{2,1,0:T(8,128)(2,1)} %bitcast.4), calls=%async_computation | async-start | bytes 655360 | tf_op jit(solution)/shard_map/all_to_all | solution.py:667
  51.4 13.6 %all-to-all-start.1 = ((bf16[16,16,512]{2,1,0:T(8,128)(2,1)}), bf16[16,16,512]{2,1,0:T(8,128)(2,1)S(1)}, u32[]{:S(2)}, u32[]{:S(2)}) async-start(bf16[16,16,512]{2,1,0:T(8,128)(2,1)} %attend.1), calls=%async_computation.1 | async-start | bytes 524288 | tf_op jit(solution)/shard_map/all_to_all | solution.py:680
  68.2 2.2 %collective-permute-start.14 = (bf16[64,5376]{1,0:T(8,128)(2,1)S(1)}, bf16[64,5376]{1,0:T(8,128)(2,1)S(1)}, u32[]{:S(2)}, u32[]{:S(2)}) collective-permute-start(bf16[64,5376]{1,0:T(8,128)(2,1)S(1)} %get-tuple-element.69), channel_id=1, source_target_pairs={{0,1},{1,0},{2,3},{3,2},{4,5},{5,4},{6,7},{7,6},{8,9},{9,8},{10,11... | collective-permute-start | bytes 2064392 | tf_op jit(solution)/shard_map/ppermute | solution.py:34
  70.8 10.3 %collective-permute-start.15 = (bf16[32,5376]{1,0:T(8,128)(2,1)S(1)}, bf16[32,5376]{1,0:T(8,128)(2,1)S(1)}, u32[]{:S(2)}, u32[]{:S(2)}) collective-permute-start(bf16[32,5376]{1,0:T(8,128)(2,1)S(1)} %slice.87), channel_id=1, source_target_pairs={{0,2},{1,3},{2,0},{3,1},{4,6},{5,7},{6,4},{7,5},{8,10},{9,11},{10,... | collective-permute-start | bytes 1032200 | tf_op jit(solution)/shard_map/ppermute | solution.py:34
  72.4 8.7 %collective-permute-start.17 = (bf16[16,2816]{1,0:T(8,128)(2,1)S(1)}, bf16[16,2816]{1,0:T(8,128)(2,1)S(1)}, u32[]{:S(2)}, u32[]{:S(2)}) collective-permute-start(bf16[16,2816]{1,0:T(8,128)(2,1)S(1)} %get-tuple-element.81), channel_id=1, source_target_pairs={{0,8},{1,9},{2,10},{3,11},{4,12},{5,13},{6,14},{7,15},{8,0},{9,1},... | collective-permute-start | bytes 270344 | tf_op jit(solution)/shard_map/ppermute | solution.py:34
  73.5 12.2 %collective-permute-start.21 = (bf16[16,2816]{1,0:T(8,128)(2,1)S(1)}, bf16[16,2816]{1,0:T(8,128)(2,1)S(1)}, u32[]{:S(2)}, u32[]{:S(2)}) collective-permute-start(bf16[16,2816]{1,0:T(8,128)(2,1)S(1)} %get-tuple-element.83), channel_id=1, source_target_pairs={{0,4},{1,5},{2,6},{3,7},{4,0},{5,1},{6,2},{7,3},{8,12},{9,13},{10,... | collective-permute-start | bytes 270344 | tf_op jit(solution)/shard_map/ppermute | solution.py:34
  74.0 11.7 %collective-permute-start.22 = (bf16[16,2816]{1,0:T(8,128)(2,1)S(1)}, bf16[16,2816]{1,0:T(8,128)(2,1)S(1)}, u32[]{:S(2)}, u32[]{:S(2)}) collective-permute-start(bf16[16,2816]{1,0:T(8,128)(2,1)S(1)} %get-tuple-element.82), channel_id=1, source_target_pairs={{0,12},{1,13},{2,14},{3,15},{4,8},{5,9},{6,10},{7,11},{8,4},{9,5},... | collective-permute-start | bytes 270344 | tf_op jit(solution)/shard_map/ppermute | solution.py:34
  81.2 9.0 %collective-permute-start.18 = (bf16[8,5376]{1,0:T(8,128)(2,1)S(1)}, bf16[8,5376]{1,0:T(8,128)(2,1)S(1)}, u32[]{:S(2)}, u32[]{:S(2)}) collective-permute-start(bf16[8,5376]{1,0:T(8,128)(2,1)S(1)} %get-tuple-element.86), channel_id=1, source_target_pairs={{0,8},{1,9},{2,10},{3,11},{4,12},{5,13},{6,14},{7,15},{8,0},{9,1},... | collective-permute-start | bytes 258056 | tf_op jit(solution)/shard_map/ppermute | solution.py:34
  82.3 8.0 %collective-permute-start.19 = (bf16[8,5376]{1,0:T(8,128)(2,1)S(1)}, bf16[8,5376]{1,0:T(8,128)(2,1)S(1)}, u32[]{:S(2)}, u32[]{:S(2)}) collective-permute-start(bf16[8,5376]{1,0:T(8,128)(2,1)S(1)} %get-tuple-element.85), channel_id=1, source_target_pairs={{0,4},{1,5},{2,6},{3,7},{4,0},{5,1},{6,2},{7,3},{8,12},{9,13},{10,... | collective-permute-start | bytes 258056 | tf_op jit(solution)/shard_map/ppermute | solution.py:34
  83.1 7.2 %collective-permute-start.20 = (bf16[8,5376]{1,0:T(8,128)(2,1)S(1)}, bf16[8,5376]{1,0:T(8,128)(2,1)S(1)}, u32[]{:S(2)}, u32[]{:S(2)}) collective-permute-start(bf16[8,5376]{1,0:T(8,128)(2,1)S(1)} %get-tuple-element.84), channel_id=1, source_target_pairs={{0,12},{1,13},{2,14},{3,15},{4,8},{5,9},{6,10},{7,11},{8,4},{9,5},... | collective-permute-start | bytes 258056 | tf_op jit(solution)/shard_map/ppermute | solution.py:34
  85.8 4.6 %collective-permute-start.23 = (bf16[8,2816]{1,0:T(8,128)(2,1)S(1)}, bf16[8,2816]{1,0:T(8,128)(2,1)S(1)}, u32[]{:S(2)}, u32[]{:S(2)}) collective-permute-start(bf16[8,2816]{1,0:T(8,128)(2,1)S(1)} %slice.88), channel_id=1, source_target_pairs={{0,2},{1,3},{2,0},{3,1},{4,6},{5,7},{6,4},{7,5},{8,10},{9,11},{10,... | collective-permute-start | bytes 135176 | tf_op jit(solution)/shard_map/ppermute | solution.py:34
  (8 other events, 43.0 us)

commit v19 on v17

--- a/solution.py
+++ b/solution.py
@@ -249,14 +249,19 @@
     def upright(x):
         return jnp.sum(jnp.where(row == column, x, 0.0), axis=1, keepdims=True)
 
+    tp = lax.axis_index("tp")
+    me = (lax.div(tp, 4), lax.rem(lax.div(tp, 2), 2), lax.rem(tp, 2), lax.axis_index("attn"))
+    cores = sizes[CORE]
+    chip = lax.div(kv_owner[...], cores)
+    core = lax.rem(lax.rem(kv_owner[...], cores) + cores - me[CORE], cores)
+
     owner = kv_owner[...].astype(jnp.float32)
     earlier = (upright(owner) == owner) & (row < column)
     slot = jnp.sum(jnp.where(earlier, 1.0, 0.0), axis=0, keepdims=True)
-    place = owner * slots + slot
-    upright_place = upright(place)
-
-    tp = lax.axis_index("tp")
-    me = (lax.div(tp, 4), lax.rem(lax.div(tp, 2), 2), lax.rem(tp, 2), lax.axis_index("attn"))
+    place = (chip * cores + core).astype(jnp.float32) * slots + slot
+    chips = int(np.prod(sizes)) // cores
+    by_core = (core * chips + chip).astype(jnp.float32) * slots + slot
+    upright_place, upright_by_core = upright(place), upright(by_core)
     rows_dev = requests // int(np.prod(sizes))
     lane = lax.broadcasted_iota(jnp.int32, (1, requests), 1)
     for order, out in zip(orders, outs):
@@ -264,7 +269,7 @@
             out[...] = place.astype(jnp.int32)
             continue
         if not order:
-            out[...] = (tp * sizes[CORE] + me[CORE]) * slots + lane
+            out[...] = tp * cores * slots + lane
             continue
         sign, axes = order
         rest = lax.div(lane, rows_dev)
@@ -277,7 +282,8 @@
         for axis in range(1, len(sizes)):
             block = block * sizes[axis] + where[axis]
         source = block * rows_dev + lax.rem(lane, rows_dev)
-        moved = jnp.sum(jnp.where(row == source, upright_place, 0.0), axis=0, keepdims=True)
+        wanted = upright_by_core if sign < 0 else upright_place
+        moved = jnp.sum(jnp.where(row == source, wanted, 0.0), axis=0, keepdims=True)
         out[...] = moved.astype(jnp.int32)
 
 
@@ -331,13 +337,14 @@
 
 
 def project_kernel(first, last, order, start, block, *refs):
-    count = len(refs) - 4 - (not first) - last
+    count = len(refs) - 4 - (not first) - 2 * last
     parts, (wq, w_kv), refs = refs[:count], refs[count : count + 2], refs[count + 2 :]
     if not first:
         before, refs = refs[0], refs[1:]
     if last:
         place, refs = refs[0], refs[1:]
-    out, total = refs
+    outs, total = refs[:-1], refs[-1]
+    out = outs[0]
     step = pl.program_id(0)
     per_query = wq.shape[1]
 
@@ -363,11 +370,13 @@
     def _():
         if last:
             rows = lax.broadcasted_iota(jnp.int32, (out.shape[0], place.shape[1]), 0)
-            route = jnp.where(rows == place[...], 1.0, 0.0).astype(jnp.bfloat16)
-            moved = jnp.dot(
-                route, total[...].astype(jnp.bfloat16), preferred_element_type=jnp.float32
-            )
-            out[...] = moved.astype(jnp.bfloat16)
+            for i, part in enumerate(outs):
+                here = rows + i * out.shape[0] == place[...]
+                route = jnp.where(here, 1.0, 0.0).astype(jnp.bfloat16)
+                moved = jnp.dot(
+                    route, total[...].astype(jnp.bfloat16), preferred_element_type=jnp.float32
+                )
+                part[...] = moved.astype(jnp.bfloat16)
         else:
             out[...] = total[...]
 
@@ -391,14 +400,14 @@
     if last:
         args.append(place)
         specs.append(vmem)
-        out = jax.ShapeDtypeStruct((slots, row_width), jnp.bfloat16)
+        out = [jax.ShapeDtypeStruct((slots // 2, row_width), jnp.bfloat16)] * 2
     else:
-        out = jax.ShapeDtypeStruct((rows, row_width), jnp.float32)
+        out = [jax.ShapeDtypeStruct((rows, row_width), jnp.float32)]
     return pl.pallas_call(
         functools.partial(project_kernel, first, last, order, start, block),
         grid=(width // block,),
         in_specs=specs,
-        out_specs=vmem,
+        out_specs=[vmem] * len(out),
         out_shape=out,
         scratch_shapes=[pltpu.VMEM((rows, row_width), jnp.float32)],
         compiler_params=pltpu.CompilerParams(vmem_limit_bytes=24 * 2**20),
@@ -421,7 +430,8 @@
     sine,
     key_pages,
     value_pages,
-    out,
+    out_own,
+    out_other,
     key_pool,
     value_pool,
     sems,
@@ -474,6 +484,14 @@
                 query_rot[head // pair, b, rows] = x[b * batch : (b + 1) * batch]
 
     piece = lax.broadcasted_iota(jnp.int32, (slots, HEAD), 1) // per_key
+    straight = jnp.broadcast_to(lax.axis_index("attn") == 0, (slots, HEAD))
+
+    def by_core(x):
+        other = jnp.where(
+            piece % 2 == 0, pltpu.roll(x, HEAD - per_key, 1), pltpu.roll(x, per_key, 1)
+        )
+        return jnp.where(straight, x, other)
+
     for g in range(kv_heads):
         key = jnp.zeros((slots, HEAD), jnp.float32)
         value = jnp.zeros((slots, HEAD), jnp.float32)
@@ -483,8 +501,8 @@
             back = (shift - per_key) % HEAD
             key = jnp.where(piece == j, pltpu.roll(tile, shift, 1) if shift else tile, key)
             value = jnp.where(piece == j, pltpu.roll(tile, back, 1) if back else tile, value)
-        key_new[:, g * HEAD : (g + 1) * HEAD] = turn(key)
-        value_own[g] = value
+        key_new[:, g * HEAD : (g + 1) * HEAD] = turn(by_core(key))
+        value_own[g] = by_core(value)
 
     scale = HEAD ** (-0.5)
     columns = pair * batch
@@ -554,7 +572,9 @@
                 own_value = value_own[g, b * batch : (b + 1) * batch]
                 halves.append(mixed[p, b, rows] + own_chances[p, b][rows] * own_value)
             column = head % heads_dev * HEAD
-            out[head // heads_dev, :, column : column + HEAD] = jnp.concatenate(
+            target = head // heads_dev
+            out = out_other if target % 2 else out_own
+            out[target // 2, :, column : column + HEAD] = jnp.concatenate(
                 halves, axis=0
             ).astype(jnp.bfloat16)
 
@@ -578,8 +598,8 @@
     return pl.pallas_call(
         functools.partial(attend_kernel, per_query, per_key),
         in_specs=[smem, vmem, vmem, vmem, vmem, hbm, hbm],
-        out_specs=vmem,
-        out_shape=jax.ShapeDtypeStruct((owners, slots, per_query), jnp.bfloat16),
+        out_specs=[vmem, vmem],
+        out_shape=[jax.ShapeDtypeStruct((owners // 2, slots, per_query), jnp.bfloat16)] * 2,
         scratch_shapes=[
             pltpu.VMEM(key_pages.shape, jnp.bfloat16),
             pltpu.VMEM(value_pages.shape, jnp.bfloat16),
@@ -644,9 +664,18 @@
     parts_a, parts_b, others, w_query = gather_rows(grid, xa, xb, first, second)
     (place, place_in, place_a, place_b, mine), w_kv_t = others
     plain = list(range(owners))
-    total = project(0, parts_a, plain, w_query, w_kv_t, None, None, all_slots)
-    total = project(cut, parts_b, order_b, w_query, w_kv_t, total, place_in, all_slots)
-    outbound = total.reshape(owners, slot_count, row_width)
+    (total,) = project(0, parts_a, plain, w_query, w_kv_t, None, None, all_slots)
+    outbound, other = project(
+        cut, parts_b, order_b, w_query, w_kv_t, total, place_in, all_slots
+    )
+    chips = owners // 2
+
+    def exchange(own, other):
+        other = grid.send(other, core=1)
+        both = [x.reshape(chips, slot_count, x.shape[-1]) for x in (own, other)]
+        both = jnp.concatenate(both, axis=1)
+        return lax.all_to_all(both, "tp", split_axis=0, concat_axis=0, tiled=True), both
+
     place = after(place, outbound).reshape(requests)
     mine = mine[0, :slot_count]
     lengths = jnp.sum(jnp.where(place[:, None] == mine[None, :], cached[:, None], 0), axis=0)
@@ -658,8 +687,9 @@
     sine_part = jnp.sin(angles)
     cosine = jnp.concatenate([cosine_part, cosine_part], axis=1)
     sine = jnp.concatenate([-sine_part, sine_part], axis=1)
-    inbound = lax.all_to_all(outbound, AXES, split_axis=0, concat_axis=0, tiled=True)
-    attended = attend(
+    inbound, _ = exchange(outbound, other)
+    inbound = inbound.reshape(owners, slot_count, row_width)
+    attended, other = attend(
         inbound,
         lengths,
         after(page_table, outbound)[0],
@@ -670,8 +700,8 @@
         per_query,
         per_key,
     )
-    (w_front,) = fetch((after(w_out, attended), (0, width // 32 * 10)), limit=48)
-    returned = lax.all_to_all(attended, AXES, split_axis=0, concat_axis=0, tiled=True)
+    returned, sent = exchange(attended, other)
+    (w_front,) = fetch((after(w_out, sent), (0, width // 32 * 10)), limit=48)
     returned = returned.reshape(all_slots, per_query)
     summed = scatter_sum(grid, place_a, place_b, returned, w_out, w_front, width // 32 * 21)
     return narrow(wide(hidden_in) + summed)

time: 91.5 us -> 93.9 us (1.026)
  Pallas kernels: 19 us -> 17.6 us
  local copies, waits for them, and re-layouts: 0.38 us -> 1.69 us
  starting transfers between devices: 32.5 us -> 33.6 us
    ppermute x24 -> x26, waiting for transfers between devices: 16.9 us -> 18.9 us  [send(): return lax.ppermute(x, AXES, pairs)]
    all_to_all x2, waiting for transfers between devices: 18.7 us -> 17.4 us  [exchange(): lax.all_to_all(both, 'tp', split_axis=0, concat_axis=0, tiled=True)]
    ppermute x24 -> x26, starting transfers between devices: 24.6 us -> 25.6 us  [send(): return lax.ppermute(x, AXES, pairs)]
  transfers between devices with their start and end apart: 26 -> 28, of which waited for: 11 -> 16; matrix products, arithmetic and copies ran while one was open for 3% -> 4% of each run, Pallas kernels for 7% -> 7%
where the time goes in v19:
time: 93.9 us; the launch traced here: 93.5 us
  waiting for transfers between devices  36.3 us (39%)
  starting transfers between devices  33.6 us (36%)
  Pallas kernels  17.6 us (19%)
  other arithmetic  4.04 us (4%)
  local copies, waits for them, and re-layouts  1.69 us (2%)
    ppermute x26, starting transfers between devices, send(): return lax.ppermute(x, AXES, pairs)  25.6 us
    ppermute x26, waiting for transfers between devices, send(): return lax.ppermute(x, AXES, pairs)  18.9 us
    all_to_all x2, waiting for transfers between devices, exchange(): lax.all_to_all(both, 'tp', split_axis=0, concat_axis=0, tiled=True)  17.4 us
    all_to_all x2, starting transfers between devices, exchange(): lax.all_to_all(both, 'tp', split_axis=0, concat_axis=0, tiled=True)  7.94 us
    pallas_call x1, Pallas kernels, attend(): pl.pallas_call(functools.partial(attend_kernel, per_query, per_key), in_s...  5.17 us
    pallas_call x2, Pallas kernels, fetch(): pl.pallas_call(functools.partial(fetch_kernel, starts), in_specs=[pl.Bloc...  5.14 us
    pallas_call x1, Pallas kernels, product(): pl.pallas_call(functools.partial(product_kernel, tuple(cuts)), in_specs=[...  3.18 us
    pallas_call x2, Pallas kernels, project(): pl.pallas_call(functools.partial(project_kernel, first, last, order, star...  2.16 us
  transfers between devices with their start and end apart: 28, of which 16 were waited for; matrix products, arithmetic and copies ran while one was open for 4% of the time, Pallas kernels for 7%

profile of v19, /device:TPU:0, one launch (start us, length us, event | category | flops | bytes accessed | tf_op | source)
XLA Modules:
  0.0 93.5 jit_solution(10029081535469237713)
XLA Ops:
  0.0 1.7 %norm.1 = (bf16[8,5632]{1,0:T(8,128)(2,1)}, bf16[8,2560]{1,0:T(8,128)(2,1)}) custom-call(bf16[8,8192]{1,0:T(8,128)(2,1)} %x.1, f32[1,8192]{1,0:T(1,128)} %bitcast.26), custom_call_target="tpu_custom_call" | custom-call | tf_op jit(solution)/shard_map/norm/pallas_call | solution.py:229
  1.7 4.1 %collective-permute-start = (bf16[8,5632]{1,0:T(8,128)(2,1)}, bf16[8,5632]{1,0:T(8,128)(2,1)S(1)}, u32[]{:S(2)}, u32[]{:S(2)}) collective-permute-start(bf16[8,5632]{1,0:T(8,128)(2,1)} %get-tuple-element.45), channel_id=1, source_target_pairs={{0,8},{1,9},{2,10},{3,11},{4,12},{5,13},{6,14},{7,15},{8,0},{9,1},... | collective-permute-start | bytes 270344 | tf_op jit(solution)/shard_map/ppermute | solution.py:34
  5.8 1.6 %collective-permute-start.1 = (bf16[8,5632]{1,0:T(8,128)(2,1)}, bf16[8,5632]{1,0:T(8,128)(2,1)S(1)}, u32[]{:S(2)}, u32[]{:S(2)}) collective-permute-start(bf16[8,5632]{1,0:T(8,128)(2,1)} %get-tuple-element.45), channel_id=1, source_target_pairs={{0,4},{1,5},{2,6},{3,7},{4,0},{5,1},{6,2},{7,3},{8,12},{9,13},{10,... | collective-permute-start | bytes 270344 | tf_op jit(solution)/shard_map/ppermute | solution.py:34
  7.4 1.7 %collective-permute-start.3 = (bf16[8,2560]{1,0:T(8,128)(2,1)}, bf16[8,2560]{1,0:T(8,128)(2,1)S(1)}, u32[]{:S(2)}, u32[]{:S(2)}) collective-permute-start(bf16[8,2560]{1,0:T(8,128)(2,1)} %get-tuple-element.46), channel_id=1, source_target_pairs={{0,2},{1,3},{2,0},{3,1},{4,6},{5,7},{6,4},{7,5},{8,10},{9,11},{10,... | collective-permute-start | bytes 122888 | tf_op jit(solution)/shard_map/ppermute | solution.py:34
  9.2 1.8 %pad_maximum_fusion.refs_5_.refs_9_ = bf16[128,8192]{1,0:T(8,128)(2,1)S(1)} fusion(bf16[64,8192]{1,0:T(8,128)(2,1)} %bitcast.23, bf16[64,8192]{1,0:T(8,128)(2,1)} %bitcast.24), kind=kLoop, calls=%fused_computation | loop fusion | flops 4194304 | bytes 4194304 | tf_op jit(solution)/shard_map/concatenate | solution.py:659
  11.7 2.3 %collective-permute-done.2 = bf16[8,5632]{1,0:T(8,128)(2,1)S(1)} collective-permute-done((bf16[8,5632]{1,0:T(8,128)(2,1)}, bf16[8,5632]{1,0:T(8,128)(2,1)S(1)}, u32[]{:S(2)}, u32[]{:S(2)}) %collective-permute-start.2) | collective-permute-done | bytes 90144 | tf_op jit(solution)/shard_map/ppermute | solution.py:34
  14.0 1.6 %collective-permute-start.4 = (bf16[32,5632]{1,0:T(8,128)(2,1)S(1)}, bf16[32,5632]{1,0:T(8,128)(2,1)S(1)}, u32[]{:S(2)}, u32[]{:S(2)}) collective-permute-start(bf16[32,5632]{1,0:T(8,128)(2,1)S(1)} %pad_maximum_fusion.1.refs_0_), channel_id=1, source_target_pairs={{0,2},{1,3},{2,0},{3,1},{4,6},{5,7},{6,4},{7,5},{8,10},{9,11},{10,... | collective-permute-start | bytes 1081352 | tf_op jit(solution)/shard_map/ppermute | solution.py:34
  15.6 3.1 %collective-permute-start.5 = (bf16[16,2560]{1,0:T(8,128)(2,1)S(1)}, bf16[16,2560]{1,0:T(8,128)(2,1)S(1)}, u32[]{:S(2)}, u32[]{:S(2)}) collective-permute-start(bf16[16,2560]{1,0:T(8,128)(2,1)S(1)} %pad_maximum_fusion.3.refs_0_), channel_id=1, source_target_pairs={{0,8},{1,9},{2,10},{3,11},{4,12},{5,13},{6,14},{7,15},{8,0},{9,1},... | collective-permute-start | bytes 245768 | tf_op jit(solution)/shard_map/ppermute | solution.py:34
  18.7 1.5 %collective-permute-start.7 = (bf16[16,2560]{1,0:T(8,128)(2,1)S(1)}, bf16[16,2560]{1,0:T(8,128)(2,1)S(1)}, u32[]{:S(2)}, u32[]{:S(2)}) collective-permute-start(bf16[16,2560]{1,0:T(8,128)(2,1)S(1)} %pad_maximum_fusion.3.refs_0_), channel_id=1, source_target_pairs={{0,12},{1,13},{2,14},{3,15},{4,8},{5,9},{6,10},{7,11},{8,4},{9,5},... | collective-permute-start | bytes 245768 | tf_op jit(solution)/shard_map/ppermute | solution.py:34
  20.2 3.4 %fetch.2.refs_4_.refs_8_ = bf16[8192,512]{1,0:T(8,128)(2,1)S(1)} custom-call(bf16[8192,512]{1,0:T(8,128)(2,1)} %refs_0_), custom_call_target="tpu_custom_call" | custom-call | bytes 16777216 | tf_op jit(solution)/shard_map/fetch/pallas_call | solution.py:325
  31.5 4.3 %all-to-all-start = ((bf16[8,32,640]{2,1,0:T(8,128)(2,1)}), bf16[8,32,640]{2,1,0:T(8,128)(2,1)S(1)}, u32[]{:S(2)}, u32[]{:S(2)}) async-start(bf16[8,32,640]{2,1,0:T(8,128)(2,1)} %pad_maximum_fusion.2), calls=%async_computation | async-start | bytes 655360 | tf_op jit(solution)/shard_map/all_to_all | solution.py:677
  36.5 9.9 %all-to-all-done = bf16[8,32,640]{2,1,0:T(8,128)(2,1)S(1)} async-done(((bf16[8,32,640]{2,1,0:T(8,128)(2,1)}), bf16[8,32,640]{2,1,0:T(8,128)(2,1)S(1)}, u32[]{:S(2)}, u32[]{:S(2)}) %all-to-all-start) | async-done | bytes 327712 | tf_op jit(solution)/shard_map/all_to_all | solution.py:677
  46.4 5.2 %attend.1 = (bf16[8,16,512]{2,1,0:T(8,128)(2,1)S(1)}, bf16[8,16,512]{2,1,0:T(8,128)(2,1)S(1)}) custom-call(s32[16,4]{1,0:T(8,128)S(1)} %copy.15.table, s32[2,1,128]{2,1,0:T(1,128)S(1)} %bitcast.18, bf16[16,16,640]{2,1,0:T(8,128)(2,1)S(1)} %bitcast.15, f32[16,128]{1,0:T(8,128)S(1)} %get-tuple-element.98.cosine, f32[16,128]{1,0:T(8,128)S(1)} %get-tuple-element.99.sine, ...), custom_call_target="tpu_custom_call" | custom-call | flops 134217728 | bytes 8388608 | tf_op jit(solution)/shard_map/attend/pallas_call | solution.py:598
  53.7 3.6 %all-to-all-start.1 = ((bf16[8,32,512]{2,1,0:T(8,128)(2,1)}), bf16[8,32,512]{2,1,0:T(8,128)(2,1)S(1)}, u32[]{:S(2)}, u32[]{:S(2)}) async-start(bf16[8,32,512]{2,1,0:T(8,128)(2,1)} %constant_dynamic-update-slice_fusion), calls=%async_computation.1 | async-start | bytes 524288 | tf_op jit(solution)/shard_map/all_to_all | solution.py:677
  57.3 1.7 %fetch.3.w_front = bf16[512,2560]{1,0:T(8,128)(2,1)S(1)} custom-call(bf16[512,8192]{1,0:T(8,128)(2,1)} %w_out.1), custom_call_target="tpu_custom_call" | custom-call | bytes 5242880 | tf_op jit(solution)/shard_map/fetch/pallas_call | solution.py:325
  59.1 7.5 %all-to-all-done.1 = bf16[8,32,512]{2,1,0:T(8,128)(2,1)S(1)} async-done(((bf16[8,32,512]{2,1,0:T(8,128)(2,1)}), bf16[8,32,512]{2,1,0:T(8,128)(2,1)S(1)}, u32[]{:S(2)}, u32[]{:S(2)}) %all-to-all-start.1) | async-done | bytes 262176 | tf_op jit(solution)/shard_map/all_to_all | solution.py:677
  66.5 3.2 %product.1 = (bf16[64,5376]{1,0:T(8,128)(2,1)S(1)}, f32[64,5376]{1,0:T(8,128)S(1)}, bf16[64,2816]{1,0:T(8,128)(2,1)S(1)}, f32[64,2816]{1,0:T(8,128)S(1)}) custom-call(s32[1,128]{1,0:T(1,128)S(1)} %get-tuple-element.54.place_a, s32[1,128]{1,0:T(1,128)S(1)} %get-tuple-element.55.place_b, bf16[256,512]{1,0:T(8,128)(2,1)S(1)} %bitcast.16, ...), custom_call_target="tpu_custom_call" | custom-call | flops 1073741824 | bytes 8388608 | tf_op jit(solution)/shard_map/product/pallas_call | solution.py:155
  69.8 2.1 %collective-permute-done.16 = bf16[64,5376]{1,0:T(8,128)(2,1)S(1)} collective-permute-done((bf16[64,5376]{1,0:T(8,128)(2,1)S(1)}, bf16[64,5376]{1,0:T(8,128)(2,1)S(1)}, u32[]{:S(2)}, u32[]{:S(2)}) %collective-permute-start.16) | collective-permute-done | bytes 688160 | tf_op jit(solution)/shard_map/ppermute | solution.py:34
  72.3 1.4 %collective-permute-start.17 = (bf16[32,5376]{1,0:T(8,128)(2,1)S(1)}, bf16[32,5376]{1,0:T(8,128)(2,1)S(1)}, u32[]{:S(2)}, u32[]{:S(2)}) collective-permute-start(bf16[32,5376]{1,0:T(8,128)(2,1)S(1)} %slice.87), channel_id=1, source_target_pairs={{0,2},{1,3},{2,0},{3,1},{4,6},{5,7},{6,4},{7,5},{8,10},{9,11},{10,... | collective-permute-start | bytes 1032200 | tf_op jit(solution)/shard_map/ppermute | solution.py:34
  76.0 2.5 %collective-permute-start.24 = (bf16[16,2816]{1,0:T(8,128)(2,1)S(1)}, bf16[16,2816]{1,0:T(8,128)(2,1)S(1)}, u32[]{:S(2)}, u32[]{:S(2)}) collective-permute-start(bf16[16,2816]{1,0:T(8,128)(2,1)S(1)} %get-tuple-element.90), channel_id=1, source_target_pairs={{0,12},{1,13},{2,14},{3,15},{4,8},{5,9},{6,10},{7,11},{8,4},{9,5},... | collective-permute-start | bytes 270344 | tf_op jit(solution)/shard_map/ppermute | solution.py:34
  78.4 4.2 %collective-permute-done.17 = bf16[32,5376]{1,0:T(8,128)(2,1)S(1)} collective-permute-done((bf16[32,5376]{1,0:T(8,128)(2,1)S(1)}, bf16[32,5376]{1,0:T(8,128)(2,1)S(1)}, u32[]{:S(2)}, u32[]{:S(2)}) %collective-permute-start.17) | collective-permute-done | bytes 344096 | tf_op jit(solution)/shard_map/ppermute | solution.py:34
  84.2 2.0 %collective-permute-start.21 = (bf16[8,5376]{1,0:T(8,128)(2,1)S(1)}, bf16[8,5376]{1,0:T(8,128)(2,1)S(1)}, u32[]{:S(2)}, u32[]{:S(2)}) collective-permute-start(bf16[8,5376]{1,0:T(8,128)(2,1)S(1)} %get-tuple-element.93), channel_id=1, source_target_pairs={{0,4},{1,5},{2,6},{3,7},{4,0},{5,1},{6,2},{7,3},{8,12},{9,13},{10,... | collective-permute-start | bytes 258056 | tf_op jit(solution)/shard_map/ppermute | solution.py:34
  86.3 2.4 %collective-permute-start.22 = (bf16[8,5376]{1,0:T(8,128)(2,1)S(1)}, bf16[8,5376]{1,0:T(8,128)(2,1)S(1)}, u32[]{:S(2)}, u32[]{:S(2)}) collective-permute-start(bf16[8,5376]{1,0:T(8,128)(2,1)S(1)} %get-tuple-element.92), channel_id=1, source_target_pairs={{0,12},{1,13},{2,14},{3,15},{4,8},{5,9},{6,10},{7,11},{8,4},{9,5},... | collective-permute-start | bytes 258056 | tf_op jit(solution)/shard_map/ppermute | solution.py:34
  88.8 2.6 %collective-permute-done.20 = bf16[8,5376]{1,0:T(8,128)(2,1)S(1)} collective-permute-done((bf16[8,5376]{1,0:T(8,128)(2,1)S(1)}, bf16[8,5376]{1,0:T(8,128)(2,1)S(1)}, u32[]{:S(2)}, u32[]{:S(2)}) %collective-permute-start.20) | collective-permute-done | bytes 86048 | tf_op jit(solution)/shard_map/ppermute | solution.py:34
  (79 shorter events, 17.8 us)
Async XLA Ops:
  1.7 9.9 %collective-permute-start = (bf16[8,5632]{1,0:T(8,128)(2,1)}, bf16[8,5632]{1,0:T(8,128)(2,1)S(1)}, u32[]{:S(2)}, u32[]{:S(2)}) collective-permute-start(bf16[8,5632]{1,0:T(8,128)(2,1)} %get-tuple-element.45), channel_id=1, source_target_pairs={{0,8},{1,9},{2,10},{3,11},{4,12},{5,13},{6,14},{7,15},{8,0},{9,1},... | collective-permute-start | bytes 270344 | tf_op jit(solution)/shard_map/ppermute | solution.py:34
  5.8 5.8 %collective-permute-start.1 = (bf16[8,5632]{1,0:T(8,128)(2,1)}, bf16[8,5632]{1,0:T(8,128)(2,1)S(1)}, u32[]{:S(2)}, u32[]{:S(2)}) collective-permute-start(bf16[8,5632]{1,0:T(8,128)(2,1)} %get-tuple-element.45), channel_id=1, source_target_pairs={{0,4},{1,5},{2,6},{3,7},{4,0},{5,1},{6,2},{7,3},{8,12},{9,13},{10,... | collective-permute-start | bytes 270344 | tf_op jit(solution)/shard_map/ppermute | solution.py:34
  7.4 6.6 %collective-permute-start.2 = (bf16[8,5632]{1,0:T(8,128)(2,1)}, bf16[8,5632]{1,0:T(8,128)(2,1)S(1)}, u32[]{:S(2)}, u32[]{:S(2)}) collective-permute-start(bf16[8,5632]{1,0:T(8,128)(2,1)} %get-tuple-element.45), channel_id=1, source_target_pairs={{0,12},{1,13},{2,14},{3,15},{4,8},{5,9},{6,10},{7,11},{8,4},{9,5},... | collective-permute-start | bytes 270344 | tf_op jit(solution)/shard_map/ppermute | solution.py:34
  7.4 4.2 %collective-permute-start.3 = (bf16[8,2560]{1,0:T(8,128)(2,1)}, bf16[8,2560]{1,0:T(8,128)(2,1)S(1)}, u32[]{:S(2)}, u32[]{:S(2)}) collective-permute-start(bf16[8,2560]{1,0:T(8,128)(2,1)} %get-tuple-element.46), channel_id=1, source_target_pairs={{0,2},{1,3},{2,0},{3,1},{4,6},{5,7},{6,4},{7,5},{8,10},{9,11},{10,... | collective-permute-start | bytes 122888 | tf_op jit(solution)/shard_map/ppermute | solution.py:34
  14.0 11.3 %collective-permute-start.4 = (bf16[32,5632]{1,0:T(8,128)(2,1)S(1)}, bf16[32,5632]{1,0:T(8,128)(2,1)S(1)}, u32[]{:S(2)}, u32[]{:S(2)}) collective-permute-start(bf16[32,5632]{1,0:T(8,128)(2,1)S(1)} %pad_maximum_fusion.1.refs_0_), channel_id=1, source_target_pairs={{0,2},{1,3},{2,0},{3,1},{4,6},{5,7},{6,4},{7,5},{8,10},{9,11},{10,... | collective-permute-start | bytes 1081352 | tf_op jit(solution)/shard_map/ppermute | solution.py:34
  15.6 8.4 %collective-permute-start.5 = (bf16[16,2560]{1,0:T(8,128)(2,1)S(1)}, bf16[16,2560]{1,0:T(8,128)(2,1)S(1)}, u32[]{:S(2)}, u32[]{:S(2)}) collective-permute-start(bf16[16,2560]{1,0:T(8,128)(2,1)S(1)} %pad_maximum_fusion.3.refs_0_), channel_id=1, source_target_pairs={{0,8},{1,9},{2,10},{3,11},{4,12},{5,13},{6,14},{7,15},{8,0},{9,1},... | collective-permute-start | bytes 245768 | tf_op jit(solution)/shard_map/ppermute | solution.py:34
  18.7 6.7 %collective-permute-start.6 = (bf16[16,2560]{1,0:T(8,128)(2,1)S(1)}, bf16[16,2560]{1,0:T(8,128)(2,1)S(1)}, u32[]{:S(2)}, u32[]{:S(2)}) collective-permute-start(bf16[16,2560]{1,0:T(8,128)(2,1)S(1)} %pad_maximum_fusion.3.refs_0_), channel_id=1, source_target_pairs={{0,4},{1,5},{2,6},{3,7},{4,0},{5,1},{6,2},{7,3},{8,12},{9,13},{10,... | collective-permute-start | bytes 245768 | tf_op jit(solution)/shard_map/ppermute | solution.py:34
  18.7 6.7 %collective-permute-start.7 = (bf16[16,2560]{1,0:T(8,128)(2,1)S(1)}, bf16[16,2560]{1,0:T(8,128)(2,1)S(1)}, u32[]{:S(2)}, u32[]{:S(2)}) collective-permute-start(bf16[16,2560]{1,0:T(8,128)(2,1)S(1)} %pad_maximum_fusion.3.refs_0_), channel_id=1, source_target_pairs={{0,12},{1,13},{2,14},{3,15},{4,8},{5,9},{6,10},{7,11},{8,4},{9,5},... | collective-permute-start | bytes 245768 | tf_op jit(solution)/shard_map/ppermute | solution.py:34
  20.2 6.2 %collective-permute-start.12 = (bf16[32,5632]{1,0:T(8,128)(2,1)S(1)}, bf16[32,5632]{1,0:T(8,128)(2,1)S(1)}, u32[]{:S(2)}, u32[]{:S(2)}) collective-permute-start(bf16[32,5632]{1,0:T(8,128)(2,1)S(1)} %pad_maximum_fusion.1.refs_0_), channel_id=1, source_target_pairs={{0,1},{1,0},{2,3},{3,2},{4,5},{5,4},{6,7},{7,6},{8,9},{9,8},{10,11... | collective-permute-start | bytes 1081352 | tf_op jit(solution)/shard_map/ppermute | solution.py:34
  25.4 3.0 %collective-permute-start.10 = (bf16[16,2560]{1,0:T(8,128)(2,1)S(1)}, bf16[16,2560]{1,0:T(8,128)(2,1)S(1)}, u32[]{:S(2)}, u32[]{:S(2)}) collective-permute-start(bf16[16,2560]{1,0:T(8,128)(2,1)S(1)} %collective-permute-done.6.refs_2_), channel_id=1, source_target_pairs={{0,1},{1,0},{2,3},{3,2},{4,5},{5,4},{6,7},{7,6},{8,9},{9,8},{10,11... | collective-permute-start | bytes 245768 | tf_op jit(solution)/shard_map/ppermute | solution.py:34
  25.9 2.5 %collective-permute-start.11 = (bf16[16,2560]{1,0:T(8,128)(2,1)S(1)}, bf16[16,2560]{1,0:T(8,128)(2,1)S(1)}, u32[]{:S(2)}, u32[]{:S(2)}) collective-permute-start(bf16[16,2560]{1,0:T(8,128)(2,1)S(1)} %collective-permute-done.7.refs_3_), channel_id=1, source_target_pairs={{0,1},{1,0},{2,3},{3,2},{4,5},{5,4},{6,7},{7,6},{8,9},{9,8},{10,11... | collective-permute-start | bytes 245768 | tf_op jit(solution)/shard_map/ppermute | solution.py:34
  26.0 2.4 %collective-permute-start.8 = (bf16[16,2560]{1,0:T(8,128)(2,1)S(1)}, bf16[16,2560]{1,0:T(8,128)(2,1)S(1)}, u32[]{:S(2)}, u32[]{:S(2)}) collective-permute-start(bf16[16,2560]{1,0:T(8,128)(2,1)S(1)} %pad_maximum_fusion.3.refs_0_), channel_id=1, source_target_pairs={{0,1},{1,0},{2,3},{3,2},{4,5},{5,4},{6,7},{7,6},{8,9},{9,8},{10,11... | collective-permute-start | bytes 245768 | tf_op jit(solution)/shard_map/ppermute | solution.py:34
  26.4 2.0 %collective-permute-start.9 = (bf16[16,2560]{1,0:T(8,128)(2,1)S(1)}, bf16[16,2560]{1,0:T(8,128)(2,1)S(1)}, u32[]{:S(2)}, u32[]{:S(2)}) collective-permute-start(bf16[16,2560]{1,0:T(8,128)(2,1)S(1)} %collective-permute-done.5.refs_1_), channel_id=1, source_target_pairs={{0,1},{1,0},{2,3},{3,2},{4,5},{5,4},{6,7},{7,6},{8,9},{9,8},{10,11... | collective-permute-start | bytes 245768 | tf_op jit(solution)/shard_map/ppermute | solution.py:34
  31.5 14.9 %all-to-all-start = ((bf16[8,32,640]{2,1,0:T(8,128)(2,1)}), bf16[8,32,640]{2,1,0:T(8,128)(2,1)S(1)}, u32[]{:S(2)}, u32[]{:S(2)}) async-start(bf16[8,32,640]{2,1,0:T(8,128)(2,1)} %pad_maximum_fusion.2), calls=%async_computation | async-start | bytes 655360 | tf_op jit(solution)/shard_map/all_to_all | solution.py:677
  53.7 12.9 %all-to-all-start.1 = ((bf16[8,32,512]{2,1,0:T(8,128)(2,1)}), bf16[8,32,512]{2,1,0:T(8,128)(2,1)S(1)}, u32[]{:S(2)}, u32[]{:S(2)}) async-start(bf16[8,32,512]{2,1,0:T(8,128)(2,1)} %constant_dynamic-update-slice_fusion), calls=%async_computation.1 | async-start | bytes 524288 | tf_op jit(solution)/shard_map/all_to_all | solution.py:677
  69.7 2.2 %collective-permute-start.16 = (bf16[64,5376]{1,0:T(8,128)(2,1)S(1)}, bf16[64,5376]{1,0:T(8,128)(2,1)S(1)}, u32[]{:S(2)}, u32[]{:S(2)}) collective-permute-start(bf16[64,5376]{1,0:T(8,128)(2,1)S(1)} %get-tuple-element.77), channel_id=1, source_target_pairs={{0,1},{1,0},{2,3},{3,2},{4,5},{5,4},{6,7},{7,6},{8,9},{9,8},{10,11... | collective-permute-start | bytes 2064392 | tf_op jit(solution)/shard_map/ppermute | solution.py:34
  72.3 10.3 %collective-permute-start.17 = (bf16[32,5376]{1,0:T(8,128)(2,1)S(1)}, bf16[32,5376]{1,0:T(8,128)(2,1)S(1)}, u32[]{:S(2)}, u32[]{:S(2)}) collective-permute-start(bf16[32,5376]{1,0:T(8,128)(2,1)S(1)} %slice.87), channel_id=1, source_target_pairs={{0,2},{1,3},{2,0},{3,1},{4,6},{5,7},{6,4},{7,5},{8,10},{9,11},{10,... | collective-permute-start | bytes 1032200 | tf_op jit(solution)/shard_map/ppermute | solution.py:34
  74.0 10.1 %collective-permute-start.19 = (bf16[16,2816]{1,0:T(8,128)(2,1)S(1)}, bf16[16,2816]{1,0:T(8,128)(2,1)S(1)}, u32[]{:S(2)}, u32[]{:S(2)}) collective-permute-start(bf16[16,2816]{1,0:T(8,128)(2,1)S(1)} %get-tuple-element.89), channel_id=1, source_target_pairs={{0,8},{1,9},{2,10},{3,11},{4,12},{5,13},{6,14},{7,15},{8,0},{9,1},... | collective-permute-start | bytes 270344 | tf_op jit(solution)/shard_map/ppermute | solution.py:34
  75.1 13.5 %collective-permute-start.23 = (bf16[16,2816]{1,0:T(8,128)(2,1)S(1)}, bf16[16,2816]{1,0:T(8,128)(2,1)S(1)}, u32[]{:S(2)}, u32[]{:S(2)}) collective-permute-start(bf16[16,2816]{1,0:T(8,128)(2,1)S(1)} %get-tuple-element.91), channel_id=1, source_target_pairs={{0,4},{1,5},{2,6},{3,7},{4,0},{5,1},{6,2},{7,3},{8,12},{9,13},{10,... | collective-permute-start | bytes 270344 | tf_op jit(solution)/shard_map/ppermute | solution.py:34
  76.0 12.6 %collective-permute-start.24 = (bf16[16,2816]{1,0:T(8,128)(2,1)S(1)}, bf16[16,2816]{1,0:T(8,128)(2,1)S(1)}, u32[]{:S(2)}, u32[]{:S(2)}) collective-permute-start(bf16[16,2816]{1,0:T(8,128)(2,1)S(1)} %get-tuple-element.90), channel_id=1, source_target_pairs={{0,12},{1,13},{2,14},{3,15},{4,8},{5,9},{6,10},{7,11},{8,4},{9,5},... | collective-permute-start | bytes 270344 | tf_op jit(solution)/shard_map/ppermute | solution.py:34
  84.2 7.3 %collective-permute-start.20 = (bf16[8,5376]{1,0:T(8,128)(2,1)S(1)}, bf16[8,5376]{1,0:T(8,128)(2,1)S(1)}, u32[]{:S(2)}, u32[]{:S(2)}) collective-permute-start(bf16[8,5376]{1,0:T(8,128)(2,1)S(1)} %get-tuple-element.94), channel_id=1, source_target_pairs={{0,8},{1,9},{2,10},{3,11},{4,12},{5,13},{6,14},{7,15},{8,0},{9,1},... | collective-permute-start | bytes 258056 | tf_op jit(solution)/shard_map/ppermute | solution.py:34
  84.2 7.2 %collective-permute-start.21 = (bf16[8,5376]{1,0:T(8,128)(2,1)S(1)}, bf16[8,5376]{1,0:T(8,128)(2,1)S(1)}, u32[]{:S(2)}, u32[]{:S(2)}) collective-permute-start(bf16[8,5376]{1,0:T(8,128)(2,1)S(1)} %get-tuple-element.93), channel_id=1, source_target_pairs={{0,4},{1,5},{2,6},{3,7},{4,0},{5,1},{6,2},{7,3},{8,12},{9,13},{10,... | collective-permute-start | bytes 258056 | tf_op jit(solution)/shard_map/ppermute | solution.py:34
  86.3 6.4 %collective-permute-start.22 = (bf16[8,5376]{1,0:T(8,128)(2,1)S(1)}, bf16[8,5376]{1,0:T(8,128)(2,1)S(1)}, u32[]{:S(2)}, u32[]{:S(2)}) collective-permute-start(bf16[8,5376]{1,0:T(8,128)(2,1)S(1)} %get-tuple-element.92), channel_id=1, source_target_pairs={{0,12},{1,13},{2,14},{3,15},{4,8},{5,9},{6,10},{7,11},{8,4},{9,5},... | collective-permute-start | bytes 258056 | tf_op jit(solution)/shard_map/ppermute | solution.py:34
  88.7 4.1 %collective-permute-start.25 = (bf16[8,2816]{1,0:T(8,128)(2,1)S(1)}, bf16[8,2816]{1,0:T(8,128)(2,1)S(1)}, u32[]{:S(2)}, u32[]{:S(2)}) collective-permute-start(bf16[8,2816]{1,0:T(8,128)(2,1)S(1)} %slice.88), channel_id=1, source_target_pairs={{0,2},{1,3},{2,0},{3,1},{4,6},{5,7},{6,4},{7,5},{8,10},{9,11},{10,... | collective-permute-start | bytes 135176 | tf_op jit(solution)/shard_map/ppermute | solution.py:34
  (10 other events, 49.5 us)

commit v20 on v17

--- a/solution.py
+++ b/solution.py
@@ -330,77 +330,40 @@
     )(*arrays)
 
 
-def project_kernel(first, last, order, start, block, *refs):
-    count = len(refs) - 4 - (not first) - last
-    parts, (wq, w_kv), refs = refs[:count], refs[count : count + 2], refs[count + 2 :]
-    if not first:
-        before, refs = refs[0], refs[1:]
-    if last:
-        place, refs = refs[0], refs[1:]
-    out, total = refs
-    step = pl.program_id(0)
-    per_query = wq.shape[1]
-
-    @pl.when(step == 0)
-    def _():
-        total[...] = jnp.zeros_like(total) if first else before[...]
-
-    here = pl.ds(pl.multiple_of(step * block, block), block)
-    there = pl.ds(pl.multiple_of(start + step * block, block), block)
-    x = jnp.concatenate([part[:, here] for part in parts], axis=0)
-    products = [
-        jnp.dot(x, wq[there, :], preferred_element_type=jnp.float32),
-        lax.dot_general(x, w_kv[:, there], (((1,), (1,)), ((), ())), preferred_element_type=jnp.float32),
-    ]
-    size = x.shape[0] // len(order)
-    for product, columns in zip(products, (slice(0, per_query), slice(per_query, None))):
-        for i, place_i in enumerate(order):
-            total[place_i * size : (place_i + 1) * size, columns] += product[
-                i * size : (i + 1) * size
-            ]
-
-    @pl.when(step == pl.num_programs(0) - 1)
-    def _():
-        if last:
-            rows = lax.broadcasted_iota(jnp.int32, (out.shape[0], place.shape[1]), 0)
-            route = jnp.where(rows == place[...], 1.0, 0.0).astype(jnp.bfloat16)
-            moved = jnp.dot(
-                route, total[...].astype(jnp.bfloat16), preferred_element_type=jnp.float32
-            )
-            out[...] = moved.astype(jnp.bfloat16)
-        else:
-            out[...] = total[...]
-
-
-def project(start, parts, order, w_query, w_kv_t, before, place, slots):
+def project_kernel(count, order, *refs):
+    parts_a, parts_b, (wq, w_kv, place, out) = refs[:count], refs[count:-4], refs[-4:]
+
+    def products(parts, features):
+        x = jnp.concatenate([part[...] for part in parts], axis=0)
+        query = jnp.dot(x, wq[features, :], preferred_element_type=jnp.float32)
+        key_value = lax.dot_general(
+            x, w_kv[:, features], (((1,), (1,)), ((), ())), preferred_element_type=jnp.float32
+        )
+        return jnp.concatenate([query, key_value], axis=1)
+
+    cut = parts_a[0].shape[1]
+    total = products(parts_a, slice(0, cut))
+    part_b = products(parts_b, slice(cut, wq.shape[0]))
+    size = part_b.shape[0] // len(order)
+    blocks = [order.index(i) for i in range(len(order))]
+    total += jnp.concatenate([part_b[i * size : (i + 1) * size] for i in blocks], axis=0)
+    rows = lax.broadcasted_iota(jnp.int32, (out.shape[0], place.shape[1]), 0)
+    route = jnp.where(rows == place[...], 1.0, 0.0).astype(jnp.bfloat16)
+    moved = jnp.dot(route, total.astype(jnp.bfloat16), preferred_element_type=jnp.float32)
+    out[...] = moved.astype(jnp.bfloat16)
+
+
+def project(parts_a, parts_b, order, w_query, w_kv_t, place, slots):
+    rows = place.shape[1]
+    width = w_query.shape[0]
     row_width = w_query.shape[1] + w_kv_t.shape[0]
-    width = parts[0].shape[1]
-    block = width
-    rows = sum(part.shape[0] for part in parts)
-    first, last = before is None, place is not None
+    args = [*parts_a, *parts_b, w_query, w_kv_t, place]
     vmem = pl.BlockSpec(memory_space=pltpu.VMEM)
-    args = [*parts, w_query, w_kv_t]
-    specs = [vmem] * len(parts)
-    specs += [
-        vmem,
-        vmem,
-    ]
-    if not first:
-        args.append(before)
-        specs.append(vmem)
-    if last:
-        args.append(place)
-        specs.append(vmem)
-        out = jax.ShapeDtypeStruct((slots, row_width), jnp.bfloat16)
-    else:
-        out = jax.ShapeDtypeStruct((rows, row_width), jnp.float32)
     return pl.pallas_call(
-        functools.partial(project_kernel, first, last, order, start, block),
-        grid=(width // block,),
-        in_specs=specs,
+        functools.partial(project_kernel, len(parts_a), order),
+        in_specs=[vmem] * len(args),
         out_specs=vmem,
-        out_shape=out,
-        scratch_shapes=[pltpu.VMEM((rows, row_width), jnp.float32)],
+        out_shape=jax.ShapeDtypeStruct((slots, row_width), jnp.bfloat16),
         compiler_params=pltpu.CompilerParams(vmem_limit_bytes=24 * 2**20),
         cost_estimate=pl.CostEstimate(
             flops=2 * rows * width * row_width,
@@ -626,7 +589,7 @@
 
     moves_a = grid.moves(ORDER_A)
     order_b = [moves_a.index(move) for move in grid.moves(ORDER_B)]
-    cut = width // 16 * 11
+    cut = width // 32 * 23
     xa, xb = norm(hidden_in, norm_gain, (cut, width - cut))
 
     def first(x):
@@ -643,9 +606,7 @@
 
     parts_a, parts_b, others, w_query = gather_rows(grid, xa, xb, first, second)
     (place, place_in, place_a, place_b, mine), w_kv_t = others
-    plain = list(range(owners))
-    total = project(0, parts_a, plain, w_query, w_kv_t, None, None, all_slots)
-    total = project(cut, parts_b, order_b, w_query, w_kv_t, total, place_in, all_slots)
+    total = project(parts_a, parts_b, order_b, w_query, w_kv_t, place_in, all_slots)
     outbound = total.reshape(owners, slot_count, row_width)
     place = after(place, outbound).reshape(requests)
     mine = mine[0, :slot_count]
@@ -670,7 +631,7 @@
         per_query,
         per_key,
     )
-    (w_front,) = fetch((after(w_out, attended), (0, width // 32 * 10)), limit=48)
+    (w_front,) = fetch((after(w_out, attended), (0, width // 32 * 11)), limit=48)
     returned = lax.all_to_all(attended, AXES, split_axis=0, concat_axis=0, tiled=True)
     returned = returned.reshape(all_slots, per_query)
     summed = scatter_sum(grid, place_a, place_b, returned, w_out, w_front, width // 32 * 21)

time: 91.5 us -> 94.4 us (1.032)
  Pallas kernels: 19 us -> 20.6 us
  local copies, waits for them, and re-layouts: 0.38 us -> 1.92 us
    pallas_call x1, Pallas kernels: 3.18 us -> 4.92 us  [product(): pl.pallas_call(functools.partial(product_kernel, tuple(cuts)), in_specs=[...]
    all_to_all x1, waiting for transfers between devices: 8.25 us -> 6.62 us  [on_device(): lax.all_to_all(attended, AXES, split_axis=0, concat_axis=0, tiled=True)]
    unnamed x12 -> x14, local copies, waits for them, and re-layouts: 0.03 us -> 1.57 us
    ppermute x24, waiting for transfers between devices: 16.9 us -> 18.1 us  [send(): return lax.ppermute(x, AXES, pairs)]
    pallas_call x2 -> x1, Pallas kernels: 2.86 us -> 2.69 us  [project(): pl.pallas_call(functools.partial(project_kernel, len(parts_a), order), in...]
  transfers between devices with their start and end apart: 26 -> 26, of which waited for: 11 -> 13; matrix products, arithmetic and copies ran while one was open for 3% -> 3% of each run, Pallas kernels for 7% -> 6%
where the time goes in v20:
time: 94.4 us; the launch traced here: 93.9 us
  waiting for transfers between devices  35.1 us (37%)
  starting transfers between devices  32.7 us (35%)
  Pallas kernels  20.6 us (22%)
  other arithmetic  3.29 us (3%)
  local copies, waits for them, and re-layouts  1.92 us (2%)
    ppermute x24, starting transfers between devices, send(): return lax.ppermute(x, AXES, pairs)  24.9 us
    ppermute x24, waiting for transfers between devices, send(): return lax.ppermute(x, AXES, pairs)  18.1 us
    all_to_all x1, waiting for transfers between devices, on_device(): lax.all_to_all(outbound, AXES, split_axis=0, concat_axis=0, tiled=True)  10.4 us
    all_to_all x1, waiting for transfers between devices, on_device(): lax.all_to_all(attended, AXES, split_axis=0, concat_axis=0, tiled=True)  6.62 us
    pallas_call x1, Pallas kernels, attend(): pl.pallas_call(functools.partial(attend_kernel, per_query, per_key), in_s...  5.86 us
    pallas_call x2, Pallas kernels, fetch(): pl.pallas_call(functools.partial(fetch_kernel, starts), in_specs=[pl.Bloc...  5.21 us
    pallas_call x1, Pallas kernels, product(): pl.pallas_call(functools.partial(product_kernel, tuple(cuts)), in_specs=[...  4.92 us
    all_to_all x1, starting transfers between devices, on_device(): lax.all_to_all(outbound, AXES, split_axis=0, concat_axis=0, tiled=True)  4.27 us
  transfers between devices with their start and end apart: 26, of which 13 were waited for; matrix products, arithmetic and copies ran while one was open for 3% of the time, Pallas kernels for 6%

profile of v20, /device:TPU:0, one launch (start us, length us, event | category | flops | bytes accessed | tf_op | source)
XLA Modules:
  0.0 93.9 jit_solution(112205973666532088)
XLA Ops:
  0.0 1.7 %norm.1 = (bf16[8,5888]{1,0:T(8,128)(2,1)}, bf16[8,2304]{1,0:T(8,128)(2,1)}) custom-call(bf16[8,8192]{1,0:T(8,128)(2,1)} %x.1, f32[1,8192]{1,0:T(1,128)} %bitcast.21), custom_call_target="tpu_custom_call" | custom-call | tf_op jit(solution)/shard_map/norm/pallas_call | solution.py:229
  1.7 4.1 %collective-permute-start = (bf16[8,5888]{1,0:T(8,128)(2,1)}, bf16[8,5888]{1,0:T(8,128)(2,1)S(1)}, u32[]{:S(2)}, u32[]{:S(2)}) collective-permute-start(bf16[8,5888]{1,0:T(8,128)(2,1)} %get-tuple-element.41), channel_id=1, source_target_pairs={{0,8},{1,9},{2,10},{3,11},{4,12},{5,13},{6,14},{7,15},{8,0},{9,1},... | collective-permute-start | bytes 282632 | tf_op jit(solution)/shard_map/ppermute | solution.py:34
  5.8 1.6 %collective-permute-start.1 = (bf16[8,5888]{1,0:T(8,128)(2,1)}, bf16[8,5888]{1,0:T(8,128)(2,1)S(1)}, u32[]{:S(2)}, u32[]{:S(2)}) collective-permute-start(bf16[8,5888]{1,0:T(8,128)(2,1)} %get-tuple-element.41), channel_id=1, source_target_pairs={{0,4},{1,5},{2,6},{3,7},{4,0},{5,1},{6,2},{7,3},{8,12},{9,13},{10,... | collective-permute-start | bytes 282632 | tf_op jit(solution)/shard_map/ppermute | solution.py:34
  7.4 1.7 %collective-permute-start.3 = (bf16[8,2304]{1,0:T(8,128)(2,1)}, bf16[8,2304]{1,0:T(8,128)(2,1)S(1)}, u32[]{:S(2)}, u32[]{:S(2)}) collective-permute-start(bf16[8,2304]{1,0:T(8,128)(2,1)} %get-tuple-element.42), channel_id=1, source_target_pairs={{0,2},{1,3},{2,0},{3,1},{4,6},{5,7},{6,4},{7,5},{8,10},{9,11},{10,... | collective-permute-start | bytes 110600 | tf_op jit(solution)/shard_map/ppermute | solution.py:34
  9.2 1.8 %pad_maximum_fusion.refs_13_ = bf16[128,8192]{1,0:T(8,128)(2,1)S(1)} fusion(bf16[64,8192]{1,0:T(8,128)(2,1)} %bitcast.19, bf16[64,8192]{1,0:T(8,128)(2,1)} %bitcast.20), kind=kLoop, calls=%fused_computation | loop fusion | flops 4194304 | bytes 4194304 | tf_op jit(solution)/shard_map/concatenate | solution.py:602
  11.6 2.4 %collective-permute-done.2 = bf16[8,5888]{1,0:T(8,128)(2,1)S(1)} collective-permute-done((bf16[8,5888]{1,0:T(8,128)(2,1)}, bf16[8,5888]{1,0:T(8,128)(2,1)S(1)}, u32[]{:S(2)}, u32[]{:S(2)}) %collective-permute-start.2) | collective-permute-done | bytes 94240 | tf_op jit(solution)/shard_map/ppermute | solution.py:34
  14.1 1.6 %collective-permute-start.4 = (bf16[32,5888]{1,0:T(8,128)(2,1)S(1)}, bf16[32,5888]{1,0:T(8,128)(2,1)S(1)}, u32[]{:S(2)}, u32[]{:S(2)}) collective-permute-start(bf16[32,5888]{1,0:T(8,128)(2,1)S(1)} %pad_maximum_fusion.1.refs_0_), channel_id=1, source_target_pairs={{0,2},{1,3},{2,0},{3,1},{4,6},{5,7},{6,4},{7,5},{8,10},{9,11},{10,... | collective-permute-start | bytes 1130504 | tf_op jit(solution)/shard_map/ppermute | solution.py:34
  15.7 3.4 %collective-permute-start.5 = (bf16[16,2304]{1,0:T(8,128)(2,1)S(1)}, bf16[16,2304]{1,0:T(8,128)(2,1)S(1)}, u32[]{:S(2)}, u32[]{:S(2)}) collective-permute-start(bf16[16,2304]{1,0:T(8,128)(2,1)S(1)} %pad_maximum_fusion.2.refs_4_), channel_id=1, source_target_pairs={{0,8},{1,9},{2,10},{3,11},{4,12},{5,13},{6,14},{7,15},{8,0},{9,1},... | collective-permute-start | bytes 221192 | tf_op jit(solution)/shard_map/ppermute | solution.py:34
  20.6 3.4 %fetch.2.refs_12_ = bf16[8192,512]{1,0:T(8,128)(2,1)S(1)} custom-call(bf16[8192,512]{1,0:T(8,128)(2,1)} %refs_0_), custom_call_target="tpu_custom_call" | custom-call | bytes 16777216 | tf_op jit(solution)/shard_map/fetch/pallas_call | solution.py:319
  24.0 2.3 %collective-permute-done.6.refs_6_ = bf16[16,2304]{1,0:T(8,128)(2,1)S(1)} collective-permute-done((bf16[16,2304]{1,0:T(8,128)(2,1)S(1)}, bf16[16,2304]{1,0:T(8,128)(2,1)S(1)}, u32[]{:S(2)}, u32[]{:S(2)}) %collective-permute-start.6) | collective-permute-done | bytes 73760 | tf_op jit(solution)/shard_map/ppermute | solution.py:34
  28.6 2.7 %project.1 = bf16[256,640]{1,0:T(8,128)(2,1)} custom-call(bf16[32,5888]{1,0:T(8,128)(2,1)S(1)} %pad_maximum_fusion.1.refs_0_, bf16[32,5888]{1,0:T(8,128)(2,1)S(1)} %collective-permute-done.4.refs_1_, bf16[32,5888]{1,0:T(8,128)(2,1)S(1)} %collective-permute-done.8.refs_2_, bf16[32,5888]{1,0:T(8,128)(2,1)S(1)} %collective-permute-done.9.refs_3_, ...), custom_call_target="tpu_custom_call" | custom-call | flops 1342177280 | bytes 10485760 | tf_op jit(solution)/shard_map/project/pallas_call | solution.py:362
  31.3 4.3 %all-to-all-start = ((bf16[16,16,640]{2,1,0:T(8,128)(2,1)}), bf16[16,16,640]{2,1,0:T(8,128)(2,1)S(1)}, u32[]{:S(2)}, u32[]{:S(2)}) async-start(bf16[16,16,640]{2,1,0:T(8,128)(2,1)} %bitcast.4), calls=%async_computation | async-start | bytes 655360 | tf_op jit(solution)/shard_map/all_to_all | solution.py:622
  36.2 10.4 %all-to-all-done.inbound = bf16[16,16,640]{2,1,0:T(8,128)(2,1)S(1)} async-done(((bf16[16,16,640]{2,1,0:T(8,128)(2,1)}), bf16[16,16,640]{2,1,0:T(8,128)(2,1)S(1)}, u32[]{:S(2)}, u32[]{:S(2)}) %all-to-all-start) | async-done | bytes 327712 | tf_op jit(solution)/shard_map/all_to_all | solution.py:622
  46.6 5.9 %attend.1 = bf16[16,16,512]{2,1,0:T(8,128)(2,1)} custom-call(s32[16,4]{1,0:T(8,128)S(1)} %copy.15.table, s32[2,1,128]{2,1,0:T(1,128)S(1)} %bitcast.14, bf16[16,16,640]{2,1,0:T(8,128)(2,1)S(1)} %all-to-all-done.inbound, f32[16,128]{1,0:T(8,128)S(1)} %get-tuple-element.90.cosine, f32[16,128]{1,0:T(8,128)S(1)} %get-tuple-element.91.sine, ...), custom_call_target="tpu_custom_call" | custom-call | flops 134217728 | bytes 8388608 | tf_op jit(solution)/shard_map/attend/pallas_call | solution.py:541
  52.5 3.5 %all-to-all-start.1 = ((bf16[16,16,512]{2,1,0:T(8,128)(2,1)}), bf16[16,16,512]{2,1,0:T(8,128)(2,1)S(1)}, u32[]{:S(2)}, u32[]{:S(2)}) async-start(bf16[16,16,512]{2,1,0:T(8,128)(2,1)} %attend.1), calls=%async_computation.1 | async-start | bytes 524288 | tf_op jit(solution)/shard_map/all_to_all | solution.py:635
  56.1 1.8 %fetch.3.w_front = bf16[512,2816]{1,0:T(8,128)(2,1)S(1)} custom-call(bf16[512,8192]{1,0:T(8,128)(2,1)} %w_out.1), custom_call_target="tpu_custom_call" | custom-call | bytes 5767168 | tf_op jit(solution)/shard_map/fetch/pallas_call | solution.py:319
  57.9 1.5 %copy-done = bf16[512,2816]{1,0:T(8,128)(2,1)} copy-done((bf16[512,2816]{1,0:T(8,128)(2,1)}, bf16[512,2816]{1,0:T(8,128)(2,1)S(1)}, u32[]{:S(2)}) %copy-start) | copy-done | bytes 2883608
  59.5 6.6 %all-to-all-done.1 = bf16[16,16,512]{2,1,0:T(8,128)(2,1)S(1)} async-done(((bf16[16,16,512]{2,1,0:T(8,128)(2,1)}), bf16[16,16,512]{2,1,0:T(8,128)(2,1)S(1)}, u32[]{:S(2)}, u32[]{:S(2)}) %all-to-all-start.1) | async-done | bytes 262176 | tf_op jit(solution)/shard_map/all_to_all | solution.py:635
  66.1 4.9 %product.1 = (bf16[64,5376]{1,0:T(8,128)(2,1)S(1)}, f32[64,5376]{1,0:T(8,128)S(1)}, bf16[64,2816]{1,0:T(8,128)(2,1)S(1)}, f32[64,2816]{1,0:T(8,128)S(1)}) custom-call(s32[1,128]{1,0:T(1,128)S(1)} %get-tuple-element.50.place_a, s32[1,128]{1,0:T(1,128)S(1)} %get-tuple-element.51.place_b, bf16[256,512]{1,0:T(8,128)(2,1)S(1)} %bitcast.13, ...), custom_call_target="tpu_custom_call" | custom-call | flops 1073741824 | bytes 8388608 | tf_op jit(solution)/shard_map/product/pallas_call | solution.py:155
  71.1 2.1 %collective-permute-done.14 = bf16[64,5376]{1,0:T(8,128)(2,1)S(1)} collective-permute-done((bf16[64,5376]{1,0:T(8,128)(2,1)S(1)}, bf16[64,5376]{1,0:T(8,128)(2,1)S(1)}, u32[]{:S(2)}, u32[]{:S(2)}) %collective-permute-start.14) | collective-permute-done | bytes 688160 | tf_op jit(solution)/shard_map/ppermute | solution.py:34
  76.9 2.9 %collective-permute-start.22 = (bf16[16,2816]{1,0:T(8,128)(2,1)S(1)}, bf16[16,2816]{1,0:T(8,128)(2,1)S(1)}, u32[]{:S(2)}, u32[]{:S(2)}) collective-permute-start(bf16[16,2816]{1,0:T(8,128)(2,1)S(1)} %get-tuple-element.82), channel_id=1, source_target_pairs={{0,12},{1,13},{2,14},{3,15},{4,8},{5,9},{6,10},{7,11},{8,4},{9,5},... | collective-permute-start | bytes 270344 | tf_op jit(solution)/shard_map/ppermute | solution.py:34
  79.7 4.2 %collective-permute-done.15 = bf16[32,5376]{1,0:T(8,128)(2,1)S(1)} collective-permute-done((bf16[32,5376]{1,0:T(8,128)(2,1)S(1)}, bf16[32,5376]{1,0:T(8,128)(2,1)S(1)}, u32[]{:S(2)}, u32[]{:S(2)}) %collective-permute-start.15) | collective-permute-done | bytes 344096 | tf_op jit(solution)/shard_map/ppermute | solution.py:34
  85.9 2.6 %collective-permute-start.20 = (bf16[8,5376]{1,0:T(8,128)(2,1)S(1)}, bf16[8,5376]{1,0:T(8,128)(2,1)S(1)}, u32[]{:S(2)}, u32[]{:S(2)}) collective-permute-start(bf16[8,5376]{1,0:T(8,128)(2,1)S(1)} %get-tuple-element.84), channel_id=1, source_target_pairs={{0,12},{1,13},{2,14},{3,15},{4,8},{5,9},{6,10},{7,11},{8,4},{9,5},... | collective-permute-start | bytes 258056 | tf_op jit(solution)/shard_map/ppermute | solution.py:34
  88.9 4.2 %collective-permute-done.18 = bf16[8,5376]{1,0:T(8,128)(2,1)S(1)} collective-permute-done((bf16[8,5376]{1,0:T(8,128)(2,1)S(1)}, bf16[8,5376]{1,0:T(8,128)(2,1)S(1)}, u32[]{:S(2)}, u32[]{:S(2)}) %collective-permute-start.18) | collective-permute-done | bytes 86048 | tf_op jit(solution)/shard_map/ppermute | solution.py:34
  (73 shorter events, 11.9 us)
Async XLA Ops:
  1.7 9.9 %collective-permute-start = (bf16[8,5888]{1,0:T(8,128)(2,1)}, bf16[8,5888]{1,0:T(8,128)(2,1)S(1)}, u32[]{:S(2)}, u32[]{:S(2)}) collective-permute-start(bf16[8,5888]{1,0:T(8,128)(2,1)} %get-tuple-element.41), channel_id=1, source_target_pairs={{0,8},{1,9},{2,10},{3,11},{4,12},{5,13},{6,14},{7,15},{8,0},{9,1},... | collective-permute-start | bytes 282632 | tf_op jit(solution)/shard_map/ppermute | solution.py:34
  5.8 5.8 %collective-permute-start.1 = (bf16[8,5888]{1,0:T(8,128)(2,1)}, bf16[8,5888]{1,0:T(8,128)(2,1)S(1)}, u32[]{:S(2)}, u32[]{:S(2)}) collective-permute-start(bf16[8,5888]{1,0:T(8,128)(2,1)} %get-tuple-element.41), channel_id=1, source_target_pairs={{0,4},{1,5},{2,6},{3,7},{4,0},{5,1},{6,2},{7,3},{8,12},{9,13},{10,... | collective-permute-start | bytes 282632 | tf_op jit(solution)/shard_map/ppermute | solution.py:34
  7.4 6.6 %collective-permute-start.2 = (bf16[8,5888]{1,0:T(8,128)(2,1)}, bf16[8,5888]{1,0:T(8,128)(2,1)S(1)}, u32[]{:S(2)}, u32[]{:S(2)}) collective-permute-start(bf16[8,5888]{1,0:T(8,128)(2,1)} %get-tuple-element.41), channel_id=1, source_target_pairs={{0,12},{1,13},{2,14},{3,15},{4,8},{5,9},{6,10},{7,11},{8,4},{9,5},... | collective-permute-start | bytes 282632 | tf_op jit(solution)/shard_map/ppermute | solution.py:34
  7.4 4.2 %collective-permute-start.3 = (bf16[8,2304]{1,0:T(8,128)(2,1)}, bf16[8,2304]{1,0:T(8,128)(2,1)S(1)}, u32[]{:S(2)}, u32[]{:S(2)}) collective-permute-start(bf16[8,2304]{1,0:T(8,128)(2,1)} %get-tuple-element.42), channel_id=1, source_target_pairs={{0,2},{1,3},{2,0},{3,1},{4,6},{5,7},{6,4},{7,5},{8,10},{9,11},{10,... | collective-permute-start | bytes 110600 | tf_op jit(solution)/shard_map/ppermute | solution.py:34
  14.1 12.2 %collective-permute-start.4 = (bf16[32,5888]{1,0:T(8,128)(2,1)S(1)}, bf16[32,5888]{1,0:T(8,128)(2,1)S(1)}, u32[]{:S(2)}, u32[]{:S(2)}) collective-permute-start(bf16[32,5888]{1,0:T(8,128)(2,1)S(1)} %pad_maximum_fusion.1.refs_0_), channel_id=1, source_target_pairs={{0,2},{1,3},{2,0},{3,1},{4,6},{5,7},{6,4},{7,5},{8,10},{9,11},{10,... | collective-permute-start | bytes 1130504 | tf_op jit(solution)/shard_map/ppermute | solution.py:34
  15.7 11.6 %collective-permute-start.8 = (bf16[32,5888]{1,0:T(8,128)(2,1)S(1)}, bf16[32,5888]{1,0:T(8,128)(2,1)S(1)}, u32[]{:S(2)}, u32[]{:S(2)}) collective-permute-start(bf16[32,5888]{1,0:T(8,128)(2,1)S(1)} %pad_maximum_fusion.1.refs_0_), channel_id=1, source_target_pairs={{0,1},{1,0},{2,3},{3,2},{4,5},{5,4},{6,7},{7,6},{8,9},{9,8},{10,11... | collective-permute-start | bytes 1130504 | tf_op jit(solution)/shard_map/ppermute | solution.py:34
  15.7 8.3 %collective-permute-start.5 = (bf16[16,2304]{1,0:T(8,128)(2,1)S(1)}, bf16[16,2304]{1,0:T(8,128)(2,1)S(1)}, u32[]{:S(2)}, u32[]{:S(2)}) collective-permute-start(bf16[16,2304]{1,0:T(8,128)(2,1)S(1)} %pad_maximum_fusion.2.refs_4_), channel_id=1, source_target_pairs={{0,8},{1,9},{2,10},{3,11},{4,12},{5,13},{6,14},{7,15},{8,0},{9,1},... | collective-permute-start | bytes 221192 | tf_op jit(solution)/shard_map/ppermute | solution.py:34
  19.1 7.2 %collective-permute-start.6 = (bf16[16,2304]{1,0:T(8,128)(2,1)S(1)}, bf16[16,2304]{1,0:T(8,128)(2,1)S(1)}, u32[]{:S(2)}, u32[]{:S(2)}) collective-permute-start(bf16[16,2304]{1,0:T(8,128)(2,1)S(1)} %pad_maximum_fusion.2.refs_4_), channel_id=1, source_target_pairs={{0,4},{1,5},{2,6},{3,7},{4,0},{5,1},{6,2},{7,3},{8,12},{9,13},{10,... | collective-permute-start | bytes 221192 | tf_op jit(solution)/shard_map/ppermute | solution.py:34
  19.1 7.2 %collective-permute-start.7 = (bf16[16,2304]{1,0:T(8,128)(2,1)S(1)}, bf16[16,2304]{1,0:T(8,128)(2,1)S(1)}, u32[]{:S(2)}, u32[]{:S(2)}) collective-permute-start(bf16[16,2304]{1,0:T(8,128)(2,1)S(1)} %pad_maximum_fusion.2.refs_4_), channel_id=1, source_target_pairs={{0,12},{1,13},{2,14},{3,15},{4,8},{5,9},{6,10},{7,11},{8,4},{9,5},... | collective-permute-start | bytes 221192 | tf_op jit(solution)/shard_map/ppermute | solution.py:34
  26.3 2.3 %collective-permute-start.9 = (bf16[32,5888]{1,0:T(8,128)(2,1)S(1)}, bf16[32,5888]{1,0:T(8,128)(2,1)S(1)}, u32[]{:S(2)}, u32[]{:S(2)}) collective-permute-start(bf16[32,5888]{1,0:T(8,128)(2,1)S(1)} %collective-permute-done.4.refs_1_), channel_id=1, source_target_pairs={{0,1},{1,0},{2,3},{3,2},{4,5},{5,4},{6,7},{7,6},{8,9},{9,8},{10,11... | collective-permute-start | bytes 1130504 | tf_op jit(solution)/shard_map/ppermute | solution.py:34
  26.3 1.8 %collective-permute-start.10 = (bf16[16,2304]{1,0:T(8,128)(2,1)S(1)}, bf16[16,2304]{1,0:T(8,128)(2,1)S(1)}, u32[]{:S(2)}, u32[]{:S(2)}) collective-permute-start(bf16[16,2304]{1,0:T(8,128)(2,1)S(1)} %pad_maximum_fusion.2.refs_4_), channel_id=1, source_target_pairs={{0,1},{1,0},{2,3},{3,2},{4,5},{5,4},{6,7},{7,6},{8,9},{9,8},{10,11... | collective-permute-start | bytes 221192 | tf_op jit(solution)/shard_map/ppermute | solution.py:34
  26.9 1.4 %collective-permute-start.12 = (bf16[16,2304]{1,0:T(8,128)(2,1)S(1)}, bf16[16,2304]{1,0:T(8,128)(2,1)S(1)}, u32[]{:S(2)}, u32[]{:S(2)}) collective-permute-start(bf16[16,2304]{1,0:T(8,128)(2,1)S(1)} %collective-permute-done.6.refs_6_), channel_id=1, source_target_pairs={{0,1},{1,0},{2,3},{3,2},{4,5},{5,4},{6,7},{7,6},{8,9},{9,8},{10,11... | collective-permute-start | bytes 221192 | tf_op jit(solution)/shard_map/ppermute | solution.py:34
  31.3 15.4 %all-to-all-start = ((bf16[16,16,640]{2,1,0:T(8,128)(2,1)}), bf16[16,16,640]{2,1,0:T(8,128)(2,1)S(1)}, u32[]{:S(2)}, u32[]{:S(2)}) async-start(bf16[16,16,640]{2,1,0:T(8,128)(2,1)} %bitcast.4), calls=%async_computation | async-start | bytes 655360 | tf_op jit(solution)/shard_map/all_to_all | solution.py:622
  52.5 13.6 %all-to-all-start.1 = ((bf16[16,16,512]{2,1,0:T(8,128)(2,1)}), bf16[16,16,512]{2,1,0:T(8,128)(2,1)S(1)}, u32[]{:S(2)}, u32[]{:S(2)}) async-start(bf16[16,16,512]{2,1,0:T(8,128)(2,1)} %attend.1), calls=%async_computation.1 | async-start | bytes 524288 | tf_op jit(solution)/shard_map/all_to_all | solution.py:635
  71.0 2.2 %collective-permute-start.14 = (bf16[64,5376]{1,0:T(8,128)(2,1)S(1)}, bf16[64,5376]{1,0:T(8,128)(2,1)S(1)}, u32[]{:S(2)}, u32[]{:S(2)}) collective-permute-start(bf16[64,5376]{1,0:T(8,128)(2,1)S(1)} %get-tuple-element.69), channel_id=1, source_target_pairs={{0,1},{1,0},{2,3},{3,2},{4,5},{5,4},{6,7},{7,6},{8,9},{9,8},{10,11... | collective-permute-start | bytes 2064392 | tf_op jit(solution)/shard_map/ppermute | solution.py:34
  73.4 1.7 %collective-permute-start.16 = (bf16[64,2816]{1,0:T(8,128)(2,1)S(1)}, bf16[64,2816]{1,0:T(8,128)(2,1)S(1)}, u32[]{:S(2)}, u32[]{:S(2)}) collective-permute-start(bf16[64,2816]{1,0:T(8,128)(2,1)S(1)} %get-tuple-element.72), channel_id=1, source_target_pairs={{0,1},{1,0},{2,3},{3,2},{4,5},{5,4},{6,7},{7,6},{8,9},{9,8},{10,11... | collective-permute-start | bytes 1081352 | tf_op jit(solution)/shard_map/ppermute | solution.py:34
  73.6 10.3 %collective-permute-start.15 = (bf16[32,5376]{1,0:T(8,128)(2,1)S(1)}, bf16[32,5376]{1,0:T(8,128)(2,1)S(1)}, u32[]{:S(2)}, u32[]{:S(2)}) collective-permute-start(bf16[32,5376]{1,0:T(8,128)(2,1)S(1)} %slice.87), channel_id=1, source_target_pairs={{0,2},{1,3},{2,0},{3,1},{4,6},{5,7},{6,4},{7,5},{8,10},{9,11},{10,... | collective-permute-start | bytes 1032200 | tf_op jit(solution)/shard_map/ppermute | solution.py:34
  75.3 8.7 %collective-permute-start.17 = (bf16[16,2816]{1,0:T(8,128)(2,1)S(1)}, bf16[16,2816]{1,0:T(8,128)(2,1)S(1)}, u32[]{:S(2)}, u32[]{:S(2)}) collective-permute-start(bf16[16,2816]{1,0:T(8,128)(2,1)S(1)} %get-tuple-element.81), channel_id=1, source_target_pairs={{0,8},{1,9},{2,10},{3,11},{4,12},{5,13},{6,14},{7,15},{8,0},{9,1},... | collective-permute-start | bytes 270344 | tf_op jit(solution)/shard_map/ppermute | solution.py:34
  76.4 12.2 %collective-permute-start.21 = (bf16[16,2816]{1,0:T(8,128)(2,1)S(1)}, bf16[16,2816]{1,0:T(8,128)(2,1)S(1)}, u32[]{:S(2)}, u32[]{:S(2)}) collective-permute-start(bf16[16,2816]{1,0:T(8,128)(2,1)S(1)} %get-tuple-element.83), channel_id=1, source_target_pairs={{0,4},{1,5},{2,6},{3,7},{4,0},{5,1},{6,2},{7,3},{8,12},{9,13},{10,... | collective-permute-start | bytes 270344 | tf_op jit(solution)/shard_map/ppermute | solution.py:34
  76.9 11.6 %collective-permute-start.22 = (bf16[16,2816]{1,0:T(8,128)(2,1)S(1)}, bf16[16,2816]{1,0:T(8,128)(2,1)S(1)}, u32[]{:S(2)}, u32[]{:S(2)}) collective-permute-start(bf16[16,2816]{1,0:T(8,128)(2,1)S(1)} %get-tuple-element.82), channel_id=1, source_target_pairs={{0,12},{1,13},{2,14},{3,15},{4,8},{5,9},{6,10},{7,11},{8,4},{9,5},... | collective-permute-start | bytes 270344 | tf_op jit(solution)/shard_map/ppermute | solution.py:34
  84.1 9.1 %collective-permute-start.18 = (bf16[8,5376]{1,0:T(8,128)(2,1)S(1)}, bf16[8,5376]{1,0:T(8,128)(2,1)S(1)}, u32[]{:S(2)}, u32[]{:S(2)}) collective-permute-start(bf16[8,5376]{1,0:T(8,128)(2,1)S(1)} %get-tuple-element.86), channel_id=1, source_target_pairs={{0,8},{1,9},{2,10},{3,11},{4,12},{5,13},{6,14},{7,15},{8,0},{9,1},... | collective-permute-start | bytes 258056 | tf_op jit(solution)/shard_map/ppermute | solution.py:34
  85.1 8.0 %collective-permute-start.19 = (bf16[8,5376]{1,0:T(8,128)(2,1)S(1)}, bf16[8,5376]{1,0:T(8,128)(2,1)S(1)}, u32[]{:S(2)}, u32[]{:S(2)}) collective-permute-start(bf16[8,5376]{1,0:T(8,128)(2,1)S(1)} %get-tuple-element.85), channel_id=1, source_target_pairs={{0,4},{1,5},{2,6},{3,7},{4,0},{5,1},{6,2},{7,3},{8,12},{9,13},{10,... | collective-permute-start | bytes 258056 | tf_op jit(solution)/shard_map/ppermute | solution.py:34
  85.9 7.2 %collective-permute-start.20 = (bf16[8,5376]{1,0:T(8,128)(2,1)S(1)}, bf16[8,5376]{1,0:T(8,128)(2,1)S(1)}, u32[]{:S(2)}, u32[]{:S(2)}) collective-permute-start(bf16[8,5376]{1,0:T(8,128)(2,1)S(1)} %get-tuple-element.84), channel_id=1, source_target_pairs={{0,12},{1,13},{2,14},{3,15},{4,8},{5,9},{6,10},{7,11},{8,4},{9,5},... | collective-permute-start | bytes 258056 | tf_op jit(solution)/shard_map/ppermute | solution.py:34
  88.6 4.6 %collective-permute-start.23 = (bf16[8,2816]{1,0:T(8,128)(2,1)S(1)}, bf16[8,2816]{1,0:T(8,128)(2,1)S(1)}, u32[]{:S(2)}, u32[]{:S(2)}) collective-permute-start(bf16[8,2816]{1,0:T(8,128)(2,1)S(1)} %slice.88), channel_id=1, source_target_pairs={{0,2},{1,3},{2,0},{3,1},{4,6},{5,7},{6,4},{7,5},{8,10},{9,11},{10,... | collective-permute-start | bytes 135176 | tf_op jit(solution)/shard_map/ppermute | solution.py:34
  (9 other events, 48.0 us)

commit v21 on v17

--- a/solution.py
+++ b/solution.py
@@ -426,6 +426,7 @@
     value_pool,
     sems,
     key_new,
+    query_tile,
     query_rot,
     value_own,
     chance,
@@ -453,7 +454,6 @@
             pltpu.make_async_copy(pool.at[part], on_chip.at[part], sem).start()
 
     fetch_pool(key_pages, key_pool, sems.at[0])
-    fetch_pool(value_pages, value_pool, sems.at[1])
 
     def held(pool, slot, columns):
         return [pool[table[slot, j], :, columns] for j in range(pages)]
@@ -498,22 +498,27 @@
     )
 
     own_chances = {}
+    for p in range(pairs):
+        for b in range(batches):
+            turned = query_rot[p, b].T.astype(jnp.bfloat16)
+            none = jnp.zeros_like(turned)
+            query_tile[p, b, :HEAD] = jnp.where(first, turned, none)
+            query_tile[p, b, HEAD:] = jnp.where(first, none, turned)
+
+    fetch_pool(value_pages, value_pool, sems.at[1])
     pltpu.make_async_copy(key_pool, key_pool, sems.at[0]).wait()
     for p in range(pairs):
         columns_p = slice(p * 2 * HEAD, (p + 1) * 2 * HEAD)
         for b in range(batches):
             valid = row < lengths[b]
-            turned = query_rot[p, b].T.astype(jnp.bfloat16)
-            none = jnp.zeros_like(turned)
-            wide = jnp.concatenate(
-                [jnp.where(first, turned, none), jnp.where(first, none, turned)], axis=0
-            )
             keys = []
             for s in range(batch):
                 keys += held(key_pool, b * batch + s, columns_p)
             keys.append(key_new[:, columns_p])
             products = jnp.dot(
-                jnp.concatenate(keys, axis=0), wide, preferred_element_type=jnp.float32
+                jnp.concatenate(keys, axis=0),
+                query_tile[p, b],
+                preferred_element_type=jnp.float32,
             )
             scores = products[:span]
             for s in range(1, batch):
@@ -585,6 +590,7 @@
             pltpu.VMEM(value_pages.shape, jnp.bfloat16),
             pltpu.SemaphoreType.DMA((2,)),
             pltpu.VMEM((slots, kv_width), jnp.bfloat16),
+            pltpu.VMEM((pairs, batches, 2 * HEAD, columns), jnp.bfloat16),
             pltpu.VMEM((pairs, batches, columns, HEAD), jnp.float32),
             pltpu.VMEM((kv_heads, slots, HEAD), jnp.float32),
             pltpu.VMEM((pairs, batches, columns, span), jnp.float32),

time: 91.5 us -> 91.8 us (level)
  no operation moved by 1% of the time
where the time goes in v21:
time: 91.8 us; the launch traced here: 91.4 us
  waiting for transfers between devices  35.6 us (39%)
  starting transfers between devices  32.5 us (35%)
  Pallas kernels  19.3 us (21%)
  other arithmetic  3.29 us (4%)
    ppermute x24, starting transfers between devices, send(): return lax.ppermute(x, AXES, pairs)  24.6 us
    ppermute x24, waiting for transfers between devices, send(): return lax.ppermute(x, AXES, pairs)  16.9 us
    all_to_all x1, waiting for transfers between devices, on_device(): lax.all_to_all(outbound, AXES, split_axis=0, concat_axis=0, tiled=True)  10.4 us
    all_to_all x1, waiting for transfers between devices, on_device(): lax.all_to_all(attended, AXES, split_axis=0, concat_axis=0, tiled=True)  8.25 us
    pallas_call x1, Pallas kernels, attend(): pl.pallas_call(functools.partial(attend_kernel, per_query, per_key), in_s...  6.21 us
    pallas_call x2, Pallas kernels, fetch(): pl.pallas_call(functools.partial(fetch_kernel, starts), in_specs=[pl.Bloc...  5.14 us
    all_to_all x1, starting transfers between devices, on_device(): lax.all_to_all(outbound, AXES, split_axis=0, concat_axis=0, tiled=True)  4.41 us
    all_to_all x1, starting transfers between devices, on_device(): lax.all_to_all(attended, AXES, split_axis=0, concat_axis=0, tiled=True)  3.54 us
  transfers between devices with their start and end apart: 26, of which 11 were waited for; matrix products, arithmetic and copies ran while one was open for 3% of the time, Pallas kernels for 7%

profile of v21, /device:TPU:0, one launch (start us, length us, event | category | flops | bytes accessed | tf_op | source)
XLA Modules:
  0.0 91.4 jit_solution(242917396723009535)
XLA Ops:
  0.0 1.7 %norm.1 = (bf16[8,5632]{1,0:T(8,128)(2,1)}, bf16[8,2560]{1,0:T(8,128)(2,1)}) custom-call(bf16[8,8192]{1,0:T(8,128)(2,1)} %x.1, f32[1,8192]{1,0:T(1,128)} %bitcast.21), custom_call_target="tpu_custom_call" | custom-call | tf_op jit(solution)/shard_map/norm/pallas_call | solution.py:229
  1.7 4.1 %collective-permute-start = (bf16[8,5632]{1,0:T(8,128)(2,1)}, bf16[8,5632]{1,0:T(8,128)(2,1)S(1)}, u32[]{:S(2)}, u32[]{:S(2)}) collective-permute-start(bf16[8,5632]{1,0:T(8,128)(2,1)} %get-tuple-element.41), channel_id=1, source_target_pairs={{0,8},{1,9},{2,10},{3,11},{4,12},{5,13},{6,14},{7,15},{8,0},{9,1},... | collective-permute-start | bytes 270344 | tf_op jit(solution)/shard_map/ppermute | solution.py:34
  5.8 1.6 %collective-permute-start.1 = (bf16[8,5632]{1,0:T(8,128)(2,1)}, bf16[8,5632]{1,0:T(8,128)(2,1)S(1)}, u32[]{:S(2)}, u32[]{:S(2)}) collective-permute-start(bf16[8,5632]{1,0:T(8,128)(2,1)} %get-tuple-element.41), channel_id=1, source_target_pairs={{0,4},{1,5},{2,6},{3,7},{4,0},{5,1},{6,2},{7,3},{8,12},{9,13},{10,... | collective-permute-start | bytes 270344 | tf_op jit(solution)/shard_map/ppermute | solution.py:34
  7.4 1.7 %collective-permute-start.3 = (bf16[8,2560]{1,0:T(8,128)(2,1)}, bf16[8,2560]{1,0:T(8,128)(2,1)S(1)}, u32[]{:S(2)}, u32[]{:S(2)}) collective-permute-start(bf16[8,2560]{1,0:T(8,128)(2,1)} %get-tuple-element.42), channel_id=1, source_target_pairs={{0,2},{1,3},{2,0},{3,1},{4,6},{5,7},{6,4},{7,5},{8,10},{9,11},{10,... | collective-permute-start | bytes 122888 | tf_op jit(solution)/shard_map/ppermute | solution.py:34
  9.2 1.8 %pad_maximum_fusion.refs_5_.refs_9_ = bf16[128,8192]{1,0:T(8,128)(2,1)S(1)} fusion(bf16[64,8192]{1,0:T(8,128)(2,1)} %bitcast.19, bf16[64,8192]{1,0:T(8,128)(2,1)} %bitcast.20), kind=kLoop, calls=%fused_computation | loop fusion | flops 4194304 | bytes 4194304 | tf_op jit(solution)/shard_map/concatenate | solution.py:645
  11.7 2.3 %collective-permute-done.2 = bf16[8,5632]{1,0:T(8,128)(2,1)S(1)} collective-permute-done((bf16[8,5632]{1,0:T(8,128)(2,1)}, bf16[8,5632]{1,0:T(8,128)(2,1)S(1)}, u32[]{:S(2)}, u32[]{:S(2)}) %collective-permute-start.2) | collective-permute-done | bytes 90144 | tf_op jit(solution)/shard_map/ppermute | solution.py:34
  14.1 1.6 %collective-permute-start.4 = (bf16[32,5632]{1,0:T(8,128)(2,1)S(1)}, bf16[32,5632]{1,0:T(8,128)(2,1)S(1)}, u32[]{:S(2)}, u32[]{:S(2)}) collective-permute-start(bf16[32,5632]{1,0:T(8,128)(2,1)S(1)} %pad_maximum_fusion.1.refs_0_), channel_id=1, source_target_pairs={{0,2},{1,3},{2,0},{3,1},{4,6},{5,7},{6,4},{7,5},{8,10},{9,11},{10,... | collective-permute-start | bytes 1081352 | tf_op jit(solution)/shard_map/ppermute | solution.py:34
  15.6 3.1 %collective-permute-start.5 = (bf16[16,2560]{1,0:T(8,128)(2,1)S(1)}, bf16[16,2560]{1,0:T(8,128)(2,1)S(1)}, u32[]{:S(2)}, u32[]{:S(2)}) collective-permute-start(bf16[16,2560]{1,0:T(8,128)(2,1)S(1)} %pad_maximum_fusion.2.refs_0_), channel_id=1, source_target_pairs={{0,8},{1,9},{2,10},{3,11},{4,12},{5,13},{6,14},{7,15},{8,0},{9,1},... | collective-permute-start | bytes 245768 | tf_op jit(solution)/shard_map/ppermute | solution.py:34
  18.7 1.5 %collective-permute-start.7 = (bf16[16,2560]{1,0:T(8,128)(2,1)S(1)}, bf16[16,2560]{1,0:T(8,128)(2,1)S(1)}, u32[]{:S(2)}, u32[]{:S(2)}) collective-permute-start(bf16[16,2560]{1,0:T(8,128)(2,1)S(1)} %pad_maximum_fusion.2.refs_0_), channel_id=1, source_target_pairs={{0,12},{1,13},{2,14},{3,15},{4,8},{5,9},{6,10},{7,11},{8,4},{9,5},... | collective-permute-start | bytes 245768 | tf_op jit(solution)/shard_map/ppermute | solution.py:34
  20.2 3.4 %fetch.2.refs_4_.refs_8_ = bf16[8192,512]{1,0:T(8,128)(2,1)S(1)} custom-call(bf16[8192,512]{1,0:T(8,128)(2,1)} %refs_0_), custom_call_target="tpu_custom_call" | custom-call | bytes 16777216 | tf_op jit(solution)/shard_map/fetch/pallas_call | solution.py:319
  24.0 1.4 %collective-permute-done.6.refs_2_ = bf16[16,2560]{1,0:T(8,128)(2,1)S(1)} collective-permute-done((bf16[16,2560]{1,0:T(8,128)(2,1)S(1)}, bf16[16,2560]{1,0:T(8,128)(2,1)S(1)}, u32[]{:S(2)}, u32[]{:S(2)}) %collective-permute-start.6) | collective-permute-done | bytes 81952 | tf_op jit(solution)/shard_map/ppermute | solution.py:34
  28.4 1.6 %project.3 = bf16[256,640]{1,0:T(8,128)(2,1)} custom-call(bf16[16,2560]{1,0:T(8,128)(2,1)S(1)} %pad_maximum_fusion.2.refs_0_, bf16[16,2560]{1,0:T(8,128)(2,1)S(1)} %collective-permute-done.5.refs_1_, bf16[16,2560]{1,0:T(8,128)(2,1)S(1)} %collective-permute-done.6.refs_2_, bf16[16,2560]{1,0:T(8,128)(2,1)S(1)} %collective-permute-done.7.refs_3_, ...), custom_call_target="tpu_custom_call" | custom-call | flops 419430400 | bytes 3276800 | tf_op jit(solution)/shard_map/project/pallas_call | solution.py:397
  30.0 4.4 %all-to-all-start = ((bf16[16,16,640]{2,1,0:T(8,128)(2,1)}), bf16[16,16,640]{2,1,0:T(8,128)(2,1)S(1)}, u32[]{:S(2)}, u32[]{:S(2)}) async-start(bf16[16,16,640]{2,1,0:T(8,128)(2,1)} %bitcast.4), calls=%async_computation | async-start | bytes 655360 | tf_op jit(solution)/shard_map/all_to_all | solution.py:667
  35.1 10.4 %all-to-all-done.inbound = bf16[16,16,640]{2,1,0:T(8,128)(2,1)S(1)} async-done(((bf16[16,16,640]{2,1,0:T(8,128)(2,1)}), bf16[16,16,640]{2,1,0:T(8,128)(2,1)S(1)}, u32[]{:S(2)}, u32[]{:S(2)}) %all-to-all-start) | async-done | bytes 327712 | tf_op jit(solution)/shard_map/all_to_all | solution.py:667
  45.5 6.2 %attend.1 = bf16[16,16,512]{2,1,0:T(8,128)(2,1)} custom-call(s32[16,4]{1,0:T(8,128)S(1)} %copy.15.table, s32[2,1,128]{2,1,0:T(1,128)S(1)} %bitcast.14, bf16[16,16,640]{2,1,0:T(8,128)(2,1)S(1)} %all-to-all-done.inbound, f32[16,128]{1,0:T(8,128)S(1)} %get-tuple-element.90.cosine, f32[16,128]{1,0:T(8,128)S(1)} %get-tuple-element.91.sine, ...), custom_call_target="tpu_custom_call" | custom-call | flops 134217728 | bytes 8388608 | tf_op jit(solution)/shard_map/attend/pallas_call | solution.py:583
  51.7 3.5 %all-to-all-start.1 = ((bf16[16,16,512]{2,1,0:T(8,128)(2,1)}), bf16[16,16,512]{2,1,0:T(8,128)(2,1)S(1)}, u32[]{:S(2)}, u32[]{:S(2)}) async-start(bf16[16,16,512]{2,1,0:T(8,128)(2,1)} %attend.1), calls=%async_computation.1 | async-start | bytes 524288 | tf_op jit(solution)/shard_map/all_to_all | solution.py:680
  55.3 1.8 %fetch.3.w_front = bf16[512,2560]{1,0:T(8,128)(2,1)S(1)} custom-call(bf16[512,8192]{1,0:T(8,128)(2,1)} %w_out.1), custom_call_target="tpu_custom_call" | custom-call | bytes 5242880 | tf_op jit(solution)/shard_map/fetch/pallas_call | solution.py:319
  57.1 8.2 %all-to-all-done.1 = bf16[16,16,512]{2,1,0:T(8,128)(2,1)S(1)} async-done(((bf16[16,16,512]{2,1,0:T(8,128)(2,1)}), bf16[16,16,512]{2,1,0:T(8,128)(2,1)S(1)}, u32[]{:S(2)}, u32[]{:S(2)}) %all-to-all-start.1) | async-done | bytes 262176 | tf_op jit(solution)/shard_map/all_to_all | solution.py:680
  65.3 3.2 %product.1 = (bf16[64,5376]{1,0:T(8,128)(2,1)S(1)}, f32[64,5376]{1,0:T(8,128)S(1)}, bf16[64,2816]{1,0:T(8,128)(2,1)S(1)}, f32[64,2816]{1,0:T(8,128)S(1)}) custom-call(s32[1,128]{1,0:T(1,128)S(1)} %get-tuple-element.50.place_a, s32[1,128]{1,0:T(1,128)S(1)} %get-tuple-element.51.place_b, bf16[256,512]{1,0:T(8,128)(2,1)S(1)} %bitcast.13, ...), custom_call_target="tpu_custom_call" | custom-call | flops 1073741824 | bytes 8388608 | tf_op jit(solution)/shard_map/product/pallas_call | solution.py:155
  68.6 2.1 %collective-permute-done.14 = bf16[64,5376]{1,0:T(8,128)(2,1)S(1)} collective-permute-done((bf16[64,5376]{1,0:T(8,128)(2,1)S(1)}, bf16[64,5376]{1,0:T(8,128)(2,1)S(1)}, u32[]{:S(2)}, u32[]{:S(2)}) %collective-permute-start.14) | collective-permute-done | bytes 688160 | tf_op jit(solution)/shard_map/ppermute | solution.py:34
  74.4 2.9 %collective-permute-start.22 = (bf16[16,2816]{1,0:T(8,128)(2,1)S(1)}, bf16[16,2816]{1,0:T(8,128)(2,1)S(1)}, u32[]{:S(2)}, u32[]{:S(2)}) collective-permute-start(bf16[16,2816]{1,0:T(8,128)(2,1)S(1)} %get-tuple-element.82), channel_id=1, source_target_pairs={{0,12},{1,13},{2,14},{3,15},{4,8},{5,9},{6,10},{7,11},{8,4},{9,5},... | collective-permute-start | bytes 270344 | tf_op jit(solution)/shard_map/ppermute | solution.py:34
  77.2 4.2 %collective-permute-done.15 = bf16[32,5376]{1,0:T(8,128)(2,1)S(1)} collective-permute-done((bf16[32,5376]{1,0:T(8,128)(2,1)S(1)}, bf16[32,5376]{1,0:T(8,128)(2,1)S(1)}, u32[]{:S(2)}, u32[]{:S(2)}) %collective-permute-start.15) | collective-permute-done | bytes 344096 | tf_op jit(solution)/shard_map/ppermute | solution.py:34
  83.4 2.6 %collective-permute-start.20 = (bf16[8,5376]{1,0:T(8,128)(2,1)S(1)}, bf16[8,5376]{1,0:T(8,128)(2,1)S(1)}, u32[]{:S(2)}, u32[]{:S(2)}) collective-permute-start(bf16[8,5376]{1,0:T(8,128)(2,1)S(1)} %get-tuple-element.84), channel_id=1, source_target_pairs={{0,12},{1,13},{2,14},{3,15},{4,8},{5,9},{6,10},{7,11},{8,4},{9,5},... | collective-permute-start | bytes 258056 | tf_op jit(solution)/shard_map/ppermute | solution.py:34
  86.5 4.2 %collective-permute-done.18 = bf16[8,5376]{1,0:T(8,128)(2,1)S(1)} collective-permute-done((bf16[8,5376]{1,0:T(8,128)(2,1)S(1)}, bf16[8,5376]{1,0:T(8,128)(2,1)S(1)}, u32[]{:S(2)}, u32[]{:S(2)}) %collective-permute-start.18) | collective-permute-done | bytes 86048 | tf_op jit(solution)/shard_map/ppermute | solution.py:34
  (72 shorter events, 11.6 us)
Async XLA Ops:
  1.7 9.9 %collective-permute-start = (bf16[8,5632]{1,0:T(8,128)(2,1)}, bf16[8,5632]{1,0:T(8,128)(2,1)S(1)}, u32[]{:S(2)}, u32[]{:S(2)}) collective-permute-start(bf16[8,5632]{1,0:T(8,128)(2,1)} %get-tuple-element.41), channel_id=1, source_target_pairs={{0,8},{1,9},{2,10},{3,11},{4,12},{5,13},{6,14},{7,15},{8,0},{9,1},... | collective-permute-start | bytes 270344 | tf_op jit(solution)/shard_map/ppermute | solution.py:34
  5.8 5.8 %collective-permute-start.1 = (bf16[8,5632]{1,0:T(8,128)(2,1)}, bf16[8,5632]{1,0:T(8,128)(2,1)S(1)}, u32[]{:S(2)}, u32[]{:S(2)}) collective-permute-start(bf16[8,5632]{1,0:T(8,128)(2,1)} %get-tuple-element.41), channel_id=1, source_target_pairs={{0,4},{1,5},{2,6},{3,7},{4,0},{5,1},{6,2},{7,3},{8,12},{9,13},{10,... | collective-permute-start | bytes 270344 | tf_op jit(solution)/shard_map/ppermute | solution.py:34
  7.4 6.6 %collective-permute-start.2 = (bf16[8,5632]{1,0:T(8,128)(2,1)}, bf16[8,5632]{1,0:T(8,128)(2,1)S(1)}, u32[]{:S(2)}, u32[]{:S(2)}) collective-permute-start(bf16[8,5632]{1,0:T(8,128)(2,1)} %get-tuple-element.41), channel_id=1, source_target_pairs={{0,12},{1,13},{2,14},{3,15},{4,8},{5,9},{6,10},{7,11},{8,4},{9,5},... | collective-permute-start | bytes 270344 | tf_op jit(solution)/shard_map/ppermute | solution.py:34
  7.4 4.2 %collective-permute-start.3 = (bf16[8,2560]{1,0:T(8,128)(2,1)}, bf16[8,2560]{1,0:T(8,128)(2,1)S(1)}, u32[]{:S(2)}, u32[]{:S(2)}) collective-permute-start(bf16[8,2560]{1,0:T(8,128)(2,1)} %get-tuple-element.42), channel_id=1, source_target_pairs={{0,2},{1,3},{2,0},{3,1},{4,6},{5,7},{6,4},{7,5},{8,10},{9,11},{10,... | collective-permute-start | bytes 122888 | tf_op jit(solution)/shard_map/ppermute | solution.py:34
  14.1 11.3 %collective-permute-start.4 = (bf16[32,5632]{1,0:T(8,128)(2,1)S(1)}, bf16[32,5632]{1,0:T(8,128)(2,1)S(1)}, u32[]{:S(2)}, u32[]{:S(2)}) collective-permute-start(bf16[32,5632]{1,0:T(8,128)(2,1)S(1)} %pad_maximum_fusion.1.refs_0_), channel_id=1, source_target_pairs={{0,2},{1,3},{2,0},{3,1},{4,6},{5,7},{6,4},{7,5},{8,10},{9,11},{10,... | collective-permute-start | bytes 1081352 | tf_op jit(solution)/shard_map/ppermute | solution.py:34
  15.6 8.4 %collective-permute-start.5 = (bf16[16,2560]{1,0:T(8,128)(2,1)S(1)}, bf16[16,2560]{1,0:T(8,128)(2,1)S(1)}, u32[]{:S(2)}, u32[]{:S(2)}) collective-permute-start(bf16[16,2560]{1,0:T(8,128)(2,1)S(1)} %pad_maximum_fusion.2.refs_0_), channel_id=1, source_target_pairs={{0,8},{1,9},{2,10},{3,11},{4,12},{5,13},{6,14},{7,15},{8,0},{9,1},... | collective-permute-start | bytes 245768 | tf_op jit(solution)/shard_map/ppermute | solution.py:34
  18.7 6.7 %collective-permute-start.6 = (bf16[16,2560]{1,0:T(8,128)(2,1)S(1)}, bf16[16,2560]{1,0:T(8,128)(2,1)S(1)}, u32[]{:S(2)}, u32[]{:S(2)}) collective-permute-start(bf16[16,2560]{1,0:T(8,128)(2,1)S(1)} %pad_maximum_fusion.2.refs_0_), channel_id=1, source_target_pairs={{0,4},{1,5},{2,6},{3,7},{4,0},{5,1},{6,2},{7,3},{8,12},{9,13},{10,... | collective-permute-start | bytes 245768 | tf_op jit(solution)/shard_map/ppermute | solution.py:34
  18.7 6.7 %collective-permute-start.7 = (bf16[16,2560]{1,0:T(8,128)(2,1)S(1)}, bf16[16,2560]{1,0:T(8,128)(2,1)S(1)}, u32[]{:S(2)}, u32[]{:S(2)}) collective-permute-start(bf16[16,2560]{1,0:T(8,128)(2,1)S(1)} %pad_maximum_fusion.2.refs_0_), channel_id=1, source_target_pairs={{0,12},{1,13},{2,14},{3,15},{4,8},{5,9},{6,10},{7,11},{8,4},{9,5},... | collective-permute-start | bytes 245768 | tf_op jit(solution)/shard_map/ppermute | solution.py:34
  20.2 6.2 %collective-permute-start.12 = (bf16[32,5632]{1,0:T(8,128)(2,1)S(1)}, bf16[32,5632]{1,0:T(8,128)(2,1)S(1)}, u32[]{:S(2)}, u32[]{:S(2)}) collective-permute-start(bf16[32,5632]{1,0:T(8,128)(2,1)S(1)} %pad_maximum_fusion.1.refs_0_), channel_id=1, source_target_pairs={{0,1},{1,0},{2,3},{3,2},{4,5},{5,4},{6,7},{7,6},{8,9},{9,8},{10,11... | collective-permute-start | bytes 1081352 | tf_op jit(solution)/shard_map/ppermute | solution.py:34
  25.4 3.0 %collective-permute-start.10 = (bf16[16,2560]{1,0:T(8,128)(2,1)S(1)}, bf16[16,2560]{1,0:T(8,128)(2,1)S(1)}, u32[]{:S(2)}, u32[]{:S(2)}) collective-permute-start(bf16[16,2560]{1,0:T(8,128)(2,1)S(1)} %collective-permute-done.6.refs_2_), channel_id=1, source_target_pairs={{0,1},{1,0},{2,3},{3,2},{4,5},{5,4},{6,7},{7,6},{8,9},{9,8},{10,11... | collective-permute-start | bytes 245768 | tf_op jit(solution)/shard_map/ppermute | solution.py:34
  25.9 2.5 %collective-permute-start.11 = (bf16[16,2560]{1,0:T(8,128)(2,1)S(1)}, bf16[16,2560]{1,0:T(8,128)(2,1)S(1)}, u32[]{:S(2)}, u32[]{:S(2)}) collective-permute-start(bf16[16,2560]{1,0:T(8,128)(2,1)S(1)} %collective-permute-done.7.refs_3_), channel_id=1, source_target_pairs={{0,1},{1,0},{2,3},{3,2},{4,5},{5,4},{6,7},{7,6},{8,9},{9,8},{10,11... | collective-permute-start | bytes 245768 | tf_op jit(solution)/shard_map/ppermute | solution.py:34
  26.0 2.4 %collective-permute-start.8 = (bf16[16,2560]{1,0:T(8,128)(2,1)S(1)}, bf16[16,2560]{1,0:T(8,128)(2,1)S(1)}, u32[]{:S(2)}, u32[]{:S(2)}) collective-permute-start(bf16[16,2560]{1,0:T(8,128)(2,1)S(1)} %pad_maximum_fusion.2.refs_0_), channel_id=1, source_target_pairs={{0,1},{1,0},{2,3},{3,2},{4,5},{5,4},{6,7},{7,6},{8,9},{9,8},{10,11... | collective-permute-start | bytes 245768 | tf_op jit(solution)/shard_map/ppermute | solution.py:34
  26.4 2.0 %collective-permute-start.9 = (bf16[16,2560]{1,0:T(8,128)(2,1)S(1)}, bf16[16,2560]{1,0:T(8,128)(2,1)S(1)}, u32[]{:S(2)}, u32[]{:S(2)}) collective-permute-start(bf16[16,2560]{1,0:T(8,128)(2,1)S(1)} %collective-permute-done.5.refs_1_), channel_id=1, source_target_pairs={{0,1},{1,0},{2,3},{3,2},{4,5},{5,4},{6,7},{7,6},{8,9},{9,8},{10,11... | collective-permute-start | bytes 245768 | tf_op jit(solution)/shard_map/ppermute | solution.py:34
  30.0 15.5 %all-to-all-start = ((bf16[16,16,640]{2,1,0:T(8,128)(2,1)}), bf16[16,16,640]{2,1,0:T(8,128)(2,1)S(1)}, u32[]{:S(2)}, u32[]{:S(2)}) async-start(bf16[16,16,640]{2,1,0:T(8,128)(2,1)} %bitcast.4), calls=%async_computation | async-start | bytes 655360 | tf_op jit(solution)/shard_map/all_to_all | solution.py:667
  51.7 13.6 %all-to-all-start.1 = ((bf16[16,16,512]{2,1,0:T(8,128)(2,1)}), bf16[16,16,512]{2,1,0:T(8,128)(2,1)S(1)}, u32[]{:S(2)}, u32[]{:S(2)}) async-start(bf16[16,16,512]{2,1,0:T(8,128)(2,1)} %attend.1), calls=%async_computation.1 | async-start | bytes 524288 | tf_op jit(solution)/shard_map/all_to_all | solution.py:680
  68.5 2.2 %collective-permute-start.14 = (bf16[64,5376]{1,0:T(8,128)(2,1)S(1)}, bf16[64,5376]{1,0:T(8,128)(2,1)S(1)}, u32[]{:S(2)}, u32[]{:S(2)}) collective-permute-start(bf16[64,5376]{1,0:T(8,128)(2,1)S(1)} %get-tuple-element.69), channel_id=1, source_target_pairs={{0,1},{1,0},{2,3},{3,2},{4,5},{5,4},{6,7},{7,6},{8,9},{9,8},{10,11... | collective-permute-start | bytes 2064392 | tf_op jit(solution)/shard_map/ppermute | solution.py:34
  71.1 10.3 %collective-permute-start.15 = (bf16[32,5376]{1,0:T(8,128)(2,1)S(1)}, bf16[32,5376]{1,0:T(8,128)(2,1)S(1)}, u32[]{:S(2)}, u32[]{:S(2)}) collective-permute-start(bf16[32,5376]{1,0:T(8,128)(2,1)S(1)} %slice.87), channel_id=1, source_target_pairs={{0,2},{1,3},{2,0},{3,1},{4,6},{5,7},{6,4},{7,5},{8,10},{9,11},{10,... | collective-permute-start | bytes 1032200 | tf_op jit(solution)/shard_map/ppermute | solution.py:34
  72.8 8.7 %collective-permute-start.17 = (bf16[16,2816]{1,0:T(8,128)(2,1)S(1)}, bf16[16,2816]{1,0:T(8,128)(2,1)S(1)}, u32[]{:S(2)}, u32[]{:S(2)}) collective-permute-start(bf16[16,2816]{1,0:T(8,128)(2,1)S(1)} %get-tuple-element.81), channel_id=1, source_target_pairs={{0,8},{1,9},{2,10},{3,11},{4,12},{5,13},{6,14},{7,15},{8,0},{9,1},... | collective-permute-start | bytes 270344 | tf_op jit(solution)/shard_map/ppermute | solution.py:34
  73.8 12.2 %collective-permute-start.21 = (bf16[16,2816]{1,0:T(8,128)(2,1)S(1)}, bf16[16,2816]{1,0:T(8,128)(2,1)S(1)}, u32[]{:S(2)}, u32[]{:S(2)}) collective-permute-start(bf16[16,2816]{1,0:T(8,128)(2,1)S(1)} %get-tuple-element.83), channel_id=1, source_target_pairs={{0,4},{1,5},{2,6},{3,7},{4,0},{5,1},{6,2},{7,3},{8,12},{9,13},{10,... | collective-permute-start | bytes 270344 | tf_op jit(solution)/shard_map/ppermute | solution.py:34
  74.4 11.7 %collective-permute-start.22 = (bf16[16,2816]{1,0:T(8,128)(2,1)S(1)}, bf16[16,2816]{1,0:T(8,128)(2,1)S(1)}, u32[]{:S(2)}, u32[]{:S(2)}) collective-permute-start(bf16[16,2816]{1,0:T(8,128)(2,1)S(1)} %get-tuple-element.82), channel_id=1, source_target_pairs={{0,12},{1,13},{2,14},{3,15},{4,8},{5,9},{6,10},{7,11},{8,4},{9,5},... | collective-permute-start | bytes 270344 | tf_op jit(solution)/shard_map/ppermute | solution.py:34
  81.6 9.0 %collective-permute-start.18 = (bf16[8,5376]{1,0:T(8,128)(2,1)S(1)}, bf16[8,5376]{1,0:T(8,128)(2,1)S(1)}, u32[]{:S(2)}, u32[]{:S(2)}) collective-permute-start(bf16[8,5376]{1,0:T(8,128)(2,1)S(1)} %get-tuple-element.86), channel_id=1, source_target_pairs={{0,8},{1,9},{2,10},{3,11},{4,12},{5,13},{6,14},{7,15},{8,0},{9,1},... | collective-permute-start | bytes 258056 | tf_op jit(solution)/shard_map/ppermute | solution.py:34
  82.6 8.0 %collective-permute-start.19 = (bf16[8,5376]{1,0:T(8,128)(2,1)S(1)}, bf16[8,5376]{1,0:T(8,128)(2,1)S(1)}, u32[]{:S(2)}, u32[]{:S(2)}) collective-permute-start(bf16[8,5376]{1,0:T(8,128)(2,1)S(1)} %get-tuple-element.85), channel_id=1, source_target_pairs={{0,4},{1,5},{2,6},{3,7},{4,0},{5,1},{6,2},{7,3},{8,12},{9,13},{10,... | collective-permute-start | bytes 258056 | tf_op jit(solution)/shard_map/ppermute | solution.py:34
  83.4 7.2 %collective-permute-start.20 = (bf16[8,5376]{1,0:T(8,128)(2,1)S(1)}, bf16[8,5376]{1,0:T(8,128)(2,1)S(1)}, u32[]{:S(2)}, u32[]{:S(2)}) collective-permute-start(bf16[8,5376]{1,0:T(8,128)(2,1)S(1)} %get-tuple-element.84), channel_id=1, source_target_pairs={{0,12},{1,13},{2,14},{3,15},{4,8},{5,9},{6,10},{7,11},{8,4},{9,5},... | collective-permute-start | bytes 258056 | tf_op jit(solution)/shard_map/ppermute | solution.py:34
  86.1 4.6 %collective-permute-start.23 = (bf16[8,2816]{1,0:T(8,128)(2,1)S(1)}, bf16[8,2816]{1,0:T(8,128)(2,1)S(1)}, u32[]{:S(2)}, u32[]{:S(2)}) collective-permute-start(bf16[8,2816]{1,0:T(8,128)(2,1)S(1)} %slice.88), channel_id=1, source_target_pairs={{0,2},{1,3},{2,0},{3,1},{4,6},{5,7},{6,4},{7,5},{8,10},{9,11},{10,... | collective-permute-start | bytes 135176 | tf_op jit(solution)/shard_map/ppermute | solution.py:34
  (8 other events, 43.0 us)

commit v22 on v21

--- a/solution.py
+++ b/solution.py
@@ -454,6 +454,7 @@
             pltpu.make_async_copy(pool.at[part], on_chip.at[part], sem).start()
 
     fetch_pool(key_pages, key_pool, sems.at[0])
+    fetch_pool(value_pages, value_pool, sems.at[1])
 
     def held(pool, slot, columns):
         return [pool[table[slot, j], :, columns] for j in range(pages)]
@@ -505,7 +506,6 @@
             query_tile[p, b, :HEAD] = jnp.where(first, turned, none)
             query_tile[p, b, HEAD:] = jnp.where(first, none, turned)
 
-    fetch_pool(value_pages, value_pool, sems.at[1])
     pltpu.make_async_copy(key_pool, key_pool, sems.at[0]).wait()
     for p in range(pairs):
         columns_p = slice(p * 2 * HEAD, (p + 1) * 2 * HEAD)

time: 91.8 us -> 91.8 us (level)
  no operation moved by 1% of the time
where the time goes in v22:
time: 91.8 us; the launch traced here: 91.4 us
  waiting for transfers between devices  35.6 us (39%)
  starting transfers between devices  32.5 us (35%)
  Pallas kernels  19.3 us (21%)
  other arithmetic  3.29 us (4%)
    ppermute x24, starting transfers between devices, send(): return lax.ppermute(x, AXES, pairs)  24.6 us
    ppermute x24, waiting for transfers between devices, send(): return lax.ppermute(x, AXES, pairs)  16.9 us
    all_to_all x1, waiting for transfers between devices, on_device(): lax.all_to_all(outbound, AXES, split_axis=0, concat_axis=0, tiled=True)  10.4 us
    all_to_all x1, waiting for transfers between devices, on_device(): lax.all_to_all(attended, AXES, split_axis=0, concat_axis=0, tiled=True)  8.25 us
    pallas_call x1, Pallas kernels, attend(): pl.pallas_call(functools.partial(attend_kernel, per_query, per_key), in_s...  6.21 us
    pallas_call x2, Pallas kernels, fetch(): pl.pallas_call(functools.partial(fetch_kernel, starts), in_specs=[pl.Bloc...  5.14 us
    all_to_all x1, starting transfers between devices, on_device(): lax.all_to_all(outbound, AXES, split_axis=0, concat_axis=0, tiled=True)  4.41 us
    all_to_all x1, starting transfers between devices, on_device(): lax.all_to_all(attended, AXES, split_axis=0, concat_axis=0, tiled=True)  3.54 us
  transfers between devices with their start and end apart: 26, of which 11 were waited for; matrix products, arithmetic and copies ran while one was open for 3% of the time, Pallas kernels for 7%

profile of v22, /device:TPU:0, one launch (start us, length us, event | category | flops | bytes accessed | tf_op | source)
XLA Modules:
  0.0 91.4 jit_solution(242917396723009535)
XLA Ops:
  0.0 1.7 %norm.1 = (bf16[8,5632]{1,0:T(8,128)(2,1)}, bf16[8,2560]{1,0:T(8,128)(2,1)}) custom-call(bf16[8,8192]{1,0:T(8,128)(2,1)} %x.1, f32[1,8192]{1,0:T(1,128)} %bitcast.21), custom_call_target="tpu_custom_call" | custom-call | tf_op jit(solution)/shard_map/norm/pallas_call | solution.py:229
  1.7 4.1 %collective-permute-start = (bf16[8,5632]{1,0:T(8,128)(2,1)}, bf16[8,5632]{1,0:T(8,128)(2,1)S(1)}, u32[]{:S(2)}, u32[]{:S(2)}) collective-permute-start(bf16[8,5632]{1,0:T(8,128)(2,1)} %get-tuple-element.41), channel_id=1, source_target_pairs={{0,8},{1,9},{2,10},{3,11},{4,12},{5,13},{6,14},{7,15},{8,0},{9,1},... | collective-permute-start | bytes 270344 | tf_op jit(solution)/shard_map/ppermute | solution.py:34
  5.8 1.6 %collective-permute-start.1 = (bf16[8,5632]{1,0:T(8,128)(2,1)}, bf16[8,5632]{1,0:T(8,128)(2,1)S(1)}, u32[]{:S(2)}, u32[]{:S(2)}) collective-permute-start(bf16[8,5632]{1,0:T(8,128)(2,1)} %get-tuple-element.41), channel_id=1, source_target_pairs={{0,4},{1,5},{2,6},{3,7},{4,0},{5,1},{6,2},{7,3},{8,12},{9,13},{10,... | collective-permute-start | bytes 270344 | tf_op jit(solution)/shard_map/ppermute | solution.py:34
  7.4 1.7 %collective-permute-start.3 = (bf16[8,2560]{1,0:T(8,128)(2,1)}, bf16[8,2560]{1,0:T(8,128)(2,1)S(1)}, u32[]{:S(2)}, u32[]{:S(2)}) collective-permute-start(bf16[8,2560]{1,0:T(8,128)(2,1)} %get-tuple-element.42), channel_id=1, source_target_pairs={{0,2},{1,3},{2,0},{3,1},{4,6},{5,7},{6,4},{7,5},{8,10},{9,11},{10,... | collective-permute-start | bytes 122888 | tf_op jit(solution)/shard_map/ppermute | solution.py:34
  9.2 1.8 %pad_maximum_fusion.refs_5_.refs_9_ = bf16[128,8192]{1,0:T(8,128)(2,1)S(1)} fusion(bf16[64,8192]{1,0:T(8,128)(2,1)} %bitcast.19, bf16[64,8192]{1,0:T(8,128)(2,1)} %bitcast.20), kind=kLoop, calls=%fused_computation | loop fusion | flops 4194304 | bytes 4194304 | tf_op jit(solution)/shard_map/concatenate | solution.py:645
  11.7 2.3 %collective-permute-done.2 = bf16[8,5632]{1,0:T(8,128)(2,1)S(1)} collective-permute-done((bf16[8,5632]{1,0:T(8,128)(2,1)}, bf16[8,5632]{1,0:T(8,128)(2,1)S(1)}, u32[]{:S(2)}, u32[]{:S(2)}) %collective-permute-start.2) | collective-permute-done | bytes 90144 | tf_op jit(solution)/shard_map/ppermute | solution.py:34
  14.1 1.6 %collective-permute-start.4 = (bf16[32,5632]{1,0:T(8,128)(2,1)S(1)}, bf16[32,5632]{1,0:T(8,128)(2,1)S(1)}, u32[]{:S(2)}, u32[]{:S(2)}) collective-permute-start(bf16[32,5632]{1,0:T(8,128)(2,1)S(1)} %pad_maximum_fusion.1.refs_0_), channel_id=1, source_target_pairs={{0,2},{1,3},{2,0},{3,1},{4,6},{5,7},{6,4},{7,5},{8,10},{9,11},{10,... | collective-permute-start | bytes 1081352 | tf_op jit(solution)/shard_map/ppermute | solution.py:34
  15.6 3.1 %collective-permute-start.5 = (bf16[16,2560]{1,0:T(8,128)(2,1)S(1)}, bf16[16,2560]{1,0:T(8,128)(2,1)S(1)}, u32[]{:S(2)}, u32[]{:S(2)}) collective-permute-start(bf16[16,2560]{1,0:T(8,128)(2,1)S(1)} %pad_maximum_fusion.2.refs_0_), channel_id=1, source_target_pairs={{0,8},{1,9},{2,10},{3,11},{4,12},{5,13},{6,14},{7,15},{8,0},{9,1},... | collective-permute-start | bytes 245768 | tf_op jit(solution)/shard_map/ppermute | solution.py:34
  18.7 1.5 %collective-permute-start.7 = (bf16[16,2560]{1,0:T(8,128)(2,1)S(1)}, bf16[16,2560]{1,0:T(8,128)(2,1)S(1)}, u32[]{:S(2)}, u32[]{:S(2)}) collective-permute-start(bf16[16,2560]{1,0:T(8,128)(2,1)S(1)} %pad_maximum_fusion.2.refs_0_), channel_id=1, source_target_pairs={{0,12},{1,13},{2,14},{3,15},{4,8},{5,9},{6,10},{7,11},{8,4},{9,5},... | collective-permute-start | bytes 245768 | tf_op jit(solution)/shard_map/ppermute | solution.py:34
  20.2 3.4 %fetch.2.refs_4_.refs_8_ = bf16[8192,512]{1,0:T(8,128)(2,1)S(1)} custom-call(bf16[8192,512]{1,0:T(8,128)(2,1)} %refs_0_), custom_call_target="tpu_custom_call" | custom-call | bytes 16777216 | tf_op jit(solution)/shard_map/fetch/pallas_call | solution.py:319
  24.0 1.4 %collective-permute-done.6.refs_2_ = bf16[16,2560]{1,0:T(8,128)(2,1)S(1)} collective-permute-done((bf16[16,2560]{1,0:T(8,128)(2,1)S(1)}, bf16[16,2560]{1,0:T(8,128)(2,1)S(1)}, u32[]{:S(2)}, u32[]{:S(2)}) %collective-permute-start.6) | collective-permute-done | bytes 81952 | tf_op jit(solution)/shard_map/ppermute | solution.py:34
  28.4 1.6 %project.3 = bf16[256,640]{1,0:T(8,128)(2,1)} custom-call(bf16[16,2560]{1,0:T(8,128)(2,1)S(1)} %pad_maximum_fusion.2.refs_0_, bf16[16,2560]{1,0:T(8,128)(2,1)S(1)} %collective-permute-done.5.refs_1_, bf16[16,2560]{1,0:T(8,128)(2,1)S(1)} %collective-permute-done.6.refs_2_, bf16[16,2560]{1,0:T(8,128)(2,1)S(1)} %collective-permute-done.7.refs_3_, ...), custom_call_target="tpu_custom_call" | custom-call | flops 419430400 | bytes 3276800 | tf_op jit(solution)/shard_map/project/pallas_call | solution.py:397
  30.0 4.4 %all-to-all-start = ((bf16[16,16,640]{2,1,0:T(8,128)(2,1)}), bf16[16,16,640]{2,1,0:T(8,128)(2,1)S(1)}, u32[]{:S(2)}, u32[]{:S(2)}) async-start(bf16[16,16,640]{2,1,0:T(8,128)(2,1)} %bitcast.4), calls=%async_computation | async-start | bytes 655360 | tf_op jit(solution)/shard_map/all_to_all | solution.py:667
  35.1 10.4 %all-to-all-done.inbound = bf16[16,16,640]{2,1,0:T(8,128)(2,1)S(1)} async-done(((bf16[16,16,640]{2,1,0:T(8,128)(2,1)}), bf16[16,16,640]{2,1,0:T(8,128)(2,1)S(1)}, u32[]{:S(2)}, u32[]{:S(2)}) %all-to-all-start) | async-done | bytes 327712 | tf_op jit(solution)/shard_map/all_to_all | solution.py:667
  45.5 6.2 %attend.1 = bf16[16,16,512]{2,1,0:T(8,128)(2,1)} custom-call(s32[16,4]{1,0:T(8,128)S(1)} %copy.15.table, s32[2,1,128]{2,1,0:T(1,128)S(1)} %bitcast.14, bf16[16,16,640]{2,1,0:T(8,128)(2,1)S(1)} %all-to-all-done.inbound, f32[16,128]{1,0:T(8,128)S(1)} %get-tuple-element.90.cosine, f32[16,128]{1,0:T(8,128)S(1)} %get-tuple-element.91.sine, ...), custom_call_target="tpu_custom_call" | custom-call | flops 134217728 | bytes 8388608 | tf_op jit(solution)/shard_map/attend/pallas_call | solution.py:583
  51.7 3.5 %all-to-all-start.1 = ((bf16[16,16,512]{2,1,0:T(8,128)(2,1)}), bf16[16,16,512]{2,1,0:T(8,128)(2,1)S(1)}, u32[]{:S(2)}, u32[]{:S(2)}) async-start(bf16[16,16,512]{2,1,0:T(8,128)(2,1)} %attend.1), calls=%async_computation.1 | async-start | bytes 524288 | tf_op jit(solution)/shard_map/all_to_all | solution.py:680
  55.3 1.8 %fetch.3.w_front = bf16[512,2560]{1,0:T(8,128)(2,1)S(1)} custom-call(bf16[512,8192]{1,0:T(8,128)(2,1)} %w_out.1), custom_call_target="tpu_custom_call" | custom-call | bytes 5242880 | tf_op jit(solution)/shard_map/fetch/pallas_call | solution.py:319
  57.1 8.2 %all-to-all-done.1 = bf16[16,16,512]{2,1,0:T(8,128)(2,1)S(1)} async-done(((bf16[16,16,512]{2,1,0:T(8,128)(2,1)}), bf16[16,16,512]{2,1,0:T(8,128)(2,1)S(1)}, u32[]{:S(2)}, u32[]{:S(2)}) %all-to-all-start.1) | async-done | bytes 262176 | tf_op jit(solution)/shard_map/all_to_all | solution.py:680
  65.3 3.2 %product.1 = (bf16[64,5376]{1,0:T(8,128)(2,1)S(1)}, f32[64,5376]{1,0:T(8,128)S(1)}, bf16[64,2816]{1,0:T(8,128)(2,1)S(1)}, f32[64,2816]{1,0:T(8,128)S(1)}) custom-call(s32[1,128]{1,0:T(1,128)S(1)} %get-tuple-element.50.place_a, s32[1,128]{1,0:T(1,128)S(1)} %get-tuple-element.51.place_b, bf16[256,512]{1,0:T(8,128)(2,1)S(1)} %bitcast.13, ...), custom_call_target="tpu_custom_call" | custom-call | flops 1073741824 | bytes 8388608 | tf_op jit(solution)/shard_map/product/pallas_call | solution.py:155
  68.6 2.1 %collective-permute-done.14 = bf16[64,5376]{1,0:T(8,128)(2,1)S(1)} collective-permute-done((bf16[64,5376]{1,0:T(8,128)(2,1)S(1)}, bf16[64,5376]{1,0:T(8,128)(2,1)S(1)}, u32[]{:S(2)}, u32[]{:S(2)}) %collective-permute-start.14) | collective-permute-done | bytes 688160 | tf_op jit(solution)/shard_map/ppermute | solution.py:34
  74.4 2.9 %collective-permute-start.22 = (bf16[16,2816]{1,0:T(8,128)(2,1)S(1)}, bf16[16,2816]{1,0:T(8,128)(2,1)S(1)}, u32[]{:S(2)}, u32[]{:S(2)}) collective-permute-start(bf16[16,2816]{1,0:T(8,128)(2,1)S(1)} %get-tuple-element.82), channel_id=1, source_target_pairs={{0,12},{1,13},{2,14},{3,15},{4,8},{5,9},{6,10},{7,11},{8,4},{9,5},... | collective-permute-start | bytes 270344 | tf_op jit(solution)/shard_map/ppermute | solution.py:34
  77.2 4.2 %collective-permute-done.15 = bf16[32,5376]{1,0:T(8,128)(2,1)S(1)} collective-permute-done((bf16[32,5376]{1,0:T(8,128)(2,1)S(1)}, bf16[32,5376]{1,0:T(8,128)(2,1)S(1)}, u32[]{:S(2)}, u32[]{:S(2)}) %collective-permute-start.15) | collective-permute-done | bytes 344096 | tf_op jit(solution)/shard_map/ppermute | solution.py:34
  83.4 2.6 %collective-permute-start.20 = (bf16[8,5376]{1,0:T(8,128)(2,1)S(1)}, bf16[8,5376]{1,0:T(8,128)(2,1)S(1)}, u32[]{:S(2)}, u32[]{:S(2)}) collective-permute-start(bf16[8,5376]{1,0:T(8,128)(2,1)S(1)} %get-tuple-element.84), channel_id=1, source_target_pairs={{0,12},{1,13},{2,14},{3,15},{4,8},{5,9},{6,10},{7,11},{8,4},{9,5},... | collective-permute-start | bytes 258056 | tf_op jit(solution)/shard_map/ppermute | solution.py:34
  86.5 4.2 %collective-permute-done.18 = bf16[8,5376]{1,0:T(8,128)(2,1)S(1)} collective-permute-done((bf16[8,5376]{1,0:T(8,128)(2,1)S(1)}, bf16[8,5376]{1,0:T(8,128)(2,1)S(1)}, u32[]{:S(2)}, u32[]{:S(2)}) %collective-permute-start.18) | collective-permute-done | bytes 86048 | tf_op jit(solution)/shard_map/ppermute | solution.py:34
  (72 shorter events, 11.6 us)
Async XLA Ops:
  1.7 9.9 %collective-permute-start = (bf16[8,5632]{1,0:T(8,128)(2,1)}, bf16[8,5632]{1,0:T(8,128)(2,1)S(1)}, u32[]{:S(2)}, u32[]{:S(2)}) collective-permute-start(bf16[8,5632]{1,0:T(8,128)(2,1)} %get-tuple-element.41), channel_id=1, source_target_pairs={{0,8},{1,9},{2,10},{3,11},{4,12},{5,13},{6,14},{7,15},{8,0},{9,1},... | collective-permute-start | bytes 270344 | tf_op jit(solution)/shard_map/ppermute | solution.py:34
  5.8 5.8 %collective-permute-start.1 = (bf16[8,5632]{1,0:T(8,128)(2,1)}, bf16[8,5632]{1,0:T(8,128)(2,1)S(1)}, u32[]{:S(2)}, u32[]{:S(2)}) collective-permute-start(bf16[8,5632]{1,0:T(8,128)(2,1)} %get-tuple-element.41), channel_id=1, source_target_pairs={{0,4},{1,5},{2,6},{3,7},{4,0},{5,1},{6,2},{7,3},{8,12},{9,13},{10,... | collective-permute-start | bytes 270344 | tf_op jit(solution)/shard_map/ppermute | solution.py:34
  7.4 6.6 %collective-permute-start.2 = (bf16[8,5632]{1,0:T(8,128)(2,1)}, bf16[8,5632]{1,0:T(8,128)(2,1)S(1)}, u32[]{:S(2)}, u32[]{:S(2)}) collective-permute-start(bf16[8,5632]{1,0:T(8,128)(2,1)} %get-tuple-element.41), channel_id=1, source_target_pairs={{0,12},{1,13},{2,14},{3,15},{4,8},{5,9},{6,10},{7,11},{8,4},{9,5},... | collective-permute-start | bytes 270344 | tf_op jit(solution)/shard_map/ppermute | solution.py:34
  7.4 4.2 %collective-permute-start.3 = (bf16[8,2560]{1,0:T(8,128)(2,1)}, bf16[8,2560]{1,0:T(8,128)(2,1)S(1)}, u32[]{:S(2)}, u32[]{:S(2)}) collective-permute-start(bf16[8,2560]{1,0:T(8,128)(2,1)} %get-tuple-element.42), channel_id=1, source_target_pairs={{0,2},{1,3},{2,0},{3,1},{4,6},{5,7},{6,4},{7,5},{8,10},{9,11},{10,... | collective-permute-start | bytes 122888 | tf_op jit(solution)/shard_map/ppermute | solution.py:34
  14.1 11.3 %collective-permute-start.4 = (bf16[32,5632]{1,0:T(8,128)(2,1)S(1)}, bf16[32,5632]{1,0:T(8,128)(2,1)S(1)}, u32[]{:S(2)}, u32[]{:S(2)}) collective-permute-start(bf16[32,5632]{1,0:T(8,128)(2,1)S(1)} %pad_maximum_fusion.1.refs_0_), channel_id=1, source_target_pairs={{0,2},{1,3},{2,0},{3,1},{4,6},{5,7},{6,4},{7,5},{8,10},{9,11},{10,... | collective-permute-start | bytes 1081352 | tf_op jit(solution)/shard_map/ppermute | solution.py:34
  15.6 8.4 %collective-permute-start.5 = (bf16[16,2560]{1,0:T(8,128)(2,1)S(1)}, bf16[16,2560]{1,0:T(8,128)(2,1)S(1)}, u32[]{:S(2)}, u32[]{:S(2)}) collective-permute-start(bf16[16,2560]{1,0:T(8,128)(2,1)S(1)} %pad_maximum_fusion.2.refs_0_), channel_id=1, source_target_pairs={{0,8},{1,9},{2,10},{3,11},{4,12},{5,13},{6,14},{7,15},{8,0},{9,1},... | collective-permute-start | bytes 245768 | tf_op jit(solution)/shard_map/ppermute | solution.py:34
  18.7 6.7 %collective-permute-start.6 = (bf16[16,2560]{1,0:T(8,128)(2,1)S(1)}, bf16[16,2560]{1,0:T(8,128)(2,1)S(1)}, u32[]{:S(2)}, u32[]{:S(2)}) collective-permute-start(bf16[16,2560]{1,0:T(8,128)(2,1)S(1)} %pad_maximum_fusion.2.refs_0_), channel_id=1, source_target_pairs={{0,4},{1,5},{2,6},{3,7},{4,0},{5,1},{6,2},{7,3},{8,12},{9,13},{10,... | collective-permute-start | bytes 245768 | tf_op jit(solution)/shard_map/ppermute | solution.py:34
  18.7 6.7 %collective-permute-start.7 = (bf16[16,2560]{1,0:T(8,128)(2,1)S(1)}, bf16[16,2560]{1,0:T(8,128)(2,1)S(1)}, u32[]{:S(2)}, u32[]{:S(2)}) collective-permute-start(bf16[16,2560]{1,0:T(8,128)(2,1)S(1)} %pad_maximum_fusion.2.refs_0_), channel_id=1, source_target_pairs={{0,12},{1,13},{2,14},{3,15},{4,8},{5,9},{6,10},{7,11},{8,4},{9,5},... | collective-permute-start | bytes 245768 | tf_op jit(solution)/shard_map/ppermute | solution.py:34
  20.2 6.2 %collective-permute-start.12 = (bf16[32,5632]{1,0:T(8,128)(2,1)S(1)}, bf16[32,5632]{1,0:T(8,128)(2,1)S(1)}, u32[]{:S(2)}, u32[]{:S(2)}) collective-permute-start(bf16[32,5632]{1,0:T(8,128)(2,1)S(1)} %pad_maximum_fusion.1.refs_0_), channel_id=1, source_target_pairs={{0,1},{1,0},{2,3},{3,2},{4,5},{5,4},{6,7},{7,6},{8,9},{9,8},{10,11... | collective-permute-start | bytes 1081352 | tf_op jit(solution)/shard_map/ppermute | solution.py:34
  25.4 3.0 %collective-permute-start.10 = (bf16[16,2560]{1,0:T(8,128)(2,1)S(1)}, bf16[16,2560]{1,0:T(8,128)(2,1)S(1)}, u32[]{:S(2)}, u32[]{:S(2)}) collective-permute-start(bf16[16,2560]{1,0:T(8,128)(2,1)S(1)} %collective-permute-done.6.refs_2_), channel_id=1, source_target_pairs={{0,1},{1,0},{2,3},{3,2},{4,5},{5,4},{6,7},{7,6},{8,9},{9,8},{10,11... | collective-permute-start | bytes 245768 | tf_op jit(solution)/shard_map/ppermute | solution.py:34
  25.9 2.5 %collective-permute-start.11 = (bf16[16,2560]{1,0:T(8,128)(2,1)S(1)}, bf16[16,2560]{1,0:T(8,128)(2,1)S(1)}, u32[]{:S(2)}, u32[]{:S(2)}) collective-permute-start(bf16[16,2560]{1,0:T(8,128)(2,1)S(1)} %collective-permute-done.7.refs_3_), channel_id=1, source_target_pairs={{0,1},{1,0},{2,3},{3,2},{4,5},{5,4},{6,7},{7,6},{8,9},{9,8},{10,11... | collective-permute-start | bytes 245768 | tf_op jit(solution)/shard_map/ppermute | solution.py:34
  26.0 2.4 %collective-permute-start.8 = (bf16[16,2560]{1,0:T(8,128)(2,1)S(1)}, bf16[16,2560]{1,0:T(8,128)(2,1)S(1)}, u32[]{:S(2)}, u32[]{:S(2)}) collective-permute-start(bf16[16,2560]{1,0:T(8,128)(2,1)S(1)} %pad_maximum_fusion.2.refs_0_), channel_id=1, source_target_pairs={{0,1},{1,0},{2,3},{3,2},{4,5},{5,4},{6,7},{7,6},{8,9},{9,8},{10,11... | collective-permute-start | bytes 245768 | tf_op jit(solution)/shard_map/ppermute | solution.py:34
  26.4 2.0 %collective-permute-start.9 = (bf16[16,2560]{1,0:T(8,128)(2,1)S(1)}, bf16[16,2560]{1,0:T(8,128)(2,1)S(1)}, u32[]{:S(2)}, u32[]{:S(2)}) collective-permute-start(bf16[16,2560]{1,0:T(8,128)(2,1)S(1)} %collective-permute-done.5.refs_1_), channel_id=1, source_target_pairs={{0,1},{1,0},{2,3},{3,2},{4,5},{5,4},{6,7},{7,6},{8,9},{9,8},{10,11... | collective-permute-start | bytes 245768 | tf_op jit(solution)/shard_map/ppermute | solution.py:34
  30.0 15.5 %all-to-all-start = ((bf16[16,16,640]{2,1,0:T(8,128)(2,1)}), bf16[16,16,640]{2,1,0:T(8,128)(2,1)S(1)}, u32[]{:S(2)}, u32[]{:S(2)}) async-start(bf16[16,16,640]{2,1,0:T(8,128)(2,1)} %bitcast.4), calls=%async_computation | async-start | bytes 655360 | tf_op jit(solution)/shard_map/all_to_all | solution.py:667
  51.7 13.6 %all-to-all-start.1 = ((bf16[16,16,512]{2,1,0:T(8,128)(2,1)}), bf16[16,16,512]{2,1,0:T(8,128)(2,1)S(1)}, u32[]{:S(2)}, u32[]{:S(2)}) async-start(bf16[16,16,512]{2,1,0:T(8,128)(2,1)} %attend.1), calls=%async_computation.1 | async-start | bytes 524288 | tf_op jit(solution)/shard_map/all_to_all | solution.py:680
  68.5 2.2 %collective-permute-start.14 = (bf16[64,5376]{1,0:T(8,128)(2,1)S(1)}, bf16[64,5376]{1,0:T(8,128)(2,1)S(1)}, u32[]{:S(2)}, u32[]{:S(2)}) collective-permute-start(bf16[64,5376]{1,0:T(8,128)(2,1)S(1)} %get-tuple-element.69), channel_id=1, source_target_pairs={{0,1},{1,0},{2,3},{3,2},{4,5},{5,4},{6,7},{7,6},{8,9},{9,8},{10,11... | collective-permute-start | bytes 2064392 | tf_op jit(solution)/shard_map/ppermute | solution.py:34
  71.1 10.3 %collective-permute-start.15 = (bf16[32,5376]{1,0:T(8,128)(2,1)S(1)}, bf16[32,5376]{1,0:T(8,128)(2,1)S(1)}, u32[]{:S(2)}, u32[]{:S(2)}) collective-permute-start(bf16[32,5376]{1,0:T(8,128)(2,1)S(1)} %slice.87), channel_id=1, source_target_pairs={{0,2},{1,3},{2,0},{3,1},{4,6},{5,7},{6,4},{7,5},{8,10},{9,11},{10,... | collective-permute-start | bytes 1032200 | tf_op jit(solution)/shard_map/ppermute | solution.py:34
  72.8 8.7 %collective-permute-start.17 = (bf16[16,2816]{1,0:T(8,128)(2,1)S(1)}, bf16[16,2816]{1,0:T(8,128)(2,1)S(1)}, u32[]{:S(2)}, u32[]{:S(2)}) collective-permute-start(bf16[16,2816]{1,0:T(8,128)(2,1)S(1)} %get-tuple-element.81), channel_id=1, source_target_pairs={{0,8},{1,9},{2,10},{3,11},{4,12},{5,13},{6,14},{7,15},{8,0},{9,1},... | collective-permute-start | bytes 270344 | tf_op jit(solution)/shard_map/ppermute | solution.py:34
  73.8 12.2 %collective-permute-start.21 = (bf16[16,2816]{1,0:T(8,128)(2,1)S(1)}, bf16[16,2816]{1,0:T(8,128)(2,1)S(1)}, u32[]{:S(2)}, u32[]{:S(2)}) collective-permute-start(bf16[16,2816]{1,0:T(8,128)(2,1)S(1)} %get-tuple-element.83), channel_id=1, source_target_pairs={{0,4},{1,5},{2,6},{3,7},{4,0},{5,1},{6,2},{7,3},{8,12},{9,13},{10,... | collective-permute-start | bytes 270344 | tf_op jit(solution)/shard_map/ppermute | solution.py:34
  74.4 11.7 %collective-permute-start.22 = (bf16[16,2816]{1,0:T(8,128)(2,1)S(1)}, bf16[16,2816]{1,0:T(8,128)(2,1)S(1)}, u32[]{:S(2)}, u32[]{:S(2)}) collective-permute-start(bf16[16,2816]{1,0:T(8,128)(2,1)S(1)} %get-tuple-element.82), channel_id=1, source_target_pairs={{0,12},{1,13},{2,14},{3,15},{4,8},{5,9},{6,10},{7,11},{8,4},{9,5},... | collective-permute-start | bytes 270344 | tf_op jit(solution)/shard_map/ppermute | solution.py:34
  81.6 9.0 %collective-permute-start.18 = (bf16[8,5376]{1,0:T(8,128)(2,1)S(1)}, bf16[8,5376]{1,0:T(8,128)(2,1)S(1)}, u32[]{:S(2)}, u32[]{:S(2)}) collective-permute-start(bf16[8,5376]{1,0:T(8,128)(2,1)S(1)} %get-tuple-element.86), channel_id=1, source_target_pairs={{0,8},{1,9},{2,10},{3,11},{4,12},{5,13},{6,14},{7,15},{8,0},{9,1},... | collective-permute-start | bytes 258056 | tf_op jit(solution)/shard_map/ppermute | solution.py:34
  82.6 8.0 %collective-permute-start.19 = (bf16[8,5376]{1,0:T(8,128)(2,1)S(1)}, bf16[8,5376]{1,0:T(8,128)(2,1)S(1)}, u32[]{:S(2)}, u32[]{:S(2)}) collective-permute-start(bf16[8,5376]{1,0:T(8,128)(2,1)S(1)} %get-tuple-element.85), channel_id=1, source_target_pairs={{0,4},{1,5},{2,6},{3,7},{4,0},{5,1},{6,2},{7,3},{8,12},{9,13},{10,... | collective-permute-start | bytes 258056 | tf_op jit(solution)/shard_map/ppermute | solution.py:34
  83.4 7.2 %collective-permute-start.20 = (bf16[8,5376]{1,0:T(8,128)(2,1)S(1)}, bf16[8,5376]{1,0:T(8,128)(2,1)S(1)}, u32[]{:S(2)}, u32[]{:S(2)}) collective-permute-start(bf16[8,5376]{1,0:T(8,128)(2,1)S(1)} %get-tuple-element.84), channel_id=1, source_target_pairs={{0,12},{1,13},{2,14},{3,15},{4,8},{5,9},{6,10},{7,11},{8,4},{9,5},... | collective-permute-start | bytes 258056 | tf_op jit(solution)/shard_map/ppermute | solution.py:34
  86.1 4.6 %collective-permute-start.23 = (bf16[8,2816]{1,0:T(8,128)(2,1)S(1)}, bf16[8,2816]{1,0:T(8,128)(2,1)S(1)}, u32[]{:S(2)}, u32[]{:S(2)}) collective-permute-start(bf16[8,2816]{1,0:T(8,128)(2,1)S(1)} %slice.88), channel_id=1, source_target_pairs={{0,2},{1,3},{2,0},{3,1},{4,6},{5,7},{6,4},{7,5},{8,10},{9,11},{10,... | collective-permute-start | bytes 135176 | tf_op jit(solution)/shard_map/ppermute | solution.py:34
  (8 other events, 43.0 us)

commit v23 on v17

--- a/solution.py
+++ b/solution.py
@@ -673,7 +673,7 @@
     (w_front,) = fetch((after(w_out, attended), (0, width // 32 * 10)), limit=48)
     returned = lax.all_to_all(attended, AXES, split_axis=0, concat_axis=0, tiled=True)
     returned = returned.reshape(all_slots, per_query)
-    summed = scatter_sum(grid, place_a, place_b, returned, w_out, w_front, width // 32 * 21)
+    summed = scatter_sum(grid, place_a, place_b, returned, w_out, w_front, width // 32 * 22)
     return narrow(wide(hidden_in) + summed)
 
 

time: 91.5 us -> 92.1 us (level)
  no operation moved by 1% of the time
where the time goes in v23:
time: 92.1 us; the launch traced here: 91.7 us
  waiting for transfers between devices  36.2 us (39%)
  starting transfers between devices  32.5 us (35%)
  Pallas kernels  19 us (21%)
  other arithmetic  3.31 us (4%)
    ppermute x24, starting transfers between devices, send(): return lax.ppermute(x, AXES, pairs)  24.5 us
    ppermute x24, waiting for transfers between devices, send(): return lax.ppermute(x, AXES, pairs)  17.6 us
    all_to_all x1, waiting for transfers between devices, on_device(): lax.all_to_all(outbound, AXES, split_axis=0, concat_axis=0, tiled=True)  10.4 us
    all_to_all x1, waiting for transfers between devices, on_device(): lax.all_to_all(attended, AXES, split_axis=0, concat_axis=0, tiled=True)  8.25 us
    pallas_call x1, Pallas kernels, attend(): pl.pallas_call(functools.partial(attend_kernel, per_query, per_key), in_s...  5.88 us
    pallas_call x2, Pallas kernels, fetch(): pl.pallas_call(functools.partial(fetch_kernel, starts), in_specs=[pl.Bloc...  5.14 us
    all_to_all x1, starting transfers between devices, on_device(): lax.all_to_all(outbound, AXES, split_axis=0, concat_axis=0, tiled=True)  4.41 us
    all_to_all x1, starting transfers between devices, on_device(): lax.all_to_all(attended, AXES, split_axis=0, concat_axis=0, tiled=True)  3.54 us
  transfers between devices with their start and end apart: 26, of which 11 were waited for; matrix products, arithmetic and copies ran while one was open for 3% of the time, Pallas kernels for 7%

profile of v23, /device:TPU:0, one launch (start us, length us, event | category | flops | bytes accessed | tf_op | source)
XLA Modules:
  0.0 91.7 jit_solution(4042646719916617648)
XLA Ops:
  0.0 1.7 %norm.1 = (bf16[8,5632]{1,0:T(8,128)(2,1)}, bf16[8,2560]{1,0:T(8,128)(2,1)}) custom-call(bf16[8,8192]{1,0:T(8,128)(2,1)} %x.1, f32[1,8192]{1,0:T(1,128)} %bitcast.21), custom_call_target="tpu_custom_call" | custom-call | tf_op jit(solution)/shard_map/norm/pallas_call | solution.py:229
  1.7 4.1 %collective-permute-start = (bf16[8,5632]{1,0:T(8,128)(2,1)}, bf16[8,5632]{1,0:T(8,128)(2,1)S(1)}, u32[]{:S(2)}, u32[]{:S(2)}) collective-permute-start(bf16[8,5632]{1,0:T(8,128)(2,1)} %get-tuple-element.41), channel_id=1, source_target_pairs={{0,8},{1,9},{2,10},{3,11},{4,12},{5,13},{6,14},{7,15},{8,0},{9,1},... | collective-permute-start | bytes 270344 | tf_op jit(solution)/shard_map/ppermute | solution.py:34
  5.8 1.6 %collective-permute-start.1 = (bf16[8,5632]{1,0:T(8,128)(2,1)}, bf16[8,5632]{1,0:T(8,128)(2,1)S(1)}, u32[]{:S(2)}, u32[]{:S(2)}) collective-permute-start(bf16[8,5632]{1,0:T(8,128)(2,1)} %get-tuple-element.41), channel_id=1, source_target_pairs={{0,4},{1,5},{2,6},{3,7},{4,0},{5,1},{6,2},{7,3},{8,12},{9,13},{10,... | collective-permute-start | bytes 270344 | tf_op jit(solution)/shard_map/ppermute | solution.py:34
  7.4 1.7 %collective-permute-start.3 = (bf16[8,2560]{1,0:T(8,128)(2,1)}, bf16[8,2560]{1,0:T(8,128)(2,1)S(1)}, u32[]{:S(2)}, u32[]{:S(2)}) collective-permute-start(bf16[8,2560]{1,0:T(8,128)(2,1)} %get-tuple-element.42), channel_id=1, source_target_pairs={{0,2},{1,3},{2,0},{3,1},{4,6},{5,7},{6,4},{7,5},{8,10},{9,11},{10,... | collective-permute-start | bytes 122888 | tf_op jit(solution)/shard_map/ppermute | solution.py:34
  9.2 1.8 %pad_maximum_fusion.refs_5_.refs_9_ = bf16[128,8192]{1,0:T(8,128)(2,1)S(1)} fusion(bf16[64,8192]{1,0:T(8,128)(2,1)} %bitcast.19, bf16[64,8192]{1,0:T(8,128)(2,1)} %bitcast.20), kind=kLoop, calls=%fused_computation | loop fusion | flops 4194304 | bytes 4194304 | tf_op jit(solution)/shard_map/concatenate | solution.py:639
  11.7 2.3 %collective-permute-done.2 = bf16[8,5632]{1,0:T(8,128)(2,1)S(1)} collective-permute-done((bf16[8,5632]{1,0:T(8,128)(2,1)}, bf16[8,5632]{1,0:T(8,128)(2,1)S(1)}, u32[]{:S(2)}, u32[]{:S(2)}) %collective-permute-start.2) | collective-permute-done | bytes 90144 | tf_op jit(solution)/shard_map/ppermute | solution.py:34
  14.1 1.6 %collective-permute-start.4 = (bf16[32,5632]{1,0:T(8,128)(2,1)S(1)}, bf16[32,5632]{1,0:T(8,128)(2,1)S(1)}, u32[]{:S(2)}, u32[]{:S(2)}) collective-permute-start(bf16[32,5632]{1,0:T(8,128)(2,1)S(1)} %pad_maximum_fusion.1.refs_0_), channel_id=1, source_target_pairs={{0,2},{1,3},{2,0},{3,1},{4,6},{5,7},{6,4},{7,5},{8,10},{9,11},{10,... | collective-permute-start | bytes 1081352 | tf_op jit(solution)/shard_map/ppermute | solution.py:34
  15.6 3.1 %collective-permute-start.5 = (bf16[16,2560]{1,0:T(8,128)(2,1)S(1)}, bf16[16,2560]{1,0:T(8,128)(2,1)S(1)}, u32[]{:S(2)}, u32[]{:S(2)}) collective-permute-start(bf16[16,2560]{1,0:T(8,128)(2,1)S(1)} %pad_maximum_fusion.2.refs_0_), channel_id=1, source_target_pairs={{0,8},{1,9},{2,10},{3,11},{4,12},{5,13},{6,14},{7,15},{8,0},{9,1},... | collective-permute-start | bytes 245768 | tf_op jit(solution)/shard_map/ppermute | solution.py:34
  18.7 1.5 %collective-permute-start.7 = (bf16[16,2560]{1,0:T(8,128)(2,1)S(1)}, bf16[16,2560]{1,0:T(8,128)(2,1)S(1)}, u32[]{:S(2)}, u32[]{:S(2)}) collective-permute-start(bf16[16,2560]{1,0:T(8,128)(2,1)S(1)} %pad_maximum_fusion.2.refs_0_), channel_id=1, source_target_pairs={{0,12},{1,13},{2,14},{3,15},{4,8},{5,9},{6,10},{7,11},{8,4},{9,5},... | collective-permute-start | bytes 245768 | tf_op jit(solution)/shard_map/ppermute | solution.py:34
  20.2 3.4 %fetch.2.refs_4_.refs_8_ = bf16[8192,512]{1,0:T(8,128)(2,1)S(1)} custom-call(bf16[8192,512]{1,0:T(8,128)(2,1)} %refs_0_), custom_call_target="tpu_custom_call" | custom-call | bytes 16777216 | tf_op jit(solution)/shard_map/fetch/pallas_call | solution.py:319
  24.0 1.4 %collective-permute-done.6.refs_2_ = bf16[16,2560]{1,0:T(8,128)(2,1)S(1)} collective-permute-done((bf16[16,2560]{1,0:T(8,128)(2,1)S(1)}, bf16[16,2560]{1,0:T(8,128)(2,1)S(1)}, u32[]{:S(2)}, u32[]{:S(2)}) %collective-permute-start.6) | collective-permute-done | bytes 81952 | tf_op jit(solution)/shard_map/ppermute | solution.py:34
  28.4 1.6 %project.3 = bf16[256,640]{1,0:T(8,128)(2,1)} custom-call(bf16[16,2560]{1,0:T(8,128)(2,1)S(1)} %pad_maximum_fusion.2.refs_0_, bf16[16,2560]{1,0:T(8,128)(2,1)S(1)} %collective-permute-done.5.refs_1_, bf16[16,2560]{1,0:T(8,128)(2,1)S(1)} %collective-permute-done.6.refs_2_, bf16[16,2560]{1,0:T(8,128)(2,1)S(1)} %collective-permute-done.7.refs_3_, ...), custom_call_target="tpu_custom_call" | custom-call | flops 419430400 | bytes 3276800 | tf_op jit(solution)/shard_map/project/pallas_call | solution.py:397
  30.0 4.4 %all-to-all-start = ((bf16[16,16,640]{2,1,0:T(8,128)(2,1)}), bf16[16,16,640]{2,1,0:T(8,128)(2,1)S(1)}, u32[]{:S(2)}, u32[]{:S(2)}) async-start(bf16[16,16,640]{2,1,0:T(8,128)(2,1)} %bitcast.4), calls=%async_computation | async-start | bytes 655360 | tf_op jit(solution)/shard_map/all_to_all | solution.py:661
  35.1 10.4 %all-to-all-done.inbound = bf16[16,16,640]{2,1,0:T(8,128)(2,1)S(1)} async-done(((bf16[16,16,640]{2,1,0:T(8,128)(2,1)}), bf16[16,16,640]{2,1,0:T(8,128)(2,1)S(1)}, u32[]{:S(2)}, u32[]{:S(2)}) %all-to-all-start) | async-done | bytes 327712 | tf_op jit(solution)/shard_map/all_to_all | solution.py:661
  45.5 5.9 %attend.1 = bf16[16,16,512]{2,1,0:T(8,128)(2,1)} custom-call(s32[16,4]{1,0:T(8,128)S(1)} %copy.15.table, s32[2,1,128]{2,1,0:T(1,128)S(1)} %bitcast.14, bf16[16,16,640]{2,1,0:T(8,128)(2,1)S(1)} %all-to-all-done.inbound, f32[16,128]{1,0:T(8,128)S(1)} %get-tuple-element.90.cosine, f32[16,128]{1,0:T(8,128)S(1)} %get-tuple-element.91.sine, ...), custom_call_target="tpu_custom_call" | custom-call | flops 134217728 | bytes 8388608 | tf_op jit(solution)/shard_map/attend/pallas_call | solution.py:578
  51.4 3.5 %all-to-all-start.1 = ((bf16[16,16,512]{2,1,0:T(8,128)(2,1)}), bf16[16,16,512]{2,1,0:T(8,128)(2,1)S(1)}, u32[]{:S(2)}, u32[]{:S(2)}) async-start(bf16[16,16,512]{2,1,0:T(8,128)(2,1)} %attend.1), calls=%async_computation.1 | async-start | bytes 524288 | tf_op jit(solution)/shard_map/all_to_all | solution.py:674
  55.0 1.8 %fetch.3.w_front = bf16[512,2560]{1,0:T(8,128)(2,1)S(1)} custom-call(bf16[512,8192]{1,0:T(8,128)(2,1)} %w_out.1), custom_call_target="tpu_custom_call" | custom-call | bytes 5242880 | tf_op jit(solution)/shard_map/fetch/pallas_call | solution.py:319
  56.7 8.2 %all-to-all-done.1 = bf16[16,16,512]{2,1,0:T(8,128)(2,1)S(1)} async-done(((bf16[16,16,512]{2,1,0:T(8,128)(2,1)}), bf16[16,16,512]{2,1,0:T(8,128)(2,1)S(1)}, u32[]{:S(2)}, u32[]{:S(2)}) %all-to-all-start.1) | async-done | bytes 262176 | tf_op jit(solution)/shard_map/all_to_all | solution.py:674
  65.0 3.1 %product.1 = (bf16[64,5632]{1,0:T(8,128)(2,1)S(1)}, f32[64,5632]{1,0:T(8,128)S(1)}, bf16[64,2560]{1,0:T(8,128)(2,1)S(1)}, f32[64,2560]{1,0:T(8,128)S(1)}) custom-call(s32[1,128]{1,0:T(1,128)S(1)} %get-tuple-element.50.place_a, s32[1,128]{1,0:T(1,128)S(1)} %get-tuple-element.51.place_b, bf16[256,512]{1,0:T(8,128)(2,1)S(1)} %bitcast.13, ...), custom_call_target="tpu_custom_call" | custom-call | flops 1073741824 | bytes 8388608 | tf_op jit(solution)/shard_map/product/pallas_call | solution.py:155
  68.2 2.2 %collective-permute-done.14 = bf16[64,5632]{1,0:T(8,128)(2,1)S(1)} collective-permute-done((bf16[64,5632]{1,0:T(8,128)(2,1)S(1)}, bf16[64,5632]{1,0:T(8,128)(2,1)S(1)}, u32[]{:S(2)}, u32[]{:S(2)}) %collective-permute-start.14) | collective-permute-done | bytes 720928 | tf_op jit(solution)/shard_map/ppermute | solution.py:34
  74.0 2.9 %collective-permute-start.22 = (bf16[16,2560]{1,0:T(8,128)(2,1)S(1)}, bf16[16,2560]{1,0:T(8,128)(2,1)S(1)}, u32[]{:S(2)}, u32[]{:S(2)}) collective-permute-start(bf16[16,2560]{1,0:T(8,128)(2,1)S(1)} %get-tuple-element.85), channel_id=1, source_target_pairs={{0,12},{1,13},{2,14},{3,15},{4,8},{5,9},{6,10},{7,11},{8,4},{9,5},... | collective-permute-start | bytes 245768 | tf_op jit(solution)/shard_map/ppermute | solution.py:34
  76.9 4.6 %collective-permute-done.15 = bf16[32,5632]{1,0:T(8,128)(2,1)S(1)} collective-permute-done((bf16[32,5632]{1,0:T(8,128)(2,1)S(1)}, bf16[32,5632]{1,0:T(8,128)(2,1)S(1)}, u32[]{:S(2)}, u32[]{:S(2)}) %collective-permute-start.15) | collective-permute-done | bytes 360480 | tf_op jit(solution)/shard_map/ppermute | solution.py:34
  83.2 2.9 %collective-permute-start.20 = (bf16[8,5632]{1,0:T(8,128)(2,1)S(1)}, bf16[8,5632]{1,0:T(8,128)(2,1)S(1)}, u32[]{:S(2)}, u32[]{:S(2)}) collective-permute-start(bf16[8,5632]{1,0:T(8,128)(2,1)S(1)} %get-tuple-element.81), channel_id=1, source_target_pairs={{0,12},{1,13},{2,14},{3,15},{4,8},{5,9},{6,10},{7,11},{8,4},{9,5},... | collective-permute-start | bytes 270344 | tf_op jit(solution)/shard_map/ppermute | solution.py:34
  86.5 4.4 %collective-permute-done.18 = bf16[8,5632]{1,0:T(8,128)(2,1)S(1)} collective-permute-done((bf16[8,5632]{1,0:T(8,128)(2,1)S(1)}, bf16[8,5632]{1,0:T(8,128)(2,1)S(1)}, u32[]{:S(2)}, u32[]{:S(2)}) %collective-permute-start.18) | collective-permute-done | bytes 90144 | tf_op jit(solution)/shard_map/ppermute | solution.py:34
  (72 shorter events, 11.3 us)
Async XLA Ops:
  1.7 9.9 %collective-permute-start = (bf16[8,5632]{1,0:T(8,128)(2,1)}, bf16[8,5632]{1,0:T(8,128)(2,1)S(1)}, u32[]{:S(2)}, u32[]{:S(2)}) collective-permute-start(bf16[8,5632]{1,0:T(8,128)(2,1)} %get-tuple-element.41), channel_id=1, source_target_pairs={{0,8},{1,9},{2,10},{3,11},{4,12},{5,13},{6,14},{7,15},{8,0},{9,1},... | collective-permute-start | bytes 270344 | tf_op jit(solution)/shard_map/ppermute | solution.py:34
  5.8 5.8 %collective-permute-start.1 = (bf16[8,5632]{1,0:T(8,128)(2,1)}, bf16[8,5632]{1,0:T(8,128)(2,1)S(1)}, u32[]{:S(2)}, u32[]{:S(2)}) collective-permute-start(bf16[8,5632]{1,0:T(8,128)(2,1)} %get-tuple-element.41), channel_id=1, source_target_pairs={{0,4},{1,5},{2,6},{3,7},{4,0},{5,1},{6,2},{7,3},{8,12},{9,13},{10,... | collective-permute-start | bytes 270344 | tf_op jit(solution)/shard_map/ppermute | solution.py:34
  7.4 6.6 %collective-permute-start.2 = (bf16[8,5632]{1,0:T(8,128)(2,1)}, bf16[8,5632]{1,0:T(8,128)(2,1)S(1)}, u32[]{:S(2)}, u32[]{:S(2)}) collective-permute-start(bf16[8,5632]{1,0:T(8,128)(2,1)} %get-tuple-element.41), channel_id=1, source_target_pairs={{0,12},{1,13},{2,14},{3,15},{4,8},{5,9},{6,10},{7,11},{8,4},{9,5},... | collective-permute-start | bytes 270344 | tf_op jit(solution)/shard_map/ppermute | solution.py:34
  7.4 4.2 %collective-permute-start.3 = (bf16[8,2560]{1,0:T(8,128)(2,1)}, bf16[8,2560]{1,0:T(8,128)(2,1)S(1)}, u32[]{:S(2)}, u32[]{:S(2)}) collective-permute-start(bf16[8,2560]{1,0:T(8,128)(2,1)} %get-tuple-element.42), channel_id=1, source_target_pairs={{0,2},{1,3},{2,0},{3,1},{4,6},{5,7},{6,4},{7,5},{8,10},{9,11},{10,... | collective-permute-start | bytes 122888 | tf_op jit(solution)/shard_map/ppermute | solution.py:34
  14.1 11.3 %collective-permute-start.4 = (bf16[32,5632]{1,0:T(8,128)(2,1)S(1)}, bf16[32,5632]{1,0:T(8,128)(2,1)S(1)}, u32[]{:S(2)}, u32[]{:S(2)}) collective-permute-start(bf16[32,5632]{1,0:T(8,128)(2,1)S(1)} %pad_maximum_fusion.1.refs_0_), channel_id=1, source_target_pairs={{0,2},{1,3},{2,0},{3,1},{4,6},{5,7},{6,4},{7,5},{8,10},{9,11},{10,... | collective-permute-start | bytes 1081352 | tf_op jit(solution)/shard_map/ppermute | solution.py:34
  15.6 8.4 %collective-permute-start.5 = (bf16[16,2560]{1,0:T(8,128)(2,1)S(1)}, bf16[16,2560]{1,0:T(8,128)(2,1)S(1)}, u32[]{:S(2)}, u32[]{:S(2)}) collective-permute-start(bf16[16,2560]{1,0:T(8,128)(2,1)S(1)} %pad_maximum_fusion.2.refs_0_), channel_id=1, source_target_pairs={{0,8},{1,9},{2,10},{3,11},{4,12},{5,13},{6,14},{7,15},{8,0},{9,1},... | collective-permute-start | bytes 245768 | tf_op jit(solution)/shard_map/ppermute | solution.py:34
  18.7 6.7 %collective-permute-start.6 = (bf16[16,2560]{1,0:T(8,128)(2,1)S(1)}, bf16[16,2560]{1,0:T(8,128)(2,1)S(1)}, u32[]{:S(2)}, u32[]{:S(2)}) collective-permute-start(bf16[16,2560]{1,0:T(8,128)(2,1)S(1)} %pad_maximum_fusion.2.refs_0_), channel_id=1, source_target_pairs={{0,4},{1,5},{2,6},{3,7},{4,0},{5,1},{6,2},{7,3},{8,12},{9,13},{10,... | collective-permute-start | bytes 245768 | tf_op jit(solution)/shard_map/ppermute | solution.py:34
  18.7 6.7 %collective-permute-start.7 = (bf16[16,2560]{1,0:T(8,128)(2,1)S(1)}, bf16[16,2560]{1,0:T(8,128)(2,1)S(1)}, u32[]{:S(2)}, u32[]{:S(2)}) collective-permute-start(bf16[16,2560]{1,0:T(8,128)(2,1)S(1)} %pad_maximum_fusion.2.refs_0_), channel_id=1, source_target_pairs={{0,12},{1,13},{2,14},{3,15},{4,8},{5,9},{6,10},{7,11},{8,4},{9,5},... | collective-permute-start | bytes 245768 | tf_op jit(solution)/shard_map/ppermute | solution.py:34
  20.2 6.2 %collective-permute-start.12 = (bf16[32,5632]{1,0:T(8,128)(2,1)S(1)}, bf16[32,5632]{1,0:T(8,128)(2,1)S(1)}, u32[]{:S(2)}, u32[]{:S(2)}) collective-permute-start(bf16[32,5632]{1,0:T(8,128)(2,1)S(1)} %pad_maximum_fusion.1.refs_0_), channel_id=1, source_target_pairs={{0,1},{1,0},{2,3},{3,2},{4,5},{5,4},{6,7},{7,6},{8,9},{9,8},{10,11... | collective-permute-start | bytes 1081352 | tf_op jit(solution)/shard_map/ppermute | solution.py:34
  25.4 3.0 %collective-permute-start.10 = (bf16[16,2560]{1,0:T(8,128)(2,1)S(1)}, bf16[16,2560]{1,0:T(8,128)(2,1)S(1)}, u32[]{:S(2)}, u32[]{:S(2)}) collective-permute-start(bf16[16,2560]{1,0:T(8,128)(2,1)S(1)} %collective-permute-done.6.refs_2_), channel_id=1, source_target_pairs={{0,1},{1,0},{2,3},{3,2},{4,5},{5,4},{6,7},{7,6},{8,9},{9,8},{10,11... | collective-permute-start | bytes 245768 | tf_op jit(solution)/shard_map/ppermute | solution.py:34
  25.9 2.5 %collective-permute-start.11 = (bf16[16,2560]{1,0:T(8,128)(2,1)S(1)}, bf16[16,2560]{1,0:T(8,128)(2,1)S(1)}, u32[]{:S(2)}, u32[]{:S(2)}) collective-permute-start(bf16[16,2560]{1,0:T(8,128)(2,1)S(1)} %collective-permute-done.7.refs_3_), channel_id=1, source_target_pairs={{0,1},{1,0},{2,3},{3,2},{4,5},{5,4},{6,7},{7,6},{8,9},{9,8},{10,11... | collective-permute-start | bytes 245768 | tf_op jit(solution)/shard_map/ppermute | solution.py:34
  26.0 2.4 %collective-permute-start.8 = (bf16[16,2560]{1,0:T(8,128)(2,1)S(1)}, bf16[16,2560]{1,0:T(8,128)(2,1)S(1)}, u32[]{:S(2)}, u32[]{:S(2)}) collective-permute-start(bf16[16,2560]{1,0:T(8,128)(2,1)S(1)} %pad_maximum_fusion.2.refs_0_), channel_id=1, source_target_pairs={{0,1},{1,0},{2,3},{3,2},{4,5},{5,4},{6,7},{7,6},{8,9},{9,8},{10,11... | collective-permute-start | bytes 245768 | tf_op jit(solution)/shard_map/ppermute | solution.py:34
  26.4 2.0 %collective-permute-start.9 = (bf16[16,2560]{1,0:T(8,128)(2,1)S(1)}, bf16[16,2560]{1,0:T(8,128)(2,1)S(1)}, u32[]{:S(2)}, u32[]{:S(2)}) collective-permute-start(bf16[16,2560]{1,0:T(8,128)(2,1)S(1)} %collective-permute-done.5.refs_1_), channel_id=1, source_target_pairs={{0,1},{1,0},{2,3},{3,2},{4,5},{5,4},{6,7},{7,6},{8,9},{9,8},{10,11... | collective-permute-start | bytes 245768 | tf_op jit(solution)/shard_map/ppermute | solution.py:34
  30.0 15.5 %all-to-all-start = ((bf16[16,16,640]{2,1,0:T(8,128)(2,1)}), bf16[16,16,640]{2,1,0:T(8,128)(2,1)S(1)}, u32[]{:S(2)}, u32[]{:S(2)}) async-start(bf16[16,16,640]{2,1,0:T(8,128)(2,1)} %bitcast.4), calls=%async_computation | async-start | bytes 655360 | tf_op jit(solution)/shard_map/all_to_all | solution.py:661
  51.4 13.6 %all-to-all-start.1 = ((bf16[16,16,512]{2,1,0:T(8,128)(2,1)}), bf16[16,16,512]{2,1,0:T(8,128)(2,1)S(1)}, u32[]{:S(2)}, u32[]{:S(2)}) async-start(bf16[16,16,512]{2,1,0:T(8,128)(2,1)} %attend.1), calls=%async_computation.1 | async-start | bytes 524288 | tf_op jit(solution)/shard_map/all_to_all | solution.py:674
  68.1 2.3 %collective-permute-start.14 = (bf16[64,5632]{1,0:T(8,128)(2,1)S(1)}, bf16[64,5632]{1,0:T(8,128)(2,1)S(1)}, u32[]{:S(2)}, u32[]{:S(2)}) collective-permute-start(bf16[64,5632]{1,0:T(8,128)(2,1)S(1)} %get-tuple-element.69), channel_id=1, source_target_pairs={{0,1},{1,0},{2,3},{3,2},{4,5},{5,4},{6,7},{7,6},{8,9},{9,8},{10,11... | collective-permute-start | bytes 2162696 | tf_op jit(solution)/shard_map/ppermute | solution.py:34
  70.8 10.7 %collective-permute-start.15 = (bf16[32,5632]{1,0:T(8,128)(2,1)S(1)}, bf16[32,5632]{1,0:T(8,128)(2,1)S(1)}, u32[]{:S(2)}, u32[]{:S(2)}) collective-permute-start(bf16[32,5632]{1,0:T(8,128)(2,1)S(1)} %slice.87), channel_id=1, source_target_pairs={{0,2},{1,3},{2,0},{3,1},{4,6},{5,7},{6,4},{7,5},{8,10},{9,11},{10,... | collective-permute-start | bytes 1081352 | tf_op jit(solution)/shard_map/ppermute | solution.py:34
  72.4 9.1 %collective-permute-start.17 = (bf16[16,2560]{1,0:T(8,128)(2,1)S(1)}, bf16[16,2560]{1,0:T(8,128)(2,1)S(1)}, u32[]{:S(2)}, u32[]{:S(2)}) collective-permute-start(bf16[16,2560]{1,0:T(8,128)(2,1)S(1)} %get-tuple-element.84), channel_id=1, source_target_pairs={{0,8},{1,9},{2,10},{3,11},{4,12},{5,13},{6,14},{7,15},{8,0},{9,1},... | collective-permute-start | bytes 245768 | tf_op jit(solution)/shard_map/ppermute | solution.py:34
  73.5 12.6 %collective-permute-start.21 = (bf16[16,2560]{1,0:T(8,128)(2,1)S(1)}, bf16[16,2560]{1,0:T(8,128)(2,1)S(1)}, u32[]{:S(2)}, u32[]{:S(2)}) collective-permute-start(bf16[16,2560]{1,0:T(8,128)(2,1)S(1)} %get-tuple-element.86), channel_id=1, source_target_pairs={{0,4},{1,5},{2,6},{3,7},{4,0},{5,1},{6,2},{7,3},{8,12},{9,13},{10,... | collective-permute-start | bytes 245768 | tf_op jit(solution)/shard_map/ppermute | solution.py:34
  74.0 12.1 %collective-permute-start.22 = (bf16[16,2560]{1,0:T(8,128)(2,1)S(1)}, bf16[16,2560]{1,0:T(8,128)(2,1)S(1)}, u32[]{:S(2)}, u32[]{:S(2)}) collective-permute-start(bf16[16,2560]{1,0:T(8,128)(2,1)S(1)} %get-tuple-element.85), channel_id=1, source_target_pairs={{0,12},{1,13},{2,14},{3,15},{4,8},{5,9},{6,10},{7,11},{8,4},{9,5},... | collective-permute-start | bytes 245768 | tf_op jit(solution)/shard_map/ppermute | solution.py:34
  81.6 9.3 %collective-permute-start.18 = (bf16[8,5632]{1,0:T(8,128)(2,1)S(1)}, bf16[8,5632]{1,0:T(8,128)(2,1)S(1)}, u32[]{:S(2)}, u32[]{:S(2)}) collective-permute-start(bf16[8,5632]{1,0:T(8,128)(2,1)S(1)} %get-tuple-element.83), channel_id=1, source_target_pairs={{0,8},{1,9},{2,10},{3,11},{4,12},{5,13},{6,14},{7,15},{8,0},{9,1},... | collective-permute-start | bytes 270344 | tf_op jit(solution)/shard_map/ppermute | solution.py:34
  82.7 8.2 %collective-permute-start.19 = (bf16[8,5632]{1,0:T(8,128)(2,1)S(1)}, bf16[8,5632]{1,0:T(8,128)(2,1)S(1)}, u32[]{:S(2)}, u32[]{:S(2)}) collective-permute-start(bf16[8,5632]{1,0:T(8,128)(2,1)S(1)} %get-tuple-element.82), channel_id=1, source_target_pairs={{0,4},{1,5},{2,6},{3,7},{4,0},{5,1},{6,2},{7,3},{8,12},{9,13},{10,... | collective-permute-start | bytes 270344 | tf_op jit(solution)/shard_map/ppermute | solution.py:34
  83.2 7.7 %collective-permute-start.20 = (bf16[8,5632]{1,0:T(8,128)(2,1)S(1)}, bf16[8,5632]{1,0:T(8,128)(2,1)S(1)}, u32[]{:S(2)}, u32[]{:S(2)}) collective-permute-start(bf16[8,5632]{1,0:T(8,128)(2,1)S(1)} %get-tuple-element.81), channel_id=1, source_target_pairs={{0,12},{1,13},{2,14},{3,15},{4,8},{5,9},{6,10},{7,11},{8,4},{9,5},... | collective-permute-start | bytes 270344 | tf_op jit(solution)/shard_map/ppermute | solution.py:34
  86.1 4.8 %collective-permute-start.23 = (bf16[8,2560]{1,0:T(8,128)(2,1)S(1)}, bf16[8,2560]{1,0:T(8,128)(2,1)S(1)}, u32[]{:S(2)}, u32[]{:S(2)}) collective-permute-start(bf16[8,2560]{1,0:T(8,128)(2,1)S(1)} %slice.88), channel_id=1, source_target_pairs={{0,2},{1,3},{2,0},{3,1},{4,6},{5,7},{6,4},{7,5},{8,10},{9,11},{10,... | collective-permute-start | bytes 122888 | tf_op jit(solution)/shard_map/ppermute | solution.py:34
  (8 other events, 42.0 us)
